TPU v7x, 32 devices: a whole 2x2x4 slice. The times are simulated.
32 devices in a mesh: tm: 16 (over z, y, x), head: 2 (over core).
Axes of the slice: x: 2, y: 2, z: 4, core: 2. Of those that a mesh axis runs over, the one named last changes fastest.
Arguments:
- frames: bfloat16 [4096, 1024], P('tm'), may hold values from -6 to 6
- x_weight: bfloat16 [1024, 2048], P('tm', 'head'), may hold values from -0.1875 to 0.1875
- z_weight: bfloat16 [1024, 2048], P('tm', 'head'), may hold values from -0.1875 to 0.1875
- bc_weight: bfloat16 [1024, 256], P('tm'), may hold values from -0.1875 to 0.1875
- log_decay: float32 [32, 4096], P('head', 'tm'), may hold values from -0.9 to 0
- norm_gain: float32 [2048], P('head'), may hold values from 0.1 to 1.9
- conv_weight: float32 [31, 2048], P(None, 'head'), may hold values from -1 to 1
- out_weight: bfloat16 [2048, 1024], P('head', 'tm'), may hold values from -0.125 to 0.125
- record_lengths: int32 [8], replicated, may hold values from 1 to 3072, 4096 in all
Outputs:
- mixed: bfloat16 [4096, 1024], P('tm', 'head')
Inputs may be any that keep to these rules, and one draw needn't show every extreme that they name: `record_lengths`: 8 recording lengths that sum to 4096; the longest has exactly 3072 frames.
All inputs are finite; a program needn't handle non-finite values.
Results may differ from a plain program's by a relative error of at most 0.02.
Values may be sent and summed in bfloat16 or wider, within the bound.
No kernel may reach another device: no remote copies, remote signals or barrier semaphores. Data moves between devices by JAX's collectives and lax.ppermute only.
A program may use at most 64 MiB of HBM per device.

v0:
```python
import jax
import jax.numpy as jnp
from jax import lax
from jax.sharding import PartitionSpec as P

SPAN = 128


highest = lax.Precision.HIGHEST


def extended_2(array, sides, width):
    for axis, dim in sides:
        peers, length = (lax.axis_size(axis), array.shape[dim])
        up = [(i, (i + 1) % peers) for i in range(peers - 1)]
        down = [(j, i) for i, j in up]
        last = lax.slice_in_dim(array, length - width, length, axis=dim)
        leading = lax.slice_in_dim(array, 0, width, axis=dim)
        before = lax.ppermute(last, axis, up)
        after = lax.ppermute(leading, axis, down)
        array = jnp.concatenate([before, array, after], axis=dim)
    return array


def segment_ids(record_lengths, positions):
    record_ends = jnp.cumsum(record_lengths)
    return jnp.sum((record_ends[None, :] <= positions[:, None]).astype(jnp.int32), axis=1)


def span_step(state, inputs):
    x_block, b_block, c_block, log_block, seg_block, seg_before = inputs
    length = seg_block.shape[0]
    cumul = jnp.cumsum(log_block, axis=1)
    lower = jnp.arange(length)[:, None] >= jnp.arange(length)[None, :]
    joined = (seg_block[:, None] == seg_block[None, :]) & lower
    spread = cumul[:, :, None] - cumul[:, None, :]
    mixing = jnp.exp(jnp.where(joined[None], spread, -jnp.inf))
    scores = jnp.dot(c_block, b_block.T, preferred_element_type=jnp.float32)
    x_float = x_block.astype(jnp.float32)
    inner = jnp.einsum("hts,shp->thp", mixing * scores[None], x_float, precision=highest)
    carried = jnp.exp(cumul) * (seg_block == seg_before).astype(jnp.float32)[None, :]
    c_float = c_block.astype(jnp.float32)
    outer = jnp.einsum("tn,hnp->thp", c_float, state, precision=highest) * carried.T[:, :, None]
    tail = (
        jnp.exp(cumul[:, -1:] - cumul) * (seg_block == seg_block[-1]).astype(jnp.float32)[None, :]
    )
    weighted = tail[:, :, None] * b_block.astype(jnp.float32)[None, :, :]
    state_next = carried[:, -1][:, None, None] * state + jnp.einsum(
        "hsn,shp->hnp", weighted, x_float, precision=highest
    )
    return (state_next, inner + outer)


def run_spans(x_rows, b_rows, c_rows, log_rows, seg_rows, seg_first, state):
    count = x_rows.shape[0] // SPAN
    heads_here = log_rows.shape[0]
    x_blocks = x_rows.reshape(count, SPAN, heads_here, -1)
    b_blocks = b_rows.reshape(count, SPAN, -1)
    c_blocks = c_rows.reshape(count, SPAN, -1)
    log_blocks = log_rows.reshape(heads_here, count, SPAN).transpose(1, 0, 2)
    seg_blocks = seg_rows.reshape(count, SPAN)
    seg_befores = jnp.concatenate([jnp.reshape(seg_first, (1,)), seg_blocks[:-1, -1]])
    state, outputs = lax.scan(
        span_step, state, (x_blocks, b_blocks, c_blocks, log_blocks, seg_blocks, seg_befores)
    )
    return (state, outputs.reshape(count * SPAN, heads_here, -1))


def gate_rows(ssd_out, z_rows, norm_gain):
    square_mean = jnp.mean(ssd_out * ssd_out, axis=-1, keepdims=True)
    normed = (ssd_out * lax.rsqrt(square_mean + 1e-05)).reshape(ssd_out.shape[0], -1)
    z_float = z_rows.astype(jnp.float32)
    return (normed * norm_gain[None, :] * z_float * jax.nn.sigmoid(z_float)).astype(jnp.bfloat16)


def conv_rows(extended, seg_extended, seg_rows, conv_weight):
    frame_count = seg_rows.shape[0]
    summed = jnp.zeros((frame_count, extended.shape[1]), jnp.float32)
    for offset in range(conv_weight.shape[0]):
        same = (seg_extended[offset : offset + frame_count] == seg_rows).astype(jnp.float32)
        summed = (
            summed
            + conv_weight[offset][None, :]
            * extended[offset : offset + frame_count].astype(jnp.float32)
            * same[:, None]
        )
    return (summed * jax.nn.sigmoid(summed)).astype(jnp.bfloat16)


def local(
    frames,
    x_weight,
    z_weight,
    bc_weight,
    log_decay,
    norm_gain,
    conv_weight,
    out_weight,
    record_lengths,
):
    frame_count = frames.shape[0]
    state_width = bc_weight.shape[1] // 2
    share = bc_weight.shape[1] // lax.axis_size("head")
    bc_share = lax.dynamic_slice_in_dim(bc_weight, lax.axis_index("head") * share, share, 1)
    pieces = (
        lax.all_gather(x_weight, "tm", axis=0, tiled=True),
        lax.all_gather(z_weight, "tm", axis=0, tiled=True),
        lax.all_gather(bc_share, "tm", axis=0, tiled=True),
    )
    x_sum, z_sum, bc_sum = tuple(
        (jnp.dot(frames, weight_rows, preferred_element_type=jnp.float32) for weight_rows in pieces)
    )
    bc_rows = lax.all_gather(bc_sum.astype(jnp.bfloat16), "head", axis=1, tiled=True)
    x_rows = x_sum.astype(jnp.bfloat16)
    z_rows = z_sum.astype(jnp.bfloat16)
    dev_start = lax.axis_index("tm") * frame_count
    positions = dev_start + jnp.arange(frame_count, dtype=jnp.int32)
    seg_rows = segment_ids(record_lengths, positions)
    seg_before_dev = segment_ids(record_lengths, jnp.reshape(dev_start - 1, (1,)))[0]
    seg_first = jnp.where(dev_start == 0, -1, seg_before_dev)
    heads_here = log_decay.shape[0]
    head_size = x_weight.shape[1] // heads_here
    empty_state = jnp.zeros((heads_here, state_width, head_size), jnp.float32)
    local_state, local_out = run_spans(
        x_rows,
        bc_rows[:, :state_width],
        bc_rows[:, state_width:],
        log_decay,
        seg_rows,
        seg_first,
        empty_state,
    )
    same_first = (seg_rows == seg_first).astype(jnp.float32)
    through = jnp.exp(jnp.sum(log_decay, axis=1)) * same_first[-1]
    all_keep, all_summaries = (
        lax.all_gather(through[None], "tm", axis=0, tiled=True),
        lax.all_gather(local_state[None], "tm", axis=0, tiled=True),
    )
    dev_index = lax.axis_index("tm")

    def absorb(position, carry_state):
        updated = all_keep[position][:, None, None] * carry_state + all_summaries[position]
        return jnp.where(position < dev_index, updated, carry_state)

    entry_state = lax.fori_loop(0, all_keep.shape[0], absorb, empty_state)
    growth = jnp.exp(jnp.cumsum(log_decay, axis=1)) * same_first[None, :]
    carried = (
        jnp.einsum(
            "tn,hnp->thp",
            bc_rows[:, state_width:].astype(jnp.float32),
            entry_state,
            precision=highest,
        )
        * growth.T[:, :, None]
    )
    ssd_out = local_out + carried
    gated = gate_rows(ssd_out, z_rows, norm_gain)
    half_width = (conv_weight.shape[0] - 1) // 2
    extended = extended_2(gated, (("tm", 0),), half_width)
    seg_extended = segment_ids(
        record_lengths,
        dev_start - half_width + jnp.arange(frame_count + 2 * half_width, dtype=jnp.int32),
    )
    act_rows = conv_rows(extended, seg_extended, seg_rows, conv_weight)
    partial_terms = jnp.dot(
        act_rows,
        lax.all_gather(out_weight, "tm", axis=1, tiled=True),
        preferred_element_type=jnp.float32,
    )
    return lax.psum_scatter(
        partial_terms.astype(jnp.bfloat16), "head", scatter_dimension=1, tiled=True
    )


def solution(mesh):
    in_specs = (
        P("tm", None),
        P("tm", "head"),
        P("tm", "head"),
        P("tm", None),
        P("head", "tm"),
        P("head"),
        P(None, "head"),
        P("head", "tm"),
        P(),
    )
    out_specs = P("tm", "head")
    return jax.shard_map(local, mesh=mesh, in_specs=in_specs, out_specs=out_specs, check_vma=False)
```

profile of v0, /device:TPU:0, one launch (start us, length us, event | category | flops | bytes accessed | tf_op | source)
XLA Modules:
  0.0 369.6 jit_solution(12098244770121501476)
XLA Ops:
  6.5 0.7 all-gather.7.cloned.1.call-update
  7.3 0.8 reduce-window.10
  8.8 0.7 constant_dynamic-slice_fusion.3
  9.6 44.3 %all_gather.21 = bf16[1024,128]{1,0:T(8,128)(2,1)S(1)} all-gather(bf16[64,128]{1,0:T(8,128)(2,1)S(1)} %constant_dynamic-slice_fusion.3), channel_id=1, replica_groups=mesh['tm'=16,'head'=2] {'tm'}, dimensions={0}, use_global_device_ids=true | all-gather | bytes 278528 | tf_op jit(solution)/shard_map/all_gather | solution.py:108
  54.2 1.9 all_gather.22
  56.3 0.7 reshape.216
  58.9 15.2 %all-gather.7.cloned.1.call-done = bf16[1024,1024]{1,0:T(8,128)(2,1)} async-done(((bf16[64,1024]{1,0:T(8,128)(2,1)}), bf16[1024,1024]{1,0:T(8,128)(2,1)}) %all-gather.7.cloned.1.call-update) | async-done | bytes 2097168 | tf_op jit(solution)/shard_map/all_gather | solution.py:106
  74.1 2.3 convolution_convert_fusion.2
  77.0 0.9 copy.45
  77.9 32.6 %while.27 = (s32[]{:T(128)}, f32[16,128,64]{1,2,0:T(8,128)S(1)}, f32[2,128,16,64]{1,0,3,2:T(2,128)}, f32[2,16,128]{2,0,1:T(2,128)S(1)}, s32[2,128]{1,0:T(2,128)S...) while((s32[]{:T(128)}, f32[16,128,64]{1,2,0:T(8,128)S(1)}, ...), condition=%wide.region_5.6_spmd.clone, body=%wide.region_3.5_spmd.clone.sunk | while | flops 610210304 | bytes 14678067 | solution.py:63
  81.5 1.3 fusion.116
  82.8 10.3 %dynamic_update_slice.6 = f32[2,128,16,64]{1,0,3,2:T(2,128)S(1)} dynamic-update-slice(f32[2,128,16,64]{1,0,3,2:T(2,128)S(1)} %copy-done.3, f32[1,128,16,64]{1,0,3,2:T(1,128)S(1)} %bitcast.159, s32[]{:T(128)} %get-tuple-element.451, s32[]{:T(128)} %constant.73.clone.1..sunk, s32[]{:T(128)} %constant.73.clone.1..sunk, s32[]{:T(128)} %constant.73.clone.1..sunk) | dynamic-update-slice | bytes 1048580 | tf_op jit(solution)/shard_map/while/body/jit(dynamic_update_index_in_dim)/dynamic_update_slice | solution.py:63
  93.4 0.8 convolution_add_fusion.2
  97.8 1.3 fusion.116
  99.1 10.3 %dynamic_update_slice.6 = f32[2,128,16,64]{1,0,3,2:T(2,128)S(1)} dynamic-update-slice(f32[2,128,16,64]{1,0,3,2:T(2,128)S(1)} %copy-done.3, f32[1,128,16,64]{1,0,3,2:T(1,128)S(1)} %bitcast.159, s32[]{:T(128)} %get-tuple-element.451, s32[]{:T(128)} %constant.73.clone.1..sunk, s32[]{:T(128)} %constant.73.clone.1..sunk, s32[]{:T(128)} %constant.73.clone.1..sunk) | dynamic-update-slice | bytes 1048580 | tf_op jit(solution)/shard_map/while/body/jit(dynamic_update_index_in_dim)/dynamic_update_slice | solution.py:63
  109.7 0.8 convolution_add_fusion.2
  110.5 0.8 copy-done.1
  111.4 0.7 all-gather.9.cloned.1.call-update
  112.9 1.4 fusion.75
  114.3 1.1 fusion.76
  118.0 40.4 %all-reduce = f32[256]{0:T(256)S(1)} all-reduce(f32[256]{0:T(256)S(1)} %multiply_dynamic-update-slice_fusion), channel_id=2, replica_groups=mesh['tm'=16,'head'=2] {'tm'}, use_global_device_ids=true, to_apply=%add | all-reduce | flops 256 | bytes 2048
  159.3 3.0 reshape.223
  162.4 61.1 %all-gather.13.cloned.1.call-done = f32[256,128,64]{1,2,0:T(8,128)} async-done(((f32[16,128,64]{1,2,0:T(8,128)}), f32[256,128,64]{1,2,0:T(8,128)}) %all-gather.13.cloned.1.call-update) | async-done | bytes 8388624 | tf_op jit(solution)/shard_map/all_gather | solution.py:137
  223.5 27.5 %while.28 = (s32[]{:T(128)}, f32[16,128,64]{2,1,0:T(8,128)S(1)}, s32[]{:T(128)}, f32[16,16]{1,0:T(8,128)S(1)}, f32[16,16,128,64]{2,3,1,0:T(8,128)}, /*index=5*/s32[]{:T(128)}, s32[]{:T(128)}) while((s32[]{:T(128)}, f32[16,128,64]{2,1,0:T(8,128)S(1)}, s32[]{:T(128)}, f32[16,16]{1,0:T(8,128)S(1)}, f32[16,16,128,64]{2,3,1,0:T(8,128)}, ...), condition=%wide.region_8.9_spmd.clone, body=%wide.region_7.8_spmd.clone.sunk | while | flops 524292 | bytes 3670313 | solution.py:145
  223.5 1.1 constant_dynamic-slice_fusion.8
  225.2 1.1 constant_dynamic-slice_fusion.8
  226.9 1.1 constant_dynamic-slice_fusion.8
  228.6 1.1 constant_dynamic-slice_fusion.8
  230.3 1.1 constant_dynamic-slice_fusion.8
  232.0 1.1 constant_dynamic-slice_fusion.8
  233.8 1.1 constant_dynamic-slice_fusion.8
  235.5 1.1 constant_dynamic-slice_fusion.8
  237.2 1.1 constant_dynamic-slice_fusion.8
  238.9 1.1 constant_dynamic-slice_fusion.8
  240.6 1.1 constant_dynamic-slice_fusion.8
  242.3 1.1 constant_dynamic-slice_fusion.8
  244.0 1.1 constant_dynamic-slice_fusion.8
  245.8 1.1 constant_dynamic-slice_fusion.8
  247.5 1.1 constant_dynamic-slice_fusion.8
  249.2 1.1 constant_dynamic-slice_fusion.8
  251.2 0.9 copy-done.2
  253.3 31.8 %all-gather.9.cloned.1.call-done = bf16[1024,1024]{1,0:T(8,128)(2,1)} async-done(((bf16[64,1024]{1,0:T(8,128)(2,1)}), bf16[1024,1024]{1,0:T(8,128)(2,1)}) %all-gather.9.cloned.1.call-update) | async-done | bytes 2097168 | tf_op jit(solution)/shard_map/all_gather | solution.py:107
  285.2 2.4 fusion.36
  287.6 3.2 collective-permute-start
  290.8 1.5 collective-permute-start.1
  292.4 54.8 %all-gather.11.cloned.1.call-done = bf16[1024,1024]{0,1:T(8,128)(2,1)} async-done(((bf16[1024,64]{0,1:T(8,128)(2,1)}), bf16[1024,1024]{0,1:T(8,128)(2,1)}) %all-gather.11.cloned.1.call-update) | async-done | bytes 2097168 | tf_op jit(solution)/shard_map/all_gather | solution.py:167
  347.2 9.1 %convolution_convert_fusion = bf16[256,1024]{1,0:T(8,128)(2,1)} fusion(bf16[1024,1024]{0,1:T(8,128)(2,1)} %all-gather.11.cloned.1.call-done, bf16[256,1024]{1,0:T(8,128)(2,1)S(1)} %fusion.36, bf16[15,1024]{1,0:T(8,128)(2,1)S(1)} %collective-permute-done.1, bf16[15,1024]{1,0:T(8,128)(2,1)S(1)} %collective-permute-done, f32[256]{0:T(256)S(1)} %get-tuple-element.312, ...), kind=kOutput, calls=%fused_computation.80 | convolution fusion | flops 594280448 | bytes 3365888 | tf_op jit(solution)/shard_map/dot_general | solution.py:165
  356.3 6.8 %reduce-scatter.2.cloned.1.call-done = bf16[256,512]{1,0:T(8,128)(2,1)} async-done(((bf16[256,1024]{1,0:T(8,128)(2,1)}), bf16[256,512]{1,0:T(8,128)(2,1)}) %reduce-scatter.2.cloned.1.call-update) | async-done | bytes 262160 | tf_op jit(solution)/shard_map/reduce_scatter | solution.py:170
  (139 shorter events, 25.4 us)
Async XLA Ops:
  6.5 47.3 %copy-start = (bf16[256,1024]{1,0:T(8,128)(2,1)S(1)}, bf16[256,1024]{1,0:T(8,128)(2,1)}, u32[]{:S(2)}) copy-start(bf16[256,1024]{1,0:T(8,128)(2,1)} %param.13) | copy-start | bytes 1572868
  6.5 67.5 %all-gather.7.cloned.1.call-start = ((), (), s32[]{:S(2)}) async-start(), calls=%async_computation.1 | async-start | bytes 2228224 | tf_op jit(solution)/shard_map/all_gather | solution.py:106
  7.3 216.2 %all-gather.13.cloned.1.call-start = ((), (), s32[]{:S(2)}) async-start(), calls=%async_computation.5 | async-start | bytes 8912896 | tf_op jit(solution)/shard_map/all_gather | solution.py:137
  77.9 34.9 %copy-start.5 = (f32[16,256]{1,0:T(8,128)S(1)}, f32[16,256]{1,0:T(8,128)}, u32[]{:S(2)}) copy-start(f32[16,256]{1,0:T(8,128)} %param.17) | copy-start | bytes 49156
  77.9 38.3 %copy-start.7 = (u32[32]{0:T(128)S(1)}, u32[32]{0:T(128)}, u32[]{:S(2)}) copy-start(u32[32]{0:T(128)} %constant.86) | copy-start | bytes 388
  77.9 4.9 %copy-start.3 = (f32[2,128,16,64]{1,0,3,2:T(2,128)S(1)}, f32[2,128,16,64]{1,0,3,2:T(2,128)}, u32[]{:S(2)}) copy-start(f32[2,128,16,64]{1,0,3,2:T(2,128)} %get-tuple-element.453) | copy-start | bytes 3145732 | tf_op jit(solution)/shard_map/while
  93.2 1.1 copy-start.4
  94.2 4.9 %copy-start.3 = (f32[2,128,16,64]{1,0,3,2:T(2,128)S(1)}, f32[2,128,16,64]{1,0,3,2:T(2,128)}, u32[]{:S(2)}) copy-start(f32[2,128,16,64]{1,0,3,2:T(2,128)} %get-tuple-element.453) | copy-start | bytes 3145732 | tf_op jit(solution)/shard_map/while
  109.5 1.1 copy-start.4
  110.5 0.8 copy-start.1
  111.4 173.8 %all-gather.9.cloned.1.call-start = ((), (), s32[]{:S(2)}) async-start(), calls=%async_computation.2 | async-start | bytes 2228224 | tf_op jit(solution)/shard_map/all_gather | solution.py:107
  112.1 235.1 %all-gather.11.cloned.1.call-start = ((), (), s32[]{:S(2)}) async-start(), calls=%async_computation.3 | async-start | bytes 2228224 | tf_op jit(solution)/shard_map/all_gather | solution.py:167
  112.7 250.4 %reduce-scatter.2.cloned.1.call-start = ((), (), s32[]{:S(2)}) async-start(), calls=%async_computation.4 | async-start | bytes 786432 | tf_op jit(solution)/shard_map/reduce_scatter | solution.py:170
  250.9 1.2 copy-start.2
  252.8 32.4 %copy-start.6 = (f32[1024]{0:T(1024)S(1)}, f32[1024]{0:T(1024)}, u32[]{:S(2)}) copy-start(f32[1024]{0:T(1024)} %param.18) | copy-start | bytes 12292
  287.6 59.6 %collective-permute-start = (bf16[15,1024]{1,0:T(8,128)(2,1)S(1)}, bf16[15,1024]{1,0:T(8,128)(2,1)S(1)}, u32[]{:S(2)}, u32[]{:S(2)}) collective-permute-start(bf16[15,1024]{1,0:T(8,128)(2,1)S(1)} %get-tuple-element.276), channel_id=1, source_target_pairs={{0,2},{2,4},{4,6},{6,8},{8,10},{10,12},{12,14},{14,16},{16,18},{18... | collective-permute-start | bytes 92168 | tf_op jit(solution)/shard_map/ppermute | solution.py:19
  290.8 56.4 %collective-permute-start.1 = (bf16[15,1024]{1,0:T(8,128)(2,1)S(1)}, bf16[15,1024]{1,0:T(8,128)(2,1)S(1)}, u32[]{:S(2)}, u32[]{:S(2)}) collective-permute-start(bf16[15,1024]{1,0:T(8,128)(2,1)S(1)} %get-tuple-element.277), channel_id=1, source_target_pairs={{2,0},{4,2},{6,4},{8,6},{10,8},{12,10},{14,12},{16,14},{18,16},{20... | collective-permute-start | bytes 92168 | tf_op jit(solution)/shard_map/ppermute | solution.py:20
Sparse Core Ops, SparseCore 0:
  10.1 63.8 all-gather.6
  111.5 111.8 all-gather.12
  226.2 58.8 all-gather.8
  287.8 59.3 all-gather.10
  356.4 6.5 reduce-scatter.1
where the time goes:
time: 371 us; the launch traced here: 370 us
  waiting for transfers between devices  172 us (46%)
  blocking collectives  86.6 us (23%)
  local copies, waits for them, and re-layouts  59.9 us (16%)
  matrix products  20 us (5%)
  between operations  14.5 us (4%)
  other arithmetic  11.3 us (3%)
  starting transfers between devices  4.81 us (1%)
    all_gather x1, waiting for transfers between devices, local(): lax.all_gather(local_state[None], 'tm', axis=0, tiled=True)  61.1 us
    all_gather x1, waiting for transfers between devices, local(): lax.all_gather(out_weight, 'tm', axis=1, tiled=True)  54.8 us
    all_gather x1, blocking collectives, local(): lax.all_gather(bc_share, 'tm', axis=0, tiled=True)  44.3 us
    unnamed x1, blocking collectives  40.4 us
    all_gather x1, waiting for transfers between devices, local(): lax.all_gather(z_weight, 'tm', axis=0, tiled=True)  31.8 us
    dynamic_slice x32, local copies, waits for them, and re-layouts, absorb(): all_summaries[position]  22.7 us
    dynamic_update_slice x2, local copies, waits for them, and re-layouts, run_spans(): lax.scan(span_step, state, (x_blocks, b_blocks, c_blocks, log_blocks, seg...  20.7 us
    all_gather x1, waiting for transfers between devices, local(): lax.all_gather(x_weight, 'tm', axis=0, tiled=True)  15.2 us
  transfers between devices with their start and end apart: 7, of which 5 were waited for; matrix products, arithmetic and copies ran while one was open for 12% of the time, Pallas kernels for 0%

commit v1 on v0

v1 whole, which is shorter than its diff:
```python
import functools

import jax
import jax.numpy as jnp
from jax import lax
from jax.experimental import pallas as pl
from jax.experimental.pallas import tpu as pltpu
from jax.sharding import PartitionSpec as P

SPAN = 128
LANES = 128
EDGE = 16
BF16 = jnp.bfloat16
F32 = jnp.float32
VMEM_BYTES = 48 * 1024 * 1024


def dot(a, b, dims=((1,), (0,)), precision=None):
    return lax.dot_general(a, b, (dims, ((), ())), precision=precision, preferred_element_type=F32)


def call(kernel, out_shape, operands, scratch=(), flops=0, smem=1):
    in_specs = [pl.BlockSpec(memory_space=pltpu.SMEM)] * smem
    in_specs += [pl.BlockSpec(memory_space=pltpu.VMEM)] * (len(operands) - smem)
    moved = sum(a.size * a.dtype.itemsize for a in operands)
    moved += sum(a.size * a.dtype.itemsize for a in jax.tree.leaves(out_shape))
    return pl.pallas_call(
        kernel,
        out_shape=out_shape,
        in_specs=in_specs,
        out_specs=jax.tree.map(lambda _: pl.BlockSpec(memory_space=pltpu.VMEM), out_shape),
        scratch_shapes=list(scratch),
        compiler_params=pltpu.CompilerParams(vmem_limit_bytes=VMEM_BYTES),
        cost_estimate=pl.CostEstimate(flops=flops, bytes_accessed=moved, transcendentals=0),
    )(*operands)


def plane_place(group):
    index = lax.axis_index("tm")
    return lax.rem(index, group), lax.div(index, group)


def record_starts(len_ref, position):
    start = jnp.zeros_like(position)
    end = jnp.int32(0)
    for record in range(len_ref.shape[0] - 1):
        end = end + len_ref[record]
        start = jnp.where(position >= end, end, start)
    return start


def spread(columns, first, heads, head_of_lane, shape):
    out = jnp.broadcast_to(columns[:, first : first + 1], shape)
    for head in range(1, heads):
        column = jnp.broadcast_to(columns[:, first + head : first + head + 1], shape)
        out = jnp.where(head_of_lane == head, column, out)
    return out


def ssd_kernel(group, heads, state, len_ref, decay_ref, weight_ref, *refs):
    frame_refs = refs[:group]
    c_ref, y_ref, step_ref, carry_ref, keep_ref, send_ref, x_ref, b_ref = refs[group:]
    place, plane = plane_place(group)
    frames = frame_refs[0].shape[0]
    total, width = x_ref.shape
    head_size = width // heads
    count = total // SPAN
    base = plane * total
    for step in range(group):
        rows = pl.ds(pl.multiple_of((place ^ step) * frames, frames), frames)
        product = dot(frame_refs[step][...], weight_ref[...])
        x_ref[rows, :] = product[:, :width].astype(BF16)
        b_ref[rows, :] = product[:, width : width + state].astype(BF16)
        c_ref[rows, :] = product[:, width + state :].astype(BF16)

    decay = decay_ref[...]
    used = decay.shape[0]
    square = (SPAN, SPAN)
    row, lane = (lax.broadcasted_iota(jnp.int32, square, dim) for dim in (0, 1))
    upper = jnp.where(row <= lane, 1.0, 0.0).astype(F32)
    cumul = dot(decay, upper, precision=lax.Precision.HIGHEST)
    whole = dot(decay, jnp.ones(square, F32), precision=lax.Precision.HIGHEST)
    first = base + lax.div(row[:used], heads) * SPAN
    position = first + lane[:used]
    start = record_starts(len_ref, position)
    start_last = record_starts(len_ref, first + (SPAN - 1))
    carried = jnp.where(start < first, jnp.exp(cumul), 0.0)
    tail = jnp.where(position >= start_last, jnp.exp(whole - cumul), 0.0)
    keep = jnp.where(start_last < first, jnp.exp(whole), 0.0)
    parts = [cumul, carried, tail, start.astype(F32)]
    if 4 * used < SPAN:
        parts.append(jnp.zeros((SPAN - 4 * used, SPAN), F32))
    columns = jnp.concatenate(parts, axis=0).T

    head_of_lane = lax.broadcasted_iota(jnp.int32, (SPAN, width), 1) // head_size
    tile_heads = LANES // head_size
    tile_lane = lax.broadcasted_iota(jnp.int32, (1, LANES), 1) // head_size
    lower = row >= lane
    entry = jnp.zeros((state, width), F32)
    through = jnp.ones((1, width), F32)
    for block in range(count):
        rows = slice(block * SPAN, (block + 1) * SPAN)
        at = block * heads
        x, b, c = x_ref[rows, :], b_ref[rows, :], c_ref[rows, :]
        scores = dot(c, b, ((1,), (1,)))
        here = (base + block * SPAN + lane).astype(F32)
        start_here = jnp.broadcast_to(columns[:, 3 * used + at : 3 * used + at + 1], square)
        joined = lower & (here >= start_here)
        keep_lanes = []
        for tile in range(width // LANES):
            mixes, values = [], []
            kept = jnp.zeros((1, LANES), F32)
            for inner in range(tile_heads):
                which = at + tile * tile_heads + inner
                gap = jnp.broadcast_to(columns[:, which : which + 1], square) - cumul[which : which + 1, :]
                mixes.append((jnp.exp(jnp.where(joined, gap, -1e30)) * scores).astype(BF16))
                mask = jnp.where(tile_lane == inner, 1.0, 0.0)
                values.append(x[:, tile * LANES : (tile + 1) * LANES] * mask.astype(BF16))
                kept = kept + mask * keep[which : which + 1, :]
            keep_lanes.append(kept)
            y_ref[rows, tile * LANES : (tile + 1) * LANES] = dot(
                jnp.concatenate(mixes, axis=1), jnp.concatenate(values, axis=0)
            )
        kept = jnp.concatenate(keep_lanes, axis=1)
        carry_ref[rows, :] = spread(columns, used + at, heads, head_of_lane, (SPAN, width))
        weighed = x.astype(F32) * spread(columns, 2 * used + at, heads, head_of_lane, (SPAN, width))
        step = dot(b, weighed.astype(BF16), ((0,), (0,)))
        step_ref[block * state : (block + 1) * state, :] = step
        keep_ref[block * 8 : (block + 1) * 8, :] = jnp.broadcast_to(kept, (8, width))
        entry = kept * entry + step
        through = through * kept
    send_ref[:state, :] = entry.astype(BF16)
    send_ref[state:, :] = jnp.broadcast_to(through, (EDGE, width)).astype(BF16)


def silu_kernel(group, gain_ref, weight_ref, *refs):
    frame_refs, out_ref = refs[:group], refs[group]
    place, _ = plane_place(group)
    frames = frame_refs[0].shape[0]
    width = weight_ref.shape[1]
    gain = gain_ref[:, pl.ds(pl.multiple_of(place * width, LANES), width)]
    for step in range(group):
        rows = pl.ds(pl.multiple_of((place ^ step) * frames, frames), frames)
        z = dot(frame_refs[step][...], weight_ref[...]).astype(BF16).astype(F32)
        out_ref[rows, :] = z / (1.0 + jnp.exp(-z)) * gain


def gate_kernel(heads, state, c_ref, y_ref, step_ref, carry_ref, keep_ref, silu_ref, *refs):
    earlier, (gated_ref, top_ref, bottom_ref) = refs[:-3], refs[-3:]
    total, width = y_ref.shape
    head_size = width // heads
    entry = jnp.zeros((state, width), F32)
    for summary in reversed(earlier):
        through = summary[state : state + EDGE, :].astype(F32)[:1]
        entry = through * entry + summary[:state, :].astype(F32)
    owner = [lax.broadcasted_iota(jnp.int32, (width, width), dim) // head_size for dim in (0, 1)]
    average = jnp.where(owner[0] == owner[1], 1.0 / head_size, 0.0).astype(BF16)
    for block in range(total // SPAN):
        rows = slice(block * SPAN, (block + 1) * SPAN)
        y = y_ref[rows, :] + carry_ref[rows, :] * dot(c_ref[rows, :], entry.astype(BF16))
        square_mean = dot((y * y).astype(BF16), average)
        gated_ref[rows, :] = (y * lax.rsqrt(square_mean + 1e-05) * silu_ref[rows, :]).astype(BF16)
        entry = keep_ref[block * 8 : block * 8 + 1, :] * entry + step_ref[block * state : (block + 1) * state, :]
    top_ref[...] = gated_ref[:EDGE, :]
    bottom_ref[...] = gated_ref[total - EDGE :, :]


def conv_kernel(group, len_ref, taps_ref, before_ref, gated_ref, after_ref, act_ref, ext_ref, ends_ref):
    place, plane = plane_place(group)
    total, width = gated_ref.shape
    taps = taps_ref.shape[0]
    half = (taps - 1) // 2
    base = plane * total
    stream = lax.axis_size("tm") // group * total
    records = len_ref.shape[0]
    ext_ref[:EDGE, :] = before_ref[...].astype(F32)
    ext_ref[EDGE : EDGE + total, :] = gated_ref[...].astype(F32)
    ext_ref[EDGE + total :, :] = after_ref[...].astype(F32)
    ends_ref[0] = 0
    for record in range(records):
        ends_ref[record + 1] = ends_ref[record] + len_ref[record]

    def record_at(position):
        found = jnp.int32(0)
        for record in range(records - 1):
            found = found + (ends_ref[record + 1] <= position).astype(jnp.int32)
        return found

    reach = SPAN + 2 * EDGE
    first_tap = EDGE - half

    def one_block(block, _):
        offset = pl.multiple_of(block * SPAN, SPAN)
        low = record_at(jnp.maximum(base + offset - half, 0))
        high = record_at(jnp.minimum(base + offset + SPAN - 1 + half, stream - 1))
        near = lax.broadcasted_iota(jnp.int32, (reach, LANES), 0) + (base + offset - EDGE)
        for tile in range(width // LANES):
            lanes = slice(tile * LANES, (tile + 1) * LANES)
            weights = taps_ref[:, pl.ds(pl.multiple_of(place * width + tile * LANES, LANES), LANES)]

            def one_record(record, done):
                inside = (near >= ends_ref[record]) & (near < ends_ref[record + 1])
                g = jnp.where(inside, ext_ref[pl.ds(offset, reach), lanes], 0.0)
                out = None
                for phase in range(8):
                    part = None
                    for at in range(phase, reach - SPAN, 8):
                        tap = at - first_tap
                        if 0 <= tap < taps:
                            aligned = at - phase
                            term = weights[tap : tap + 1, :] * g[aligned : aligned + SPAN + 8, :]
                            part = term if part is None else part + term
                    if part is not None:
                        moved = part[phase : phase + SPAN, :]
                        out = moved if out is None else out + moved
                return jnp.where(inside[EDGE : EDGE + SPAN], out, done)

            conv = lax.fori_loop(low, high + 1, one_record, jnp.zeros((SPAN, LANES), F32))
            act_ref[pl.ds(offset, SPAN), lanes] = (conv / (1.0 + jnp.exp(-conv))).astype(BF16)
        return 0

    lax.fori_loop(0, total // SPAN, one_block, 0)


def out_kernel(group, cores, *refs):
    acts, weights, outs = refs[:cores], refs[cores : 2 * cores], refs[2 * cores :]
    place, _ = plane_place(group)
    frames = outs[0].shape[0]
    for step in reversed(range(group)):
        rows = pl.ds(pl.multiple_of((place ^ step) * frames, frames), frames)
        total = None
        for act, weight in zip(acts, weights):
            product = dot(act[rows, :], weight[...], ((1,), (1,)))
            total = product if total is None else total + product
        outs[step][...] = total.astype(outs[step].dtype)


def local(
    frames,
    x_weight,
    z_weight,
    bc_weight,
    log_decay,
    norm_gain,
    conv_weight,
    out_weight,
    record_lengths,
):
    times, cores = lax.axis_size("tm"), lax.axis_size("head")
    frame_count, depth = frames.shape
    heads_here, channels = log_decay.shape[0], x_weight.shape[1]
    state = bc_weight.shape[1] // 2
    group = 4
    while group > 1 and (channels // group % LANES or times % group or heads_here % group):
        group //= 2
    planes = times // group
    width, heads = channels // group, heads_here // group
    total = frame_count * group
    count = total // SPAN
    index, core = lax.axis_index("tm"), lax.axis_index("head")
    place = lax.rem(index, group)

    def in_plane(array, step):
        return lax.ppermute(array, "tm", [(i, i ^ step) for i in range(times)])

    def later(array, step):
        return lax.ppermute(array, "tm", [(i, i + step * group) for i in range(times - step * group)])

    def earlier(array, step):
        return lax.ppermute(array, "tm", [(i + step * group, i) for i in range(times - step * group)])

    def across(array, step):
        return lax.ppermute(array, "head", [(i, i ^ step) for i in range(cores)])

    def to_owners(blocks):
        whole = jnp.broadcast_to(blocks[None], (planes,) + blocks.shape)
        whole = whole.reshape((times,) + blocks.shape[1:])
        moved = lax.all_to_all(whole, "tm", split_axis=0, concat_axis=0, tiled=True)
        return moved.reshape(-1, moved.shape[-1])

    def columns(weight):
        return weight.reshape(weight.shape[0], group, width).transpose(1, 0, 2)

    shared = jnp.broadcast_to(bc_weight[None], (group,) + bc_weight.shape)
    xbc = to_owners(jnp.concatenate([columns(x_weight), shared], axis=2))
    frame_parts = [frames] + [in_plane(frames, step) for step in range(1, group)]
    decay_groups = [[plane * group + q for q in range(group)] for plane in range(planes)]
    decay = lax.all_to_all(
        log_decay.reshape(group, heads, frame_count),
        "tm",
        split_axis=0,
        concat_axis=0,
        axis_index_groups=decay_groups,
        tiled=True,
    )
    decay = decay.reshape(group, heads, -1, SPAN).transpose(0, 2, 1, 3).reshape(-1, SPAN)
    z_columns = to_owners(columns(z_weight))
    out_rows = to_owners(columns(out_weight.T))
    share = depth // cores
    out_parts = [lax.dynamic_slice_in_dim(out_rows, core * share, share, 0)]
    for step in range(1, cores):
        sent = lax.dynamic_slice_in_dim(out_rows, (core ^ step) * share, share, 0)
        out_parts.append(across(sent, step))

    shape = jax.ShapeDtypeStruct
    c_rows, y, steps, carry, keep, summary = call(
        functools.partial(ssd_kernel, group, heads, state),
        (
            shape((total, state), BF16),
            shape((total, width), F32),
            shape((count * state, width), F32),
            shape((total, width), F32),
            shape((count * 8, width), F32),
            shape((state + EDGE, width), BF16),
        ),
        [record_lengths, decay, xbc, *frame_parts],
        [pltpu.VMEM((total, width), BF16), pltpu.VMEM((total, state), BF16)],
        flops=2 * total * depth * (width + 2 * state),
    )
    summaries = [later(summary, step) for step in range(1, planes)]
    silu = call(
        functools.partial(silu_kernel, group),
        shape((total, width), F32),
        [norm_gain[None], z_columns, *frame_parts],
        flops=2 * total * depth * width,
        smem=0,
    )
    gated, top, bottom = call(
        functools.partial(gate_kernel, heads, state),
        (shape((total, width), BF16), shape((EDGE, width), BF16), shape((EDGE, width), BF16)),
        [c_rows, y, steps, carry, keep, silu, *summaries],
        flops=2 * total * state * width,
        smem=0,
    )
    before, after = later(bottom, 1), earlier(top, 1)
    act = call(
        functools.partial(conv_kernel, group),
        shape((total, width), BF16),
        [record_lengths, conv_weight, before, gated, after],
        [pltpu.VMEM((total + 2 * EDGE, width), F32), pltpu.SMEM((record_lengths.shape[0] + 1,), jnp.int32)],
        flops=2 * total * width * conv_weight.shape[0],
    )
    acts = [act] + [across(act, step) for step in range(1, cores)]
    outs = call(
        functools.partial(out_kernel, group, cores),
        tuple(shape((frame_count, share), BF16 if step else F32) for step in range(group)),
        [*acts, *out_parts],
        flops=2 * total * width * cores * share,
        smem=0,
    )
    mixed = outs[0]
    for step in range(1, group):
        mixed = mixed + in_plane(outs[step], step).astype(F32)
    return mixed.astype(BF16)


def solution(mesh):
    in_specs = (
        P("tm", None),
        P("tm", "head"),
        P("tm", "head"),
        P("tm", None),
        P("head", "tm"),
        P("head"),
        P(None, "head"),
        P("head", "tm"),
        P(),
    )
    out_specs = P("tm", "head")
    return jax.shard_map(local, mesh=mesh, in_specs=in_specs, out_specs=out_specs, check_vma=False)
```

time: 371 us -> 147 us (0.40)
  waiting for transfers between devices: 172 us -> 84.6 us
  blocking collectives: 86.6 us -> 0 us
  local copies, waits for them, and re-layouts: 59.9 us -> 6.84 us
  starting transfers between devices: 4.81 us -> 39.6 us
  matrix products: 20 us -> 0 us
  Pallas kernels: 0 us -> 15.6 us
  between operations: 14.5 us -> 0.26 us
  other arithmetic: 11.3 us -> 0.96 us
    all_gather x4 -> x0, waiting for transfers between devices: 163 us -> none  [the longest x1 61.1 us: local(): lax.all_gather(local_state[None], 'tm', axis=0, tiled=True)]
    all_gather x2 -> x0, blocking collectives: 46.2 us -> none  [the longest x1 44.3 us: local(): lax.all_gather(bc_share, 'tm', axis=0, tiled=True)]
    ppermute x2 -> x13, waiting for transfers between devices: 0.01 us -> 44.9 us  [the longest x6 36.9 us: in_plane(): return lax.ppermute(array, 'tm', [(i, i ^ step) for i in range(times)])]
    unnamed x1 -> x0, blocking collectives: 40.4 us -> none
    all_to_all x0 -> x4, waiting for transfers between devices: none -> 39.7 us  [the longest x3 36 us: to_owners(): moved = lax.all_to_all(whole, 'tm', split_axis=0, concat_axis=0, tiled=True)]
    dynamic_slice x37 -> x1, local copies, waits for them, and re-layouts: 24.6 us -> 0.04 us  [local(): sent = lax.dynamic_slice_in_dim(out_rows, (core ^ step) * share, share, 0)]
    dynamic_update_slice x2 -> x0, local copies, waits for them, and re-layouts: 20.7 us -> none  [run_spans(): lax.scan(span_step, state, (x_blocks, b_blocks, c_blocks, log_blocks, seg...]
    all_to_all x0 -> x4, starting transfers between devices: none -> 20.4 us  [the longest x3 15.2 us: to_owners(): moved = lax.all_to_all(whole, 'tm', split_axis=0, concat_axis=0, tiled=True)]
  transfers between devices with their start and end apart: 7 -> 17, of which waited for: 5 -> 11; matrix products, arithmetic and copies ran while one was open for 12% -> 1% of each run, Pallas kernels for 0% -> 10%
where the time goes in v1:
time: 147 us; the launch traced here: 148 us
  waiting for transfers between devices  84.6 us (58%)
  starting transfers between devices  39.6 us (27%)
  Pallas kernels  15.6 us (11%)
  local copies, waits for them, and re-layouts  6.84 us (5%)
    ppermute x6, waiting for transfers between devices, in_plane(): return lax.ppermute(array, 'tm', [(i, i ^ step) for i in range(times)])  36.9 us
    all_to_all x3, waiting for transfers between devices, to_owners(): moved = lax.all_to_all(whole, 'tm', split_axis=0, concat_axis=0, tiled=True)  36 us
    pallas_call x5, Pallas kernels, call(): pl.pallas_call(kernel, out_shape=out_shape, in_specs=in_specs, out_specs=...  15.6 us
    all_to_all x3, starting transfers between devices, to_owners(): moved = lax.all_to_all(whole, 'tm', split_axis=0, concat_axis=0, tiled=True)  15.2 us
    ppermute x4, starting transfers between devices, later(): lax.ppermute(array, 'tm', [(i, i + step * group) for i in range(times - s...  10.2 us
    ppermute x6, starting transfers between devices, in_plane(): return lax.ppermute(array, 'tm', [(i, i ^ step) for i in range(times)])  7.11 us
    ppermute x1, waiting for transfers between devices, earlier(): lax.ppermute(array, 'tm', [(i + step * group, i) for i in range(times - s...  5.34 us
    all_to_all x1, starting transfers between devices, local(): lax.all_to_all(log_decay.reshape(group, heads, frame_count), 'tm', split_...  5.16 us
  transfers between devices with their start and end apart: 17, of which 11 were waited for; matrix products, arithmetic and copies ran while one was open for 1% of the time, Pallas kernels for 10%

profile of v1, /device:TPU:0, one launch (start us, length us, event | category | flops | bytes accessed | tf_op | source)
XLA Modules:
  0.0 147.9 jit_solution(17199053347364209416)
XLA Ops:
  0.0 1.3 reshape.40
  1.3 5.2 %all-to-all-start = ((f32[4,4,256]{2,1,0:T(4,128)}), f32[4,4,256]{2,1,0:T(4,128)S(1)}, u32[]{:S(2)}, u32[]{:S(2)}) async-start(f32[4,4,256]{2,1,0:T(4,128)} %reshape.40), calls=%async_computation | async-start | bytes 32768 | tf_op jit(solution)/shard_map/all_to_all | solution.py:288
  6.5 1.0 reshape.46
  7.5 3.7 %all-to-all-done = f32[4,4,256]{2,1,0:T(4,128)S(1)} async-done(((f32[4,4,256]{2,1,0:T(4,128)}), f32[4,4,256]{2,1,0:T(4,128)S(1)}, u32[]{:S(2)}, u32[]{:S(2)}) %all-to-all-start) | async-done | bytes 16416 | tf_op jit(solution)/shard_map/all_to_all | solution.py:288
  11.2 0.9 broadcast_in_dim.13
  12.1 5.2 %all-to-all-start.2 = ((bf16[16,64,256]{2,1,0:T(8,128)(2,1)}), bf16[16,64,256]{2,1,0:T(8,128)(2,1)S(1)}, u32[]{:S(2)}, u32[]{:S(2)}) async-start(bf16[16,64,256]{2,1,0:T(8,128)(2,1)} %bitcast.8), calls=%async_computation.2 | async-start | bytes 1048576 | tf_op jit(solution)/shard_map/all_to_all | solution.py:278
  17.3 0.0 copy-start.7
  17.3 0.1 reshape.43
  17.3 0.7 copy-done.7
  18.1 0.1 pad_maximum_fusion
  18.2 13.0 %all-to-all-done.2 = bf16[16,64,256]{2,1,0:T(8,128)(2,1)S(1)} async-done(((bf16[16,64,256]{2,1,0:T(8,128)(2,1)}), bf16[16,64,256]{2,1,0:T(8,128)(2,1)S(1)}, u32[]{:S(2)}, u32[]{:S(2)}) %all-to-all-start.2) | async-done | bytes 524320 | tf_op jit(solution)/shard_map/all_to_all | solution.py:278
  31.2 1.1 broadcast_in_dim.11
  32.3 4.0 %all-to-all-start.1 = ((bf16[16,64,512]{2,1,0:T(8,128)(2,1)}), bf16[16,64,512]{2,1,0:T(8,128)(2,1)S(1)}, u32[]{:S(2)}, u32[]{:S(2)}) async-start(bf16[16,64,512]{2,1,0:T(8,128)(2,1)} %bitcast.4), calls=%async_computation.1 | async-start | bytes 2097152 | tf_op jit(solution)/shard_map/all_to_all | solution.py:278
  36.3 0.1 reshape.49
  36.4 23.0 %all-to-all-done.1 = bf16[16,64,512]{2,1,0:T(8,128)(2,1)S(1)} async-done(((bf16[16,64,512]{2,1,0:T(8,128)(2,1)}), bf16[16,64,512]{2,1,0:T(8,128)(2,1)S(1)}, u32[]{:S(2)}, u32[]{:S(2)}) %all-to-all-start.1) | async-done | bytes 1048608 | tf_op jit(solution)/shard_map/all_to_all | solution.py:278
  59.4 0.9 broadcast_in_dim.14
  60.3 6.1 %all-to-all-start.3 = ((bf16[16,64,256]{2,1,0:T(8,128)(2,1)}), bf16[16,64,256]{2,1,0:T(8,128)(2,1)S(1)}, u32[]{:S(2)}, u32[]{:S(2)}) async-start(bf16[16,64,256]{2,1,0:T(8,128)(2,1)} %bitcast.12), calls=%async_computation.3 | async-start | bytes 1048576 | tf_op jit(solution)/shard_map/all_to_all | solution.py:278
  66.4 2.0 %collective-permute-start = (bf16[256,1024]{1,0:T(8,128)(2,1)S(1)}, bf16[256,1024]{1,0:T(8,128)(2,1)S(1)}, u32[]{:S(2)}, u32[]{:S(2)}) collective-permute-start(bf16[256,1024]{1,0:T(8,128)(2,1)S(1)} %copy-done), channel_id=1, source_target_pairs={{0,2},{2,0},{4,6},{6,4},{8,10},{10,8},{12,14},{14,12},{16,18},{18,... | collective-permute-start | bytes 1572872 | tf_op jit(solution)/shard_map/ppermute | solution.py:264
  68.4 1.5 collective-permute-start.1
  69.9 0.1 collective-permute-start.2
  70.0 16.5 %collective-permute-done.refs_1_ = bf16[256,1024]{1,0:T(8,128)(2,1)S(1)} collective-permute-done((bf16[256,1024]{1,0:T(8,128)(2,1)S(1)}, bf16[256,1024]{1,0:T(8,128)(2,1)S(1)}, u32[]{:S(2)}, u32[]{:S(2)}) %collective-permute-start) | collective-permute-done | bytes 524320 | tf_op jit(solution)/shard_map/ppermute | solution.py:264
  86.5 0.2 collective-permute-done.1.refs_2_
  86.7 9.4 %collective-permute-done.2.refs_3_ = bf16[256,1024]{1,0:T(8,128)(2,1)S(1)} collective-permute-done((bf16[256,1024]{1,0:T(8,128)(2,1)S(1)}, bf16[256,1024]{1,0:T(8,128)(2,1)S(1)}, u32[]{:S(2)}, u32[]{:S(2)}) %collective-permute-start.2) | collective-permute-done | bytes 524320 | tf_op jit(solution)/shard_map/ppermute | solution.py:264
  96.1 0.7 copy-done.3
  96.7 5.3 %shard_map.91 = (bf16[1024,128]{1,0:T(8,128)(2,1)S(1)}, f32[1024,256]{1,0:T(8,128)S(1)}, f32[1024,256]{1,0:T(8,128)S(1)}, f32[1024,256]{1,0:T(8,128)S(1)}, f32[6...) custom-call(s32[8]{0:T(128)S(1)} %copy-done.3, f32[32,128]{1,0:T(8,128)S(1)} %bitcast.17, bf16[1024,512]{1,0:T(8,128)(2,1)} %bitcast.20, ...), custom_call_target="tpu_custom_call" | custom-call | flops 1073741824 | bytes 6709280 | tf_op jit(solution)/shard_map/pallas_call | solution.py:27
  102.1 0.0 copy-start.2
  102.1 3.4 %collective-permute-start.3 = (bf16[144,256]{1,0:T(8,128)(2,1)S(1)}, bf16[144,256]{1,0:T(8,128)(2,1)S(1)}, u32[]{:S(2)}, u32[]{:S(2)}) collective-permute-start(bf16[144,256]{1,0:T(8,128)(2,1)S(1)} %get-tuple-element.23), channel_id=1, source_target_pairs={{0,8},{2,10},{4,12},{6,14},{8,16},{10,18},{12,20},{14,22},{16,24},... | collective-permute-start | bytes 221192 | tf_op jit(solution)/shard_map/ppermute | solution.py:267
  105.5 4.3 %collective-permute-start.4 = (bf16[144,256]{1,0:T(8,128)(2,1)S(1)}, bf16[144,256]{1,0:T(8,128)(2,1)S(1)}, u32[]{:S(2)}, u32[]{:S(2)}) collective-permute-start(bf16[144,256]{1,0:T(8,128)(2,1)S(1)} %get-tuple-element.23), channel_id=1, source_target_pairs={{0,16},{2,18},{4,20},{6,22},{8,24},{10,26},{12,28},{14,30},{1,17},... | collective-permute-start | bytes 221192 | tf_op jit(solution)/shard_map/ppermute | solution.py:267
  109.8 1.3 collective-permute-start.5
  111.1 1.0 shard_map.92.silu_ref
  112.0 0.0 collective-permute-done.3.refs_0_
  112.1 1.0 collective-permute-done.5.refs_2_
  113.0 0.6 shard_map.93
  113.6 1.3 collective-permute-start.6
  114.9 1.3 collective-permute-start.7
  116.2 0.0 collective-permute-done.6.before_ref
  116.3 5.3 %collective-permute-done.7.after_ref = bf16[16,256]{1,0:T(8,128)(2,1)S(1)} collective-permute-done((bf16[16,256]{1,0:T(8,128)(2,1)S(1)}, bf16[16,256]{1,0:T(8,128)(2,1)S(1)}, u32[]{:S(2)}, u32[]{:S(2)}) %collective-permute-start.7) | collective-permute-done | bytes 8224 | tf_op jit(solution)/shard_map/ppermute | solution.py:270
  121.6 7.9 %shard_map.94.refs_0_ = bf16[1024,256]{1,0:T(8,128)(2,1)S(1)} custom-call(s32[8]{0:T(128)S(1)} %copy-done.3, f32[31,1024]{1,0:T(8,128)S(1)} %copy-done.1, bf16[16,256]{1,0:T(8,128)(2,1)S(1)} %collective-permute-done.6.before_ref, bf16[1024,256]{1,0:T(8,128)(2,1)S(1)} %get-tuple-element.25.gated_ref, bf16[16,256]{1,0:T(8,128)(2,1)S(1)} %collective-permute-done.7.after_ref), custom_call_target="tpu_custom_call" | custom-call | flops 16252928 | bytes 1191968 | tf_op jit(solution)/shard_map/pallas_call | solution.py:27
  129.6 0.1 collective-permute-start.8
  129.7 0.5 collective-permute-start.9
  130.3 1.7 %collective-permute-done.9.refs_3_ = bf16[512,256]{1,0:T(8,128)(2,1)S(1)} collective-permute-done((bf16[512,256]{1,0:T(8,128)(2,1)S(1)}, bf16[512,256]{1,0:T(8,128)(2,1)S(1)}, u32[]{:S(2)}, u32[]{:S(2)}) %collective-permute-start.9) | collective-permute-done | bytes 262176 | tf_op jit(solution)/shard_map/ppermute | solution.py:273
  131.9 0.7 shard_map.95
  132.7 0.6 collective-permute-start.12
  133.3 1.4 collective-permute-start.11
  134.8 1.5 collective-permute-start.10
  136.2 6.6 %collective-permute-done.12 = bf16[256,512]{1,0:T(8,128)(2,1)S(1)} collective-permute-done((bf16[256,512]{1,0:T(8,128)(2,1)S(1)}, bf16[256,512]{1,0:T(8,128)(2,1)S(1)}, u32[]{:S(2)}, u32[]{:S(2)}) %collective-permute-start.12) | collective-permute-done | bytes 262176 | tf_op jit(solution)/shard_map/ppermute | solution.py:264
  142.8 4.2 %collective-permute-done.11 = bf16[256,512]{1,0:T(8,128)(2,1)S(1)} collective-permute-done((bf16[256,512]{1,0:T(8,128)(2,1)S(1)}, bf16[256,512]{1,0:T(8,128)(2,1)S(1)}, u32[]{:S(2)}, u32[]{:S(2)}) %collective-permute-start.11) | collective-permute-done | bytes 262176 | tf_op jit(solution)/shard_map/ppermute | solution.py:264
  147.0 0.8 add_convert_fusion
  (21 shorter events, 0.2 us)
Async XLA Ops:
  1.3 9.9 %all-to-all-start = ((f32[4,4,256]{2,1,0:T(4,128)}), f32[4,4,256]{2,1,0:T(4,128)S(1)}, u32[]{:S(2)}, u32[]{:S(2)}) async-start(f32[4,4,256]{2,1,0:T(4,128)} %reshape.40), calls=%async_computation | async-start | bytes 32768 | tf_op jit(solution)/shard_map/all_to_all | solution.py:288
  12.1 5.2 %copy-start.5 = (bf16[64,1024]{1,0:T(8,128)(2,1)S(1)}, bf16[64,1024]{1,0:T(8,128)(2,1)}, u32[]{:S(2)}) copy-start(bf16[64,1024]{1,0:T(8,128)(2,1)} %param.10) | copy-start | bytes 393220
  12.1 19.1 %all-to-all-start.2 = ((bf16[16,64,256]{2,1,0:T(8,128)(2,1)}), bf16[16,64,256]{2,1,0:T(8,128)(2,1)S(1)}, u32[]{:S(2)}, u32[]{:S(2)}) async-start(bf16[16,64,256]{2,1,0:T(8,128)(2,1)} %bitcast.8), calls=%async_computation.2 | async-start | bytes 1048576 | tf_op jit(solution)/shard_map/all_to_all | solution.py:278
  17.3 0.8 copy-start.7
  32.3 4.0 %copy-start.6 = (bf16[1024,64]{0,1:T(8,128)(2,1)S(1)}, bf16[1024,64]{0,1:T(8,128)(2,1)}, u32[]{:S(2)}) copy-start(bf16[1024,64]{0,1:T(8,128)(2,1)} %param.16) | copy-start | bytes 393220
  32.3 27.1 %all-to-all-start.1 = ((bf16[16,64,512]{2,1,0:T(8,128)(2,1)}), bf16[16,64,512]{2,1,0:T(8,128)(2,1)S(1)}, u32[]{:S(2)}, u32[]{:S(2)}) async-start(bf16[16,64,512]{2,1,0:T(8,128)(2,1)} %bitcast.4), calls=%async_computation.1 | async-start | bytes 2097152 | tf_op jit(solution)/shard_map/all_to_all | solution.py:278
  59.4 36.7 %copy-start.4 = (bf16[16,64,512]{2,1,0:T(8,128)(2,1)}, bf16[16,64,512]{2,1,0:T(8,128)(2,1)S(1)}, u32[]{:S(2)}) copy-start(bf16[16,64,512]{2,1,0:T(8,128)(2,1)S(1)} %all-to-all-done.1) | copy-start | bytes 3145732
  60.3 6.1 %copy-start = (bf16[256,1024]{1,0:T(8,128)(2,1)S(1)}, bf16[256,1024]{1,0:T(8,128)(2,1)}, u32[]{:S(2)}) copy-start(bf16[256,1024]{1,0:T(8,128)(2,1)} %refs_0_.3) | copy-start | bytes 1572868
  60.3 69.3 %all-to-all-start.3 = ((bf16[16,64,256]{2,1,0:T(8,128)(2,1)}), bf16[16,64,256]{2,1,0:T(8,128)(2,1)S(1)}, u32[]{:S(2)}, u32[]{:S(2)}) async-start(bf16[16,64,256]{2,1,0:T(8,128)(2,1)} %bitcast.12), calls=%async_computation.3 | async-start | bytes 1048576 | tf_op jit(solution)/shard_map/all_to_all | solution.py:278
  66.4 20.1 %collective-permute-start = (bf16[256,1024]{1,0:T(8,128)(2,1)S(1)}, bf16[256,1024]{1,0:T(8,128)(2,1)S(1)}, u32[]{:S(2)}, u32[]{:S(2)}) collective-permute-start(bf16[256,1024]{1,0:T(8,128)(2,1)S(1)} %copy-done), channel_id=1, source_target_pairs={{0,2},{2,0},{4,6},{6,4},{8,10},{10,8},{12,14},{14,12},{16,18},{18,... | collective-permute-start | bytes 1572872 | tf_op jit(solution)/shard_map/ppermute | solution.py:264
  68.4 18.3 %collective-permute-start.1 = (bf16[256,1024]{1,0:T(8,128)(2,1)S(1)}, bf16[256,1024]{1,0:T(8,128)(2,1)S(1)}, u32[]{:S(2)}, u32[]{:S(2)}) collective-permute-start(bf16[256,1024]{1,0:T(8,128)(2,1)S(1)} %copy-done), channel_id=1, source_target_pairs={{0,4},{2,6},{4,0},{6,2},{8,12},{10,14},{12,8},{14,10},{16,20},{18,... | collective-permute-start | bytes 1572872 | tf_op jit(solution)/shard_map/ppermute | solution.py:264
  69.9 26.2 %collective-permute-start.2 = (bf16[256,1024]{1,0:T(8,128)(2,1)S(1)}, bf16[256,1024]{1,0:T(8,128)(2,1)S(1)}, u32[]{:S(2)}, u32[]{:S(2)}) collective-permute-start(bf16[256,1024]{1,0:T(8,128)(2,1)S(1)} %copy-done), channel_id=1, source_target_pairs={{0,6},{2,4},{4,2},{6,0},{8,14},{10,12},{12,10},{14,8},{16,22},{18,... | collective-permute-start | bytes 1572872 | tf_op jit(solution)/shard_map/ppermute | solution.py:264
  96.1 0.7 copy-start.3
  102.1 9.0 %copy-start.2 = (f32[1024]{0:T(1024)S(1)}, f32[1024]{0:T(1024)}, u32[]{:S(2)}) copy-start(f32[1024]{0:T(1024)} %param.14) | copy-start | bytes 12292
  102.1 9.9 %collective-permute-start.3 = (bf16[144,256]{1,0:T(8,128)(2,1)S(1)}, bf16[144,256]{1,0:T(8,128)(2,1)S(1)}, u32[]{:S(2)}, u32[]{:S(2)}) collective-permute-start(bf16[144,256]{1,0:T(8,128)(2,1)S(1)} %get-tuple-element.23), channel_id=1, source_target_pairs={{0,8},{2,10},{4,12},{6,14},{8,16},{10,18},{12,20},{14,22},{16,24},... | collective-permute-start | bytes 221192 | tf_op jit(solution)/shard_map/ppermute | solution.py:267
  105.5 6.6 %collective-permute-start.4 = (bf16[144,256]{1,0:T(8,128)(2,1)S(1)}, bf16[144,256]{1,0:T(8,128)(2,1)S(1)}, u32[]{:S(2)}, u32[]{:S(2)}) collective-permute-start(bf16[144,256]{1,0:T(8,128)(2,1)S(1)} %get-tuple-element.23), channel_id=1, source_target_pairs={{0,16},{2,18},{4,20},{6,22},{8,24},{10,26},{12,28},{14,30},{1,17},... | collective-permute-start | bytes 221192 | tf_op jit(solution)/shard_map/ppermute | solution.py:267
  109.8 3.3 %collective-permute-start.5 = (bf16[144,256]{1,0:T(8,128)(2,1)S(1)}, bf16[144,256]{1,0:T(8,128)(2,1)S(1)}, u32[]{:S(2)}, u32[]{:S(2)}) collective-permute-start(bf16[144,256]{1,0:T(8,128)(2,1)S(1)} %get-tuple-element.23), channel_id=1, source_target_pairs={{0,24},{2,26},{4,28},{6,30},{1,25},{3,27},{5,29},{7,31}} | collective-permute-start | bytes 221192 | tf_op jit(solution)/shard_map/ppermute | solution.py:267
  113.0 8.6 %copy-start.1 = (f32[31,1024]{1,0:T(8,128)S(1)}, f32[31,1024]{1,0:T(8,128)}, u32[]{:S(2)}) copy-start(f32[31,1024]{1,0:T(8,128)} %taps_ref.1) | copy-start | bytes 380932
  113.6 2.6 %collective-permute-start.6 = (bf16[16,256]{1,0:T(8,128)(2,1)S(1)}, bf16[16,256]{1,0:T(8,128)(2,1)S(1)}, u32[]{:S(2)}, u32[]{:S(2)}) collective-permute-start(bf16[16,256]{1,0:T(8,128)(2,1)S(1)} %get-tuple-element.24), channel_id=1, source_target_pairs={{0,8},{2,10},{4,12},{6,14},{8,16},{10,18},{12,20},{14,22},{16,24},... | collective-permute-start | bytes 24584 | tf_op jit(solution)/shard_map/ppermute | solution.py:267
  114.9 6.7 %collective-permute-start.7 = (bf16[16,256]{1,0:T(8,128)(2,1)S(1)}, bf16[16,256]{1,0:T(8,128)(2,1)S(1)}, u32[]{:S(2)}, u32[]{:S(2)}) collective-permute-start(bf16[16,256]{1,0:T(8,128)(2,1)S(1)} %get-tuple-element.26), channel_id=1, source_target_pairs={{8,0},{10,2},{12,4},{14,6},{16,8},{18,10},{20,12},{22,14},{24,16},... | collective-permute-start | bytes 24584 | tf_op jit(solution)/shard_map/ppermute | solution.py:270
  129.6 2.4 %collective-permute-start.8 = (bf16[1024,256]{1,0:T(8,128)(2,1)S(1)}, bf16[1024,256]{1,0:T(8,128)(2,1)S(1)}, u32[]{:S(2)}, u32[]{:S(2)}) collective-permute-start(bf16[1024,256]{1,0:T(8,128)(2,1)S(1)} %shard_map.94.refs_0_), channel_id=1, source_target_pairs={{0,1},{1,0},{2,3},{3,2},{4,5},{5,4},{6,7},{7,6},{8,9},{9,8},{10,11... | collective-permute-start | bytes 1572872 | tf_op jit(solution)/shard_map/ppermute | solution.py:273
  129.7 2.2 %collective-permute-start.9 = (bf16[512,256]{1,0:T(8,128)(2,1)S(1)}, bf16[512,256]{1,0:T(8,128)(2,1)S(1)}, u32[]{:S(2)}, u32[]{:S(2)}) collective-permute-start(bf16[512,256]{1,0:T(8,128)(2,1)S(1)} %get-tuple-element.31), channel_id=1, source_target_pairs={{0,1},{1,0},{2,3},{3,2},{4,5},{5,4},{6,7},{7,6},{8,9},{9,8},{10,11... | collective-permute-start | bytes 786440 | tf_op jit(solution)/shard_map/ppermute | solution.py:273
  132.7 10.2 %collective-permute-start.12 = (bf16[256,512]{1,0:T(8,128)(2,1)S(1)}, bf16[256,512]{1,0:T(8,128)(2,1)S(1)}, u32[]{:S(2)}, u32[]{:S(2)}) collective-permute-start(bf16[256,512]{1,0:T(8,128)(2,1)S(1)} %get-tuple-element.30), channel_id=1, source_target_pairs={{0,6},{2,4},{4,2},{6,0},{8,14},{10,12},{12,10},{14,8},{16,22},{18,... | collective-permute-start | bytes 786440 | tf_op jit(solution)/shard_map/ppermute | solution.py:264
  133.3 13.7 %collective-permute-start.11 = (bf16[256,512]{1,0:T(8,128)(2,1)S(1)}, bf16[256,512]{1,0:T(8,128)(2,1)S(1)}, u32[]{:S(2)}, u32[]{:S(2)}) collective-permute-start(bf16[256,512]{1,0:T(8,128)(2,1)S(1)} %get-tuple-element.29), channel_id=1, source_target_pairs={{0,4},{2,6},{4,0},{6,2},{8,12},{10,14},{12,8},{14,10},{16,20},{18,... | collective-permute-start | bytes 786440 | tf_op jit(solution)/shard_map/ppermute | solution.py:264
  134.8 12.2 %collective-permute-start.10 = (bf16[256,512]{1,0:T(8,128)(2,1)S(1)}, bf16[256,512]{1,0:T(8,128)(2,1)S(1)}, u32[]{:S(2)}, u32[]{:S(2)}) collective-permute-start(bf16[256,512]{1,0:T(8,128)(2,1)S(1)} %get-tuple-element.28), channel_id=1, source_target_pairs={{0,2},{2,0},{4,6},{6,4},{8,10},{10,8},{12,14},{14,12},{16,18},{18,... | collective-permute-start | bytes 786440 | tf_op jit(solution)/shard_map/ppermute | solution.py:264

commit v2 on v1

v2 whole, which is shorter than its diff:
```python
import functools

import jax
import jax.numpy as jnp
from jax import lax
from jax.experimental import pallas as pl
from jax.experimental.pallas import tpu as pltpu
from jax.sharding import PartitionSpec as P

SPAN = 128
LANES = 128
EDGE = 16
BF16 = jnp.bfloat16
F32 = jnp.float32
VMEM_BYTES = 48 * 1024 * 1024


def dot(a, b, dims=((1,), (0,)), precision=None):
    return lax.dot_general(a, b, (dims, ((), ())), precision=precision, preferred_element_type=F32)


def call(kernel, out_shape, operands, scratch=(), flops=0, smem=1):
    in_specs = [pl.BlockSpec(memory_space=pltpu.SMEM)] * smem
    in_specs += [pl.BlockSpec(memory_space=pltpu.VMEM)] * (len(operands) - smem)
    moved = sum(a.size * a.dtype.itemsize for a in operands)
    moved += sum(a.size * a.dtype.itemsize for a in jax.tree.leaves(out_shape))
    return pl.pallas_call(
        kernel,
        out_shape=out_shape,
        in_specs=in_specs,
        out_specs=jax.tree.map(lambda _: pl.BlockSpec(memory_space=pltpu.VMEM), out_shape),
        scratch_shapes=list(scratch),
        compiler_params=pltpu.CompilerParams(vmem_limit_bytes=VMEM_BYTES),
        cost_estimate=pl.CostEstimate(flops=flops, bytes_accessed=moved, transcendentals=0),
    )(*operands)


def plane_place(group):
    index = lax.axis_index("tm")
    return lax.rem(index, group), lax.div(index, group)


def record_starts(len_ref, position):
    start = jnp.zeros_like(position)
    end = jnp.int32(0)
    for record in range(len_ref.shape[0] - 1):
        end = end + len_ref[record]
        start = jnp.where(position >= end, end, start)
    return start


def spread(columns, first, heads, head_of_lane, shape):
    out = jnp.broadcast_to(columns[:, first : first + 1], shape)
    for head in range(1, heads):
        column = jnp.broadcast_to(columns[:, first + head : first + head + 1], shape)
        out = jnp.where(head_of_lane == head, column, out)
    return out


def fill_planes(plane, dest_ref, pieces, offsets, lanes=slice(None)):
    rows = pieces[0].shape[0]
    for offset in sorted(set(offsets)):
        same = [piece[:, lanes] for piece, at in zip(pieces, offsets) if at == offset]
        value = same[0] if len(same) == 1 else same[0] + same[1]
        dest_ref[pl.ds(pl.multiple_of((plane ^ offset) * rows, rows), rows), :] = value


def pack_x_kernel(group, decay_ref, x_ref, bc_ref, *out_refs):
    place, _ = plane_place(group)
    rows = x_ref.shape[0]
    width = x_ref.shape[1] // group
    frames = decay_ref.shape[2]
    for step, out_ref in enumerate(out_refs):
        block = place ^ step
        out_ref[:rows, :width] = x_ref[:, pl.ds(pl.multiple_of(block * width, LANES), width)]
        out_ref[:rows, width:] = bc_ref[...]
        left = decay_ref[block]
        terms = []
        for _ in range(3):
            term = left.astype(BF16).astype(F32)
            terms.append(term)
            left = left - term
        terms.append(jnp.zeros_like(left))
        out_ref[rows:, :frames] = jnp.concatenate(terms, axis=0).astype(BF16)
        out_ref[rows:, frames:] = jnp.zeros((4 * 8, out_ref.shape[1] - frames), BF16)


def stack_x_kernel(group, *refs):
    parts, (stack_ref, decay_ref) = refs[:group], refs[group:]
    place, _ = plane_place(group)
    rows = stack_ref.shape[0] // group
    frames = decay_ref.shape[2]
    for step, part in enumerate(parts):
        block = place ^ step
        stack_ref[pl.ds(pl.multiple_of(block * rows, rows), rows), :] = part[:rows, :]
        terms = part[rows:, :frames].astype(F32)
        decay_ref[block] = terms[:8] + terms[8:16] + terms[16:24]


def pack_zo_kernel(group, z_ref, out_w_ref, *out_refs):
    place, _ = plane_place(group)
    width = z_ref.shape[1] // group
    for step, out_ref in enumerate(out_refs):
        lanes = pl.ds(pl.multiple_of((place ^ step) * width, LANES), width)
        out_ref[:, :width] = z_ref[:, lanes]
        out_ref[:, width:] = out_w_ref[:, lanes]


def stack_zo_kernel(group, *refs):
    parts, (z_ref, o_ref) = refs[:group], refs[group:]
    place, _ = plane_place(group)
    rows, width = z_ref.shape[0] // group, z_ref.shape[1]
    for step, part in enumerate(parts):
        at = pl.ds(pl.multiple_of((place ^ step) * rows, rows), rows)
        z_ref[at, :] = part[:, :width]
        o_ref[at, :] = part[:, width:]


def state_kernel(group, heads, state, offsets, len_ref, decay_ref, *refs):
    frame_refs, refs = refs[:group], refs[group:]
    pieces, refs = refs[: len(offsets)], refs[len(offsets) :]
    x_ref, b_ref, c_ref, columns_ref, cumul_ref, step_ref, carry_ref, keep_ref, send_ref, weight_ref = refs
    place, plane = plane_place(group)
    frames = frame_refs[0].shape[0]
    total, width = x_ref.shape
    head_size = width // heads
    count = total // SPAN
    base = plane * total
    fill_planes(plane, weight_ref, pieces, offsets)
    for step in range(group):
        rows = pl.ds(pl.multiple_of((place ^ step) * frames, frames), frames)
        product = dot(frame_refs[step][...], weight_ref[...])
        x_ref[rows, :] = product[:, :width].astype(BF16)
        b_ref[rows, :] = product[:, width : width + state].astype(BF16)
        c_ref[rows, :] = product[:, width + state :].astype(BF16)

    spans = frames // SPAN
    decay = jnp.concatenate(
        [decay_ref[block // spans][:, block % spans * SPAN : (block % spans + 1) * SPAN] for block in range(count)],
        axis=0,
    )
    used = decay.shape[0]
    square = (SPAN, SPAN)
    row, lane = (lax.broadcasted_iota(jnp.int32, square, dim) for dim in (0, 1))
    upper = jnp.where(row <= lane, 1.0, 0.0).astype(F32)
    cumul = dot(decay, upper, precision=lax.Precision.HIGHEST)
    whole = dot(decay, jnp.ones(square, F32), precision=lax.Precision.HIGHEST)
    first = base + lax.broadcasted_iota(jnp.int32, (used, SPAN), 0) // 8 * SPAN
    position = first + lane[:1]
    start = record_starts(len_ref, position)
    start_last = record_starts(len_ref, first + (SPAN - 1))
    carried = jnp.where(start < first, jnp.exp(cumul), 0.0)
    tail = jnp.where(position >= start_last, jnp.exp(whole - cumul), 0.0)
    keep = jnp.where(start_last < first, jnp.exp(whole), 0.0)
    parts = [cumul, carried, tail, start.astype(F32)]
    if 4 * used % SPAN:
        parts.append(jnp.zeros((SPAN - 4 * used % SPAN, SPAN), F32))
    columns = jnp.concatenate(parts, axis=0).T
    columns_ref[...] = columns
    cumul_ref[...] = cumul

    head_of_lane = lax.broadcasted_iota(jnp.int32, (SPAN, width), 1) // head_size
    entry = jnp.zeros((state, width), F32)
    through = jnp.ones((1, width), F32)
    for block in range(count):
        rows = slice(block * SPAN, (block + 1) * SPAN)
        at = block * 8
        kept = jnp.broadcast_to(keep[at : at + 1, :1], (1, width))
        for head in range(1, heads):
            other = jnp.broadcast_to(keep[at + head : at + head + 1, :1], (1, width))
            kept = jnp.where(head_of_lane[:1] == head, other, kept)
        carry_ref[rows, :] = spread(columns, used + at, heads, head_of_lane, (SPAN, width))
        weighed = x_ref[rows, :].astype(F32) * spread(columns, 2 * used + at, heads, head_of_lane, (SPAN, width))
        step = dot(b_ref[rows, :], weighed.astype(BF16), ((0,), (0,)))
        step_ref[block * state : (block + 1) * state, :] = step
        keep_ref[block * 8 : (block + 1) * 8, :] = jnp.broadcast_to(kept, (8, width))
        entry = kept * entry + step
        through = through * kept
    send_ref[:state, :] = entry.astype(BF16)
    send_ref[state:, :] = jnp.broadcast_to(through, (EDGE, width)).astype(BF16)


def inner_kernel(group, heads, x_ref, b_ref, c_ref, columns_ref, cumul_ref, y_ref):
    _, plane = plane_place(group)
    total, width = x_ref.shape
    head_size = width // heads
    count = total // SPAN
    base = plane * total
    used = cumul_ref.shape[0]
    square = (SPAN, SPAN)
    row, lane = (lax.broadcasted_iota(jnp.int32, square, dim) for dim in (0, 1))
    lower = row >= lane
    tile_heads = LANES // head_size
    tile_lane = lax.broadcasted_iota(jnp.int32, (1, LANES), 1) // head_size
    masks = [jnp.where(tile_lane == inner, 1.0, 0.0).astype(BF16) for inner in range(tile_heads)]
    for block in range(count):
        rows = slice(block * SPAN, (block + 1) * SPAN)
        at = block * 8
        x = x_ref[rows, :]
        scores = dot(c_ref[rows, :], b_ref[rows, :], ((1,), (1,)))
        here = (base + block * SPAN + lane).astype(F32)
        start_here = jnp.broadcast_to(columns_ref[:, 3 * used + at : 3 * used + at + 1], square)
        joined = lower & (here >= start_here)
        for tile in range(width // LANES):
            mixes, values = [], []
            for inner in range(tile_heads):
                which = at + tile * tile_heads + inner
                column = jnp.broadcast_to(columns_ref[:, which : which + 1], square)
                gap = jnp.where(joined, column - cumul_ref[which : which + 1, :], -1e30)
                mixes.append((jnp.exp(gap) * scores).astype(BF16))
                values.append(x[:, tile * LANES : (tile + 1) * LANES] * masks[inner])
            y_ref[rows, tile * LANES : (tile + 1) * LANES] = dot(
                jnp.concatenate(mixes, axis=1), jnp.concatenate(values, axis=0)
            )


def silu_kernel(group, offsets, gain_ref, *refs):
    frame_refs, refs = refs[:group], refs[group:]
    pieces, (out_ref, weight_ref) = refs[: len(offsets)], refs[len(offsets) :]
    place, plane = plane_place(group)
    frames = frame_refs[0].shape[0]
    width = weight_ref.shape[1]
    gain = gain_ref[:, pl.ds(pl.multiple_of(place * width, LANES), width)]
    fill_planes(plane, weight_ref, pieces, offsets)
    for step in range(group):
        rows = pl.ds(pl.multiple_of((place ^ step) * frames, frames), frames)
        z = dot(frame_refs[step][...], weight_ref[...]).astype(BF16).astype(F32)
        out_ref[rows, :] = z / (1.0 + jnp.exp(-z)) * gain


def share_kernel(group, cores, offsets, *refs):
    pieces, refs = refs[: len(offsets)], refs[len(offsets) :]
    outs, weight_ref = refs[:cores], refs[cores]
    _, plane = plane_place(group)
    core = lax.axis_index("head")
    fill_planes(plane, weight_ref, pieces, offsets)
    for step, out_ref in enumerate(outs):
        rows = out_ref.shape[0]
        out_ref[...] = weight_ref[pl.ds(pl.multiple_of((core ^ step) * rows, rows), rows), :]


def gate_kernel(heads, state, c_ref, y_ref, step_ref, carry_ref, keep_ref, silu_ref, *refs):
    earlier, (gated_ref, top_ref, bottom_ref) = refs[:-3], refs[-3:]
    total, width = y_ref.shape
    head_size = width // heads
    entry = jnp.zeros((state, width), F32)
    for summary in reversed(earlier):
        through = summary[state : state + EDGE, :].astype(F32)[:1]
        entry = through * entry + summary[:state, :].astype(F32)
    owner = [lax.broadcasted_iota(jnp.int32, (width, width), dim) // head_size for dim in (0, 1)]
    average = jnp.where(owner[0] == owner[1], 1.0 / head_size, 0.0).astype(BF16)
    for block in range(total // SPAN):
        rows = slice(block * SPAN, (block + 1) * SPAN)
        y = y_ref[rows, :] + carry_ref[rows, :] * dot(c_ref[rows, :], entry.astype(BF16))
        square_mean = dot((y * y).astype(BF16), average)
        gated_ref[rows, :] = (y * lax.rsqrt(square_mean + 1e-05) * silu_ref[rows, :]).astype(BF16)
        entry = keep_ref[block * 8 : block * 8 + 1, :] * entry + step_ref[block * state : (block + 1) * state, :]
    top_ref[...] = gated_ref[:EDGE, :]
    bottom_ref[...] = gated_ref[total - EDGE :, :]


def conv_kernel(group, edges, len_ref, taps_ref, gated_ref, *refs):
    if edges:
        before_ref, after_ref, inner_ref, act_ref, ext_ref, ends_ref = refs
    else:
        act_ref, ext_ref, ends_ref = refs
    place, plane = plane_place(group)
    total, width = gated_ref.shape
    count = total // SPAN
    taps = taps_ref.shape[0]
    half = (taps - 1) // 2
    base = plane * total
    stream = lax.axis_size("tm") // group * total
    records = len_ref.shape[0]
    reach = SPAN + 2 * EDGE
    first_tap = EDGE - half
    if edges:
        act_ref[SPAN : total - SPAN, :] = inner_ref[...]
        ext_ref[:EDGE, :] = before_ref[...].astype(F32)
        ext_ref[EDGE:reach, :] = gated_ref[: SPAN + EDGE, :].astype(F32)
        ext_ref[reach : 2 * reach - EDGE, :] = gated_ref[total - SPAN - EDGE :, :].astype(F32)
        ext_ref[2 * reach - EDGE :, :] = after_ref[...].astype(F32)
    else:
        ext_ref[...] = gated_ref[SPAN - EDGE : total - SPAN + EDGE, :].astype(F32)
    ends_ref[0] = 0
    for record in range(records):
        ends_ref[record + 1] = ends_ref[record] + len_ref[record]

    def record_at(position):
        found = jnp.int32(0)
        for record in range(records - 1):
            found = found + (ends_ref[record + 1] <= position).astype(jnp.int32)
        return found

    def one_block(at, source, target):
        low = record_at(jnp.maximum(base + at - half, 0))
        high = record_at(jnp.minimum(base + at + SPAN - 1 + half, stream - 1))
        near = lax.broadcasted_iota(jnp.int32, (reach, LANES), 0) + (base + at - EDGE)
        for tile in range(width // LANES):
            lanes = slice(tile * LANES, (tile + 1) * LANES)
            weights = taps_ref[:, pl.ds(pl.multiple_of(place * width + tile * LANES, LANES), LANES)]

            def one_record(record, done):
                inside = (near >= ends_ref[record]) & (near < ends_ref[record + 1])
                g = jnp.where(inside, ext_ref[pl.ds(source, reach), lanes], 0.0)
                out = None
                for phase in range(8):
                    part = None
                    for offset in range(phase, reach - SPAN, 8):
                        tap = offset - first_tap
                        if 0 <= tap < taps:
                            aligned = offset - phase
                            term = weights[tap : tap + 1, :] * g[aligned : aligned + SPAN + 8, :]
                            part = term if part is None else part + term
                    if part is not None:
                        moved = part[phase : phase + SPAN, :]
                        out = moved if out is None else out + moved
                return jnp.where(inside[EDGE : EDGE + SPAN], out, done)

            conv = lax.fori_loop(low, high + 1, one_record, jnp.zeros((SPAN, LANES), F32))
            act_ref[pl.ds(target, SPAN), lanes] = (conv / (1.0 + jnp.exp(-conv))).astype(BF16)
        return 0

    if edges:

        def edge(number, _):
            at = pl.multiple_of(number * (total - SPAN), SPAN)
            return one_block(at, pl.multiple_of(number * reach, reach), at)

        lax.fori_loop(0, 2, edge, 0)
    else:

        def inner(number, _):
            at = pl.multiple_of(number * SPAN, SPAN)
            return one_block(at + SPAN, at, at)

        lax.fori_loop(0, count - 2, inner, 0)


def out_kernel(group, cores, *refs):
    acts, weights, outs = refs[:cores], refs[cores : 2 * cores], refs[2 * cores :]
    place, _ = plane_place(group)
    frames = outs[0].shape[0]
    for step in reversed(range(group)):
        rows = pl.ds(pl.multiple_of((place ^ step) * frames, frames), frames)
        total = None
        for act, weight in zip(acts, weights):
            product = dot(act[rows, :], weight[...], ((1,), (1,)))
            total = product if total is None else total + product
        outs[step][...] = total.astype(outs[step].dtype)


def local(
    frames,
    x_weight,
    z_weight,
    bc_weight,
    log_decay,
    norm_gain,
    conv_weight,
    out_weight,
    record_lengths,
):
    times, cores = lax.axis_size("tm"), lax.axis_size("head")
    frame_count, depth = frames.shape
    heads_here, channels = log_decay.shape[0], x_weight.shape[1]
    state = bc_weight.shape[1] // 2
    group = 4
    while group > 1 and (channels // group % LANES or times % group or heads_here % group):
        group //= 2
    planes = times // group
    width, heads = channels // group, heads_here // group
    total = frame_count * group
    count = total // SPAN
    index, core = lax.axis_index("tm"), lax.axis_index("head")
    place = lax.rem(index, group)

    def in_plane(array, step):
        return lax.ppermute(array, "tm", [(i, i ^ step) for i in range(times)])

    def later(array, step):
        return lax.ppermute(array, "tm", [(i, i + step * group) for i in range(times - step * group)])

    def earlier(array, step):
        return lax.ppermute(array, "tm", [(i + step * group, i) for i in range(times - step * group)])

    def across(array, step):
        return lax.ppermute(array, "head", [(i, i ^ step) for i in range(cores)])

    def along_planes(stack):
        if planes != 4:
            moved = [
                lax.ppermute(stack, "tm", [(i, i ^ (step * group)) for i in range(times)]) for step in range(1, planes)
            ]
            return [stack, *moved], tuple(range(planes))

        def pairs(chosen):
            return [(a * group + q, b * group + q) for a, b in chosen for q in range(group)]

        second = lax.ppermute(stack, "tm", pairs([(0, 2), (2, 0), (1, 3), (3, 1)]))
        first = lax.ppermute(stack, "tm", pairs([(0, 1), (1, 0), (2, 3), (3, 2)]))
        again, stack_then = lax.optimization_barrier((second, stack))
        third = lax.ppermute(again, "tm", pairs([(1, 0), (2, 3)]))
        middle = lax.ppermute(stack_then, "tm", pairs([(1, 2), (2, 1)]))
        return [stack, first, second, third, middle], (0, 1, 2, 3, 3)

    shape = jax.ShapeDtypeStruct
    rows = x_weight.shape[0]
    decay_blocks = jnp.pad(log_decay.reshape(group, heads, frame_count), ((0, 0), (0, 8 - heads), (0, 0)))
    packed = call(
        functools.partial(pack_x_kernel, group),
        tuple(shape((rows + 32, width + 2 * state), BF16) for _ in range(group)),
        [decay_blocks, x_weight, bc_weight],
        smem=0,
    )
    parts = [packed[0]] + [in_plane(packed[step], step) for step in range(1, group)]
    frame_parts = [frames] + [in_plane(frames, step) for step in range(1, group)]
    stack, decay = call(
        functools.partial(stack_x_kernel, group),
        (shape((group * rows, width + 2 * state), BF16), shape((group, 8, frame_count), F32)),
        parts,
        smem=0,
    )
    x_pieces, offsets = along_planes(stack)

    packed = call(
        functools.partial(pack_zo_kernel, group),
        tuple(shape((rows, 2 * width), BF16) for _ in range(group)),
        [z_weight, out_weight.T],
        smem=0,
    )
    parts = [packed[0]] + [in_plane(packed[step], step) for step in range(1, group)]
    z_stack, o_stack = call(
        functools.partial(stack_zo_kernel, group),
        (shape((group * rows, width), BF16), shape((group * rows, width), BF16)),
        parts,
        smem=0,
    )
    (z_stack, o_stack), x_last = lax.optimization_barrier(((z_stack, o_stack), x_pieces[-1]))
    x_pieces = [*x_pieces[:-1], x_last]
    z_pieces, _ = along_planes(z_stack)

    used = count * 8
    x_rows, b_rows, c_rows, decays, cumul, steps, carry, keep, summary = call(
        functools.partial(state_kernel, group, heads, state, offsets),
        (
            shape((total, width), BF16),
            shape((total, state), BF16),
            shape((total, state), BF16),
            shape((SPAN, -(-4 * used // SPAN) * SPAN), F32),
            shape((used, SPAN), F32),
            shape((count * state, width), F32),
            shape((total, width), F32),
            shape((count * 8, width), F32),
            shape((state + EDGE, width), BF16),
        ),
        [record_lengths, decay, *frame_parts, *x_pieces],
        [pltpu.VMEM((depth, width + 2 * state), BF16)],
        flops=2 * total * depth * (width + 2 * state),
    )
    summaries = [later(summary, step) for step in range(1, planes)]
    y = call(
        functools.partial(inner_kernel, group, heads),
        shape((total, width), F32),
        [x_rows, b_rows, c_rows, decays, cumul],
        flops=4 * total * SPAN * width,
        smem=0,
    )
    silu = call(
        functools.partial(silu_kernel, group, offsets),
        shape((total, width), F32),
        [norm_gain[None], *frame_parts, *z_pieces],
        [pltpu.VMEM((depth, width), BF16)],
        flops=2 * total * depth * width,
        smem=0,
    )
    o_stack, z_last = lax.optimization_barrier((o_stack, z_pieces[-1]))
    o_pieces, _ = along_planes(o_stack)
    gated, top, bottom = call(
        functools.partial(gate_kernel, heads, state),
        (shape((total, width), BF16), shape((EDGE, width), BF16), shape((EDGE, width), BF16)),
        [c_rows, y, steps, carry, keep, silu, *summaries],
        flops=2 * total * state * width,
        smem=0,
    )
    before, after = later(bottom, 1), earlier(top, 1)
    ends = pltpu.SMEM((record_lengths.shape[0] + 1,), jnp.int32)
    inner = call(
        functools.partial(conv_kernel, group, False),
        shape((total - 2 * SPAN, width), BF16),
        [record_lengths, conv_weight, gated],
        [pltpu.VMEM((total - 2 * SPAN + 2 * EDGE, width), F32), ends],
        flops=2 * total * width * conv_weight.shape[0],
    )
    act = call(
        functools.partial(conv_kernel, group, True),
        shape((total, width), BF16),
        [record_lengths, conv_weight, gated, before, after, inner],
        [pltpu.VMEM((2 * SPAN + 4 * EDGE, width), F32), ends],
        flops=4 * SPAN * width * conv_weight.shape[0],
    )
    share = depth // cores
    out_parts = call(
        functools.partial(share_kernel, group, cores, offsets),
        tuple(shape((share, width), BF16) for _ in range(cores)),
        o_pieces,
        [pltpu.VMEM((depth, width), BF16)],
        smem=0,
    )
    out_parts = [out_parts[0]] + [across(out_parts[step], step) for step in range(1, cores)]
    acts = [act] + [across(act, step) for step in range(1, cores)]
    outs = call(
        functools.partial(out_kernel, group, cores),
        tuple(shape((frame_count, share), BF16 if step else F32) for step in range(group)),
        [*acts, *out_parts],
        flops=2 * total * width * cores * share,
        smem=0,
    )
    mixed = outs[0]
    for step in range(1, group):
        mixed = mixed + in_plane(outs[step], step).astype(F32)
    return mixed.astype(BF16)


def solution(mesh):
    in_specs = (
        P("tm", None),
        P("tm", "head"),
        P("tm", "head"),
        P("tm", None),
        P("head", "tm"),
        P("head"),
        P(None, "head"),
        P("head", "tm"),
        P(),
    )
    out_specs = P("tm", "head")
    return jax.shard_map(local, mesh=mesh, in_specs=in_specs, out_specs=out_specs, check_vma=False)
```

time: 147 us -> 123 us (0.84)
  waiting for transfers between devices: 84.6 us -> 58.1 us
  starting transfers between devices: 39.6 us -> 44.2 us
  local copies, waits for them, and re-layouts: 6.84 us -> 3.53 us
    all_to_all x4 -> x0, waiting for transfers between devices: 39.7 us -> none  [the longest x3 36 us: to_owners(): moved = lax.all_to_all(whole, 'tm', split_axis=0, concat_axis=0, tiled=True)]
    ppermute x0 -> x12, waiting for transfers between devices: none -> 25.3 us  [the longest x3 11.6 us: along_planes(): first = lax.ppermute(stack, 'tm', pairs([(0, 1), (1, 0), (2, 3), (3, 2)]))]
    all_to_all x4 -> x0, starting transfers between devices: 20.4 us -> none  [the longest x3 15.2 us: to_owners(): moved = lax.all_to_all(whole, 'tm', split_axis=0, concat_axis=0, tiled=True)]
    ppermute x0 -> x12, starting transfers between devices: none -> 15.8 us  [the longest x3 7.86 us: along_planes(): second = lax.ppermute(stack, 'tm', pairs([(0, 2), (2, 0), (1, 3), (3, 1)]))]
    ppermute x6 -> x12, starting transfers between devices: 7.11 us -> 15.2 us  [in_plane(): return lax.ppermute(array, 'tm', [(i, i ^ step) for i in range(times)])]
    ppermute x6 -> x12, waiting for transfers between devices: 36.9 us -> 31.3 us  [in_plane(): return lax.ppermute(array, 'tm', [(i, i ^ step) for i in range(times)])]
    ppermute x1, waiting for transfers between devices: 5.34 us -> 0.01 us  [earlier(): lax.ppermute(array, 'tm', [(i + step * group, i) for i in range(times - s...]
    broadcast_in_dim x4 -> x0, local copies, waits for them, and re-layouts: 2.9 us -> none  [the longest x3 2.87 us: to_owners(): whole = jnp.broadcast_to(blocks[None], (planes,) + blocks.shape)]
  transfers between devices with their start and end apart: 17 -> 31, of which waited for: 11 -> 13; matrix products, arithmetic and copies ran while one was open for 1% -> 0% of each run, Pallas kernels for 10% -> 11%
where the time goes in v2:
time: 123 us; the launch traced here: 122 us
  waiting for transfers between devices  58.1 us (47%)
  starting transfers between devices  44.2 us (36%)
  Pallas kernels  15.4 us (13%)
  local copies, waits for them, and re-layouts  3.53 us (3%)
    ppermute x12, waiting for transfers between devices, in_plane(): return lax.ppermute(array, 'tm', [(i, i ^ step) for i in range(times)])  31.3 us
    pallas_call x12, Pallas kernels, call(): pl.pallas_call(kernel, out_shape=out_shape, in_specs=in_specs, out_specs=...  15.4 us
    ppermute x12, starting transfers between devices, in_plane(): return lax.ppermute(array, 'tm', [(i, i ^ step) for i in range(times)])  15.2 us
    ppermute x4, starting transfers between devices, later(): lax.ppermute(array, 'tm', [(i, i + step * group) for i in range(times - s...  11.7 us
    ppermute x3, waiting for transfers between devices, along_planes(): first = lax.ppermute(stack, 'tm', pairs([(0, 1), (1, 0), (2, 3), (3, 2)]))  11.6 us
    ppermute x3, waiting for transfers between devices, along_planes(): second = lax.ppermute(stack, 'tm', pairs([(0, 2), (2, 0), (1, 3), (3, 1)]))  11.3 us
    ppermute x3, starting transfers between devices, along_planes(): second = lax.ppermute(stack, 'tm', pairs([(0, 2), (2, 0), (1, 3), (3, 1)]))  7.86 us
    ppermute x3, starting transfers between devices, along_planes(): third = lax.ppermute(again, 'tm', pairs([(1, 0), (2, 3)]))  3.84 us
  transfers between devices with their start and end apart: 31, of which 13 were waited for; matrix products, arithmetic and copies ran while one was open for 0% of the time, Pallas kernels for 11%

profile of v2, /device:TPU:0, one launch (start us, length us, event | category | flops | bytes accessed | tf_op | source)
XLA Modules:
  0.0 122.4 jit_solution(904972586763084402)
XLA Ops:
  0.0 0.8 reshape.3
  0.8 0.9 copy-done.3
  1.7 0.8 copy-done.6
  2.5 3.0 %collective-permute-start = (bf16[96,512]{1,0:T(8,128)(2,1)S(1)}, bf16[96,512]{1,0:T(8,128)(2,1)S(1)}, u32[]{:S(2)}, u32[]{:S(2)}) collective-permute-start(bf16[96,512]{1,0:T(8,128)(2,1)S(1)} %get-tuple-element.46), channel_id=1, source_target_pairs={{0,2},{2,0},{4,6},{6,4},{8,10},{10,8},{12,14},{14,12},{16,18},{18,... | collective-permute-start | bytes 294920 | tf_op jit(solution)/shard_map/ppermute | solution.py:379
  5.5 1.5 %collective-permute-start.1 = (bf16[96,512]{1,0:T(8,128)(2,1)S(1)}, bf16[96,512]{1,0:T(8,128)(2,1)S(1)}, u32[]{:S(2)}, u32[]{:S(2)}) collective-permute-start(bf16[96,512]{1,0:T(8,128)(2,1)S(1)} %get-tuple-element.47), channel_id=1, source_target_pairs={{0,4},{2,6},{4,0},{6,2},{8,12},{10,14},{12,8},{14,10},{16,20},{18,... | collective-permute-start | bytes 294920 | tf_op jit(solution)/shard_map/ppermute | solution.py:379
  7.0 1.5 %collective-permute-done.refs_1_ = bf16[96,512]{1,0:T(8,128)(2,1)S(1)} collective-permute-done((bf16[96,512]{1,0:T(8,128)(2,1)S(1)}, bf16[96,512]{1,0:T(8,128)(2,1)S(1)}, u32[]{:S(2)}, u32[]{:S(2)}) %collective-permute-start) | collective-permute-done | bytes 98336 | tf_op jit(solution)/shard_map/ppermute | solution.py:379
  8.6 2.6 %collective-permute-done.1.refs_2_ = bf16[96,512]{1,0:T(8,128)(2,1)S(1)} collective-permute-done((bf16[96,512]{1,0:T(8,128)(2,1)S(1)}, bf16[96,512]{1,0:T(8,128)(2,1)S(1)}, u32[]{:S(2)}, u32[]{:S(2)}) %collective-permute-start.1) | collective-permute-done | bytes 98336 | tf_op jit(solution)/shard_map/ppermute | solution.py:379
  11.2 1.4 %collective-permute-done.2.refs_3_ = bf16[96,512]{1,0:T(8,128)(2,1)S(1)} collective-permute-done((bf16[96,512]{1,0:T(8,128)(2,1)S(1)}, bf16[96,512]{1,0:T(8,128)(2,1)S(1)}, u32[]{:S(2)}, u32[]{:S(2)}) %collective-permute-start.2) | collective-permute-done | bytes 98336 | tf_op jit(solution)/shard_map/ppermute | solution.py:379
  12.6 2.7 %collective-permute-start.7 = (bf16[256,512]{1,0:T(8,128)(2,1)S(1)}, bf16[256,512]{1,0:T(8,128)(2,1)S(1)}, u32[]{:S(2)}, u32[]{:S(2)}) collective-permute-start(bf16[256,512]{1,0:T(8,128)(2,1)S(1)} %get-tuple-element.58.refs_4_), channel_id=1, source_target_pairs={{0,16},{2,18},{4,20},{6,22},{16,0},{18,2},{20,4},{22,6},{8,24},{10... | collective-permute-start | bytes 786440 | tf_op jit(solution)/shard_map/ppermute | solution.py:400
  15.2 0.9 copy-done.5
  16.2 0.7 collective-permute-start.9
  16.9 1.0 collective-permute-start.10
  17.9 1.3 %collective-permute-start.3 = (bf16[256,1024]{1,0:T(8,128)(2,1)S(1)}, bf16[256,1024]{1,0:T(8,128)(2,1)S(1)}, u32[]{:S(2)}, u32[]{:S(2)}) collective-permute-start(bf16[256,1024]{1,0:T(8,128)(2,1)S(1)} %copy-done.1), channel_id=1, source_target_pairs={{0,2},{2,0},{4,6},{6,4},{8,10},{10,8},{12,14},{14,12},{16,18},{18,... | collective-permute-start | bytes 1572872 | tf_op jit(solution)/shard_map/ppermute | solution.py:379
  19.2 1.1 collective-permute-start.4
  20.3 5.3 %collective-permute-done.7.refs_6_ = bf16[256,512]{1,0:T(8,128)(2,1)S(1)} collective-permute-done((bf16[256,512]{1,0:T(8,128)(2,1)S(1)}, bf16[256,512]{1,0:T(8,128)(2,1)S(1)}, u32[]{:S(2)}, u32[]{:S(2)}) %collective-permute-start.7) | collective-permute-done | bytes 262176 | tf_op jit(solution)/shard_map/ppermute | solution.py:400
  25.6 0.7 collective-permute-start.12
  26.3 1.6 %collective-permute-start.5 = (bf16[256,1024]{1,0:T(8,128)(2,1)S(1)}, bf16[256,1024]{1,0:T(8,128)(2,1)S(1)}, u32[]{:S(2)}, u32[]{:S(2)}) collective-permute-start(bf16[256,1024]{1,0:T(8,128)(2,1)S(1)} %copy-done.1), channel_id=1, source_target_pairs={{0,6},{2,4},{4,2},{6,0},{8,14},{10,12},{12,10},{14,8},{16,22},{18,... | collective-permute-start | bytes 1572872 | tf_op jit(solution)/shard_map/ppermute | solution.py:379
  27.9 1.4 %collective-permute-start.11 = (bf16[64,512]{1,0:T(8,128)(2,1)S(1)}, bf16[64,512]{1,0:T(8,128)(2,1)S(1)}, u32[]{:S(2)}, u32[]{:S(2)}) collective-permute-start(bf16[64,512]{1,0:T(8,128)(2,1)S(1)} %get-tuple-element.55), channel_id=1, source_target_pairs={{0,6},{2,4},{4,2},{6,0},{8,14},{10,12},{12,10},{14,8},{16,22},{18,... | collective-permute-start | bytes 196616 | tf_op jit(solution)/shard_map/ppermute | solution.py:379
  29.3 14.5 %collective-permute-done.11.refs_3_ = bf16[64,512]{1,0:T(8,128)(2,1)S(1)} collective-permute-done((bf16[64,512]{1,0:T(8,128)(2,1)S(1)}, bf16[64,512]{1,0:T(8,128)(2,1)S(1)}, u32[]{:S(2)}, u32[]{:S(2)}) %collective-permute-start.11) | collective-permute-done | bytes 65568 | tf_op jit(solution)/shard_map/ppermute | solution.py:379
  43.8 1.6 %collective-permute-start.6 = (bf16[256,512]{1,0:T(8,128)(2,1)S(1)}, bf16[256,512]{1,0:T(8,128)(2,1)S(1)}, u32[]{:S(2)}, u32[]{:S(2)}) collective-permute-start(bf16[256,512]{1,0:T(8,128)(2,1)S(1)} %get-tuple-element.58.refs_4_), channel_id=1, source_target_pairs={{0,8},{2,10},{4,12},{6,14},{8,0},{10,2},{12,4},{14,6},{16,24},{18,... | collective-permute-start | bytes 786440 | tf_op jit(solution)/shard_map/ppermute | solution.py:401
  45.4 1.3 %collective-permute-start.8 = (bf16[256,512]{1,0:T(8,128)(2,1)S(1)}, bf16[256,512]{1,0:T(8,128)(2,1)S(1)}, u32[]{:S(2)}, u32[]{:S(2)}) collective-permute-start(bf16[256,512]{1,0:T(8,128)(2,1)S(1)} %collective-permute-done.7.refs_6_), channel_id=1, source_target_pairs={{8,0},{10,2},{12,4},{14,6},{16,24},{18,26},{20,28},{22,30},{9,1},{... | collective-permute-start | bytes 786440 | tf_op jit(solution)/shard_map/ppermute | solution.py:403
  46.7 7.7 %collective-permute-done.6.refs_5_ = bf16[256,512]{1,0:T(8,128)(2,1)S(1)} collective-permute-done((bf16[256,512]{1,0:T(8,128)(2,1)S(1)}, bf16[256,512]{1,0:T(8,128)(2,1)S(1)}, u32[]{:S(2)}, u32[]{:S(2)}) %collective-permute-start.6) | collective-permute-done | bytes 262176 | tf_op jit(solution)/shard_map/ppermute | solution.py:401
  54.4 6.0 %collective-permute-done.14.refs_6_ = bf16[256,256]{1,0:T(8,128)(2,1)S(1)} collective-permute-done((bf16[256,256]{1,0:T(8,128)(2,1)S(1)}, bf16[256,256]{1,0:T(8,128)(2,1)S(1)}, u32[]{:S(2)}, u32[]{:S(2)}) %collective-permute-start.14) | collective-permute-done | bytes 131104 | tf_op jit(solution)/shard_map/ppermute | solution.py:400
  60.4 1.3 %collective-permute-start.15 = (bf16[256,256]{1,0:T(8,128)(2,1)S(1)}, bf16[256,256]{1,0:T(8,128)(2,1)S(1)}, u32[]{:S(2)}, u32[]{:S(2)}) collective-permute-start(bf16[256,256]{1,0:T(8,128)(2,1)S(1)} %collective-permute-done.14.refs_6_), channel_id=1, source_target_pairs={{8,0},{10,2},{12,4},{14,6},{16,24},{18,26},{20,28},{22,30},{9,1},{... | collective-permute-start | bytes 393224 | tf_op jit(solution)/shard_map/ppermute | solution.py:403
  61.7 0.7 collective-permute-start.16
  62.4 4.7 %shard_map.95 = (bf16[1024,256]{1,0:T(8,128)(2,1)S(1)}, bf16[1024,128]{1,0:T(8,128)(2,1)S(1)}, bf16[1024,128]{1,0:T(8,128)(2,1)S(1)}, f32[128,256]{1,0:T(8,128)S...) custom-call(s32[8]{0:T(128)S(1)} %copy-done.8, ...), custom_call_target="tpu_custom_call" | custom-call | flops 1073741824 | bytes 6889504 | tf_op jit(solution)/shard_map/pallas_call | solution.py:27
  67.1 7.2 %collective-permute-start.17 = (bf16[144,256]{1,0:T(8,128)(2,1)S(1)}, bf16[144,256]{1,0:T(8,128)(2,1)S(1)}, u32[]{:S(2)}, u32[]{:S(2)}) collective-permute-start(bf16[144,256]{1,0:T(8,128)(2,1)S(1)} %get-tuple-element.71), channel_id=1, source_target_pairs={{0,8},{2,10},{4,12},{6,14},{8,16},{10,18},{12,20},{14,22},{16,24},... | collective-permute-start | bytes 221192 | tf_op jit(solution)/shard_map/ppermute | solution.py:382
  74.3 2.0 %collective-permute-start.18 = (bf16[144,256]{1,0:T(8,128)(2,1)S(1)}, bf16[144,256]{1,0:T(8,128)(2,1)S(1)}, u32[]{:S(2)}, u32[]{:S(2)}) collective-permute-start(bf16[144,256]{1,0:T(8,128)(2,1)S(1)} %get-tuple-element.71), channel_id=1, source_target_pairs={{0,16},{2,18},{4,20},{6,22},{8,24},{10,26},{12,28},{14,30},{1,17},... | collective-permute-start | bytes 221192 | tf_op jit(solution)/shard_map/ppermute | solution.py:382
  76.3 1.3 %collective-permute-start.19 = (bf16[144,256]{1,0:T(8,128)(2,1)S(1)}, bf16[144,256]{1,0:T(8,128)(2,1)S(1)}, u32[]{:S(2)}, u32[]{:S(2)}) collective-permute-start(bf16[144,256]{1,0:T(8,128)(2,1)S(1)} %get-tuple-element.71), channel_id=1, source_target_pairs={{0,24},{2,26},{4,28},{6,30},{1,25},{3,27},{5,29},{7,31}} | collective-permute-start | bytes 221192 | tf_op jit(solution)/shard_map/ppermute | solution.py:382
  77.6 1.5 %shard_map.96.y_ref = f32[1024,256]{1,0:T(8,128)S(1)} custom-call(bf16[1024,256]{1,0:T(8,128)(2,1)S(1)} %get-tuple-element.61.x_ref, bf16[1024,128]{1,0:T(8,128)(2,1)S(1)} %get-tuple-element.62.b_ref, bf16[1024,128]{1,0:T(8,128)(2,1)S(1)} %get-tuple-element.60.c_ref, f32[128,256]{1,0:T(8,128)S(1)} %get-tuple-element.63.columns_ref, ...), custom_call_target="tpu_custom_call" | custom-call | flops 134217728 | bytes 2260992 | tf_op jit(solution)/shard_map/pallas_call | solution.py:27
  79.2 1.0 shard_map.97.silu_ref
  81.1 1.3 %collective-permute-start.20 = (bf16[16,256]{1,0:T(8,128)(2,1)S(1)}, bf16[16,256]{1,0:T(8,128)(2,1)S(1)}, u32[]{:S(2)}, u32[]{:S(2)}) collective-permute-start(bf16[16,256]{1,0:T(8,128)(2,1)S(1)} %get-tuple-element.73), channel_id=1, source_target_pairs={{0,8},{2,10},{4,12},{6,14},{8,16},{10,18},{12,20},{14,22},{16,24},... | collective-permute-start | bytes 24584 | tf_op jit(solution)/shard_map/ppermute | solution.py:382
  82.4 1.3 %collective-permute-start.21 = (bf16[16,256]{1,0:T(8,128)(2,1)S(1)}, bf16[16,256]{1,0:T(8,128)(2,1)S(1)}, u32[]{:S(2)}, u32[]{:S(2)}) collective-permute-start(bf16[16,256]{1,0:T(8,128)(2,1)S(1)} %get-tuple-element.74), channel_id=1, source_target_pairs={{8,0},{10,2},{12,4},{14,6},{16,8},{18,10},{20,12},{22,14},{24,16},... | collective-permute-start | bytes 24584 | tf_op jit(solution)/shard_map/ppermute | solution.py:385
  83.7 5.2 %collective-permute-start.24 = (bf16[256,256]{1,0:T(8,128)(2,1)S(1)}, bf16[256,256]{1,0:T(8,128)(2,1)S(1)}, u32[]{:S(2)}, u32[]{:S(2)}) collective-permute-start(bf16[256,256]{1,0:T(8,128)(2,1)S(1)} %get-tuple-element.78.refs_0_), channel_id=1, source_target_pairs={{0,16},{2,18},{4,20},{6,22},{16,0},{18,2},{20,4},{22,6},{8,24},{10... | collective-permute-start | bytes 393224 | tf_op jit(solution)/shard_map/ppermute | solution.py:400
  88.9 4.6 %shard_map.99.refs_2_ = bf16[768,256]{1,0:T(8,128)(2,1)S(1)} custom-call(s32[8]{0:T(128)S(1)} %copy-done.8, f32[31,1024]{1,0:T(8,128)S(1)} %copy-done.2, bf16[1024,256]{1,0:T(8,128)(2,1)S(1)} %get-tuple-element.72.gated_ref), custom_call_target="tpu_custom_call" | custom-call | flops 16252928 | bytes 1044512 | tf_op jit(solution)/shard_map/pallas_call | solution.py:27
  93.5 1.9 %shard_map.100.refs_0_ = bf16[1024,256]{1,0:T(8,128)(2,1)S(1)} custom-call(s32[8]{0:T(128)S(1)} %copy-done.8, f32[31,1024]{1,0:T(8,128)S(1)} %copy-done.2, bf16[1024,256]{1,0:T(8,128)(2,1)S(1)} %get-tuple-element.72.gated_ref, bf16[16,256]{1,0:T(8,128)(2,1)S(1)} %collective-permute-done.20.refs_0_, bf16[16,256]{1,0:T(8,128)(2,1)S(1)} %collective-permute-done.21.refs_1_, ...), custom_call_target="tpu_custom_call" | custom-call | flops 4063232 | bytes 1585184 | tf_op jit(solution)/shard_map/pallas_call | solution.py:27
  96.1 1.3 %collective-permute-start.25 = (bf16[256,256]{1,0:T(8,128)(2,1)S(1)}, bf16[256,256]{1,0:T(8,128)(2,1)S(1)}, u32[]{:S(2)}, u32[]{:S(2)}) collective-permute-start(bf16[256,256]{1,0:T(8,128)(2,1)S(1)} %collective-permute-done.24.refs_2_), channel_id=1, source_target_pairs={{8,0},{10,2},{12,4},{14,6},{16,24},{18,26},{20,28},{22,30},{9,1},{... | collective-permute-start | bytes 393224 | tf_op jit(solution)/shard_map/ppermute | solution.py:403
  97.4 0.7 collective-permute-start.26
  98.1 3.9 %collective-permute-done.23.refs_1_ = bf16[256,256]{1,0:T(8,128)(2,1)S(1)} collective-permute-done((bf16[256,256]{1,0:T(8,128)(2,1)S(1)}, bf16[256,256]{1,0:T(8,128)(2,1)S(1)}, u32[]{:S(2)}, u32[]{:S(2)}) %collective-permute-start.23) | collective-permute-done | bytes 131104 | tf_op jit(solution)/shard_map/ppermute | solution.py:401
  101.9 2.4 %collective-permute-done.25.refs_3_ = bf16[256,256]{1,0:T(8,128)(2,1)S(1)} collective-permute-done((bf16[256,256]{1,0:T(8,128)(2,1)S(1)}, bf16[256,256]{1,0:T(8,128)(2,1)S(1)}, u32[]{:S(2)}, u32[]{:S(2)}) %collective-permute-start.25) | collective-permute-done | bytes 131104 | tf_op jit(solution)/shard_map/ppermute | solution.py:403
  104.5 1.5 %collective-permute-done.27.refs_3_ = bf16[512,256]{1,0:T(8,128)(2,1)S(1)} collective-permute-done((bf16[512,256]{1,0:T(8,128)(2,1)S(1)}, bf16[512,256]{1,0:T(8,128)(2,1)S(1)}, u32[]{:S(2)}, u32[]{:S(2)}) %collective-permute-start.27) | collective-permute-done | bytes 262176 | tf_op jit(solution)/shard_map/ppermute | solution.py:388
  106.0 0.7 shard_map.102
  106.7 0.9 collective-permute-start.30
  107.7 1.4 %collective-permute-start.29 = (bf16[256,512]{1,0:T(8,128)(2,1)S(1)}, bf16[256,512]{1,0:T(8,128)(2,1)S(1)}, u32[]{:S(2)}, u32[]{:S(2)}) collective-permute-start(bf16[256,512]{1,0:T(8,128)(2,1)S(1)} %get-tuple-element.83), channel_id=1, source_target_pairs={{0,4},{2,6},{4,0},{6,2},{8,12},{10,14},{12,8},{14,10},{16,20},{18,... | collective-permute-start | bytes 786440 | tf_op jit(solution)/shard_map/ppermute | solution.py:379
  109.1 1.2 collective-permute-start.28
  110.3 6.6 %collective-permute-done.30 = bf16[256,512]{1,0:T(8,128)(2,1)S(1)} collective-permute-done((bf16[256,512]{1,0:T(8,128)(2,1)S(1)}, bf16[256,512]{1,0:T(8,128)(2,1)S(1)}, u32[]{:S(2)}, u32[]{:S(2)}) %collective-permute-start.30) | collective-permute-done | bytes 262176 | tf_op jit(solution)/shard_map/ppermute | solution.py:379
  116.9 4.5 %collective-permute-done.29 = bf16[256,512]{1,0:T(8,128)(2,1)S(1)} collective-permute-done((bf16[256,512]{1,0:T(8,128)(2,1)S(1)}, bf16[256,512]{1,0:T(8,128)(2,1)S(1)}, u32[]{:S(2)}, u32[]{:S(2)}) %collective-permute-start.29) | collective-permute-done | bytes 262176 | tf_op jit(solution)/shard_map/ppermute | solution.py:379
  121.6 0.8 add_convert_fusion
  (47 shorter events, 2.0 us)
Async XLA Ops:
  0.0 17.9 %copy-start.1 = (bf16[256,1024]{1,0:T(8,128)(2,1)S(1)}, bf16[256,1024]{1,0:T(8,128)(2,1)}, u32[]{:S(2)}) copy-start(bf16[256,1024]{1,0:T(8,128)(2,1)} %refs_0_.3) | copy-start | bytes 1572868
  0.8 0.9 copy-start.3
  1.7 0.8 copy-start.6
  2.5 6.1 %collective-permute-start = (bf16[96,512]{1,0:T(8,128)(2,1)S(1)}, bf16[96,512]{1,0:T(8,128)(2,1)S(1)}, u32[]{:S(2)}, u32[]{:S(2)}) collective-permute-start(bf16[96,512]{1,0:T(8,128)(2,1)S(1)} %get-tuple-element.46), channel_id=1, source_target_pairs={{0,2},{2,0},{4,6},{6,4},{8,10},{10,8},{12,14},{14,12},{16,18},{18,... | collective-permute-start | bytes 294920 | tf_op jit(solution)/shard_map/ppermute | solution.py:379
  5.5 5.7 %collective-permute-start.1 = (bf16[96,512]{1,0:T(8,128)(2,1)S(1)}, bf16[96,512]{1,0:T(8,128)(2,1)S(1)}, u32[]{:S(2)}, u32[]{:S(2)}) collective-permute-start(bf16[96,512]{1,0:T(8,128)(2,1)S(1)} %get-tuple-element.47), channel_id=1, source_target_pairs={{0,4},{2,6},{4,0},{6,2},{8,12},{10,14},{12,8},{14,10},{16,20},{18,... | collective-permute-start | bytes 294920 | tf_op jit(solution)/shard_map/ppermute | solution.py:379
  7.0 5.5 %collective-permute-start.2 = (bf16[96,512]{1,0:T(8,128)(2,1)S(1)}, bf16[96,512]{1,0:T(8,128)(2,1)S(1)}, u32[]{:S(2)}, u32[]{:S(2)}) collective-permute-start(bf16[96,512]{1,0:T(8,128)(2,1)S(1)} %get-tuple-element.48), channel_id=1, source_target_pairs={{0,6},{2,4},{4,2},{6,0},{8,14},{10,12},{12,10},{14,8},{16,22},{18,... | collective-permute-start | bytes 294920 | tf_op jit(solution)/shard_map/ppermute | solution.py:379
  12.5 2.7 %copy-start.4 = (bf16[64,1024]{1,0:T(8,128)(2,1)S(1)}, bf16[64,1024]{1,0:T(8,128)(2,1)}, u32[]{:S(2)}) copy-start(bf16[64,1024]{1,0:T(8,128)(2,1)} %z_ref.1) | copy-start | bytes 393220
  12.6 13.0 %collective-permute-start.7 = (bf16[256,512]{1,0:T(8,128)(2,1)S(1)}, bf16[256,512]{1,0:T(8,128)(2,1)S(1)}, u32[]{:S(2)}, u32[]{:S(2)}) collective-permute-start(bf16[256,512]{1,0:T(8,128)(2,1)S(1)} %get-tuple-element.58.refs_4_), channel_id=1, source_target_pairs={{0,16},{2,18},{4,20},{6,22},{16,0},{18,2},{20,4},{22,6},{8,24},{10... | collective-permute-start | bytes 786440 | tf_op jit(solution)/shard_map/ppermute | solution.py:400
  15.2 0.9 copy-start.5
  16.2 10.1 %collective-permute-start.9 = (bf16[64,512]{1,0:T(8,128)(2,1)S(1)}, bf16[64,512]{1,0:T(8,128)(2,1)S(1)}, u32[]{:S(2)}, u32[]{:S(2)}) collective-permute-start(bf16[64,512]{1,0:T(8,128)(2,1)S(1)} %get-tuple-element.53), channel_id=1, source_target_pairs={{0,2},{2,0},{4,6},{6,4},{8,10},{10,8},{12,14},{14,12},{16,18},{18,... | collective-permute-start | bytes 196616 | tf_op jit(solution)/shard_map/ppermute | solution.py:379
  16.9 11.0 %collective-permute-start.10 = (bf16[64,512]{1,0:T(8,128)(2,1)S(1)}, bf16[64,512]{1,0:T(8,128)(2,1)S(1)}, u32[]{:S(2)}, u32[]{:S(2)}) collective-permute-start(bf16[64,512]{1,0:T(8,128)(2,1)S(1)} %get-tuple-element.54), channel_id=1, source_target_pairs={{0,4},{2,6},{4,0},{6,2},{8,12},{10,14},{12,8},{14,10},{16,20},{18,... | collective-permute-start | bytes 196616 | tf_op jit(solution)/shard_map/ppermute | solution.py:379
  17.9 42.6 %collective-permute-start.3 = (bf16[256,1024]{1,0:T(8,128)(2,1)S(1)}, bf16[256,1024]{1,0:T(8,128)(2,1)S(1)}, u32[]{:S(2)}, u32[]{:S(2)}) collective-permute-start(bf16[256,1024]{1,0:T(8,128)(2,1)S(1)} %copy-done.1), channel_id=1, source_target_pairs={{0,2},{2,0},{4,6},{6,4},{8,10},{10,8},{12,14},{14,12},{16,18},{18,... | collective-permute-start | bytes 1572872 | tf_op jit(solution)/shard_map/ppermute | solution.py:379
  19.2 42.5 %collective-permute-start.4 = (bf16[256,1024]{1,0:T(8,128)(2,1)S(1)}, bf16[256,1024]{1,0:T(8,128)(2,1)S(1)}, u32[]{:S(2)}, u32[]{:S(2)}) collective-permute-start(bf16[256,1024]{1,0:T(8,128)(2,1)S(1)} %copy-done.1), channel_id=1, source_target_pairs={{0,4},{2,6},{4,0},{6,2},{8,12},{10,14},{12,8},{14,10},{16,20},{18,... | collective-permute-start | bytes 1572872 | tf_op jit(solution)/shard_map/ppermute | solution.py:379
  25.6 19.8 %collective-permute-start.12 = (bf16[256,512]{1,0:T(8,128)(2,1)S(1)}, bf16[256,512]{1,0:T(8,128)(2,1)S(1)}, u32[]{:S(2)}, u32[]{:S(2)}) collective-permute-start(bf16[256,512]{1,0:T(8,128)(2,1)S(1)} %get-tuple-element.58.refs_4_), channel_id=1, source_target_pairs={{8,16},{10,18},{12,20},{14,22},{16,8},{18,10},{20,12},{22,14},{9,1... | collective-permute-start | bytes 786440 | tf_op jit(solution)/shard_map/ppermute | solution.py:404
  26.3 36.1 %collective-permute-start.5 = (bf16[256,1024]{1,0:T(8,128)(2,1)S(1)}, bf16[256,1024]{1,0:T(8,128)(2,1)S(1)}, u32[]{:S(2)}, u32[]{:S(2)}) collective-permute-start(bf16[256,1024]{1,0:T(8,128)(2,1)S(1)} %copy-done.1), channel_id=1, source_target_pairs={{0,6},{2,4},{4,2},{6,0},{8,14},{10,12},{12,10},{14,8},{16,22},{18,... | collective-permute-start | bytes 1572872 | tf_op jit(solution)/shard_map/ppermute | solution.py:379
  27.9 15.9 %collective-permute-start.11 = (bf16[64,512]{1,0:T(8,128)(2,1)S(1)}, bf16[64,512]{1,0:T(8,128)(2,1)S(1)}, u32[]{:S(2)}, u32[]{:S(2)}) collective-permute-start(bf16[64,512]{1,0:T(8,128)(2,1)S(1)} %get-tuple-element.55), channel_id=1, source_target_pairs={{0,6},{2,4},{4,2},{6,0},{8,14},{10,12},{12,10},{14,8},{16,22},{18,... | collective-permute-start | bytes 196616 | tf_op jit(solution)/shard_map/ppermute | solution.py:379
  43.8 10.7 %collective-permute-start.6 = (bf16[256,512]{1,0:T(8,128)(2,1)S(1)}, bf16[256,512]{1,0:T(8,128)(2,1)S(1)}, u32[]{:S(2)}, u32[]{:S(2)}) collective-permute-start(bf16[256,512]{1,0:T(8,128)(2,1)S(1)} %get-tuple-element.58.refs_4_), channel_id=1, source_target_pairs={{0,8},{2,10},{4,12},{6,14},{8,0},{10,2},{12,4},{14,6},{16,24},{18,... | collective-permute-start | bytes 786440 | tf_op jit(solution)/shard_map/ppermute | solution.py:401
  45.4 17.0 %collective-permute-start.8 = (bf16[256,512]{1,0:T(8,128)(2,1)S(1)}, bf16[256,512]{1,0:T(8,128)(2,1)S(1)}, u32[]{:S(2)}, u32[]{:S(2)}) collective-permute-start(bf16[256,512]{1,0:T(8,128)(2,1)S(1)} %collective-permute-done.7.refs_6_), channel_id=1, source_target_pairs={{8,0},{10,2},{12,4},{14,6},{16,24},{18,26},{20,28},{22,30},{9,1},{... | collective-permute-start | bytes 786440 | tf_op jit(solution)/shard_map/ppermute | solution.py:403
  46.7 15.7 %copy-start.8 = (s32[8]{0:T(128)S(1)}, s32[8]{0:T(128)}, u32[]{:S(2)}) copy-start(s32[8]{0:T(128)} %len_ref.5) | copy-start | bytes 100
  54.4 6.0 %collective-permute-start.14 = (bf16[256,256]{1,0:T(8,128)(2,1)S(1)}, bf16[256,256]{1,0:T(8,128)(2,1)S(1)}, u32[]{:S(2)}, u32[]{:S(2)}) collective-permute-start(bf16[256,256]{1,0:T(8,128)(2,1)S(1)} %get-tuple-element.70.refs_4_), channel_id=1, source_target_pairs={{0,16},{2,18},{4,20},{6,22},{16,0},{18,2},{20,4},{22,6},{8,24},{10... | collective-permute-start | bytes 393224 | tf_op jit(solution)/shard_map/ppermute | solution.py:400
  60.4 15.9 %collective-permute-start.13 = (bf16[256,256]{1,0:T(8,128)(2,1)S(1)}, bf16[256,256]{1,0:T(8,128)(2,1)S(1)}, u32[]{:S(2)}, u32[]{:S(2)}) collective-permute-start(bf16[256,256]{1,0:T(8,128)(2,1)S(1)} %get-tuple-element.70.refs_4_), channel_id=1, source_target_pairs={{0,8},{2,10},{4,12},{6,14},{8,0},{10,2},{12,4},{14,6},{16,24},{18,... | collective-permute-start | bytes 393224 | tf_op jit(solution)/shard_map/ppermute | solution.py:401
  60.4 18.8 %collective-permute-start.15 = (bf16[256,256]{1,0:T(8,128)(2,1)S(1)}, bf16[256,256]{1,0:T(8,128)(2,1)S(1)}, u32[]{:S(2)}, u32[]{:S(2)}) collective-permute-start(bf16[256,256]{1,0:T(8,128)(2,1)S(1)} %collective-permute-done.14.refs_6_), channel_id=1, source_target_pairs={{8,0},{10,2},{12,4},{14,6},{16,24},{18,26},{20,28},{22,30},{9,1},{... | collective-permute-start | bytes 393224 | tf_op jit(solution)/shard_map/ppermute | solution.py:403
  61.7 17.5 %collective-permute-start.16 = (bf16[256,256]{1,0:T(8,128)(2,1)S(1)}, bf16[256,256]{1,0:T(8,128)(2,1)S(1)}, u32[]{:S(2)}, u32[]{:S(2)}) collective-permute-start(bf16[256,256]{1,0:T(8,128)(2,1)S(1)} %get-tuple-element.70.refs_4_), channel_id=1, source_target_pairs={{8,16},{10,18},{12,20},{14,22},{16,8},{18,10},{20,12},{22,14},{9,1... | collective-permute-start | bytes 393224 | tf_op jit(solution)/shard_map/ppermute | solution.py:404
  67.1 13.1 %collective-permute-start.17 = (bf16[144,256]{1,0:T(8,128)(2,1)S(1)}, bf16[144,256]{1,0:T(8,128)(2,1)S(1)}, u32[]{:S(2)}, u32[]{:S(2)}) collective-permute-start(bf16[144,256]{1,0:T(8,128)(2,1)S(1)} %get-tuple-element.71), channel_id=1, source_target_pairs={{0,8},{2,10},{4,12},{6,14},{8,16},{10,18},{12,20},{14,22},{16,24},... | collective-permute-start | bytes 221192 | tf_op jit(solution)/shard_map/ppermute | solution.py:382
  74.3 5.9 %collective-permute-start.18 = (bf16[144,256]{1,0:T(8,128)(2,1)S(1)}, bf16[144,256]{1,0:T(8,128)(2,1)S(1)}, u32[]{:S(2)}, u32[]{:S(2)}) collective-permute-start(bf16[144,256]{1,0:T(8,128)(2,1)S(1)} %get-tuple-element.71), channel_id=1, source_target_pairs={{0,16},{2,18},{4,20},{6,22},{8,24},{10,26},{12,28},{14,30},{1,17},... | collective-permute-start | bytes 221192 | tf_op jit(solution)/shard_map/ppermute | solution.py:382
  76.3 4.0 %collective-permute-start.19 = (bf16[144,256]{1,0:T(8,128)(2,1)S(1)}, bf16[144,256]{1,0:T(8,128)(2,1)S(1)}, u32[]{:S(2)}, u32[]{:S(2)}) collective-permute-start(bf16[144,256]{1,0:T(8,128)(2,1)S(1)} %get-tuple-element.71), channel_id=1, source_target_pairs={{0,24},{2,26},{4,28},{6,30},{1,25},{3,27},{5,29},{7,31}} | collective-permute-start | bytes 221192 | tf_op jit(solution)/shard_map/ppermute | solution.py:382
  77.6 1.6 %copy-start.7 = (f32[1024]{0:T(1024)S(1)}, f32[1024]{0:T(1024)}, u32[]{:S(2)}) copy-start(f32[1024]{0:T(1024)} %param.14) | copy-start | bytes 12292
  79.2 1.2 %copy-start = (f32[1024,256]{1,0:T(8,128)S(1)}, f32[1024,256]{1,0:T(8,128)}, u32[]{:S(2)}) copy-start(f32[1024,256]{1,0:T(8,128)} %get-tuple-element.66.carry_ref) | copy-start | bytes 3145732
  80.4 8.4 %copy-start.2 = (f32[31,1024]{1,0:T(8,128)S(1)}, f32[31,1024]{1,0:T(8,128)}, u32[]{:S(2)}) copy-start(f32[31,1024]{1,0:T(8,128)} %taps_ref.3) | copy-start | bytes 380932
  81.1 12.4 %collective-permute-start.20 = (bf16[16,256]{1,0:T(8,128)(2,1)S(1)}, bf16[16,256]{1,0:T(8,128)(2,1)S(1)}, u32[]{:S(2)}, u32[]{:S(2)}) collective-permute-start(bf16[16,256]{1,0:T(8,128)(2,1)S(1)} %get-tuple-element.73), channel_id=1, source_target_pairs={{0,8},{2,10},{4,12},{6,14},{8,16},{10,18},{12,20},{14,22},{16,24},... | collective-permute-start | bytes 24584 | tf_op jit(solution)/shard_map/ppermute | solution.py:382
  82.4 11.2 %collective-permute-start.21 = (bf16[16,256]{1,0:T(8,128)(2,1)S(1)}, bf16[16,256]{1,0:T(8,128)(2,1)S(1)}, u32[]{:S(2)}, u32[]{:S(2)}) collective-permute-start(bf16[16,256]{1,0:T(8,128)(2,1)S(1)} %get-tuple-element.74), channel_id=1, source_target_pairs={{8,0},{10,2},{12,4},{14,6},{16,8},{18,10},{20,12},{22,14},{24,16},... | collective-permute-start | bytes 24584 | tf_op jit(solution)/shard_map/ppermute | solution.py:385
  83.7 12.4 %collective-permute-start.24 = (bf16[256,256]{1,0:T(8,128)(2,1)S(1)}, bf16[256,256]{1,0:T(8,128)(2,1)S(1)}, u32[]{:S(2)}, u32[]{:S(2)}) collective-permute-start(bf16[256,256]{1,0:T(8,128)(2,1)S(1)} %get-tuple-element.78.refs_0_), channel_id=1, source_target_pairs={{0,16},{2,18},{4,20},{6,22},{16,0},{18,2},{20,4},{22,6},{8,24},{10... | collective-permute-start | bytes 393224 | tf_op jit(solution)/shard_map/ppermute | solution.py:400
  95.5 10.5 %collective-permute-start.22 = (bf16[1024,256]{1,0:T(8,128)(2,1)S(1)}, bf16[1024,256]{1,0:T(8,128)(2,1)S(1)}, u32[]{:S(2)}, u32[]{:S(2)}) collective-permute-start(bf16[1024,256]{1,0:T(8,128)(2,1)S(1)} %shard_map.100.refs_0_), channel_id=1, source_target_pairs={{0,1},{1,0},{2,3},{3,2},{4,5},{5,4},{6,7},{7,6},{8,9},{9,8},{10,11... | collective-permute-start | bytes 1572872 | tf_op jit(solution)/shard_map/ppermute | solution.py:388
  95.6 6.4 %collective-permute-start.23 = (bf16[256,256]{1,0:T(8,128)(2,1)S(1)}, bf16[256,256]{1,0:T(8,128)(2,1)S(1)}, u32[]{:S(2)}, u32[]{:S(2)}) collective-permute-start(bf16[256,256]{1,0:T(8,128)(2,1)S(1)} %get-tuple-element.78.refs_0_), channel_id=1, source_target_pairs={{0,8},{2,10},{4,12},{6,14},{8,0},{10,2},{12,4},{14,6},{16,24},{18,... | collective-permute-start | bytes 393224 | tf_op jit(solution)/shard_map/ppermute | solution.py:401
  96.1 8.2 %collective-permute-start.25 = (bf16[256,256]{1,0:T(8,128)(2,1)S(1)}, bf16[256,256]{1,0:T(8,128)(2,1)S(1)}, u32[]{:S(2)}, u32[]{:S(2)}) collective-permute-start(bf16[256,256]{1,0:T(8,128)(2,1)S(1)} %collective-permute-done.24.refs_2_), channel_id=1, source_target_pairs={{8,0},{10,2},{12,4},{14,6},{16,24},{18,26},{20,28},{22,30},{9,1},{... | collective-permute-start | bytes 393224 | tf_op jit(solution)/shard_map/ppermute | solution.py:403
  97.4 6.9 %collective-permute-start.26 = (bf16[256,256]{1,0:T(8,128)(2,1)S(1)}, bf16[256,256]{1,0:T(8,128)(2,1)S(1)}, u32[]{:S(2)}, u32[]{:S(2)}) collective-permute-start(bf16[256,256]{1,0:T(8,128)(2,1)S(1)} %get-tuple-element.78.refs_0_), channel_id=1, source_target_pairs={{8,16},{10,18},{12,20},{14,22},{16,8},{18,10},{20,12},{22,14},{9,1... | collective-permute-start | bytes 393224 | tf_op jit(solution)/shard_map/ppermute | solution.py:404
  104.4 1.6 %collective-permute-start.27 = (bf16[512,256]{1,0:T(8,128)(2,1)S(1)}, bf16[512,256]{1,0:T(8,128)(2,1)S(1)}, u32[]{:S(2)}, u32[]{:S(2)}) collective-permute-start(bf16[512,256]{1,0:T(8,128)(2,1)S(1)} %get-tuple-element.80), channel_id=1, source_target_pairs={{0,1},{1,0},{2,3},{3,2},{4,5},{5,4},{6,7},{7,6},{8,9},{9,8},{10,11... | collective-permute-start | bytes 786440 | tf_op jit(solution)/shard_map/ppermute | solution.py:388
  106.7 10.2 %collective-permute-start.30 = (bf16[256,512]{1,0:T(8,128)(2,1)S(1)}, bf16[256,512]{1,0:T(8,128)(2,1)S(1)}, u32[]{:S(2)}, u32[]{:S(2)}) collective-permute-start(bf16[256,512]{1,0:T(8,128)(2,1)S(1)} %get-tuple-element.84), channel_id=1, source_target_pairs={{0,6},{2,4},{4,2},{6,0},{8,14},{10,12},{12,10},{14,8},{16,22},{18,... | collective-permute-start | bytes 786440 | tf_op jit(solution)/shard_map/ppermute | solution.py:379
  107.7 13.7 %collective-permute-start.29 = (bf16[256,512]{1,0:T(8,128)(2,1)S(1)}, bf16[256,512]{1,0:T(8,128)(2,1)S(1)}, u32[]{:S(2)}, u32[]{:S(2)}) collective-permute-start(bf16[256,512]{1,0:T(8,128)(2,1)S(1)} %get-tuple-element.83), channel_id=1, source_target_pairs={{0,4},{2,6},{4,0},{6,2},{8,12},{10,14},{12,8},{14,10},{16,20},{18,... | collective-permute-start | bytes 786440 | tf_op jit(solution)/shard_map/ppermute | solution.py:379
  109.1 12.5 %collective-permute-start.28 = (bf16[256,512]{1,0:T(8,128)(2,1)S(1)}, bf16[256,512]{1,0:T(8,128)(2,1)S(1)}, u32[]{:S(2)}, u32[]{:S(2)}) collective-permute-start(bf16[256,512]{1,0:T(8,128)(2,1)S(1)} %get-tuple-element.82), channel_id=1, source_target_pairs={{0,2},{2,0},{4,6},{6,4},{8,10},{10,8},{12,14},{14,12},{16,18},{18,... | collective-permute-start | bytes 786440 | tf_op jit(solution)/shard_map/ppermute | solution.py:379

commit v3 on v2

--- a/solution.py
+++ b/solution.py
@@ -57,88 +57,98 @@
     return out
 
 
-def fill_planes(plane, dest_ref, pieces, offsets, lanes=slice(None)):
-    rows = pieces[0].shape[0]
-    for offset in sorted(set(offsets)):
-        same = [piece[:, lanes] for piece, at in zip(pieces, offsets) if at == offset]
-        value = same[0] if len(same) == 1 else same[0] + same[1]
-        dest_ref[pl.ds(pl.multiple_of((plane ^ offset) * rows, rows), rows), :] = value
-
-
-def pack_x_kernel(group, decay_ref, x_ref, bc_ref, *out_refs):
+def pack_kernel(group, *refs):
+    weight_refs, out_ref = refs[:-1], refs[-1]
+    width = weight_refs[0].shape[1] // group
+    for target in range(out_ref.shape[0]):
+        block = target % group
+        for number, weight_ref in enumerate(weight_refs):
+            columns = weight_ref[:, block * width : (block + 1) * width]
+            out_ref[target, :, number * width : (number + 1) * width] = columns
+
+
+def share_bc_kernel(group, decay_ref, *refs):
+    bc_refs, out_refs = refs[:-group], refs[-group:]
     place, _ = plane_place(group)
-    rows = x_ref.shape[0]
-    width = x_ref.shape[1] // group
-    frames = decay_ref.shape[2]
+    rows = bc_refs[0].shape[0]
+    below = len(bc_refs) * rows
     for step, out_ref in enumerate(out_refs):
-        block = place ^ step
-        out_ref[:rows, :width] = x_ref[:, pl.ds(pl.multiple_of(block * width, LANES), width)]
-        out_ref[:rows, width:] = bc_ref[...]
-        left = decay_ref[block]
+        for number, bc_ref in enumerate(bc_refs):
+            out_ref[number * rows : (number + 1) * rows, :] = bc_ref[...]
+        left = decay_ref[place ^ step]
         terms = []
         for _ in range(3):
             term = left.astype(BF16).astype(F32)
             terms.append(term)
             left = left - term
         terms.append(jnp.zeros_like(left))
-        out_ref[rows:, :frames] = jnp.concatenate(terms, axis=0).astype(BF16)
-        out_ref[rows:, frames:] = jnp.zeros((4 * 8, out_ref.shape[1] - frames), BF16)
-
-
-def stack_x_kernel(group, *refs):
-    parts, (stack_ref, decay_ref) = refs[:group], refs[group:]
-    place, _ = plane_place(group)
-    rows = stack_ref.shape[0] // group
-    frames = decay_ref.shape[2]
-    for step, part in enumerate(parts):
+        terms = jnp.concatenate(terms, axis=0).astype(BF16)
+        for span in range(terms.shape[1] // SPAN):
+            rows_here = slice(below + span * 32, below + (span + 1) * 32)
+            out_ref[rows_here, :] = terms[:, span * SPAN : (span + 1) * SPAN]
+
+
+def swap_kernel(group, rows, *refs):
+    part_refs, half_refs = refs[:group], refs[group : 2 * group - 1]
+    swap_ref, bc_ref, decay_ref = refs[2 * group - 1 :]
+    place, plane = plane_place(group)
+    planes = bc_ref.shape[0] // (group * rows)
+    below = planes * rows
+    spans = (part_refs[0].shape[0] - below) // 32
+    for step, part_ref in enumerate(part_refs):
         block = place ^ step
-        stack_ref[pl.ds(pl.multiple_of(block * rows, rows), rows), :] = part[:rows, :]
-        terms = part[rows:, :frames].astype(F32)
-        decay_ref[block] = terms[:8] + terms[8:16] + terms[16:24]
-
-
-def pack_zo_kernel(group, z_ref, out_w_ref, *out_refs):
-    place, _ = plane_place(group)
-    width = z_ref.shape[1] // group
-    for step, out_ref in enumerate(out_refs):
-        lanes = pl.ds(pl.multiple_of((place ^ step) * width, LANES), width)
-        out_ref[:, :width] = z_ref[:, lanes]
-        out_ref[:, width:] = out_w_ref[:, lanes]
-
-
-def stack_zo_kernel(group, *refs):
-    parts, (z_ref, o_ref) = refs[:group], refs[group:]
-    place, _ = plane_place(group)
-    rows, width = z_ref.shape[0] // group, z_ref.shape[1]
-    for step, part in enumerate(parts):
-        at = pl.ds(pl.multiple_of((place ^ step) * rows, rows), rows)
-        z_ref[at, :] = part[:, :width]
-        o_ref[at, :] = part[:, width:]
-
-
-def state_kernel(group, heads, state, offsets, len_ref, decay_ref, *refs):
-    frame_refs, refs = refs[:group], refs[group:]
-    pieces, refs = refs[: len(offsets)], refs[len(offsets) :]
-    x_ref, b_ref, c_ref, columns_ref, cumul_ref, step_ref, carry_ref, keep_ref, send_ref, weight_ref = refs
+        for offset in range(planes):
+            at = pl.multiple_of(((plane ^ offset) * group + block) * rows, rows)
+            bc_ref[pl.ds(at, rows), :] = part_ref[offset * rows : (offset + 1) * rows, :]
+        for span in range(spans):
+            terms = part_ref[below + span * 32 : below + (span + 1) * 32, :].astype(F32)
+            at = pl.multiple_of((block * spans + span) * 8, 8)
+            decay_ref[pl.ds(at, 8), :] = terms[:8] + terms[8:16] + terms[16:24]
+    half = half_refs[0].shape[0]
+    for number, half_ref in enumerate(half_refs):
+        swap_ref[number * half : (number + 1) * half, :] = half_ref[...]
+    top = len(half_refs) * half
+    height = swap_ref.shape[0] - top
+    for number in range(bc_ref.shape[0] // height):
+        lanes = slice(number * LANES, (number + 1) * LANES)
+        swap_ref[top:, lanes] = bc_ref[number * height : (number + 1) * height, :]
+
+
+def state_kernel(group, heads, state, len_ref, decay_ref, xz_ref, bc_half_ref, own_ref, swap_ref, *refs):
+    half_refs, refs = refs[: group - 1], refs[group - 1 :]
+    frames_ref, x_ref, b_ref, c_ref, columns_ref, cumul_ref, step_ref, carry_ref, keep_ref, send_ref, weight_ref = refs
     place, plane = plane_place(group)
-    frames = frame_refs[0].shape[0]
+    parity = lax.rem(lax.axis_index("head"), 2)
     total, width = x_ref.shape
+    frames = total // group
+    half = frames // 2
     head_size = width // heads
     count = total // SPAN
     base = plane * total
-    fill_planes(plane, weight_ref, pieces, offsets)
-    for step in range(group):
-        rows = pl.ds(pl.multiple_of((place ^ step) * frames, frames), frames)
-        product = dot(frame_refs[step][...], weight_ref[...])
+    frames_ref[pl.ds(pl.multiple_of(place * frames, frames), frames), :] = own_ref[...]
+    for number, half_ref in enumerate(half_refs):
+        block = (place ^ (number + 1)) * frames
+        mine = pl.ds(pl.multiple_of(block + parity * half, half), half)
+        other = pl.ds(pl.multiple_of(block + (1 - parity) * half, half), half)
+        frames_ref[mine, :] = half_ref[...]
+        frames_ref[other, :] = swap_ref[number * half : (number + 1) * half, :]
+    weight_ref[:, :width] = xz_ref[:, :width]
+    mine = pl.ds(pl.multiple_of(width + parity * LANES, LANES), LANES)
+    other = pl.ds(pl.multiple_of(width + (1 - parity) * LANES, LANES), LANES)
+    weight_ref[:, mine] = bc_half_ref[...]
+    top = len(half_refs) * half
+    height = swap_ref.shape[0] - top
+    for number in range(weight_ref.shape[0] // height):
+        lanes = slice(number * LANES, (number + 1) * LANES)
+        weight_ref[number * height : (number + 1) * height, other] = swap_ref[top:, lanes]
+    for block in range(group):
+        rows = slice(block * frames, (block + 1) * frames)
+        product = dot(frames_ref[rows, :], weight_ref[...])
         x_ref[rows, :] = product[:, :width].astype(BF16)
         b_ref[rows, :] = product[:, width : width + state].astype(BF16)
         c_ref[rows, :] = product[:, width + state :].astype(BF16)
 
-    spans = frames // SPAN
-    decay = jnp.concatenate(
-        [decay_ref[block // spans][:, block % spans * SPAN : (block % spans + 1) * SPAN] for block in range(count)],
-        axis=0,
-    )
+    decay = decay_ref[...]
     used = decay.shape[0]
     square = (SPAN, SPAN)
     row, lane = (lax.broadcasted_iota(jnp.int32, square, dim) for dim in (0, 1))
@@ -214,29 +224,14 @@
             )
 
 
-def silu_kernel(group, offsets, gain_ref, *refs):
-    frame_refs, refs = refs[:group], refs[group:]
-    pieces, (out_ref, weight_ref) = refs[: len(offsets)], refs[len(offsets) :]
-    place, plane = plane_place(group)
-    frames = frame_refs[0].shape[0]
-    width = weight_ref.shape[1]
+def silu_kernel(group, gain_ref, frames_ref, xz_ref, out_ref):
+    place, _ = plane_place(group)
+    total, width = out_ref.shape
     gain = gain_ref[:, pl.ds(pl.multiple_of(place * width, LANES), width)]
-    fill_planes(plane, weight_ref, pieces, offsets)
-    for step in range(group):
-        rows = pl.ds(pl.multiple_of((place ^ step) * frames, frames), frames)
-        z = dot(frame_refs[step][...], weight_ref[...]).astype(BF16).astype(F32)
+    for block in range(group):
+        rows = slice(block * (total // group), (block + 1) * (total // group))
+        z = dot(frames_ref[rows, :], xz_ref[:, width:]).astype(BF16).astype(F32)
         out_ref[rows, :] = z / (1.0 + jnp.exp(-z)) * gain
-
-
-def share_kernel(group, cores, offsets, *refs):
-    pieces, refs = refs[: len(offsets)], refs[len(offsets) :]
-    outs, weight_ref = refs[:cores], refs[cores]
-    _, plane = plane_place(group)
-    core = lax.axis_index("head")
-    fill_planes(plane, weight_ref, pieces, offsets)
-    for step, out_ref in enumerate(outs):
-        rows = out_ref.shape[0]
-        out_ref[...] = weight_ref[pl.ds(pl.multiple_of((core ^ step) * rows, rows), rows), :]
 
 
 def gate_kernel(heads, state, c_ref, y_ref, step_ref, carry_ref, keep_ref, silu_ref, *refs):
@@ -387,63 +382,55 @@
     def across(array, step):
         return lax.ppermute(array, "head", [(i, i ^ step) for i in range(cores)])
 
-    def along_planes(stack):
-        if planes != 4:
-            moved = [
-                lax.ppermute(stack, "tm", [(i, i ^ (step * group)) for i in range(times)]) for step in range(1, planes)
-            ]
-            return [stack, *moved], tuple(range(planes))
-
-        def pairs(chosen):
-            return [(a * group + q, b * group + q) for a, b in chosen for q in range(group)]
-
-        second = lax.ppermute(stack, "tm", pairs([(0, 2), (2, 0), (1, 3), (3, 1)]))
-        first = lax.ppermute(stack, "tm", pairs([(0, 1), (1, 0), (2, 3), (3, 2)]))
-        again, stack_then = lax.optimization_barrier((second, stack))
-        third = lax.ppermute(again, "tm", pairs([(1, 0), (2, 3)]))
-        middle = lax.ppermute(stack_then, "tm", pairs([(1, 2), (2, 1)]))
-        return [stack, first, second, third, middle], (0, 1, 2, 3, 3)
+    def between_planes(array, step):
+        return lax.ppermute(array, "tm", [(i, i ^ (step * group)) for i in range(times)])
 
     shape = jax.ShapeDtypeStruct
     rows = x_weight.shape[0]
+    parity = lax.rem(core, 2)
+
+    def to_owners(*weights):
+        blocks = call(
+            functools.partial(pack_kernel, group),
+            shape((times, rows, len(weights) * width), BF16),
+            list(weights),
+            smem=0,
+        )
+        moved = lax.all_to_all(blocks, "tm", split_axis=0, concat_axis=0, tiled=True)
+        return moved.reshape(times * rows, -1)
+
+    xz = to_owners(x_weight, z_weight)
+    bc_half = lax.dynamic_slice_in_dim(bc_weight, parity * LANES, LANES, 1)
+    bc_pieces = [bc_half] + [between_planes(bc_half, step) for step in range(1, planes)]
+    half_count = frame_count // 2
+    frame_half = lax.dynamic_slice_in_dim(frames, parity * half_count, half_count, 0)
+    half_parts = [in_plane(frame_half, step) for step in range(1, group)]
     decay_blocks = jnp.pad(log_decay.reshape(group, heads, frame_count), ((0, 0), (0, 8 - heads), (0, 0)))
-    packed = call(
-        functools.partial(pack_x_kernel, group),
-        tuple(shape((rows + 32, width + 2 * state), BF16) for _ in range(group)),
-        [decay_blocks, x_weight, bc_weight],
+    bc_parts = call(
+        functools.partial(share_bc_kernel, group),
+        tuple(shape((planes * rows + frame_count // SPAN * 32, LANES), BF16) for _ in range(group)),
+        [decay_blocks, *bc_pieces],
         smem=0,
     )
-    parts = [packed[0]] + [in_plane(packed[step], step) for step in range(1, group)]
-    frame_parts = [frames] + [in_plane(frames, step) for step in range(1, group)]
-    stack, decay = call(
-        functools.partial(stack_x_kernel, group),
-        (shape((group * rows, width + 2 * state), BF16), shape((group, 8, frame_count), F32)),
-        parts,
+    bc_parts = [bc_parts[0]] + [in_plane(bc_parts[step], step) for step in range(1, group)]
+    height = depth * LANES // depth
+    swap, bc_mine, decay = call(
+        functools.partial(swap_kernel, group, rows),
+        (
+            shape(((group - 1) * half_count + height, depth), BF16),
+            shape((depth, LANES), BF16),
+            shape((count * 8, SPAN), F32),
+        ),
+        [*bc_parts, *half_parts],
         smem=0,
     )
-    x_pieces, offsets = along_planes(stack)
-
-    packed = call(
-        functools.partial(pack_zo_kernel, group),
-        tuple(shape((rows, 2 * width), BF16) for _ in range(group)),
-        [z_weight, out_weight.T],
-        smem=0,
-    )
-    parts = [packed[0]] + [in_plane(packed[step], step) for step in range(1, group)]
-    z_stack, o_stack = call(
-        functools.partial(stack_zo_kernel, group),
-        (shape((group * rows, width), BF16), shape((group * rows, width), BF16)),
-        parts,
-        smem=0,
-    )
-    (z_stack, o_stack), x_last = lax.optimization_barrier(((z_stack, o_stack), x_pieces[-1]))
-    x_pieces = [*x_pieces[:-1], x_last]
-    z_pieces, _ = along_planes(z_stack)
+    swap = across(swap, 1)
 
     used = count * 8
-    x_rows, b_rows, c_rows, decays, cumul, steps, carry, keep, summary = call(
-        functools.partial(state_kernel, group, heads, state, offsets),
+    frame_rows, x_rows, b_rows, c_rows, decays, cumul, steps, carry, keep, summary = call(
+        functools.partial(state_kernel, group, heads, state),
         (
+            shape((total, depth), BF16),
             shape((total, width), BF16),
             shape((total, state), BF16),
             shape((total, state), BF16),
@@ -454,7 +441,7 @@
             shape((count * 8, width), F32),
             shape((state + EDGE, width), BF16),
         ),
-        [record_lengths, decay, *frame_parts, *x_pieces],
+        [record_lengths, decay, xz, bc_mine, frames, swap, *half_parts],
         [pltpu.VMEM((depth, width + 2 * state), BF16)],
         flops=2 * total * depth * (width + 2 * state),
     )
@@ -467,15 +454,12 @@
         smem=0,
     )
     silu = call(
-        functools.partial(silu_kernel, group, offsets),
+        functools.partial(silu_kernel, group),
         shape((total, width), F32),
-        [norm_gain[None], *frame_parts, *z_pieces],
-        [pltpu.VMEM((depth, width), BF16)],
+        [norm_gain[None], frame_rows, xz],
         flops=2 * total * depth * width,
         smem=0,
     )
-    o_stack, z_last = lax.optimization_barrier((o_stack, z_pieces[-1]))
-    o_pieces, _ = along_planes(o_stack)
     gated, top, bottom = call(
         functools.partial(gate_kernel, heads, state),
         (shape((total, width), BF16), shape((EDGE, width), BF16), shape((EDGE, width), BF16)),
@@ -499,15 +483,13 @@
         [pltpu.VMEM((2 * SPAN + 4 * EDGE, width), F32), ends],
         flops=4 * SPAN * width * conv_weight.shape[0],
     )
+    out_columns, _ = lax.optimization_barrier((out_weight.T, xz))
+    out_rows = to_owners(out_columns)
     share = depth // cores
-    out_parts = call(
-        functools.partial(share_kernel, group, cores, offsets),
-        tuple(shape((share, width), BF16) for _ in range(cores)),
-        o_pieces,
-        [pltpu.VMEM((depth, width), BF16)],
-        smem=0,
-    )
-    out_parts = [out_parts[0]] + [across(out_parts[step], step) for step in range(1, cores)]
+    out_parts = [lax.dynamic_slice_in_dim(out_rows, core * share, share, 0)]
+    for step in range(1, cores):
+        sent = lax.dynamic_slice_in_dim(out_rows, (core ^ step) * share, share, 0)
+        out_parts.append(across(sent, step))
     acts = [act] + [across(act, step) for step in range(1, cores)]
     outs = call(
         functools.partial(out_kernel, group, cores),

time: 123 us -> 107 us (0.87)
  waiting for transfers between devices: 58.1 us -> 32.5 us
  starting transfers between devices: 44.2 us -> 50.9 us
  Pallas kernels: 15.4 us -> 19.3 us
  local copies, waits for them, and re-layouts: 3.53 us -> 1.94 us
    ppermute x12 -> x9, waiting for transfers between devices: 31.3 us -> 15.6 us  [in_plane(): return lax.ppermute(array, 'tm', [(i, i ^ step) for i in range(times)])]
    all_to_all x0 -> x2, starting transfers between devices: none -> 13.3 us  [to_owners(): lax.all_to_all(blocks, 'tm', split_axis=0, concat_axis=0, tiled=True)]
    ppermute x12 -> x3, waiting for transfers between devices: 25.3 us -> 15.2 us  [between_planes(): lax.ppermute(array, 'tm', [(i, i ^ step * group) for i in range(times)])]
    ppermute x12 -> x3, starting transfers between devices: 15.8 us -> 8.01 us  [between_planes(): lax.ppermute(array, 'tm', [(i, i ^ step * group) for i in range(times)])]
    pallas_call x12 -> x11, Pallas kernels: 15.4 us -> 19.3 us  [call(): pl.pallas_call(kernel, out_shape=out_shape, in_specs=in_specs, out_specs=...]
    ppermute x4, starting transfers between devices: 11.7 us -> 14.6 us  [later(): lax.ppermute(array, 'tm', [(i, i + step * group) for i in range(times - s...]
    ppermute x12 -> x9, starting transfers between devices: 15.2 us -> 13 us  [in_plane(): return lax.ppermute(array, 'tm', [(i, i ^ step) for i in range(times)])]
    unnamed x18 -> x20, local copies, waits for them, and re-layouts: 2.74 us -> 1.85 us
  transfers between devices with their start and end apart: 31 -> 22, of which waited for: 13 -> 8; matrix products, arithmetic and copies ran while one was open for 0% -> 0% of each run, Pallas kernels for 11% -> 17%
where the time goes in v3:
time: 107 us; the launch traced here: 106 us
  starting transfers between devices  50.9 us (48%)
  waiting for transfers between devices  32.5 us (30%)
  Pallas kernels  19.3 us (18%)
  local copies, waits for them, and re-layouts  1.94 us (2%)
    pallas_call x11, Pallas kernels, call(): pl.pallas_call(kernel, out_shape=out_shape, in_specs=in_specs, out_specs=...  19.3 us
    ppermute x9, waiting for transfers between devices, in_plane(): return lax.ppermute(array, 'tm', [(i, i ^ step) for i in range(times)])  15.6 us
    ppermute x3, waiting for transfers between devices, between_planes(): lax.ppermute(array, 'tm', [(i, i ^ step * group) for i in range(times)])  15.2 us
    ppermute x4, starting transfers between devices, later(): lax.ppermute(array, 'tm', [(i, i + step * group) for i in range(times - s...  14.6 us
    all_to_all x2, starting transfers between devices, to_owners(): lax.all_to_all(blocks, 'tm', split_axis=0, concat_axis=0, tiled=True)  13.3 us
    ppermute x9, starting transfers between devices, in_plane(): return lax.ppermute(array, 'tm', [(i, i ^ step) for i in range(times)])  13 us
    ppermute x3, starting transfers between devices, between_planes(): lax.ppermute(array, 'tm', [(i, i ^ step * group) for i in range(times)])  8.01 us
  transfers between devices with their start and end apart: 22, of which 8 were waited for; matrix products, arithmetic and copies ran while one was open for 0% of the time, Pallas kernels for 17%

profile of v3, /device:TPU:0, one launch (start us, length us, event | category | flops | bytes accessed | tf_op | source)
XLA Modules:
  0.0 105.8 jit_solution(15209127831806522847)
XLA Ops:
  0.0 0.9 copy-done.3
  0.9 0.9 copy-done.4
  1.8 1.1 shard_map.93
  2.9 8.4 %all-to-all-start = ((bf16[16,64,512]{2,1,0:T(8,128)(2,1)}), bf16[16,64,512]{2,1,0:T(8,128)(2,1)S(1)}, u32[]{:S(2)}, u32[]{:S(2)}) async-start(bf16[16,64,512]{2,1,0:T(8,128)(2,1)} %shard_map.93), calls=%async_computation | async-start | bytes 2097152 | tf_op jit(solution)/shard_map/all_to_all | solution.py:399
  11.3 0.0 copy-start.8
  11.4 2.0 %collective-permute-start.6 = (bf16[128,1024]{1,0:T(8,128)(2,1)S(1)}, bf16[128,1024]{1,0:T(8,128)(2,1)S(1)}, u32[]{:S(2)}, u32[]{:S(2)}) collective-permute-start(bf16[128,1024]{1,0:T(8,128)(2,1)S(1)} %constant_dynamic-slice_fusion.2), channel_id=1, source_target_pairs={{0,2},{2,0},{4,6},{6,4},{8,10},{10,8},{12,14},{14,12},{16,18},{18,... | collective-permute-start | bytes 786440 | tf_op jit(solution)/shard_map/ppermute | solution.py:374
  13.4 1.5 %collective-permute-start.7 = (bf16[128,1024]{1,0:T(8,128)(2,1)S(1)}, bf16[128,1024]{1,0:T(8,128)(2,1)S(1)}, u32[]{:S(2)}, u32[]{:S(2)}) collective-permute-start(bf16[128,1024]{1,0:T(8,128)(2,1)S(1)} %constant_dynamic-slice_fusion.2), channel_id=1, source_target_pairs={{0,4},{2,6},{4,0},{6,2},{8,12},{10,14},{12,8},{14,10},{16,20},{18,... | collective-permute-start | bytes 786440 | tf_op jit(solution)/shard_map/ppermute | solution.py:374
  14.8 0.1 collective-permute-start.8
  15.0 1.9 %collective-permute-start = (bf16[64,128]{1,0:T(8,128)(2,1)S(1)}, bf16[64,128]{1,0:T(8,128)(2,1)S(1)}, u32[]{:S(2)}, u32[]{:S(2)}) collective-permute-start(bf16[64,128]{1,0:T(8,128)(2,1)S(1)} %constant_dynamic-slice_fusion.3.refs_0_), channel_id=1, source_target_pairs={{0,8},{2,10},{4,12},{6,14},{8,0},{10,2},{12,4},{14,6},{16,24},{18,... | collective-permute-start | bytes 49160 | tf_op jit(solution)/shard_map/ppermute | solution.py:386
  16.9 2.4 %collective-permute-start.1 = (bf16[64,128]{1,0:T(8,128)(2,1)S(1)}, bf16[64,128]{1,0:T(8,128)(2,1)S(1)}, u32[]{:S(2)}, u32[]{:S(2)}) collective-permute-start(bf16[64,128]{1,0:T(8,128)(2,1)S(1)} %constant_dynamic-slice_fusion.3.refs_0_), channel_id=1, source_target_pairs={{0,16},{2,18},{4,20},{6,22},{8,24},{10,26},{12,28},{14,30},{16,0},... | collective-permute-start | bytes 49160 | tf_op jit(solution)/shard_map/ppermute | solution.py:386
  19.2 9.6 %collective-permute-done.refs_1_ = bf16[64,128]{1,0:T(8,128)(2,1)S(1)} collective-permute-done((bf16[64,128]{1,0:T(8,128)(2,1)S(1)}, bf16[64,128]{1,0:T(8,128)(2,1)S(1)}, u32[]{:S(2)}, u32[]{:S(2)}) %collective-permute-start) | collective-permute-done | bytes 16416 | tf_op jit(solution)/shard_map/ppermute | solution.py:386
  28.9 3.7 %collective-permute-start.2 = (bf16[64,128]{1,0:T(8,128)(2,1)S(1)}, bf16[64,128]{1,0:T(8,128)(2,1)S(1)}, u32[]{:S(2)}, u32[]{:S(2)}) collective-permute-start(bf16[64,128]{1,0:T(8,128)(2,1)S(1)} %constant_dynamic-slice_fusion.3.refs_0_), channel_id=1, source_target_pairs={{0,24},{2,26},{4,28},{6,30},{8,16},{10,18},{12,20},{14,22},{16,8},... | collective-permute-start | bytes 49160 | tf_op jit(solution)/shard_map/ppermute | solution.py:386
  32.6 5.6 %collective-permute-done.1.refs_2_ = bf16[64,128]{1,0:T(8,128)(2,1)S(1)} collective-permute-done((bf16[64,128]{1,0:T(8,128)(2,1)S(1)}, bf16[64,128]{1,0:T(8,128)(2,1)S(1)}, u32[]{:S(2)}, u32[]{:S(2)}) %collective-permute-start.1) | collective-permute-done | bytes 16416 | tf_op jit(solution)/shard_map/ppermute | solution.py:386
  38.3 1.5 %collective-permute-start.3 = (bf16[320,128]{1,0:T(8,128)(2,1)S(1)}, bf16[320,128]{1,0:T(8,128)(2,1)S(1)}, u32[]{:S(2)}, u32[]{:S(2)}) collective-permute-start(bf16[320,128]{1,0:T(8,128)(2,1)S(1)} %get-tuple-element.31), channel_id=1, source_target_pairs={{0,2},{2,0},{4,6},{6,4},{8,10},{10,8},{12,14},{14,12},{16,18},{18,... | collective-permute-start | bytes 245768 | tf_op jit(solution)/shard_map/ppermute | solution.py:374
  39.8 1.7 %collective-permute-start.4 = (bf16[320,128]{1,0:T(8,128)(2,1)S(1)}, bf16[320,128]{1,0:T(8,128)(2,1)S(1)}, u32[]{:S(2)}, u32[]{:S(2)}) collective-permute-start(bf16[320,128]{1,0:T(8,128)(2,1)S(1)} %get-tuple-element.32), channel_id=1, source_target_pairs={{0,4},{2,6},{4,0},{6,2},{8,12},{10,14},{12,8},{14,10},{16,20},{18,... | collective-permute-start | bytes 245768 | tf_op jit(solution)/shard_map/ppermute | solution.py:374
  41.5 1.3 %collective-permute-done.3.refs_1_ = bf16[320,128]{1,0:T(8,128)(2,1)S(1)} collective-permute-done((bf16[320,128]{1,0:T(8,128)(2,1)S(1)}, bf16[320,128]{1,0:T(8,128)(2,1)S(1)}, u32[]{:S(2)}, u32[]{:S(2)}) %collective-permute-start.3) | collective-permute-done | bytes 81952 | tf_op jit(solution)/shard_map/ppermute | solution.py:374
  42.8 2.8 %collective-permute-start.5 = (bf16[320,128]{1,0:T(8,128)(2,1)S(1)}, bf16[320,128]{1,0:T(8,128)(2,1)S(1)}, u32[]{:S(2)}, u32[]{:S(2)}) collective-permute-start(bf16[320,128]{1,0:T(8,128)(2,1)S(1)} %get-tuple-element.33), channel_id=1, source_target_pairs={{0,6},{2,4},{4,2},{6,0},{8,14},{10,12},{12,10},{14,8},{16,22},{18,... | collective-permute-start | bytes 245768 | tf_op jit(solution)/shard_map/ppermute | solution.py:374
  45.5 2.6 %collective-permute-done.5.refs_3_ = bf16[320,128]{1,0:T(8,128)(2,1)S(1)} collective-permute-done((bf16[320,128]{1,0:T(8,128)(2,1)S(1)}, bf16[320,128]{1,0:T(8,128)(2,1)S(1)}, u32[]{:S(2)}, u32[]{:S(2)}) %collective-permute-start.5) | collective-permute-done | bytes 81952 | tf_op jit(solution)/shard_map/ppermute | solution.py:374
  48.1 1.1 %shard_map.92 = (bf16[512,1024]{1,0:T(8,128)(2,1)}, bf16[1024,128]{1,0:T(8,128)(2,1)S(1)}, f32[64,128]{1,0:T(8,128)S(1)}) custom-call(bf16[320,128]{1,0:T(8,128)(2,1)S(1)} %get-tuple-element.30.refs_0_, bf16[320,128]{1,0:T(8,128)(2,1)S(1)} %collective-permute-done.3.refs_1_, bf16[320,128]{1,0:T(8,128)(2,1)S(1)} %collective-permute-done.4.refs_2_, ...), custom_call_target="tpu_custom_call" | custom-call | bytes 2457600 | tf_op jit(solution)/shard_map/pallas_call | solution.py:27
  49.3 0.0 collective-permute-start.9
  49.3 0.0 all-to-all-done
  49.3 0.8 shard_map.100
  50.1 4.9 %all-to-all-start.1 = ((bf16[16,64,256]{2,1,0:T(8,128)(2,1)}), bf16[16,64,256]{2,1,0:T(8,128)(2,1)S(1)}, u32[]{:S(2)}, u32[]{:S(2)}) async-start(bf16[16,64,256]{2,1,0:T(8,128)(2,1)} %shard_map.100), calls=%async_computation.1 | async-start | bytes 1048576 | tf_op jit(solution)/shard_map/all_to_all | solution.py:399
  55.0 0.0 collective-permute-done.9.swap_ref
  55.0 4.7 %shard_map.94 = (bf16[1024,1024]{1,0:T(8,128)(2,1)}, bf16[1024,256]{1,0:T(8,128)(2,1)S(1)}, bf16[1024,128]{1,0:T(8,128)(2,1)S(1)}, bf16[1024,128]{1,0:T(8,128)(2...) custom-call(s32[8]{0:T(128)S(1)} %copy-done.8, ...), custom_call_target="tpu_custom_call" | custom-call | flops 1073741824 | bytes 9248800 | tf_op jit(solution)/shard_map/pallas_call | solution.py:27
  59.7 0.0 copy-start.7
  59.7 4.0 %collective-permute-start.10 = (bf16[144,256]{1,0:T(8,128)(2,1)S(1)}, bf16[144,256]{1,0:T(8,128)(2,1)S(1)}, u32[]{:S(2)}, u32[]{:S(2)}) collective-permute-start(bf16[144,256]{1,0:T(8,128)(2,1)S(1)} %get-tuple-element.46), channel_id=1, source_target_pairs={{0,8},{2,10},{4,12},{6,14},{8,16},{10,18},{12,20},{14,22},{16,24},... | collective-permute-start | bytes 221192 | tf_op jit(solution)/shard_map/ppermute | solution.py:377
  63.7 4.3 %collective-permute-start.11 = (bf16[144,256]{1,0:T(8,128)(2,1)S(1)}, bf16[144,256]{1,0:T(8,128)(2,1)S(1)}, u32[]{:S(2)}, u32[]{:S(2)}) collective-permute-start(bf16[144,256]{1,0:T(8,128)(2,1)S(1)} %get-tuple-element.46), channel_id=1, source_target_pairs={{0,16},{2,18},{4,20},{6,22},{8,24},{10,26},{12,28},{14,30},{1,17},... | collective-permute-start | bytes 221192 | tf_op jit(solution)/shard_map/ppermute | solution.py:377
  68.0 1.3 %collective-permute-start.12 = (bf16[144,256]{1,0:T(8,128)(2,1)S(1)}, bf16[144,256]{1,0:T(8,128)(2,1)S(1)}, u32[]{:S(2)}, u32[]{:S(2)}) collective-permute-start(bf16[144,256]{1,0:T(8,128)(2,1)S(1)} %get-tuple-element.46), channel_id=1, source_target_pairs={{0,24},{2,26},{4,28},{6,30},{1,25},{3,27},{5,29},{7,31}} | collective-permute-start | bytes 221192 | tf_op jit(solution)/shard_map/ppermute | solution.py:377
  69.3 1.5 %shard_map.95.y_ref = f32[1024,256]{1,0:T(8,128)S(1)} custom-call(bf16[1024,256]{1,0:T(8,128)(2,1)S(1)} %get-tuple-element.38.x_ref, bf16[1024,128]{1,0:T(8,128)(2,1)S(1)} %get-tuple-element.39.b_ref, bf16[1024,128]{1,0:T(8,128)(2,1)S(1)} %get-tuple-element.37.c_ref, f32[128,256]{1,0:T(8,128)S(1)} %get-tuple-element.40.columns_ref, ...), custom_call_target="tpu_custom_call" | custom-call | flops 134217728 | bytes 2260992 | tf_op jit(solution)/shard_map/pallas_call | solution.py:27
  70.9 0.9 shard_map.96.silu_ref
  71.8 0.0 copy-start.2
  71.8 0.6 shard_map.97
  72.5 5.1 %collective-permute-start.13 = (bf16[16,256]{1,0:T(8,128)(2,1)S(1)}, bf16[16,256]{1,0:T(8,128)(2,1)S(1)}, u32[]{:S(2)}, u32[]{:S(2)}) collective-permute-start(bf16[16,256]{1,0:T(8,128)(2,1)S(1)} %get-tuple-element.48), channel_id=1, source_target_pairs={{0,8},{2,10},{4,12},{6,14},{8,16},{10,18},{12,20},{14,22},{16,24},... | collective-permute-start | bytes 24584 | tf_op jit(solution)/shard_map/ppermute | solution.py:377
  77.6 1.3 %collective-permute-start.14 = (bf16[16,256]{1,0:T(8,128)(2,1)S(1)}, bf16[16,256]{1,0:T(8,128)(2,1)S(1)}, u32[]{:S(2)}, u32[]{:S(2)}) collective-permute-start(bf16[16,256]{1,0:T(8,128)(2,1)S(1)} %get-tuple-element.49), channel_id=1, source_target_pairs={{8,0},{10,2},{12,4},{14,6},{16,8},{18,10},{20,12},{22,14},{24,16},... | collective-permute-start | bytes 24584 | tf_op jit(solution)/shard_map/ppermute | solution.py:380
  78.9 6.2 %shard_map.98.refs_2_ = bf16[768,256]{1,0:T(8,128)(2,1)S(1)} custom-call(s32[8]{0:T(128)S(1)} %copy-done.8, f32[31,1024]{1,0:T(8,128)S(1)} %copy-done.2, bf16[1024,256]{1,0:T(8,128)(2,1)S(1)} %get-tuple-element.47.gated_ref), custom_call_target="tpu_custom_call" | custom-call | flops 16252928 | bytes 1044512 | tf_op jit(solution)/shard_map/pallas_call | solution.py:27
  85.1 1.5 %shard_map.99.refs_0_ = bf16[1024,256]{1,0:T(8,128)(2,1)S(1)} custom-call(s32[8]{0:T(128)S(1)} %copy-done.8, f32[31,1024]{1,0:T(8,128)S(1)} %copy-done.2, bf16[1024,256]{1,0:T(8,128)(2,1)S(1)} %get-tuple-element.47.gated_ref, bf16[16,256]{1,0:T(8,128)(2,1)S(1)} %collective-permute-done.13.refs_0_, bf16[16,256]{1,0:T(8,128)(2,1)S(1)} %collective-permute-done.14.refs_1_, ...), custom_call_target="tpu_custom_call" | custom-call | flops 4063232 | bytes 1585184 | tf_op jit(solution)/shard_map/pallas_call | solution.py:27
  86.7 0.1 collective-permute-start.15
  86.8 0.5 collective-permute-start.16
  87.4 1.3 %collective-permute-done.15.refs_1_ = bf16[1024,256]{1,0:T(8,128)(2,1)S(1)} collective-permute-done((bf16[1024,256]{1,0:T(8,128)(2,1)S(1)}, bf16[1024,256]{1,0:T(8,128)(2,1)S(1)}, u32[]{:S(2)}, u32[]{:S(2)}) %collective-permute-start.15) | collective-permute-done | bytes 524320 | tf_op jit(solution)/shard_map/ppermute | solution.py:383
  88.6 0.4 collective-permute-done.16.refs_3_
  89.0 0.7 shard_map.101
  89.8 1.5 %collective-permute-start.17 = (bf16[256,512]{1,0:T(8,128)(2,1)S(1)}, bf16[256,512]{1,0:T(8,128)(2,1)S(1)}, u32[]{:S(2)}, u32[]{:S(2)}) collective-permute-start(bf16[256,512]{1,0:T(8,128)(2,1)S(1)} %get-tuple-element.52), channel_id=1, source_target_pairs={{0,2},{2,0},{4,6},{6,4},{8,10},{10,8},{12,14},{14,12},{16,18},{18,... | collective-permute-start | bytes 786440 | tf_op jit(solution)/shard_map/ppermute | solution.py:374
  91.3 1.5 %collective-permute-start.18 = (bf16[256,512]{1,0:T(8,128)(2,1)S(1)}, bf16[256,512]{1,0:T(8,128)(2,1)S(1)}, u32[]{:S(2)}, u32[]{:S(2)}) collective-permute-start(bf16[256,512]{1,0:T(8,128)(2,1)S(1)} %get-tuple-element.53), channel_id=1, source_target_pairs={{0,4},{2,6},{4,0},{6,2},{8,12},{10,14},{12,8},{14,10},{16,20},{18,... | collective-permute-start | bytes 786440 | tf_op jit(solution)/shard_map/ppermute | solution.py:374
  92.8 0.6 collective-permute-start.19
  93.3 5.7 %collective-permute-done.17 = bf16[256,512]{1,0:T(8,128)(2,1)S(1)} collective-permute-done((bf16[256,512]{1,0:T(8,128)(2,1)S(1)}, bf16[256,512]{1,0:T(8,128)(2,1)S(1)}, u32[]{:S(2)}, u32[]{:S(2)}) %collective-permute-start.17) | collective-permute-done | bytes 262176 | tf_op jit(solution)/shard_map/ppermute | solution.py:374
  99.0 6.0 %collective-permute-done.18 = bf16[256,512]{1,0:T(8,128)(2,1)S(1)} collective-permute-done((bf16[256,512]{1,0:T(8,128)(2,1)S(1)}, bf16[256,512]{1,0:T(8,128)(2,1)S(1)}, u32[]{:S(2)}, u32[]{:S(2)}) %collective-permute-start.18) | collective-permute-done | bytes 262176 | tf_op jit(solution)/shard_map/ppermute | solution.py:374
  105.0 0.8 add_convert_fusion
  (33 shorter events, 0.2 us)
Async XLA Ops:
  0.0 15.0 %copy-start = (bf16[64,256]{1,0:T(8,128)(2,1)S(1)}, bf16[64,256]{1,0:T(8,128)(2,1)}, u32[]{:S(2)}) copy-start(bf16[64,256]{1,0:T(8,128)(2,1)} %param.12) | copy-start | bytes 98308
  0.0 0.9 copy-start.3
  0.9 0.9 copy-start.4
  1.8 9.5 %copy-start.6 = (bf16[256,1024]{1,0:T(8,128)(2,1)S(1)}, bf16[256,1024]{1,0:T(8,128)(2,1)}, u32[]{:S(2)}) copy-start(bf16[256,1024]{1,0:T(8,128)(2,1)} %own_ref.1) | copy-start | bytes 1572868
  1.8 30.8 %copy-start.9 = (f32[16,256]{1,0:T(8,128)S(1)}, f32[16,256]{1,0:T(8,128)}, u32[]{:S(2)}) copy-start(f32[16,256]{1,0:T(8,128)} %param.13) | copy-start | bytes 49156
  2.9 46.4 %copy-start.5 = (bf16[1024,64]{0,1:T(8,128)(2,1)S(1)}, bf16[1024,64]{0,1:T(8,128)(2,1)}, u32[]{:S(2)}) copy-start(bf16[1024,64]{0,1:T(8,128)(2,1)} %param.16) | copy-start | bytes 393220
  2.9 46.4 %all-to-all-start = ((bf16[16,64,512]{2,1,0:T(8,128)(2,1)}), bf16[16,64,512]{2,1,0:T(8,128)(2,1)S(1)}, u32[]{:S(2)}, u32[]{:S(2)}) async-start(bf16[16,64,512]{2,1,0:T(8,128)(2,1)} %shard_map.93), calls=%async_computation | async-start | bytes 2097152 | tf_op jit(solution)/shard_map/all_to_all | solution.py:399
  11.3 43.7 %copy-start.8 = (s32[8]{0:T(128)S(1)}, s32[8]{0:T(128)}, u32[]{:S(2)}) copy-start(s32[8]{0:T(128)} %len_ref.5) | copy-start | bytes 100
  11.4 36.7 %collective-permute-start.6 = (bf16[128,1024]{1,0:T(8,128)(2,1)S(1)}, bf16[128,1024]{1,0:T(8,128)(2,1)S(1)}, u32[]{:S(2)}, u32[]{:S(2)}) collective-permute-start(bf16[128,1024]{1,0:T(8,128)(2,1)S(1)} %constant_dynamic-slice_fusion.2), channel_id=1, source_target_pairs={{0,2},{2,0},{4,6},{6,4},{8,10},{10,8},{12,14},{14,12},{16,18},{18,... | collective-permute-start | bytes 786440 | tf_op jit(solution)/shard_map/ppermute | solution.py:374
  13.4 34.8 %collective-permute-start.7 = (bf16[128,1024]{1,0:T(8,128)(2,1)S(1)}, bf16[128,1024]{1,0:T(8,128)(2,1)S(1)}, u32[]{:S(2)}, u32[]{:S(2)}) collective-permute-start(bf16[128,1024]{1,0:T(8,128)(2,1)S(1)} %constant_dynamic-slice_fusion.2), channel_id=1, source_target_pairs={{0,4},{2,6},{4,0},{6,2},{8,12},{10,14},{12,8},{14,10},{16,20},{18,... | collective-permute-start | bytes 786440 | tf_op jit(solution)/shard_map/ppermute | solution.py:374
  14.8 33.3 %collective-permute-start.8 = (bf16[128,1024]{1,0:T(8,128)(2,1)S(1)}, bf16[128,1024]{1,0:T(8,128)(2,1)S(1)}, u32[]{:S(2)}, u32[]{:S(2)}) collective-permute-start(bf16[128,1024]{1,0:T(8,128)(2,1)S(1)} %constant_dynamic-slice_fusion.2), channel_id=1, source_target_pairs={{0,6},{2,4},{4,2},{6,0},{8,14},{10,12},{12,10},{14,8},{16,22},{18,... | collective-permute-start | bytes 786440 | tf_op jit(solution)/shard_map/ppermute | solution.py:374
  15.0 13.9 %collective-permute-start = (bf16[64,128]{1,0:T(8,128)(2,1)S(1)}, bf16[64,128]{1,0:T(8,128)(2,1)S(1)}, u32[]{:S(2)}, u32[]{:S(2)}) collective-permute-start(bf16[64,128]{1,0:T(8,128)(2,1)S(1)} %constant_dynamic-slice_fusion.3.refs_0_), channel_id=1, source_target_pairs={{0,8},{2,10},{4,12},{6,14},{8,0},{10,2},{12,4},{14,6},{16,24},{18,... | collective-permute-start | bytes 49160 | tf_op jit(solution)/shard_map/ppermute | solution.py:386
  16.9 21.4 %collective-permute-start.1 = (bf16[64,128]{1,0:T(8,128)(2,1)S(1)}, bf16[64,128]{1,0:T(8,128)(2,1)S(1)}, u32[]{:S(2)}, u32[]{:S(2)}) collective-permute-start(bf16[64,128]{1,0:T(8,128)(2,1)S(1)} %constant_dynamic-slice_fusion.3.refs_0_), channel_id=1, source_target_pairs={{0,16},{2,18},{4,20},{6,22},{8,24},{10,26},{12,28},{14,30},{16,0},... | collective-permute-start | bytes 49160 | tf_op jit(solution)/shard_map/ppermute | solution.py:386
  28.9 9.4 %collective-permute-start.2 = (bf16[64,128]{1,0:T(8,128)(2,1)S(1)}, bf16[64,128]{1,0:T(8,128)(2,1)S(1)}, u32[]{:S(2)}, u32[]{:S(2)}) collective-permute-start(bf16[64,128]{1,0:T(8,128)(2,1)S(1)} %constant_dynamic-slice_fusion.3.refs_0_), channel_id=1, source_target_pairs={{0,24},{2,26},{4,28},{6,30},{8,16},{10,18},{12,20},{14,22},{16,8},... | collective-permute-start | bytes 49160 | tf_op jit(solution)/shard_map/ppermute | solution.py:386
  38.3 4.5 %collective-permute-start.3 = (bf16[320,128]{1,0:T(8,128)(2,1)S(1)}, bf16[320,128]{1,0:T(8,128)(2,1)S(1)}, u32[]{:S(2)}, u32[]{:S(2)}) collective-permute-start(bf16[320,128]{1,0:T(8,128)(2,1)S(1)} %get-tuple-element.31), channel_id=1, source_target_pairs={{0,2},{2,0},{4,6},{6,4},{8,10},{10,8},{12,14},{14,12},{16,18},{18,... | collective-permute-start | bytes 245768 | tf_op jit(solution)/shard_map/ppermute | solution.py:374
  39.8 5.7 %collective-permute-start.4 = (bf16[320,128]{1,0:T(8,128)(2,1)S(1)}, bf16[320,128]{1,0:T(8,128)(2,1)S(1)}, u32[]{:S(2)}, u32[]{:S(2)}) collective-permute-start(bf16[320,128]{1,0:T(8,128)(2,1)S(1)} %get-tuple-element.32), channel_id=1, source_target_pairs={{0,4},{2,6},{4,0},{6,2},{8,12},{10,14},{12,8},{14,10},{16,20},{18,... | collective-permute-start | bytes 245768 | tf_op jit(solution)/shard_map/ppermute | solution.py:374
  42.8 5.3 %collective-permute-start.5 = (bf16[320,128]{1,0:T(8,128)(2,1)S(1)}, bf16[320,128]{1,0:T(8,128)(2,1)S(1)}, u32[]{:S(2)}, u32[]{:S(2)}) collective-permute-start(bf16[320,128]{1,0:T(8,128)(2,1)S(1)} %get-tuple-element.33), channel_id=1, source_target_pairs={{0,6},{2,4},{4,2},{6,0},{8,14},{10,12},{12,10},{14,8},{16,22},{18,... | collective-permute-start | bytes 245768 | tf_op jit(solution)/shard_map/ppermute | solution.py:374
  49.3 5.7 %collective-permute-start.9 = (bf16[512,1024]{1,0:T(8,128)(2,1)}, bf16[512,1024]{1,0:T(8,128)(2,1)}, u32[]{:S(2)}, u32[]{:S(2)}) collective-permute-start(bf16[512,1024]{1,0:T(8,128)(2,1)} %get-tuple-element.36), channel_id=1, source_target_pairs={{0,1},{1,0},{2,3},{3,2},{4,5},{5,4},{6,7},{7,6},{8,9},{9,8},{10,11... | collective-permute-start | bytes 3145736 | tf_op jit(solution)/shard_map/ppermute | solution.py:383
  50.1 36.7 %all-to-all-start.1 = ((bf16[16,64,256]{2,1,0:T(8,128)(2,1)}), bf16[16,64,256]{2,1,0:T(8,128)(2,1)S(1)}, u32[]{:S(2)}, u32[]{:S(2)}) async-start(bf16[16,64,256]{2,1,0:T(8,128)(2,1)} %shard_map.100), calls=%async_computation.1 | async-start | bytes 1048576 | tf_op jit(solution)/shard_map/all_to_all | solution.py:399
  59.7 11.1 %copy-start.1 = (bf16[1024,1024]{1,0:T(8,128)(2,1)S(1)}, bf16[1024,1024]{1,0:T(8,128)(2,1)}, u32[]{:S(2)}) copy-start(bf16[1024,1024]{1,0:T(8,128)(2,1)} %get-tuple-element.45.frames_ref) | copy-start | bytes 6291460
  59.7 11.1 %copy-start.7 = (f32[1024]{0:T(1024)S(1)}, f32[1024]{0:T(1024)}, u32[]{:S(2)}) copy-start(f32[1024]{0:T(1024)} %param.14) | copy-start | bytes 12292
  59.7 12.0 %collective-permute-start.10 = (bf16[144,256]{1,0:T(8,128)(2,1)S(1)}, bf16[144,256]{1,0:T(8,128)(2,1)S(1)}, u32[]{:S(2)}, u32[]{:S(2)}) collective-permute-start(bf16[144,256]{1,0:T(8,128)(2,1)S(1)} %get-tuple-element.46), channel_id=1, source_target_pairs={{0,8},{2,10},{4,12},{6,14},{8,16},{10,18},{12,20},{14,22},{16,24},... | collective-permute-start | bytes 221192 | tf_op jit(solution)/shard_map/ppermute | solution.py:377
  63.7 8.1 %collective-permute-start.11 = (bf16[144,256]{1,0:T(8,128)(2,1)S(1)}, bf16[144,256]{1,0:T(8,128)(2,1)S(1)}, u32[]{:S(2)}, u32[]{:S(2)}) collective-permute-start(bf16[144,256]{1,0:T(8,128)(2,1)S(1)} %get-tuple-element.46), channel_id=1, source_target_pairs={{0,16},{2,18},{4,20},{6,22},{8,24},{10,26},{12,28},{14,30},{1,17},... | collective-permute-start | bytes 221192 | tf_op jit(solution)/shard_map/ppermute | solution.py:377
  68.0 3.8 %collective-permute-start.12 = (bf16[144,256]{1,0:T(8,128)(2,1)S(1)}, bf16[144,256]{1,0:T(8,128)(2,1)S(1)}, u32[]{:S(2)}, u32[]{:S(2)}) collective-permute-start(bf16[144,256]{1,0:T(8,128)(2,1)S(1)} %get-tuple-element.46), channel_id=1, source_target_pairs={{0,24},{2,26},{4,28},{6,30},{1,25},{3,27},{5,29},{7,31}} | collective-permute-start | bytes 221192 | tf_op jit(solution)/shard_map/ppermute | solution.py:377
  71.8 7.1 %copy-start.2 = (f32[31,1024]{1,0:T(8,128)S(1)}, f32[31,1024]{1,0:T(8,128)}, u32[]{:S(2)}) copy-start(f32[31,1024]{1,0:T(8,128)} %taps_ref.3) | copy-start | bytes 380932
  72.5 12.6 %collective-permute-start.13 = (bf16[16,256]{1,0:T(8,128)(2,1)S(1)}, bf16[16,256]{1,0:T(8,128)(2,1)S(1)}, u32[]{:S(2)}, u32[]{:S(2)}) collective-permute-start(bf16[16,256]{1,0:T(8,128)(2,1)S(1)} %get-tuple-element.48), channel_id=1, source_target_pairs={{0,8},{2,10},{4,12},{6,14},{8,16},{10,18},{12,20},{14,22},{16,24},... | collective-permute-start | bytes 24584 | tf_op jit(solution)/shard_map/ppermute | solution.py:377
  77.6 7.5 %collective-permute-start.14 = (bf16[16,256]{1,0:T(8,128)(2,1)S(1)}, bf16[16,256]{1,0:T(8,128)(2,1)S(1)}, u32[]{:S(2)}, u32[]{:S(2)}) collective-permute-start(bf16[16,256]{1,0:T(8,128)(2,1)S(1)} %get-tuple-element.49), channel_id=1, source_target_pairs={{8,0},{10,2},{12,4},{14,6},{16,8},{18,10},{20,12},{22,14},{24,16},... | collective-permute-start | bytes 24584 | tf_op jit(solution)/shard_map/ppermute | solution.py:380
  86.7 2.0 %collective-permute-start.15 = (bf16[1024,256]{1,0:T(8,128)(2,1)S(1)}, bf16[1024,256]{1,0:T(8,128)(2,1)S(1)}, u32[]{:S(2)}, u32[]{:S(2)}) collective-permute-start(bf16[1024,256]{1,0:T(8,128)(2,1)S(1)} %shard_map.99.refs_0_), channel_id=1, source_target_pairs={{0,1},{1,0},{2,3},{3,2},{4,5},{5,4},{6,7},{7,6},{8,9},{9,8},{10,11... | collective-permute-start | bytes 1572872 | tf_op jit(solution)/shard_map/ppermute | solution.py:383
  86.8 2.2 %collective-permute-start.16 = (bf16[512,256]{1,0:T(8,128)(2,1)S(1)}, bf16[512,256]{1,0:T(8,128)(2,1)S(1)}, u32[]{:S(2)}, u32[]{:S(2)}) collective-permute-start(bf16[512,256]{1,0:T(8,128)(2,1)S(1)} %get-tuple-element.55), channel_id=1, source_target_pairs={{0,1},{1,0},{2,3},{3,2},{4,5},{5,4},{6,7},{7,6},{8,9},{9,8},{10,11... | collective-permute-start | bytes 786440 | tf_op jit(solution)/shard_map/ppermute | solution.py:383
  89.8 9.2 %collective-permute-start.17 = (bf16[256,512]{1,0:T(8,128)(2,1)S(1)}, bf16[256,512]{1,0:T(8,128)(2,1)S(1)}, u32[]{:S(2)}, u32[]{:S(2)}) collective-permute-start(bf16[256,512]{1,0:T(8,128)(2,1)S(1)} %get-tuple-element.52), channel_id=1, source_target_pairs={{0,2},{2,0},{4,6},{6,4},{8,10},{10,8},{12,14},{14,12},{16,18},{18,... | collective-permute-start | bytes 786440 | tf_op jit(solution)/shard_map/ppermute | solution.py:374
  91.3 13.7 %collective-permute-start.18 = (bf16[256,512]{1,0:T(8,128)(2,1)S(1)}, bf16[256,512]{1,0:T(8,128)(2,1)S(1)}, u32[]{:S(2)}, u32[]{:S(2)}) collective-permute-start(bf16[256,512]{1,0:T(8,128)(2,1)S(1)} %get-tuple-element.53), channel_id=1, source_target_pairs={{0,4},{2,6},{4,0},{6,2},{8,12},{10,14},{12,8},{14,10},{16,20},{18,... | collective-permute-start | bytes 786440 | tf_op jit(solution)/shard_map/ppermute | solution.py:374
  92.8 12.2 %collective-permute-start.19 = (bf16[256,512]{1,0:T(8,128)(2,1)S(1)}, bf16[256,512]{1,0:T(8,128)(2,1)S(1)}, u32[]{:S(2)}, u32[]{:S(2)}) collective-permute-start(bf16[256,512]{1,0:T(8,128)(2,1)S(1)} %get-tuple-element.54), channel_id=1, source_target_pairs={{0,6},{2,4},{4,2},{6,0},{8,14},{10,12},{12,10},{14,8},{16,22},{18,... | collective-permute-start | bytes 786440 | tf_op jit(solution)/shard_map/ppermute | solution.py:374

commit v4 on v3

--- a/solution.py
+++ b/solution.py
@@ -57,14 +57,35 @@
     return out
 
 
+def fill_planes(plane, dest_ref, pieces, offsets, lanes=slice(None)):
+    rows = pieces[0].shape[0]
+    for offset in sorted(set(offsets)):
+        same = [piece[:, lanes] for piece, at in zip(pieces, offsets) if at == offset]
+        value = same[0] if len(same) == 1 else same[0] + same[1]
+        dest_ref[pl.ds(pl.multiple_of((plane ^ offset) * rows, rows), rows), : value.shape[1]] = value
+
+
 def pack_kernel(group, *refs):
-    weight_refs, out_ref = refs[:-1], refs[-1]
+    weight_refs, out_refs = refs[:-group], refs[-group:]
     width = weight_refs[0].shape[1] // group
-    for target in range(out_ref.shape[0]):
-        block = target % group
+    place, _ = plane_place(group)
+    for step, out_ref in enumerate(out_refs):
+        lanes = pl.ds(pl.multiple_of((place ^ step) * width, LANES), width)
         for number, weight_ref in enumerate(weight_refs):
-            columns = weight_ref[:, block * width : (block + 1) * width]
-            out_ref[target, :, number * width : (number + 1) * width] = columns
+            out_ref[:, number * width : (number + 1) * width] = weight_ref[:, lanes]
+
+
+def stack_kernel(group, *refs):
+    parts, stack_refs = refs[:group], refs[group:]
+    place, _ = plane_place(group)
+    rows = parts[0].shape[0]
+    for step, part in enumerate(parts):
+        at = pl.ds(pl.multiple_of((place ^ step) * rows, rows), rows)
+        first = 0
+        for stack_ref in stack_refs:
+            width = stack_ref.shape[1]
+            stack_ref[at, :] = part[:, first : first + width]
+            first += width
 
 
 def share_bc_kernel(group, decay_ref, *refs):
@@ -114,9 +135,10 @@
         swap_ref[top:, lanes] = bc_ref[number * height : (number + 1) * height, :]
 
 
-def state_kernel(group, heads, state, len_ref, decay_ref, xz_ref, bc_half_ref, own_ref, swap_ref, *refs):
+def state_kernel(group, heads, state, offsets, len_ref, decay_ref, bc_half_ref, own_ref, swap_ref, *refs):
     half_refs, refs = refs[: group - 1], refs[group - 1 :]
-    frames_ref, x_ref, b_ref, c_ref, columns_ref, cumul_ref, step_ref, carry_ref, keep_ref, send_ref, weight_ref = refs
+    pieces, refs = refs[: len(offsets)], refs[len(offsets) :]
+    frames_ref, z_ref, x_ref, b_ref, c_ref, columns_ref, cumul_ref, step_ref, carry_ref, keep_ref, send_ref, weight_ref = refs
     place, plane = plane_place(group)
     parity = lax.rem(lax.axis_index("head"), 2)
     total, width = x_ref.shape
@@ -132,7 +154,8 @@
         other = pl.ds(pl.multiple_of(block + (1 - parity) * half, half), half)
         frames_ref[mine, :] = half_ref[...]
         frames_ref[other, :] = swap_ref[number * half : (number + 1) * half, :]
-    weight_ref[:, :width] = xz_ref[:, :width]
+    fill_planes(plane, weight_ref, pieces, offsets, slice(0, width))
+    fill_planes(plane, z_ref, pieces, offsets, slice(width, 2 * width))
     mine = pl.ds(pl.multiple_of(width + parity * LANES, LANES), LANES)
     other = pl.ds(pl.multiple_of(width + (1 - parity) * LANES, LANES), LANES)
     weight_ref[:, mine] = bc_half_ref[...]
@@ -224,14 +247,25 @@
             )
 
 
-def silu_kernel(group, gain_ref, frames_ref, xz_ref, out_ref):
+def silu_kernel(group, gain_ref, frames_ref, weight_ref, out_ref):
     place, _ = plane_place(group)
     total, width = out_ref.shape
     gain = gain_ref[:, pl.ds(pl.multiple_of(place * width, LANES), width)]
     for block in range(group):
         rows = slice(block * (total // group), (block + 1) * (total // group))
-        z = dot(frames_ref[rows, :], xz_ref[:, width:]).astype(BF16).astype(F32)
+        z = dot(frames_ref[rows, :], weight_ref[...]).astype(BF16).astype(F32)
         out_ref[rows, :] = z / (1.0 + jnp.exp(-z)) * gain
+
+
+def share_kernel(cores, offsets, group, *refs):
+    pieces, refs = refs[: len(offsets)], refs[len(offsets) :]
+    outs, weight_ref = refs[:cores], refs[cores]
+    _, plane = plane_place(group)
+    core = lax.axis_index("head")
+    fill_planes(plane, weight_ref, pieces, offsets)
+    for step, out_ref in enumerate(outs):
+        rows = out_ref.shape[0]
+        out_ref[...] = weight_ref[pl.ds(pl.multiple_of((core ^ step) * rows, rows), rows), :]
 
 
 def gate_kernel(heads, state, c_ref, y_ref, step_ref, carry_ref, keep_ref, silu_ref, *refs):
@@ -389,22 +423,36 @@
     rows = x_weight.shape[0]
     parity = lax.rem(core, 2)
 
-    def to_owners(*weights):
-        blocks = call(
-            functools.partial(pack_kernel, group),
-            shape((times, rows, len(weights) * width), BF16),
-            list(weights),
-            smem=0,
-        )
-        moved = lax.all_to_all(blocks, "tm", split_axis=0, concat_axis=0, tiled=True)
-        return moved.reshape(times * rows, -1)
-
-    xz = to_owners(x_weight, z_weight)
+    def along_planes(stack):
+        if planes != 4:
+            return [stack] + [between_planes(stack, step) for step in range(1, planes)], tuple(range(planes))
+
+        def pairs(chosen):
+            return [(a * group + q, b * group + q) for a, b in chosen for q in range(group)]
+
+        second = between_planes(stack, 2)
+        first = between_planes(stack, 1)
+        again, stack_then = lax.optimization_barrier((second, stack))
+        third = lax.ppermute(again, "tm", pairs([(1, 0), (2, 3)]))
+        middle = lax.ppermute(stack_then, "tm", pairs([(1, 2), (2, 1)]))
+        return [stack, first, second, third, middle], (0, 1, 2, 3, 3)
+
     bc_half = lax.dynamic_slice_in_dim(bc_weight, parity * LANES, LANES, 1)
     bc_pieces = [bc_half] + [between_planes(bc_half, step) for step in range(1, planes)]
-    half_count = frame_count // 2
-    frame_half = lax.dynamic_slice_in_dim(frames, parity * half_count, half_count, 0)
-    half_parts = [in_plane(frame_half, step) for step in range(1, group)]
+    packed = call(
+        functools.partial(pack_kernel, group),
+        tuple(shape((rows, 3 * width), BF16) for _ in range(group)),
+        [x_weight, z_weight, out_weight.T],
+        smem=0,
+    )
+    parts = [packed[0]] + [in_plane(packed[step], step) for step in range(1, group)]
+    xz_stack, out_stack = call(
+        functools.partial(stack_kernel, group),
+        (shape((group * rows, 2 * width), BF16), shape((group * rows, width), BF16)),
+        parts,
+        smem=0,
+    )
+    xz_pieces, offsets = along_planes(xz_stack)
     decay_blocks = jnp.pad(log_decay.reshape(group, heads, frame_count), ((0, 0), (0, 8 - heads), (0, 0)))
     bc_parts = call(
         functools.partial(share_bc_kernel, group),
@@ -413,6 +461,10 @@
         smem=0,
     )
     bc_parts = [bc_parts[0]] + [in_plane(bc_parts[step], step) for step in range(1, group)]
+    half_count = frame_count // 2
+    frame_half = lax.dynamic_slice_in_dim(frames, parity * half_count, half_count, 0)
+    frame_half, out_stack, bc_parts = lax.optimization_barrier((frame_half, out_stack, bc_parts))
+    half_parts = [in_plane(frame_half, step) for step in range(1, group)]
     height = depth * LANES // depth
     swap, bc_mine, decay = call(
         functools.partial(swap_kernel, group, rows),
@@ -427,10 +479,11 @@
     swap = across(swap, 1)
 
     used = count * 8
-    frame_rows, x_rows, b_rows, c_rows, decays, cumul, steps, carry, keep, summary = call(
-        functools.partial(state_kernel, group, heads, state),
+    frame_rows, z_columns, x_rows, b_rows, c_rows, decays, cumul, steps, carry, keep, summary = call(
+        functools.partial(state_kernel, group, heads, state, offsets),
         (
             shape((total, depth), BF16),
+            shape((depth, width), BF16),
             shape((total, width), BF16),
             shape((total, state), BF16),
             shape((total, state), BF16),
@@ -441,7 +494,7 @@
             shape((count * 8, width), F32),
             shape((state + EDGE, width), BF16),
         ),
-        [record_lengths, decay, xz, bc_mine, frames, swap, *half_parts],
+        [record_lengths, decay, bc_mine, frames, swap, *half_parts, *xz_pieces],
         [pltpu.VMEM((depth, width + 2 * state), BF16)],
         flops=2 * total * depth * (width + 2 * state),
     )
@@ -453,10 +506,12 @@
         flops=4 * total * SPAN * width,
         smem=0,
     )
+    out_stack, y = lax.optimization_barrier((out_stack, y))
+    out_pieces = [out_stack] + [between_planes(out_stack, step) for step in range(1, planes)]
     silu = call(
         functools.partial(silu_kernel, group),
         shape((total, width), F32),
-        [norm_gain[None], frame_rows, xz],
+        [norm_gain[None], frame_rows, z_columns],
         flops=2 * total * depth * width,
         smem=0,
     )
@@ -483,13 +538,15 @@
         [pltpu.VMEM((2 * SPAN + 4 * EDGE, width), F32), ends],
         flops=4 * SPAN * width * conv_weight.shape[0],
     )
-    out_columns, _ = lax.optimization_barrier((out_weight.T, xz))
-    out_rows = to_owners(out_columns)
     share = depth // cores
-    out_parts = [lax.dynamic_slice_in_dim(out_rows, core * share, share, 0)]
-    for step in range(1, cores):
-        sent = lax.dynamic_slice_in_dim(out_rows, (core ^ step) * share, share, 0)
-        out_parts.append(across(sent, step))
+    out_parts = call(
+        functools.partial(share_kernel, cores, tuple(range(planes)), group),
+        tuple(shape((share, width), BF16) for _ in range(cores)),
+        out_pieces,
+        [pltpu.VMEM((depth, width), BF16)],
+        smem=0,
+    )
+    out_parts = [out_parts[0]] + [across(out_parts[step], step) for step in range(1, cores)]
     acts = [act] + [across(act, step) for step in range(1, cores)]
     outs = call(
         functools.partial(out_kernel, group, cores),

time: 107 us -> 123 us (1.15)
  waiting for transfers between devices: 32.5 us -> 53.8 us
  starting transfers between devices: 50.9 us -> 45.5 us
  local copies, waits for them, and re-layouts: 1.94 us -> 5.65 us
  Pallas kernels: 19.3 us -> 16.8 us
    all_to_all x2 -> x0, starting transfers between devices: 13.3 us -> none  [to_owners(): lax.all_to_all(blocks, 'tm', split_axis=0, concat_axis=0, tiled=True)]
    ppermute x0 -> x2, waiting for transfers between devices: none -> 7.71 us  [the longest x1 7.71 us: along_planes(): third = lax.ppermute(again, 'tm', pairs([(1, 0), (2, 3)]))]
    ppermute x3 -> x8, waiting for transfers between devices: 15.2 us -> 22.2 us  [between_planes(): lax.ppermute(array, 'tm', [(i, i ^ step * group) for i in range(times)])]
    ppermute x9 -> x12, waiting for transfers between devices: 15.6 us -> 22.3 us  [in_plane(): return lax.ppermute(array, 'tm', [(i, i ^ step) for i in range(times)])]
    ppermute x3 -> x8, starting transfers between devices: 8.01 us -> 13 us  [between_planes(): lax.ppermute(array, 'tm', [(i, i ^ step * group) for i in range(times)])]
    ppermute x9 -> x12, starting transfers between devices: 13 us -> 15.7 us  [in_plane(): return lax.ppermute(array, 'tm', [(i, i ^ step) for i in range(times)])]
    pallas_call x11 -> x12, Pallas kernels: 19.3 us -> 16.8 us  [call(): pl.pallas_call(kernel, out_shape=out_shape, in_specs=in_specs, out_specs=...]
    unnamed x20 -> x22, local copies, waits for them, and re-layouts: 1.85 us -> 3.95 us
  transfers between devices with their start and end apart: 22 -> 30, of which waited for: 8 -> 14; matrix products, arithmetic and copies ran while one was open for 0% -> 1% of each run, Pallas kernels for 17% -> 6%
where the time goes in v4:
time: 123 us
  waiting for transfers between devices  53.8 us (44%)
  starting transfers between devices  45.5 us (37%)
  Pallas kernels  16.8 us (14%)
  local copies, waits for them, and re-layouts  5.65 us (5%)
    ppermute x12, waiting for transfers between devices, in_plane(): return lax.ppermute(array, 'tm', [(i, i ^ step) for i in range(times)])  22.3 us
    ppermute x8, waiting for transfers between devices, between_planes(): lax.ppermute(array, 'tm', [(i, i ^ step * group) for i in range(times)])  22.2 us
    pallas_call x12, Pallas kernels, call(): pl.pallas_call(kernel, out_shape=out_shape, in_specs=in_specs, out_specs=...  16.8 us
    ppermute x12, starting transfers between devices, in_plane(): return lax.ppermute(array, 'tm', [(i, i ^ step) for i in range(times)])  15.7 us
    ppermute x4, starting transfers between devices, later(): lax.ppermute(array, 'tm', [(i, i + step * group) for i in range(times - s...  13.4 us
    ppermute x8, starting transfers between devices, between_planes(): lax.ppermute(array, 'tm', [(i, i ^ step * group) for i in range(times)])  13 us
    ppermute x1, waiting for transfers between devices, along_planes(): third = lax.ppermute(again, 'tm', pairs([(1, 0), (2, 3)]))  7.71 us
    unnamed x22, local copies, waits for them, and re-layouts  3.95 us
  transfers between devices with their start and end apart: 30, of which 14 were waited for; matrix products, arithmetic and copies ran while one was open for 1% of the time, Pallas kernels for 6%

profile of v4, /device:TPU:0, one launch (start us, length us, event | category | flops | bytes accessed | tf_op | source)
XLA Modules:
  0.0 122.9 jit_solution(5716492986532001854)
XLA Ops:
  0.0 0.9 copy-done.4
  0.9 0.9 copy-done.5
  1.8 0.9 copy-done.6
  2.8 3.0 %collective-permute-start = (bf16[64,768]{1,0:T(8,128)(2,1)S(1)}, bf16[64,768]{1,0:T(8,128)(2,1)S(1)}, u32[]{:S(2)}, u32[]{:S(2)}) collective-permute-start(bf16[64,768]{1,0:T(8,128)(2,1)S(1)} %get-tuple-element.49), channel_id=1, source_target_pairs={{0,2},{2,0},{4,6},{6,4},{8,10},{10,8},{12,14},{14,12},{16,18},{18,... | collective-permute-start | bytes 294920 | tf_op jit(solution)/shard_map/ppermute | solution.py:408
  5.8 3.6 %collective-permute-start.5 = (bf16[64,128]{1,0:T(8,128)(2,1)S(1)}, bf16[64,128]{1,0:T(8,128)(2,1)S(1)}, u32[]{:S(2)}, u32[]{:S(2)}) collective-permute-start(bf16[64,128]{1,0:T(8,128)(2,1)S(1)} %constant_dynamic-slice_fusion.refs_0_), channel_id=1, source_target_pairs={{0,24},{2,26},{4,28},{6,30},{8,16},{10,18},{12,20},{14,22},{16,8},... | collective-permute-start | bytes 49160 | tf_op jit(solution)/shard_map/ppermute | solution.py:420
  9.4 0.8 collective-permute-start.3
  10.2 1.5 %collective-permute-start.1 = (bf16[64,768]{1,0:T(8,128)(2,1)S(1)}, bf16[64,768]{1,0:T(8,128)(2,1)S(1)}, u32[]{:S(2)}, u32[]{:S(2)}) collective-permute-start(bf16[64,768]{1,0:T(8,128)(2,1)S(1)} %get-tuple-element.50), channel_id=1, source_target_pairs={{0,4},{2,6},{4,0},{6,2},{8,12},{10,14},{12,8},{14,10},{16,20},{18,... | collective-permute-start | bytes 294920 | tf_op jit(solution)/shard_map/ppermute | solution.py:408
  11.7 0.7 reshape.3
  13.0 1.0 collective-permute-done.4.refs_2_
  14.7 1.5 %collective-permute-start.7 = (bf16[320,128]{1,0:T(8,128)(2,1)S(1)}, bf16[320,128]{1,0:T(8,128)(2,1)S(1)}, u32[]{:S(2)}, u32[]{:S(2)}) collective-permute-start(bf16[320,128]{1,0:T(8,128)(2,1)S(1)} %get-tuple-element.55), channel_id=1, source_target_pairs={{0,4},{2,6},{4,0},{6,2},{8,12},{10,14},{12,8},{14,10},{16,20},{18,... | collective-permute-start | bytes 245768 | tf_op jit(solution)/shard_map/ppermute | solution.py:408
  16.2 1.4 %collective-permute-start.8 = (bf16[320,128]{1,0:T(8,128)(2,1)S(1)}, bf16[320,128]{1,0:T(8,128)(2,1)S(1)}, u32[]{:S(2)}, u32[]{:S(2)}) collective-permute-start(bf16[320,128]{1,0:T(8,128)(2,1)S(1)} %get-tuple-element.56), channel_id=1, source_target_pairs={{0,6},{2,4},{4,2},{6,0},{8,14},{10,12},{12,10},{14,8},{16,22},{18,... | collective-permute-start | bytes 245768 | tf_op jit(solution)/shard_map/ppermute | solution.py:408
  17.6 1.0 constant_dynamic-slice_fusion.1
  18.9 0.9 collective-permute-done.7.refs_2_
  19.8 1.8 %collective-permute-done.8.refs_3_ = bf16[320,128]{1,0:T(8,128)(2,1)S(1)} collective-permute-done((bf16[320,128]{1,0:T(8,128)(2,1)S(1)}, bf16[320,128]{1,0:T(8,128)(2,1)S(1)}, u32[]{:S(2)}, u32[]{:S(2)}) %collective-permute-start.8) | collective-permute-done | bytes 81952 | tf_op jit(solution)/shard_map/ppermute | solution.py:408
  21.5 1.4 %collective-permute-start.11 = (bf16[128,1024]{1,0:T(8,128)(2,1)S(1)}, bf16[128,1024]{1,0:T(8,128)(2,1)S(1)}, u32[]{:S(2)}, u32[]{:S(2)}) collective-permute-start(bf16[128,1024]{1,0:T(8,128)(2,1)S(1)} %constant_dynamic-slice_fusion.1), channel_id=1, source_target_pairs={{0,6},{2,4},{4,2},{6,0},{8,14},{10,12},{12,10},{14,8},{16,22},{18,... | collective-permute-start | bytes 786440 | tf_op jit(solution)/shard_map/ppermute | solution.py:408
  23.0 1.5 %collective-permute-start.10 = (bf16[128,1024]{1,0:T(8,128)(2,1)S(1)}, bf16[128,1024]{1,0:T(8,128)(2,1)S(1)}, u32[]{:S(2)}, u32[]{:S(2)}) collective-permute-start(bf16[128,1024]{1,0:T(8,128)(2,1)S(1)} %constant_dynamic-slice_fusion.1), channel_id=1, source_target_pairs={{0,4},{2,6},{4,0},{6,2},{8,12},{10,14},{12,8},{14,10},{16,20},{18,... | collective-permute-start | bytes 786440 | tf_op jit(solution)/shard_map/ppermute | solution.py:408
  25.0 6.0 %collective-permute-done.11.refs_6_.refs_2_ = bf16[128,1024]{1,0:T(8,128)(2,1)S(1)} collective-permute-done((bf16[128,1024]{1,0:T(8,128)(2,1)S(1)}, bf16[128,1024]{1,0:T(8,128)(2,1)S(1)}, u32[]{:S(2)}, u32[]{:S(2)}) %collective-permute-start.11) | collective-permute-done | bytes 262176 | tf_op jit(solution)/shard_map/ppermute | solution.py:408
  31.0 2.7 %collective-permute-done.10.refs_5_.refs_1_ = bf16[128,1024]{1,0:T(8,128)(2,1)S(1)} collective-permute-done((bf16[128,1024]{1,0:T(8,128)(2,1)S(1)}, bf16[128,1024]{1,0:T(8,128)(2,1)S(1)}, u32[]{:S(2)}, u32[]{:S(2)}) %collective-permute-start.10) | collective-permute-done | bytes 262176 | tf_op jit(solution)/shard_map/ppermute | solution.py:408
  33.9 2.5 %collective-permute-start.14 = (bf16[256,512]{1,0:T(8,128)(2,1)S(1)}, bf16[256,512]{1,0:T(8,128)(2,1)S(1)}, u32[]{:S(2)}, u32[]{:S(2)}) collective-permute-start(bf16[256,512]{1,0:T(8,128)(2,1)S(1)} %get-tuple-element.67.refs_3_), channel_id=1, source_target_pairs={{0,16},{2,18},{4,20},{6,22},{8,24},{10,26},{12,28},{14,30},{16,0},... | collective-permute-start | bytes 786440 | tf_op jit(solution)/shard_map/ppermute | solution.py:420
  36.4 1.7 %collective-permute-start.13 = (bf16[256,512]{1,0:T(8,128)(2,1)S(1)}, bf16[256,512]{1,0:T(8,128)(2,1)S(1)}, u32[]{:S(2)}, u32[]{:S(2)}) collective-permute-start(bf16[256,512]{1,0:T(8,128)(2,1)S(1)} %get-tuple-element.67.refs_3_), channel_id=1, source_target_pairs={{0,8},{2,10},{4,12},{6,14},{8,0},{10,2},{12,4},{14,6},{16,24},{18,... | collective-permute-start | bytes 786440 | tf_op jit(solution)/shard_map/ppermute | solution.py:420
  38.1 11.2 %collective-permute-done.14.refs_5_ = bf16[256,512]{1,0:T(8,128)(2,1)S(1)} collective-permute-done((bf16[256,512]{1,0:T(8,128)(2,1)S(1)}, bf16[256,512]{1,0:T(8,128)(2,1)S(1)}, u32[]{:S(2)}, u32[]{:S(2)}) %collective-permute-start.14) | collective-permute-done | bytes 262176 | tf_op jit(solution)/shard_map/ppermute | solution.py:420
  49.2 1.3 %collective-permute-start.15 = (bf16[256,512]{1,0:T(8,128)(2,1)S(1)}, bf16[256,512]{1,0:T(8,128)(2,1)S(1)}, u32[]{:S(2)}, u32[]{:S(2)}) collective-permute-start(bf16[256,512]{1,0:T(8,128)(2,1)S(1)} %collective-permute-done.14.refs_5_), channel_id=1, source_target_pairs={{8,0},{10,2},{12,4},{14,6},{16,24},{18,26},{20,28},{22,30},{9,1},{... | collective-permute-start | bytes 786440 | tf_op jit(solution)/shard_map/ppermute | solution.py:436
  50.5 0.7 collective-permute-start.16
  51.2 7.7 %collective-permute-done.15.refs_6_ = bf16[256,512]{1,0:T(8,128)(2,1)S(1)} collective-permute-done((bf16[256,512]{1,0:T(8,128)(2,1)S(1)}, bf16[256,512]{1,0:T(8,128)(2,1)S(1)}, u32[]{:S(2)}, u32[]{:S(2)}) %collective-permute-start.15) | collective-permute-done | bytes 262176 | tf_op jit(solution)/shard_map/ppermute | solution.py:436
  58.9 1.0 copy-done.10
  59.9 5.6 %shard_map.95 = (bf16[1024,1024]{1,0:T(8,128)(2,1)}, bf16[1024,256]{1,0:T(8,128)(2,1)S(1)}, bf16[1024,256]{1,0:T(8,128)(2,1)S(1)}, bf16[1024,128]{1,0:T(8,128)(2...) custom-call(s32[8]{0:T(128)S(1)} %copy-done.9, ...), custom_call_target="tpu_custom_call" | custom-call | flops 1073741824 | bytes 10035232 | tf_op jit(solution)/shard_map/pallas_call | solution.py:27
  65.6 5.7 %collective-permute-start.19 = (bf16[144,256]{1,0:T(8,128)(2,1)S(1)}, bf16[144,256]{1,0:T(8,128)(2,1)S(1)}, u32[]{:S(2)}, u32[]{:S(2)}) collective-permute-start(bf16[144,256]{1,0:T(8,128)(2,1)S(1)} %get-tuple-element.80), channel_id=1, source_target_pairs={{0,24},{2,26},{4,28},{6,30},{1,25},{3,27},{5,29},{7,31}} | collective-permute-start | bytes 221192 | tf_op jit(solution)/shard_map/ppermute | solution.py:411
  71.3 2.9 %collective-permute-start.18 = (bf16[144,256]{1,0:T(8,128)(2,1)S(1)}, bf16[144,256]{1,0:T(8,128)(2,1)S(1)}, u32[]{:S(2)}, u32[]{:S(2)}) collective-permute-start(bf16[144,256]{1,0:T(8,128)(2,1)S(1)} %get-tuple-element.80), channel_id=1, source_target_pairs={{0,16},{2,18},{4,20},{6,22},{8,24},{10,26},{12,28},{14,30},{1,17},... | collective-permute-start | bytes 221192 | tf_op jit(solution)/shard_map/ppermute | solution.py:411
  74.2 1.3 %collective-permute-start.17 = (bf16[144,256]{1,0:T(8,128)(2,1)S(1)}, bf16[144,256]{1,0:T(8,128)(2,1)S(1)}, u32[]{:S(2)}, u32[]{:S(2)}) collective-permute-start(bf16[144,256]{1,0:T(8,128)(2,1)S(1)} %get-tuple-element.80), channel_id=1, source_target_pairs={{0,8},{2,10},{4,12},{6,14},{8,16},{10,18},{12,20},{14,22},{16,24},... | collective-permute-start | bytes 221192 | tf_op jit(solution)/shard_map/ppermute | solution.py:411
  75.5 1.5 %shard_map.96.y_ref = f32[1024,256]{1,0:T(8,128)S(1)} custom-call(bf16[1024,256]{1,0:T(8,128)(2,1)S(1)} %get-tuple-element.70.x_ref, bf16[1024,128]{1,0:T(8,128)(2,1)S(1)} %get-tuple-element.71.b_ref, bf16[1024,128]{1,0:T(8,128)(2,1)S(1)} %get-tuple-element.68.c_ref, f32[128,256]{1,0:T(8,128)S(1)} %get-tuple-element.72.columns_ref, ...), custom_call_target="tpu_custom_call" | custom-call | flops 134217728 | bytes 2260992 | tf_op jit(solution)/shard_map/pallas_call | solution.py:27
  77.0 0.9 shard_map.97.silu_ref
  78.2 0.6 shard_map.98
  78.9 3.5 %collective-permute-start.20 = (bf16[16,256]{1,0:T(8,128)(2,1)S(1)}, bf16[16,256]{1,0:T(8,128)(2,1)S(1)}, u32[]{:S(2)}, u32[]{:S(2)}) collective-permute-start(bf16[16,256]{1,0:T(8,128)(2,1)S(1)} %get-tuple-element.82), channel_id=1, source_target_pairs={{0,8},{2,10},{4,12},{6,14},{8,16},{10,18},{12,20},{14,22},{16,24},... | collective-permute-start | bytes 24584 | tf_op jit(solution)/shard_map/ppermute | solution.py:411
  82.3 1.3 %collective-permute-start.21 = (bf16[16,256]{1,0:T(8,128)(2,1)S(1)}, bf16[16,256]{1,0:T(8,128)(2,1)S(1)}, u32[]{:S(2)}, u32[]{:S(2)}) collective-permute-start(bf16[16,256]{1,0:T(8,128)(2,1)S(1)} %get-tuple-element.83), channel_id=1, source_target_pairs={{8,0},{10,2},{12,4},{14,6},{16,8},{18,10},{20,12},{22,14},{24,16},... | collective-permute-start | bytes 24584 | tf_op jit(solution)/shard_map/ppermute | solution.py:414
  83.7 5.0 %shard_map.99.refs_2_ = bf16[768,256]{1,0:T(8,128)(2,1)S(1)} custom-call(s32[8]{0:T(128)S(1)} %copy-done.9, f32[31,1024]{1,0:T(8,128)S(1)} %copy-done.3, bf16[1024,256]{1,0:T(8,128)(2,1)S(1)} %get-tuple-element.81.gated_ref), custom_call_target="tpu_custom_call" | custom-call | flops 16252928 | bytes 1044512 | tf_op jit(solution)/shard_map/pallas_call | solution.py:27
  88.7 1.9 %shard_map.100.refs_0_ = bf16[1024,256]{1,0:T(8,128)(2,1)S(1)} custom-call(s32[8]{0:T(128)S(1)} %copy-done.9, f32[31,1024]{1,0:T(8,128)S(1)} %copy-done.3, bf16[1024,256]{1,0:T(8,128)(2,1)S(1)} %get-tuple-element.81.gated_ref, bf16[16,256]{1,0:T(8,128)(2,1)S(1)} %collective-permute-done.20.refs_0_, bf16[16,256]{1,0:T(8,128)(2,1)S(1)} %collective-permute-done.21.refs_1_, ...), custom_call_target="tpu_custom_call" | custom-call | flops 4063232 | bytes 1585184 | tf_op jit(solution)/shard_map/pallas_call | solution.py:27
  90.7 3.0 %collective-permute-start.25 = (bf16[256,256]{1,0:T(8,128)(2,1)S(1)}, bf16[256,256]{1,0:T(8,128)(2,1)S(1)}, u32[]{:S(2)}, u32[]{:S(2)}) collective-permute-start(bf16[256,256]{1,0:T(8,128)(2,1)S(1)} %get-tuple-element.84.refs_0_), channel_id=1, source_target_pairs={{0,24},{2,26},{4,28},{6,30},{8,16},{10,18},{12,20},{14,22},{16,8},... | collective-permute-start | bytes 393224 | tf_op jit(solution)/shard_map/ppermute | solution.py:420
  93.8 1.4 %collective-permute-start.23 = (bf16[256,256]{1,0:T(8,128)(2,1)S(1)}, bf16[256,256]{1,0:T(8,128)(2,1)S(1)}, u32[]{:S(2)}, u32[]{:S(2)}) collective-permute-start(bf16[256,256]{1,0:T(8,128)(2,1)S(1)} %get-tuple-element.84.refs_0_), channel_id=1, source_target_pairs={{0,8},{2,10},{4,12},{6,14},{8,0},{10,2},{12,4},{14,6},{16,24},{18,... | collective-permute-start | bytes 393224 | tf_op jit(solution)/shard_map/ppermute | solution.py:420
  95.2 3.8 %collective-permute-done.25.refs_3_ = bf16[256,256]{1,0:T(8,128)(2,1)S(1)} collective-permute-done((bf16[256,256]{1,0:T(8,128)(2,1)S(1)}, bf16[256,256]{1,0:T(8,128)(2,1)S(1)}, u32[]{:S(2)}, u32[]{:S(2)}) %collective-permute-start.25) | collective-permute-done | bytes 131104 | tf_op jit(solution)/shard_map/ppermute | solution.py:420
  99.0 6.2 %collective-permute-done.24.refs_2_ = bf16[256,256]{1,0:T(8,128)(2,1)S(1)} collective-permute-done((bf16[256,256]{1,0:T(8,128)(2,1)S(1)}, bf16[256,256]{1,0:T(8,128)(2,1)S(1)}, u32[]{:S(2)}, u32[]{:S(2)}) %collective-permute-start.24) | collective-permute-done | bytes 131104 | tf_op jit(solution)/shard_map/ppermute | solution.py:420
  105.4 1.5 %collective-permute-done.26.refs_3_ = bf16[512,256]{1,0:T(8,128)(2,1)S(1)} collective-permute-done((bf16[512,256]{1,0:T(8,128)(2,1)S(1)}, bf16[512,256]{1,0:T(8,128)(2,1)S(1)}, u32[]{:S(2)}, u32[]{:S(2)}) %collective-permute-start.26) | collective-permute-done | bytes 262176 | tf_op jit(solution)/shard_map/ppermute | solution.py:417
  106.9 0.7 shard_map.102
  107.7 0.7 collective-permute-start.27
  108.3 1.1 collective-permute-start.28
  109.5 1.8 %collective-permute-start.29 = (bf16[256,512]{1,0:T(8,128)(2,1)S(1)}, bf16[256,512]{1,0:T(8,128)(2,1)S(1)}, u32[]{:S(2)}, u32[]{:S(2)}) collective-permute-start(bf16[256,512]{1,0:T(8,128)(2,1)S(1)} %get-tuple-element.90), channel_id=1, source_target_pairs={{0,6},{2,4},{4,2},{6,0},{8,14},{10,12},{12,10},{14,8},{16,22},{18,... | collective-permute-start | bytes 786440 | tf_op jit(solution)/shard_map/ppermute | solution.py:408
  111.2 5.7 %collective-permute-done.27 = bf16[256,512]{1,0:T(8,128)(2,1)S(1)} collective-permute-done((bf16[256,512]{1,0:T(8,128)(2,1)S(1)}, bf16[256,512]{1,0:T(8,128)(2,1)S(1)}, u32[]{:S(2)}, u32[]{:S(2)}) %collective-permute-start.27) | collective-permute-done | bytes 262176 | tf_op jit(solution)/shard_map/ppermute | solution.py:408
  117.2 4.8 %collective-permute-done.29 = bf16[256,512]{1,0:T(8,128)(2,1)S(1)} collective-permute-done((bf16[256,512]{1,0:T(8,128)(2,1)S(1)}, bf16[256,512]{1,0:T(8,128)(2,1)S(1)}, u32[]{:S(2)}, u32[]{:S(2)}) %collective-permute-start.29) | collective-permute-done | bytes 262176 | tf_op jit(solution)/shard_map/ppermute | solution.py:408
  122.0 0.8 add_convert_fusion
  (51 shorter events, 3.2 us)
Async XLA Ops:
  0.0 5.8 %copy-start = (bf16[64,256]{1,0:T(8,128)(2,1)S(1)}, bf16[64,256]{1,0:T(8,128)(2,1)}, u32[]{:S(2)}) copy-start(bf16[64,256]{1,0:T(8,128)(2,1)} %param.12) | copy-start | bytes 98308
  0.0 59.9 %copy-start.9 = (s32[8]{0:T(128)S(1)}, s32[8]{0:T(128)}, u32[]{:S(2)}) copy-start(s32[8]{0:T(128)} %len_ref.5) | copy-start | bytes 100
  0.0 0.9 copy-start.4
  0.9 0.9 copy-start.5
  1.8 0.9 copy-start.6
  2.7 57.2 %copy-start.7 = (bf16[256,1024]{1,0:T(8,128)(2,1)S(1)}, bf16[256,1024]{1,0:T(8,128)(2,1)}, u32[]{:S(2)}) copy-start(bf16[256,1024]{1,0:T(8,128)(2,1)} %own_ref.1) | copy-start | bytes 1572868
  2.8 13.4 %collective-permute-start = (bf16[64,768]{1,0:T(8,128)(2,1)S(1)}, bf16[64,768]{1,0:T(8,128)(2,1)S(1)}, u32[]{:S(2)}, u32[]{:S(2)}) collective-permute-start(bf16[64,768]{1,0:T(8,128)(2,1)S(1)} %get-tuple-element.49), channel_id=1, source_target_pairs={{0,2},{2,0},{4,6},{6,4},{8,10},{10,8},{12,14},{14,12},{16,18},{18,... | collective-permute-start | bytes 294920 | tf_op jit(solution)/shard_map/ppermute | solution.py:408
  5.8 6.6 %collective-permute-start.5 = (bf16[64,128]{1,0:T(8,128)(2,1)S(1)}, bf16[64,128]{1,0:T(8,128)(2,1)S(1)}, u32[]{:S(2)}, u32[]{:S(2)}) collective-permute-start(bf16[64,128]{1,0:T(8,128)(2,1)S(1)} %constant_dynamic-slice_fusion.refs_0_), channel_id=1, source_target_pairs={{0,24},{2,26},{4,28},{6,30},{8,16},{10,18},{12,20},{14,22},{16,8},... | collective-permute-start | bytes 49160 | tf_op jit(solution)/shard_map/ppermute | solution.py:420
  9.4 4.6 %collective-permute-start.4 = (bf16[64,128]{1,0:T(8,128)(2,1)S(1)}, bf16[64,128]{1,0:T(8,128)(2,1)S(1)}, u32[]{:S(2)}, u32[]{:S(2)}) collective-permute-start(bf16[64,128]{1,0:T(8,128)(2,1)S(1)} %constant_dynamic-slice_fusion.refs_0_), channel_id=1, source_target_pairs={{0,16},{2,18},{4,20},{6,22},{8,24},{10,26},{12,28},{14,30},{16,0},... | collective-permute-start | bytes 49160 | tf_op jit(solution)/shard_map/ppermute | solution.py:420
  9.4 4.6 %collective-permute-start.3 = (bf16[64,128]{1,0:T(8,128)(2,1)S(1)}, bf16[64,128]{1,0:T(8,128)(2,1)S(1)}, u32[]{:S(2)}, u32[]{:S(2)}) collective-permute-start(bf16[64,128]{1,0:T(8,128)(2,1)S(1)} %constant_dynamic-slice_fusion.refs_0_), channel_id=1, source_target_pairs={{0,8},{2,10},{4,12},{6,14},{8,0},{10,2},{12,4},{14,6},{16,24},{18,... | collective-permute-start | bytes 49160 | tf_op jit(solution)/shard_map/ppermute | solution.py:420
  10.2 8.4 %collective-permute-start.1 = (bf16[64,768]{1,0:T(8,128)(2,1)S(1)}, bf16[64,768]{1,0:T(8,128)(2,1)S(1)}, u32[]{:S(2)}, u32[]{:S(2)}) collective-permute-start(bf16[64,768]{1,0:T(8,128)(2,1)S(1)} %get-tuple-element.50), channel_id=1, source_target_pairs={{0,4},{2,6},{4,0},{6,2},{8,12},{10,14},{12,8},{14,10},{16,20},{18,... | collective-permute-start | bytes 294920 | tf_op jit(solution)/shard_map/ppermute | solution.py:408
  12.4 6.4 %collective-permute-start.2 = (bf16[64,768]{1,0:T(8,128)(2,1)S(1)}, bf16[64,768]{1,0:T(8,128)(2,1)S(1)}, u32[]{:S(2)}, u32[]{:S(2)}) collective-permute-start(bf16[64,768]{1,0:T(8,128)(2,1)S(1)} %get-tuple-element.51), channel_id=1, source_target_pairs={{0,6},{2,4},{4,2},{6,0},{8,14},{10,12},{12,10},{14,8},{16,22},{18,... | collective-permute-start | bytes 294920 | tf_op jit(solution)/shard_map/ppermute | solution.py:408
  14.1 4.8 %collective-permute-start.6 = (bf16[320,128]{1,0:T(8,128)(2,1)S(1)}, bf16[320,128]{1,0:T(8,128)(2,1)S(1)}, u32[]{:S(2)}, u32[]{:S(2)}) collective-permute-start(bf16[320,128]{1,0:T(8,128)(2,1)S(1)} %get-tuple-element.54), channel_id=1, source_target_pairs={{0,2},{2,0},{4,6},{6,4},{8,10},{10,8},{12,14},{14,12},{16,18},{18,... | collective-permute-start | bytes 245768 | tf_op jit(solution)/shard_map/ppermute | solution.py:408
  14.7 5.1 %collective-permute-start.7 = (bf16[320,128]{1,0:T(8,128)(2,1)S(1)}, bf16[320,128]{1,0:T(8,128)(2,1)S(1)}, u32[]{:S(2)}, u32[]{:S(2)}) collective-permute-start(bf16[320,128]{1,0:T(8,128)(2,1)S(1)} %get-tuple-element.55), channel_id=1, source_target_pairs={{0,4},{2,6},{4,0},{6,2},{8,12},{10,14},{12,8},{14,10},{16,20},{18,... | collective-permute-start | bytes 245768 | tf_op jit(solution)/shard_map/ppermute | solution.py:408
  16.2 5.3 %collective-permute-start.8 = (bf16[320,128]{1,0:T(8,128)(2,1)S(1)}, bf16[320,128]{1,0:T(8,128)(2,1)S(1)}, u32[]{:S(2)}, u32[]{:S(2)}) collective-permute-start(bf16[320,128]{1,0:T(8,128)(2,1)S(1)} %get-tuple-element.56), channel_id=1, source_target_pairs={{0,6},{2,4},{4,2},{6,0},{8,14},{10,12},{12,10},{14,8},{16,22},{18,... | collective-permute-start | bytes 245768 | tf_op jit(solution)/shard_map/ppermute | solution.py:408
  21.5 9.4 %collective-permute-start.11 = (bf16[128,1024]{1,0:T(8,128)(2,1)S(1)}, bf16[128,1024]{1,0:T(8,128)(2,1)S(1)}, u32[]{:S(2)}, u32[]{:S(2)}) collective-permute-start(bf16[128,1024]{1,0:T(8,128)(2,1)S(1)} %constant_dynamic-slice_fusion.1), channel_id=1, source_target_pairs={{0,6},{2,4},{4,2},{6,0},{8,14},{10,12},{12,10},{14,8},{16,22},{18,... | collective-permute-start | bytes 786440 | tf_op jit(solution)/shard_map/ppermute | solution.py:408
  23.0 10.7 %collective-permute-start.10 = (bf16[128,1024]{1,0:T(8,128)(2,1)S(1)}, bf16[128,1024]{1,0:T(8,128)(2,1)S(1)}, u32[]{:S(2)}, u32[]{:S(2)}) collective-permute-start(bf16[128,1024]{1,0:T(8,128)(2,1)S(1)} %constant_dynamic-slice_fusion.1), channel_id=1, source_target_pairs={{0,4},{2,6},{4,0},{6,2},{8,12},{10,14},{12,8},{14,10},{16,20},{18,... | collective-permute-start | bytes 786440 | tf_op jit(solution)/shard_map/ppermute | solution.py:408
  24.5 9.2 %collective-permute-start.9 = (bf16[128,1024]{1,0:T(8,128)(2,1)S(1)}, bf16[128,1024]{1,0:T(8,128)(2,1)S(1)}, u32[]{:S(2)}, u32[]{:S(2)}) collective-permute-start(bf16[128,1024]{1,0:T(8,128)(2,1)S(1)} %constant_dynamic-slice_fusion.1), channel_id=1, source_target_pairs={{0,2},{2,0},{4,6},{6,4},{8,10},{10,8},{12,14},{14,12},{16,18},{18,... | collective-permute-start | bytes 786440 | tf_op jit(solution)/shard_map/ppermute | solution.py:408
  33.8 25.1 %collective-permute-start.12 = (bf16[512,1024]{1,0:T(8,128)(2,1)S(1)}, bf16[512,1024]{1,0:T(8,128)(2,1)S(1)}, u32[]{:S(2)}, u32[]{:S(2)}) collective-permute-start(bf16[512,1024]{1,0:T(8,128)(2,1)S(1)} %get-tuple-element.64), channel_id=1, source_target_pairs={{0,1},{1,0},{2,3},{3,2},{4,5},{5,4},{6,7},{7,6},{8,9},{9,8},{10,11... | collective-permute-start | bytes 3145736 | tf_op jit(solution)/shard_map/ppermute | solution.py:417
  33.9 15.3 %collective-permute-start.14 = (bf16[256,512]{1,0:T(8,128)(2,1)S(1)}, bf16[256,512]{1,0:T(8,128)(2,1)S(1)}, u32[]{:S(2)}, u32[]{:S(2)}) collective-permute-start(bf16[256,512]{1,0:T(8,128)(2,1)S(1)} %get-tuple-element.67.refs_3_), channel_id=1, source_target_pairs={{0,16},{2,18},{4,20},{6,22},{8,24},{10,26},{12,28},{14,30},{16,0},... | collective-permute-start | bytes 786440 | tf_op jit(solution)/shard_map/ppermute | solution.py:420
  36.4 14.8 %collective-permute-start.13 = (bf16[256,512]{1,0:T(8,128)(2,1)S(1)}, bf16[256,512]{1,0:T(8,128)(2,1)S(1)}, u32[]{:S(2)}, u32[]{:S(2)}) collective-permute-start(bf16[256,512]{1,0:T(8,128)(2,1)S(1)} %get-tuple-element.67.refs_3_), channel_id=1, source_target_pairs={{0,8},{2,10},{4,12},{6,14},{8,0},{10,2},{12,4},{14,6},{16,24},{18,... | collective-permute-start | bytes 786440 | tf_op jit(solution)/shard_map/ppermute | solution.py:420
  49.2 9.7 %collective-permute-start.15 = (bf16[256,512]{1,0:T(8,128)(2,1)S(1)}, bf16[256,512]{1,0:T(8,128)(2,1)S(1)}, u32[]{:S(2)}, u32[]{:S(2)}) collective-permute-start(bf16[256,512]{1,0:T(8,128)(2,1)S(1)} %collective-permute-done.14.refs_5_), channel_id=1, source_target_pairs={{8,0},{10,2},{12,4},{14,6},{16,24},{18,26},{20,28},{22,30},{9,1},{... | collective-permute-start | bytes 786440 | tf_op jit(solution)/shard_map/ppermute | solution.py:436
  50.5 8.4 %collective-permute-start.16 = (bf16[256,512]{1,0:T(8,128)(2,1)S(1)}, bf16[256,512]{1,0:T(8,128)(2,1)S(1)}, u32[]{:S(2)}, u32[]{:S(2)}) collective-permute-start(bf16[256,512]{1,0:T(8,128)(2,1)S(1)} %get-tuple-element.67.refs_3_), channel_id=1, source_target_pairs={{8,16},{10,18},{12,20},{14,22},{16,8},{18,10},{20,12},{22,14},{9,1... | collective-permute-start | bytes 786440 | tf_op jit(solution)/shard_map/ppermute | solution.py:437
  58.9 1.0 copy-start.10
  65.5 11.5 %copy-start.1 = (bf16[1024,1024]{1,0:T(8,128)(2,1)S(1)}, bf16[1024,1024]{1,0:T(8,128)(2,1)}, u32[]{:S(2)}) copy-start(bf16[1024,1024]{1,0:T(8,128)(2,1)} %get-tuple-element.78.frames_ref) | copy-start | bytes 6291460
  65.6 11.5 %copy-start.8 = (f32[1024]{0:T(1024)S(1)}, f32[1024]{0:T(1024)}, u32[]{:S(2)}) copy-start(f32[1024]{0:T(1024)} %param.14) | copy-start | bytes 12292
  65.6 12.4 %collective-permute-start.19 = (bf16[144,256]{1,0:T(8,128)(2,1)S(1)}, bf16[144,256]{1,0:T(8,128)(2,1)S(1)}, u32[]{:S(2)}, u32[]{:S(2)}) collective-permute-start(bf16[144,256]{1,0:T(8,128)(2,1)S(1)} %get-tuple-element.80), channel_id=1, source_target_pairs={{0,24},{2,26},{4,28},{6,30},{1,25},{3,27},{5,29},{7,31}} | collective-permute-start | bytes 221192 | tf_op jit(solution)/shard_map/ppermute | solution.py:411
  71.3 6.7 %collective-permute-start.18 = (bf16[144,256]{1,0:T(8,128)(2,1)S(1)}, bf16[144,256]{1,0:T(8,128)(2,1)S(1)}, u32[]{:S(2)}, u32[]{:S(2)}) collective-permute-start(bf16[144,256]{1,0:T(8,128)(2,1)S(1)} %get-tuple-element.80), channel_id=1, source_target_pairs={{0,16},{2,18},{4,20},{6,22},{8,24},{10,26},{12,28},{14,30},{1,17},... | collective-permute-start | bytes 221192 | tf_op jit(solution)/shard_map/ppermute | solution.py:411
  74.2 3.8 %collective-permute-start.17 = (bf16[144,256]{1,0:T(8,128)(2,1)S(1)}, bf16[144,256]{1,0:T(8,128)(2,1)S(1)}, u32[]{:S(2)}, u32[]{:S(2)}) collective-permute-start(bf16[144,256]{1,0:T(8,128)(2,1)S(1)} %get-tuple-element.80), channel_id=1, source_target_pairs={{0,8},{2,10},{4,12},{6,14},{8,16},{10,18},{12,20},{14,22},{16,24},... | collective-permute-start | bytes 221192 | tf_op jit(solution)/shard_map/ppermute | solution.py:411
  77.0 1.2 copy-start.2
  78.2 5.4 %copy-start.3 = (f32[31,1024]{1,0:T(8,128)S(1)}, f32[31,1024]{1,0:T(8,128)}, u32[]{:S(2)}) copy-start(f32[31,1024]{1,0:T(8,128)} %taps_ref.3) | copy-start | bytes 380932
  78.9 9.8 %collective-permute-start.20 = (bf16[16,256]{1,0:T(8,128)(2,1)S(1)}, bf16[16,256]{1,0:T(8,128)(2,1)S(1)}, u32[]{:S(2)}, u32[]{:S(2)}) collective-permute-start(bf16[16,256]{1,0:T(8,128)(2,1)S(1)} %get-tuple-element.82), channel_id=1, source_target_pairs={{0,8},{2,10},{4,12},{6,14},{8,16},{10,18},{12,20},{14,22},{16,24},... | collective-permute-start | bytes 24584 | tf_op jit(solution)/shard_map/ppermute | solution.py:411
  82.3 6.4 %collective-permute-start.21 = (bf16[16,256]{1,0:T(8,128)(2,1)S(1)}, bf16[16,256]{1,0:T(8,128)(2,1)S(1)}, u32[]{:S(2)}, u32[]{:S(2)}) collective-permute-start(bf16[16,256]{1,0:T(8,128)(2,1)S(1)} %get-tuple-element.83), channel_id=1, source_target_pairs={{8,0},{10,2},{12,4},{14,6},{16,8},{18,10},{20,12},{22,14},{24,16},... | collective-permute-start | bytes 24584 | tf_op jit(solution)/shard_map/ppermute | solution.py:414
  90.7 16.2 %collective-permute-start.22 = (bf16[1024,256]{1,0:T(8,128)(2,1)S(1)}, bf16[1024,256]{1,0:T(8,128)(2,1)S(1)}, u32[]{:S(2)}, u32[]{:S(2)}) collective-permute-start(bf16[1024,256]{1,0:T(8,128)(2,1)S(1)} %shard_map.100.refs_0_), channel_id=1, source_target_pairs={{0,1},{1,0},{2,3},{3,2},{4,5},{5,4},{6,7},{7,6},{8,9},{9,8},{10,11... | collective-permute-start | bytes 1572872 | tf_op jit(solution)/shard_map/ppermute | solution.py:417
  90.7 8.3 %collective-permute-start.25 = (bf16[256,256]{1,0:T(8,128)(2,1)S(1)}, bf16[256,256]{1,0:T(8,128)(2,1)S(1)}, u32[]{:S(2)}, u32[]{:S(2)}) collective-permute-start(bf16[256,256]{1,0:T(8,128)(2,1)S(1)} %get-tuple-element.84.refs_0_), channel_id=1, source_target_pairs={{0,24},{2,26},{4,28},{6,30},{8,16},{10,18},{12,20},{14,22},{16,8},... | collective-permute-start | bytes 393224 | tf_op jit(solution)/shard_map/ppermute | solution.py:420
  93.8 11.4 %collective-permute-start.24 = (bf16[256,256]{1,0:T(8,128)(2,1)S(1)}, bf16[256,256]{1,0:T(8,128)(2,1)S(1)}, u32[]{:S(2)}, u32[]{:S(2)}) collective-permute-start(bf16[256,256]{1,0:T(8,128)(2,1)S(1)} %get-tuple-element.84.refs_0_), channel_id=1, source_target_pairs={{0,16},{2,18},{4,20},{6,22},{8,24},{10,26},{12,28},{14,30},{16,0},... | collective-permute-start | bytes 393224 | tf_op jit(solution)/shard_map/ppermute | solution.py:420
  93.8 11.4 %collective-permute-start.23 = (bf16[256,256]{1,0:T(8,128)(2,1)S(1)}, bf16[256,256]{1,0:T(8,128)(2,1)S(1)}, u32[]{:S(2)}, u32[]{:S(2)}) collective-permute-start(bf16[256,256]{1,0:T(8,128)(2,1)S(1)} %get-tuple-element.84.refs_0_), channel_id=1, source_target_pairs={{0,8},{2,10},{4,12},{6,14},{8,0},{10,2},{12,4},{14,6},{16,24},{18,... | collective-permute-start | bytes 393224 | tf_op jit(solution)/shard_map/ppermute | solution.py:420
  105.3 1.6 %collective-permute-start.26 = (bf16[512,256]{1,0:T(8,128)(2,1)S(1)}, bf16[512,256]{1,0:T(8,128)(2,1)S(1)}, u32[]{:S(2)}, u32[]{:S(2)}) collective-permute-start(bf16[512,256]{1,0:T(8,128)(2,1)S(1)} %get-tuple-element.86), channel_id=1, source_target_pairs={{0,1},{1,0},{2,3},{3,2},{4,5},{5,4},{6,7},{7,6},{8,9},{9,8},{10,11... | collective-permute-start | bytes 786440 | tf_op jit(solution)/shard_map/ppermute | solution.py:417
  107.7 9.2 %collective-permute-start.27 = (bf16[256,512]{1,0:T(8,128)(2,1)S(1)}, bf16[256,512]{1,0:T(8,128)(2,1)S(1)}, u32[]{:S(2)}, u32[]{:S(2)}) collective-permute-start(bf16[256,512]{1,0:T(8,128)(2,1)S(1)} %get-tuple-element.88), channel_id=1, source_target_pairs={{0,2},{2,0},{4,6},{6,4},{8,10},{10,8},{12,14},{14,12},{16,18},{18,... | collective-permute-start | bytes 786440 | tf_op jit(solution)/shard_map/ppermute | solution.py:408
  108.3 8.9 %collective-permute-start.28 = (bf16[256,512]{1,0:T(8,128)(2,1)S(1)}, bf16[256,512]{1,0:T(8,128)(2,1)S(1)}, u32[]{:S(2)}, u32[]{:S(2)}) collective-permute-start(bf16[256,512]{1,0:T(8,128)(2,1)S(1)} %get-tuple-element.89), channel_id=1, source_target_pairs={{0,4},{2,6},{4,0},{6,2},{8,12},{10,14},{12,8},{14,10},{16,20},{18,... | collective-permute-start | bytes 786440 | tf_op jit(solution)/shard_map/ppermute | solution.py:408
  109.5 12.6 %collective-permute-start.29 = (bf16[256,512]{1,0:T(8,128)(2,1)S(1)}, bf16[256,512]{1,0:T(8,128)(2,1)S(1)}, u32[]{:S(2)}, u32[]{:S(2)}) collective-permute-start(bf16[256,512]{1,0:T(8,128)(2,1)S(1)} %get-tuple-element.90), channel_id=1, source_target_pairs={{0,6},{2,4},{4,2},{6,0},{8,14},{10,12},{12,10},{14,8},{16,22},{18,... | collective-permute-start | bytes 786440 | tf_op jit(solution)/shard_map/ppermute | solution.py:408

commit v5 on v4

--- a/solution.py
+++ b/solution.py
@@ -49,14 +49,6 @@
     return start
 
 
-def spread(columns, first, heads, head_of_lane, shape):
-    out = jnp.broadcast_to(columns[:, first : first + 1], shape)
-    for head in range(1, heads):
-        column = jnp.broadcast_to(columns[:, first + head : first + head + 1], shape)
-        out = jnp.where(head_of_lane == head, column, out)
-    return out
-
-
 def fill_planes(plane, dest_ref, pieces, offsets, lanes=slice(None)):
     rows = pieces[0].shape[0]
     for offset in sorted(set(offsets)):
@@ -73,6 +65,16 @@
         lanes = pl.ds(pl.multiple_of((place ^ step) * width, LANES), width)
         for number, weight_ref in enumerate(weight_refs):
             out_ref[:, number * width : (number + 1) * width] = weight_ref[:, lanes]
+
+
+def pack_all_kernel(group, *refs):
+    weight_refs, out_ref = refs[:-1], refs[-1]
+    width = weight_refs[0].shape[1] // group
+    for target in range(out_ref.shape[0]):
+        block = target % group
+        for number, weight_ref in enumerate(weight_refs):
+            columns = weight_ref[:, block * width : (block + 1) * width]
+            out_ref[target, :, number * width : (number + 1) * width] = columns
 
 
 def stack_kernel(group, *refs):
@@ -135,10 +137,18 @@
         swap_ref[top:, lanes] = bc_ref[number * height : (number + 1) * height, :]
 
 
-def state_kernel(group, heads, state, offsets, len_ref, decay_ref, bc_half_ref, own_ref, swap_ref, *refs):
+def lanes_of(rows, width, head_size):
+    high = rows.astype(BF16)
+    low = (rows - high.astype(F32)).astype(BF16)
+    owner = lax.broadcasted_iota(jnp.int32, (16, width), 1) // head_size
+    chosen = jnp.where((lax.broadcasted_iota(jnp.int32, (16, width), 0) & 7) == owner, 1.0, 0.0).astype(BF16)
+    both = jnp.concatenate([high.astype(F32), low.astype(F32)], axis=0).astype(BF16)
+    return dot(both, chosen, ((0,), (0,)))
+
+
+def state_kernel(group, heads, state, len_ref, decay_ref, xz_ref, bc_half_ref, own_ref, swap_ref, *refs):
     half_refs, refs = refs[: group - 1], refs[group - 1 :]
-    pieces, refs = refs[: len(offsets)], refs[len(offsets) :]
-    frames_ref, z_ref, x_ref, b_ref, c_ref, columns_ref, cumul_ref, step_ref, carry_ref, keep_ref, send_ref, weight_ref = refs
+    frames_ref, x_ref, b_ref, c_ref, rows_ref, step_ref, keep_ref, send_ref, weight_ref = refs
     place, plane = plane_place(group)
     parity = lax.rem(lax.axis_index("head"), 2)
     total, width = x_ref.shape
@@ -154,22 +164,14 @@
         other = pl.ds(pl.multiple_of(block + (1 - parity) * half, half), half)
         frames_ref[mine, :] = half_ref[...]
         frames_ref[other, :] = swap_ref[number * half : (number + 1) * half, :]
-    fill_planes(plane, weight_ref, pieces, offsets, slice(0, width))
-    fill_planes(plane, z_ref, pieces, offsets, slice(width, 2 * width))
-    mine = pl.ds(pl.multiple_of(width + parity * LANES, LANES), LANES)
-    other = pl.ds(pl.multiple_of(width + (1 - parity) * LANES, LANES), LANES)
+    mine = pl.ds(pl.multiple_of(parity * LANES, LANES), LANES)
+    other = pl.ds(pl.multiple_of((1 - parity) * LANES, LANES), LANES)
     weight_ref[:, mine] = bc_half_ref[...]
     top = len(half_refs) * half
     height = swap_ref.shape[0] - top
     for number in range(weight_ref.shape[0] // height):
         lanes = slice(number * LANES, (number + 1) * LANES)
         weight_ref[number * height : (number + 1) * height, other] = swap_ref[top:, lanes]
-    for block in range(group):
-        rows = slice(block * frames, (block + 1) * frames)
-        product = dot(frames_ref[rows, :], weight_ref[...])
-        x_ref[rows, :] = product[:, :width].astype(BF16)
-        b_ref[rows, :] = product[:, width : width + state].astype(BF16)
-        c_ref[rows, :] = product[:, width + state :].astype(BF16)
 
     decay = decay_ref[...]
     used = decay.shape[0]
@@ -185,42 +187,45 @@
     carried = jnp.where(start < first, jnp.exp(cumul), 0.0)
     tail = jnp.where(position >= start_last, jnp.exp(whole - cumul), 0.0)
     keep = jnp.where(start_last < first, jnp.exp(whole), 0.0)
-    parts = [cumul, carried, tail, start.astype(F32)]
-    if 4 * used % SPAN:
-        parts.append(jnp.zeros((SPAN - 4 * used % SPAN, SPAN), F32))
-    columns = jnp.concatenate(parts, axis=0).T
-    columns_ref[...] = columns
-    cumul_ref[...] = cumul
-
-    head_of_lane = lax.broadcasted_iota(jnp.int32, (SPAN, width), 1) // head_size
+    rows_ref[:used, :] = cumul
+    rows_ref[used : 2 * used, :] = start.astype(F32)
+    rows_ref[2 * used :, :] = carried
+
+    for block in range(group):
+        rows = slice(block * frames, (block + 1) * frames)
+        x_ref[rows, :] = dot(frames_ref[rows, :], xz_ref[:, :width]).astype(BF16)
+        product = dot(frames_ref[rows, :], weight_ref[...])
+        b_ref[rows, :] = product[:, :state].astype(BF16)
+        c_ref[rows, :] = product[:, state:].astype(BF16)
+
     entry = jnp.zeros((state, width), F32)
-    through = jnp.ones((1, width), F32)
+    through = jnp.ones((8, width), F32)
     for block in range(count):
         rows = slice(block * SPAN, (block + 1) * SPAN)
-        at = block * 8
-        kept = jnp.broadcast_to(keep[at : at + 1, :1], (1, width))
-        for head in range(1, heads):
-            other = jnp.broadcast_to(keep[at + head : at + head + 1, :1], (1, width))
-            kept = jnp.where(head_of_lane[:1] == head, other, kept)
-        carry_ref[rows, :] = spread(columns, used + at, heads, head_of_lane, (SPAN, width))
-        weighed = x_ref[rows, :].astype(F32) * spread(columns, 2 * used + at, heads, head_of_lane, (SPAN, width))
+        at = slice(block * 8, (block + 1) * 8)
+        kept = lanes_of(keep[at], width, head_size)
+        weighed = x_ref[rows, :].astype(F32) * lanes_of(tail[at], width, head_size)
         step = dot(b_ref[rows, :], weighed.astype(BF16), ((0,), (0,)))
         step_ref[block * state : (block + 1) * state, :] = step
-        keep_ref[block * 8 : (block + 1) * 8, :] = jnp.broadcast_to(kept, (8, width))
-        entry = kept * entry + step
-        through = through * kept
+        keep_ref[at, :] = kept[:8]
+        entry = kept[:1] * entry + step
+        through = through * kept[:8]
     send_ref[:state, :] = entry.astype(BF16)
-    send_ref[state:, :] = jnp.broadcast_to(through, (EDGE, width)).astype(BF16)
-
-
-def inner_kernel(group, heads, x_ref, b_ref, c_ref, columns_ref, cumul_ref, y_ref):
+    send_ref[state:, :] = jnp.concatenate([through, through], axis=0).astype(BF16)
+
+
+def inner_kernel(group, heads, x_ref, b_ref, c_ref, rows_ref, y_ref):
     _, plane = plane_place(group)
     total, width = x_ref.shape
     head_size = width // heads
     count = total // SPAN
     base = plane * total
-    used = cumul_ref.shape[0]
+    used = rows_ref.shape[0] // 3
     square = (SPAN, SPAN)
+    parts = [rows_ref[: 2 * used, :]]
+    if 2 * used % SPAN:
+        parts.append(jnp.zeros((SPAN - 2 * used % SPAN, SPAN), F32))
+    columns = jnp.concatenate(parts, axis=0).T
     row, lane = (lax.broadcasted_iota(jnp.int32, square, dim) for dim in (0, 1))
     lower = row >= lane
     tile_heads = LANES // head_size
@@ -232,14 +237,14 @@
         x = x_ref[rows, :]
         scores = dot(c_ref[rows, :], b_ref[rows, :], ((1,), (1,)))
         here = (base + block * SPAN + lane).astype(F32)
-        start_here = jnp.broadcast_to(columns_ref[:, 3 * used + at : 3 * used + at + 1], square)
+        start_here = jnp.broadcast_to(columns[:, used + at : used + at + 1], square)
         joined = lower & (here >= start_here)
         for tile in range(width // LANES):
             mixes, values = [], []
             for inner in range(tile_heads):
                 which = at + tile * tile_heads + inner
-                column = jnp.broadcast_to(columns_ref[:, which : which + 1], square)
-                gap = jnp.where(joined, column - cumul_ref[which : which + 1, :], -1e30)
+                column = jnp.broadcast_to(columns[:, which : which + 1], square)
+                gap = jnp.where(joined, column - rows_ref[which : which + 1, :], -1e30)
                 mixes.append((jnp.exp(gap) * scores).astype(BF16))
                 values.append(x[:, tile * LANES : (tile + 1) * LANES] * masks[inner])
             y_ref[rows, tile * LANES : (tile + 1) * LANES] = dot(
@@ -247,13 +252,13 @@
             )
 
 
-def silu_kernel(group, gain_ref, frames_ref, weight_ref, out_ref):
+def silu_kernel(group, gain_ref, frames_ref, xz_ref, out_ref):
     place, _ = plane_place(group)
     total, width = out_ref.shape
     gain = gain_ref[:, pl.ds(pl.multiple_of(place * width, LANES), width)]
     for block in range(group):
         rows = slice(block * (total // group), (block + 1) * (total // group))
-        z = dot(frames_ref[rows, :], weight_ref[...]).astype(BF16).astype(F32)
+        z = dot(frames_ref[rows, :], xz_ref[:, width:]).astype(BF16).astype(F32)
         out_ref[rows, :] = z / (1.0 + jnp.exp(-z)) * gain
 
 
@@ -268,10 +273,11 @@
         out_ref[...] = weight_ref[pl.ds(pl.multiple_of((core ^ step) * rows, rows), rows), :]
 
 
-def gate_kernel(heads, state, c_ref, y_ref, step_ref, carry_ref, keep_ref, silu_ref, *refs):
+def gate_kernel(heads, state, c_ref, y_ref, step_ref, rows_ref, keep_ref, silu_ref, *refs):
     earlier, (gated_ref, top_ref, bottom_ref) = refs[:-3], refs[-3:]
     total, width = y_ref.shape
     head_size = width // heads
+    used = rows_ref.shape[0] // 3
     entry = jnp.zeros((state, width), F32)
     for summary in reversed(earlier):
         through = summary[state : state + EDGE, :].astype(F32)[:1]
@@ -280,7 +286,8 @@
     average = jnp.where(owner[0] == owner[1], 1.0 / head_size, 0.0).astype(BF16)
     for block in range(total // SPAN):
         rows = slice(block * SPAN, (block + 1) * SPAN)
-        y = y_ref[rows, :] + carry_ref[rows, :] * dot(c_ref[rows, :], entry.astype(BF16))
+        carried = lanes_of(rows_ref[2 * used + block * 8 : 2 * used + (block + 1) * 8, :], width, head_size)
+        y = y_ref[rows, :] + carried * dot(c_ref[rows, :], entry.astype(BF16))
         square_mean = dot((y * y).astype(BF16), average)
         gated_ref[rows, :] = (y * lax.rsqrt(square_mean + 1e-05) * silu_ref[rows, :]).astype(BF16)
         entry = keep_ref[block * 8 : block * 8 + 1, :] * entry + step_ref[block * state : (block + 1) * state, :]
@@ -423,36 +430,16 @@
     rows = x_weight.shape[0]
     parity = lax.rem(core, 2)
 
-    def along_planes(stack):
-        if planes != 4:
-            return [stack] + [between_planes(stack, step) for step in range(1, planes)], tuple(range(planes))
-
-        def pairs(chosen):
-            return [(a * group + q, b * group + q) for a, b in chosen for q in range(group)]
-
-        second = between_planes(stack, 2)
-        first = between_planes(stack, 1)
-        again, stack_then = lax.optimization_barrier((second, stack))
-        third = lax.ppermute(again, "tm", pairs([(1, 0), (2, 3)]))
-        middle = lax.ppermute(stack_then, "tm", pairs([(1, 2), (2, 1)]))
-        return [stack, first, second, third, middle], (0, 1, 2, 3, 3)
-
     bc_half = lax.dynamic_slice_in_dim(bc_weight, parity * LANES, LANES, 1)
     bc_pieces = [bc_half] + [between_planes(bc_half, step) for step in range(1, planes)]
-    packed = call(
-        functools.partial(pack_kernel, group),
-        tuple(shape((rows, 3 * width), BF16) for _ in range(group)),
-        [x_weight, z_weight, out_weight.T],
-        smem=0,
-    )
-    parts = [packed[0]] + [in_plane(packed[step], step) for step in range(1, group)]
-    xz_stack, out_stack = call(
-        functools.partial(stack_kernel, group),
-        (shape((group * rows, 2 * width), BF16), shape((group * rows, width), BF16)),
-        parts,
-        smem=0,
-    )
-    xz_pieces, offsets = along_planes(xz_stack)
+    bc_pieces, x_weight, z_weight = lax.optimization_barrier((bc_pieces, x_weight, z_weight))
+    blocks = call(
+        functools.partial(pack_all_kernel, group),
+        shape((times, rows, 2 * width), BF16),
+        [x_weight, z_weight],
+        smem=0,
+    )
+    xz = lax.all_to_all(blocks, "tm", split_axis=0, concat_axis=0, tiled=True).reshape(depth, 2 * width)
     decay_blocks = jnp.pad(log_decay.reshape(group, heads, frame_count), ((0, 0), (0, 8 - heads), (0, 0)))
     bc_parts = call(
         functools.partial(share_bc_kernel, group),
@@ -463,66 +450,76 @@
     bc_parts = [bc_parts[0]] + [in_plane(bc_parts[step], step) for step in range(1, group)]
     half_count = frame_count // 2
     frame_half = lax.dynamic_slice_in_dim(frames, parity * half_count, half_count, 0)
-    frame_half, out_stack, bc_parts = lax.optimization_barrier((frame_half, out_stack, bc_parts))
     half_parts = [in_plane(frame_half, step) for step in range(1, group)]
-    height = depth * LANES // depth
     swap, bc_mine, decay = call(
         functools.partial(swap_kernel, group, rows),
         (
-            shape(((group - 1) * half_count + height, depth), BF16),
+            shape(((group - 1) * half_count + LANES, depth), BF16),
             shape((depth, LANES), BF16),
             shape((count * 8, SPAN), F32),
         ),
         [*bc_parts, *half_parts],
         smem=0,
     )
+    out_columns, half_parts = lax.optimization_barrier((out_weight.T, half_parts))
+    packed = call(
+        functools.partial(pack_kernel, group),
+        tuple(shape((rows, width), BF16) for _ in range(group)),
+        [out_columns],
+        smem=0,
+    )
+    parts = [packed[0]] + [in_plane(packed[step], step) for step in range(1, group)]
+    swap, parts = lax.optimization_barrier((swap, parts))
     swap = across(swap, 1)
-
-    used = count * 8
-    frame_rows, z_columns, x_rows, b_rows, c_rows, decays, cumul, steps, carry, keep, summary = call(
-        functools.partial(state_kernel, group, heads, state, offsets),
+    out_stack = call(
+        functools.partial(stack_kernel, group),
+        shape((group * rows, width), BF16),
+        parts,
+        smem=0,
+    )
+
+    frame_rows, x_rows, b_rows, c_rows, decay_rows, steps, keep, summary = call(
+        functools.partial(state_kernel, group, heads, state),
         (
             shape((total, depth), BF16),
-            shape((depth, width), BF16),
             shape((total, width), BF16),
             shape((total, state), BF16),
             shape((total, state), BF16),
-            shape((SPAN, -(-4 * used // SPAN) * SPAN), F32),
-            shape((used, SPAN), F32),
+            shape((3 * count * 8, SPAN), F32),
             shape((count * state, width), F32),
-            shape((total, width), F32),
             shape((count * 8, width), F32),
             shape((state + EDGE, width), BF16),
         ),
-        [record_lengths, decay, bc_mine, frames, swap, *half_parts, *xz_pieces],
-        [pltpu.VMEM((depth, width + 2 * state), BF16)],
+        [record_lengths, decay, xz, bc_mine, frames, swap, *half_parts],
+        [pltpu.VMEM((depth, 2 * state), BF16)],
         flops=2 * total * depth * (width + 2 * state),
     )
     summaries = [later(summary, step) for step in range(1, planes)]
     y = call(
         functools.partial(inner_kernel, group, heads),
         shape((total, width), F32),
-        [x_rows, b_rows, c_rows, decays, cumul],
+        [x_rows, b_rows, c_rows, decay_rows],
         flops=4 * total * SPAN * width,
         smem=0,
     )
-    out_stack, y = lax.optimization_barrier((out_stack, y))
-    out_pieces = [out_stack] + [between_planes(out_stack, step) for step in range(1, planes)]
     silu = call(
         functools.partial(silu_kernel, group),
         shape((total, width), F32),
-        [norm_gain[None], frame_rows, z_columns],
+        [norm_gain[None], frame_rows, xz],
         flops=2 * total * depth * width,
         smem=0,
     )
+    out_stack, summaries, y = lax.optimization_barrier((out_stack, summaries, y))
+    out_pieces = [out_stack] + [between_planes(out_stack, step) for step in range(1, planes)]
     gated, top, bottom = call(
         functools.partial(gate_kernel, heads, state),
         (shape((total, width), BF16), shape((EDGE, width), BF16), shape((EDGE, width), BF16)),
-        [c_rows, y, steps, carry, keep, silu, *summaries],
+        [c_rows, y, steps, decay_rows, keep, silu, *summaries],
         flops=2 * total * state * width,
         smem=0,
     )
     before, after = later(bottom, 1), earlier(top, 1)
+    gated, out_pieces[1] = lax.optimization_barrier((gated, out_pieces[1]))
     ends = pltpu.SMEM((record_lengths.shape[0] + 1,), jnp.int32)
     inner = call(
         functools.partial(conv_kernel, group, False),
@@ -531,6 +528,7 @@
         [pltpu.VMEM((total - 2 * SPAN + 2 * EDGE, width), F32), ends],
         flops=2 * total * width * conv_weight.shape[0],
     )
+    inner, out_pieces[2:] = lax.optimization_barrier((inner, out_pieces[2:]))
     act = call(
         functools.partial(conv_kernel, group, True),
         shape((total, width), BF16),

time: 123 us -> 112 us (0.911); the launches traced: 123 us -> 110 us
  waiting for transfers between devices: 53.8 us -> 43.4 us
    ppermute x8 -> x6, waiting for transfers between devices: 22.2 us -> 4.65 us  [between_planes(): lax.ppermute(array, 'tm', [(i, i ^ step * group) for i in range(times)])]
    ppermute x12, waiting for transfers between devices: 22.3 us -> 34 us  [in_plane(): return lax.ppermute(array, 'tm', [(i, i ^ step) for i in range(times)])]
    ppermute x2 -> x0, waiting for transfers between devices: 7.71 us -> none  [the longest x1 7.71 us: along_planes(): third = lax.ppermute(again, 'tm', pairs([(1, 0), (2, 3)]))]
    all_to_all x0 -> x1, starting transfers between devices: none -> 5.42 us  [local(): lax.all_to_all(blocks, 'tm', split_axis=0, concat_axis=0, tiled=True)]
    ppermute x3, waiting for transfers between devices: 1.53 us -> 4.28 us  [across(): return lax.ppermute(array, 'head', [(i, i ^ step) for i in range(cores)])]
    ppermute x2 -> x0, starting transfers between devices: 1.96 us -> none  [the longest x1 1.28 us: along_planes(): third = lax.ppermute(again, 'tm', pairs([(1, 0), (2, 3)]))]
    ppermute x8 -> x6, starting transfers between devices: 13 us -> 11.3 us  [between_planes(): lax.ppermute(array, 'tm', [(i, i ^ step * group) for i in range(times)])]
    ppermute x12, starting transfers between devices: 15.7 us -> 14.1 us  [in_plane(): return lax.ppermute(array, 'tm', [(i, i ^ step) for i in range(times)])]
  transfers between devices with their start and end apart: 30 -> 27, of which waited for: 14 -> 15; matrix products, arithmetic and copies ran while one was open for 1% -> 0% of each run, Pallas kernels for 6% -> 7%
where the time goes in v5:
time: 112 us; the launch traced here: 110 us
  starting transfers between devices  44.7 us (40%)
  waiting for transfers between devices  43.4 us (39%)
  Pallas kernels  16.3 us (15%)
  local copies, waits for them, and re-layouts  4.84 us (4%)
    ppermute x12, waiting for transfers between devices, in_plane(): return lax.ppermute(array, 'tm', [(i, i ^ step) for i in range(times)])  34 us
    pallas_call x13, Pallas kernels, call(): pl.pallas_call(kernel, out_shape=out_shape, in_specs=in_specs, out_specs=...  16.3 us
    ppermute x12, starting transfers between devices, in_plane(): return lax.ppermute(array, 'tm', [(i, i ^ step) for i in range(times)])  14.1 us
    ppermute x4, starting transfers between devices, later(): lax.ppermute(array, 'tm', [(i, i + step * group) for i in range(times - s...  12 us
    ppermute x6, starting transfers between devices, between_planes(): lax.ppermute(array, 'tm', [(i, i ^ step * group) for i in range(times)])  11.3 us
    all_to_all x1, starting transfers between devices, local(): lax.all_to_all(blocks, 'tm', split_axis=0, concat_axis=0, tiled=True)  5.42 us
    unnamed x24, local copies, waits for them, and re-layouts  4.79 us
    ppermute x6, waiting for transfers between devices, between_planes(): lax.ppermute(array, 'tm', [(i, i ^ step * group) for i in range(times)])  4.65 us
  transfers between devices with their start and end apart: 27, of which 15 were waited for; matrix products, arithmetic and copies ran while one was open for 0% of the time, Pallas kernels for 7%

profile of v5, /device:TPU:0, one launch (start us, length us, event | category | flops | bytes accessed | tf_op | source)
XLA Modules:
  0.0 110.4 jit_solution(2310113944853032097)
XLA Ops:
  0.0 0.8 copy-done
  0.8 5.0 %collective-permute-start.2 = (bf16[64,128]{1,0:T(8,128)(2,1)S(1)}, bf16[64,128]{1,0:T(8,128)(2,1)S(1)}, u32[]{:S(2)}, u32[]{:S(2)}) collective-permute-start(bf16[64,128]{1,0:T(8,128)(2,1)S(1)} %constant_dynamic-slice_fusion.1.refs_0_), channel_id=1, source_target_pairs={{0,24},{2,26},{4,28},{6,30},{8,16},{10,18},{12,20},{14,22},{16,8},... | collective-permute-start | bytes 49160 | tf_op jit(solution)/shard_map/ppermute | solution.py:427
  5.8 0.6 collective-permute-start
  6.4 1.1 %collective-permute-done.2.refs_3_ = bf16[64,128]{1,0:T(8,128)(2,1)S(1)} collective-permute-done((bf16[64,128]{1,0:T(8,128)(2,1)S(1)}, bf16[64,128]{1,0:T(8,128)(2,1)S(1)}, u32[]{:S(2)}, u32[]{:S(2)}) %collective-permute-start.2) | collective-permute-done | bytes 16416 | tf_op jit(solution)/shard_map/ppermute | solution.py:427
  7.5 2.9 %collective-permute-done.1.refs_2_ = bf16[64,128]{1,0:T(8,128)(2,1)S(1)} collective-permute-done((bf16[64,128]{1,0:T(8,128)(2,1)S(1)}, bf16[64,128]{1,0:T(8,128)(2,1)S(1)}, u32[]{:S(2)}, u32[]{:S(2)}) %collective-permute-start.1) | collective-permute-done | bytes 16416 | tf_op jit(solution)/shard_map/ppermute | solution.py:427
  10.5 0.9 copy-done.3
  11.4 0.9 copy-done.4
  12.3 1.1 shard_map.93
  13.4 5.4 %all-to-all-start = ((bf16[16,64,512]{2,1,0:T(8,128)(2,1)}), bf16[16,64,512]{2,1,0:T(8,128)(2,1)S(1)}, u32[]{:S(2)}, u32[]{:S(2)}) async-start(bf16[16,64,512]{2,1,0:T(8,128)(2,1)} %shard_map.93), calls=%async_computation | async-start | bytes 2097152 | tf_op jit(solution)/shard_map/all_to_all | solution.py:442
  18.8 2.9 %collective-permute-start.8 = (bf16[128,1024]{1,0:T(8,128)(2,1)S(1)}, bf16[128,1024]{1,0:T(8,128)(2,1)S(1)}, u32[]{:S(2)}, u32[]{:S(2)}) collective-permute-start(bf16[128,1024]{1,0:T(8,128)(2,1)S(1)} %constant_dynamic-slice_fusion), channel_id=1, source_target_pairs={{0,6},{2,4},{4,2},{6,0},{8,14},{10,12},{12,10},{14,8},{16,22},{18,... | collective-permute-start | bytes 786440 | tf_op jit(solution)/shard_map/ppermute | solution.py:415
  21.7 0.6 collective-permute-start.7
  22.5 2.0 %collective-permute-start.3 = (bf16[320,128]{1,0:T(8,128)(2,1)S(1)}, bf16[320,128]{1,0:T(8,128)(2,1)S(1)}, u32[]{:S(2)}, u32[]{:S(2)}) collective-permute-start(bf16[320,128]{1,0:T(8,128)(2,1)S(1)} %get-tuple-element.63), channel_id=1, source_target_pairs={{0,2},{2,0},{4,6},{6,4},{8,10},{10,8},{12,14},{14,12},{16,18},{18,... | collective-permute-start | bytes 245768 | tf_op jit(solution)/shard_map/ppermute | solution.py:415
  24.4 1.5 %collective-permute-start.4 = (bf16[320,128]{1,0:T(8,128)(2,1)S(1)}, bf16[320,128]{1,0:T(8,128)(2,1)S(1)}, u32[]{:S(2)}, u32[]{:S(2)}) collective-permute-start(bf16[320,128]{1,0:T(8,128)(2,1)S(1)} %get-tuple-element.64), channel_id=1, source_target_pairs={{0,4},{2,6},{4,0},{6,2},{8,12},{10,14},{12,8},{14,10},{16,20},{18,... | collective-permute-start | bytes 245768 | tf_op jit(solution)/shard_map/ppermute | solution.py:415
  25.9 13.5 %collective-permute-done.8.refs_6_.refs_2_ = bf16[128,1024]{1,0:T(8,128)(2,1)S(1)} collective-permute-done((bf16[128,1024]{1,0:T(8,128)(2,1)S(1)}, bf16[128,1024]{1,0:T(8,128)(2,1)S(1)}, u32[]{:S(2)}, u32[]{:S(2)}) %collective-permute-start.8) | collective-permute-done | bytes 262176 | tf_op jit(solution)/shard_map/ppermute | solution.py:415
  39.4 3.5 %collective-permute-done.7.refs_5_.refs_1_ = bf16[128,1024]{1,0:T(8,128)(2,1)S(1)} collective-permute-done((bf16[128,1024]{1,0:T(8,128)(2,1)S(1)}, bf16[128,1024]{1,0:T(8,128)(2,1)S(1)}, u32[]{:S(2)}, u32[]{:S(2)}) %collective-permute-start.7) | collective-permute-done | bytes 262176 | tf_op jit(solution)/shard_map/ppermute | solution.py:415
  42.9 2.2 %collective-permute-done.6.refs_4_.refs_0_ = bf16[128,1024]{1,0:T(8,128)(2,1)S(1)} collective-permute-done((bf16[128,1024]{1,0:T(8,128)(2,1)S(1)}, bf16[128,1024]{1,0:T(8,128)(2,1)S(1)}, u32[]{:S(2)}, u32[]{:S(2)}) %collective-permute-start.6) | collective-permute-done | bytes 262176 | tf_op jit(solution)/shard_map/ppermute | solution.py:415
  45.1 0.7 collective-permute-start.9
  45.8 2.1 %collective-permute-start.10 = (bf16[64,256]{1,0:T(8,128)(2,1)S(1)}, bf16[64,256]{1,0:T(8,128)(2,1)S(1)}, u32[]{:S(2)}, u32[]{:S(2)}) collective-permute-start(bf16[64,256]{1,0:T(8,128)(2,1)S(1)} %get-tuple-element.74), channel_id=1, source_target_pairs={{0,4},{2,6},{4,0},{6,2},{8,12},{10,14},{12,8},{14,10},{16,20},{18,... | collective-permute-start | bytes 98312 | tf_op jit(solution)/shard_map/ppermute | solution.py:415
  47.9 0.7 collective-permute-start.11
  49.1 0.7 collective-permute-done.10.refs_2_
  49.8 2.9 %collective-permute-done.11.refs_3_ = bf16[64,256]{1,0:T(8,128)(2,1)S(1)} collective-permute-done((bf16[64,256]{1,0:T(8,128)(2,1)S(1)}, bf16[64,256]{1,0:T(8,128)(2,1)S(1)}, u32[]{:S(2)}, u32[]{:S(2)}) %collective-permute-start.11) | collective-permute-done | bytes 32800 | tf_op jit(solution)/shard_map/ppermute | solution.py:415
  52.8 2.7 %collective-permute-done.12.swap_ref = bf16[512,1024]{1,0:T(8,128)(2,1)S(1)} collective-permute-done((bf16[512,1024]{1,0:T(8,128)(2,1)S(1)}, bf16[512,1024]{1,0:T(8,128)(2,1)S(1)}, u32[]{:S(2)}, u32[]{:S(2)}) %collective-permute-start.12) | collective-permute-done | bytes 1048608 | tf_op jit(solution)/shard_map/ppermute | solution.py:424
  55.4 1.0 copy-done.9
  56.4 1.2 %copy-done.10 = bf16[512,1024]{1,0:T(8,128)(2,1)S(1)} copy-done((bf16[512,1024]{1,0:T(8,128)(2,1)S(1)}, bf16[512,1024]{1,0:T(8,128)(2,1)}, u32[]{:S(2)}) %copy-start.10) | copy-done | bytes 1048600
  57.6 4.8 %shard_map.95 = (bf16[1024,1024]{1,0:T(8,128)(2,1)}, bf16[1024,256]{1,0:T(8,128)(2,1)S(1)}, bf16[1024,128]{1,0:T(8,128)(2,1)S(1)}, bf16[1024,128]{1,0:T(8,128)(2...) custom-call(s32[8]{0:T(128)S(1)} %copy-done.8, ...), custom_call_target="tpu_custom_call" | custom-call | flops 1073741824 | bytes 8134688 | tf_op jit(solution)/shard_map/pallas_call | solution.py:27
  62.4 5.3 %collective-permute-start.15 = (bf16[144,256]{1,0:T(8,128)(2,1)S(1)}, bf16[144,256]{1,0:T(8,128)(2,1)S(1)}, u32[]{:S(2)}, u32[]{:S(2)}) collective-permute-start(bf16[144,256]{1,0:T(8,128)(2,1)S(1)} %get-tuple-element.85), channel_id=1, source_target_pairs={{0,24},{2,26},{4,28},{6,30},{1,25},{3,27},{5,29},{7,31}} | collective-permute-start | bytes 221192 | tf_op jit(solution)/shard_map/ppermute | solution.py:418
  67.7 1.3 %collective-permute-start.14 = (bf16[144,256]{1,0:T(8,128)(2,1)S(1)}, bf16[144,256]{1,0:T(8,128)(2,1)S(1)}, u32[]{:S(2)}, u32[]{:S(2)}) collective-permute-start(bf16[144,256]{1,0:T(8,128)(2,1)S(1)} %get-tuple-element.85), channel_id=1, source_target_pairs={{0,16},{2,18},{4,20},{6,22},{8,24},{10,26},{12,28},{14,30},{1,17},... | collective-permute-start | bytes 221192 | tf_op jit(solution)/shard_map/ppermute | solution.py:418
  69.0 2.5 %collective-permute-start.13 = (bf16[144,256]{1,0:T(8,128)(2,1)S(1)}, bf16[144,256]{1,0:T(8,128)(2,1)S(1)}, u32[]{:S(2)}, u32[]{:S(2)}) collective-permute-start(bf16[144,256]{1,0:T(8,128)(2,1)S(1)} %get-tuple-element.85), channel_id=1, source_target_pairs={{0,8},{2,10},{4,12},{6,14},{8,16},{10,18},{12,20},{14,22},{16,24},... | collective-permute-start | bytes 221192 | tf_op jit(solution)/shard_map/ppermute | solution.py:418
  71.5 1.6 %shard_map.97.y_ref = f32[1024,256]{1,0:T(8,128)S(1)} custom-call(bf16[1024,256]{1,0:T(8,128)(2,1)S(1)} %get-tuple-element.86.x_ref, bf16[1024,128]{1,0:T(8,128)(2,1)S(1)} %get-tuple-element.87.b_ref, bf16[1024,128]{1,0:T(8,128)(2,1)S(1)} %get-tuple-element.80.c_ref, f32[192,128]{1,0:T(8,128)S(1)} %get-tuple-element.88.rows_ref), custom_call_target="tpu_custom_call" | custom-call | flops 134217728 | bytes 2195456 | tf_op jit(solution)/shard_map/pallas_call | solution.py:27
  73.1 0.3 collective-permute-done.13.refs_0_
  73.4 2.4 %collective-permute-start.16 = (bf16[256,256]{1,0:T(8,128)(2,1)S(1)}, bf16[256,256]{1,0:T(8,128)(2,1)S(1)}, u32[]{:S(2)}, u32[]{:S(2)}) collective-permute-start(bf16[256,256]{1,0:T(8,128)(2,1)S(1)} %shard_map.96.refs_0_), channel_id=1, source_target_pairs={{0,8},{2,10},{4,12},{6,14},{8,0},{10,2},{12,4},{14,6},{16,24},{18,... | collective-permute-start | bytes 393224 | tf_op jit(solution)/shard_map/ppermute | solution.py:427
  75.8 3.3 %collective-permute-start.20 = (bf16[256,256]{1,0:T(8,128)(2,1)S(1)}, bf16[256,256]{1,0:T(8,128)(2,1)S(1)}, u32[]{:S(2)}, u32[]{:S(2)}) collective-permute-start(bf16[256,256]{1,0:T(8,128)(2,1)S(1)} %shard_map.96.refs_0_), channel_id=1, source_target_pairs={{0,24},{2,26},{4,28},{6,30},{8,16},{10,18},{12,20},{14,22},{16,8},... | collective-permute-start | bytes 393224 | tf_op jit(solution)/shard_map/ppermute | solution.py:427
  79.1 0.9 shard_map.98.silu_ref
  80.0 1.5 %shard_map.99 = (bf16[1024,256]{1,0:T(8,128)(2,1)S(1)}, bf16[16,256]{1,0:T(8,128)(2,1)S(1)}, bf16[16,256]{1,0:T(8,128)(2,1)S(1)}) custom-call(bf16[1024,128]{1,0:T(8,128)(2,1)S(1)} %get-tuple-element.80.c_ref, f32[1024,256]{1,0:T(8,128)S(1)} %shard_map.97.y_ref, f32[1024,256]{1,0:T(8,128)S(1)} %get-tuple-element.90.step_ref, ...), custom_call_target="tpu_custom_call" | custom-call | flops 67108864 | bytes 4333568 | tf_op jit(solution)/shard_map/pallas_call | solution.py:27
  81.5 3.0 %collective-permute-start.17 = (bf16[16,256]{1,0:T(8,128)(2,1)S(1)}, bf16[16,256]{1,0:T(8,128)(2,1)S(1)}, u32[]{:S(2)}, u32[]{:S(2)}) collective-permute-start(bf16[16,256]{1,0:T(8,128)(2,1)S(1)} %get-tuple-element.99), channel_id=1, source_target_pairs={{0,8},{2,10},{4,12},{6,14},{8,16},{10,18},{12,20},{14,22},{16,24},... | collective-permute-start | bytes 24584 | tf_op jit(solution)/shard_map/ppermute | solution.py:418
  84.5 1.3 %collective-permute-start.18 = (bf16[16,256]{1,0:T(8,128)(2,1)S(1)}, bf16[16,256]{1,0:T(8,128)(2,1)S(1)}, u32[]{:S(2)}, u32[]{:S(2)}) collective-permute-start(bf16[16,256]{1,0:T(8,128)(2,1)S(1)} %get-tuple-element.100), channel_id=1, source_target_pairs={{8,0},{10,2},{12,4},{14,6},{16,8},{18,10},{20,12},{22,14},{24,16},... | collective-permute-start | bytes 24584 | tf_op jit(solution)/shard_map/ppermute | solution.py:421
  85.9 3.9 %shard_map.100.refs_2_ = bf16[768,256]{1,0:T(8,128)(2,1)S(1)} custom-call(s32[8]{0:T(128)S(1)} %copy-done.8, f32[31,1024]{1,0:T(8,128)S(1)} %copy-done.2, bf16[1024,256]{1,0:T(8,128)(2,1)S(1)} %get-tuple-element.98.gated_ref), custom_call_target="tpu_custom_call" | custom-call | flops 16252928 | bytes 1044512 | tf_op jit(solution)/shard_map/pallas_call | solution.py:27
  89.7 0.6 collective-permute-done.19.refs_2_
  90.5 1.5 %shard_map.101.refs_0_ = bf16[1024,256]{1,0:T(8,128)(2,1)S(1)} custom-call(s32[8]{0:T(128)S(1)} %copy-done.8, f32[31,1024]{1,0:T(8,128)S(1)} %copy-done.2, bf16[1024,256]{1,0:T(8,128)(2,1)S(1)} %get-tuple-element.98.gated_ref, bf16[16,256]{1,0:T(8,128)(2,1)S(1)} %collective-permute-done.17.refs_0_, bf16[16,256]{1,0:T(8,128)(2,1)S(1)} %collective-permute-done.18.refs_1_, ...), custom_call_target="tpu_custom_call" | custom-call | flops 4063232 | bytes 1585184 | tf_op jit(solution)/shard_map/pallas_call | solution.py:27
  92.2 0.6 collective-permute-start.22
  92.7 1.6 %collective-permute-done.22.refs_3_ = bf16[512,256]{1,0:T(8,128)(2,1)S(1)} collective-permute-done((bf16[512,256]{1,0:T(8,128)(2,1)S(1)}, bf16[512,256]{1,0:T(8,128)(2,1)S(1)}, u32[]{:S(2)}, u32[]{:S(2)}) %collective-permute-start.22) | collective-permute-done | bytes 262176 | tf_op jit(solution)/shard_map/ppermute | solution.py:424
  94.4 0.7 shard_map.103
  95.1 0.7 collective-permute-start.23
  95.9 0.9 collective-permute-start.24
  96.7 1.9 %collective-permute-start.25 = (bf16[256,512]{1,0:T(8,128)(2,1)S(1)}, bf16[256,512]{1,0:T(8,128)(2,1)S(1)}, u32[]{:S(2)}, u32[]{:S(2)}) collective-permute-start(bf16[256,512]{1,0:T(8,128)(2,1)S(1)} %get-tuple-element.110), channel_id=1, source_target_pairs={{0,6},{2,4},{4,2},{6,0},{8,14},{10,12},{12,10},{14,8},{16,22},{18,... | collective-permute-start | bytes 786440 | tf_op jit(solution)/shard_map/ppermute | solution.py:415
  98.7 5.7 %collective-permute-done.23 = bf16[256,512]{1,0:T(8,128)(2,1)S(1)} collective-permute-done((bf16[256,512]{1,0:T(8,128)(2,1)S(1)}, bf16[256,512]{1,0:T(8,128)(2,1)S(1)}, u32[]{:S(2)}, u32[]{:S(2)}) %collective-permute-start.23) | collective-permute-done | bytes 262176 | tf_op jit(solution)/shard_map/ppermute | solution.py:415
  104.3 5.2 %collective-permute-done.24 = bf16[256,512]{1,0:T(8,128)(2,1)S(1)} collective-permute-done((bf16[256,512]{1,0:T(8,128)(2,1)S(1)}, bf16[256,512]{1,0:T(8,128)(2,1)S(1)}, u32[]{:S(2)}, u32[]{:S(2)}) %collective-permute-start.24) | collective-permute-done | bytes 262176 | tf_op jit(solution)/shard_map/ppermute | solution.py:415
  109.5 0.8 add_convert_fusion
  (48 shorter events, 1.0 us)
Async XLA Ops:
  0.0 0.8 copy-start
  0.0 22.4 %copy-start.11 = (f32[16,256]{1,0:T(8,128)S(1)}, f32[16,256]{1,0:T(8,128)}, u32[]{:S(2)}) copy-start(f32[16,256]{1,0:T(8,128)} %param.13) | copy-start | bytes 49156
  0.8 6.8 %collective-permute-start.2 = (bf16[64,128]{1,0:T(8,128)(2,1)S(1)}, bf16[64,128]{1,0:T(8,128)(2,1)S(1)}, u32[]{:S(2)}, u32[]{:S(2)}) collective-permute-start(bf16[64,128]{1,0:T(8,128)(2,1)S(1)} %constant_dynamic-slice_fusion.1.refs_0_), channel_id=1, source_target_pairs={{0,24},{2,26},{4,28},{6,30},{8,16},{10,18},{12,20},{14,22},{16,8},... | collective-permute-start | bytes 49160 | tf_op jit(solution)/shard_map/ppermute | solution.py:427
  5.8 4.6 %collective-permute-start.1 = (bf16[64,128]{1,0:T(8,128)(2,1)S(1)}, bf16[64,128]{1,0:T(8,128)(2,1)S(1)}, u32[]{:S(2)}, u32[]{:S(2)}) collective-permute-start(bf16[64,128]{1,0:T(8,128)(2,1)S(1)} %constant_dynamic-slice_fusion.1.refs_0_), channel_id=1, source_target_pairs={{0,16},{2,18},{4,20},{6,22},{8,24},{10,26},{12,28},{14,30},{16,0},... | collective-permute-start | bytes 49160 | tf_op jit(solution)/shard_map/ppermute | solution.py:427
  5.8 4.6 %collective-permute-start = (bf16[64,128]{1,0:T(8,128)(2,1)S(1)}, bf16[64,128]{1,0:T(8,128)(2,1)S(1)}, u32[]{:S(2)}, u32[]{:S(2)}) collective-permute-start(bf16[64,128]{1,0:T(8,128)(2,1)S(1)} %constant_dynamic-slice_fusion.1.refs_0_), channel_id=1, source_target_pairs={{0,8},{2,10},{4,12},{6,14},{8,0},{10,2},{12,4},{14,6},{16,24},{18,... | collective-permute-start | bytes 49160 | tf_op jit(solution)/shard_map/ppermute | solution.py:427
  10.5 0.9 copy-start.3
  11.4 0.9 copy-start.4
  12.3 6.5 %copy-start.5 = (bf16[256,1024]{1,0:T(8,128)(2,1)S(1)}, bf16[256,1024]{1,0:T(8,128)(2,1)}, u32[]{:S(2)}) copy-start(bf16[256,1024]{1,0:T(8,128)(2,1)} %own_ref.1) | copy-start | bytes 1572868
  12.3 32.8 %copy-start.6 = (bf16[1024,64]{0,1:T(8,128)(2,1)S(1)}, bf16[1024,64]{0,1:T(8,128)(2,1)}, u32[]{:S(2)}) copy-start(bf16[1024,64]{0,1:T(8,128)(2,1)} %param.16) | copy-start | bytes 393220
  13.4 43.0 %copy-start.8 = (s32[8]{0:T(128)S(1)}, s32[8]{0:T(128)}, u32[]{:S(2)}) copy-start(s32[8]{0:T(128)} %len_ref.5) | copy-start | bytes 100
  13.4 43.0 %all-to-all-start = ((bf16[16,64,512]{2,1,0:T(8,128)(2,1)}), bf16[16,64,512]{2,1,0:T(8,128)(2,1)S(1)}, u32[]{:S(2)}, u32[]{:S(2)}) async-start(bf16[16,64,512]{2,1,0:T(8,128)(2,1)} %shard_map.93), calls=%async_computation | async-start | bytes 2097152 | tf_op jit(solution)/shard_map/all_to_all | solution.py:442
  18.8 20.5 %collective-permute-start.8 = (bf16[128,1024]{1,0:T(8,128)(2,1)S(1)}, bf16[128,1024]{1,0:T(8,128)(2,1)S(1)}, u32[]{:S(2)}, u32[]{:S(2)}) collective-permute-start(bf16[128,1024]{1,0:T(8,128)(2,1)S(1)} %constant_dynamic-slice_fusion), channel_id=1, source_target_pairs={{0,6},{2,4},{4,2},{6,0},{8,14},{10,12},{12,10},{14,8},{16,22},{18,... | collective-permute-start | bytes 786440 | tf_op jit(solution)/shard_map/ppermute | solution.py:415
  21.7 21.2 %collective-permute-start.7 = (bf16[128,1024]{1,0:T(8,128)(2,1)S(1)}, bf16[128,1024]{1,0:T(8,128)(2,1)S(1)}, u32[]{:S(2)}, u32[]{:S(2)}) collective-permute-start(bf16[128,1024]{1,0:T(8,128)(2,1)S(1)} %constant_dynamic-slice_fusion), channel_id=1, source_target_pairs={{0,4},{2,6},{4,0},{6,2},{8,12},{10,14},{12,8},{14,10},{16,20},{18,... | collective-permute-start | bytes 786440 | tf_op jit(solution)/shard_map/ppermute | solution.py:415
  22.3 22.8 %collective-permute-start.6 = (bf16[128,1024]{1,0:T(8,128)(2,1)S(1)}, bf16[128,1024]{1,0:T(8,128)(2,1)S(1)}, u32[]{:S(2)}, u32[]{:S(2)}) collective-permute-start(bf16[128,1024]{1,0:T(8,128)(2,1)S(1)} %constant_dynamic-slice_fusion), channel_id=1, source_target_pairs={{0,2},{2,0},{4,6},{6,4},{8,10},{10,8},{12,14},{14,12},{16,18},{18,... | collective-permute-start | bytes 786440 | tf_op jit(solution)/shard_map/ppermute | solution.py:415
  22.5 25.5 %collective-permute-start.3 = (bf16[320,128]{1,0:T(8,128)(2,1)S(1)}, bf16[320,128]{1,0:T(8,128)(2,1)S(1)}, u32[]{:S(2)}, u32[]{:S(2)}) collective-permute-start(bf16[320,128]{1,0:T(8,128)(2,1)S(1)} %get-tuple-element.63), channel_id=1, source_target_pairs={{0,2},{2,0},{4,6},{6,4},{8,10},{10,8},{12,14},{14,12},{16,18},{18,... | collective-permute-start | bytes 245768 | tf_op jit(solution)/shard_map/ppermute | solution.py:415
  24.4 24.2 %collective-permute-start.4 = (bf16[320,128]{1,0:T(8,128)(2,1)S(1)}, bf16[320,128]{1,0:T(8,128)(2,1)S(1)}, u32[]{:S(2)}, u32[]{:S(2)}) collective-permute-start(bf16[320,128]{1,0:T(8,128)(2,1)S(1)} %get-tuple-element.64), channel_id=1, source_target_pairs={{0,4},{2,6},{4,0},{6,2},{8,12},{10,14},{12,8},{14,10},{16,20},{18,... | collective-permute-start | bytes 245768 | tf_op jit(solution)/shard_map/ppermute | solution.py:415
  39.4 9.3 %collective-permute-start.5 = (bf16[320,128]{1,0:T(8,128)(2,1)S(1)}, bf16[320,128]{1,0:T(8,128)(2,1)S(1)}, u32[]{:S(2)}, u32[]{:S(2)}) collective-permute-start(bf16[320,128]{1,0:T(8,128)(2,1)S(1)} %get-tuple-element.65), channel_id=1, source_target_pairs={{0,6},{2,4},{4,2},{6,0},{8,14},{10,12},{12,10},{14,8},{16,22},{18,... | collective-permute-start | bytes 245768 | tf_op jit(solution)/shard_map/ppermute | solution.py:415
  45.1 4.0 %collective-permute-start.9 = (bf16[64,256]{1,0:T(8,128)(2,1)S(1)}, bf16[64,256]{1,0:T(8,128)(2,1)S(1)}, u32[]{:S(2)}, u32[]{:S(2)}) collective-permute-start(bf16[64,256]{1,0:T(8,128)(2,1)S(1)} %get-tuple-element.73), channel_id=1, source_target_pairs={{0,2},{2,0},{4,6},{6,4},{8,10},{10,8},{12,14},{14,12},{16,18},{18,... | collective-permute-start | bytes 98312 | tf_op jit(solution)/shard_map/ppermute | solution.py:415
  45.8 4.0 %collective-permute-start.10 = (bf16[64,256]{1,0:T(8,128)(2,1)S(1)}, bf16[64,256]{1,0:T(8,128)(2,1)S(1)}, u32[]{:S(2)}, u32[]{:S(2)}) collective-permute-start(bf16[64,256]{1,0:T(8,128)(2,1)S(1)} %get-tuple-element.74), channel_id=1, source_target_pairs={{0,4},{2,6},{4,0},{6,2},{8,12},{10,14},{12,8},{14,10},{16,20},{18,... | collective-permute-start | bytes 98312 | tf_op jit(solution)/shard_map/ppermute | solution.py:415
  47.9 4.8 %collective-permute-start.11 = (bf16[64,256]{1,0:T(8,128)(2,1)S(1)}, bf16[64,256]{1,0:T(8,128)(2,1)S(1)}, u32[]{:S(2)}, u32[]{:S(2)}) collective-permute-start(bf16[64,256]{1,0:T(8,128)(2,1)S(1)} %get-tuple-element.75), channel_id=1, source_target_pairs={{0,6},{2,4},{4,2},{6,0},{8,14},{10,12},{12,10},{14,8},{16,22},{18,... | collective-permute-start | bytes 98312 | tf_op jit(solution)/shard_map/ppermute | solution.py:415
  52.8 2.7 %collective-permute-start.12 = (bf16[512,1024]{1,0:T(8,128)(2,1)S(1)}, bf16[512,1024]{1,0:T(8,128)(2,1)S(1)}, u32[]{:S(2)}, u32[]{:S(2)}) collective-permute-start(bf16[512,1024]{1,0:T(8,128)(2,1)S(1)} %get-tuple-element.76), channel_id=1, source_target_pairs={{0,1},{1,0},{2,3},{3,2},{4,5},{5,4},{6,7},{7,6},{8,9},{9,8},{10,11... | collective-permute-start | bytes 3145736 | tf_op jit(solution)/shard_map/ppermute | solution.py:424
  55.4 1.0 copy-start.9
  56.4 1.2 %copy-start.10 = (bf16[512,1024]{1,0:T(8,128)(2,1)S(1)}, bf16[512,1024]{1,0:T(8,128)(2,1)}, u32[]{:S(2)}) copy-start(bf16[512,1024]{1,0:T(8,128)(2,1)} %copy-done.9) | copy-start | bytes 3145732
  62.4 16.7 %copy-start.1 = (bf16[1024,1024]{1,0:T(8,128)(2,1)S(1)}, bf16[1024,1024]{1,0:T(8,128)(2,1)}, u32[]{:S(2)}) copy-start(bf16[1024,1024]{1,0:T(8,128)(2,1)} %get-tuple-element.92.frames_ref) | copy-start | bytes 6291460
  62.4 16.7 %copy-start.7 = (f32[1024]{0:T(1024)S(1)}, f32[1024]{0:T(1024)}, u32[]{:S(2)}) copy-start(f32[1024]{0:T(1024)} %param.14) | copy-start | bytes 12292
  62.4 10.6 %collective-permute-start.15 = (bf16[144,256]{1,0:T(8,128)(2,1)S(1)}, bf16[144,256]{1,0:T(8,128)(2,1)S(1)}, u32[]{:S(2)}, u32[]{:S(2)}) collective-permute-start(bf16[144,256]{1,0:T(8,128)(2,1)S(1)} %get-tuple-element.85), channel_id=1, source_target_pairs={{0,24},{2,26},{4,28},{6,30},{1,25},{3,27},{5,29},{7,31}} | collective-permute-start | bytes 221192 | tf_op jit(solution)/shard_map/ppermute | solution.py:418
  67.7 5.4 %collective-permute-start.14 = (bf16[144,256]{1,0:T(8,128)(2,1)S(1)}, bf16[144,256]{1,0:T(8,128)(2,1)S(1)}, u32[]{:S(2)}, u32[]{:S(2)}) collective-permute-start(bf16[144,256]{1,0:T(8,128)(2,1)S(1)} %get-tuple-element.85), channel_id=1, source_target_pairs={{0,16},{2,18},{4,20},{6,22},{8,24},{10,26},{12,28},{14,30},{1,17},... | collective-permute-start | bytes 221192 | tf_op jit(solution)/shard_map/ppermute | solution.py:418
  69.0 4.4 %collective-permute-start.13 = (bf16[144,256]{1,0:T(8,128)(2,1)S(1)}, bf16[144,256]{1,0:T(8,128)(2,1)S(1)}, u32[]{:S(2)}, u32[]{:S(2)}) collective-permute-start(bf16[144,256]{1,0:T(8,128)(2,1)S(1)} %get-tuple-element.85), channel_id=1, source_target_pairs={{0,8},{2,10},{4,12},{6,14},{8,16},{10,18},{12,20},{14,22},{16,24},... | collective-permute-start | bytes 221192 | tf_op jit(solution)/shard_map/ppermute | solution.py:418
  73.4 12.4 %collective-permute-start.16 = (bf16[256,256]{1,0:T(8,128)(2,1)S(1)}, bf16[256,256]{1,0:T(8,128)(2,1)S(1)}, u32[]{:S(2)}, u32[]{:S(2)}) collective-permute-start(bf16[256,256]{1,0:T(8,128)(2,1)S(1)} %shard_map.96.refs_0_), channel_id=1, source_target_pairs={{0,8},{2,10},{4,12},{6,14},{8,0},{10,2},{12,4},{14,6},{16,24},{18,... | collective-permute-start | bytes 393224 | tf_op jit(solution)/shard_map/ppermute | solution.py:427
  75.8 13.9 %collective-permute-start.20 = (bf16[256,256]{1,0:T(8,128)(2,1)S(1)}, bf16[256,256]{1,0:T(8,128)(2,1)S(1)}, u32[]{:S(2)}, u32[]{:S(2)}) collective-permute-start(bf16[256,256]{1,0:T(8,128)(2,1)S(1)} %shard_map.96.refs_0_), channel_id=1, source_target_pairs={{0,24},{2,26},{4,28},{6,30},{8,16},{10,18},{12,20},{14,22},{16,8},... | collective-permute-start | bytes 393224 | tf_op jit(solution)/shard_map/ppermute | solution.py:427
  79.1 11.2 %collective-permute-start.19 = (bf16[256,256]{1,0:T(8,128)(2,1)S(1)}, bf16[256,256]{1,0:T(8,128)(2,1)S(1)}, u32[]{:S(2)}, u32[]{:S(2)}) collective-permute-start(bf16[256,256]{1,0:T(8,128)(2,1)S(1)} %shard_map.96.refs_0_), channel_id=1, source_target_pairs={{0,16},{2,18},{4,20},{6,22},{8,24},{10,26},{12,28},{14,30},{16,0},... | collective-permute-start | bytes 393224 | tf_op jit(solution)/shard_map/ppermute | solution.py:427
  80.0 5.8 %copy-start.2 = (f32[31,1024]{1,0:T(8,128)S(1)}, f32[31,1024]{1,0:T(8,128)}, u32[]{:S(2)}) copy-start(f32[31,1024]{1,0:T(8,128)} %taps_ref.3) | copy-start | bytes 380932
  81.5 8.8 %collective-permute-start.17 = (bf16[16,256]{1,0:T(8,128)(2,1)S(1)}, bf16[16,256]{1,0:T(8,128)(2,1)S(1)}, u32[]{:S(2)}, u32[]{:S(2)}) collective-permute-start(bf16[16,256]{1,0:T(8,128)(2,1)S(1)} %get-tuple-element.99), channel_id=1, source_target_pairs={{0,8},{2,10},{4,12},{6,14},{8,16},{10,18},{12,20},{14,22},{16,24},... | collective-permute-start | bytes 24584 | tf_op jit(solution)/shard_map/ppermute | solution.py:418
  84.5 5.9 %collective-permute-start.18 = (bf16[16,256]{1,0:T(8,128)(2,1)S(1)}, bf16[16,256]{1,0:T(8,128)(2,1)S(1)}, u32[]{:S(2)}, u32[]{:S(2)}) collective-permute-start(bf16[16,256]{1,0:T(8,128)(2,1)S(1)} %get-tuple-element.100), channel_id=1, source_target_pairs={{8,0},{10,2},{12,4},{14,6},{16,8},{18,10},{20,12},{22,14},{24,16},... | collective-permute-start | bytes 24584 | tf_op jit(solution)/shard_map/ppermute | solution.py:421
  92.0 2.4 %collective-permute-start.21 = (bf16[1024,256]{1,0:T(8,128)(2,1)S(1)}, bf16[1024,256]{1,0:T(8,128)(2,1)S(1)}, u32[]{:S(2)}, u32[]{:S(2)}) collective-permute-start(bf16[1024,256]{1,0:T(8,128)(2,1)S(1)} %shard_map.101.refs_0_), channel_id=1, source_target_pairs={{0,1},{1,0},{2,3},{3,2},{4,5},{5,4},{6,7},{7,6},{8,9},{9,8},{10,11... | collective-permute-start | bytes 1572872 | tf_op jit(solution)/shard_map/ppermute | solution.py:424
  92.2 2.2 %collective-permute-start.22 = (bf16[512,256]{1,0:T(8,128)(2,1)S(1)}, bf16[512,256]{1,0:T(8,128)(2,1)S(1)}, u32[]{:S(2)}, u32[]{:S(2)}) collective-permute-start(bf16[512,256]{1,0:T(8,128)(2,1)S(1)} %get-tuple-element.106), channel_id=1, source_target_pairs={{0,1},{1,0},{2,3},{3,2},{4,5},{5,4},{6,7},{7,6},{8,9},{9,8},{10,11... | collective-permute-start | bytes 786440 | tf_op jit(solution)/shard_map/ppermute | solution.py:424
  95.1 9.2 %collective-permute-start.23 = (bf16[256,512]{1,0:T(8,128)(2,1)S(1)}, bf16[256,512]{1,0:T(8,128)(2,1)S(1)}, u32[]{:S(2)}, u32[]{:S(2)}) collective-permute-start(bf16[256,512]{1,0:T(8,128)(2,1)S(1)} %get-tuple-element.108), channel_id=1, source_target_pairs={{0,2},{2,0},{4,6},{6,4},{8,10},{10,8},{12,14},{14,12},{16,18},{18,... | collective-permute-start | bytes 786440 | tf_op jit(solution)/shard_map/ppermute | solution.py:415
  95.9 13.7 %collective-permute-start.24 = (bf16[256,512]{1,0:T(8,128)(2,1)S(1)}, bf16[256,512]{1,0:T(8,128)(2,1)S(1)}, u32[]{:S(2)}, u32[]{:S(2)}) collective-permute-start(bf16[256,512]{1,0:T(8,128)(2,1)S(1)} %get-tuple-element.109), channel_id=1, source_target_pairs={{0,4},{2,6},{4,0},{6,2},{8,12},{10,14},{12,8},{14,10},{16,20},{18,... | collective-permute-start | bytes 786440 | tf_op jit(solution)/shard_map/ppermute | solution.py:415
  96.7 12.8 %collective-permute-start.25 = (bf16[256,512]{1,0:T(8,128)(2,1)S(1)}, bf16[256,512]{1,0:T(8,128)(2,1)S(1)}, u32[]{:S(2)}, u32[]{:S(2)}) collective-permute-start(bf16[256,512]{1,0:T(8,128)(2,1)S(1)} %get-tuple-element.110), channel_id=1, source_target_pairs={{0,6},{2,4},{4,2},{6,0},{8,14},{10,12},{12,10},{14,8},{16,22},{18,... | collective-permute-start | bytes 786440 | tf_op jit(solution)/shard_map/ppermute | solution.py:415

commit v6 on v5

--- a/solution.py
+++ b/solution.py
@@ -12,6 +12,9 @@
 EDGE = 16
 BF16 = jnp.bfloat16
 F32 = jnp.float32
+STACK_HINT = 40_000_000_000
+ASSEMBLE_HINT = 40_000_000_000
+ALL_VMEM_BYTES = 63 * 1024 * 1024
 VMEM_BYTES = 48 * 1024 * 1024
 
 
@@ -19,9 +22,10 @@
     return lax.dot_general(a, b, (dims, ((), ())), precision=precision, preferred_element_type=F32)
 
 
-def call(kernel, out_shape, operands, scratch=(), flops=0, smem=1):
+def call(kernel, out_shape, operands, scratch=(), flops=0, smem=1, anywhere=0, vmem=VMEM_BYTES):
     in_specs = [pl.BlockSpec(memory_space=pltpu.SMEM)] * smem
-    in_specs += [pl.BlockSpec(memory_space=pltpu.VMEM)] * (len(operands) - smem)
+    in_specs += [pl.BlockSpec(memory_space=pltpu.VMEM)] * (len(operands) - smem - anywhere)
+    in_specs += [pl.BlockSpec(memory_space=pl.ANY)] * anywhere
     moved = sum(a.size * a.dtype.itemsize for a in operands)
     moved += sum(a.size * a.dtype.itemsize for a in jax.tree.leaves(out_shape))
     return pl.pallas_call(
@@ -30,7 +34,7 @@
         in_specs=in_specs,
         out_specs=jax.tree.map(lambda _: pl.BlockSpec(memory_space=pltpu.VMEM), out_shape),
         scratch_shapes=list(scratch),
-        compiler_params=pltpu.CompilerParams(vmem_limit_bytes=VMEM_BYTES),
+        compiler_params=pltpu.CompilerParams(vmem_limit_bytes=vmem),
         cost_estimate=pl.CostEstimate(flops=flops, bytes_accessed=moved, transcendentals=0),
     )(*operands)
 
@@ -57,24 +61,22 @@
         dest_ref[pl.ds(pl.multiple_of((plane ^ offset) * rows, rows), rows), : value.shape[1]] = value
 
 
-def pack_kernel(group, *refs):
-    weight_refs, out_refs = refs[:-group], refs[-group:]
+def cut_kernel(group, bc_ref, *refs):
+    weight_refs, refs = refs[:3], refs[3:]
+    bc_half_ref, out_refs, sems = refs[0], refs[1:-1], refs[-1]
+    place, _ = plane_place(group)
+    parity = lax.rem(lax.axis_index("head"), 2)
     width = weight_refs[0].shape[1] // group
-    place, _ = plane_place(group)
+    copies = [(bc_ref.at[:, pl.ds(pl.multiple_of(parity * LANES, LANES), LANES)], bc_half_ref)]
     for step, out_ref in enumerate(out_refs):
         lanes = pl.ds(pl.multiple_of((place ^ step) * width, LANES), width)
         for number, weight_ref in enumerate(weight_refs):
-            out_ref[:, number * width : (number + 1) * width] = weight_ref[:, lanes]
-
-
-def pack_all_kernel(group, *refs):
-    weight_refs, out_ref = refs[:-1], refs[-1]
-    width = weight_refs[0].shape[1] // group
-    for target in range(out_ref.shape[0]):
-        block = target % group
-        for number, weight_ref in enumerate(weight_refs):
-            columns = weight_ref[:, block * width : (block + 1) * width]
-            out_ref[target, :, number * width : (number + 1) * width] = columns
+            copies.append((weight_ref.at[:, lanes], out_ref.at[:, number * width : (number + 1) * width]))
+    started = [pltpu.make_async_copy(a, b, sems.at[number]) for number, (a, b) in enumerate(copies)]
+    for copy in started:
+        copy.start()
+    for copy in started:
+        copy.wait()
 
 
 def stack_kernel(group, *refs):
@@ -90,14 +92,32 @@
             first += width
 
 
-def share_bc_kernel(group, decay_ref, *refs):
+def assemble_kernel(group, offsets, *refs):
+    pieces, dest_refs = refs[: len(offsets)], refs[len(offsets) :]
+    _, plane = plane_place(group)
+    first = 0
+    for dest_ref in dest_refs:
+        width = dest_ref.shape[1]
+        fill_planes(plane, dest_ref, pieces, offsets, slice(first, first + width))
+        first += width
+
+
+def tiles_below(half, number):
+    return slice(half + number // 8 * 16, half + number // 8 * 16 + 16), slice(number % 8 * LANES, (number % 8 + 1) * LANES)
+
+
+def payload_kernel(group, decay_ref, frames_ref, *refs):
     bc_refs, out_refs = refs[:-group], refs[-group:]
     place, _ = plane_place(group)
-    rows = bc_refs[0].shape[0]
-    below = len(bc_refs) * rows
+    half, rows = frames_ref.shape[0] // 2, bc_refs[0].shape[0]
+    mine = pl.ds(pl.multiple_of(lax.rem(lax.axis_index("head"), 2) * half, half), half)
     for step, out_ref in enumerate(out_refs):
-        for number, bc_ref in enumerate(bc_refs):
-            out_ref[number * rows : (number + 1) * rows, :] = bc_ref[...]
+        out_ref[:half, :] = frames_ref[mine, :]
+        tile = 0
+        for bc_ref in bc_refs:
+            for at in range(0, rows, 16):
+                out_ref[tiles_below(half, tile)] = bc_ref[at : at + 16, :]
+                tile += 1
         left = decay_ref[place ^ step]
         terms = []
         for _ in range(3):
@@ -107,30 +127,33 @@
         terms.append(jnp.zeros_like(left))
         terms = jnp.concatenate(terms, axis=0).astype(BF16)
         for span in range(terms.shape[1] // SPAN):
-            rows_here = slice(below + span * 32, below + (span + 1) * 32)
-            out_ref[rows_here, :] = terms[:, span * SPAN : (span + 1) * SPAN]
-
-
-def swap_kernel(group, rows, *refs):
-    part_refs, half_refs = refs[:group], refs[group : 2 * group - 1]
-    swap_ref, bc_ref, decay_ref = refs[2 * group - 1 :]
+            for at in (0, 16):
+                out_ref[tiles_below(half, tile)] = terms[at : at + 16, span * SPAN : (span + 1) * SPAN]
+                tile += 1
+
+
+def swap_kernel(group, rows, half, *refs):
+    part_refs, (swap_ref, bc_ref, decay_ref) = refs[:group], refs[group:]
     place, plane = plane_place(group)
     planes = bc_ref.shape[0] // (group * rows)
-    below = planes * rows
-    spans = (part_refs[0].shape[0] - below) // 32
+    spans = 2 * half // SPAN
     for step, part_ref in enumerate(part_refs):
         block = place ^ step
+        tile = 0
         for offset in range(planes):
-            at = pl.multiple_of(((plane ^ offset) * group + block) * rows, rows)
-            bc_ref[pl.ds(at, rows), :] = part_ref[offset * rows : (offset + 1) * rows, :]
+            first = ((plane ^ offset) * group + block) * rows
+            for at in range(0, rows, 16):
+                bc_ref[pl.ds(pl.multiple_of(first + at, 16), 16), :] = part_ref[tiles_below(half, tile)]
+                tile += 1
         for span in range(spans):
-            terms = part_ref[below + span * 32 : below + (span + 1) * 32, :].astype(F32)
+            top = part_ref[tiles_below(half, tile)].astype(F32)
+            bottom = part_ref[tiles_below(half, tile + 1)].astype(F32)
+            tile += 2
             at = pl.multiple_of((block * spans + span) * 8, 8)
-            decay_ref[pl.ds(at, 8), :] = terms[:8] + terms[8:16] + terms[16:24]
-    half = half_refs[0].shape[0]
-    for number, half_ref in enumerate(half_refs):
-        swap_ref[number * half : (number + 1) * half, :] = half_ref[...]
-    top = len(half_refs) * half
+            decay_ref[pl.ds(at, 8), :] = top[:8] + top[8:] + bottom[:8]
+        if step:
+            swap_ref[(step - 1) * half : step * half, :] = part_ref[:half, :]
+    top = (group - 1) * half
     height = swap_ref.shape[0] - top
     for number in range(bc_ref.shape[0] // height):
         lanes = slice(number * LANES, (number + 1) * LANES)
@@ -146,7 +169,7 @@
     return dot(both, chosen, ((0,), (0,)))
 
 
-def state_kernel(group, heads, state, len_ref, decay_ref, xz_ref, bc_half_ref, own_ref, swap_ref, *refs):
+def state_kernel(group, heads, state, len_ref, decay_ref, x_weight_ref, bc_half_ref, own_ref, swap_ref, *refs):
     half_refs, refs = refs[: group - 1], refs[group - 1 :]
     frames_ref, x_ref, b_ref, c_ref, rows_ref, step_ref, keep_ref, send_ref, weight_ref = refs
     place, plane = plane_place(group)
@@ -162,7 +185,7 @@
         block = (place ^ (number + 1)) * frames
         mine = pl.ds(pl.multiple_of(block + parity * half, half), half)
         other = pl.ds(pl.multiple_of(block + (1 - parity) * half, half), half)
-        frames_ref[mine, :] = half_ref[...]
+        frames_ref[mine, :] = half_ref[:half, :]
         frames_ref[other, :] = swap_ref[number * half : (number + 1) * half, :]
     mine = pl.ds(pl.multiple_of(parity * LANES, LANES), LANES)
     other = pl.ds(pl.multiple_of((1 - parity) * LANES, LANES), LANES)
@@ -193,7 +216,7 @@
 
     for block in range(group):
         rows = slice(block * frames, (block + 1) * frames)
-        x_ref[rows, :] = dot(frames_ref[rows, :], xz_ref[:, :width]).astype(BF16)
+        x_ref[rows, :] = dot(frames_ref[rows, :], x_weight_ref[...]).astype(BF16)
         product = dot(frames_ref[rows, :], weight_ref[...])
         b_ref[rows, :] = product[:, :state].astype(BF16)
         c_ref[rows, :] = product[:, state:].astype(BF16)
@@ -252,13 +275,13 @@
             )
 
 
-def silu_kernel(group, gain_ref, frames_ref, xz_ref, out_ref):
+def silu_kernel(group, gain_ref, frames_ref, weight_ref, out_ref):
     place, _ = plane_place(group)
     total, width = out_ref.shape
     gain = gain_ref[:, pl.ds(pl.multiple_of(place * width, LANES), width)]
     for block in range(group):
         rows = slice(block * (total // group), (block + 1) * (total // group))
-        z = dot(frames_ref[rows, :], xz_ref[:, width:]).astype(BF16).astype(F32)
+        z = dot(frames_ref[rows, :], weight_ref[...]).astype(BF16).astype(F32)
         out_ref[rows, :] = z / (1.0 + jnp.exp(-z)) * gain
 
 
@@ -430,53 +453,71 @@
     rows = x_weight.shape[0]
     parity = lax.rem(core, 2)
 
-    bc_half = lax.dynamic_slice_in_dim(bc_weight, parity * LANES, LANES, 1)
+    def along_planes(stack):
+        if planes != 4:
+            return [stack] + [between_planes(stack, step) for step in range(1, planes)], tuple(range(planes))
+
+        def pairs(chosen):
+            return [(a * group + q, b * group + q) for a, b in chosen for q in range(group)]
+
+        second = between_planes(stack, 2)
+        first = between_planes(stack, 1)
+        again, stack_then, first = lax.optimization_barrier((second, stack, first))
+        third = lax.ppermute(again, "tm", pairs([(1, 0), (2, 3)]))
+        middle = lax.ppermute(stack_then, "tm", pairs([(1, 2), (2, 1)]))
+        return [stack, first, second, third, middle], (0, 1, 2, 3, 3)
+
+    half_count = frame_count // 2
+    bc_half, *packed = call(
+        functools.partial(cut_kernel, group),
+        (
+            shape((rows, LANES), BF16),
+            *(shape((rows, 3 * width), BF16) for _ in range(group)),
+        ),
+        [bc_weight, x_weight, z_weight, out_weight.T],
+        [pltpu.SemaphoreType.DMA((1 + 3 * group,))],
+        smem=0,
+        anywhere=4,
+        vmem=ALL_VMEM_BYTES,
+    )
+    parts = [packed[0]] + [in_plane(packed[step], step) for step in range(1, group)]
     bc_pieces = [bc_half] + [between_planes(bc_half, step) for step in range(1, planes)]
-    bc_pieces, x_weight, z_weight = lax.optimization_barrier((bc_pieces, x_weight, z_weight))
-    blocks = call(
-        functools.partial(pack_all_kernel, group),
-        shape((times, rows, 2 * width), BF16),
-        [x_weight, z_weight],
-        smem=0,
-    )
-    xz = lax.all_to_all(blocks, "tm", split_axis=0, concat_axis=0, tiled=True).reshape(depth, 2 * width)
+    parts, bc_pieces = lax.optimization_barrier((parts, bc_pieces))
+    xz_stack, out_stack = call(
+        functools.partial(stack_kernel, group),
+        (shape((group * rows, 2 * width), BF16), shape((group * rows, width), BF16)),
+        parts,
+        flops=STACK_HINT,
+        smem=0,
+    )
+    xz_pieces, offsets = along_planes(xz_stack)
+    x_columns, z_columns = call(
+        functools.partial(assemble_kernel, group, offsets),
+        (shape((depth, width), BF16), shape((depth, width), BF16)),
+        xz_pieces,
+        flops=ASSEMBLE_HINT,
+        smem=0,
+    )
     decay_blocks = jnp.pad(log_decay.reshape(group, heads, frame_count), ((0, 0), (0, 8 - heads), (0, 0)))
-    bc_parts = call(
-        functools.partial(share_bc_kernel, group),
-        tuple(shape((planes * rows + frame_count // SPAN * 32, LANES), BF16) for _ in range(group)),
-        [decay_blocks, *bc_pieces],
-        smem=0,
-    )
-    bc_parts = [bc_parts[0]] + [in_plane(bc_parts[step], step) for step in range(1, group)]
-    half_count = frame_count // 2
-    frame_half = lax.dynamic_slice_in_dim(frames, parity * half_count, half_count, 0)
-    half_parts = [in_plane(frame_half, step) for step in range(1, group)]
+    tiles = planes * rows // 16 + frame_count // SPAN * 2
+    payloads = call(
+        functools.partial(payload_kernel, group),
+        tuple(shape((half_count + -(-tiles // 8) * 16, depth), BF16) for _ in range(group)),
+        [decay_blocks, frames, *bc_pieces],
+        smem=0,
+    )
+    payloads = [payloads[0]] + [in_plane(payloads[step], step) for step in range(1, group)]
     swap, bc_mine, decay = call(
-        functools.partial(swap_kernel, group, rows),
+        functools.partial(swap_kernel, group, rows, half_count),
         (
             shape(((group - 1) * half_count + LANES, depth), BF16),
             shape((depth, LANES), BF16),
             shape((count * 8, SPAN), F32),
         ),
-        [*bc_parts, *half_parts],
-        smem=0,
-    )
-    out_columns, half_parts = lax.optimization_barrier((out_weight.T, half_parts))
-    packed = call(
-        functools.partial(pack_kernel, group),
-        tuple(shape((rows, width), BF16) for _ in range(group)),
-        [out_columns],
-        smem=0,
-    )
-    parts = [packed[0]] + [in_plane(packed[step], step) for step in range(1, group)]
-    swap, parts = lax.optimization_barrier((swap, parts))
+        payloads,
+        smem=0,
+    )
     swap = across(swap, 1)
-    out_stack = call(
-        functools.partial(stack_kernel, group),
-        shape((group * rows, width), BF16),
-        parts,
-        smem=0,
-    )
 
     frame_rows, x_rows, b_rows, c_rows, decay_rows, steps, keep, summary = call(
         functools.partial(state_kernel, group, heads, state),
@@ -490,7 +531,7 @@
             shape((count * 8, width), F32),
             shape((state + EDGE, width), BF16),
         ),
-        [record_lengths, decay, xz, bc_mine, frames, swap, *half_parts],
+        [record_lengths, decay, x_columns, bc_mine, frames, swap, *payloads[1:]],
         [pltpu.VMEM((depth, 2 * state), BF16)],
         flops=2 * total * depth * (width + 2 * state),
     )
@@ -505,7 +546,7 @@
     silu = call(
         functools.partial(silu_kernel, group),
         shape((total, width), F32),
-        [norm_gain[None], frame_rows, xz],
+        [norm_gain[None], frame_rows, z_columns],
         flops=2 * total * depth * width,
         smem=0,
     )

time: 112 us -> 94.3 us (0.84)
  waiting for transfers between devices: 43.4 us -> 32.3 us
  starting transfers between devices: 44.7 us -> 40.2 us
  local copies, waits for them, and re-layouts: 4.84 us -> 0.94 us
  Pallas kernels: 16.3 us -> 18.8 us
    ppermute x12 -> x9, waiting for transfers between devices: 34 us -> 16.9 us  [in_plane(): return lax.ppermute(array, 'tm', [(i, i ^ step) for i in range(times)])]
    ppermute x6 -> x8, waiting for transfers between devices: 4.65 us -> 10.9 us  [between_planes(): lax.ppermute(array, 'tm', [(i, i ^ step * group) for i in range(times)])]
    all_to_all x1 -> x0, starting transfers between devices: 5.42 us -> none  [local(): lax.all_to_all(blocks, 'tm', split_axis=0, concat_axis=0, tiled=True)]
    unnamed x24 -> x16, local copies, waits for them, and re-layouts: 4.79 us -> 0.92 us
    pallas_call x13, Pallas kernels: 16.3 us -> 18.8 us  [call(): pl.pallas_call(kernel, out_shape=out_shape, in_specs=in_specs, out_specs=...]
    ppermute x12 -> x9, starting transfers between devices: 14.1 us -> 11.6 us  [in_plane(): return lax.ppermute(array, 'tm', [(i, i ^ step) for i in range(times)])]
    ppermute x6 -> x8, starting transfers between devices: 11.3 us -> 13.4 us  [between_planes(): lax.ppermute(array, 'tm', [(i, i ^ step * group) for i in range(times)])]
    ppermute x0 -> x2, starting transfers between devices: none -> 1.96 us  [the longest x1 1.28 us: along_planes(): third = lax.ppermute(again, 'tm', pairs([(1, 0), (2, 3)]))]
  transfers between devices with their start and end apart: 27 -> 27, of which waited for: 15 -> 12; matrix products, arithmetic and copies ran while one was open for 0% -> 0% of each run, Pallas kernels for 7% -> 10%
where the time goes in v6:
time: 94.3 us; the launch traced here: 93.4 us
  starting transfers between devices  40.2 us (43%)
  waiting for transfers between devices  32.3 us (34%)
  Pallas kernels  18.8 us (20%)
    pallas_call x13, Pallas kernels, call(): pl.pallas_call(kernel, out_shape=out_shape, in_specs=in_specs, out_specs=...  18.8 us
    ppermute x9, waiting for transfers between devices, in_plane(): return lax.ppermute(array, 'tm', [(i, i ^ step) for i in range(times)])  16.9 us
    ppermute x8, starting transfers between devices, between_planes(): lax.ppermute(array, 'tm', [(i, i ^ step * group) for i in range(times)])  13.4 us
    ppermute x9, starting transfers between devices, in_plane(): return lax.ppermute(array, 'tm', [(i, i ^ step) for i in range(times)])  11.6 us
    ppermute x4, starting transfers between devices, later(): lax.ppermute(array, 'tm', [(i, i + step * group) for i in range(times - s...  11.1 us
    ppermute x8, waiting for transfers between devices, between_planes(): lax.ppermute(array, 'tm', [(i, i ^ step * group) for i in range(times)])  10.9 us
    ppermute x3, waiting for transfers between devices, across(): return lax.ppermute(array, 'head', [(i, i ^ step) for i in range(cores)])  3.11 us
  transfers between devices with their start and end apart: 27, of which 12 were waited for; matrix products, arithmetic and copies ran while one was open for 0% of the time, Pallas kernels for 10%

profile of v6, /device:TPU:0, one launch (start us, length us, event | category | flops | bytes accessed | tf_op | source)
XLA Modules:
  0.0 93.4 jit_solution(6461942343538558810)
XLA Ops:
  0.0 1.8 %shard_map.91 = (bf16[64,128]{1,0:T(8,128)(2,1)}, bf16[64,768]{1,0:T(8,128)(2,1)}, bf16[64,768]{1,0:T(8,128)(2,1)}, bf16[64,768]{1,0:T(8,128)(2,1)}, bf16[64,768]{1,0:T(8,128)(2,1)}) custom-call(bf16[64,256]{1,0:T(8,128)(2,1)} %bc_ref.1, bf16[64,1024]{1,0:T(8,128)(2,1)} %refs_0_.1, bf16[64,1024]{1,0:T(8,128)(2,1)} %refs_1_.1, bf16[64,1024]{1,0:T(8,128)(2,1)} %bitcast.3), custom_call_target="tpu_custom_call" | custom-call | bytes 835584 | tf_op jit(solution)/shard_map/pallas_call | solution.py:31
  1.8 3.0 %collective-permute-start = (bf16[64,768]{1,0:T(8,128)(2,1)}, bf16[64,768]{1,0:T(8,128)(2,1)S(1)}, u32[]{:S(2)}, u32[]{:S(2)}) collective-permute-start(bf16[64,768]{1,0:T(8,128)(2,1)} %get-tuple-element.60), channel_id=1, source_target_pairs={{0,2},{2,0},{4,6},{6,4},{8,10},{10,8},{12,14},{14,12},{16,18},{18,... | collective-permute-start | bytes 294920 | tf_op jit(solution)/shard_map/ppermute | solution.py:438
  4.8 1.5 %collective-permute-start.1 = (bf16[64,768]{1,0:T(8,128)(2,1)}, bf16[64,768]{1,0:T(8,128)(2,1)S(1)}, u32[]{:S(2)}, u32[]{:S(2)}) collective-permute-start(bf16[64,768]{1,0:T(8,128)(2,1)} %get-tuple-element.61), channel_id=1, source_target_pairs={{0,4},{2,6},{4,0},{6,2},{8,12},{10,14},{12,8},{14,10},{16,20},{18,... | collective-permute-start | bytes 294920 | tf_op jit(solution)/shard_map/ppermute | solution.py:438
  6.4 4.1 %collective-permute-start.5 = (bf16[64,128]{1,0:T(8,128)(2,1)}, bf16[64,128]{1,0:T(8,128)(2,1)S(1)}, u32[]{:S(2)}, u32[]{:S(2)}) collective-permute-start(bf16[64,128]{1,0:T(8,128)(2,1)} %get-tuple-element.64.refs_0_), channel_id=1, source_target_pairs={{0,24},{2,26},{4,28},{6,30},{8,16},{10,18},{12,20},{14,22},{16,8},... | collective-permute-start | bytes 49160 | tf_op jit(solution)/shard_map/ppermute | solution.py:450
  10.4 1.9 %collective-permute-done.5.refs_3_ = bf16[64,128]{1,0:T(8,128)(2,1)S(1)} collective-permute-done((bf16[64,128]{1,0:T(8,128)(2,1)}, bf16[64,128]{1,0:T(8,128)(2,1)S(1)}, u32[]{:S(2)}, u32[]{:S(2)}) %collective-permute-start.5) | collective-permute-done | bytes 16416 | tf_op jit(solution)/shard_map/ppermute | solution.py:450
  12.4 2.9 %collective-permute-done.4.refs_2_ = bf16[64,128]{1,0:T(8,128)(2,1)S(1)} collective-permute-done((bf16[64,128]{1,0:T(8,128)(2,1)}, bf16[64,128]{1,0:T(8,128)(2,1)S(1)}, u32[]{:S(2)}, u32[]{:S(2)}) %collective-permute-start.4) | collective-permute-done | bytes 16416 | tf_op jit(solution)/shard_map/ppermute | solution.py:450
  15.3 1.0 %collective-permute-done.3.refs_1_ = bf16[64,128]{1,0:T(8,128)(2,1)S(1)} collective-permute-done((bf16[64,128]{1,0:T(8,128)(2,1)}, bf16[64,128]{1,0:T(8,128)(2,1)S(1)}, u32[]{:S(2)}, u32[]{:S(2)}) %collective-permute-start.3) | collective-permute-done | bytes 16416 | tf_op jit(solution)/shard_map/ppermute | solution.py:450
  16.3 0.9 copy-done.6
  17.3 0.1 collective-permute-start.10
  17.3 4.4 %collective-permute-start.9 = (bf16[256,512]{1,0:T(8,128)(2,1)S(1)}, bf16[256,512]{1,0:T(8,128)(2,1)S(1)}, u32[]{:S(2)}, u32[]{:S(2)}) collective-permute-start(bf16[256,512]{1,0:T(8,128)(2,1)S(1)} %get-tuple-element.80.refs_0_), channel_id=1, source_target_pairs={{0,16},{2,18},{4,20},{6,22},{8,24},{10,26},{12,28},{14,30},{16,0},... | collective-permute-start | bytes 786440 | tf_op jit(solution)/shard_map/ppermute | solution.py:450
  21.8 0.1 shard_map.92
  21.9 1.6 %collective-permute-start.6 = (bf16[176,1024]{1,0:T(8,128)(2,1)S(1)}, bf16[176,1024]{1,0:T(8,128)(2,1)S(1)}, u32[]{:S(2)}, u32[]{:S(2)}) collective-permute-start(bf16[176,1024]{1,0:T(8,128)(2,1)S(1)} %get-tuple-element.69), channel_id=1, source_target_pairs={{0,2},{2,0},{4,6},{6,4},{8,10},{10,8},{12,14},{14,12},{16,18},{18,... | collective-permute-start | bytes 1081352 | tf_op jit(solution)/shard_map/ppermute | solution.py:438
  23.4 1.5 %collective-permute-start.7 = (bf16[176,1024]{1,0:T(8,128)(2,1)S(1)}, bf16[176,1024]{1,0:T(8,128)(2,1)S(1)}, u32[]{:S(2)}, u32[]{:S(2)}) collective-permute-start(bf16[176,1024]{1,0:T(8,128)(2,1)S(1)} %get-tuple-element.70), channel_id=1, source_target_pairs={{0,4},{2,6},{4,0},{6,2},{8,12},{10,14},{12,8},{14,10},{16,20},{18,... | collective-permute-start | bytes 1081352 | tf_op jit(solution)/shard_map/ppermute | solution.py:438
  24.9 0.5 collective-permute-start.8
  25.4 2.5 %collective-permute-done.10.refs_1_ = bf16[256,512]{1,0:T(8,128)(2,1)S(1)} collective-permute-done((bf16[256,512]{1,0:T(8,128)(2,1)S(1)}, bf16[256,512]{1,0:T(8,128)(2,1)S(1)}, u32[]{:S(2)}, u32[]{:S(2)}) %collective-permute-start.10) | collective-permute-done | bytes 262176 | tf_op jit(solution)/shard_map/ppermute | solution.py:450
  27.9 2.5 %collective-permute-done.9.refs_2_ = bf16[256,512]{1,0:T(8,128)(2,1)S(1)} collective-permute-done((bf16[256,512]{1,0:T(8,128)(2,1)S(1)}, bf16[256,512]{1,0:T(8,128)(2,1)S(1)}, u32[]{:S(2)}, u32[]{:S(2)}) %collective-permute-start.9) | collective-permute-done | bytes 262176 | tf_op jit(solution)/shard_map/ppermute | solution.py:450
  30.4 1.3 %collective-permute-start.11 = (bf16[256,512]{1,0:T(8,128)(2,1)S(1)}, bf16[256,512]{1,0:T(8,128)(2,1)S(1)}, u32[]{:S(2)}, u32[]{:S(2)}) collective-permute-start(bf16[256,512]{1,0:T(8,128)(2,1)S(1)} %collective-permute-done.9.refs_2_), channel_id=1, source_target_pairs={{8,0},{10,2},{12,4},{14,6},{16,24},{18,26},{20,28},{22,30},{9,1},{... | collective-permute-start | bytes 786440 | tf_op jit(solution)/shard_map/ppermute | solution.py:466
  31.7 0.7 collective-permute-start.12
  32.4 4.9 %collective-permute-done.7.refs_2_.refs_1_ = bf16[176,1024]{1,0:T(8,128)(2,1)S(1)} collective-permute-done((bf16[176,1024]{1,0:T(8,128)(2,1)S(1)}, bf16[176,1024]{1,0:T(8,128)(2,1)S(1)}, u32[]{:S(2)}, u32[]{:S(2)}) %collective-permute-start.7) | collective-permute-done | bytes 360480 | tf_op jit(solution)/shard_map/ppermute | solution.py:438
  37.3 0.2 shard_map.93
  37.5 0.1 collective-permute-start.13
  37.6 1.1 %collective-permute-done.11.refs_3_ = bf16[256,512]{1,0:T(8,128)(2,1)S(1)} collective-permute-done((bf16[256,512]{1,0:T(8,128)(2,1)S(1)}, bf16[256,512]{1,0:T(8,128)(2,1)S(1)}, u32[]{:S(2)}, u32[]{:S(2)}) %collective-permute-start.11) | collective-permute-done | bytes 262176 | tf_op jit(solution)/shard_map/ppermute | solution.py:466
  38.7 0.1 shard_map.95
  38.8 1.5 %collective-permute-done.13.swap_ref = bf16[512,1024]{1,0:T(8,128)(2,1)S(1)} collective-permute-done((bf16[512,1024]{1,0:T(8,128)(2,1)S(1)}, bf16[512,1024]{1,0:T(8,128)(2,1)S(1)}, u32[]{:S(2)}, u32[]{:S(2)}) %collective-permute-start.13) | collective-permute-done | bytes 1048608 | tf_op jit(solution)/shard_map/ppermute | solution.py:447
  40.3 4.8 %shard_map.96 = (bf16[1024,1024]{1,0:T(8,128)(2,1)}, bf16[1024,256]{1,0:T(8,128)(2,1)S(1)}, bf16[1024,128]{1,0:T(8,128)(2,1)S(1)}, bf16[1024,128]{1,0:T(8,128)(2...) custom-call(s32[8]{0:T(128)S(1)} %copy-done.5, ...), custom_call_target="tpu_custom_call" | custom-call | flops 1073741824 | bytes 7905312 | tf_op jit(solution)/shard_map/pallas_call | solution.py:31
  45.1 3.0 %collective-permute-start.16 = (bf16[144,256]{1,0:T(8,128)(2,1)S(1)}, bf16[144,256]{1,0:T(8,128)(2,1)S(1)}, u32[]{:S(2)}, u32[]{:S(2)}) collective-permute-start(bf16[144,256]{1,0:T(8,128)(2,1)S(1)} %get-tuple-element.86), channel_id=1, source_target_pairs={{0,24},{2,26},{4,28},{6,30},{1,25},{3,27},{5,29},{7,31}} | collective-permute-start | bytes 221192 | tf_op jit(solution)/shard_map/ppermute | solution.py:441
  48.1 3.1 %collective-permute-start.15 = (bf16[144,256]{1,0:T(8,128)(2,1)S(1)}, bf16[144,256]{1,0:T(8,128)(2,1)S(1)}, u32[]{:S(2)}, u32[]{:S(2)}) collective-permute-start(bf16[144,256]{1,0:T(8,128)(2,1)S(1)} %get-tuple-element.86), channel_id=1, source_target_pairs={{0,16},{2,18},{4,20},{6,22},{8,24},{10,26},{12,28},{14,30},{1,17},... | collective-permute-start | bytes 221192 | tf_op jit(solution)/shard_map/ppermute | solution.py:441
  51.2 1.3 %collective-permute-start.14 = (bf16[144,256]{1,0:T(8,128)(2,1)S(1)}, bf16[144,256]{1,0:T(8,128)(2,1)S(1)}, u32[]{:S(2)}, u32[]{:S(2)}) collective-permute-start(bf16[144,256]{1,0:T(8,128)(2,1)S(1)} %get-tuple-element.86), channel_id=1, source_target_pairs={{0,8},{2,10},{4,12},{6,14},{8,16},{10,18},{12,20},{14,22},{16,24},... | collective-permute-start | bytes 221192 | tf_op jit(solution)/shard_map/ppermute | solution.py:441
  52.5 1.6 %shard_map.97.y_ref = f32[1024,256]{1,0:T(8,128)S(1)} custom-call(bf16[1024,256]{1,0:T(8,128)(2,1)S(1)} %get-tuple-element.87.x_ref, bf16[1024,128]{1,0:T(8,128)(2,1)S(1)} %get-tuple-element.88.b_ref, bf16[1024,128]{1,0:T(8,128)(2,1)S(1)} %get-tuple-element.84.c_ref, f32[192,128]{1,0:T(8,128)S(1)} %get-tuple-element.89.rows_ref), custom_call_target="tpu_custom_call" | custom-call | flops 134217728 | bytes 2195456 | tf_op jit(solution)/shard_map/pallas_call | solution.py:31
  54.1 0.4 collective-permute-done.14.refs_0_
  54.5 2.4 %collective-permute-start.17 = (bf16[256,256]{1,0:T(8,128)(2,1)S(1)}, bf16[256,256]{1,0:T(8,128)(2,1)S(1)}, u32[]{:S(2)}, u32[]{:S(2)}) collective-permute-start(bf16[256,256]{1,0:T(8,128)(2,1)S(1)} %get-tuple-element.99.refs_0_), channel_id=1, source_target_pairs={{0,8},{2,10},{4,12},{6,14},{8,0},{10,2},{12,4},{14,6},{16,24},{18,... | collective-permute-start | bytes 393224 | tf_op jit(solution)/shard_map/ppermute | solution.py:450
  56.9 2.6 %collective-permute-start.21 = (bf16[256,256]{1,0:T(8,128)(2,1)S(1)}, bf16[256,256]{1,0:T(8,128)(2,1)S(1)}, u32[]{:S(2)}, u32[]{:S(2)}) collective-permute-start(bf16[256,256]{1,0:T(8,128)(2,1)S(1)} %get-tuple-element.99.refs_0_), channel_id=1, source_target_pairs={{0,24},{2,26},{4,28},{6,30},{8,16},{10,18},{12,20},{14,22},{16,8},... | collective-permute-start | bytes 393224 | tf_op jit(solution)/shard_map/ppermute | solution.py:450
  59.4 0.9 shard_map.98.silu_ref
  60.4 1.5 %shard_map.99 = (bf16[1024,256]{1,0:T(8,128)(2,1)S(1)}, bf16[16,256]{1,0:T(8,128)(2,1)S(1)}, bf16[16,256]{1,0:T(8,128)(2,1)S(1)}) custom-call(bf16[1024,128]{1,0:T(8,128)(2,1)S(1)} %get-tuple-element.84.c_ref, f32[1024,256]{1,0:T(8,128)S(1)} %shard_map.97.y_ref, f32[1024,256]{1,0:T(8,128)S(1)} %get-tuple-element.91.step_ref, ...), custom_call_target="tpu_custom_call" | custom-call | flops 67108864 | bytes 4333568 | tf_op jit(solution)/shard_map/pallas_call | solution.py:31
  61.9 3.7 %collective-permute-start.18 = (bf16[16,256]{1,0:T(8,128)(2,1)S(1)}, bf16[16,256]{1,0:T(8,128)(2,1)S(1)}, u32[]{:S(2)}, u32[]{:S(2)}) collective-permute-start(bf16[16,256]{1,0:T(8,128)(2,1)S(1)} %get-tuple-element.101), channel_id=1, source_target_pairs={{0,8},{2,10},{4,12},{6,14},{8,16},{10,18},{12,20},{14,22},{16,24},... | collective-permute-start | bytes 24584 | tf_op jit(solution)/shard_map/ppermute | solution.py:441
  65.6 1.3 %collective-permute-start.19 = (bf16[16,256]{1,0:T(8,128)(2,1)S(1)}, bf16[16,256]{1,0:T(8,128)(2,1)S(1)}, u32[]{:S(2)}, u32[]{:S(2)}) collective-permute-start(bf16[16,256]{1,0:T(8,128)(2,1)S(1)} %get-tuple-element.102), channel_id=1, source_target_pairs={{8,0},{10,2},{12,4},{14,6},{16,8},{18,10},{20,12},{22,14},{24,16},... | collective-permute-start | bytes 24584 | tf_op jit(solution)/shard_map/ppermute | solution.py:444
  66.9 5.0 %shard_map.100.refs_2_ = bf16[768,256]{1,0:T(8,128)(2,1)S(1)} custom-call(s32[8]{0:T(128)S(1)} %copy-done.5, f32[31,1024]{1,0:T(8,128)S(1)} %copy-done.2, bf16[1024,256]{1,0:T(8,128)(2,1)S(1)} %get-tuple-element.100.gated_ref), custom_call_target="tpu_custom_call" | custom-call | flops 16252928 | bytes 1044512 | tf_op jit(solution)/shard_map/pallas_call | solution.py:31
  72.0 1.9 %shard_map.101.refs_0_ = bf16[1024,256]{1,0:T(8,128)(2,1)S(1)} custom-call(s32[8]{0:T(128)S(1)} %copy-done.5, f32[31,1024]{1,0:T(8,128)S(1)} %copy-done.2, bf16[1024,256]{1,0:T(8,128)(2,1)S(1)} %get-tuple-element.100.gated_ref, bf16[16,256]{1,0:T(8,128)(2,1)S(1)} %collective-permute-done.18.refs_0_, bf16[16,256]{1,0:T(8,128)(2,1)S(1)} %collective-permute-done.19.refs_1_, ...), custom_call_target="tpu_custom_call" | custom-call | flops 4063232 | bytes 1585184 | tf_op jit(solution)/shard_map/pallas_call | solution.py:31
  73.9 0.1 collective-permute-start.22
  74.0 0.1 shard_map.102
  74.1 0.6 collective-permute-start.23
  74.7 1.6 %collective-permute-done.23.refs_3_ = bf16[512,256]{1,0:T(8,128)(2,1)S(1)} collective-permute-done((bf16[512,256]{1,0:T(8,128)(2,1)S(1)}, bf16[512,256]{1,0:T(8,128)(2,1)S(1)}, u32[]{:S(2)}, u32[]{:S(2)}) %collective-permute-start.23) | collective-permute-done | bytes 262176 | tf_op jit(solution)/shard_map/ppermute | solution.py:447
  76.3 0.7 shard_map.103
  77.0 1.6 %collective-permute-start.24 = (bf16[256,512]{1,0:T(8,128)(2,1)S(1)}, bf16[256,512]{1,0:T(8,128)(2,1)S(1)}, u32[]{:S(2)}, u32[]{:S(2)}) collective-permute-start(bf16[256,512]{1,0:T(8,128)(2,1)S(1)} %get-tuple-element.110), channel_id=1, source_target_pairs={{0,2},{2,0},{4,6},{6,4},{8,10},{10,8},{12,14},{14,12},{16,18},{18,... | collective-permute-start | bytes 786440 | tf_op jit(solution)/shard_map/ppermute | solution.py:438
  78.6 2.0 %collective-permute-start.25 = (bf16[256,512]{1,0:T(8,128)(2,1)S(1)}, bf16[256,512]{1,0:T(8,128)(2,1)S(1)}, u32[]{:S(2)}, u32[]{:S(2)}) collective-permute-start(bf16[256,512]{1,0:T(8,128)(2,1)S(1)} %get-tuple-element.111), channel_id=1, source_target_pairs={{0,4},{2,6},{4,0},{6,2},{8,12},{10,14},{12,8},{14,10},{16,20},{18,... | collective-permute-start | bytes 786440 | tf_op jit(solution)/shard_map/ppermute | solution.py:438
  80.6 5.7 %collective-permute-done.24 = bf16[256,512]{1,0:T(8,128)(2,1)S(1)} collective-permute-done((bf16[256,512]{1,0:T(8,128)(2,1)S(1)}, bf16[256,512]{1,0:T(8,128)(2,1)S(1)}, u32[]{:S(2)}, u32[]{:S(2)}) %collective-permute-start.24) | collective-permute-done | bytes 262176 | tf_op jit(solution)/shard_map/ppermute | solution.py:438
  86.3 6.3 %collective-permute-done.25 = bf16[256,512]{1,0:T(8,128)(2,1)S(1)} collective-permute-done((bf16[256,512]{1,0:T(8,128)(2,1)S(1)}, bf16[256,512]{1,0:T(8,128)(2,1)S(1)}, u32[]{:S(2)}, u32[]{:S(2)}) %collective-permute-start.25) | collective-permute-done | bytes 262176 | tf_op jit(solution)/shard_map/ppermute | solution.py:438
  92.5 0.8 add_convert_fusion
  (38 shorter events, 0.2 us)
Async XLA Ops:
  1.8 14.5 %collective-permute-start = (bf16[64,768]{1,0:T(8,128)(2,1)}, bf16[64,768]{1,0:T(8,128)(2,1)S(1)}, u32[]{:S(2)}, u32[]{:S(2)}) collective-permute-start(bf16[64,768]{1,0:T(8,128)(2,1)} %get-tuple-element.60), channel_id=1, source_target_pairs={{0,2},{2,0},{4,6},{6,4},{8,10},{10,8},{12,14},{14,12},{16,18},{18,... | collective-permute-start | bytes 294920 | tf_op jit(solution)/shard_map/ppermute | solution.py:438
  4.8 11.5 %collective-permute-start.1 = (bf16[64,768]{1,0:T(8,128)(2,1)}, bf16[64,768]{1,0:T(8,128)(2,1)S(1)}, u32[]{:S(2)}, u32[]{:S(2)}) collective-permute-start(bf16[64,768]{1,0:T(8,128)(2,1)} %get-tuple-element.61), channel_id=1, source_target_pairs={{0,4},{2,6},{4,0},{6,2},{8,12},{10,14},{12,8},{14,10},{16,20},{18,... | collective-permute-start | bytes 294920 | tf_op jit(solution)/shard_map/ppermute | solution.py:438
  6.3 10.0 %collective-permute-start.2 = (bf16[64,768]{1,0:T(8,128)(2,1)}, bf16[64,768]{1,0:T(8,128)(2,1)S(1)}, u32[]{:S(2)}, u32[]{:S(2)}) collective-permute-start(bf16[64,768]{1,0:T(8,128)(2,1)} %get-tuple-element.62), channel_id=1, source_target_pairs={{0,6},{2,4},{4,2},{6,0},{8,14},{10,12},{12,10},{14,8},{16,22},{18,... | collective-permute-start | bytes 294920 | tf_op jit(solution)/shard_map/ppermute | solution.py:438
  6.4 6.0 %collective-permute-start.5 = (bf16[64,128]{1,0:T(8,128)(2,1)}, bf16[64,128]{1,0:T(8,128)(2,1)S(1)}, u32[]{:S(2)}, u32[]{:S(2)}) collective-permute-start(bf16[64,128]{1,0:T(8,128)(2,1)} %get-tuple-element.64.refs_0_), channel_id=1, source_target_pairs={{0,24},{2,26},{4,28},{6,30},{8,16},{10,18},{12,20},{14,22},{16,8},... | collective-permute-start | bytes 49160 | tf_op jit(solution)/shard_map/ppermute | solution.py:450
  10.4 4.8 %collective-permute-start.4 = (bf16[64,128]{1,0:T(8,128)(2,1)}, bf16[64,128]{1,0:T(8,128)(2,1)S(1)}, u32[]{:S(2)}, u32[]{:S(2)}) collective-permute-start(bf16[64,128]{1,0:T(8,128)(2,1)} %get-tuple-element.64.refs_0_), channel_id=1, source_target_pairs={{0,16},{2,18},{4,20},{6,22},{8,24},{10,26},{12,28},{14,30},{16,0},... | collective-permute-start | bytes 49160 | tf_op jit(solution)/shard_map/ppermute | solution.py:450
  12.3 3.9 %collective-permute-start.3 = (bf16[64,128]{1,0:T(8,128)(2,1)}, bf16[64,128]{1,0:T(8,128)(2,1)S(1)}, u32[]{:S(2)}, u32[]{:S(2)}) collective-permute-start(bf16[64,128]{1,0:T(8,128)(2,1)} %get-tuple-element.64.refs_0_), channel_id=1, source_target_pairs={{0,8},{2,10},{4,12},{6,14},{8,0},{10,2},{12,4},{14,6},{16,24},{18,... | collective-permute-start | bytes 49160 | tf_op jit(solution)/shard_map/ppermute | solution.py:450
  16.3 0.9 copy-start.6
  17.2 4.5 %copy-start.7 = (f32[16,256]{1,0:T(8,128)S(1)}, f32[16,256]{1,0:T(8,128)}, u32[]{:S(2)}) copy-start(f32[16,256]{1,0:T(8,128)} %param.13) | copy-start | bytes 49156
  17.2 4.5 %copy-start.1 = (bf16[256,1024]{1,0:T(8,128)(2,1)S(1)}, bf16[256,1024]{1,0:T(8,128)(2,1)}, u32[]{:S(2)}) copy-start(bf16[256,1024]{1,0:T(8,128)(2,1)} %own_ref.1) | copy-start | bytes 1572868
  17.2 4.5 %copy-start.3 = (bf16[64,128]{1,0:T(8,128)(2,1)S(1)}, bf16[64,128]{1,0:T(8,128)(2,1)}, u32[]{:S(2)}) copy-start(bf16[64,128]{1,0:T(8,128)(2,1)} %get-tuple-element.64.refs_0_) | copy-start | bytes 49156
  17.3 10.6 %collective-permute-start.10 = (bf16[256,512]{1,0:T(8,128)(2,1)S(1)}, bf16[256,512]{1,0:T(8,128)(2,1)S(1)}, u32[]{:S(2)}, u32[]{:S(2)}) collective-permute-start(bf16[256,512]{1,0:T(8,128)(2,1)S(1)} %get-tuple-element.80.refs_0_), channel_id=1, source_target_pairs={{0,8},{2,10},{4,12},{6,14},{8,0},{10,2},{12,4},{14,6},{16,24},{18,... | collective-permute-start | bytes 786440 | tf_op jit(solution)/shard_map/ppermute | solution.py:450
  17.3 13.1 %collective-permute-start.9 = (bf16[256,512]{1,0:T(8,128)(2,1)S(1)}, bf16[256,512]{1,0:T(8,128)(2,1)S(1)}, u32[]{:S(2)}, u32[]{:S(2)}) collective-permute-start(bf16[256,512]{1,0:T(8,128)(2,1)S(1)} %get-tuple-element.80.refs_0_), channel_id=1, source_target_pairs={{0,16},{2,18},{4,20},{6,22},{8,24},{10,26},{12,28},{14,30},{16,0},... | collective-permute-start | bytes 786440 | tf_op jit(solution)/shard_map/ppermute | solution.py:450
  21.9 10.5 %collective-permute-start.6 = (bf16[176,1024]{1,0:T(8,128)(2,1)S(1)}, bf16[176,1024]{1,0:T(8,128)(2,1)S(1)}, u32[]{:S(2)}, u32[]{:S(2)}) collective-permute-start(bf16[176,1024]{1,0:T(8,128)(2,1)S(1)} %get-tuple-element.69), channel_id=1, source_target_pairs={{0,2},{2,0},{4,6},{6,4},{8,10},{10,8},{12,14},{14,12},{16,18},{18,... | collective-permute-start | bytes 1081352 | tf_op jit(solution)/shard_map/ppermute | solution.py:438
  23.4 13.9 %collective-permute-start.7 = (bf16[176,1024]{1,0:T(8,128)(2,1)S(1)}, bf16[176,1024]{1,0:T(8,128)(2,1)S(1)}, u32[]{:S(2)}, u32[]{:S(2)}) collective-permute-start(bf16[176,1024]{1,0:T(8,128)(2,1)S(1)} %get-tuple-element.70), channel_id=1, source_target_pairs={{0,4},{2,6},{4,0},{6,2},{8,12},{10,14},{12,8},{14,10},{16,20},{18,... | collective-permute-start | bytes 1081352 | tf_op jit(solution)/shard_map/ppermute | solution.py:438
  24.9 12.4 %collective-permute-start.8 = (bf16[176,1024]{1,0:T(8,128)(2,1)S(1)}, bf16[176,1024]{1,0:T(8,128)(2,1)S(1)}, u32[]{:S(2)}, u32[]{:S(2)}) collective-permute-start(bf16[176,1024]{1,0:T(8,128)(2,1)S(1)} %get-tuple-element.71), channel_id=1, source_target_pairs={{0,6},{2,4},{4,2},{6,0},{8,14},{10,12},{12,10},{14,8},{16,22},{18,... | collective-permute-start | bytes 1081352 | tf_op jit(solution)/shard_map/ppermute | solution.py:438
  30.4 8.3 %collective-permute-start.11 = (bf16[256,512]{1,0:T(8,128)(2,1)S(1)}, bf16[256,512]{1,0:T(8,128)(2,1)S(1)}, u32[]{:S(2)}, u32[]{:S(2)}) collective-permute-start(bf16[256,512]{1,0:T(8,128)(2,1)S(1)} %collective-permute-done.9.refs_2_), channel_id=1, source_target_pairs={{8,0},{10,2},{12,4},{14,6},{16,24},{18,26},{20,28},{22,30},{9,1},{... | collective-permute-start | bytes 786440 | tf_op jit(solution)/shard_map/ppermute | solution.py:466
  31.7 7.0 %collective-permute-start.12 = (bf16[256,512]{1,0:T(8,128)(2,1)S(1)}, bf16[256,512]{1,0:T(8,128)(2,1)S(1)}, u32[]{:S(2)}, u32[]{:S(2)}) collective-permute-start(bf16[256,512]{1,0:T(8,128)(2,1)S(1)} %get-tuple-element.80.refs_0_), channel_id=1, source_target_pairs={{8,16},{10,18},{12,20},{14,22},{16,8},{18,10},{20,12},{22,14},{9,1... | collective-permute-start | bytes 786440 | tf_op jit(solution)/shard_map/ppermute | solution.py:467
  37.5 2.7 %copy-start.5 = (s32[8]{0:T(128)S(1)}, s32[8]{0:T(128)}, u32[]{:S(2)}) copy-start(s32[8]{0:T(128)} %len_ref.5) | copy-start | bytes 100
  37.5 2.7 %collective-permute-start.13 = (bf16[512,1024]{1,0:T(8,128)(2,1)S(1)}, bf16[512,1024]{1,0:T(8,128)(2,1)S(1)}, u32[]{:S(2)}, u32[]{:S(2)}) collective-permute-start(bf16[512,1024]{1,0:T(8,128)(2,1)S(1)} %get-tuple-element.83), channel_id=1, source_target_pairs={{0,1},{1,0},{2,3},{3,2},{4,5},{5,4},{6,7},{7,6},{8,9},{9,8},{10,11... | collective-permute-start | bytes 3145736 | tf_op jit(solution)/shard_map/ppermute | solution.py:447
  45.1 14.3 %copy-start = (bf16[1024,1024]{1,0:T(8,128)(2,1)S(1)}, bf16[1024,1024]{1,0:T(8,128)(2,1)}, u32[]{:S(2)}) copy-start(bf16[1024,1024]{1,0:T(8,128)(2,1)} %get-tuple-element.93.frames_ref) | copy-start | bytes 6291460
  45.1 14.3 %copy-start.4 = (f32[1024]{0:T(1024)S(1)}, f32[1024]{0:T(1024)}, u32[]{:S(2)}) copy-start(f32[1024]{0:T(1024)} %param.14) | copy-start | bytes 12292
  45.1 9.0 %collective-permute-start.16 = (bf16[144,256]{1,0:T(8,128)(2,1)S(1)}, bf16[144,256]{1,0:T(8,128)(2,1)S(1)}, u32[]{:S(2)}, u32[]{:S(2)}) collective-permute-start(bf16[144,256]{1,0:T(8,128)(2,1)S(1)} %get-tuple-element.86), channel_id=1, source_target_pairs={{0,24},{2,26},{4,28},{6,30},{1,25},{3,27},{5,29},{7,31}} | collective-permute-start | bytes 221192 | tf_op jit(solution)/shard_map/ppermute | solution.py:441
  48.1 6.0 %collective-permute-start.15 = (bf16[144,256]{1,0:T(8,128)(2,1)S(1)}, bf16[144,256]{1,0:T(8,128)(2,1)S(1)}, u32[]{:S(2)}, u32[]{:S(2)}) collective-permute-start(bf16[144,256]{1,0:T(8,128)(2,1)S(1)} %get-tuple-element.86), channel_id=1, source_target_pairs={{0,16},{2,18},{4,20},{6,22},{8,24},{10,26},{12,28},{14,30},{1,17},... | collective-permute-start | bytes 221192 | tf_op jit(solution)/shard_map/ppermute | solution.py:441
  51.2 3.3 %collective-permute-start.14 = (bf16[144,256]{1,0:T(8,128)(2,1)S(1)}, bf16[144,256]{1,0:T(8,128)(2,1)S(1)}, u32[]{:S(2)}, u32[]{:S(2)}) collective-permute-start(bf16[144,256]{1,0:T(8,128)(2,1)S(1)} %get-tuple-element.86), channel_id=1, source_target_pairs={{0,8},{2,10},{4,12},{6,14},{8,16},{10,18},{12,20},{14,22},{16,24},... | collective-permute-start | bytes 221192 | tf_op jit(solution)/shard_map/ppermute | solution.py:441
  54.5 12.4 %collective-permute-start.17 = (bf16[256,256]{1,0:T(8,128)(2,1)S(1)}, bf16[256,256]{1,0:T(8,128)(2,1)S(1)}, u32[]{:S(2)}, u32[]{:S(2)}) collective-permute-start(bf16[256,256]{1,0:T(8,128)(2,1)S(1)} %get-tuple-element.99.refs_0_), channel_id=1, source_target_pairs={{0,8},{2,10},{4,12},{6,14},{8,0},{10,2},{12,4},{14,6},{16,24},{18,... | collective-permute-start | bytes 393224 | tf_op jit(solution)/shard_map/ppermute | solution.py:450
  56.9 15.1 %collective-permute-start.21 = (bf16[256,256]{1,0:T(8,128)(2,1)S(1)}, bf16[256,256]{1,0:T(8,128)(2,1)S(1)}, u32[]{:S(2)}, u32[]{:S(2)}) collective-permute-start(bf16[256,256]{1,0:T(8,128)(2,1)S(1)} %get-tuple-element.99.refs_0_), channel_id=1, source_target_pairs={{0,24},{2,26},{4,28},{6,30},{8,16},{10,18},{12,20},{14,22},{16,8},... | collective-permute-start | bytes 393224 | tf_op jit(solution)/shard_map/ppermute | solution.py:450
  59.4 12.6 %collective-permute-start.20 = (bf16[256,256]{1,0:T(8,128)(2,1)S(1)}, bf16[256,256]{1,0:T(8,128)(2,1)S(1)}, u32[]{:S(2)}, u32[]{:S(2)}) collective-permute-start(bf16[256,256]{1,0:T(8,128)(2,1)S(1)} %get-tuple-element.99.refs_0_), channel_id=1, source_target_pairs={{0,16},{2,18},{4,20},{6,22},{8,24},{10,26},{12,28},{14,30},{16,0},... | collective-permute-start | bytes 393224 | tf_op jit(solution)/shard_map/ppermute | solution.py:450
  60.4 6.6 %copy-start.2 = (f32[31,1024]{1,0:T(8,128)S(1)}, f32[31,1024]{1,0:T(8,128)}, u32[]{:S(2)}) copy-start(f32[31,1024]{1,0:T(8,128)} %taps_ref.3) | copy-start | bytes 380932
  61.9 10.1 %collective-permute-start.18 = (bf16[16,256]{1,0:T(8,128)(2,1)S(1)}, bf16[16,256]{1,0:T(8,128)(2,1)S(1)}, u32[]{:S(2)}, u32[]{:S(2)}) collective-permute-start(bf16[16,256]{1,0:T(8,128)(2,1)S(1)} %get-tuple-element.101), channel_id=1, source_target_pairs={{0,8},{2,10},{4,12},{6,14},{8,16},{10,18},{12,20},{14,22},{16,24},... | collective-permute-start | bytes 24584 | tf_op jit(solution)/shard_map/ppermute | solution.py:441
  65.6 6.4 %collective-permute-start.19 = (bf16[16,256]{1,0:T(8,128)(2,1)S(1)}, bf16[16,256]{1,0:T(8,128)(2,1)S(1)}, u32[]{:S(2)}, u32[]{:S(2)}) collective-permute-start(bf16[16,256]{1,0:T(8,128)(2,1)S(1)} %get-tuple-element.102), channel_id=1, source_target_pairs={{8,0},{10,2},{12,4},{14,6},{16,8},{18,10},{20,12},{22,14},{24,16},... | collective-permute-start | bytes 24584 | tf_op jit(solution)/shard_map/ppermute | solution.py:444
  73.9 2.4 %collective-permute-start.22 = (bf16[1024,256]{1,0:T(8,128)(2,1)S(1)}, bf16[1024,256]{1,0:T(8,128)(2,1)S(1)}, u32[]{:S(2)}, u32[]{:S(2)}) collective-permute-start(bf16[1024,256]{1,0:T(8,128)(2,1)S(1)} %shard_map.101.refs_0_), channel_id=1, source_target_pairs={{0,1},{1,0},{2,3},{3,2},{4,5},{5,4},{6,7},{7,6},{8,9},{9,8},{10,11... | collective-permute-start | bytes 1572872 | tf_op jit(solution)/shard_map/ppermute | solution.py:447
  74.1 2.2 %collective-permute-start.23 = (bf16[512,256]{1,0:T(8,128)(2,1)S(1)}, bf16[512,256]{1,0:T(8,128)(2,1)S(1)}, u32[]{:S(2)}, u32[]{:S(2)}) collective-permute-start(bf16[512,256]{1,0:T(8,128)(2,1)S(1)} %get-tuple-element.108), channel_id=1, source_target_pairs={{0,1},{1,0},{2,3},{3,2},{4,5},{5,4},{6,7},{7,6},{8,9},{9,8},{10,11... | collective-permute-start | bytes 786440 | tf_op jit(solution)/shard_map/ppermute | solution.py:447
  77.0 9.2 %collective-permute-start.24 = (bf16[256,512]{1,0:T(8,128)(2,1)S(1)}, bf16[256,512]{1,0:T(8,128)(2,1)S(1)}, u32[]{:S(2)}, u32[]{:S(2)}) collective-permute-start(bf16[256,512]{1,0:T(8,128)(2,1)S(1)} %get-tuple-element.110), channel_id=1, source_target_pairs={{0,2},{2,0},{4,6},{6,4},{8,10},{10,8},{12,14},{14,12},{16,18},{18,... | collective-permute-start | bytes 786440 | tf_op jit(solution)/shard_map/ppermute | solution.py:438
  78.6 13.9 %collective-permute-start.25 = (bf16[256,512]{1,0:T(8,128)(2,1)S(1)}, bf16[256,512]{1,0:T(8,128)(2,1)S(1)}, u32[]{:S(2)}, u32[]{:S(2)}) collective-permute-start(bf16[256,512]{1,0:T(8,128)(2,1)S(1)} %get-tuple-element.111), channel_id=1, source_target_pairs={{0,4},{2,6},{4,0},{6,2},{8,12},{10,14},{12,8},{14,10},{16,20},{18,... | collective-permute-start | bytes 786440 | tf_op jit(solution)/shard_map/ppermute | solution.py:438
  80.6 11.9 %collective-permute-start.26 = (bf16[256,512]{1,0:T(8,128)(2,1)S(1)}, bf16[256,512]{1,0:T(8,128)(2,1)S(1)}, u32[]{:S(2)}, u32[]{:S(2)}) collective-permute-start(bf16[256,512]{1,0:T(8,128)(2,1)S(1)} %get-tuple-element.112), channel_id=1, source_target_pairs={{0,6},{2,4},{4,2},{6,0},{8,14},{10,12},{12,10},{14,8},{16,22},{18,... | collective-permute-start | bytes 786440 | tf_op jit(solution)/shard_map/ppermute | solution.py:438

commit v7 on v6

--- a/solution.py
+++ b/solution.py
@@ -10,12 +10,13 @@
 SPAN = 128
 LANES = 128
 EDGE = 16
+CONV_ROWS = 64
 BF16 = jnp.bfloat16
 F32 = jnp.float32
 STACK_HINT = 40_000_000_000
 ASSEMBLE_HINT = 40_000_000_000
 ALL_VMEM_BYTES = 63 * 1024 * 1024
-VMEM_BYTES = 48 * 1024 * 1024
+VMEM_BYTES = 20 * 1024 * 1024
 
 
 def dot(a, b, dims=((1,), (0,)), precision=None):
@@ -161,17 +162,19 @@
 
 
 def lanes_of(rows, width, head_size):
-    high = rows.astype(BF16)
-    low = (rows - high.astype(F32)).astype(BF16)
+    high = rows.astype(BF16).astype(F32)
     owner = lax.broadcasted_iota(jnp.int32, (16, width), 1) // head_size
     chosen = jnp.where((lax.broadcasted_iota(jnp.int32, (16, width), 0) & 7) == owner, 1.0, 0.0).astype(BF16)
-    both = jnp.concatenate([high.astype(F32), low.astype(F32)], axis=0).astype(BF16)
-    return dot(both, chosen, ((0,), (0,)))
+    return dot(jnp.concatenate([high, rows - high], axis=0).astype(BF16), chosen, ((0,), (0,)))
+
+
+def spans_in_lanes(rows):
+    return jnp.concatenate([rows[at : at + 8] for at in range(0, rows.shape[0], 8)], axis=1)
 
 
 def state_kernel(group, heads, state, len_ref, decay_ref, x_weight_ref, bc_half_ref, own_ref, swap_ref, *refs):
     half_refs, refs = refs[: group - 1], refs[group - 1 :]
-    frames_ref, x_ref, b_ref, c_ref, rows_ref, step_ref, keep_ref, send_ref, weight_ref = refs
+    frames_ref, x_ref, b_ref, c_ref, rows_ref, step_ref, keep_ref, send_ref, weight_ref, tail_ref = refs
     place, plane = plane_place(group)
     parity = lax.rem(lax.axis_index("head"), 2)
     total, width = x_ref.shape
@@ -221,23 +224,26 @@
         b_ref[rows, :] = product[:, :state].astype(BF16)
         c_ref[rows, :] = product[:, state:].astype(BF16)
 
+    tail_ref[...] = lanes_of(spans_in_lanes(tail), width, head_size)
+    by_span = jnp.zeros((8, SPAN), F32)
+    for block in range(count):
+        by_span = jnp.where(lane[:8] == block, keep[block * 8 : (block + 1) * 8], by_span)
+    kept = lanes_of(by_span, width, head_size)[: keep_ref.shape[0]]
+    keep_ref[...] = kept
     entry = jnp.zeros((state, width), F32)
-    through = jnp.ones((8, width), F32)
+    through = jnp.ones((1, width), F32)
     for block in range(count):
         rows = slice(block * SPAN, (block + 1) * SPAN)
-        at = slice(block * 8, (block + 1) * 8)
-        kept = lanes_of(keep[at], width, head_size)
-        weighed = x_ref[rows, :].astype(F32) * lanes_of(tail[at], width, head_size)
+        weighed = x_ref[rows, :].astype(F32) * tail_ref[rows, :]
         step = dot(b_ref[rows, :], weighed.astype(BF16), ((0,), (0,)))
         step_ref[block * state : (block + 1) * state, :] = step
-        keep_ref[at, :] = kept[:8]
-        entry = kept[:1] * entry + step
-        through = through * kept[:8]
+        entry = kept[block : block + 1] * entry + step
+        through = through * kept[block : block + 1]
     send_ref[:state, :] = entry.astype(BF16)
-    send_ref[state:, :] = jnp.concatenate([through, through], axis=0).astype(BF16)
-
-
-def inner_kernel(group, heads, x_ref, b_ref, c_ref, rows_ref, y_ref):
+    send_ref[state:, :] = jnp.broadcast_to(through, (EDGE, width)).astype(BF16)
+
+
+def inner_kernel(group, heads, x_ref, b_ref, c_ref, rows_ref, y_ref, carry_ref):
     _, plane = plane_place(group)
     total, width = x_ref.shape
     head_size = width // heads
@@ -249,6 +255,7 @@
     if 2 * used % SPAN:
         parts.append(jnp.zeros((SPAN - 2 * used % SPAN, SPAN), F32))
     columns = jnp.concatenate(parts, axis=0).T
+    carry_ref[...] = lanes_of(spans_in_lanes(rows_ref[2 * used :, :]), width, head_size)
     row, lane = (lax.broadcasted_iota(jnp.int32, square, dim) for dim in (0, 1))
     lower = row >= lane
     tile_heads = LANES // head_size
@@ -296,11 +303,10 @@
         out_ref[...] = weight_ref[pl.ds(pl.multiple_of((core ^ step) * rows, rows), rows), :]
 
 
-def gate_kernel(heads, state, c_ref, y_ref, step_ref, rows_ref, keep_ref, silu_ref, *refs):
+def gate_kernel(heads, state, c_ref, y_ref, step_ref, carry_ref, keep_ref, silu_ref, *refs):
     earlier, (gated_ref, top_ref, bottom_ref) = refs[:-3], refs[-3:]
     total, width = y_ref.shape
     head_size = width // heads
-    used = rows_ref.shape[0] // 3
     entry = jnp.zeros((state, width), F32)
     for summary in reversed(earlier):
         through = summary[state : state + EDGE, :].astype(F32)[:1]
@@ -309,41 +315,38 @@
     average = jnp.where(owner[0] == owner[1], 1.0 / head_size, 0.0).astype(BF16)
     for block in range(total // SPAN):
         rows = slice(block * SPAN, (block + 1) * SPAN)
-        carried = lanes_of(rows_ref[2 * used + block * 8 : 2 * used + (block + 1) * 8, :], width, head_size)
-        y = y_ref[rows, :] + carried * dot(c_ref[rows, :], entry.astype(BF16))
+        y = y_ref[rows, :] + carry_ref[rows, :] * dot(c_ref[rows, :], entry.astype(BF16))
         square_mean = dot((y * y).astype(BF16), average)
         gated_ref[rows, :] = (y * lax.rsqrt(square_mean + 1e-05) * silu_ref[rows, :]).astype(BF16)
-        entry = keep_ref[block * 8 : block * 8 + 1, :] * entry + step_ref[block * state : (block + 1) * state, :]
+        entry = keep_ref[block : block + 1, :] * entry + step_ref[block * state : (block + 1) * state, :]
     top_ref[...] = gated_ref[:EDGE, :]
     bottom_ref[...] = gated_ref[total - EDGE :, :]
 
 
-def conv_kernel(group, edges, len_ref, taps_ref, gated_ref, *refs):
-    if edges:
-        before_ref, after_ref, inner_ref, act_ref, ext_ref, ends_ref = refs
-    else:
-        act_ref, ext_ref, ends_ref = refs
+def conv_kernel(group, steps, len_ref, taps_ref, gated_ref, before_ref, after_ref, act_ref, ext_ref, ends_ref):
     place, plane = plane_place(group)
     total, width = gated_ref.shape
-    count = total // SPAN
+    frames = total // group
     taps = taps_ref.shape[0]
     half = (taps - 1) // 2
-    base = plane * total
     stream = lax.axis_size("tm") // group * total
     records = len_ref.shape[0]
-    reach = SPAN + 2 * EDGE
+    reach = CONV_ROWS + 2 * EDGE
     first_tap = EDGE - half
-    if edges:
-        act_ref[SPAN : total - SPAN, :] = inner_ref[...]
-        ext_ref[:EDGE, :] = before_ref[...].astype(F32)
-        ext_ref[EDGE:reach, :] = gated_ref[: SPAN + EDGE, :].astype(F32)
-        ext_ref[reach : 2 * reach - EDGE, :] = gated_ref[total - SPAN - EDGE :, :].astype(F32)
-        ext_ref[2 * reach - EDGE :, :] = after_ref[...].astype(F32)
-    else:
-        ext_ref[...] = gated_ref[SPAN - EDGE : total - SPAN + EDGE, :].astype(F32)
+    pitch = frames + 2 * EDGE
     ends_ref[0] = 0
     for record in range(records):
         ends_ref[record + 1] = ends_ref[record] + len_ref[record]
+    for number, step in enumerate(steps):
+        owner = place ^ step
+        first = pl.multiple_of(owner * frames, frames)
+        top = gated_ref[pl.ds(pl.multiple_of(jnp.maximum(first - EDGE, 0), EDGE), EDGE), :].astype(F32)
+        below = pl.multiple_of(jnp.minimum(first + frames, total - EDGE), EDGE)
+        bottom = gated_ref[pl.ds(below, EDGE), :].astype(F32)
+        at = number * pitch
+        ext_ref[at : at + EDGE, :] = jnp.where(owner == 0, before_ref[...].astype(F32), top)
+        ext_ref[at + EDGE : at + EDGE + frames, :] = gated_ref[pl.ds(first, frames), :].astype(F32)
+        ext_ref[at + EDGE + frames : at + pitch, :] = jnp.where(owner == group - 1, after_ref[...].astype(F32), bottom)
 
     def record_at(position):
         found = jnp.int32(0)
@@ -351,62 +354,55 @@
             found = found + (ends_ref[record + 1] <= position).astype(jnp.int32)
         return found
 
-    def one_block(at, source, target):
-        low = record_at(jnp.maximum(base + at - half, 0))
-        high = record_at(jnp.minimum(base + at + SPAN - 1 + half, stream - 1))
-        near = lax.broadcasted_iota(jnp.int32, (reach, LANES), 0) + (base + at - EDGE)
-        for tile in range(width // LANES):
-            lanes = slice(tile * LANES, (tile + 1) * LANES)
-            weights = taps_ref[:, pl.ds(pl.multiple_of(place * width + tile * LANES, LANES), LANES)]
-
-            def one_record(record, done):
-                inside = (near >= ends_ref[record]) & (near < ends_ref[record + 1])
-                g = jnp.where(inside, ext_ref[pl.ds(source, reach), lanes], 0.0)
-                out = None
-                for phase in range(8):
-                    part = None
-                    for offset in range(phase, reach - SPAN, 8):
-                        tap = offset - first_tap
-                        if 0 <= tap < taps:
-                            aligned = offset - phase
-                            term = weights[tap : tap + 1, :] * g[aligned : aligned + SPAN + 8, :]
-                            part = term if part is None else part + term
-                    if part is not None:
-                        moved = part[phase : phase + SPAN, :]
-                        out = moved if out is None else out + moved
-                return jnp.where(inside[EDGE : EDGE + SPAN], out, done)
-
-            conv = lax.fori_loop(low, high + 1, one_record, jnp.zeros((SPAN, LANES), F32))
-            act_ref[pl.ds(target, SPAN), lanes] = (conv / (1.0 + jnp.exp(-conv))).astype(BF16)
-        return 0
-
-    if edges:
-
-        def edge(number, _):
-            at = pl.multiple_of(number * (total - SPAN), SPAN)
-            return one_block(at, pl.multiple_of(number * reach, reach), at)
-
-        lax.fori_loop(0, 2, edge, 0)
-    else:
-
-        def inner(number, _):
-            at = pl.multiple_of(number * SPAN, SPAN)
-            return one_block(at + SPAN, at, at)
-
-        lax.fori_loop(0, count - 2, inner, 0)
-
-
-def out_kernel(group, cores, *refs):
+    for number, step in enumerate(steps):
+        base = plane * total + (place ^ step) * frames
+
+        def one_block(block, _, number=number, base=base):
+            inside_part = pl.multiple_of(block * CONV_ROWS, CONV_ROWS)
+            source = pl.multiple_of(number * pitch + inside_part, EDGE)
+            target = pl.multiple_of(number * frames + inside_part, CONV_ROWS)
+            at = base + inside_part
+            low = record_at(jnp.maximum(at - half, 0))
+            high = record_at(jnp.minimum(at + CONV_ROWS - 1 + half, stream - 1))
+            near = lax.broadcasted_iota(jnp.int32, (reach, LANES), 0) + (at - EDGE)
+            for tile in range(width // LANES):
+                lanes = slice(tile * LANES, (tile + 1) * LANES)
+                weights = taps_ref[:, pl.ds(pl.multiple_of(place * width + tile * LANES, LANES), LANES)]
+
+                def one_record(record, done):
+                    inside = (near >= ends_ref[record]) & (near < ends_ref[record + 1])
+                    g = jnp.where(inside, ext_ref[pl.ds(source, reach), lanes], 0.0)
+                    out = None
+                    for phase in range(8):
+                        part = None
+                        for offset in range(phase, reach - CONV_ROWS, 8):
+                            tap = offset - first_tap
+                            if 0 <= tap < taps:
+                                aligned = offset - phase
+                                term = weights[tap : tap + 1, :] * g[aligned : aligned + CONV_ROWS + 8, :]
+                                part = term if part is None else part + term
+                        if part is not None:
+                            moved = part[phase : phase + CONV_ROWS, :]
+                            out = moved if out is None else out + moved
+                    return jnp.where(inside[EDGE : EDGE + CONV_ROWS], out, done)
+
+                conv = lax.fori_loop(low, high + 1, one_record, jnp.zeros((CONV_ROWS, LANES), F32))
+                act_ref[pl.ds(target, CONV_ROWS), lanes] = (conv / (1.0 + jnp.exp(-conv))).astype(BF16)
+            return 0
+
+        lax.fori_loop(0, frames // CONV_ROWS, one_block, 0)
+
+
+def out_kernel(cores, *refs):
     acts, weights, outs = refs[:cores], refs[cores : 2 * cores], refs[2 * cores :]
-    place, _ = plane_place(group)
     frames = outs[0].shape[0]
-    for step in reversed(range(group)):
-        rows = pl.ds(pl.multiple_of((place ^ step) * frames, frames), frames)
+    for number, out_ref in enumerate(outs):
+        rows = slice(number * frames, (number + 1) * frames)
         total = None
         for act, weight in zip(acts, weights):
             product = dot(act[rows, :], weight[...], ((1,), (1,)))
             total = product if total is None else total + product
-        outs[step][...] = total.astype(outs[step].dtype)
+        out_ref[...] = total.astype(out_ref.dtype)
 
 
 def local(
@@ -528,17 +524,17 @@
             shape((total, state), BF16),
             shape((3 * count * 8, SPAN), F32),
             shape((count * state, width), F32),
-            shape((count * 8, width), F32),
+            shape((-(-count // 8) * 8, width), F32),
             shape((state + EDGE, width), BF16),
         ),
         [record_lengths, decay, x_columns, bc_mine, frames, swap, *payloads[1:]],
-        [pltpu.VMEM((depth, 2 * state), BF16)],
+        [pltpu.VMEM((depth, 2 * state), BF16), pltpu.VMEM((total, width), F32)],
         flops=2 * total * depth * (width + 2 * state),
     )
     summaries = [later(summary, step) for step in range(1, planes)]
-    y = call(
+    y, carry = call(
         functools.partial(inner_kernel, group, heads),
-        shape((total, width), F32),
+        (shape((total, width), F32), shape((total, width), F32)),
         [x_rows, b_rows, c_rows, decay_rows],
         flops=4 * total * SPAN * width,
         smem=0,
@@ -550,34 +546,48 @@
         flops=2 * total * depth * width,
         smem=0,
     )
+    silu = call(
+        functools.partial(silu_kernel, group),
+        shape((total, width), F32),
+        [norm_gain[None], frame_rows, z_columns],
+        flops=2 * total * depth * width,
+        smem=0,
+    )
     out_stack, summaries, y = lax.optimization_barrier((out_stack, summaries, y))
     out_pieces = [out_stack] + [between_planes(out_stack, step) for step in range(1, planes)]
     gated, top, bottom = call(
         functools.partial(gate_kernel, heads, state),
         (shape((total, width), BF16), shape((EDGE, width), BF16), shape((EDGE, width), BF16)),
-        [c_rows, y, steps, decay_rows, keep, silu, *summaries],
+        [c_rows, y, steps, carry, keep, silu, *summaries],
         flops=2 * total * state * width,
         smem=0,
     )
     before, after = later(bottom, 1), earlier(top, 1)
-    gated, out_pieces[1] = lax.optimization_barrier((gated, out_pieces[1]))
     ends = pltpu.SMEM((record_lengths.shape[0] + 1,), jnp.int32)
-    inner = call(
-        functools.partial(conv_kernel, group, False),
-        shape((total - 2 * SPAN, width), BF16),
-        [record_lengths, conv_weight, gated],
-        [pltpu.VMEM((total - 2 * SPAN + 2 * EDGE, width), F32), ends],
-        flops=2 * total * width * conv_weight.shape[0],
-    )
-    inner, out_pieces[2:] = lax.optimization_barrier((inner, out_pieces[2:]))
-    act = call(
-        functools.partial(conv_kernel, group, True),
-        shape((total, width), BF16),
-        [record_lengths, conv_weight, gated, before, after, inner],
-        [pltpu.VMEM((2 * SPAN + 4 * EDGE, width), F32), ends],
-        flops=4 * SPAN * width * conv_weight.shape[0],
-    )
     share = depth // cores
+    far, near = (group - 1,), (*range(1, group - 1), 0)
+
+    def conv(steps, gated):
+        return call(
+            functools.partial(conv_kernel, group, steps),
+            shape((len(steps) * frame_count, width), BF16),
+            [record_lengths, conv_weight, gated, before, after],
+            [pltpu.VMEM((len(steps) * (frame_count + 2 * EDGE), width), F32), ends],
+            flops=2 * len(steps) * frame_count * width * conv_weight.shape[0],
+        )
+
+    def out(steps, act, swapped):
+        return call(
+            functools.partial(out_kernel, cores),
+            tuple(shape((frame_count, share), BF16 if step else F32) for step in steps),
+            [act, *swapped, *out_parts],
+            flops=2 * len(steps) * frame_count * width * cores * share,
+            smem=0,
+        )
+
+    far_act = conv(far, gated)
+    far_swapped = [across(far_act, step) for step in range(1, cores)]
+    far_act, out_pieces = lax.optimization_barrier((far_act, out_pieces))
     out_parts = call(
         functools.partial(share_kernel, cores, tuple(range(planes)), group),
         tuple(shape((share, width), BF16) for _ in range(cores)),
@@ -586,17 +596,17 @@
         smem=0,
     )
     out_parts = [out_parts[0]] + [across(out_parts[step], step) for step in range(1, cores)]
-    acts = [act] + [across(act, step) for step in range(1, cores)]
-    outs = call(
-        functools.partial(out_kernel, group, cores),
-        tuple(shape((frame_count, share), BF16 if step else F32) for step in range(group)),
-        [*acts, *out_parts],
-        flops=2 * total * width * cores * share,
-        smem=0,
-    )
-    mixed = outs[0]
-    for step in range(1, group):
-        mixed = mixed + in_plane(outs[step], step).astype(F32)
+    gated, far_act = lax.optimization_barrier((gated, far_act))
+    near_act = conv(near, gated)
+    near_act, far_swapped, out_parts = lax.optimization_barrier((near_act, far_swapped, out_parts))
+    (far_out,) = out(far, far_act, far_swapped)
+    near_act, far_out = lax.optimization_barrier((near_act, far_out))
+    far_out = in_plane(far_out, far[0])
+    near_swapped = [across(near_act, step) for step in range(1, cores)]
+    near_outs = out(near, near_act, near_swapped)
+    mixed = near_outs[-1] + far_out.astype(F32)
+    for step, partial in zip(near[:-1], near_outs[:-1]):
+        mixed = mixed + in_plane(partial, step).astype(F32)
     return mixed.astype(BF16)
 
 

time: 94.3 us -> 90.8 us (0.963)
  Pallas kernels: 18.8 us -> 15.2 us
    ppermute x1, waiting for transfers between devices: 0.01 us -> 4.15 us  [earlier(): lax.ppermute(array, 'tm', [(i + step * group, i) for i in range(times - s...]
    pallas_call x13 -> x14, Pallas kernels: 18.8 us -> 15.2 us  [call(): pl.pallas_call(kernel, out_shape=out_shape, in_specs=in_specs, out_specs=...]
    ppermute x9, waiting for transfers between devices: 16.9 us -> 14.9 us  [in_plane(): return lax.ppermute(array, 'tm', [(i, i ^ step) for i in range(times)])]
    ppermute x3 -> x4, waiting for transfers between devices: 3.11 us -> 1.5 us  [across(): return lax.ppermute(array, 'head', [(i, i ^ step) for i in range(cores)])]
    ppermute x9, starting transfers between devices: 11.6 us -> 12.8 us  [in_plane(): return lax.ppermute(array, 'tm', [(i, i ^ step) for i in range(times)])]
  transfers between devices with their start and end apart: 27 -> 28, of which waited for: 12 -> 13; matrix products, arithmetic and copies ran while one was open for 0% -> 0% of each run, Pallas kernels for 10% -> 11%
where the time goes in v7:
time: 90.8 us; the launch traced here: 90.7 us
  starting transfers between devices  40.4 us (44%)
  waiting for transfers between devices  33 us (36%)
  Pallas kernels  15.2 us (17%)
  local copies, waits for them, and re-layouts  0.93 us (1%)
    pallas_call x14, Pallas kernels, call(): pl.pallas_call(kernel, out_shape=out_shape, in_specs=in_specs, out_specs=...  15.2 us
    ppermute x9, waiting for transfers between devices, in_plane(): return lax.ppermute(array, 'tm', [(i, i ^ step) for i in range(times)])  14.9 us
    ppermute x8, starting transfers between devices, between_planes(): lax.ppermute(array, 'tm', [(i, i ^ step * group) for i in range(times)])  12.9 us
    ppermute x9, starting transfers between devices, in_plane(): return lax.ppermute(array, 'tm', [(i, i ^ step) for i in range(times)])  12.8 us
    ppermute x8, waiting for transfers between devices, between_planes(): lax.ppermute(array, 'tm', [(i, i ^ step * group) for i in range(times)])  10.9 us
    ppermute x4, starting transfers between devices, later(): lax.ppermute(array, 'tm', [(i, i + step * group) for i in range(times - s...  10.7 us
    ppermute x1, waiting for transfers between devices, earlier(): lax.ppermute(array, 'tm', [(i + step * group, i) for i in range(times - s...  4.15 us
  transfers between devices with their start and end apart: 28, of which 13 were waited for; matrix products, arithmetic and copies ran while one was open for 0% of the time, Pallas kernels for 11%

profile of v7, /device:TPU:0, one launch (start us, length us, event | category | flops | bytes accessed | tf_op | source)
XLA Modules:
  0.0 90.7 jit_solution(1549902642309235570)
XLA Ops:
  0.0 1.8 %shard_map.91 = (bf16[64,128]{1,0:T(8,128)(2,1)}, bf16[64,768]{1,0:T(8,128)(2,1)}, bf16[64,768]{1,0:T(8,128)(2,1)}, bf16[64,768]{1,0:T(8,128)(2,1)}, bf16[64,768]{1,0:T(8,128)(2,1)}) custom-call(bf16[64,256]{1,0:T(8,128)(2,1)} %bc_ref.1, bf16[64,1024]{1,0:T(8,128)(2,1)} %refs_0_.1, bf16[64,1024]{1,0:T(8,128)(2,1)} %refs_1_.1, bf16[64,1024]{1,0:T(8,128)(2,1)} %bitcast.3), custom_call_target="tpu_custom_call" | custom-call | bytes 835584 | tf_op jit(solution)/shard_map/pallas_call | solution.py:32
  1.8 3.0 %collective-permute-start = (bf16[64,768]{1,0:T(8,128)(2,1)}, bf16[64,768]{1,0:T(8,128)(2,1)S(1)}, u32[]{:S(2)}, u32[]{:S(2)}) collective-permute-start(bf16[64,768]{1,0:T(8,128)(2,1)} %get-tuple-element.69), channel_id=1, source_target_pairs={{0,2},{2,0},{4,6},{6,4},{8,10},{10,8},{12,14},{14,12},{16,18},{18,... | collective-permute-start | bytes 294920 | tf_op jit(solution)/shard_map/ppermute | solution.py:434
  4.8 1.5 %collective-permute-start.1 = (bf16[64,768]{1,0:T(8,128)(2,1)}, bf16[64,768]{1,0:T(8,128)(2,1)S(1)}, u32[]{:S(2)}, u32[]{:S(2)}) collective-permute-start(bf16[64,768]{1,0:T(8,128)(2,1)} %get-tuple-element.70), channel_id=1, source_target_pairs={{0,4},{2,6},{4,0},{6,2},{8,12},{10,14},{12,8},{14,10},{16,20},{18,... | collective-permute-start | bytes 294920 | tf_op jit(solution)/shard_map/ppermute | solution.py:434
  6.4 4.1 %collective-permute-start.5 = (bf16[64,128]{1,0:T(8,128)(2,1)}, bf16[64,128]{1,0:T(8,128)(2,1)S(1)}, u32[]{:S(2)}, u32[]{:S(2)}) collective-permute-start(bf16[64,128]{1,0:T(8,128)(2,1)} %get-tuple-element.73.refs_0_), channel_id=1, source_target_pairs={{0,24},{2,26},{4,28},{6,30},{8,16},{10,18},{12,20},{14,22},{16,8},... | collective-permute-start | bytes 49160 | tf_op jit(solution)/shard_map/ppermute | solution.py:446
  10.4 1.9 %collective-permute-done.5.refs_3_ = bf16[64,128]{1,0:T(8,128)(2,1)S(1)} collective-permute-done((bf16[64,128]{1,0:T(8,128)(2,1)}, bf16[64,128]{1,0:T(8,128)(2,1)S(1)}, u32[]{:S(2)}, u32[]{:S(2)}) %collective-permute-start.5) | collective-permute-done | bytes 16416 | tf_op jit(solution)/shard_map/ppermute | solution.py:446
  12.4 2.9 %collective-permute-done.4.refs_2_ = bf16[64,128]{1,0:T(8,128)(2,1)S(1)} collective-permute-done((bf16[64,128]{1,0:T(8,128)(2,1)}, bf16[64,128]{1,0:T(8,128)(2,1)S(1)}, u32[]{:S(2)}, u32[]{:S(2)}) %collective-permute-start.4) | collective-permute-done | bytes 16416 | tf_op jit(solution)/shard_map/ppermute | solution.py:446
  15.3 1.0 %collective-permute-done.3.refs_1_ = bf16[64,128]{1,0:T(8,128)(2,1)S(1)} collective-permute-done((bf16[64,128]{1,0:T(8,128)(2,1)}, bf16[64,128]{1,0:T(8,128)(2,1)S(1)}, u32[]{:S(2)}, u32[]{:S(2)}) %collective-permute-start.3) | collective-permute-done | bytes 16416 | tf_op jit(solution)/shard_map/ppermute | solution.py:446
  16.3 0.9 copy-done.5
  17.3 4.4 %collective-permute-start.9 = (bf16[256,512]{1,0:T(8,128)(2,1)S(1)}, bf16[256,512]{1,0:T(8,128)(2,1)S(1)}, u32[]{:S(2)}, u32[]{:S(2)}) collective-permute-start(bf16[256,512]{1,0:T(8,128)(2,1)S(1)} %get-tuple-element.89.refs_0_), channel_id=1, source_target_pairs={{0,16},{2,18},{4,20},{6,22},{8,24},{10,26},{12,28},{14,30},{16,0},... | collective-permute-start | bytes 786440 | tf_op jit(solution)/shard_map/ppermute | solution.py:446
  21.8 0.1 shard_map.92
  21.9 1.6 %collective-permute-start.6 = (bf16[176,1024]{1,0:T(8,128)(2,1)S(1)}, bf16[176,1024]{1,0:T(8,128)(2,1)S(1)}, u32[]{:S(2)}, u32[]{:S(2)}) collective-permute-start(bf16[176,1024]{1,0:T(8,128)(2,1)S(1)} %get-tuple-element.78), channel_id=1, source_target_pairs={{0,2},{2,0},{4,6},{6,4},{8,10},{10,8},{12,14},{14,12},{16,18},{18,... | collective-permute-start | bytes 1081352 | tf_op jit(solution)/shard_map/ppermute | solution.py:434
  23.4 1.5 %collective-permute-start.7 = (bf16[176,1024]{1,0:T(8,128)(2,1)S(1)}, bf16[176,1024]{1,0:T(8,128)(2,1)S(1)}, u32[]{:S(2)}, u32[]{:S(2)}) collective-permute-start(bf16[176,1024]{1,0:T(8,128)(2,1)S(1)} %get-tuple-element.79), channel_id=1, source_target_pairs={{0,4},{2,6},{4,0},{6,2},{8,12},{10,14},{12,8},{14,10},{16,20},{18,... | collective-permute-start | bytes 1081352 | tf_op jit(solution)/shard_map/ppermute | solution.py:434
  25.0 0.5 collective-permute-start.8
  25.4 2.5 %collective-permute-done.10.refs_1_ = bf16[256,512]{1,0:T(8,128)(2,1)S(1)} collective-permute-done((bf16[256,512]{1,0:T(8,128)(2,1)S(1)}, bf16[256,512]{1,0:T(8,128)(2,1)S(1)}, u32[]{:S(2)}, u32[]{:S(2)}) %collective-permute-start.10) | collective-permute-done | bytes 262176 | tf_op jit(solution)/shard_map/ppermute | solution.py:446
  27.9 2.5 %collective-permute-done.9.refs_2_ = bf16[256,512]{1,0:T(8,128)(2,1)S(1)} collective-permute-done((bf16[256,512]{1,0:T(8,128)(2,1)S(1)}, bf16[256,512]{1,0:T(8,128)(2,1)S(1)}, u32[]{:S(2)}, u32[]{:S(2)}) %collective-permute-start.9) | collective-permute-done | bytes 262176 | tf_op jit(solution)/shard_map/ppermute | solution.py:446
  30.4 1.3 %collective-permute-start.11 = (bf16[256,512]{1,0:T(8,128)(2,1)S(1)}, bf16[256,512]{1,0:T(8,128)(2,1)S(1)}, u32[]{:S(2)}, u32[]{:S(2)}) collective-permute-start(bf16[256,512]{1,0:T(8,128)(2,1)S(1)} %collective-permute-done.9.refs_2_), channel_id=1, source_target_pairs={{8,0},{10,2},{12,4},{14,6},{16,24},{18,26},{20,28},{22,30},{9,1},{... | collective-permute-start | bytes 786440 | tf_op jit(solution)/shard_map/ppermute | solution.py:462
  31.7 0.7 collective-permute-start.12
  32.4 4.9 %collective-permute-done.7.refs_2_.refs_1_ = bf16[176,1024]{1,0:T(8,128)(2,1)S(1)} collective-permute-done((bf16[176,1024]{1,0:T(8,128)(2,1)S(1)}, bf16[176,1024]{1,0:T(8,128)(2,1)S(1)}, u32[]{:S(2)}, u32[]{:S(2)}) %collective-permute-start.7) | collective-permute-done | bytes 360480 | tf_op jit(solution)/shard_map/ppermute | solution.py:434
  37.3 0.2 shard_map.93
  37.6 1.1 %collective-permute-done.11.refs_3_ = bf16[256,512]{1,0:T(8,128)(2,1)S(1)} collective-permute-done((bf16[256,512]{1,0:T(8,128)(2,1)S(1)}, bf16[256,512]{1,0:T(8,128)(2,1)S(1)}, u32[]{:S(2)}, u32[]{:S(2)}) %collective-permute-start.11) | collective-permute-done | bytes 262176 | tf_op jit(solution)/shard_map/ppermute | solution.py:462
  38.8 1.5 %collective-permute-done.13.swap_ref = bf16[512,1024]{1,0:T(8,128)(2,1)S(1)} collective-permute-done((bf16[512,1024]{1,0:T(8,128)(2,1)S(1)}, bf16[512,1024]{1,0:T(8,128)(2,1)S(1)}, u32[]{:S(2)}, u32[]{:S(2)}) %collective-permute-start.13) | collective-permute-done | bytes 1048608 | tf_op jit(solution)/shard_map/ppermute | solution.py:443
  40.3 2.6 %shard_map.96 = (bf16[1024,1024]{1,0:T(8,128)(2,1)S(1)}, bf16[1024,256]{1,0:T(8,128)(2,1)S(1)}, bf16[1024,128]{1,0:T(8,128)(2,1)S(1)}, bf16[1024,128]{1,0:T(8,12...) custom-call(s32[8]{0:T(128)S(1)} %copy-done.4, ...), custom_call_target="tpu_custom_call" | custom-call | flops 1073741824 | bytes 7847968 | tf_op jit(solution)/shard_map/pallas_call | solution.py:32
  42.9 2.8 %collective-permute-start.16 = (bf16[144,256]{1,0:T(8,128)(2,1)S(1)}, bf16[144,256]{1,0:T(8,128)(2,1)S(1)}, u32[]{:S(2)}, u32[]{:S(2)}) collective-permute-start(bf16[144,256]{1,0:T(8,128)(2,1)S(1)} %get-tuple-element.95), channel_id=1, source_target_pairs={{0,24},{2,26},{4,28},{6,30},{1,25},{3,27},{5,29},{7,31}} | collective-permute-start | bytes 221192 | tf_op jit(solution)/shard_map/ppermute | solution.py:437
  45.7 3.2 %collective-permute-start.15 = (bf16[144,256]{1,0:T(8,128)(2,1)S(1)}, bf16[144,256]{1,0:T(8,128)(2,1)S(1)}, u32[]{:S(2)}, u32[]{:S(2)}) collective-permute-start(bf16[144,256]{1,0:T(8,128)(2,1)S(1)} %get-tuple-element.95), channel_id=1, source_target_pairs={{0,16},{2,18},{4,20},{6,22},{8,24},{10,26},{12,28},{14,30},{1,17},... | collective-permute-start | bytes 221192 | tf_op jit(solution)/shard_map/ppermute | solution.py:437
  48.9 1.3 %collective-permute-start.14 = (bf16[144,256]{1,0:T(8,128)(2,1)S(1)}, bf16[144,256]{1,0:T(8,128)(2,1)S(1)}, u32[]{:S(2)}, u32[]{:S(2)}) collective-permute-start(bf16[144,256]{1,0:T(8,128)(2,1)S(1)} %get-tuple-element.95), channel_id=1, source_target_pairs={{0,8},{2,10},{4,12},{6,14},{8,16},{10,18},{12,20},{14,22},{16,24},... | collective-permute-start | bytes 221192 | tf_op jit(solution)/shard_map/ppermute | solution.py:437
  50.2 1.5 %shard_map.97 = (f32[1024,256]{1,0:T(8,128)S(1)}, f32[1024,256]{1,0:T(8,128)S(1)}) custom-call(bf16[1024,256]{1,0:T(8,128)(2,1)S(1)} %get-tuple-element.96.x_ref, bf16[1024,128]{1,0:T(8,128)(2,1)S(1)} %get-tuple-element.97.b_ref, bf16[1024,128]{1,0:T(8,128)(2,1)S(1)} %get-tuple-element.93.c_ref, f32[192,128]{1,0:T(8,128)S(1)} %get-tuple-element.98.rows_ref), custom_call_target="tpu_custom_call" | custom-call | flops 134217728 | bytes 3244032 | tf_op jit(solution)/shard_map/pallas_call | solution.py:32
  51.7 0.4 collective-permute-done.14.refs_0_
  52.1 2.8 %collective-permute-start.21 = (bf16[256,256]{1,0:T(8,128)(2,1)S(1)}, bf16[256,256]{1,0:T(8,128)(2,1)S(1)}, u32[]{:S(2)}, u32[]{:S(2)}) collective-permute-start(bf16[256,256]{1,0:T(8,128)(2,1)S(1)} %get-tuple-element.115.refs_0_), channel_id=1, source_target_pairs={{0,24},{2,26},{4,28},{6,30},{8,16},{10,18},{12,20},{14,22},{16,8},... | collective-permute-start | bytes 393224 | tf_op jit(solution)/shard_map/ppermute | solution.py:446
  54.9 1.1 %collective-permute-start.20 = (bf16[256,256]{1,0:T(8,128)(2,1)S(1)}, bf16[256,256]{1,0:T(8,128)(2,1)S(1)}, u32[]{:S(2)}, u32[]{:S(2)}) collective-permute-start(bf16[256,256]{1,0:T(8,128)(2,1)S(1)} %get-tuple-element.115.refs_0_), channel_id=1, source_target_pairs={{0,16},{2,18},{4,20},{6,22},{8,24},{10,26},{12,28},{14,30},{16,0},... | collective-permute-start | bytes 393224 | tf_op jit(solution)/shard_map/ppermute | solution.py:446
  56.0 0.6 collective-permute-start.19
  56.5 0.9 %shard_map.98.silu_ref = f32[1024,256]{1,0:T(8,128)S(1)} custom-call(f32[1,1024]{1,0:T(1,128)S(1)} %bitcast.2, bf16[1024,1024]{1,0:T(8,128)(2,1)S(1)} %get-tuple-element.104.frames_ref, bf16[1024,256]{1,0:T(8,128)(2,1)S(1)} %get-tuple-element.105.weight_ref), custom_call_target="tpu_custom_call" | custom-call | flops 536870912 | bytes 3674112 | tf_op jit(solution)/shard_map/pallas_call | solution.py:32
  57.5 0.6 shard_map.99
  58.1 3.4 %collective-permute-start.17 = (bf16[16,256]{1,0:T(8,128)(2,1)S(1)}, bf16[16,256]{1,0:T(8,128)(2,1)S(1)}, u32[]{:S(2)}, u32[]{:S(2)}) collective-permute-start(bf16[16,256]{1,0:T(8,128)(2,1)S(1)} %get-tuple-element.110), channel_id=1, source_target_pairs={{0,8},{2,10},{4,12},{6,14},{8,16},{10,18},{12,20},{14,22},{16,24},... | collective-permute-start | bytes 24584 | tf_op jit(solution)/shard_map/ppermute | solution.py:437
  61.5 1.3 %collective-permute-start.18 = (bf16[16,256]{1,0:T(8,128)(2,1)S(1)}, bf16[16,256]{1,0:T(8,128)(2,1)S(1)}, u32[]{:S(2)}, u32[]{:S(2)}) collective-permute-start(bf16[16,256]{1,0:T(8,128)(2,1)S(1)} %get-tuple-element.111), channel_id=1, source_target_pairs={{8,0},{10,2},{12,4},{14,6},{16,8},{18,10},{20,12},{22,14},{24,16},... | collective-permute-start | bytes 24584 | tf_op jit(solution)/shard_map/ppermute | solution.py:440
  62.8 0.1 collective-permute-done.17.before_ref
  62.9 4.2 %collective-permute-done.18.after_ref = bf16[16,256]{1,0:T(8,128)(2,1)S(1)} collective-permute-done((bf16[16,256]{1,0:T(8,128)(2,1)S(1)}, bf16[16,256]{1,0:T(8,128)(2,1)S(1)}, u32[]{:S(2)}, u32[]{:S(2)}) %collective-permute-start.18) | collective-permute-done | bytes 8224 | tf_op jit(solution)/shard_map/ppermute | solution.py:440
  67.1 1.6 %shard_map.100.refs_0_ = bf16[256,256]{1,0:T(8,128)(2,1)S(1)} custom-call(s32[8]{0:T(128)S(1)} %copy-done.4, f32[31,1024]{1,0:T(8,128)S(1)} %copy-done.1, bf16[1024,256]{1,0:T(8,128)(2,1)S(1)} %get-tuple-element.114.gated_ref, bf16[16,256]{1,0:T(8,128)(2,1)S(1)} %collective-permute-done.17.before_ref, bf16[16,256]{1,0:T(8,128)(2,1)S(1)} %collective-permute-done.18.after_ref), custom_call_target="tpu_custom_call" | custom-call | flops 4063232 | bytes 798752 | tf_op jit(solution)/shard_map/pallas_call | solution.py:32
  68.9 0.5 collective-permute-start.22
  69.4 4.7 %shard_map.101.refs_0_ = bf16[768,256]{1,0:T(8,128)(2,1)S(1)} custom-call(s32[8]{0:T(128)S(1)} %copy-done.4, f32[31,1024]{1,0:T(8,128)S(1)} %copy-done.1, bf16[1024,256]{1,0:T(8,128)(2,1)S(1)} %get-tuple-element.114.gated_ref, bf16[16,256]{1,0:T(8,128)(2,1)S(1)} %collective-permute-done.17.before_ref, bf16[16,256]{1,0:T(8,128)(2,1)S(1)} %collective-permute-done.18.after_ref), custom_call_target="tpu_custom_call" | custom-call | flops 12189696 | bytes 1060896 | tf_op jit(solution)/shard_map/pallas_call | solution.py:32
  74.1 0.3 shard_map.103
  74.4 0.1 collective-permute-start.24
  74.6 2.4 %collective-permute-start.25 = (bf16[256,512]{1,0:T(8,128)(2,1)S(1)}, bf16[256,512]{1,0:T(8,128)(2,1)S(1)}, u32[]{:S(2)}, u32[]{:S(2)}) collective-permute-start(bf16[256,512]{1,0:T(8,128)(2,1)S(1)} %shard_map.103), channel_id=1, source_target_pairs={{0,6},{2,4},{4,2},{6,0},{8,14},{10,12},{12,10},{14,8},{16,22},{18,... | collective-permute-start | bytes 786440 | tf_op jit(solution)/shard_map/ppermute | solution.py:434
  77.0 0.6 shard_map.104
  77.6 0.8 collective-permute-start.26
  78.4 1.5 %collective-permute-start.27 = (bf16[256,512]{1,0:T(8,128)(2,1)S(1)}, bf16[256,512]{1,0:T(8,128)(2,1)S(1)}, u32[]{:S(2)}, u32[]{:S(2)}) collective-permute-start(bf16[256,512]{1,0:T(8,128)(2,1)S(1)} %get-tuple-element.130), channel_id=1, source_target_pairs={{0,4},{2,6},{4,0},{6,2},{8,12},{10,14},{12,8},{14,10},{16,20},{18,... | collective-permute-start | bytes 786440 | tf_op jit(solution)/shard_map/ppermute | solution.py:434
  79.9 4.7 %collective-permute-done.25 = bf16[256,512]{1,0:T(8,128)(2,1)S(1)} collective-permute-done((bf16[256,512]{1,0:T(8,128)(2,1)S(1)}, bf16[256,512]{1,0:T(8,128)(2,1)S(1)}, u32[]{:S(2)}, u32[]{:S(2)}) %collective-permute-start.25) | collective-permute-done | bytes 262176 | tf_op jit(solution)/shard_map/ppermute | solution.py:434
  84.6 5.2 %collective-permute-done.26 = bf16[256,512]{1,0:T(8,128)(2,1)S(1)} collective-permute-done((bf16[256,512]{1,0:T(8,128)(2,1)S(1)}, bf16[256,512]{1,0:T(8,128)(2,1)S(1)}, u32[]{:S(2)}, u32[]{:S(2)}) %collective-permute-start.26) | collective-permute-done | bytes 262176 | tf_op jit(solution)/shard_map/ppermute | solution.py:434
  89.9 0.8 add_convert_fusion
  (39 shorter events, 0.5 us)
Async XLA Ops:
  1.8 14.5 %collective-permute-start = (bf16[64,768]{1,0:T(8,128)(2,1)}, bf16[64,768]{1,0:T(8,128)(2,1)S(1)}, u32[]{:S(2)}, u32[]{:S(2)}) collective-permute-start(bf16[64,768]{1,0:T(8,128)(2,1)} %get-tuple-element.69), channel_id=1, source_target_pairs={{0,2},{2,0},{4,6},{6,4},{8,10},{10,8},{12,14},{14,12},{16,18},{18,... | collective-permute-start | bytes 294920 | tf_op jit(solution)/shard_map/ppermute | solution.py:434
  4.8 11.5 %collective-permute-start.1 = (bf16[64,768]{1,0:T(8,128)(2,1)}, bf16[64,768]{1,0:T(8,128)(2,1)S(1)}, u32[]{:S(2)}, u32[]{:S(2)}) collective-permute-start(bf16[64,768]{1,0:T(8,128)(2,1)} %get-tuple-element.70), channel_id=1, source_target_pairs={{0,4},{2,6},{4,0},{6,2},{8,12},{10,14},{12,8},{14,10},{16,20},{18,... | collective-permute-start | bytes 294920 | tf_op jit(solution)/shard_map/ppermute | solution.py:434
  6.3 10.0 %collective-permute-start.2 = (bf16[64,768]{1,0:T(8,128)(2,1)}, bf16[64,768]{1,0:T(8,128)(2,1)S(1)}, u32[]{:S(2)}, u32[]{:S(2)}) collective-permute-start(bf16[64,768]{1,0:T(8,128)(2,1)} %get-tuple-element.71), channel_id=1, source_target_pairs={{0,6},{2,4},{4,2},{6,0},{8,14},{10,12},{12,10},{14,8},{16,22},{18,... | collective-permute-start | bytes 294920 | tf_op jit(solution)/shard_map/ppermute | solution.py:434
  6.4 6.0 %collective-permute-start.5 = (bf16[64,128]{1,0:T(8,128)(2,1)}, bf16[64,128]{1,0:T(8,128)(2,1)S(1)}, u32[]{:S(2)}, u32[]{:S(2)}) collective-permute-start(bf16[64,128]{1,0:T(8,128)(2,1)} %get-tuple-element.73.refs_0_), channel_id=1, source_target_pairs={{0,24},{2,26},{4,28},{6,30},{8,16},{10,18},{12,20},{14,22},{16,8},... | collective-permute-start | bytes 49160 | tf_op jit(solution)/shard_map/ppermute | solution.py:446
  10.4 4.8 %collective-permute-start.4 = (bf16[64,128]{1,0:T(8,128)(2,1)}, bf16[64,128]{1,0:T(8,128)(2,1)S(1)}, u32[]{:S(2)}, u32[]{:S(2)}) collective-permute-start(bf16[64,128]{1,0:T(8,128)(2,1)} %get-tuple-element.73.refs_0_), channel_id=1, source_target_pairs={{0,16},{2,18},{4,20},{6,22},{8,24},{10,26},{12,28},{14,30},{16,0},... | collective-permute-start | bytes 49160 | tf_op jit(solution)/shard_map/ppermute | solution.py:446
  12.4 3.9 %collective-permute-start.3 = (bf16[64,128]{1,0:T(8,128)(2,1)}, bf16[64,128]{1,0:T(8,128)(2,1)S(1)}, u32[]{:S(2)}, u32[]{:S(2)}) collective-permute-start(bf16[64,128]{1,0:T(8,128)(2,1)} %get-tuple-element.73.refs_0_), channel_id=1, source_target_pairs={{0,8},{2,10},{4,12},{6,14},{8,0},{10,2},{12,4},{14,6},{16,24},{18,... | collective-permute-start | bytes 49160 | tf_op jit(solution)/shard_map/ppermute | solution.py:446
  16.3 0.9 copy-start.5
  17.2 4.5 %copy-start.6 = (f32[16,256]{1,0:T(8,128)S(1)}, f32[16,256]{1,0:T(8,128)}, u32[]{:S(2)}) copy-start(f32[16,256]{1,0:T(8,128)} %param.13) | copy-start | bytes 49156
  17.2 4.5 %copy-start = (bf16[256,1024]{1,0:T(8,128)(2,1)S(1)}, bf16[256,1024]{1,0:T(8,128)(2,1)}, u32[]{:S(2)}) copy-start(bf16[256,1024]{1,0:T(8,128)(2,1)} %own_ref.1) | copy-start | bytes 1572868
  17.2 4.5 %copy-start.2 = (bf16[64,128]{1,0:T(8,128)(2,1)S(1)}, bf16[64,128]{1,0:T(8,128)(2,1)}, u32[]{:S(2)}) copy-start(bf16[64,128]{1,0:T(8,128)(2,1)} %get-tuple-element.73.refs_0_) | copy-start | bytes 49156
  17.3 10.6 %collective-permute-start.10 = (bf16[256,512]{1,0:T(8,128)(2,1)S(1)}, bf16[256,512]{1,0:T(8,128)(2,1)S(1)}, u32[]{:S(2)}, u32[]{:S(2)}) collective-permute-start(bf16[256,512]{1,0:T(8,128)(2,1)S(1)} %get-tuple-element.89.refs_0_), channel_id=1, source_target_pairs={{0,8},{2,10},{4,12},{6,14},{8,0},{10,2},{12,4},{14,6},{16,24},{18,... | collective-permute-start | bytes 786440 | tf_op jit(solution)/shard_map/ppermute | solution.py:446
  17.3 13.1 %collective-permute-start.9 = (bf16[256,512]{1,0:T(8,128)(2,1)S(1)}, bf16[256,512]{1,0:T(8,128)(2,1)S(1)}, u32[]{:S(2)}, u32[]{:S(2)}) collective-permute-start(bf16[256,512]{1,0:T(8,128)(2,1)S(1)} %get-tuple-element.89.refs_0_), channel_id=1, source_target_pairs={{0,16},{2,18},{4,20},{6,22},{8,24},{10,26},{12,28},{14,30},{16,0},... | collective-permute-start | bytes 786440 | tf_op jit(solution)/shard_map/ppermute | solution.py:446
  21.9 10.5 %collective-permute-start.6 = (bf16[176,1024]{1,0:T(8,128)(2,1)S(1)}, bf16[176,1024]{1,0:T(8,128)(2,1)S(1)}, u32[]{:S(2)}, u32[]{:S(2)}) collective-permute-start(bf16[176,1024]{1,0:T(8,128)(2,1)S(1)} %get-tuple-element.78), channel_id=1, source_target_pairs={{0,2},{2,0},{4,6},{6,4},{8,10},{10,8},{12,14},{14,12},{16,18},{18,... | collective-permute-start | bytes 1081352 | tf_op jit(solution)/shard_map/ppermute | solution.py:434
  23.4 13.9 %collective-permute-start.7 = (bf16[176,1024]{1,0:T(8,128)(2,1)S(1)}, bf16[176,1024]{1,0:T(8,128)(2,1)S(1)}, u32[]{:S(2)}, u32[]{:S(2)}) collective-permute-start(bf16[176,1024]{1,0:T(8,128)(2,1)S(1)} %get-tuple-element.79), channel_id=1, source_target_pairs={{0,4},{2,6},{4,0},{6,2},{8,12},{10,14},{12,8},{14,10},{16,20},{18,... | collective-permute-start | bytes 1081352 | tf_op jit(solution)/shard_map/ppermute | solution.py:434
  25.0 12.4 %collective-permute-start.8 = (bf16[176,1024]{1,0:T(8,128)(2,1)S(1)}, bf16[176,1024]{1,0:T(8,128)(2,1)S(1)}, u32[]{:S(2)}, u32[]{:S(2)}) collective-permute-start(bf16[176,1024]{1,0:T(8,128)(2,1)S(1)} %get-tuple-element.80), channel_id=1, source_target_pairs={{0,6},{2,4},{4,2},{6,0},{8,14},{10,12},{12,10},{14,8},{16,22},{18,... | collective-permute-start | bytes 1081352 | tf_op jit(solution)/shard_map/ppermute | solution.py:434
  30.4 8.3 %collective-permute-start.11 = (bf16[256,512]{1,0:T(8,128)(2,1)S(1)}, bf16[256,512]{1,0:T(8,128)(2,1)S(1)}, u32[]{:S(2)}, u32[]{:S(2)}) collective-permute-start(bf16[256,512]{1,0:T(8,128)(2,1)S(1)} %collective-permute-done.9.refs_2_), channel_id=1, source_target_pairs={{8,0},{10,2},{12,4},{14,6},{16,24},{18,26},{20,28},{22,30},{9,1},{... | collective-permute-start | bytes 786440 | tf_op jit(solution)/shard_map/ppermute | solution.py:462
  31.7 7.0 %collective-permute-start.12 = (bf16[256,512]{1,0:T(8,128)(2,1)S(1)}, bf16[256,512]{1,0:T(8,128)(2,1)S(1)}, u32[]{:S(2)}, u32[]{:S(2)}) collective-permute-start(bf16[256,512]{1,0:T(8,128)(2,1)S(1)} %get-tuple-element.89.refs_0_), channel_id=1, source_target_pairs={{8,16},{10,18},{12,20},{14,22},{16,8},{18,10},{20,12},{22,14},{9,1... | collective-permute-start | bytes 786440 | tf_op jit(solution)/shard_map/ppermute | solution.py:463
  37.5 2.7 %copy-start.4 = (s32[8]{0:T(128)S(1)}, s32[8]{0:T(128)}, u32[]{:S(2)}) copy-start(s32[8]{0:T(128)} %len_ref.5) | copy-start | bytes 100
  37.5 2.7 %collective-permute-start.13 = (bf16[512,1024]{1,0:T(8,128)(2,1)S(1)}, bf16[512,1024]{1,0:T(8,128)(2,1)S(1)}, u32[]{:S(2)}, u32[]{:S(2)}) collective-permute-start(bf16[512,1024]{1,0:T(8,128)(2,1)S(1)} %get-tuple-element.92), channel_id=1, source_target_pairs={{0,1},{1,0},{2,3},{3,2},{4,5},{5,4},{6,7},{7,6},{8,9},{9,8},{10,11... | collective-permute-start | bytes 3145736 | tf_op jit(solution)/shard_map/ppermute | solution.py:443
  40.3 16.3 %copy-start.3 = (f32[1024]{0:T(1024)S(1)}, f32[1024]{0:T(1024)}, u32[]{:S(2)}) copy-start(f32[1024]{0:T(1024)} %param.14) | copy-start | bytes 12292
  42.9 8.9 %collective-permute-start.16 = (bf16[144,256]{1,0:T(8,128)(2,1)S(1)}, bf16[144,256]{1,0:T(8,128)(2,1)S(1)}, u32[]{:S(2)}, u32[]{:S(2)}) collective-permute-start(bf16[144,256]{1,0:T(8,128)(2,1)S(1)} %get-tuple-element.95), channel_id=1, source_target_pairs={{0,24},{2,26},{4,28},{6,30},{1,25},{3,27},{5,29},{7,31}} | collective-permute-start | bytes 221192 | tf_op jit(solution)/shard_map/ppermute | solution.py:437
  45.7 6.0 %collective-permute-start.15 = (bf16[144,256]{1,0:T(8,128)(2,1)S(1)}, bf16[144,256]{1,0:T(8,128)(2,1)S(1)}, u32[]{:S(2)}, u32[]{:S(2)}) collective-permute-start(bf16[144,256]{1,0:T(8,128)(2,1)S(1)} %get-tuple-element.95), channel_id=1, source_target_pairs={{0,16},{2,18},{4,20},{6,22},{8,24},{10,26},{12,28},{14,30},{1,17},... | collective-permute-start | bytes 221192 | tf_op jit(solution)/shard_map/ppermute | solution.py:437
  48.9 3.3 %collective-permute-start.14 = (bf16[144,256]{1,0:T(8,128)(2,1)S(1)}, bf16[144,256]{1,0:T(8,128)(2,1)S(1)}, u32[]{:S(2)}, u32[]{:S(2)}) collective-permute-start(bf16[144,256]{1,0:T(8,128)(2,1)S(1)} %get-tuple-element.95), channel_id=1, source_target_pairs={{0,8},{2,10},{4,12},{6,14},{8,16},{10,18},{12,20},{14,22},{16,24},... | collective-permute-start | bytes 221192 | tf_op jit(solution)/shard_map/ppermute | solution.py:437
  52.1 16.6 %collective-permute-start.21 = (bf16[256,256]{1,0:T(8,128)(2,1)S(1)}, bf16[256,256]{1,0:T(8,128)(2,1)S(1)}, u32[]{:S(2)}, u32[]{:S(2)}) collective-permute-start(bf16[256,256]{1,0:T(8,128)(2,1)S(1)} %get-tuple-element.115.refs_0_), channel_id=1, source_target_pairs={{0,24},{2,26},{4,28},{6,30},{8,16},{10,18},{12,20},{14,22},{16,8},... | collective-permute-start | bytes 393224 | tf_op jit(solution)/shard_map/ppermute | solution.py:446
  54.9 13.8 %collective-permute-start.20 = (bf16[256,256]{1,0:T(8,128)(2,1)S(1)}, bf16[256,256]{1,0:T(8,128)(2,1)S(1)}, u32[]{:S(2)}, u32[]{:S(2)}) collective-permute-start(bf16[256,256]{1,0:T(8,128)(2,1)S(1)} %get-tuple-element.115.refs_0_), channel_id=1, source_target_pairs={{0,16},{2,18},{4,20},{6,22},{8,24},{10,26},{12,28},{14,30},{16,0},... | collective-permute-start | bytes 393224 | tf_op jit(solution)/shard_map/ppermute | solution.py:446
  56.0 12.8 %collective-permute-start.19 = (bf16[256,256]{1,0:T(8,128)(2,1)S(1)}, bf16[256,256]{1,0:T(8,128)(2,1)S(1)}, u32[]{:S(2)}, u32[]{:S(2)}) collective-permute-start(bf16[256,256]{1,0:T(8,128)(2,1)S(1)} %get-tuple-element.115.refs_0_), channel_id=1, source_target_pairs={{0,8},{2,10},{4,12},{6,14},{8,0},{10,2},{12,4},{14,6},{16,24},{18,... | collective-permute-start | bytes 393224 | tf_op jit(solution)/shard_map/ppermute | solution.py:446
  57.5 9.6 %copy-start.1 = (f32[31,1024]{1,0:T(8,128)S(1)}, f32[31,1024]{1,0:T(8,128)}, u32[]{:S(2)}) copy-start(f32[31,1024]{1,0:T(8,128)} %taps_ref.3) | copy-start | bytes 380932
  58.1 4.8 %collective-permute-start.17 = (bf16[16,256]{1,0:T(8,128)(2,1)S(1)}, bf16[16,256]{1,0:T(8,128)(2,1)S(1)}, u32[]{:S(2)}, u32[]{:S(2)}) collective-permute-start(bf16[16,256]{1,0:T(8,128)(2,1)S(1)} %get-tuple-element.110), channel_id=1, source_target_pairs={{0,8},{2,10},{4,12},{6,14},{8,16},{10,18},{12,20},{14,22},{16,24},... | collective-permute-start | bytes 24584 | tf_op jit(solution)/shard_map/ppermute | solution.py:437
  61.5 5.5 %collective-permute-start.18 = (bf16[16,256]{1,0:T(8,128)(2,1)S(1)}, bf16[16,256]{1,0:T(8,128)(2,1)S(1)}, u32[]{:S(2)}, u32[]{:S(2)}) collective-permute-start(bf16[16,256]{1,0:T(8,128)(2,1)S(1)} %get-tuple-element.111), channel_id=1, source_target_pairs={{8,0},{10,2},{12,4},{14,6},{16,8},{18,10},{20,12},{22,14},{24,16},... | collective-permute-start | bytes 24584 | tf_op jit(solution)/shard_map/ppermute | solution.py:440
  68.8 5.2 %collective-permute-start.23 = (bf16[512,256]{1,0:T(8,128)(2,1)S(1)}, bf16[512,256]{1,0:T(8,128)(2,1)S(1)}, u32[]{:S(2)}, u32[]{:S(2)}) collective-permute-start(bf16[512,256]{1,0:T(8,128)(2,1)S(1)} %get-tuple-element.120), channel_id=1, source_target_pairs={{0,1},{1,0},{2,3},{3,2},{4,5},{5,4},{6,7},{7,6},{8,9},{9,8},{10,11... | collective-permute-start | bytes 786440 | tf_op jit(solution)/shard_map/ppermute | solution.py:443
  68.9 5.2 %collective-permute-start.22 = (bf16[256,256]{1,0:T(8,128)(2,1)S(1)}, bf16[256,256]{1,0:T(8,128)(2,1)S(1)}, u32[]{:S(2)}, u32[]{:S(2)}) collective-permute-start(bf16[256,256]{1,0:T(8,128)(2,1)S(1)} %shard_map.100.refs_0_), channel_id=1, source_target_pairs={{0,1},{1,0},{2,3},{3,2},{4,5},{5,4},{6,7},{7,6},{8,9},{9,8},{10,11... | collective-permute-start | bytes 393224 | tf_op jit(solution)/shard_map/ppermute | solution.py:443
  74.4 2.6 %collective-permute-start.24 = (bf16[768,256]{1,0:T(8,128)(2,1)S(1)}, bf16[768,256]{1,0:T(8,128)(2,1)S(1)}, u32[]{:S(2)}, u32[]{:S(2)}) collective-permute-start(bf16[768,256]{1,0:T(8,128)(2,1)S(1)} %shard_map.101.refs_0_), channel_id=1, source_target_pairs={{0,1},{1,0},{2,3},{3,2},{4,5},{5,4},{6,7},{7,6},{8,9},{9,8},{10,11... | collective-permute-start | bytes 1179656 | tf_op jit(solution)/shard_map/ppermute | solution.py:443
  74.6 10.0 %collective-permute-start.25 = (bf16[256,512]{1,0:T(8,128)(2,1)S(1)}, bf16[256,512]{1,0:T(8,128)(2,1)S(1)}, u32[]{:S(2)}, u32[]{:S(2)}) collective-permute-start(bf16[256,512]{1,0:T(8,128)(2,1)S(1)} %shard_map.103), channel_id=1, source_target_pairs={{0,6},{2,4},{4,2},{6,0},{8,14},{10,12},{12,10},{14,8},{16,22},{18,... | collective-permute-start | bytes 786440 | tf_op jit(solution)/shard_map/ppermute | solution.py:434
  77.6 12.2 %collective-permute-start.26 = (bf16[256,512]{1,0:T(8,128)(2,1)S(1)}, bf16[256,512]{1,0:T(8,128)(2,1)S(1)}, u32[]{:S(2)}, u32[]{:S(2)}) collective-permute-start(bf16[256,512]{1,0:T(8,128)(2,1)S(1)} %get-tuple-element.129), channel_id=1, source_target_pairs={{0,2},{2,0},{4,6},{6,4},{8,10},{10,8},{12,14},{14,12},{16,18},{18,... | collective-permute-start | bytes 786440 | tf_op jit(solution)/shard_map/ppermute | solution.py:434
  78.4 11.5 %collective-permute-start.27 = (bf16[256,512]{1,0:T(8,128)(2,1)S(1)}, bf16[256,512]{1,0:T(8,128)(2,1)S(1)}, u32[]{:S(2)}, u32[]{:S(2)}) collective-permute-start(bf16[256,512]{1,0:T(8,128)(2,1)S(1)} %get-tuple-element.130), channel_id=1, source_target_pairs={{0,4},{2,6},{4,0},{6,2},{8,12},{10,14},{12,8},{14,10},{16,20},{18,... | collective-permute-start | bytes 786440 | tf_op jit(solution)/shard_map/ppermute | solution.py:434

commit v8 on v7

--- a/solution.py
+++ b/solution.py
@@ -449,19 +449,22 @@
     rows = x_weight.shape[0]
     parity = lax.rem(core, 2)
 
-    def along_planes(stack):
+    offsets = (0, 1, 2, 3, 3) if planes == 4 else tuple(range(planes))
+
+    def first_hops(stack):
+        return [stack] + [between_planes(stack, step) for step in range(1, 3 if planes == 4 else planes)]
+
+    def last_hops(pieces, ready):
         if planes != 4:
-            return [stack] + [between_planes(stack, step) for step in range(1, planes)], tuple(range(planes))
+            return pieces, ready
 
         def pairs(chosen):
             return [(a * group + q, b * group + q) for a, b in chosen for q in range(group)]
 
-        second = between_planes(stack, 2)
-        first = between_planes(stack, 1)
-        again, stack_then, first = lax.optimization_barrier((second, stack, first))
-        third = lax.ppermute(again, "tm", pairs([(1, 0), (2, 3)]))
-        middle = lax.ppermute(stack_then, "tm", pairs([(1, 2), (2, 1)]))
-        return [stack, first, second, third, middle], (0, 1, 2, 3, 3)
+        pieces, ready = lax.optimization_barrier((pieces, ready))
+        third = lax.ppermute(pieces[2], "tm", pairs([(1, 0), (2, 3)]))
+        middle = lax.ppermute(pieces[0], "tm", pairs([(1, 2), (2, 1)]))
+        return [*pieces, third, middle], ready
 
     half_count = frame_count // 2
     bc_half, *packed = call(
@@ -486,7 +489,8 @@
         flops=STACK_HINT,
         smem=0,
     )
-    xz_pieces, offsets = along_planes(xz_stack)
+    xz_pieces, _ = last_hops(first_hops(xz_stack), ())
+    out_stack, xz_pieces = lax.optimization_barrier((out_stack, xz_pieces))
     x_columns, z_columns = call(
         functools.partial(assemble_kernel, group, offsets),
         (shape((depth, width), BF16), shape((depth, width), BF16)),
@@ -531,6 +535,7 @@
         [pltpu.VMEM((depth, 2 * state), BF16), pltpu.VMEM((total, width), F32)],
         flops=2 * total * depth * (width + 2 * state),
     )
+    out_pieces, summary = lax.optimization_barrier((first_hops(out_stack), summary))
     summaries = [later(summary, step) for step in range(1, planes)]
     y, carry = call(
         functools.partial(inner_kernel, group, heads),
@@ -546,15 +551,8 @@
         flops=2 * total * depth * width,
         smem=0,
     )
-    silu = call(
-        functools.partial(silu_kernel, group),
-        shape((total, width), F32),
-        [norm_gain[None], frame_rows, z_columns],
-        flops=2 * total * depth * width,
-        smem=0,
-    )
-    out_stack, summaries, y = lax.optimization_barrier((out_stack, summaries, y))
-    out_pieces = [out_stack] + [between_planes(out_stack, step) for step in range(1, planes)]
+    out_pieces, (summaries, y) = last_hops(out_pieces, (summaries, y))
+    silu, out_pieces[3:] = lax.optimization_barrier((silu, out_pieces[3:]))
     gated, top, bottom = call(
         functools.partial(gate_kernel, heads, state),
         (shape((total, width), BF16), shape((EDGE, width), BF16), shape((EDGE, width), BF16)),
@@ -589,7 +587,7 @@
     far_swapped = [across(far_act, step) for step in range(1, cores)]
     far_act, out_pieces = lax.optimization_barrier((far_act, out_pieces))
     out_parts = call(
-        functools.partial(share_kernel, cores, tuple(range(planes)), group),
+        functools.partial(share_kernel, cores, offsets, group),
         tuple(shape((share, width), BF16) for _ in range(cores)),
         out_pieces,
         [pltpu.VMEM((depth, width), BF16)],

time: 90.8 us -> 104 us (1.15)
  starting transfers between devices: 40.4 us -> 49.1 us
  waiting for transfers between devices: 33 us -> 36.8 us
    ppermute x2 -> x4, waiting for transfers between devices: 1.07 us -> 5.18 us  [the longest x2 5.18 us: last_hops(): third = lax.ppermute(pieces[2], 'tm', pairs([(1, 0), (2, 3)]))]
    ppermute x4, starting transfers between devices: 10.7 us -> 14.5 us  [later(): lax.ppermute(array, 'tm', [(i, i + step * group) for i in range(times - s...]
    ppermute x8 -> x7, starting transfers between devices: 12.9 us -> 15.8 us  [between_planes(): lax.ppermute(array, 'tm', [(i, i ^ step * group) for i in range(times)])]
    ppermute x2 -> x4, starting transfers between devices: 1.96 us -> 3.91 us  [the longest x2 2.56 us: last_hops(): third = lax.ppermute(pieces[2], 'tm', pairs([(1, 0), (2, 3)]))]
    ppermute x4, waiting for transfers between devices: 1.5 us -> 0.01 us  [across(): return lax.ppermute(array, 'head', [(i, i ^ step) for i in range(cores)])]
    ppermute x8 -> x7, waiting for transfers between devices: 10.9 us -> 11.4 us  [between_planes(): lax.ppermute(array, 'tm', [(i, i ^ step * group) for i in range(times)])]
  transfers between devices with their start and end apart: 28 -> 29, of which waited for: 13 -> 13; matrix products, arithmetic and copies ran while one was open for 0% -> 0% of each run, Pallas kernels for 11% -> 11%
where the time goes in v8:
time: 104 us; the launch traced here: 103 us
  starting transfers between devices  49.1 us (47%)
  waiting for transfers between devices  36.8 us (35%)
  Pallas kernels  15.5 us (15%)
    ppermute x7, starting transfers between devices, between_planes(): lax.ppermute(array, 'tm', [(i, i ^ step * group) for i in range(times)])  15.8 us
    ppermute x9, waiting for transfers between devices, in_plane(): return lax.ppermute(array, 'tm', [(i, i ^ step) for i in range(times)])  15.6 us
    pallas_call x14, Pallas kernels, call(): pl.pallas_call(kernel, out_shape=out_shape, in_specs=in_specs, out_specs=...  15.5 us
    ppermute x4, starting transfers between devices, later(): lax.ppermute(array, 'tm', [(i, i + step * group) for i in range(times - s...  14.5 us
    ppermute x9, starting transfers between devices, in_plane(): return lax.ppermute(array, 'tm', [(i, i ^ step) for i in range(times)])  12.8 us
    ppermute x7, waiting for transfers between devices, between_planes(): lax.ppermute(array, 'tm', [(i, i ^ step * group) for i in range(times)])  11.4 us
    ppermute x2, waiting for transfers between devices, last_hops(): third = lax.ppermute(pieces[2], 'tm', pairs([(1, 0), (2, 3)]))  5.18 us
    ppermute x1, waiting for transfers between devices, earlier(): lax.ppermute(array, 'tm', [(i + step * group, i) for i in range(times - s...  4.2 us
  transfers between devices with their start and end apart: 29, of which 13 were waited for; matrix products, arithmetic and copies ran while one was open for 0% of the time, Pallas kernels for 11%

profile of v8, /device:TPU:0, one launch (start us, length us, event | category | flops | bytes accessed | tf_op | source)
XLA Modules:
  0.0 103.4 jit_solution(6518891137748412665)
XLA Ops:
  0.0 1.8 %shard_map.91 = (bf16[64,128]{1,0:T(8,128)(2,1)}, bf16[64,768]{1,0:T(8,128)(2,1)}, bf16[64,768]{1,0:T(8,128)(2,1)}, bf16[64,768]{1,0:T(8,128)(2,1)}, bf16[64,768]{1,0:T(8,128)(2,1)}) custom-call(bf16[64,256]{1,0:T(8,128)(2,1)} %bc_ref.1, bf16[64,1024]{1,0:T(8,128)(2,1)} %refs_0_.1, bf16[64,1024]{1,0:T(8,128)(2,1)} %refs_1_.1, bf16[64,1024]{1,0:T(8,128)(2,1)} %bitcast.3), custom_call_target="tpu_custom_call" | custom-call | bytes 835584 | tf_op jit(solution)/shard_map/pallas_call | solution.py:32
  1.8 3.0 %collective-permute-start = (bf16[64,768]{1,0:T(8,128)(2,1)}, bf16[64,768]{1,0:T(8,128)(2,1)S(1)}, u32[]{:S(2)}, u32[]{:S(2)}) collective-permute-start(bf16[64,768]{1,0:T(8,128)(2,1)} %get-tuple-element.85), channel_id=1, source_target_pairs={{0,2},{2,0},{4,6},{6,4},{8,10},{10,8},{12,14},{14,12},{16,18},{18,... | collective-permute-start | bytes 294920 | tf_op jit(solution)/shard_map/ppermute | solution.py:434
  4.8 1.5 %collective-permute-start.1 = (bf16[64,768]{1,0:T(8,128)(2,1)}, bf16[64,768]{1,0:T(8,128)(2,1)S(1)}, u32[]{:S(2)}, u32[]{:S(2)}) collective-permute-start(bf16[64,768]{1,0:T(8,128)(2,1)} %get-tuple-element.86), channel_id=1, source_target_pairs={{0,4},{2,6},{4,0},{6,2},{8,12},{10,14},{12,8},{14,10},{16,20},{18,... | collective-permute-start | bytes 294920 | tf_op jit(solution)/shard_map/ppermute | solution.py:434
  6.4 2.0 %collective-permute-start.3 = (bf16[64,128]{1,0:T(8,128)(2,1)}, bf16[64,128]{1,0:T(8,128)(2,1)S(1)}, u32[]{:S(2)}, u32[]{:S(2)}) collective-permute-start(bf16[64,128]{1,0:T(8,128)(2,1)} %get-tuple-element.89.refs_0_), channel_id=1, source_target_pairs={{0,8},{2,10},{4,12},{6,14},{8,0},{10,2},{12,4},{14,6},{16,24},{18,... | collective-permute-start | bytes 49160 | tf_op jit(solution)/shard_map/ppermute | solution.py:446
  8.4 2.6 %collective-permute-start.4 = (bf16[64,128]{1,0:T(8,128)(2,1)}, bf16[64,128]{1,0:T(8,128)(2,1)S(1)}, u32[]{:S(2)}, u32[]{:S(2)}) collective-permute-start(bf16[64,128]{1,0:T(8,128)(2,1)} %get-tuple-element.89.refs_0_), channel_id=1, source_target_pairs={{0,16},{2,18},{4,20},{6,22},{8,24},{10,26},{12,28},{14,30},{16,0},... | collective-permute-start | bytes 49160 | tf_op jit(solution)/shard_map/ppermute | solution.py:446
  11.0 3.4 %collective-permute-start.5 = (bf16[64,128]{1,0:T(8,128)(2,1)}, bf16[64,128]{1,0:T(8,128)(2,1)S(1)}, u32[]{:S(2)}, u32[]{:S(2)}) collective-permute-start(bf16[64,128]{1,0:T(8,128)(2,1)} %get-tuple-element.89.refs_0_), channel_id=1, source_target_pairs={{0,24},{2,26},{4,28},{6,30},{8,16},{10,18},{12,20},{14,22},{16,8},... | collective-permute-start | bytes 49160 | tf_op jit(solution)/shard_map/ppermute | solution.py:446
  14.4 2.4 %collective-permute-done.5.refs_3_ = bf16[64,128]{1,0:T(8,128)(2,1)S(1)} collective-permute-done((bf16[64,128]{1,0:T(8,128)(2,1)}, bf16[64,128]{1,0:T(8,128)(2,1)S(1)}, u32[]{:S(2)}, u32[]{:S(2)}) %collective-permute-start.5) | collective-permute-done | bytes 16416 | tf_op jit(solution)/shard_map/ppermute | solution.py:446
  16.8 0.9 copy-done.5
  17.7 0.6 collective-permute-start.10
  18.3 3.5 %collective-permute-start.9 = (bf16[256,512]{1,0:T(8,128)(2,1)S(1)}, bf16[256,512]{1,0:T(8,128)(2,1)S(1)}, u32[]{:S(2)}, u32[]{:S(2)}) collective-permute-start(bf16[256,512]{1,0:T(8,128)(2,1)S(1)} %get-tuple-element.107.refs_0_), channel_id=1, source_target_pairs={{0,8},{2,10},{4,12},{6,14},{8,0},{10,2},{12,4},{14,6},{16,24},{18,... | collective-permute-start | bytes 786440 | tf_op jit(solution)/shard_map/ppermute | solution.py:446
  22.0 1.6 %collective-permute-start.6 = (bf16[176,1024]{1,0:T(8,128)(2,1)S(1)}, bf16[176,1024]{1,0:T(8,128)(2,1)S(1)}, u32[]{:S(2)}, u32[]{:S(2)}) collective-permute-start(bf16[176,1024]{1,0:T(8,128)(2,1)S(1)} %get-tuple-element.94), channel_id=1, source_target_pairs={{0,2},{2,0},{4,6},{6,4},{8,10},{10,8},{12,14},{14,12},{16,18},{18,... | collective-permute-start | bytes 1081352 | tf_op jit(solution)/shard_map/ppermute | solution.py:434
  23.6 1.5 %collective-permute-start.7 = (bf16[176,1024]{1,0:T(8,128)(2,1)S(1)}, bf16[176,1024]{1,0:T(8,128)(2,1)S(1)}, u32[]{:S(2)}, u32[]{:S(2)}) collective-permute-start(bf16[176,1024]{1,0:T(8,128)(2,1)S(1)} %get-tuple-element.95), channel_id=1, source_target_pairs={{0,4},{2,6},{4,0},{6,2},{8,12},{10,14},{12,8},{14,10},{16,20},{18,... | collective-permute-start | bytes 1081352 | tf_op jit(solution)/shard_map/ppermute | solution.py:434
  25.1 0.4 collective-permute-start.8
  25.5 4.4 %collective-permute-done.10.refs_2_ = bf16[256,512]{1,0:T(8,128)(2,1)S(1)} collective-permute-done((bf16[256,512]{1,0:T(8,128)(2,1)S(1)}, bf16[256,512]{1,0:T(8,128)(2,1)S(1)}, u32[]{:S(2)}, u32[]{:S(2)}) %collective-permute-start.10) | collective-permute-done | bytes 262176 | tf_op jit(solution)/shard_map/ppermute | solution.py:446
  30.1 1.3 %collective-permute-start.11 = (bf16[256,512]{1,0:T(8,128)(2,1)S(1)}, bf16[256,512]{1,0:T(8,128)(2,1)S(1)}, u32[]{:S(2)}, u32[]{:S(2)}) collective-permute-start(bf16[256,512]{1,0:T(8,128)(2,1)S(1)} %collective-permute-done.10.refs_2_), channel_id=1, source_target_pairs={{8,0},{10,2},{12,4},{14,6},{16,24},{18,26},{20,28},{22,30},{9,1},{... | collective-permute-start | bytes 786440 | tf_op jit(solution)/shard_map/ppermute | solution.py:465
  31.3 0.7 collective-permute-start.12
  32.0 0.5 collective-permute-done.6.refs_1_.refs_0_
  32.6 5.1 %collective-permute-done.7.refs_2_.refs_1_ = bf16[176,1024]{1,0:T(8,128)(2,1)S(1)} collective-permute-done((bf16[176,1024]{1,0:T(8,128)(2,1)S(1)}, bf16[176,1024]{1,0:T(8,128)(2,1)S(1)}, u32[]{:S(2)}, u32[]{:S(2)}) %collective-permute-start.7) | collective-permute-done | bytes 360480 | tf_op jit(solution)/shard_map/ppermute | solution.py:434
  37.6 0.2 shard_map.93
  37.9 1.2 %collective-permute-done.11.refs_3_ = bf16[256,512]{1,0:T(8,128)(2,1)S(1)} collective-permute-done((bf16[256,512]{1,0:T(8,128)(2,1)S(1)}, bf16[256,512]{1,0:T(8,128)(2,1)S(1)}, u32[]{:S(2)}, u32[]{:S(2)}) %collective-permute-start.11) | collective-permute-done | bytes 262176 | tf_op jit(solution)/shard_map/ppermute | solution.py:465
  39.1 3.7 %collective-permute-start.14 = (bf16[256,256]{1,0:T(8,128)(2,1)S(1)}, bf16[256,256]{1,0:T(8,128)(2,1)S(1)}, u32[]{:S(2)}, u32[]{:S(2)}) collective-permute-start(bf16[256,256]{1,0:T(8,128)(2,1)S(1)} %get-tuple-element.146.refs_0_), channel_id=1, source_target_pairs={{0,8},{2,10},{4,12},{6,14},{8,0},{10,2},{12,4},{14,6},{16,24},{18,... | collective-permute-start | bytes 393224 | tf_op jit(solution)/shard_map/ppermute | solution.py:446
  42.9 2.6 %shard_map.96 = (bf16[1024,1024]{1,0:T(8,128)(2,1)S(1)}, bf16[1024,256]{1,0:T(8,128)(2,1)S(1)}, bf16[1024,128]{1,0:T(8,128)(2,1)S(1)}, bf16[1024,128]{1,0:T(8,12...) custom-call(s32[8]{0:T(128)S(1)} %copy-done.4, ...), custom_call_target="tpu_custom_call" | custom-call | flops 1073741824 | bytes 7847968 | tf_op jit(solution)/shard_map/pallas_call | solution.py:32
  45.5 1.6 %collective-permute-done.14.refs_1_ = bf16[256,256]{1,0:T(8,128)(2,1)S(1)} collective-permute-done((bf16[256,256]{1,0:T(8,128)(2,1)S(1)}, bf16[256,256]{1,0:T(8,128)(2,1)S(1)}, u32[]{:S(2)}, u32[]{:S(2)}) %collective-permute-start.14) | collective-permute-done | bytes 131104 | tf_op jit(solution)/shard_map/ppermute | solution.py:446
  47.1 2.9 %collective-permute-done.15.refs_2_ = bf16[256,256]{1,0:T(8,128)(2,1)S(1)} collective-permute-done((bf16[256,256]{1,0:T(8,128)(2,1)S(1)}, bf16[256,256]{1,0:T(8,128)(2,1)S(1)}, u32[]{:S(2)}, u32[]{:S(2)}) %collective-permute-start.15) | collective-permute-done | bytes 131104 | tf_op jit(solution)/shard_map/ppermute | solution.py:446
  50.0 1.3 %collective-permute-start.16 = (bf16[144,256]{1,0:T(8,128)(2,1)S(1)}, bf16[144,256]{1,0:T(8,128)(2,1)S(1)}, u32[]{:S(2)}, u32[]{:S(2)}) collective-permute-start(bf16[144,256]{1,0:T(8,128)(2,1)S(1)} %get-tuple-element.121), channel_id=1, source_target_pairs={{0,8},{2,10},{4,12},{6,14},{8,16},{10,18},{12,20},{14,22},{16,24},... | collective-permute-start | bytes 221192 | tf_op jit(solution)/shard_map/ppermute | solution.py:437
  51.3 4.7 %collective-permute-start.17 = (bf16[144,256]{1,0:T(8,128)(2,1)S(1)}, bf16[144,256]{1,0:T(8,128)(2,1)S(1)}, u32[]{:S(2)}, u32[]{:S(2)}) collective-permute-start(bf16[144,256]{1,0:T(8,128)(2,1)S(1)} %get-tuple-element.121), channel_id=1, source_target_pairs={{0,16},{2,18},{4,20},{6,22},{8,24},{10,26},{12,28},{14,30},{1,17},... | collective-permute-start | bytes 221192 | tf_op jit(solution)/shard_map/ppermute | solution.py:437
  56.0 1.3 %collective-permute-start.18 = (bf16[144,256]{1,0:T(8,128)(2,1)S(1)}, bf16[144,256]{1,0:T(8,128)(2,1)S(1)}, u32[]{:S(2)}, u32[]{:S(2)}) collective-permute-start(bf16[144,256]{1,0:T(8,128)(2,1)S(1)} %get-tuple-element.121), channel_id=1, source_target_pairs={{0,24},{2,26},{4,28},{6,30},{1,25},{3,27},{5,29},{7,31}} | collective-permute-start | bytes 221192 | tf_op jit(solution)/shard_map/ppermute | solution.py:437
  57.3 1.5 %shard_map.97 = (f32[1024,256]{1,0:T(8,128)S(1)}, f32[1024,256]{1,0:T(8,128)S(1)}) custom-call(bf16[1024,256]{1,0:T(8,128)(2,1)S(1)} %get-tuple-element.122.x_ref, bf16[1024,128]{1,0:T(8,128)(2,1)S(1)} %get-tuple-element.123.b_ref, bf16[1024,128]{1,0:T(8,128)(2,1)S(1)} %get-tuple-element.115.c_ref, f32[192,128]{1,0:T(8,128)S(1)} %get-tuple-element.124.rows_ref), custom_call_target="tpu_custom_call" | custom-call | flops 134217728 | bytes 3244032 | tf_op jit(solution)/shard_map/pallas_call | solution.py:32
  58.9 0.4 collective-permute-done.18.refs_2_
  59.3 1.3 %collective-permute-start.19 = (bf16[256,256]{1,0:T(8,128)(2,1)S(1)}, bf16[256,256]{1,0:T(8,128)(2,1)S(1)}, u32[]{:S(2)}, u32[]{:S(2)}) collective-permute-start(bf16[256,256]{1,0:T(8,128)(2,1)S(1)} %collective-permute-done.15.refs_2_), channel_id=1, source_target_pairs={{8,0},{10,2},{12,4},{14,6},{16,24},{18,26},{20,28},{22,30},{9,1},{... | collective-permute-start | bytes 393224 | tf_op jit(solution)/shard_map/ppermute | solution.py:465
  60.6 0.7 collective-permute-start.20
  61.3 0.9 shard_map.98.silu_ref
  62.2 3.9 %collective-permute-done.19.refs_3_ = bf16[256,256]{1,0:T(8,128)(2,1)S(1)} collective-permute-done((bf16[256,256]{1,0:T(8,128)(2,1)S(1)}, bf16[256,256]{1,0:T(8,128)(2,1)S(1)}, u32[]{:S(2)}, u32[]{:S(2)}) %collective-permute-start.19) | collective-permute-done | bytes 131104 | tf_op jit(solution)/shard_map/ppermute | solution.py:465
  66.1 0.6 shard_map.99
  66.8 7.2 %collective-permute-start.21 = (bf16[16,256]{1,0:T(8,128)(2,1)S(1)}, bf16[16,256]{1,0:T(8,128)(2,1)S(1)}, u32[]{:S(2)}, u32[]{:S(2)}) collective-permute-start(bf16[16,256]{1,0:T(8,128)(2,1)S(1)} %get-tuple-element.139), channel_id=1, source_target_pairs={{0,8},{2,10},{4,12},{6,14},{8,16},{10,18},{12,20},{14,22},{16,24},... | collective-permute-start | bytes 24584 | tf_op jit(solution)/shard_map/ppermute | solution.py:437
  74.0 1.3 %collective-permute-start.22 = (bf16[16,256]{1,0:T(8,128)(2,1)S(1)}, bf16[16,256]{1,0:T(8,128)(2,1)S(1)}, u32[]{:S(2)}, u32[]{:S(2)}) collective-permute-start(bf16[16,256]{1,0:T(8,128)(2,1)S(1)} %get-tuple-element.140), channel_id=1, source_target_pairs={{8,0},{10,2},{12,4},{14,6},{16,8},{18,10},{20,12},{22,14},{24,16},... | collective-permute-start | bytes 24584 | tf_op jit(solution)/shard_map/ppermute | solution.py:440
  75.4 4.2 %collective-permute-done.22.after_ref = bf16[16,256]{1,0:T(8,128)(2,1)S(1)} collective-permute-done((bf16[16,256]{1,0:T(8,128)(2,1)S(1)}, bf16[16,256]{1,0:T(8,128)(2,1)S(1)}, u32[]{:S(2)}, u32[]{:S(2)}) %collective-permute-start.22) | collective-permute-done | bytes 8224 | tf_op jit(solution)/shard_map/ppermute | solution.py:440
  79.6 1.6 %shard_map.100.refs_0_ = bf16[256,256]{1,0:T(8,128)(2,1)S(1)} custom-call(s32[8]{0:T(128)S(1)} %copy-done.4, f32[31,1024]{1,0:T(8,128)S(1)} %copy-done.1, bf16[1024,256]{1,0:T(8,128)(2,1)S(1)} %get-tuple-element.145.gated_ref, bf16[16,256]{1,0:T(8,128)(2,1)S(1)} %collective-permute-done.21.before_ref, bf16[16,256]{1,0:T(8,128)(2,1)S(1)} %collective-permute-done.22.after_ref), custom_call_target="tpu_custom_call" | custom-call | flops 4063232 | bytes 798752 | tf_op jit(solution)/shard_map/pallas_call | solution.py:32
  81.4 0.5 collective-permute-start.23
  81.9 4.9 %shard_map.101.refs_0_ = bf16[768,256]{1,0:T(8,128)(2,1)S(1)} custom-call(s32[8]{0:T(128)S(1)} %copy-done.4, f32[31,1024]{1,0:T(8,128)S(1)} %copy-done.1, bf16[1024,256]{1,0:T(8,128)(2,1)S(1)} %get-tuple-element.145.gated_ref, bf16[16,256]{1,0:T(8,128)(2,1)S(1)} %collective-permute-done.21.before_ref, bf16[16,256]{1,0:T(8,128)(2,1)S(1)} %collective-permute-done.22.after_ref), custom_call_target="tpu_custom_call" | custom-call | flops 12189696 | bytes 1060896 | tf_op jit(solution)/shard_map/pallas_call | solution.py:32
  86.8 0.3 shard_map.103
  87.3 2.4 %collective-permute-start.26 = (bf16[256,512]{1,0:T(8,128)(2,1)S(1)}, bf16[256,512]{1,0:T(8,128)(2,1)S(1)}, u32[]{:S(2)}, u32[]{:S(2)}) collective-permute-start(bf16[256,512]{1,0:T(8,128)(2,1)S(1)} %shard_map.103), channel_id=1, source_target_pairs={{0,6},{2,4},{4,2},{6,0},{8,14},{10,12},{12,10},{14,8},{16,22},{18,... | collective-permute-start | bytes 786440 | tf_op jit(solution)/shard_map/ppermute | solution.py:434
  89.7 0.6 shard_map.104
  90.3 0.8 collective-permute-start.27
  91.1 1.5 %collective-permute-start.28 = (bf16[256,512]{1,0:T(8,128)(2,1)S(1)}, bf16[256,512]{1,0:T(8,128)(2,1)S(1)}, u32[]{:S(2)}, u32[]{:S(2)}) collective-permute-start(bf16[256,512]{1,0:T(8,128)(2,1)S(1)} %get-tuple-element.162), channel_id=1, source_target_pairs={{0,4},{2,6},{4,0},{6,2},{8,12},{10,14},{12,8},{14,10},{16,20},{18,... | collective-permute-start | bytes 786440 | tf_op jit(solution)/shard_map/ppermute | solution.py:434
  92.6 4.7 %collective-permute-done.26 = bf16[256,512]{1,0:T(8,128)(2,1)S(1)} collective-permute-done((bf16[256,512]{1,0:T(8,128)(2,1)S(1)}, bf16[256,512]{1,0:T(8,128)(2,1)S(1)}, u32[]{:S(2)}, u32[]{:S(2)}) %collective-permute-start.26) | collective-permute-done | bytes 262176 | tf_op jit(solution)/shard_map/ppermute | solution.py:434
  97.3 5.2 %collective-permute-done.27 = bf16[256,512]{1,0:T(8,128)(2,1)S(1)} collective-permute-done((bf16[256,512]{1,0:T(8,128)(2,1)S(1)}, bf16[256,512]{1,0:T(8,128)(2,1)S(1)}, u32[]{:S(2)}, u32[]{:S(2)}) %collective-permute-start.27) | collective-permute-done | bytes 262176 | tf_op jit(solution)/shard_map/ppermute | solution.py:434
  102.5 0.8 add_convert_fusion
  (41 shorter events, 0.9 us)
Async XLA Ops:
  1.8 14.9 %collective-permute-start = (bf16[64,768]{1,0:T(8,128)(2,1)}, bf16[64,768]{1,0:T(8,128)(2,1)S(1)}, u32[]{:S(2)}, u32[]{:S(2)}) collective-permute-start(bf16[64,768]{1,0:T(8,128)(2,1)} %get-tuple-element.85), channel_id=1, source_target_pairs={{0,2},{2,0},{4,6},{6,4},{8,10},{10,8},{12,14},{14,12},{16,18},{18,... | collective-permute-start | bytes 294920 | tf_op jit(solution)/shard_map/ppermute | solution.py:434
  4.8 11.9 %collective-permute-start.1 = (bf16[64,768]{1,0:T(8,128)(2,1)}, bf16[64,768]{1,0:T(8,128)(2,1)S(1)}, u32[]{:S(2)}, u32[]{:S(2)}) collective-permute-start(bf16[64,768]{1,0:T(8,128)(2,1)} %get-tuple-element.86), channel_id=1, source_target_pairs={{0,4},{2,6},{4,0},{6,2},{8,12},{10,14},{12,8},{14,10},{16,20},{18,... | collective-permute-start | bytes 294920 | tf_op jit(solution)/shard_map/ppermute | solution.py:434
  6.4 10.4 %collective-permute-start.2 = (bf16[64,768]{1,0:T(8,128)(2,1)}, bf16[64,768]{1,0:T(8,128)(2,1)S(1)}, u32[]{:S(2)}, u32[]{:S(2)}) collective-permute-start(bf16[64,768]{1,0:T(8,128)(2,1)} %get-tuple-element.87), channel_id=1, source_target_pairs={{0,6},{2,4},{4,2},{6,0},{8,14},{10,12},{12,10},{14,8},{16,22},{18,... | collective-permute-start | bytes 294920 | tf_op jit(solution)/shard_map/ppermute | solution.py:434
  6.4 4.6 %collective-permute-start.3 = (bf16[64,128]{1,0:T(8,128)(2,1)}, bf16[64,128]{1,0:T(8,128)(2,1)S(1)}, u32[]{:S(2)}, u32[]{:S(2)}) collective-permute-start(bf16[64,128]{1,0:T(8,128)(2,1)} %get-tuple-element.89.refs_0_), channel_id=1, source_target_pairs={{0,8},{2,10},{4,12},{6,14},{8,0},{10,2},{12,4},{14,6},{16,24},{18,... | collective-permute-start | bytes 49160 | tf_op jit(solution)/shard_map/ppermute | solution.py:446
  8.4 6.0 %collective-permute-start.4 = (bf16[64,128]{1,0:T(8,128)(2,1)}, bf16[64,128]{1,0:T(8,128)(2,1)S(1)}, u32[]{:S(2)}, u32[]{:S(2)}) collective-permute-start(bf16[64,128]{1,0:T(8,128)(2,1)} %get-tuple-element.89.refs_0_), channel_id=1, source_target_pairs={{0,16},{2,18},{4,20},{6,22},{8,24},{10,26},{12,28},{14,30},{16,0},... | collective-permute-start | bytes 49160 | tf_op jit(solution)/shard_map/ppermute | solution.py:446
  11.0 5.7 %collective-permute-start.5 = (bf16[64,128]{1,0:T(8,128)(2,1)}, bf16[64,128]{1,0:T(8,128)(2,1)S(1)}, u32[]{:S(2)}, u32[]{:S(2)}) collective-permute-start(bf16[64,128]{1,0:T(8,128)(2,1)} %get-tuple-element.89.refs_0_), channel_id=1, source_target_pairs={{0,24},{2,26},{4,28},{6,30},{8,16},{10,18},{12,20},{14,22},{16,8},... | collective-permute-start | bytes 49160 | tf_op jit(solution)/shard_map/ppermute | solution.py:446
  16.8 0.9 copy-start.5
  17.7 4.2 %copy-start.6 = (f32[16,256]{1,0:T(8,128)S(1)}, f32[16,256]{1,0:T(8,128)}, u32[]{:S(2)}) copy-start(f32[16,256]{1,0:T(8,128)} %param.13) | copy-start | bytes 49156
  17.7 4.2 %copy-start = (bf16[256,1024]{1,0:T(8,128)(2,1)S(1)}, bf16[256,1024]{1,0:T(8,128)(2,1)}, u32[]{:S(2)}) copy-start(bf16[256,1024]{1,0:T(8,128)(2,1)} %own_ref.1) | copy-start | bytes 1572868
  17.7 4.2 %copy-start.2 = (bf16[64,128]{1,0:T(8,128)(2,1)S(1)}, bf16[64,128]{1,0:T(8,128)(2,1)}, u32[]{:S(2)}) copy-start(bf16[64,128]{1,0:T(8,128)(2,1)} %get-tuple-element.89.refs_0_) | copy-start | bytes 49156
  17.7 12.2 %collective-permute-start.10 = (bf16[256,512]{1,0:T(8,128)(2,1)S(1)}, bf16[256,512]{1,0:T(8,128)(2,1)S(1)}, u32[]{:S(2)}, u32[]{:S(2)}) collective-permute-start(bf16[256,512]{1,0:T(8,128)(2,1)S(1)} %get-tuple-element.107.refs_0_), channel_id=1, source_target_pairs={{0,16},{2,18},{4,20},{6,22},{8,24},{10,26},{12,28},{14,30},{16,0},... | collective-permute-start | bytes 786440 | tf_op jit(solution)/shard_map/ppermute | solution.py:446
  18.3 11.7 %collective-permute-start.9 = (bf16[256,512]{1,0:T(8,128)(2,1)S(1)}, bf16[256,512]{1,0:T(8,128)(2,1)S(1)}, u32[]{:S(2)}, u32[]{:S(2)}) collective-permute-start(bf16[256,512]{1,0:T(8,128)(2,1)S(1)} %get-tuple-element.107.refs_0_), channel_id=1, source_target_pairs={{0,8},{2,10},{4,12},{6,14},{8,0},{10,2},{12,4},{14,6},{16,24},{18,... | collective-permute-start | bytes 786440 | tf_op jit(solution)/shard_map/ppermute | solution.py:446
  22.0 10.6 %collective-permute-start.6 = (bf16[176,1024]{1,0:T(8,128)(2,1)S(1)}, bf16[176,1024]{1,0:T(8,128)(2,1)S(1)}, u32[]{:S(2)}, u32[]{:S(2)}) collective-permute-start(bf16[176,1024]{1,0:T(8,128)(2,1)S(1)} %get-tuple-element.94), channel_id=1, source_target_pairs={{0,2},{2,0},{4,6},{6,4},{8,10},{10,8},{12,14},{14,12},{16,18},{18,... | collective-permute-start | bytes 1081352 | tf_op jit(solution)/shard_map/ppermute | solution.py:434
  23.6 14.0 %collective-permute-start.7 = (bf16[176,1024]{1,0:T(8,128)(2,1)S(1)}, bf16[176,1024]{1,0:T(8,128)(2,1)S(1)}, u32[]{:S(2)}, u32[]{:S(2)}) collective-permute-start(bf16[176,1024]{1,0:T(8,128)(2,1)S(1)} %get-tuple-element.95), channel_id=1, source_target_pairs={{0,4},{2,6},{4,0},{6,2},{8,12},{10,14},{12,8},{14,10},{16,20},{18,... | collective-permute-start | bytes 1081352 | tf_op jit(solution)/shard_map/ppermute | solution.py:434
  25.1 12.5 %collective-permute-start.8 = (bf16[176,1024]{1,0:T(8,128)(2,1)S(1)}, bf16[176,1024]{1,0:T(8,128)(2,1)S(1)}, u32[]{:S(2)}, u32[]{:S(2)}) collective-permute-start(bf16[176,1024]{1,0:T(8,128)(2,1)S(1)} %get-tuple-element.96), channel_id=1, source_target_pairs={{0,6},{2,4},{4,2},{6,0},{8,14},{10,12},{12,10},{14,8},{16,22},{18,... | collective-permute-start | bytes 1081352 | tf_op jit(solution)/shard_map/ppermute | solution.py:434
  30.1 9.1 %collective-permute-start.11 = (bf16[256,512]{1,0:T(8,128)(2,1)S(1)}, bf16[256,512]{1,0:T(8,128)(2,1)S(1)}, u32[]{:S(2)}, u32[]{:S(2)}) collective-permute-start(bf16[256,512]{1,0:T(8,128)(2,1)S(1)} %collective-permute-done.10.refs_2_), channel_id=1, source_target_pairs={{8,0},{10,2},{12,4},{14,6},{16,24},{18,26},{20,28},{22,30},{9,1},{... | collective-permute-start | bytes 786440 | tf_op jit(solution)/shard_map/ppermute | solution.py:465
  31.3 7.8 %collective-permute-start.12 = (bf16[256,512]{1,0:T(8,128)(2,1)S(1)}, bf16[256,512]{1,0:T(8,128)(2,1)S(1)}, u32[]{:S(2)}, u32[]{:S(2)}) collective-permute-start(bf16[256,512]{1,0:T(8,128)(2,1)S(1)} %get-tuple-element.107.refs_0_), channel_id=1, source_target_pairs={{8,16},{10,18},{12,20},{14,22},{16,8},{18,10},{20,12},{22,14},{9,1... | collective-permute-start | bytes 786440 | tf_op jit(solution)/shard_map/ppermute | solution.py:466
  37.8 5.1 %collective-permute-start.13 = (bf16[512,1024]{1,0:T(8,128)(2,1)S(1)}, bf16[512,1024]{1,0:T(8,128)(2,1)S(1)}, u32[]{:S(2)}, u32[]{:S(2)}) collective-permute-start(bf16[512,1024]{1,0:T(8,128)(2,1)S(1)} %get-tuple-element.114), channel_id=1, source_target_pairs={{0,1},{1,0},{2,3},{3,2},{4,5},{5,4},{6,7},{7,6},{8,9},{9,8},{10,11... | collective-permute-start | bytes 3145736 | tf_op jit(solution)/shard_map/ppermute | solution.py:443
  39.1 3.8 %copy-start.4 = (s32[8]{0:T(128)S(1)}, s32[8]{0:T(128)}, u32[]{:S(2)}) copy-start(s32[8]{0:T(128)} %len_ref.5) | copy-start | bytes 100
  39.1 8.0 %collective-permute-start.14 = (bf16[256,256]{1,0:T(8,128)(2,1)S(1)}, bf16[256,256]{1,0:T(8,128)(2,1)S(1)}, u32[]{:S(2)}, u32[]{:S(2)}) collective-permute-start(bf16[256,256]{1,0:T(8,128)(2,1)S(1)} %get-tuple-element.146.refs_0_), channel_id=1, source_target_pairs={{0,8},{2,10},{4,12},{6,14},{8,0},{10,2},{12,4},{14,6},{16,24},{18,... | collective-permute-start | bytes 393224 | tf_op jit(solution)/shard_map/ppermute | solution.py:446
  42.8 7.2 %collective-permute-start.15 = (bf16[256,256]{1,0:T(8,128)(2,1)S(1)}, bf16[256,256]{1,0:T(8,128)(2,1)S(1)}, u32[]{:S(2)}, u32[]{:S(2)}) collective-permute-start(bf16[256,256]{1,0:T(8,128)(2,1)S(1)} %get-tuple-element.146.refs_0_), channel_id=1, source_target_pairs={{0,16},{2,18},{4,20},{6,22},{8,24},{10,26},{12,28},{14,30},{16,0},... | collective-permute-start | bytes 393224 | tf_op jit(solution)/shard_map/ppermute | solution.py:446
  42.9 18.3 %copy-start.3 = (f32[1024]{0:T(1024)S(1)}, f32[1024]{0:T(1024)}, u32[]{:S(2)}) copy-start(f32[1024]{0:T(1024)} %param.14) | copy-start | bytes 12292
  50.0 8.9 %collective-permute-start.16 = (bf16[144,256]{1,0:T(8,128)(2,1)S(1)}, bf16[144,256]{1,0:T(8,128)(2,1)S(1)}, u32[]{:S(2)}, u32[]{:S(2)}) collective-permute-start(bf16[144,256]{1,0:T(8,128)(2,1)S(1)} %get-tuple-element.121), channel_id=1, source_target_pairs={{0,8},{2,10},{4,12},{6,14},{8,16},{10,18},{12,20},{14,22},{16,24},... | collective-permute-start | bytes 221192 | tf_op jit(solution)/shard_map/ppermute | solution.py:437
  51.3 7.6 %collective-permute-start.17 = (bf16[144,256]{1,0:T(8,128)(2,1)S(1)}, bf16[144,256]{1,0:T(8,128)(2,1)S(1)}, u32[]{:S(2)}, u32[]{:S(2)}) collective-permute-start(bf16[144,256]{1,0:T(8,128)(2,1)S(1)} %get-tuple-element.121), channel_id=1, source_target_pairs={{0,16},{2,18},{4,20},{6,22},{8,24},{10,26},{12,28},{14,30},{1,17},... | collective-permute-start | bytes 221192 | tf_op jit(solution)/shard_map/ppermute | solution.py:437
  56.0 3.3 %collective-permute-start.18 = (bf16[144,256]{1,0:T(8,128)(2,1)S(1)}, bf16[144,256]{1,0:T(8,128)(2,1)S(1)}, u32[]{:S(2)}, u32[]{:S(2)}) collective-permute-start(bf16[144,256]{1,0:T(8,128)(2,1)S(1)} %get-tuple-element.121), channel_id=1, source_target_pairs={{0,24},{2,26},{4,28},{6,30},{1,25},{3,27},{5,29},{7,31}} | collective-permute-start | bytes 221192 | tf_op jit(solution)/shard_map/ppermute | solution.py:437
  59.3 6.8 %collective-permute-start.19 = (bf16[256,256]{1,0:T(8,128)(2,1)S(1)}, bf16[256,256]{1,0:T(8,128)(2,1)S(1)}, u32[]{:S(2)}, u32[]{:S(2)}) collective-permute-start(bf16[256,256]{1,0:T(8,128)(2,1)S(1)} %collective-permute-done.15.refs_2_), channel_id=1, source_target_pairs={{8,0},{10,2},{12,4},{14,6},{16,24},{18,26},{20,28},{22,30},{9,1},{... | collective-permute-start | bytes 393224 | tf_op jit(solution)/shard_map/ppermute | solution.py:465
  60.6 5.6 %collective-permute-start.20 = (bf16[256,256]{1,0:T(8,128)(2,1)S(1)}, bf16[256,256]{1,0:T(8,128)(2,1)S(1)}, u32[]{:S(2)}, u32[]{:S(2)}) collective-permute-start(bf16[256,256]{1,0:T(8,128)(2,1)S(1)} %get-tuple-element.146.refs_0_), channel_id=1, source_target_pairs={{8,16},{10,18},{12,20},{14,22},{16,8},{18,10},{20,12},{22,14},{9,1... | collective-permute-start | bytes 393224 | tf_op jit(solution)/shard_map/ppermute | solution.py:466
  66.1 13.4 %copy-start.1 = (f32[31,1024]{1,0:T(8,128)S(1)}, f32[31,1024]{1,0:T(8,128)}, u32[]{:S(2)}) copy-start(f32[31,1024]{1,0:T(8,128)} %taps_ref.3) | copy-start | bytes 380932
  66.8 8.6 %collective-permute-start.21 = (bf16[16,256]{1,0:T(8,128)(2,1)S(1)}, bf16[16,256]{1,0:T(8,128)(2,1)S(1)}, u32[]{:S(2)}, u32[]{:S(2)}) collective-permute-start(bf16[16,256]{1,0:T(8,128)(2,1)S(1)} %get-tuple-element.139), channel_id=1, source_target_pairs={{0,8},{2,10},{4,12},{6,14},{8,16},{10,18},{12,20},{14,22},{16,24},... | collective-permute-start | bytes 24584 | tf_op jit(solution)/shard_map/ppermute | solution.py:437
  74.0 5.5 %collective-permute-start.22 = (bf16[16,256]{1,0:T(8,128)(2,1)S(1)}, bf16[16,256]{1,0:T(8,128)(2,1)S(1)}, u32[]{:S(2)}, u32[]{:S(2)}) collective-permute-start(bf16[16,256]{1,0:T(8,128)(2,1)S(1)} %get-tuple-element.140), channel_id=1, source_target_pairs={{8,0},{10,2},{12,4},{14,6},{16,8},{18,10},{20,12},{22,14},{24,16},... | collective-permute-start | bytes 24584 | tf_op jit(solution)/shard_map/ppermute | solution.py:440
  81.3 5.5 %collective-permute-start.24 = (bf16[512,256]{1,0:T(8,128)(2,1)S(1)}, bf16[512,256]{1,0:T(8,128)(2,1)S(1)}, u32[]{:S(2)}, u32[]{:S(2)}) collective-permute-start(bf16[512,256]{1,0:T(8,128)(2,1)S(1)} %get-tuple-element.152), channel_id=1, source_target_pairs={{0,1},{1,0},{2,3},{3,2},{4,5},{5,4},{6,7},{7,6},{8,9},{9,8},{10,11... | collective-permute-start | bytes 786440 | tf_op jit(solution)/shard_map/ppermute | solution.py:443
  81.4 5.4 %collective-permute-start.23 = (bf16[256,256]{1,0:T(8,128)(2,1)S(1)}, bf16[256,256]{1,0:T(8,128)(2,1)S(1)}, u32[]{:S(2)}, u32[]{:S(2)}) collective-permute-start(bf16[256,256]{1,0:T(8,128)(2,1)S(1)} %shard_map.100.refs_0_), channel_id=1, source_target_pairs={{0,1},{1,0},{2,3},{3,2},{4,5},{5,4},{6,7},{7,6},{8,9},{9,8},{10,11... | collective-permute-start | bytes 393224 | tf_op jit(solution)/shard_map/ppermute | solution.py:443
  87.1 2.6 %collective-permute-start.25 = (bf16[768,256]{1,0:T(8,128)(2,1)S(1)}, bf16[768,256]{1,0:T(8,128)(2,1)S(1)}, u32[]{:S(2)}, u32[]{:S(2)}) collective-permute-start(bf16[768,256]{1,0:T(8,128)(2,1)S(1)} %shard_map.101.refs_0_), channel_id=1, source_target_pairs={{0,1},{1,0},{2,3},{3,2},{4,5},{5,4},{6,7},{7,6},{8,9},{9,8},{10,11... | collective-permute-start | bytes 1179656 | tf_op jit(solution)/shard_map/ppermute | solution.py:443
  87.3 10.0 %collective-permute-start.26 = (bf16[256,512]{1,0:T(8,128)(2,1)S(1)}, bf16[256,512]{1,0:T(8,128)(2,1)S(1)}, u32[]{:S(2)}, u32[]{:S(2)}) collective-permute-start(bf16[256,512]{1,0:T(8,128)(2,1)S(1)} %shard_map.103), channel_id=1, source_target_pairs={{0,6},{2,4},{4,2},{6,0},{8,14},{10,12},{12,10},{14,8},{16,22},{18,... | collective-permute-start | bytes 786440 | tf_op jit(solution)/shard_map/ppermute | solution.py:434
  90.3 12.2 %collective-permute-start.27 = (bf16[256,512]{1,0:T(8,128)(2,1)S(1)}, bf16[256,512]{1,0:T(8,128)(2,1)S(1)}, u32[]{:S(2)}, u32[]{:S(2)}) collective-permute-start(bf16[256,512]{1,0:T(8,128)(2,1)S(1)} %get-tuple-element.161), channel_id=1, source_target_pairs={{0,2},{2,0},{4,6},{6,4},{8,10},{10,8},{12,14},{14,12},{16,18},{18,... | collective-permute-start | bytes 786440 | tf_op jit(solution)/shard_map/ppermute | solution.py:434
  91.1 11.5 %collective-permute-start.28 = (bf16[256,512]{1,0:T(8,128)(2,1)S(1)}, bf16[256,512]{1,0:T(8,128)(2,1)S(1)}, u32[]{:S(2)}, u32[]{:S(2)}) collective-permute-start(bf16[256,512]{1,0:T(8,128)(2,1)S(1)} %get-tuple-element.162), channel_id=1, source_target_pairs={{0,4},{2,6},{4,0},{6,2},{8,12},{10,14},{12,8},{14,10},{16,20},{18,... | collective-permute-start | bytes 786440 | tf_op jit(solution)/shard_map/ppermute | solution.py:434

commit v9 on v7

--- a/solution.py
+++ b/solution.py
@@ -62,13 +62,14 @@
         dest_ref[pl.ds(pl.multiple_of((plane ^ offset) * rows, rows), rows), : value.shape[1]] = value
 
 
-def cut_kernel(group, bc_ref, *refs):
-    weight_refs, refs = refs[:3], refs[3:]
-    bc_half_ref, out_refs, sems = refs[0], refs[1:-1], refs[-1]
+def cut_kernel(group, frames_ref, *refs):
+    weight_refs, refs = refs[:2], refs[2:]
+    half_ref, out_refs, sems = refs[0], refs[1:-1], refs[-1]
     place, _ = plane_place(group)
     parity = lax.rem(lax.axis_index("head"), 2)
     width = weight_refs[0].shape[1] // group
-    copies = [(bc_ref.at[:, pl.ds(pl.multiple_of(parity * LANES, LANES), LANES)], bc_half_ref)]
+    half = half_ref.shape[0]
+    copies = [(frames_ref.at[pl.ds(pl.multiple_of(parity * half, half), half), :], half_ref)]
     for step, out_ref in enumerate(out_refs):
         lanes = pl.ds(pl.multiple_of((place ^ step) * width, LANES), width)
         for number, weight_ref in enumerate(weight_refs):
@@ -103,58 +104,158 @@
         first += width
 
 
-def tiles_below(half, number):
-    return slice(half + number // 8 * 16, half + number // 8 * 16 + 16), slice(number % 8 * LANES, (number % 8 + 1) * LANES)
-
-
-def payload_kernel(group, decay_ref, frames_ref, *refs):
-    bc_refs, out_refs = refs[:-group], refs[-group:]
-    place, _ = plane_place(group)
-    half, rows = frames_ref.shape[0] // 2, bc_refs[0].shape[0]
-    mine = pl.ds(pl.multiple_of(lax.rem(lax.axis_index("head"), 2) * half, half), half)
+def tile(number):
+    return slice(number // 8 * 16, number // 8 * 16 + 16), slice(number % 8 * LANES, (number % 8 + 1) * LANES)
+
+
+def put(out_ref, number, array):
+    for at in range(0, array.shape[0], 16):
+        for lane in range(0, array.shape[1], LANES):
+            out_ref[tile(number)] = array[at : at + 16, lane : lane + LANES]
+            number += 1
+    return number
+
+
+def three_terms(value):
+    terms = []
+    for _ in range(3):
+        term = value.astype(BF16).astype(F32)
+        terms.append(term)
+        value = value - term
+    return terms
+
+
+def outward_kernel(group, planes, out_w_ref, bc_ref, frames_ref, decay_ref, *out_refs):
+    _, plane = plane_place(group)
+    parity = lax.rem(lax.axis_index("head"), 2)
+    frames = frames_ref.shape[0]
+    lane = lax.broadcasted_iota(jnp.int32, (8, LANES), 1)
+    decays = []
+    for first in (0, frames - LANES):
+        rows = [jnp.zeros((8, LANES), F32), jnp.zeros((8, LANES), F32)]
+        for block in range(group):
+            for number, term in enumerate(three_terms(decay_ref[block, :, first : first + LANES])):
+                slot = number * group + block
+                moved = pltpu.roll(term, (slot % 8 * EDGE + (EDGE if first else 0)) % LANES, 1)
+                rows[slot // 8] = jnp.where(lane // EDGE == slot % 8, moved, rows[slot // 8])
+        decays.append(jnp.concatenate(rows, axis=0))
     for step, out_ref in enumerate(out_refs):
-        out_ref[:half, :] = frames_ref[mine, :]
-        tile = 0
-        for bc_ref in bc_refs:
-            for at in range(0, rows, 16):
-                out_ref[tiles_below(half, tile)] = bc_ref[at : at + 16, :]
-                tile += 1
-        left = decay_ref[place ^ step]
-        terms = []
-        for _ in range(3):
-            term = left.astype(BF16).astype(F32)
-            terms.append(term)
-            left = left - term
-        terms.append(jnp.zeros_like(left))
-        terms = jnp.concatenate(terms, axis=0).astype(BF16)
+        number = put(out_ref, 0, out_w_ref[...])
+        number = put(out_ref, number, bc_ref[:, pl.ds(pl.multiple_of(parity * LANES, LANES), LANES)])
+        later = (plane ^ step) > plane
+        edge = pl.multiple_of(jnp.where(later, frames - EDGE, 0), EDGE)
+        number = put(out_ref, number, frames_ref[pl.ds(edge, EDGE), :])
+        put(out_ref, number, jnp.where(later, decays[1], decays[0]).astype(BF16))
+
+
+def inward_kernel(group, rows, channels, decay_ref, *refs):
+    piece_refs, out_refs = refs[:-group], refs[-group:]
+    place, plane = plane_place(group)
+    width = channels // group
+    planes = len(piece_refs)
+    wanted = jnp.clip(jnp.where(place == 0, plane + 1, plane - 1), 0, planes - 1)
+    depth_tiles = out_refs[0].shape[1] // LANES
+    across, down = channels // LANES, rows // 16
+    for step, out_ref in enumerate(out_refs):
+        block = place ^ step
+        number = 0
+        for piece_ref in piece_refs:
+            for at in range(down):
+                for lane in range(width // LANES):
+                    if across == 8:
+                        lanes = pl.ds(pl.multiple_of(block * width + lane * LANES, LANES), LANES)
+                        out_ref[tile(number)] = piece_ref[at * 16 : at * 16 + 16, lanes]
+                    else:
+                        value = piece_ref[tile(at * across + lane)]
+                        for other in range(1, group):
+                            there = piece_ref[tile(at * across + other * (width // LANES) + lane)]
+                            value = jnp.where(block == other, there, value)
+                        out_ref[tile(number)] = value
+                    number += 1
+            for at in range(down):
+                out_ref[tile(number)] = piece_ref[tile(down * across + at)]
+                number += 1
+        for offset, piece_ref in enumerate(piece_refs):
+
+            @pl.when((plane ^ offset) == wanted)
+            def _(piece_ref=piece_ref, number=number):
+                for at in range(depth_tiles + 1):
+                    out_ref[tile(number + at)] = piece_ref[tile(down * (across + 1) + at)]
+
+        number += depth_tiles + 1
+        terms = three_terms(decay_ref[block])
+        terms = jnp.concatenate([*terms, jnp.zeros_like(terms[0])], axis=0).astype(BF16)
         for span in range(terms.shape[1] // SPAN):
-            for at in (0, 16):
-                out_ref[tiles_below(half, tile)] = terms[at : at + 16, span * SPAN : (span + 1) * SPAN]
-                tile += 1
-
-
-def swap_kernel(group, rows, half, *refs):
-    part_refs, (swap_ref, bc_ref, decay_ref) = refs[:group], refs[group:]
+            number = put(out_ref, number, terms[:, span * SPAN : (span + 1) * SPAN])
+
+
+def swap_kernel(group, rows, *refs):
+    part_refs, half_refs = refs[:group], refs[group : 2 * group - 1]
+    swap_ref, bc_ref, halo_ref, decay_ref, own_out_ref, other_out_ref, out_ref, span_ref = refs[2 * group - 1 :]
     place, plane = plane_place(group)
     planes = bc_ref.shape[0] // (group * rows)
-    spans = 2 * half // SPAN
+    width = out_ref.shape[1]
+    count = span_ref.shape[0]
+    spans = count // group
+    down = rows // 16
+    depth_tiles = swap_ref.shape[1] // LANES
+    lane = lax.broadcasted_iota(jnp.int32, (8, LANES), 1)
     for step, part_ref in enumerate(part_refs):
         block = place ^ step
-        tile = 0
+        number = 0
         for offset in range(planes):
             first = ((plane ^ offset) * group + block) * rows
-            for at in range(0, rows, 16):
-                bc_ref[pl.ds(pl.multiple_of(first + at, 16), 16), :] = part_ref[tiles_below(half, tile)]
-                tile += 1
+            for at in range(down):
+                for column in range(width // LANES):
+                    lanes = slice(column * LANES, (column + 1) * LANES)
+                    out_ref[pl.ds(pl.multiple_of(first + at * 16, 16), 16), lanes] = part_ref[tile(number)]
+                    number += 1
+            for at in range(down):
+                bc_ref[pl.ds(pl.multiple_of(first + at * 16, 16), 16), :] = part_ref[tile(number)]
+                number += 1
+        for side, owner in enumerate((group - 1, 0)):
+
+            @pl.when(block == owner)
+            def _(part_ref=part_ref, number=number, side=side):
+                for at in range(depth_tiles):
+                    halo_ref[side * EDGE : (side + 1) * EDGE, at * LANES : (at + 1) * LANES] = part_ref[tile(number + at)]
+                packed = part_ref[tile(number + depth_tiles)].astype(F32)
+                chosen = jnp.zeros((8, LANES), F32)
+                for head_block in range(group):
+                    value = jnp.zeros((8, LANES), F32)
+                    for term in range(3):
+                        slot = term * group + head_block
+                        half = packed[slot // 8 * 8 : slot // 8 * 8 + 8]
+                        value = value + pltpu.roll(half, (LANES - slot % 8 * EDGE) % LANES, 1)
+                    chosen = jnp.where(place == head_block, value, chosen)
+                if side:
+                    last = pltpu.roll(chosen, EDGE, 1)
+                    decay_ref[count * 8 :, :] = jnp.where((lane >= EDGE) & (lane < 2 * EDGE), last, 0.0)
+                else:
+                    decay_ref[:8, :] = jnp.where(lane < EDGE, chosen, 0.0)
+
+        number += depth_tiles + 1
         for span in range(spans):
-            top = part_ref[tiles_below(half, tile)].astype(F32)
-            bottom = part_ref[tiles_below(half, tile + 1)].astype(F32)
-            tile += 2
-            at = pl.multiple_of((block * spans + span) * 8, 8)
-            decay_ref[pl.ds(at, 8), :] = top[:8] + top[8:] + bottom[:8]
-        if step:
-            swap_ref[(step - 1) * half : step * half, :] = part_ref[:half, :]
-    top = (group - 1) * half
+            top = part_ref[tile(number)].astype(F32)
+            bottom = part_ref[tile(number + 1)].astype(F32)
+            number += 2
+            span_ref[block * spans + span] = top[:8] + top[8:] + bottom[:8]
+    for span in range(count):
+        moved = pltpu.roll(span_ref[span], EDGE, 1)
+        here, after = slice(span * 8, span * 8 + 8), slice(span * 8 + 8, span * 8 + 16)
+        decay_ref[here, :] = jnp.where(lane < EDGE, decay_ref[here, :], moved)
+        kept = decay_ref[after, :] if span == count - 1 else jnp.zeros((8, LANES), F32)
+        decay_ref[after, :] = jnp.where(lane < EDGE, moved, kept)
+    core = lax.axis_index("head")
+    share = own_out_ref.shape[0]
+    own_out_ref[...] = out_ref[pl.ds(pl.multiple_of(core * share, share), share), :]
+    for step in range(1, other_out_ref.shape[0] // share + 1):
+        at = pl.ds(pl.multiple_of((core ^ step) * share, share), share)
+        other_out_ref[(step - 1) * share : step * share, :] = out_ref[at, :]
+    half = half_refs[0].shape[0]
+    for number, half_ref in enumerate(half_refs):
+        swap_ref[number * half : (number + 1) * half, :] = half_ref[...]
+    top = len(half_refs) * half
     height = swap_ref.shape[0] - top
     for number in range(bc_ref.shape[0] // height):
         lanes = slice(number * LANES, (number + 1) * LANES)
@@ -172,23 +273,32 @@
     return jnp.concatenate([rows[at : at + 8] for at in range(0, rows.shape[0], 8)], axis=1)
 
 
-def state_kernel(group, heads, state, len_ref, decay_ref, x_weight_ref, bc_half_ref, own_ref, swap_ref, *refs):
+def row_blocks(total, wide):
+    return [slice(at, at + 256) for at in range(0, total, 256)] + [slice(total, wide)]
+
+
+def state_kernel(group, heads, state, len_ref, decay_ref, x_weight_ref, bc_half_ref, own_ref, swap_ref, halo_ref, *refs):
     half_refs, refs = refs[: group - 1], refs[group - 1 :]
     frames_ref, x_ref, b_ref, c_ref, rows_ref, step_ref, keep_ref, send_ref, weight_ref, tail_ref = refs
     place, plane = plane_place(group)
     parity = lax.rem(lax.axis_index("head"), 2)
-    total, width = x_ref.shape
-    frames = total // group
+    width = x_ref.shape[1]
+    frames = own_ref.shape[0]
+    total = frames * group
     half = frames // 2
     head_size = width // heads
     count = total // SPAN
-    base = plane * total
-    frames_ref[pl.ds(pl.multiple_of(place * frames, frames), frames), :] = own_ref[...]
+    base = plane * total - EDGE
+    wide = total + 2 * EDGE
+    frames_ref[:EDGE, :] = halo_ref[:EDGE, :]
+    frames_ref[total + EDGE : wide, :] = halo_ref[EDGE:, :]
+    frames_ref[wide:, :] = jnp.zeros((frames_ref.shape[0] - wide, frames_ref.shape[1]), BF16)
+    frames_ref[pl.ds(pl.multiple_of(EDGE + place * frames, EDGE), frames), :] = own_ref[...]
     for number, half_ref in enumerate(half_refs):
-        block = (place ^ (number + 1)) * frames
-        mine = pl.ds(pl.multiple_of(block + parity * half, half), half)
-        other = pl.ds(pl.multiple_of(block + (1 - parity) * half, half), half)
-        frames_ref[mine, :] = half_ref[:half, :]
+        block = EDGE + (place ^ (number + 1)) * frames
+        mine = pl.ds(pl.multiple_of(block + parity * half, EDGE), half)
+        other = pl.ds(pl.multiple_of(block + (1 - parity) * half, EDGE), half)
+        frames_ref[mine, :] = half_ref[...]
         frames_ref[other, :] = swap_ref[number * half : (number + 1) * half, :]
     mine = pl.ds(pl.multiple_of(parity * LANES, LANES), LANES)
     other = pl.ds(pl.multiple_of((1 - parity) * LANES, LANES), LANES)
@@ -217,14 +327,15 @@
     rows_ref[used : 2 * used, :] = start.astype(F32)
     rows_ref[2 * used :, :] = carried
 
-    for block in range(group):
-        rows = slice(block * frames, (block + 1) * frames)
+    for rows in row_blocks(total, wide):
         x_ref[rows, :] = dot(frames_ref[rows, :], x_weight_ref[...]).astype(BF16)
         product = dot(frames_ref[rows, :], weight_ref[...])
         b_ref[rows, :] = product[:, :state].astype(BF16)
         c_ref[rows, :] = product[:, state:].astype(BF16)
-
-    tail_ref[...] = lanes_of(spans_in_lanes(tail), width, head_size)
+    for ref in (x_ref, b_ref, c_ref):
+        ref[wide:, :] = jnp.zeros((ref.shape[0] - wide, ref.shape[1]), BF16)
+
+    tail_ref[...] = lanes_of(spans_in_lanes(tail[: count * 8]), width, head_size)
     by_span = jnp.zeros((8, SPAN), F32)
     for block in range(count):
         by_span = jnp.where(lane[:8] == block, keep[block * 8 : (block + 1) * 8], by_span)
@@ -248,7 +359,7 @@
     total, width = x_ref.shape
     head_size = width // heads
     count = total // SPAN
-    base = plane * total
+    base = plane * (total - SPAN) - EDGE
     used = rows_ref.shape[0] // 3
     square = (SPAN, SPAN)
     parts = [rows_ref[: 2 * used, :]]
@@ -284,48 +395,40 @@
 
 def silu_kernel(group, gain_ref, frames_ref, weight_ref, out_ref):
     place, _ = plane_place(group)
-    total, width = out_ref.shape
+    rows_all, width = out_ref.shape
+    total = rows_all - SPAN
+    wide = total + 2 * EDGE
     gain = gain_ref[:, pl.ds(pl.multiple_of(place * width, LANES), width)]
-    for block in range(group):
-        rows = slice(block * (total // group), (block + 1) * (total // group))
+    for rows in row_blocks(total, wide):
         z = dot(frames_ref[rows, :], weight_ref[...]).astype(BF16).astype(F32)
         out_ref[rows, :] = z / (1.0 + jnp.exp(-z)) * gain
-
-
-def share_kernel(cores, offsets, group, *refs):
-    pieces, refs = refs[: len(offsets)], refs[len(offsets) :]
-    outs, weight_ref = refs[:cores], refs[cores]
-    _, plane = plane_place(group)
-    core = lax.axis_index("head")
-    fill_planes(plane, weight_ref, pieces, offsets)
-    for step, out_ref in enumerate(outs):
-        rows = out_ref.shape[0]
-        out_ref[...] = weight_ref[pl.ds(pl.multiple_of((core ^ step) * rows, rows), rows), :]
+    out_ref[wide:, :] = jnp.zeros((rows_all - wide, width), F32)
 
 
 def gate_kernel(heads, state, c_ref, y_ref, step_ref, carry_ref, keep_ref, silu_ref, *refs):
-    earlier, (gated_ref, top_ref, bottom_ref) = refs[:-3], refs[-3:]
+    earlier, gated_ref = refs[:-1], refs[-1]
     total, width = y_ref.shape
     head_size = width // heads
+    count = total // SPAN
     entry = jnp.zeros((state, width), F32)
     for summary in reversed(earlier):
         through = summary[state : state + EDGE, :].astype(F32)[:1]
         entry = through * entry + summary[:state, :].astype(F32)
     owner = [lax.broadcasted_iota(jnp.int32, (width, width), dim) // head_size for dim in (0, 1)]
     average = jnp.where(owner[0] == owner[1], 1.0 / head_size, 0.0).astype(BF16)
-    for block in range(total // SPAN):
+    for block in range(count):
         rows = slice(block * SPAN, (block + 1) * SPAN)
         y = y_ref[rows, :] + carry_ref[rows, :] * dot(c_ref[rows, :], entry.astype(BF16))
         square_mean = dot((y * y).astype(BF16), average)
         gated_ref[rows, :] = (y * lax.rsqrt(square_mean + 1e-05) * silu_ref[rows, :]).astype(BF16)
-        entry = keep_ref[block : block + 1, :] * entry + step_ref[block * state : (block + 1) * state, :]
-    top_ref[...] = gated_ref[:EDGE, :]
-    bottom_ref[...] = gated_ref[total - EDGE :, :]
-
-
-def conv_kernel(group, steps, len_ref, taps_ref, gated_ref, before_ref, after_ref, act_ref, ext_ref, ends_ref):
+        if block < count - 1:
+            entry = keep_ref[block : block + 1, :] * entry + step_ref[block * state : (block + 1) * state, :]
+
+
+def conv_kernel(group, steps, len_ref, taps_ref, gated_ref, act_ref, ext_ref, ends_ref):
     place, plane = plane_place(group)
-    total, width = gated_ref.shape
+    rows_all, width = gated_ref.shape
+    total = rows_all - SPAN
     frames = total // group
     taps = taps_ref.shape[0]
     half = (taps - 1) // 2
@@ -338,15 +441,8 @@
     for record in range(records):
         ends_ref[record + 1] = ends_ref[record] + len_ref[record]
     for number, step in enumerate(steps):
-        owner = place ^ step
-        first = pl.multiple_of(owner * frames, frames)
-        top = gated_ref[pl.ds(pl.multiple_of(jnp.maximum(first - EDGE, 0), EDGE), EDGE), :].astype(F32)
-        below = pl.multiple_of(jnp.minimum(first + frames, total - EDGE), EDGE)
-        bottom = gated_ref[pl.ds(below, EDGE), :].astype(F32)
-        at = number * pitch
-        ext_ref[at : at + EDGE, :] = jnp.where(owner == 0, before_ref[...].astype(F32), top)
-        ext_ref[at + EDGE : at + EDGE + frames, :] = gated_ref[pl.ds(first, frames), :].astype(F32)
-        ext_ref[at + EDGE + frames : at + pitch, :] = jnp.where(owner == group - 1, after_ref[...].astype(F32), bottom)
+        first = pl.multiple_of((place ^ step) * frames, frames)
+        ext_ref[number * pitch : (number + 1) * pitch, :] = gated_ref[pl.ds(first, pitch), :].astype(F32)
 
     def record_at(position):
         found = jnp.int32(0)
@@ -436,9 +532,6 @@
     def later(array, step):
         return lax.ppermute(array, "tm", [(i, i + step * group) for i in range(times - step * group)])
 
-    def earlier(array, step):
-        return lax.ppermute(array, "tm", [(i + step * group, i) for i in range(times - step * group)])
-
     def across(array, step):
         return lax.ppermute(array, "head", [(i, i ^ step) for i in range(cores)])
 
@@ -464,24 +557,19 @@
         return [stack, first, second, third, middle], (0, 1, 2, 3, 3)
 
     half_count = frame_count // 2
-    bc_half, *packed = call(
+    frame_half, *packed = call(
         functools.partial(cut_kernel, group),
-        (
-            shape((rows, LANES), BF16),
-            *(shape((rows, 3 * width), BF16) for _ in range(group)),
-        ),
-        [bc_weight, x_weight, z_weight, out_weight.T],
-        [pltpu.SemaphoreType.DMA((1 + 3 * group,))],
-        smem=0,
-        anywhere=4,
+        (shape((half_count, depth), BF16), *(shape((rows, 2 * width), BF16) for _ in range(group))),
+        [frames, x_weight, z_weight],
+        [pltpu.SemaphoreType.DMA((1 + 2 * group,))],
+        smem=0,
+        anywhere=3,
         vmem=ALL_VMEM_BYTES,
     )
     parts = [packed[0]] + [in_plane(packed[step], step) for step in range(1, group)]
-    bc_pieces = [bc_half] + [between_planes(bc_half, step) for step in range(1, planes)]
-    parts, bc_pieces = lax.optimization_barrier((parts, bc_pieces))
-    xz_stack, out_stack = call(
+    (xz_stack,) = call(
         functools.partial(stack_kernel, group),
-        (shape((group * rows, 2 * width), BF16), shape((group * rows, width), BF16)),
+        (shape((group * rows, 2 * width), BF16),),
         parts,
         flops=STACK_HINT,
         smem=0,
@@ -495,83 +583,88 @@
         smem=0,
     )
     decay_blocks = jnp.pad(log_decay.reshape(group, heads, frame_count), ((0, 0), (0, 8 - heads), (0, 0)))
-    tiles = planes * rows // 16 + frame_count // SPAN * 2
-    payloads = call(
-        functools.partial(payload_kernel, group),
-        tuple(shape((half_count + -(-tiles // 8) * 16, depth), BF16) for _ in range(group)),
-        [decay_blocks, frames, *bc_pieces],
-        smem=0,
-    )
-    payloads = [payloads[0]] + [in_plane(payloads[step], step) for step in range(1, group)]
-    swap, bc_mine, decay = call(
-        functools.partial(swap_kernel, group, rows, half_count),
+    down, across_tiles, depth_tiles = rows // 16, channels // LANES, depth // LANES
+    tiles = down * (across_tiles + 1) + depth_tiles + 1
+    outward = call(
+        functools.partial(outward_kernel, group, planes),
+        tuple(shape((-(-tiles // 8) * 16, depth), BF16) for _ in range(planes)),
+        [out_weight.T, bc_weight, frames, decay_blocks],
+        smem=0,
+    )
+    pieces = [outward[0]] + [between_planes(outward[step], step) for step in range(1, planes)]
+    half_parts = [in_plane(frame_half, step) for step in range(1, group)]
+    tiles = planes * down * (width // LANES + 1) + depth_tiles + 1 + frame_count // SPAN * 2
+    inward = call(
+        functools.partial(inward_kernel, group, rows, channels),
+        tuple(shape((-(-tiles // 8) * 16, depth), BF16) for _ in range(group)),
+        [decay_blocks, *pieces],
+        smem=0,
+    )
+    inward = [inward[0]] + [in_plane(inward[step], step) for step in range(1, group)]
+    share = depth // cores
+    swap, bc_mine, halo, decay, *out_parts = call(
+        functools.partial(swap_kernel, group, rows),
         (
             shape(((group - 1) * half_count + LANES, depth), BF16),
             shape((depth, LANES), BF16),
-            shape((count * 8, SPAN), F32),
+            shape((2 * EDGE, depth), BF16),
+            shape((count * 8 + 8, SPAN), F32),
+            shape((share, width), BF16),
+            shape(((cores - 1) * share, width), BF16),
         ),
-        payloads,
+        [*inward, *half_parts],
+        [pltpu.VMEM((depth, width), BF16), pltpu.VMEM((count, 8, SPAN), F32)],
         smem=0,
     )
     swap = across(swap, 1)
+    all_rows = total + SPAN
 
     frame_rows, x_rows, b_rows, c_rows, decay_rows, steps, keep, summary = call(
         functools.partial(state_kernel, group, heads, state),
         (
-            shape((total, depth), BF16),
-            shape((total, width), BF16),
-            shape((total, state), BF16),
-            shape((total, state), BF16),
-            shape((3 * count * 8, SPAN), F32),
+            shape((all_rows, depth), BF16),
+            shape((all_rows, width), BF16),
+            shape((all_rows, state), BF16),
+            shape((all_rows, state), BF16),
+            shape((3 * (count + 1) * 8, SPAN), F32),
             shape((count * state, width), F32),
             shape((-(-count // 8) * 8, width), F32),
             shape((state + EDGE, width), BF16),
         ),
-        [record_lengths, decay, x_columns, bc_mine, frames, swap, *payloads[1:]],
+        [record_lengths, decay, x_columns, bc_mine, frames, swap, halo, *half_parts],
         [pltpu.VMEM((depth, 2 * state), BF16), pltpu.VMEM((total, width), F32)],
         flops=2 * total * depth * (width + 2 * state),
     )
     summaries = [later(summary, step) for step in range(1, planes)]
     y, carry = call(
         functools.partial(inner_kernel, group, heads),
-        (shape((total, width), F32), shape((total, width), F32)),
+        (shape((all_rows, width), F32), shape((all_rows, width), F32)),
         [x_rows, b_rows, c_rows, decay_rows],
         flops=4 * total * SPAN * width,
         smem=0,
     )
     silu = call(
         functools.partial(silu_kernel, group),
-        shape((total, width), F32),
+        shape((all_rows, width), F32),
         [norm_gain[None], frame_rows, z_columns],
         flops=2 * total * depth * width,
         smem=0,
     )
-    silu = call(
-        functools.partial(silu_kernel, group),
-        shape((total, width), F32),
-        [norm_gain[None], frame_rows, z_columns],
-        flops=2 * total * depth * width,
-        smem=0,
-    )
-    out_stack, summaries, y = lax.optimization_barrier((out_stack, summaries, y))
-    out_pieces = [out_stack] + [between_planes(out_stack, step) for step in range(1, planes)]
-    gated, top, bottom = call(
+    gated = call(
         functools.partial(gate_kernel, heads, state),
-        (shape((total, width), BF16), shape((EDGE, width), BF16), shape((EDGE, width), BF16)),
+        shape((all_rows, width), BF16),
         [c_rows, y, steps, carry, keep, silu, *summaries],
         flops=2 * total * state * width,
         smem=0,
     )
-    before, after = later(bottom, 1), earlier(top, 1)
     ends = pltpu.SMEM((record_lengths.shape[0] + 1,), jnp.int32)
-    share = depth // cores
     far, near = (group - 1,), (*range(1, group - 1), 0)
 
     def conv(steps, gated):
         return call(
             functools.partial(conv_kernel, group, steps),
             shape((len(steps) * frame_count, width), BF16),
-            [record_lengths, conv_weight, gated, before, after],
+            [record_lengths, conv_weight, gated],
             [pltpu.VMEM((len(steps) * (frame_count + 2 * EDGE), width), F32), ends],
             flops=2 * len(steps) * frame_count * width * conv_weight.shape[0],
         )
@@ -587,15 +680,10 @@
 
     far_act = conv(far, gated)
     far_swapped = [across(far_act, step) for step in range(1, cores)]
-    far_act, out_pieces = lax.optimization_barrier((far_act, out_pieces))
-    out_parts = call(
-        functools.partial(share_kernel, cores, tuple(range(planes)), group),
-        tuple(shape((share, width), BF16) for _ in range(cores)),
-        out_pieces,
-        [pltpu.VMEM((depth, width), BF16)],
-        smem=0,
-    )
-    out_parts = [out_parts[0]] + [across(out_parts[step], step) for step in range(1, cores)]
+    own_out, other_out = out_parts
+    out_parts = [own_out]
+    for step in range(1, cores):
+        out_parts.append(across(other_out[(step - 1) * share : step * share], step))
     gated, far_act = lax.optimization_barrier((gated, far_act))
     near_act = conv(near, gated)
     near_act, far_swapped, out_parts = lax.optimization_barrier((near_act, far_swapped, out_parts))

time: 90.8 us -> 93.8 us (1.033)
  starting transfers between devices: 40.4 us -> 33.8 us
  waiting for transfers between devices: 33 us -> 38.1 us
  local copies, waits for them, and re-layouts: 0.93 us -> 3.47 us
  Pallas kernels: 15.2 us -> 16.3 us
    ppermute x8 -> x5, waiting for transfers between devices: 10.9 us -> 19.9 us  [between_planes(): lax.ppermute(array, 'tm', [(i, i ^ step * group) for i in range(times)])]
    ppermute x8 -> x5, starting transfers between devices: 12.9 us -> 6.58 us  [between_planes(): lax.ppermute(array, 'tm', [(i, i ^ step * group) for i in range(times)])]
    ppermute x1 -> x0, waiting for transfers between devices: 4.15 us -> none  [earlier(): lax.ppermute(array, 'tm', [(i + step * group, i) for i in range(times - s...]
    ppermute x9 -> x12, starting transfers between devices: 12.8 us -> 15.2 us  [in_plane(): return lax.ppermute(array, 'tm', [(i, i ^ step) for i in range(times)])]
    ppermute x4 -> x3, starting transfers between devices: 10.7 us -> 8.83 us  [later(): lax.ppermute(array, 'tm', [(i, i + step * group) for i in range(times - s...]
    unnamed x14 -> x16, local copies, waits for them, and re-layouts: 0.92 us -> 2.73 us
    ppermute x1 -> x0, starting transfers between devices: 1.29 us -> none  [earlier(): lax.ppermute(array, 'tm', [(i + step * group, i) for i in range(times - s...]
    pallas_call x14, Pallas kernels: 15.2 us -> 16.3 us  [call(): pl.pallas_call(kernel, out_shape=out_shape, in_specs=in_specs, out_specs=...]
  transfers between devices with their start and end apart: 28 -> 26, of which waited for: 13 -> 10; matrix products, arithmetic and copies ran while one was open for 0% -> 1% of each run, Pallas kernels for 11% -> 15%
where the time goes in v9:
time: 93.8 us; the launch traced here: 92.9 us
  waiting for transfers between devices  38.1 us (41%)
  starting transfers between devices  33.8 us (36%)
  Pallas kernels  16.3 us (17%)
  local copies, waits for them, and re-layouts  3.47 us (4%)
    ppermute x5, waiting for transfers between devices, between_planes(): lax.ppermute(array, 'tm', [(i, i ^ step * group) for i in range(times)])  19.9 us
    pallas_call x14, Pallas kernels, call(): pl.pallas_call(kernel, out_shape=out_shape, in_specs=in_specs, out_specs=...  16.3 us
    ppermute x12, waiting for transfers between devices, in_plane(): return lax.ppermute(array, 'tm', [(i, i ^ step) for i in range(times)])  15.4 us
    ppermute x12, starting transfers between devices, in_plane(): return lax.ppermute(array, 'tm', [(i, i ^ step) for i in range(times)])  15.2 us
    ppermute x3, starting transfers between devices, later(): lax.ppermute(array, 'tm', [(i, i + step * group) for i in range(times - s...  8.83 us
    ppermute x5, starting transfers between devices, between_planes(): lax.ppermute(array, 'tm', [(i, i ^ step * group) for i in range(times)])  6.58 us
    unnamed x16, local copies, waits for them, and re-layouts  2.73 us
    ppermute x4, waiting for transfers between devices, across(): return lax.ppermute(array, 'head', [(i, i ^ step) for i in range(cores)])  2.49 us
  transfers between devices with their start and end apart: 26, of which 10 were waited for; matrix products, arithmetic and copies ran while one was open for 1% of the time, Pallas kernels for 15%

profile of v9, /device:TPU:0, one launch (start us, length us, event | category | flops | bytes accessed | tf_op | source)
XLA Modules:
  0.0 92.9 jit_solution(5071083226135133245)
XLA Ops:
  0.0 1.9 %shard_map.93 = (bf16[128,1024]{1,0:T(8,128)(2,1)}, bf16[64,512]{1,0:T(8,128)(2,1)}, bf16[64,512]{1,0:T(8,128)(2,1)}, bf16[64,512]{1,0:T(8,128)(2,1)}, bf16[64,512]{1,0:T(8,128)(2,1)}) custom-call(bf16[256,1024]{1,0:T(8,128)(2,1)} %own_ref.1, bf16[64,1024]{1,0:T(8,128)(2,1)} %refs_0_.1, bf16[64,1024]{1,0:T(8,128)(2,1)} %refs_1_.1), custom_call_target="tpu_custom_call" | custom-call | bytes 1310720 | tf_op jit(solution)/shard_map/pallas_call | solution.py:32
  1.9 3.0 %collective-permute-start.9 = (bf16[64,512]{1,0:T(8,128)(2,1)}, bf16[64,512]{1,0:T(8,128)(2,1)S(1)}, u32[]{:S(2)}, u32[]{:S(2)}) collective-permute-start(bf16[64,512]{1,0:T(8,128)(2,1)} %get-tuple-element.61), channel_id=1, source_target_pairs={{0,2},{2,0},{4,6},{6,4},{8,10},{10,8},{12,14},{14,12},{16,18},{18,... | collective-permute-start | bytes 196616 | tf_op jit(solution)/shard_map/ppermute | solution.py:530
  4.9 1.5 %collective-permute-start.10 = (bf16[64,512]{1,0:T(8,128)(2,1)}, bf16[64,512]{1,0:T(8,128)(2,1)S(1)}, u32[]{:S(2)}, u32[]{:S(2)}) collective-permute-start(bf16[64,512]{1,0:T(8,128)(2,1)} %get-tuple-element.62), channel_id=1, source_target_pairs={{0,4},{2,6},{4,0},{6,2},{8,12},{10,14},{12,8},{14,10},{16,20},{18,... | collective-permute-start | bytes 196616 | tf_op jit(solution)/shard_map/ppermute | solution.py:530
  6.4 2.9 %collective-permute-start.8 = (bf16[128,1024]{1,0:T(8,128)(2,1)}, bf16[128,1024]{1,0:T(8,128)(2,1)S(1)}, u32[]{:S(2)}, u32[]{:S(2)}) collective-permute-start(bf16[128,1024]{1,0:T(8,128)(2,1)} %get-tuple-element.58), channel_id=1, source_target_pairs={{0,6},{2,4},{4,2},{6,0},{8,14},{10,12},{12,10},{14,8},{16,22},{18,... | collective-permute-start | bytes 786440 | tf_op jit(solution)/shard_map/ppermute | solution.py:530
  9.3 0.7 reshape.3
  10.1 0.9 copy-done.2
  11.0 0.8 copy-done.3
  11.9 1.6 %collective-permute-start = (bf16[96,1024]{1,0:T(8,128)(2,1)S(1)}, bf16[96,1024]{1,0:T(8,128)(2,1)S(1)}, u32[]{:S(2)}, u32[]{:S(2)}) collective-permute-start(bf16[96,1024]{1,0:T(8,128)(2,1)S(1)} %get-tuple-element.51), channel_id=1, source_target_pairs={{0,8},{2,10},{4,12},{6,14},{8,0},{10,2},{12,4},{14,6},{16,24},{18,... | collective-permute-start | bytes 589832 | tf_op jit(solution)/shard_map/ppermute | solution.py:539
  13.5 2.6 %collective-permute-start.1 = (bf16[96,1024]{1,0:T(8,128)(2,1)S(1)}, bf16[96,1024]{1,0:T(8,128)(2,1)S(1)}, u32[]{:S(2)}, u32[]{:S(2)}) collective-permute-start(bf16[96,1024]{1,0:T(8,128)(2,1)S(1)} %get-tuple-element.52), channel_id=1, source_target_pairs={{0,16},{2,18},{4,20},{6,22},{8,24},{10,26},{12,28},{14,30},{16,0},... | collective-permute-start | bytes 589832 | tf_op jit(solution)/shard_map/ppermute | solution.py:539
  16.1 0.2 collective-permute-start.2
  16.3 0.8 copy-done.6
  17.2 0.7 collective-permute-start.13
  17.9 5.2 %collective-permute-done.refs_1_ = bf16[96,1024]{1,0:T(8,128)(2,1)S(1)} collective-permute-done((bf16[96,1024]{1,0:T(8,128)(2,1)S(1)}, bf16[96,1024]{1,0:T(8,128)(2,1)S(1)}, u32[]{:S(2)}, u32[]{:S(2)}) %collective-permute-start) | collective-permute-done | bytes 196640 | tf_op jit(solution)/shard_map/ppermute | solution.py:539
  23.1 1.4 %collective-permute-start.12 = (bf16[256,512]{1,0:T(8,128)(2,1)S(1)}, bf16[256,512]{1,0:T(8,128)(2,1)S(1)}, u32[]{:S(2)}, u32[]{:S(2)}) collective-permute-start(bf16[256,512]{1,0:T(8,128)(2,1)S(1)} %shard_map.95.refs_0_), channel_id=1, source_target_pairs={{0,16},{2,18},{4,20},{6,22},{8,24},{10,26},{12,28},{14,30},{16,0},... | collective-permute-start | bytes 786440 | tf_op jit(solution)/shard_map/ppermute | solution.py:539
  24.5 5.8 %collective-permute-done.1.refs_2_ = bf16[96,1024]{1,0:T(8,128)(2,1)S(1)} collective-permute-done((bf16[96,1024]{1,0:T(8,128)(2,1)S(1)}, bf16[96,1024]{1,0:T(8,128)(2,1)S(1)}, u32[]{:S(2)}, u32[]{:S(2)}) %collective-permute-start.1) | collective-permute-done | bytes 196640 | tf_op jit(solution)/shard_map/ppermute | solution.py:539
  30.3 0.5 collective-permute-start.7
  30.8 0.5 collective-permute-start.6
  31.5 1.6 %collective-permute-start.3 = (bf16[128,1024]{1,0:T(8,128)(2,1)S(1)}, bf16[128,1024]{1,0:T(8,128)(2,1)S(1)}, u32[]{:S(2)}, u32[]{:S(2)}) collective-permute-start(bf16[128,1024]{1,0:T(8,128)(2,1)S(1)} %get-tuple-element.55), channel_id=1, source_target_pairs={{0,2},{2,0},{4,6},{6,4},{8,10},{10,8},{12,14},{14,12},{16,18},{18,... | collective-permute-start | bytes 786440 | tf_op jit(solution)/shard_map/ppermute | solution.py:530
  33.1 1.5 %collective-permute-start.4 = (bf16[128,1024]{1,0:T(8,128)(2,1)S(1)}, bf16[128,1024]{1,0:T(8,128)(2,1)S(1)}, u32[]{:S(2)}, u32[]{:S(2)}) collective-permute-start(bf16[128,1024]{1,0:T(8,128)(2,1)S(1)} %get-tuple-element.56), channel_id=1, source_target_pairs={{0,4},{2,6},{4,0},{6,2},{8,12},{10,14},{12,8},{14,10},{16,20},{18,... | collective-permute-start | bytes 786440 | tf_op jit(solution)/shard_map/ppermute | solution.py:530
  34.6 8.9 %collective-permute-done.12.refs_2_ = bf16[256,512]{1,0:T(8,128)(2,1)S(1)} collective-permute-done((bf16[256,512]{1,0:T(8,128)(2,1)S(1)}, bf16[256,512]{1,0:T(8,128)(2,1)S(1)}, u32[]{:S(2)}, u32[]{:S(2)}) %collective-permute-start.12) | collective-permute-done | bytes 262176 | tf_op jit(solution)/shard_map/ppermute | solution.py:539
  43.6 0.5 collective-permute-start.5
  44.0 1.3 %collective-permute-start.14 = (bf16[256,512]{1,0:T(8,128)(2,1)S(1)}, bf16[256,512]{1,0:T(8,128)(2,1)S(1)}, u32[]{:S(2)}, u32[]{:S(2)}) collective-permute-start(bf16[256,512]{1,0:T(8,128)(2,1)S(1)} %collective-permute-done.12.refs_2_), channel_id=1, source_target_pairs={{8,0},{10,2},{12,4},{14,6},{16,24},{18,26},{20,28},{22,30},{9,1},{... | collective-permute-start | bytes 786440 | tf_op jit(solution)/shard_map/ppermute | solution.py:555
  45.3 0.7 collective-permute-start.15
  46.1 4.8 %collective-permute-done.5.refs_3_ = bf16[128,1024]{1,0:T(8,128)(2,1)S(1)} collective-permute-done((bf16[128,1024]{1,0:T(8,128)(2,1)S(1)}, bf16[128,1024]{1,0:T(8,128)(2,1)S(1)}, u32[]{:S(2)}, u32[]{:S(2)}) %collective-permute-start.5) | collective-permute-done | bytes 262176 | tf_op jit(solution)/shard_map/ppermute | solution.py:530
  50.8 0.6 shard_map.94
  51.5 0.5 collective-permute-start.16
  52.0 0.3 collective-permute-done.14.refs_3_
  52.4 2.1 %collective-permute-done.16.swap_ref = bf16[512,1024]{1,0:T(8,128)(2,1)S(1)} collective-permute-done((bf16[512,1024]{1,0:T(8,128)(2,1)S(1)}, bf16[512,1024]{1,0:T(8,128)(2,1)S(1)}, u32[]{:S(2)}, u32[]{:S(2)}) %collective-permute-start.16) | collective-permute-done | bytes 1048608 | tf_op jit(solution)/shard_map/ppermute | solution.py:536
  54.5 2.8 %shard_map.97 = (bf16[1152,1024]{1,0:T(8,128)(2,1)S(1)}, bf16[1152,256]{1,0:T(8,128)(2,1)S(1)}, bf16[1152,128]{1,0:T(8,128)(2,1)S(1)}, bf16[1152,128]{1,0:T(8,12...) custom-call(s32[8]{0:T(128)S(1)} %copy-done.5, ...), custom_call_target="tpu_custom_call" | custom-call | flops 1073741824 | bytes 8028192 | tf_op jit(solution)/shard_map/pallas_call | solution.py:32
  57.3 4.6 %collective-permute-start.19 = (bf16[144,256]{1,0:T(8,128)(2,1)S(1)}, bf16[144,256]{1,0:T(8,128)(2,1)S(1)}, u32[]{:S(2)}, u32[]{:S(2)}) collective-permute-start(bf16[144,256]{1,0:T(8,128)(2,1)S(1)} %get-tuple-element.81), channel_id=1, source_target_pairs={{0,24},{2,26},{4,28},{6,30},{1,25},{3,27},{5,29},{7,31}} | collective-permute-start | bytes 221192 | tf_op jit(solution)/shard_map/ppermute | solution.py:533
  61.9 3.0 %collective-permute-start.18 = (bf16[144,256]{1,0:T(8,128)(2,1)S(1)}, bf16[144,256]{1,0:T(8,128)(2,1)S(1)}, u32[]{:S(2)}, u32[]{:S(2)}) collective-permute-start(bf16[144,256]{1,0:T(8,128)(2,1)S(1)} %get-tuple-element.81), channel_id=1, source_target_pairs={{0,16},{2,18},{4,20},{6,22},{8,24},{10,26},{12,28},{14,30},{1,17},... | collective-permute-start | bytes 221192 | tf_op jit(solution)/shard_map/ppermute | solution.py:533
  64.9 1.3 %collective-permute-start.17 = (bf16[144,256]{1,0:T(8,128)(2,1)S(1)}, bf16[144,256]{1,0:T(8,128)(2,1)S(1)}, u32[]{:S(2)}, u32[]{:S(2)}) collective-permute-start(bf16[144,256]{1,0:T(8,128)(2,1)S(1)} %get-tuple-element.81), channel_id=1, source_target_pairs={{0,8},{2,10},{4,12},{6,14},{8,16},{10,18},{12,20},{14,22},{16,24},... | collective-permute-start | bytes 221192 | tf_op jit(solution)/shard_map/ppermute | solution.py:533
  66.2 1.9 %shard_map.98 = (f32[1152,256]{1,0:T(8,128)S(1)}, f32[1152,256]{1,0:T(8,128)S(1)}) custom-call(bf16[1152,256]{1,0:T(8,128)(2,1)S(1)} %get-tuple-element.72.x_ref, bf16[1152,128]{1,0:T(8,128)(2,1)S(1)} %get-tuple-element.73.b_ref, bf16[1152,128]{1,0:T(8,128)(2,1)S(1)} %get-tuple-element.71.c_ref, f32[216,128]{1,0:T(8,128)S(1)} %get-tuple-element.74.rows_ref), custom_call_target="tpu_custom_call" | custom-call | flops 134217728 | bytes 3649536 | tf_op jit(solution)/shard_map/pallas_call | solution.py:32
  68.1 0.9 shard_map.99.silu_ref
  69.0 0.7 shard_map.100.gated_ref
  69.9 1.6 %shard_map.101.refs_0_ = bf16[256,256]{1,0:T(8,128)(2,1)S(1)} custom-call(s32[8]{0:T(128)S(1)} %copy-done.5, f32[31,1024]{1,0:T(8,128)S(1)} %copy-done.1, bf16[1152,256]{1,0:T(8,128)(2,1)S(1)} %shard_map.100.gated_ref), custom_call_target="tpu_custom_call" | custom-call | flops 4063232 | bytes 847904 | tf_op jit(solution)/shard_map/pallas_call | solution.py:32
  71.6 4.7 %shard_map.102.refs_0_ = bf16[768,256]{1,0:T(8,128)(2,1)S(1)} custom-call(s32[8]{0:T(128)S(1)} %copy-done.5, f32[31,1024]{1,0:T(8,128)S(1)} %copy-done.1, bf16[1152,256]{1,0:T(8,128)(2,1)S(1)} %shard_map.100.gated_ref), custom_call_target="tpu_custom_call" | custom-call | flops 12189696 | bytes 1110048 | tf_op jit(solution)/shard_map/pallas_call | solution.py:32
  76.3 0.3 shard_map.103
  76.6 0.6 collective-permute-start.22
  77.2 1.0 %collective-permute-start.23 = (bf16[256,512]{1,0:T(8,128)(2,1)S(1)}, bf16[256,512]{1,0:T(8,128)(2,1)S(1)}, u32[]{:S(2)}, u32[]{:S(2)}) collective-permute-start(bf16[256,512]{1,0:T(8,128)(2,1)S(1)} %shard_map.103), channel_id=1, source_target_pairs={{0,6},{2,4},{4,2},{6,0},{8,14},{10,12},{12,10},{14,8},{16,22},{18,... | collective-permute-start | bytes 786440 | tf_op jit(solution)/shard_map/ppermute | solution.py:530
  78.2 0.4 collective-permute-done.22.refs_1_
  78.6 0.6 shard_map.104
  79.2 1.2 %collective-permute-start.24 = (bf16[256,512]{1,0:T(8,128)(2,1)S(1)}, bf16[256,512]{1,0:T(8,128)(2,1)S(1)}, u32[]{:S(2)}, u32[]{:S(2)}) collective-permute-start(bf16[256,512]{1,0:T(8,128)(2,1)S(1)} %get-tuple-element.93), channel_id=1, source_target_pairs={{0,2},{2,0},{4,6},{6,4},{8,10},{10,8},{12,14},{14,12},{16,18},{18,... | collective-permute-start | bytes 786440 | tf_op jit(solution)/shard_map/ppermute | solution.py:530
  80.3 1.0 %collective-permute-start.25 = (bf16[256,512]{1,0:T(8,128)(2,1)S(1)}, bf16[256,512]{1,0:T(8,128)(2,1)S(1)}, u32[]{:S(2)}, u32[]{:S(2)}) collective-permute-start(bf16[256,512]{1,0:T(8,128)(2,1)S(1)} %get-tuple-element.94), channel_id=1, source_target_pairs={{0,4},{2,6},{4,0},{6,2},{8,12},{10,14},{12,8},{14,10},{16,20},{18,... | collective-permute-start | bytes 786440 | tf_op jit(solution)/shard_map/ppermute | solution.py:530
  81.4 5.9 %collective-permute-done.23 = bf16[256,512]{1,0:T(8,128)(2,1)S(1)} collective-permute-done((bf16[256,512]{1,0:T(8,128)(2,1)S(1)}, bf16[256,512]{1,0:T(8,128)(2,1)S(1)}, u32[]{:S(2)}, u32[]{:S(2)}) %collective-permute-start.23) | collective-permute-done | bytes 262176 | tf_op jit(solution)/shard_map/ppermute | solution.py:530
  87.3 4.3 %collective-permute-done.24 = bf16[256,512]{1,0:T(8,128)(2,1)S(1)} collective-permute-done((bf16[256,512]{1,0:T(8,128)(2,1)S(1)}, bf16[256,512]{1,0:T(8,128)(2,1)S(1)}, u32[]{:S(2)}, u32[]{:S(2)}) %collective-permute-start.24) | collective-permute-done | bytes 262176 | tf_op jit(solution)/shard_map/ppermute | solution.py:530
  91.6 0.4 collective-permute-done.25
  92.0 0.8 add_convert_fusion
  (37 shorter events, 0.9 us)
Async XLA Ops:
  0.0 10.1 %copy-start = (bf16[256,1024]{1,0:T(8,128)(2,1)S(1)}, bf16[256,1024]{1,0:T(8,128)(2,1)}, u32[]{:S(2)}) copy-start(bf16[256,1024]{1,0:T(8,128)(2,1)} %own_ref.1) | copy-start | bytes 1572868
  1.9 11.6 %collective-permute-start.9 = (bf16[64,512]{1,0:T(8,128)(2,1)}, bf16[64,512]{1,0:T(8,128)(2,1)S(1)}, u32[]{:S(2)}, u32[]{:S(2)}) collective-permute-start(bf16[64,512]{1,0:T(8,128)(2,1)} %get-tuple-element.61), channel_id=1, source_target_pairs={{0,2},{2,0},{4,6},{6,4},{8,10},{10,8},{12,14},{14,12},{16,18},{18,... | collective-permute-start | bytes 196616 | tf_op jit(solution)/shard_map/ppermute | solution.py:530
  4.9 11.2 %collective-permute-start.10 = (bf16[64,512]{1,0:T(8,128)(2,1)}, bf16[64,512]{1,0:T(8,128)(2,1)S(1)}, u32[]{:S(2)}, u32[]{:S(2)}) collective-permute-start(bf16[64,512]{1,0:T(8,128)(2,1)} %get-tuple-element.62), channel_id=1, source_target_pairs={{0,4},{2,6},{4,0},{6,2},{8,12},{10,14},{12,8},{14,10},{16,20},{18,... | collective-permute-start | bytes 196616 | tf_op jit(solution)/shard_map/ppermute | solution.py:530
  6.4 9.9 %collective-permute-start.11 = (bf16[64,512]{1,0:T(8,128)(2,1)}, bf16[64,512]{1,0:T(8,128)(2,1)S(1)}, u32[]{:S(2)}, u32[]{:S(2)}) collective-permute-start(bf16[64,512]{1,0:T(8,128)(2,1)} %get-tuple-element.63), channel_id=1, source_target_pairs={{0,6},{2,4},{4,2},{6,0},{8,14},{10,12},{12,10},{14,8},{16,22},{18,... | collective-permute-start | bytes 196616 | tf_op jit(solution)/shard_map/ppermute | solution.py:530
  6.4 25.1 %collective-permute-start.8 = (bf16[128,1024]{1,0:T(8,128)(2,1)}, bf16[128,1024]{1,0:T(8,128)(2,1)S(1)}, u32[]{:S(2)}, u32[]{:S(2)}) collective-permute-start(bf16[128,1024]{1,0:T(8,128)(2,1)} %get-tuple-element.58), channel_id=1, source_target_pairs={{0,6},{2,4},{4,2},{6,0},{8,14},{10,12},{12,10},{14,8},{16,22},{18,... | collective-permute-start | bytes 786440 | tf_op jit(solution)/shard_map/ppermute | solution.py:530
  10.1 0.9 copy-start.2
  11.0 0.8 copy-start.3
  11.9 11.3 %collective-permute-start = (bf16[96,1024]{1,0:T(8,128)(2,1)S(1)}, bf16[96,1024]{1,0:T(8,128)(2,1)S(1)}, u32[]{:S(2)}, u32[]{:S(2)}) collective-permute-start(bf16[96,1024]{1,0:T(8,128)(2,1)S(1)} %get-tuple-element.51), channel_id=1, source_target_pairs={{0,8},{2,10},{4,12},{6,14},{8,0},{10,2},{12,4},{14,6},{16,24},{18,... | collective-permute-start | bytes 589832 | tf_op jit(solution)/shard_map/ppermute | solution.py:539
  13.5 16.8 %collective-permute-start.1 = (bf16[96,1024]{1,0:T(8,128)(2,1)S(1)}, bf16[96,1024]{1,0:T(8,128)(2,1)S(1)}, u32[]{:S(2)}, u32[]{:S(2)}) collective-permute-start(bf16[96,1024]{1,0:T(8,128)(2,1)S(1)} %get-tuple-element.52), channel_id=1, source_target_pairs={{0,16},{2,18},{4,20},{6,22},{8,24},{10,26},{12,28},{14,30},{16,0},... | collective-permute-start | bytes 589832 | tf_op jit(solution)/shard_map/ppermute | solution.py:539
  16.1 14.7 %collective-permute-start.2 = (bf16[96,1024]{1,0:T(8,128)(2,1)S(1)}, bf16[96,1024]{1,0:T(8,128)(2,1)S(1)}, u32[]{:S(2)}, u32[]{:S(2)}) collective-permute-start(bf16[96,1024]{1,0:T(8,128)(2,1)S(1)} %get-tuple-element.53), channel_id=1, source_target_pairs={{0,24},{2,26},{4,28},{6,30},{8,16},{10,18},{12,20},{14,22},{16,8},... | collective-permute-start | bytes 589832 | tf_op jit(solution)/shard_map/ppermute | solution.py:539
  16.3 0.8 copy-start.6
  17.2 13.1 %copy-start.7 = (bf16[128,1024]{1,0:T(8,128)(2,1)S(1)}, bf16[128,1024]{1,0:T(8,128)(2,1)}, u32[]{:S(2)}) copy-start(bf16[128,1024]{1,0:T(8,128)(2,1)} %get-tuple-element.58) | copy-start | bytes 786436
  17.2 15.9 %collective-permute-start.13 = (bf16[256,512]{1,0:T(8,128)(2,1)S(1)}, bf16[256,512]{1,0:T(8,128)(2,1)S(1)}, u32[]{:S(2)}, u32[]{:S(2)}) collective-permute-start(bf16[256,512]{1,0:T(8,128)(2,1)S(1)} %shard_map.95.refs_0_), channel_id=1, source_target_pairs={{0,8},{2,10},{4,12},{6,14},{8,0},{10,2},{12,4},{14,6},{16,24},{18,... | collective-permute-start | bytes 786440 | tf_op jit(solution)/shard_map/ppermute | solution.py:539
  23.1 20.4 %collective-permute-start.12 = (bf16[256,512]{1,0:T(8,128)(2,1)S(1)}, bf16[256,512]{1,0:T(8,128)(2,1)S(1)}, u32[]{:S(2)}, u32[]{:S(2)}) collective-permute-start(bf16[256,512]{1,0:T(8,128)(2,1)S(1)} %shard_map.95.refs_0_), channel_id=1, source_target_pairs={{0,16},{2,18},{4,20},{6,22},{8,24},{10,26},{12,28},{14,30},{16,0},... | collective-permute-start | bytes 786440 | tf_op jit(solution)/shard_map/ppermute | solution.py:539
  30.3 13.8 %collective-permute-start.7 = (bf16[128,1024]{1,0:T(8,128)(2,1)S(1)}, bf16[128,1024]{1,0:T(8,128)(2,1)S(1)}, u32[]{:S(2)}, u32[]{:S(2)}) collective-permute-start(bf16[128,1024]{1,0:T(8,128)(2,1)S(1)} %copy-done.7), channel_id=1, source_target_pairs={{0,4},{2,6},{4,0},{6,2},{8,12},{10,14},{12,8},{14,10},{16,20},{18,... | collective-permute-start | bytes 786440 | tf_op jit(solution)/shard_map/ppermute | solution.py:530
  30.8 14.5 %collective-permute-start.6 = (bf16[128,1024]{1,0:T(8,128)(2,1)S(1)}, bf16[128,1024]{1,0:T(8,128)(2,1)S(1)}, u32[]{:S(2)}, u32[]{:S(2)}) collective-permute-start(bf16[128,1024]{1,0:T(8,128)(2,1)S(1)} %copy-done.7), channel_id=1, source_target_pairs={{0,2},{2,0},{4,6},{6,4},{8,10},{10,8},{12,14},{14,12},{16,18},{18,... | collective-permute-start | bytes 786440 | tf_op jit(solution)/shard_map/ppermute | solution.py:530
  31.5 14.5 %collective-permute-start.3 = (bf16[128,1024]{1,0:T(8,128)(2,1)S(1)}, bf16[128,1024]{1,0:T(8,128)(2,1)S(1)}, u32[]{:S(2)}, u32[]{:S(2)}) collective-permute-start(bf16[128,1024]{1,0:T(8,128)(2,1)S(1)} %get-tuple-element.55), channel_id=1, source_target_pairs={{0,2},{2,0},{4,6},{6,4},{8,10},{10,8},{12,14},{14,12},{16,18},{18,... | collective-permute-start | bytes 786440 | tf_op jit(solution)/shard_map/ppermute | solution.py:530
  33.1 12.9 %collective-permute-start.4 = (bf16[128,1024]{1,0:T(8,128)(2,1)S(1)}, bf16[128,1024]{1,0:T(8,128)(2,1)S(1)}, u32[]{:S(2)}, u32[]{:S(2)}) collective-permute-start(bf16[128,1024]{1,0:T(8,128)(2,1)S(1)} %get-tuple-element.56), channel_id=1, source_target_pairs={{0,4},{2,6},{4,0},{6,2},{8,12},{10,14},{12,8},{14,10},{16,20},{18,... | collective-permute-start | bytes 786440 | tf_op jit(solution)/shard_map/ppermute | solution.py:530
  43.6 7.3 %collective-permute-start.5 = (bf16[128,1024]{1,0:T(8,128)(2,1)S(1)}, bf16[128,1024]{1,0:T(8,128)(2,1)S(1)}, u32[]{:S(2)}, u32[]{:S(2)}) collective-permute-start(bf16[128,1024]{1,0:T(8,128)(2,1)S(1)} %get-tuple-element.57), channel_id=1, source_target_pairs={{0,6},{2,4},{4,2},{6,0},{8,14},{10,12},{12,10},{14,8},{16,22},{18,... | collective-permute-start | bytes 786440 | tf_op jit(solution)/shard_map/ppermute | solution.py:530
  44.0 8.3 %collective-permute-start.14 = (bf16[256,512]{1,0:T(8,128)(2,1)S(1)}, bf16[256,512]{1,0:T(8,128)(2,1)S(1)}, u32[]{:S(2)}, u32[]{:S(2)}) collective-permute-start(bf16[256,512]{1,0:T(8,128)(2,1)S(1)} %collective-permute-done.12.refs_2_), channel_id=1, source_target_pairs={{8,0},{10,2},{12,4},{14,6},{16,24},{18,26},{20,28},{22,30},{9,1},{... | collective-permute-start | bytes 786440 | tf_op jit(solution)/shard_map/ppermute | solution.py:555
  45.3 7.0 %collective-permute-start.15 = (bf16[256,512]{1,0:T(8,128)(2,1)S(1)}, bf16[256,512]{1,0:T(8,128)(2,1)S(1)}, u32[]{:S(2)}, u32[]{:S(2)}) collective-permute-start(bf16[256,512]{1,0:T(8,128)(2,1)S(1)} %shard_map.95.refs_0_), channel_id=1, source_target_pairs={{8,16},{10,18},{12,20},{14,22},{16,8},{18,10},{20,12},{22,14},{9,1... | collective-permute-start | bytes 786440 | tf_op jit(solution)/shard_map/ppermute | solution.py:556
  51.4 24.9 %collective-permute-start.21 = (bf16[512,256]{1,0:T(8,128)(2,1)S(1)}, bf16[512,256]{1,0:T(8,128)(2,1)S(1)}, u32[]{:S(2)}, u32[]{:S(2)}) collective-permute-start(bf16[512,256]{1,0:T(8,128)(2,1)S(1)} %get-tuple-element.84), channel_id=1, source_target_pairs={{0,1},{1,0},{2,3},{3,2},{4,5},{5,4},{6,7},{7,6},{8,9},{9,8},{10,11... | collective-permute-start | bytes 786440 | tf_op jit(solution)/shard_map/ppermute | solution.py:536
  51.5 3.0 %copy-start.5 = (s32[8]{0:T(128)S(1)}, s32[8]{0:T(128)}, u32[]{:S(2)}) copy-start(s32[8]{0:T(128)} %len_ref.5) | copy-start | bytes 100
  51.5 3.0 %collective-permute-start.16 = (bf16[512,1024]{1,0:T(8,128)(2,1)S(1)}, bf16[512,1024]{1,0:T(8,128)(2,1)S(1)}, u32[]{:S(2)}, u32[]{:S(2)}) collective-permute-start(bf16[512,1024]{1,0:T(8,128)(2,1)S(1)} %get-tuple-element.69), channel_id=1, source_target_pairs={{0,1},{1,0},{2,3},{3,2},{4,5},{5,4},{6,7},{7,6},{8,9},{9,8},{10,11... | collective-permute-start | bytes 3145736 | tf_op jit(solution)/shard_map/ppermute | solution.py:536
  57.3 10.8 %copy-start.4 = (f32[1024]{0:T(1024)S(1)}, f32[1024]{0:T(1024)}, u32[]{:S(2)}) copy-start(f32[1024]{0:T(1024)} %param.14) | copy-start | bytes 12292
  57.3 11.6 %collective-permute-start.19 = (bf16[144,256]{1,0:T(8,128)(2,1)S(1)}, bf16[144,256]{1,0:T(8,128)(2,1)S(1)}, u32[]{:S(2)}, u32[]{:S(2)}) collective-permute-start(bf16[144,256]{1,0:T(8,128)(2,1)S(1)} %get-tuple-element.81), channel_id=1, source_target_pairs={{0,24},{2,26},{4,28},{6,30},{1,25},{3,27},{5,29},{7,31}} | collective-permute-start | bytes 221192 | tf_op jit(solution)/shard_map/ppermute | solution.py:533
  61.9 7.1 %collective-permute-start.18 = (bf16[144,256]{1,0:T(8,128)(2,1)S(1)}, bf16[144,256]{1,0:T(8,128)(2,1)S(1)}, u32[]{:S(2)}, u32[]{:S(2)}) collective-permute-start(bf16[144,256]{1,0:T(8,128)(2,1)S(1)} %get-tuple-element.81), channel_id=1, source_target_pairs={{0,16},{2,18},{4,20},{6,22},{8,24},{10,26},{12,28},{14,30},{1,17},... | collective-permute-start | bytes 221192 | tf_op jit(solution)/shard_map/ppermute | solution.py:533
  64.9 4.1 %collective-permute-start.17 = (bf16[144,256]{1,0:T(8,128)(2,1)S(1)}, bf16[144,256]{1,0:T(8,128)(2,1)S(1)}, u32[]{:S(2)}, u32[]{:S(2)}) collective-permute-start(bf16[144,256]{1,0:T(8,128)(2,1)S(1)} %get-tuple-element.81), channel_id=1, source_target_pairs={{0,8},{2,10},{4,12},{6,14},{8,16},{10,18},{12,20},{14,22},{16,24},... | collective-permute-start | bytes 221192 | tf_op jit(solution)/shard_map/ppermute | solution.py:533
  69.0 0.9 copy-start.1
  71.5 4.8 %collective-permute-start.20 = (bf16[256,256]{1,0:T(8,128)(2,1)S(1)}, bf16[256,256]{1,0:T(8,128)(2,1)S(1)}, u32[]{:S(2)}, u32[]{:S(2)}) collective-permute-start(bf16[256,256]{1,0:T(8,128)(2,1)S(1)} %shard_map.101.refs_0_), channel_id=1, source_target_pairs={{0,1},{1,0},{2,3},{3,2},{4,5},{5,4},{6,7},{7,6},{8,9},{9,8},{10,11... | collective-permute-start | bytes 393224 | tf_op jit(solution)/shard_map/ppermute | solution.py:536
  76.6 1.9 %collective-permute-start.22 = (bf16[768,256]{1,0:T(8,128)(2,1)S(1)}, bf16[768,256]{1,0:T(8,128)(2,1)S(1)}, u32[]{:S(2)}, u32[]{:S(2)}) collective-permute-start(bf16[768,256]{1,0:T(8,128)(2,1)S(1)} %shard_map.102.refs_0_), channel_id=1, source_target_pairs={{0,1},{1,0},{2,3},{3,2},{4,5},{5,4},{6,7},{7,6},{8,9},{9,8},{10,11... | collective-permute-start | bytes 1179656 | tf_op jit(solution)/shard_map/ppermute | solution.py:536
  77.2 10.1 %collective-permute-start.23 = (bf16[256,512]{1,0:T(8,128)(2,1)S(1)}, bf16[256,512]{1,0:T(8,128)(2,1)S(1)}, u32[]{:S(2)}, u32[]{:S(2)}) collective-permute-start(bf16[256,512]{1,0:T(8,128)(2,1)S(1)} %shard_map.103), channel_id=1, source_target_pairs={{0,6},{2,4},{4,2},{6,0},{8,14},{10,12},{12,10},{14,8},{16,22},{18,... | collective-permute-start | bytes 786440 | tf_op jit(solution)/shard_map/ppermute | solution.py:530
  79.2 12.4 %collective-permute-start.24 = (bf16[256,512]{1,0:T(8,128)(2,1)S(1)}, bf16[256,512]{1,0:T(8,128)(2,1)S(1)}, u32[]{:S(2)}, u32[]{:S(2)}) collective-permute-start(bf16[256,512]{1,0:T(8,128)(2,1)S(1)} %get-tuple-element.93), channel_id=1, source_target_pairs={{0,2},{2,0},{4,6},{6,4},{8,10},{10,8},{12,14},{14,12},{16,18},{18,... | collective-permute-start | bytes 786440 | tf_op jit(solution)/shard_map/ppermute | solution.py:530
  80.3 11.7 %collective-permute-start.25 = (bf16[256,512]{1,0:T(8,128)(2,1)S(1)}, bf16[256,512]{1,0:T(8,128)(2,1)S(1)}, u32[]{:S(2)}, u32[]{:S(2)}) collective-permute-start(bf16[256,512]{1,0:T(8,128)(2,1)S(1)} %get-tuple-element.94), channel_id=1, source_target_pairs={{0,4},{2,6},{4,0},{6,2},{8,12},{10,14},{12,8},{14,10},{16,20},{18,... | collective-permute-start | bytes 786440 | tf_op jit(solution)/shard_map/ppermute | solution.py:530

commit v10 on v9

--- a/solution.py
+++ b/solution.py
@@ -13,7 +13,7 @@
 CONV_ROWS = 64
 BF16 = jnp.bfloat16
 F32 = jnp.float32
-STACK_HINT = 40_000_000_000
+INWARD_HINT = 40_000_000_000
 ASSEMBLE_HINT = 40_000_000_000
 ALL_VMEM_BYTES = 63 * 1024 * 1024
 VMEM_BYTES = 20 * 1024 * 1024
@@ -62,36 +62,73 @@
         dest_ref[pl.ds(pl.multiple_of((plane ^ offset) * rows, rows), rows), : value.shape[1]] = value
 
 
-def cut_kernel(group, frames_ref, *refs):
+def first_kernel(group, planes, log_decay_ref, bc_ref, out_w_ref, frames_ref, *refs):
     weight_refs, refs = refs[:2], refs[2:]
-    half_ref, out_refs, sems = refs[0], refs[1:-1], refs[-1]
-    place, _ = plane_place(group)
+    inner_refs, outer_refs, refs = refs[:group], refs[group : group + planes], refs[group + planes :]
+    bc_half_ref, out_copy_ref, edge_ref, decay_ref, sems = refs
+    place, plane = plane_place(group)
     parity = lax.rem(lax.axis_index("head"), 2)
     width = weight_refs[0].shape[1] // group
-    half = half_ref.shape[0]
-    copies = [(frames_ref.at[pl.ds(pl.multiple_of(parity * half, half), half), :], half_ref)]
-    for step, out_ref in enumerate(out_refs):
+    frames = frames_ref.shape[0]
+    heads = log_decay_ref.shape[0] // group
+    half = frames // 2
+    fold = inner_refs[0].shape[1] // (2 * width)
+    height = weight_refs[0].shape[0] // fold
+    copies = [
+        (out_w_ref, out_copy_ref),
+        (bc_ref.at[:, pl.ds(pl.multiple_of(parity * LANES, LANES), LANES)], bc_half_ref),
+        (frames_ref.at[:EDGE, :], edge_ref.at[0]),
+        (frames_ref.at[frames - EDGE :, :], edge_ref.at[1]),
+        (log_decay_ref, decay_ref),
+    ]
+    for step, inner_ref in enumerate(inner_refs):
+        top = inner_ref.shape[0] - height
         lanes = pl.ds(pl.multiple_of((place ^ step) * width, LANES), width)
         for number, weight_ref in enumerate(weight_refs):
-            copies.append((weight_ref.at[:, lanes], out_ref.at[:, number * width : (number + 1) * width]))
+            for part in range(fold):
+                at = (2 * part + number) * width
+                source = weight_ref.at[part * height : (part + 1) * height, lanes]
+                copies.append((source, inner_ref.at[top:, at : at + width]))
+        if step:
+            source = frames_ref.at[pl.ds(pl.multiple_of(parity * half, half), half), :]
+            copies.append((source, inner_ref.at[:half, : frames_ref.shape[1]]))
     started = [pltpu.make_async_copy(a, b, sems.at[number]) for number, (a, b) in enumerate(copies)]
     for copy in started:
         copy.start()
-    for copy in started:
+    for copy in started[:5]:
         copy.wait()
+    lane = lax.broadcasted_iota(jnp.int32, (8, LANES), 1)
+    decays = []
+    for first in (0, frames - LANES):
+        rows = [jnp.zeros((8, LANES), F32), jnp.zeros((8, LANES), F32)]
+        for block in range(group):
+            here = decay_ref[block * heads : (block + 1) * heads, first : first + LANES]
+            here = jnp.concatenate([here, jnp.zeros((8 - heads, LANES), F32)], axis=0)
+            for number, term in enumerate(three_terms(here)):
+                slot = number * group + block
+                moved = pltpu.roll(term, (slot % 8 * EDGE + (EDGE if first else 0)) % LANES, 1)
+                rows[slot // 8] = jnp.where(lane // EDGE == slot % 8, moved, rows[slot // 8])
+        decays.append(jnp.concatenate(rows, axis=0))
+    for step, out_ref in enumerate(outer_refs):
+        number = put(out_ref, 0, out_copy_ref[...])
+        number = put(out_ref, number, bc_half_ref[...])
+        later = (plane ^ step) > plane
+        number = put(out_ref, number, jnp.where(later, edge_ref[1].astype(F32), edge_ref[0].astype(F32)).astype(BF16))
+        put(out_ref, number, jnp.where(later, decays[1], decays[0]).astype(BF16))
+    for copy in started[5:]:
+        copy.wait()
 
 
 def stack_kernel(group, *refs):
-    parts, stack_refs = refs[:group], refs[group:]
+    parts, stack_ref = refs[:group], refs[group]
     place, _ = plane_place(group)
-    rows = parts[0].shape[0]
+    width = stack_ref.shape[1]
+    height = parts[0].shape[0]
+    fold = parts[0].shape[1] // width
     for step, part in enumerate(parts):
-        at = pl.ds(pl.multiple_of((place ^ step) * rows, rows), rows)
-        first = 0
-        for stack_ref in stack_refs:
-            width = stack_ref.shape[1]
-            stack_ref[at, :] = part[:, first : first + width]
-            first += width
+        for number in range(fold):
+            at = pl.multiple_of(((place ^ step) * fold + number) * height, 16)
+            stack_ref[pl.ds(at, height), :] = part[part.shape[0] - height :, number * width : (number + 1) * width]
 
 
 def assemble_kernel(group, offsets, *refs):
@@ -125,34 +162,13 @@
     return terms
 
 
-def outward_kernel(group, planes, out_w_ref, bc_ref, frames_ref, decay_ref, *out_refs):
-    _, plane = plane_place(group)
-    parity = lax.rem(lax.axis_index("head"), 2)
-    frames = frames_ref.shape[0]
-    lane = lax.broadcasted_iota(jnp.int32, (8, LANES), 1)
-    decays = []
-    for first in (0, frames - LANES):
-        rows = [jnp.zeros((8, LANES), F32), jnp.zeros((8, LANES), F32)]
-        for block in range(group):
-            for number, term in enumerate(three_terms(decay_ref[block, :, first : first + LANES])):
-                slot = number * group + block
-                moved = pltpu.roll(term, (slot % 8 * EDGE + (EDGE if first else 0)) % LANES, 1)
-                rows[slot // 8] = jnp.where(lane // EDGE == slot % 8, moved, rows[slot // 8])
-        decays.append(jnp.concatenate(rows, axis=0))
-    for step, out_ref in enumerate(out_refs):
-        number = put(out_ref, 0, out_w_ref[...])
-        number = put(out_ref, number, bc_ref[:, pl.ds(pl.multiple_of(parity * LANES, LANES), LANES)])
-        later = (plane ^ step) > plane
-        edge = pl.multiple_of(jnp.where(later, frames - EDGE, 0), EDGE)
-        number = put(out_ref, number, frames_ref[pl.ds(edge, EDGE), :])
-        put(out_ref, number, jnp.where(later, decays[1], decays[0]).astype(BF16))
-
-
-def inward_kernel(group, rows, channels, decay_ref, *refs):
-    piece_refs, out_refs = refs[:-group], refs[-group:]
+def inward_kernel(group, planes, rows, channels, decay_ref, *refs):
+    piece_refs, out_refs, whole_ref = refs[: -group - 1], refs[-group - 1 : -1], refs[-1]
     place, plane = plane_place(group)
     width = channels // group
-    planes = len(piece_refs)
+    if len(piece_refs) > planes:
+        whole_ref[...] = piece_refs[-2][...] + piece_refs[-1][...]
+        piece_refs = [*piece_refs[: planes - 1], whole_ref]
     wanted = jnp.clip(jnp.where(place == 0, plane + 1, plane - 1), 0, planes - 1)
     depth_tiles = out_refs[0].shape[1] // LANES
     across, down = channels // LANES, rows // 16
@@ -252,11 +268,11 @@
     for step in range(1, other_out_ref.shape[0] // share + 1):
         at = pl.ds(pl.multiple_of((core ^ step) * share, share), share)
         other_out_ref[(step - 1) * share : step * share, :] = out_ref[at, :]
-    half = half_refs[0].shape[0]
+    height = LANES
+    top = swap_ref.shape[0] - height
+    half = top // len(half_refs)
     for number, half_ref in enumerate(half_refs):
-        swap_ref[number * half : (number + 1) * half, :] = half_ref[...]
-    top = len(half_refs) * half
-    height = swap_ref.shape[0] - top
+        swap_ref[number * half : (number + 1) * half, :] = half_ref[:half, : swap_ref.shape[1]]
     for number in range(bc_ref.shape[0] // height):
         lanes = slice(number * LANES, (number + 1) * LANES)
         swap_ref[top:, lanes] = bc_ref[number * height : (number + 1) * height, :]
@@ -298,7 +314,7 @@
         block = EDGE + (place ^ (number + 1)) * frames
         mine = pl.ds(pl.multiple_of(block + parity * half, EDGE), half)
         other = pl.ds(pl.multiple_of(block + (1 - parity) * half, EDGE), half)
-        frames_ref[mine, :] = half_ref[...]
+        frames_ref[mine, :] = half_ref[:half, : frames_ref.shape[1]]
         frames_ref[other, :] = swap_ref[number * half : (number + 1) * half, :]
     mine = pl.ds(pl.multiple_of(parity * LANES, LANES), LANES)
     other = pl.ds(pl.multiple_of((1 - parity) * LANES, LANES), LANES)
@@ -542,39 +558,55 @@
     rows = x_weight.shape[0]
     parity = lax.rem(core, 2)
 
-    def along_planes(stack):
+    def along_planes(stacks):
         if planes != 4:
-            return [stack] + [between_planes(stack, step) for step in range(1, planes)], tuple(range(planes))
+            return [stacks[0]] + [between_planes(stacks[step], step) for step in range(1, planes)]
 
         def pairs(chosen):
             return [(a * group + q, b * group + q) for a, b in chosen for q in range(group)]
 
-        second = between_planes(stack, 2)
-        first = between_planes(stack, 1)
-        again, stack_then, first = lax.optimization_barrier((second, stack, first))
+        second = between_planes(stacks[2], 2)
+        first = between_planes(stacks[1], 1)
+        again, last, first = lax.optimization_barrier((second, stacks[3], first))
         third = lax.ppermute(again, "tm", pairs([(1, 0), (2, 3)]))
-        middle = lax.ppermute(stack_then, "tm", pairs([(1, 2), (2, 1)]))
-        return [stack, first, second, third, middle], (0, 1, 2, 3, 3)
-
+        middle = lax.ppermute(last, "tm", pairs([(1, 2), (2, 1)]))
+        return [stacks[0], first, second, third, middle]
+
+    offsets = (0, 1, 2, 3, 3) if planes == 4 else tuple(range(planes))
     half_count = frame_count // 2
-    frame_half, *packed = call(
-        functools.partial(cut_kernel, group),
-        (shape((half_count, depth), BF16), *(shape((rows, 2 * width), BF16) for _ in range(group))),
-        [frames, x_weight, z_weight],
-        [pltpu.SemaphoreType.DMA((1 + 2 * group,))],
+    down, across_tiles, depth_tiles = rows // 16, channels // LANES, depth // LANES
+    tiles = down * (across_tiles + 1) + depth_tiles + 1
+    fold = max(1, min(depth // (2 * width), down))
+    inner_shape = (half_count + rows // fold, max(depth, fold * 2 * width))
+    payloads = call(
+        functools.partial(first_kernel, group, planes),
+        (
+            shape((rows // fold, fold * 2 * width), BF16),
+            *(shape(inner_shape, BF16) for _ in range(1, group)),
+            *(shape((-(-tiles // 8) * 16, depth), BF16) for _ in range(planes)),
+        ),
+        [log_decay, bc_weight, out_weight.T, frames, x_weight, z_weight],
+        [
+            pltpu.VMEM((rows, LANES), BF16),
+            pltpu.VMEM((rows, channels), BF16),
+            pltpu.VMEM((2, EDGE, depth), BF16),
+            pltpu.VMEM(log_decay.shape, F32),
+            pltpu.SemaphoreType.DMA((4 + group * (2 * fold + 1),)),
+        ],
         smem=0,
-        anywhere=3,
+        anywhere=6,
         vmem=ALL_VMEM_BYTES,
     )
-    parts = [packed[0]] + [in_plane(packed[step], step) for step in range(1, group)]
-    (xz_stack,) = call(
+    inner, outer = payloads[:group], payloads[group:]
+    parts = [inner[0]] + [in_plane(inner[step], step) for step in range(1, group)]
+    pieces = along_planes(outer)
+    xz_stack = call(
         functools.partial(stack_kernel, group),
-        (shape((group * rows, 2 * width), BF16),),
+        shape((group * rows, 2 * width), BF16),
         parts,
-        flops=STACK_HINT,
         smem=0,
     )
-    xz_pieces, offsets = along_planes(xz_stack)
+    xz_pieces = along_planes([xz_stack] * planes)
     x_columns, z_columns = call(
         functools.partial(assemble_kernel, group, offsets),
         (shape((depth, width), BF16), shape((depth, width), BF16)),
@@ -583,21 +615,13 @@
         smem=0,
     )
     decay_blocks = jnp.pad(log_decay.reshape(group, heads, frame_count), ((0, 0), (0, 8 - heads), (0, 0)))
-    down, across_tiles, depth_tiles = rows // 16, channels // LANES, depth // LANES
-    tiles = down * (across_tiles + 1) + depth_tiles + 1
-    outward = call(
-        functools.partial(outward_kernel, group, planes),
-        tuple(shape((-(-tiles // 8) * 16, depth), BF16) for _ in range(planes)),
-        [out_weight.T, bc_weight, frames, decay_blocks],
-        smem=0,
-    )
-    pieces = [outward[0]] + [between_planes(outward[step], step) for step in range(1, planes)]
-    half_parts = [in_plane(frame_half, step) for step in range(1, group)]
     tiles = planes * down * (width // LANES + 1) + depth_tiles + 1 + frame_count // SPAN * 2
     inward = call(
-        functools.partial(inward_kernel, group, rows, channels),
+        functools.partial(inward_kernel, group, planes, rows, channels),
         tuple(shape((-(-tiles // 8) * 16, depth), BF16) for _ in range(group)),
         [decay_blocks, *pieces],
+        [pltpu.VMEM(pieces[0].shape, BF16)],
+        flops=INWARD_HINT,
         smem=0,
     )
     inward = [inward[0]] + [in_plane(inward[step], step) for step in range(1, group)]
@@ -612,7 +636,7 @@
             shape((share, width), BF16),
             shape(((cores - 1) * share, width), BF16),
         ),
-        [*inward, *half_parts],
+        [*inward, *parts[1:]],
         [pltpu.VMEM((depth, width), BF16), pltpu.VMEM((count, 8, SPAN), F32)],
         smem=0,
     )
@@ -631,7 +655,7 @@
             shape((-(-count // 8) * 8, width), F32),
             shape((state + EDGE, width), BF16),
         ),
-        [record_lengths, decay, x_columns, bc_mine, frames, swap, halo, *half_parts],
+        [record_lengths, decay, x_columns, bc_mine, frames, swap, halo, *parts[1:]],
         [pltpu.VMEM((depth, 2 * state), BF16), pltpu.VMEM((total, width), F32)],
         flops=2 * total * depth * (width + 2 * state),
     )
@@ -681,6 +705,7 @@
     far_act = conv(far, gated)
     far_swapped = [across(far_act, step) for step in range(1, cores)]
     own_out, other_out = out_parts
+    other_out, gated = lax.optimization_barrier((other_out, gated))
     out_parts = [own_out]
     for step in range(1, cores):
         out_parts.append(across(other_out[(step - 1) * share : step * share], step))

time: 93.8 us -> 88.9 us (0.948)
  waiting for transfers between devices: 38.1 us -> 35.8 us
  local copies, waits for them, and re-layouts: 3.47 us -> 1.74 us
  starting transfers between devices: 33.8 us -> 32.2 us
  Pallas kernels: 16.3 us -> 17.6 us
    ppermute x5 -> x4, waiting for transfers between devices: 19.9 us -> 13.7 us  [between_planes(): lax.ppermute(array, 'tm', [(i, i ^ step * group) for i in range(times)])]
    ppermute x1 -> x2, waiting for transfers between devices: 0.32 us -> 5.57 us  [along_planes(): third = lax.ppermute(again, 'tm', pairs([(1, 0), (2, 3)]))]
    ppermute x12 -> x9, starting transfers between devices: 15.2 us -> 11.7 us  [in_plane(): return lax.ppermute(array, 'tm', [(i, i ^ step) for i in range(times)])]
    ppermute x4, waiting for transfers between devices: 2.49 us -> 0.01 us  [across(): return lax.ppermute(array, 'head', [(i, i ^ step) for i in range(cores)])]
    unnamed x16 -> x12, local copies, waits for them, and re-layouts: 2.73 us -> 1 us
    ppermute x1 -> x2, starting transfers between devices: 1.28 us -> 2.56 us  [along_planes(): third = lax.ppermute(again, 'tm', pairs([(1, 0), (2, 3)]))]
    pallas_call x14 -> x13, Pallas kernels: 16.3 us -> 17.6 us  [call(): pl.pallas_call(kernel, out_shape=out_shape, in_specs=in_specs, out_specs=...]
    ppermute x12 -> x9, waiting for transfers between devices: 15.4 us -> 16.5 us  [in_plane(): return lax.ppermute(array, 'tm', [(i, i ^ step) for i in range(times)])]
  transfers between devices with their start and end apart: 26 -> 24, of which waited for: 10 -> 9; matrix products, arithmetic and copies ran while one was open for 1% -> 1% of each run, Pallas kernels for 15% -> 12%
where the time goes in v10:
time: 88.9 us; the launch traced here: 88.5 us
  waiting for transfers between devices  35.8 us (40%)
  starting transfers between devices  32.2 us (36%)
  Pallas kernels  17.6 us (20%)
  local copies, waits for them, and re-layouts  1.74 us (2%)
    pallas_call x13, Pallas kernels, call(): pl.pallas_call(kernel, out_shape=out_shape, in_specs=in_specs, out_specs=...  17.6 us
    ppermute x9, waiting for transfers between devices, in_plane(): return lax.ppermute(array, 'tm', [(i, i ^ step) for i in range(times)])  16.5 us
    ppermute x4, waiting for transfers between devices, between_planes(): lax.ppermute(array, 'tm', [(i, i ^ step * group) for i in range(times)])  13.7 us
    ppermute x9, starting transfers between devices, in_plane(): return lax.ppermute(array, 'tm', [(i, i ^ step) for i in range(times)])  11.7 us
    ppermute x3, starting transfers between devices, later(): lax.ppermute(array, 'tm', [(i, i + step * group) for i in range(times - s...  9.25 us
    ppermute x4, starting transfers between devices, between_planes(): lax.ppermute(array, 'tm', [(i, i ^ step * group) for i in range(times)])  6.56 us
    ppermute x2, waiting for transfers between devices, along_planes(): third = lax.ppermute(again, 'tm', pairs([(1, 0), (2, 3)]))  5.57 us
    ppermute x2, starting transfers between devices, along_planes(): third = lax.ppermute(again, 'tm', pairs([(1, 0), (2, 3)]))  2.56 us
  transfers between devices with their start and end apart: 24, of which 9 were waited for; matrix products, arithmetic and copies ran while one was open for 1% of the time, Pallas kernels for 12%

profile of v10, /device:TPU:0, one launch (start us, length us, event | category | flops | bytes accessed | tf_op | source)
XLA Modules:
  0.0 88.5 jit_solution(13035990231551254747)
XLA Ops:
  0.0 2.8 %shard_map.91 = (bf16[32,1024]{1,0:T(8,128)(2,1)}, bf16[160,1024]{1,0:T(8,128)(2,1)}, bf16[160,1024]{1,0:T(8,128)(2,1)}, bf16[160,1024]{1,0:T(8,128)(2,1)}, bf16...) custom-call(f32[16,256]{1,0:T(8,128)} %log_decay_ref.1, ...), custom_call_target="tpu_custom_call" | custom-call | bytes 2801664 | tf_op jit(solution)/shard_map/pallas_call | solution.py:32
  2.8 4.1 %collective-permute-start = (bf16[96,1024]{1,0:T(8,128)(2,1)}, bf16[96,1024]{1,0:T(8,128)(2,1)S(1)}, u32[]{:S(2)}, u32[]{:S(2)}) collective-permute-start(bf16[96,1024]{1,0:T(8,128)(2,1)} %get-tuple-element.55), channel_id=1, source_target_pairs={{0,16},{2,18},{4,20},{6,22},{8,24},{10,26},{12,28},{14,30},{16,0},... | collective-permute-start | bytes 589832 | tf_op jit(solution)/shard_map/ppermute | solution.py:555
  6.9 1.6 %collective-permute-start.1 = (bf16[96,1024]{1,0:T(8,128)(2,1)}, bf16[96,1024]{1,0:T(8,128)(2,1)S(1)}, u32[]{:S(2)}, u32[]{:S(2)}) collective-permute-start(bf16[96,1024]{1,0:T(8,128)(2,1)} %get-tuple-element.57), channel_id=1, source_target_pairs={{0,8},{2,10},{4,12},{6,14},{8,0},{10,2},{12,4},{14,6},{16,24},{18,... | collective-permute-start | bytes 589832 | tf_op jit(solution)/shard_map/ppermute | solution.py:555
  8.5 1.5 %collective-permute-start.7 = (bf16[160,1024]{1,0:T(8,128)(2,1)}, bf16[160,1024]{1,0:T(8,128)(2,1)S(1)}, u32[]{:S(2)}, u32[]{:S(2)}) collective-permute-start(bf16[160,1024]{1,0:T(8,128)(2,1)} %get-tuple-element.65), channel_id=1, source_target_pairs={{0,2},{2,0},{4,6},{6,4},{8,10},{10,8},{12,14},{14,12},{16,18},{18,... | collective-permute-start | bytes 983048 | tf_op jit(solution)/shard_map/ppermute | solution.py:546
  10.0 1.5 %collective-permute-start.8 = (bf16[160,1024]{1,0:T(8,128)(2,1)}, bf16[160,1024]{1,0:T(8,128)(2,1)S(1)}, u32[]{:S(2)}, u32[]{:S(2)}) collective-permute-start(bf16[160,1024]{1,0:T(8,128)(2,1)} %get-tuple-element.66), channel_id=1, source_target_pairs={{0,4},{2,6},{4,0},{6,2},{8,12},{10,14},{12,8},{14,10},{16,20},{18,... | collective-permute-start | bytes 983048 | tf_op jit(solution)/shard_map/ppermute | solution.py:546
  11.5 0.5 collective-permute-start.9
  12.0 4.4 %collective-permute-done.refs_2_ = bf16[96,1024]{1,0:T(8,128)(2,1)S(1)} collective-permute-done((bf16[96,1024]{1,0:T(8,128)(2,1)}, bf16[96,1024]{1,0:T(8,128)(2,1)S(1)}, u32[]{:S(2)}, u32[]{:S(2)}) %collective-permute-start) | collective-permute-done | bytes 196640 | tf_op jit(solution)/shard_map/ppermute | solution.py:555
  16.3 0.2 collective-permute-done.1.refs_1_
  16.5 1.3 %collective-permute-start.2 = (bf16[96,1024]{1,0:T(8,128)(2,1)S(1)}, bf16[96,1024]{1,0:T(8,128)(2,1)S(1)}, u32[]{:S(2)}, u32[]{:S(2)}) collective-permute-start(bf16[96,1024]{1,0:T(8,128)(2,1)S(1)} %collective-permute-done.refs_2_), channel_id=1, source_target_pairs={{8,0},{10,2},{12,4},{14,6},{16,24},{18,26},{20,28},{22,30},{9,1},{... | collective-permute-start | bytes 589832 | tf_op jit(solution)/shard_map/ppermute | solution.py:571
  17.8 0.7 collective-permute-start.3
  18.5 0.7 reshape.3
  19.2 0.1 collective-permute-done.7.refs_4_.refs_1_.refs_0_
  19.4 6.5 %collective-permute-done.8.refs_5_.refs_2_.refs_1_ = bf16[160,1024]{1,0:T(8,128)(2,1)S(1)} collective-permute-done((bf16[160,1024]{1,0:T(8,128)(2,1)}, bf16[160,1024]{1,0:T(8,128)(2,1)S(1)}, u32[]{:S(2)}, u32[]{:S(2)}) %collective-permute-start.8) | collective-permute-done | bytes 327712 | tf_op jit(solution)/shard_map/ppermute | solution.py:546
  25.8 0.8 copy-done.2
  26.7 0.5 collective-permute-start.11
  27.2 0.4 collective-permute-start.10
  27.6 0.2 shard_map.92
  27.8 1.3 %collective-permute-start.4 = (bf16[128,1024]{1,0:T(8,128)(2,1)S(1)}, bf16[128,1024]{1,0:T(8,128)(2,1)S(1)}, u32[]{:S(2)}, u32[]{:S(2)}) collective-permute-start(bf16[128,1024]{1,0:T(8,128)(2,1)S(1)} %get-tuple-element.62), channel_id=1, source_target_pairs={{0,2},{2,0},{4,6},{6,4},{8,10},{10,8},{12,14},{14,12},{16,18},{18,... | collective-permute-start | bytes 786440 | tf_op jit(solution)/shard_map/ppermute | solution.py:546
  29.1 0.8 collective-permute-start.5
  30.0 1.4 %collective-permute-start.6 = (bf16[128,1024]{1,0:T(8,128)(2,1)S(1)}, bf16[128,1024]{1,0:T(8,128)(2,1)S(1)}, u32[]{:S(2)}, u32[]{:S(2)}) collective-permute-start(bf16[128,1024]{1,0:T(8,128)(2,1)S(1)} %get-tuple-element.64), channel_id=1, source_target_pairs={{0,6},{2,4},{4,2},{6,0},{8,14},{10,12},{12,10},{14,8},{16,22},{18,... | collective-permute-start | bytes 786440 | tf_op jit(solution)/shard_map/ppermute | solution.py:546
  31.4 5.9 %collective-permute-done.11.refs_1_ = bf16[256,512]{1,0:T(8,128)(2,1)S(1)} collective-permute-done((bf16[256,512]{1,0:T(8,128)(2,1)S(1)}, bf16[256,512]{1,0:T(8,128)(2,1)S(1)}, u32[]{:S(2)}, u32[]{:S(2)}) %collective-permute-start.11) | collective-permute-done | bytes 262176 | tf_op jit(solution)/shard_map/ppermute | solution.py:555
  37.3 3.3 %collective-permute-done.10.refs_2_ = bf16[256,512]{1,0:T(8,128)(2,1)S(1)} collective-permute-done((bf16[256,512]{1,0:T(8,128)(2,1)S(1)}, bf16[256,512]{1,0:T(8,128)(2,1)S(1)}, u32[]{:S(2)}, u32[]{:S(2)}) %collective-permute-start.10) | collective-permute-done | bytes 262176 | tf_op jit(solution)/shard_map/ppermute | solution.py:555
  40.6 1.3 %collective-permute-start.12 = (bf16[256,512]{1,0:T(8,128)(2,1)S(1)}, bf16[256,512]{1,0:T(8,128)(2,1)S(1)}, u32[]{:S(2)}, u32[]{:S(2)}) collective-permute-start(bf16[256,512]{1,0:T(8,128)(2,1)S(1)} %collective-permute-done.10.refs_2_), channel_id=1, source_target_pairs={{8,0},{10,2},{12,4},{14,6},{16,24},{18,26},{20,28},{22,30},{9,1},{... | collective-permute-start | bytes 786440 | tf_op jit(solution)/shard_map/ppermute | solution.py:571
  41.8 0.7 collective-permute-start.13
  42.6 0.6 shard_map.93
  43.2 0.1 collective-permute-start.14
  43.2 5.6 %collective-permute-done.12.refs_3_ = bf16[256,512]{1,0:T(8,128)(2,1)S(1)} collective-permute-done((bf16[256,512]{1,0:T(8,128)(2,1)S(1)}, bf16[256,512]{1,0:T(8,128)(2,1)S(1)}, u32[]{:S(2)}, u32[]{:S(2)}) %collective-permute-start.12) | collective-permute-done | bytes 262176 | tf_op jit(solution)/shard_map/ppermute | solution.py:571
  48.8 0.1 shard_map.95
  48.9 2.8 %shard_map.96 = (bf16[1152,1024]{1,0:T(8,128)(2,1)S(1)}, bf16[1152,256]{1,0:T(8,128)(2,1)S(1)}, bf16[1152,128]{1,0:T(8,128)(2,1)S(1)}, bf16[1152,128]{1,0:T(8,12...) custom-call(s32[8]{0:T(128)S(1)} %copy-done.4, ...), custom_call_target="tpu_custom_call" | custom-call | flops 1073741824 | bytes 8224800 | tf_op jit(solution)/shard_map/pallas_call | solution.py:32
  51.8 5.1 %collective-permute-start.17 = (bf16[144,256]{1,0:T(8,128)(2,1)S(1)}, bf16[144,256]{1,0:T(8,128)(2,1)S(1)}, u32[]{:S(2)}, u32[]{:S(2)}) collective-permute-start(bf16[144,256]{1,0:T(8,128)(2,1)S(1)} %get-tuple-element.88), channel_id=1, source_target_pairs={{0,24},{2,26},{4,28},{6,30},{1,25},{3,27},{5,29},{7,31}} | collective-permute-start | bytes 221192 | tf_op jit(solution)/shard_map/ppermute | solution.py:549
  56.9 2.9 %collective-permute-start.16 = (bf16[144,256]{1,0:T(8,128)(2,1)S(1)}, bf16[144,256]{1,0:T(8,128)(2,1)S(1)}, u32[]{:S(2)}, u32[]{:S(2)}) collective-permute-start(bf16[144,256]{1,0:T(8,128)(2,1)S(1)} %get-tuple-element.88), channel_id=1, source_target_pairs={{0,16},{2,18},{4,20},{6,22},{8,24},{10,26},{12,28},{14,30},{1,17},... | collective-permute-start | bytes 221192 | tf_op jit(solution)/shard_map/ppermute | solution.py:549
  59.7 1.3 %collective-permute-start.15 = (bf16[144,256]{1,0:T(8,128)(2,1)S(1)}, bf16[144,256]{1,0:T(8,128)(2,1)S(1)}, u32[]{:S(2)}, u32[]{:S(2)}) collective-permute-start(bf16[144,256]{1,0:T(8,128)(2,1)S(1)} %get-tuple-element.88), channel_id=1, source_target_pairs={{0,8},{2,10},{4,12},{6,14},{8,16},{10,18},{12,20},{14,22},{16,24},... | collective-permute-start | bytes 221192 | tf_op jit(solution)/shard_map/ppermute | solution.py:549
  61.0 1.9 %shard_map.97 = (f32[1152,256]{1,0:T(8,128)S(1)}, f32[1152,256]{1,0:T(8,128)S(1)}) custom-call(bf16[1152,256]{1,0:T(8,128)(2,1)S(1)} %get-tuple-element.79.x_ref, bf16[1152,128]{1,0:T(8,128)(2,1)S(1)} %get-tuple-element.80.b_ref, bf16[1152,128]{1,0:T(8,128)(2,1)S(1)} %get-tuple-element.78.c_ref, f32[216,128]{1,0:T(8,128)S(1)} %get-tuple-element.81.rows_ref), custom_call_target="tpu_custom_call" | custom-call | flops 134217728 | bytes 3649536 | tf_op jit(solution)/shard_map/pallas_call | solution.py:32
  62.9 0.9 shard_map.98.silu_ref
  63.9 0.7 shard_map.99.gated_ref
  64.6 0.1 copy-done.1
  64.8 1.6 %shard_map.100.refs_0_ = bf16[256,256]{1,0:T(8,128)(2,1)S(1)} custom-call(s32[8]{0:T(128)S(1)} %copy-done.4, f32[31,1024]{1,0:T(8,128)S(1)} %copy-done.1, bf16[1152,256]{1,0:T(8,128)(2,1)S(1)} %shard_map.99.gated_ref), custom_call_target="tpu_custom_call" | custom-call | flops 4063232 | bytes 847904 | tf_op jit(solution)/shard_map/pallas_call | solution.py:32
  66.4 0.4 collective-permute-start.18
  66.8 5.1 %shard_map.101.refs_0_ = bf16[768,256]{1,0:T(8,128)(2,1)S(1)} custom-call(s32[8]{0:T(128)S(1)} %copy-done.4, f32[31,1024]{1,0:T(8,128)S(1)} %copy-done.1, bf16[1152,256]{1,0:T(8,128)(2,1)S(1)} %shard_map.99.gated_ref), custom_call_target="tpu_custom_call" | custom-call | flops 12189696 | bytes 1110048 | tf_op jit(solution)/shard_map/pallas_call | solution.py:32
  71.9 0.3 shard_map.102
  72.3 0.2 collective-permute-start.20
  72.5 2.5 %collective-permute-start.21 = (bf16[256,512]{1,0:T(8,128)(2,1)S(1)}, bf16[256,512]{1,0:T(8,128)(2,1)S(1)}, u32[]{:S(2)}, u32[]{:S(2)}) collective-permute-start(bf16[256,512]{1,0:T(8,128)(2,1)S(1)} %shard_map.102), channel_id=1, source_target_pairs={{0,6},{2,4},{4,2},{6,0},{8,14},{10,12},{12,10},{14,8},{16,22},{18,... | collective-permute-start | bytes 786440 | tf_op jit(solution)/shard_map/ppermute | solution.py:546
  75.0 0.6 shard_map.103
  75.6 0.6 collective-permute-start.22
  76.2 1.6 %collective-permute-start.23 = (bf16[256,512]{1,0:T(8,128)(2,1)S(1)}, bf16[256,512]{1,0:T(8,128)(2,1)S(1)}, u32[]{:S(2)}, u32[]{:S(2)}) collective-permute-start(bf16[256,512]{1,0:T(8,128)(2,1)S(1)} %get-tuple-element.102), channel_id=1, source_target_pairs={{0,4},{2,6},{4,0},{6,2},{8,12},{10,14},{12,8},{14,10},{16,20},{18,... | collective-permute-start | bytes 786440 | tf_op jit(solution)/shard_map/ppermute | solution.py:546
  77.8 4.8 %collective-permute-done.21 = bf16[256,512]{1,0:T(8,128)(2,1)S(1)} collective-permute-done((bf16[256,512]{1,0:T(8,128)(2,1)S(1)}, bf16[256,512]{1,0:T(8,128)(2,1)S(1)}, u32[]{:S(2)}, u32[]{:S(2)}) %collective-permute-start.21) | collective-permute-done | bytes 262176 | tf_op jit(solution)/shard_map/ppermute | solution.py:546
  82.6 5.1 %collective-permute-done.22 = bf16[256,512]{1,0:T(8,128)(2,1)S(1)} collective-permute-done((bf16[256,512]{1,0:T(8,128)(2,1)S(1)}, bf16[256,512]{1,0:T(8,128)(2,1)S(1)}, u32[]{:S(2)}, u32[]{:S(2)}) %collective-permute-start.22) | collective-permute-done | bytes 262176 | tf_op jit(solution)/shard_map/ppermute | solution.py:546
  87.7 0.8 add_convert_fusion
  (28 shorter events, 0.2 us)
Async XLA Ops:
  2.8 13.5 %collective-permute-start = (bf16[96,1024]{1,0:T(8,128)(2,1)}, bf16[96,1024]{1,0:T(8,128)(2,1)S(1)}, u32[]{:S(2)}, u32[]{:S(2)}) collective-permute-start(bf16[96,1024]{1,0:T(8,128)(2,1)} %get-tuple-element.55), channel_id=1, source_target_pairs={{0,16},{2,18},{4,20},{6,22},{8,24},{10,26},{12,28},{14,30},{16,0},... | collective-permute-start | bytes 589832 | tf_op jit(solution)/shard_map/ppermute | solution.py:555
  6.9 9.6 %collective-permute-start.1 = (bf16[96,1024]{1,0:T(8,128)(2,1)}, bf16[96,1024]{1,0:T(8,128)(2,1)S(1)}, u32[]{:S(2)}, u32[]{:S(2)}) collective-permute-start(bf16[96,1024]{1,0:T(8,128)(2,1)} %get-tuple-element.57), channel_id=1, source_target_pairs={{0,8},{2,10},{4,12},{6,14},{8,0},{10,2},{12,4},{14,6},{16,24},{18,... | collective-permute-start | bytes 589832 | tf_op jit(solution)/shard_map/ppermute | solution.py:555
  8.5 10.9 %collective-permute-start.7 = (bf16[160,1024]{1,0:T(8,128)(2,1)}, bf16[160,1024]{1,0:T(8,128)(2,1)S(1)}, u32[]{:S(2)}, u32[]{:S(2)}) collective-permute-start(bf16[160,1024]{1,0:T(8,128)(2,1)} %get-tuple-element.65), channel_id=1, source_target_pairs={{0,2},{2,0},{4,6},{6,4},{8,10},{10,8},{12,14},{14,12},{16,18},{18,... | collective-permute-start | bytes 983048 | tf_op jit(solution)/shard_map/ppermute | solution.py:546
  10.0 15.8 %collective-permute-start.8 = (bf16[160,1024]{1,0:T(8,128)(2,1)}, bf16[160,1024]{1,0:T(8,128)(2,1)S(1)}, u32[]{:S(2)}, u32[]{:S(2)}) collective-permute-start(bf16[160,1024]{1,0:T(8,128)(2,1)} %get-tuple-element.66), channel_id=1, source_target_pairs={{0,4},{2,6},{4,0},{6,2},{8,12},{10,14},{12,8},{14,10},{16,20},{18,... | collective-permute-start | bytes 983048 | tf_op jit(solution)/shard_map/ppermute | solution.py:546
  11.5 14.3 %collective-permute-start.9 = (bf16[160,1024]{1,0:T(8,128)(2,1)}, bf16[160,1024]{1,0:T(8,128)(2,1)S(1)}, u32[]{:S(2)}, u32[]{:S(2)}) collective-permute-start(bf16[160,1024]{1,0:T(8,128)(2,1)} %get-tuple-element.67), channel_id=1, source_target_pairs={{0,6},{2,4},{4,2},{6,0},{8,14},{10,12},{12,10},{14,8},{16,22},{18,... | collective-permute-start | bytes 983048 | tf_op jit(solution)/shard_map/ppermute | solution.py:546
  16.5 11.1 %collective-permute-start.2 = (bf16[96,1024]{1,0:T(8,128)(2,1)S(1)}, bf16[96,1024]{1,0:T(8,128)(2,1)S(1)}, u32[]{:S(2)}, u32[]{:S(2)}) collective-permute-start(bf16[96,1024]{1,0:T(8,128)(2,1)S(1)} %collective-permute-done.refs_2_), channel_id=1, source_target_pairs={{8,0},{10,2},{12,4},{14,6},{16,24},{18,26},{20,28},{22,30},{9,1},{... | collective-permute-start | bytes 589832 | tf_op jit(solution)/shard_map/ppermute | solution.py:571
  17.8 9.8 %collective-permute-start.3 = (bf16[96,1024]{1,0:T(8,128)(2,1)}, bf16[96,1024]{1,0:T(8,128)(2,1)S(1)}, u32[]{:S(2)}, u32[]{:S(2)}) collective-permute-start(bf16[96,1024]{1,0:T(8,128)(2,1)} %get-tuple-element.60), channel_id=1, source_target_pairs={{8,16},{10,18},{12,20},{14,22},{16,8},{18,10},{20,12},{22,14},{9,1... | collective-permute-start | bytes 589832 | tf_op jit(solution)/shard_map/ppermute | solution.py:572
  25.8 0.8 copy-start.2
  26.7 0.9 %copy-start.5 = (bf16[96,1024]{1,0:T(8,128)(2,1)S(1)}, bf16[96,1024]{1,0:T(8,128)(2,1)}, u32[]{:S(2)}) copy-start(bf16[96,1024]{1,0:T(8,128)(2,1)} %get-tuple-element.54.refs_0_) | copy-start | bytes 589828
  26.7 10.6 %collective-permute-start.11 = (bf16[256,512]{1,0:T(8,128)(2,1)S(1)}, bf16[256,512]{1,0:T(8,128)(2,1)S(1)}, u32[]{:S(2)}, u32[]{:S(2)}) collective-permute-start(bf16[256,512]{1,0:T(8,128)(2,1)S(1)} %shard_map.94.refs_0_), channel_id=1, source_target_pairs={{0,8},{2,10},{4,12},{6,14},{8,0},{10,2},{12,4},{14,6},{16,24},{18,... | collective-permute-start | bytes 786440 | tf_op jit(solution)/shard_map/ppermute | solution.py:555
  27.2 13.3 %collective-permute-start.10 = (bf16[256,512]{1,0:T(8,128)(2,1)S(1)}, bf16[256,512]{1,0:T(8,128)(2,1)S(1)}, u32[]{:S(2)}, u32[]{:S(2)}) collective-permute-start(bf16[256,512]{1,0:T(8,128)(2,1)S(1)} %shard_map.94.refs_0_), channel_id=1, source_target_pairs={{0,16},{2,18},{4,20},{6,22},{8,24},{10,26},{12,28},{14,30},{16,0},... | collective-permute-start | bytes 786440 | tf_op jit(solution)/shard_map/ppermute | solution.py:555
  27.8 14.7 %collective-permute-start.4 = (bf16[128,1024]{1,0:T(8,128)(2,1)S(1)}, bf16[128,1024]{1,0:T(8,128)(2,1)S(1)}, u32[]{:S(2)}, u32[]{:S(2)}) collective-permute-start(bf16[128,1024]{1,0:T(8,128)(2,1)S(1)} %get-tuple-element.62), channel_id=1, source_target_pairs={{0,2},{2,0},{4,6},{6,4},{8,10},{10,8},{12,14},{14,12},{16,18},{18,... | collective-permute-start | bytes 786440 | tf_op jit(solution)/shard_map/ppermute | solution.py:546
  29.1 13.4 %collective-permute-start.5 = (bf16[128,1024]{1,0:T(8,128)(2,1)S(1)}, bf16[128,1024]{1,0:T(8,128)(2,1)S(1)}, u32[]{:S(2)}, u32[]{:S(2)}) collective-permute-start(bf16[128,1024]{1,0:T(8,128)(2,1)S(1)} %get-tuple-element.63), channel_id=1, source_target_pairs={{0,4},{2,6},{4,0},{6,2},{8,12},{10,14},{12,8},{14,10},{16,20},{18,... | collective-permute-start | bytes 786440 | tf_op jit(solution)/shard_map/ppermute | solution.py:546
  30.0 12.6 %collective-permute-start.6 = (bf16[128,1024]{1,0:T(8,128)(2,1)S(1)}, bf16[128,1024]{1,0:T(8,128)(2,1)S(1)}, u32[]{:S(2)}, u32[]{:S(2)}) collective-permute-start(bf16[128,1024]{1,0:T(8,128)(2,1)S(1)} %get-tuple-element.64), channel_id=1, source_target_pairs={{0,6},{2,4},{4,2},{6,0},{8,14},{10,12},{12,10},{14,8},{16,22},{18,... | collective-permute-start | bytes 786440 | tf_op jit(solution)/shard_map/ppermute | solution.py:546
  40.6 8.3 %collective-permute-start.12 = (bf16[256,512]{1,0:T(8,128)(2,1)S(1)}, bf16[256,512]{1,0:T(8,128)(2,1)S(1)}, u32[]{:S(2)}, u32[]{:S(2)}) collective-permute-start(bf16[256,512]{1,0:T(8,128)(2,1)S(1)} %collective-permute-done.10.refs_2_), channel_id=1, source_target_pairs={{8,0},{10,2},{12,4},{14,6},{16,24},{18,26},{20,28},{22,30},{9,1},{... | collective-permute-start | bytes 786440 | tf_op jit(solution)/shard_map/ppermute | solution.py:571
  41.8 7.0 %collective-permute-start.13 = (bf16[256,512]{1,0:T(8,128)(2,1)S(1)}, bf16[256,512]{1,0:T(8,128)(2,1)S(1)}, u32[]{:S(2)}, u32[]{:S(2)}) collective-permute-start(bf16[256,512]{1,0:T(8,128)(2,1)S(1)} %shard_map.94.refs_0_), channel_id=1, source_target_pairs={{8,16},{10,18},{12,20},{14,22},{16,8},{18,10},{20,12},{22,14},{9,1... | collective-permute-start | bytes 786440 | tf_op jit(solution)/shard_map/ppermute | solution.py:572
  43.1 5.8 %copy-start = (bf16[256,1024]{1,0:T(8,128)(2,1)S(1)}, bf16[256,1024]{1,0:T(8,128)(2,1)}, u32[]{:S(2)}) copy-start(bf16[256,1024]{1,0:T(8,128)(2,1)} %own_ref.1) | copy-start | bytes 1572868
  43.2 5.8 %copy-start.4 = (s32[8]{0:T(128)S(1)}, s32[8]{0:T(128)}, u32[]{:S(2)}) copy-start(s32[8]{0:T(128)} %len_ref.5) | copy-start | bytes 100
  43.2 5.7 %collective-permute-start.14 = (bf16[512,1024]{1,0:T(8,128)(2,1)S(1)}, bf16[512,1024]{1,0:T(8,128)(2,1)S(1)}, u32[]{:S(2)}, u32[]{:S(2)}) collective-permute-start(bf16[512,1024]{1,0:T(8,128)(2,1)S(1)} %get-tuple-element.76), channel_id=1, source_target_pairs={{0,1},{1,0},{2,3},{3,2},{4,5},{5,4},{6,7},{7,6},{8,9},{9,8},{10,11... | collective-permute-start | bytes 3145736 | tf_op jit(solution)/shard_map/ppermute | solution.py:552
  51.8 11.2 %copy-start.3 = (f32[1024]{0:T(1024)S(1)}, f32[1024]{0:T(1024)}, u32[]{:S(2)}) copy-start(f32[1024]{0:T(1024)} %param.14) | copy-start | bytes 12292
  51.8 12.1 %collective-permute-start.17 = (bf16[144,256]{1,0:T(8,128)(2,1)S(1)}, bf16[144,256]{1,0:T(8,128)(2,1)S(1)}, u32[]{:S(2)}, u32[]{:S(2)}) collective-permute-start(bf16[144,256]{1,0:T(8,128)(2,1)S(1)} %get-tuple-element.88), channel_id=1, source_target_pairs={{0,24},{2,26},{4,28},{6,30},{1,25},{3,27},{5,29},{7,31}} | collective-permute-start | bytes 221192 | tf_op jit(solution)/shard_map/ppermute | solution.py:549
  56.9 7.0 %collective-permute-start.16 = (bf16[144,256]{1,0:T(8,128)(2,1)S(1)}, bf16[144,256]{1,0:T(8,128)(2,1)S(1)}, u32[]{:S(2)}, u32[]{:S(2)}) collective-permute-start(bf16[144,256]{1,0:T(8,128)(2,1)S(1)} %get-tuple-element.88), channel_id=1, source_target_pairs={{0,16},{2,18},{4,20},{6,22},{8,24},{10,26},{12,28},{14,30},{1,17},... | collective-permute-start | bytes 221192 | tf_op jit(solution)/shard_map/ppermute | solution.py:549
  59.7 4.1 %collective-permute-start.15 = (bf16[144,256]{1,0:T(8,128)(2,1)S(1)}, bf16[144,256]{1,0:T(8,128)(2,1)S(1)}, u32[]{:S(2)}, u32[]{:S(2)}) collective-permute-start(bf16[144,256]{1,0:T(8,128)(2,1)S(1)} %get-tuple-element.88), channel_id=1, source_target_pairs={{0,8},{2,10},{4,12},{6,14},{8,16},{10,18},{12,20},{14,22},{16,24},... | collective-permute-start | bytes 221192 | tf_op jit(solution)/shard_map/ppermute | solution.py:549
  63.8 0.9 %copy-start.1 = (f32[31,1024]{1,0:T(8,128)S(1)}, f32[31,1024]{1,0:T(8,128)}, u32[]{:S(2)}) copy-start(f32[31,1024]{1,0:T(8,128)} %taps_ref.3) | copy-start | bytes 380932
  64.5 7.4 %collective-permute-start.19 = (bf16[512,256]{1,0:T(8,128)(2,1)S(1)}, bf16[512,256]{1,0:T(8,128)(2,1)S(1)}, u32[]{:S(2)}, u32[]{:S(2)}) collective-permute-start(bf16[512,256]{1,0:T(8,128)(2,1)S(1)} %get-tuple-element.92), channel_id=1, source_target_pairs={{0,1},{1,0},{2,3},{3,2},{4,5},{5,4},{6,7},{7,6},{8,9},{9,8},{10,11... | collective-permute-start | bytes 786440 | tf_op jit(solution)/shard_map/ppermute | solution.py:552
  66.4 5.5 %collective-permute-start.18 = (bf16[256,256]{1,0:T(8,128)(2,1)S(1)}, bf16[256,256]{1,0:T(8,128)(2,1)S(1)}, u32[]{:S(2)}, u32[]{:S(2)}) collective-permute-start(bf16[256,256]{1,0:T(8,128)(2,1)S(1)} %shard_map.100.refs_0_), channel_id=1, source_target_pairs={{0,1},{1,0},{2,3},{3,2},{4,5},{5,4},{6,7},{7,6},{8,9},{9,8},{10,11... | collective-permute-start | bytes 393224 | tf_op jit(solution)/shard_map/ppermute | solution.py:552
  72.3 2.7 %collective-permute-start.20 = (bf16[768,256]{1,0:T(8,128)(2,1)S(1)}, bf16[768,256]{1,0:T(8,128)(2,1)S(1)}, u32[]{:S(2)}, u32[]{:S(2)}) collective-permute-start(bf16[768,256]{1,0:T(8,128)(2,1)S(1)} %shard_map.101.refs_0_), channel_id=1, source_target_pairs={{0,1},{1,0},{2,3},{3,2},{4,5},{5,4},{6,7},{7,6},{8,9},{9,8},{10,11... | collective-permute-start | bytes 1179656 | tf_op jit(solution)/shard_map/ppermute | solution.py:552
  72.5 10.1 %collective-permute-start.21 = (bf16[256,512]{1,0:T(8,128)(2,1)S(1)}, bf16[256,512]{1,0:T(8,128)(2,1)S(1)}, u32[]{:S(2)}, u32[]{:S(2)}) collective-permute-start(bf16[256,512]{1,0:T(8,128)(2,1)S(1)} %shard_map.102), channel_id=1, source_target_pairs={{0,6},{2,4},{4,2},{6,0},{8,14},{10,12},{12,10},{14,8},{16,22},{18,... | collective-permute-start | bytes 786440 | tf_op jit(solution)/shard_map/ppermute | solution.py:546
  75.6 12.1 %collective-permute-start.22 = (bf16[256,512]{1,0:T(8,128)(2,1)S(1)}, bf16[256,512]{1,0:T(8,128)(2,1)S(1)}, u32[]{:S(2)}, u32[]{:S(2)}) collective-permute-start(bf16[256,512]{1,0:T(8,128)(2,1)S(1)} %get-tuple-element.101), channel_id=1, source_target_pairs={{0,2},{2,0},{4,6},{6,4},{8,10},{10,8},{12,14},{14,12},{16,18},{18,... | collective-permute-start | bytes 786440 | tf_op jit(solution)/shard_map/ppermute | solution.py:546
  76.2 11.5 %collective-permute-start.23 = (bf16[256,512]{1,0:T(8,128)(2,1)S(1)}, bf16[256,512]{1,0:T(8,128)(2,1)S(1)}, u32[]{:S(2)}, u32[]{:S(2)}) collective-permute-start(bf16[256,512]{1,0:T(8,128)(2,1)S(1)} %get-tuple-element.102), channel_id=1, source_target_pairs={{0,4},{2,6},{4,0},{6,2},{8,12},{10,14},{12,8},{14,10},{16,20},{18,... | collective-permute-start | bytes 786440 | tf_op jit(solution)/shard_map/ppermute | solution.py:546

commit v11 on v10

--- a/solution.py
+++ b/solution.py
@@ -13,6 +13,7 @@
 CONV_ROWS = 64
 BF16 = jnp.bfloat16
 F32 = jnp.float32
+STACK_HINT = 40_000_000_000
 INWARD_HINT = 40_000_000_000
 ASSEMBLE_HINT = 40_000_000_000
 ALL_VMEM_BYTES = 63 * 1024 * 1024
@@ -62,40 +63,29 @@
         dest_ref[pl.ds(pl.multiple_of((plane ^ offset) * rows, rows), rows), : value.shape[1]] = value
 
 
-def first_kernel(group, planes, log_decay_ref, bc_ref, out_w_ref, frames_ref, *refs):
-    weight_refs, refs = refs[:2], refs[2:]
+def first_kernel(group, planes, log_decay_ref, bc_ref, frames_ref, *refs):
+    weight_refs, refs = refs[:3], refs[3:]
     inner_refs, outer_refs, refs = refs[:group], refs[group : group + planes], refs[group + planes :]
-    bc_half_ref, out_copy_ref, edge_ref, decay_ref, sems = refs
+    bc_half_ref, edge_ref, decay_ref, sems = refs
     place, plane = plane_place(group)
     parity = lax.rem(lax.axis_index("head"), 2)
     width = weight_refs[0].shape[1] // group
     frames = frames_ref.shape[0]
     heads = log_decay_ref.shape[0] // group
-    half = frames // 2
-    fold = inner_refs[0].shape[1] // (2 * width)
-    height = weight_refs[0].shape[0] // fold
     copies = [
-        (out_w_ref, out_copy_ref),
         (bc_ref.at[:, pl.ds(pl.multiple_of(parity * LANES, LANES), LANES)], bc_half_ref),
         (frames_ref.at[:EDGE, :], edge_ref.at[0]),
         (frames_ref.at[frames - EDGE :, :], edge_ref.at[1]),
         (log_decay_ref, decay_ref),
     ]
     for step, inner_ref in enumerate(inner_refs):
-        top = inner_ref.shape[0] - height
         lanes = pl.ds(pl.multiple_of((place ^ step) * width, LANES), width)
         for number, weight_ref in enumerate(weight_refs):
-            for part in range(fold):
-                at = (2 * part + number) * width
-                source = weight_ref.at[part * height : (part + 1) * height, lanes]
-                copies.append((source, inner_ref.at[top:, at : at + width]))
-        if step:
-            source = frames_ref.at[pl.ds(pl.multiple_of(parity * half, half), half), :]
-            copies.append((source, inner_ref.at[:half, : frames_ref.shape[1]]))
+            copies.append((weight_ref.at[:, lanes], inner_ref.at[:, number * width : (number + 1) * width]))
     started = [pltpu.make_async_copy(a, b, sems.at[number]) for number, (a, b) in enumerate(copies)]
     for copy in started:
         copy.start()
-    for copy in started[:5]:
+    for copy in started[:4]:
         copy.wait()
     lane = lax.broadcasted_iota(jnp.int32, (8, LANES), 1)
     decays = []
@@ -110,25 +100,25 @@
                 rows[slot // 8] = jnp.where(lane // EDGE == slot % 8, moved, rows[slot // 8])
         decays.append(jnp.concatenate(rows, axis=0))
     for step, out_ref in enumerate(outer_refs):
-        number = put(out_ref, 0, out_copy_ref[...])
-        number = put(out_ref, number, bc_half_ref[...])
+        number = put(out_ref, 0, bc_half_ref[...])
         later = (plane ^ step) > plane
         number = put(out_ref, number, jnp.where(later, edge_ref[1].astype(F32), edge_ref[0].astype(F32)).astype(BF16))
         put(out_ref, number, jnp.where(later, decays[1], decays[0]).astype(BF16))
-    for copy in started[5:]:
+    for copy in started[4:]:
         copy.wait()
 
 
 def stack_kernel(group, *refs):
-    parts, stack_ref = refs[:group], refs[group]
+    parts, stack_refs = refs[:group], refs[group:]
     place, _ = plane_place(group)
-    width = stack_ref.shape[1]
-    height = parts[0].shape[0]
-    fold = parts[0].shape[1] // width
+    rows = parts[0].shape[0]
     for step, part in enumerate(parts):
-        for number in range(fold):
-            at = pl.multiple_of(((place ^ step) * fold + number) * height, 16)
-            stack_ref[pl.ds(at, height), :] = part[part.shape[0] - height :, number * width : (number + 1) * width]
+        at = pl.ds(pl.multiple_of((place ^ step) * rows, rows), rows)
+        first = 0
+        for stack_ref in stack_refs:
+            width = stack_ref.shape[1]
+            stack_ref[at, :] = part[:, first : first + width]
+            first += width
 
 
 def assemble_kernel(group, offsets, *refs):
@@ -162,70 +152,54 @@
     return terms
 
 
-def inward_kernel(group, planes, rows, channels, decay_ref, *refs):
-    piece_refs, out_refs, whole_ref = refs[: -group - 1], refs[-group - 1 : -1], refs[-1]
+def inward_kernel(group, rows, decay_ref, frames_ref, *refs):
+    piece_refs, out_refs = refs[:-group], refs[-group:]
     place, plane = plane_place(group)
-    width = channels // group
-    if len(piece_refs) > planes:
-        whole_ref[...] = piece_refs[-2][...] + piece_refs[-1][...]
-        piece_refs = [*piece_refs[: planes - 1], whole_ref]
+    planes = len(piece_refs)
+    half = frames_ref.shape[0] // 2
+    mine = pl.ds(pl.multiple_of(lax.rem(lax.axis_index("head"), 2) * half, half), half)
     wanted = jnp.clip(jnp.where(place == 0, plane + 1, plane - 1), 0, planes - 1)
-    depth_tiles = out_refs[0].shape[1] // LANES
-    across, down = channels // LANES, rows // 16
+    depth_tiles = frames_ref.shape[1] // LANES
+    down = rows // 16
     for step, out_ref in enumerate(out_refs):
-        block = place ^ step
-        number = 0
+        out_ref[:half, :] = frames_ref[mine, :]
+        number = half // 16 * depth_tiles
         for piece_ref in piece_refs:
             for at in range(down):
-                for lane in range(width // LANES):
-                    if across == 8:
-                        lanes = pl.ds(pl.multiple_of(block * width + lane * LANES, LANES), LANES)
-                        out_ref[tile(number)] = piece_ref[at * 16 : at * 16 + 16, lanes]
-                    else:
-                        value = piece_ref[tile(at * across + lane)]
-                        for other in range(1, group):
-                            there = piece_ref[tile(at * across + other * (width // LANES) + lane)]
-                            value = jnp.where(block == other, there, value)
-                        out_ref[tile(number)] = value
-                    number += 1
-            for at in range(down):
-                out_ref[tile(number)] = piece_ref[tile(down * across + at)]
+                out_ref[tile(number)] = piece_ref[tile(at)]
                 number += 1
         for offset, piece_ref in enumerate(piece_refs):
 
             @pl.when((plane ^ offset) == wanted)
-            def _(piece_ref=piece_ref, number=number):
+            def _(piece_ref=piece_ref, number=number, out_ref=out_ref):
                 for at in range(depth_tiles + 1):
-                    out_ref[tile(number + at)] = piece_ref[tile(down * (across + 1) + at)]
+                    out_ref[tile(number + at)] = piece_ref[tile(down + at)]
 
         number += depth_tiles + 1
-        terms = three_terms(decay_ref[block])
+        terms = three_terms(decay_ref[place ^ step])
         terms = jnp.concatenate([*terms, jnp.zeros_like(terms[0])], axis=0).astype(BF16)
         for span in range(terms.shape[1] // SPAN):
             number = put(out_ref, number, terms[:, span * SPAN : (span + 1) * SPAN])
 
 
 def swap_kernel(group, rows, *refs):
-    part_refs, half_refs = refs[:group], refs[group : 2 * group - 1]
-    swap_ref, bc_ref, halo_ref, decay_ref, own_out_ref, other_out_ref, out_ref, span_ref = refs[2 * group - 1 :]
+    part_refs, (swap_ref, bc_ref, halo_ref, decay_ref, span_ref) = refs[:group], refs[group:]
+    half_refs = part_refs[1:]
     place, plane = plane_place(group)
     planes = bc_ref.shape[0] // (group * rows)
-    width = out_ref.shape[1]
     count = span_ref.shape[0]
     spans = count // group
     down = rows // 16
     depth_tiles = swap_ref.shape[1] // LANES
+    height = LANES
+    top = swap_ref.shape[0] - height
+    half = top // len(half_refs)
     lane = lax.broadcasted_iota(jnp.int32, (8, LANES), 1)
     for step, part_ref in enumerate(part_refs):
         block = place ^ step
-        number = 0
+        number = half // 16 * depth_tiles
         for offset in range(planes):
             first = ((plane ^ offset) * group + block) * rows
-            for at in range(down):
-                for column in range(width // LANES):
-                    lanes = slice(column * LANES, (column + 1) * LANES)
-                    out_ref[pl.ds(pl.multiple_of(first + at * 16, 16), 16), lanes] = part_ref[tile(number)]
-                    number += 1
             for at in range(down):
                 bc_ref[pl.ds(pl.multiple_of(first + at * 16, 16), 16), :] = part_ref[tile(number)]
                 number += 1
@@ -252,25 +226,16 @@
 
         number += depth_tiles + 1
         for span in range(spans):
-            top = part_ref[tile(number)].astype(F32)
-            bottom = part_ref[tile(number + 1)].astype(F32)
+            upper = part_ref[tile(number)].astype(F32)
+            lower = part_ref[tile(number + 1)].astype(F32)
             number += 2
-            span_ref[block * spans + span] = top[:8] + top[8:] + bottom[:8]
+            span_ref[block * spans + span] = upper[:8] + upper[8:] + lower[:8]
     for span in range(count):
         moved = pltpu.roll(span_ref[span], EDGE, 1)
         here, after = slice(span * 8, span * 8 + 8), slice(span * 8 + 8, span * 8 + 16)
         decay_ref[here, :] = jnp.where(lane < EDGE, decay_ref[here, :], moved)
         kept = decay_ref[after, :] if span == count - 1 else jnp.zeros((8, LANES), F32)
         decay_ref[after, :] = jnp.where(lane < EDGE, moved, kept)
-    core = lax.axis_index("head")
-    share = own_out_ref.shape[0]
-    own_out_ref[...] = out_ref[pl.ds(pl.multiple_of(core * share, share), share), :]
-    for step in range(1, other_out_ref.shape[0] // share + 1):
-        at = pl.ds(pl.multiple_of((core ^ step) * share, share), share)
-        other_out_ref[(step - 1) * share : step * share, :] = out_ref[at, :]
-    height = LANES
-    top = swap_ref.shape[0] - height
-    half = top // len(half_refs)
     for number, half_ref in enumerate(half_refs):
         swap_ref[number * half : (number + 1) * half, :] = half_ref[:half, : swap_ref.shape[1]]
     for number in range(bc_ref.shape[0] // height):
@@ -421,6 +386,17 @@
     out_ref[wide:, :] = jnp.zeros((rows_all - wide, width), F32)
 
 
+def share_kernel(cores, offsets, group, *refs):
+    pieces, refs = refs[: len(offsets)], refs[len(offsets) :]
+    outs, weight_ref = refs[:cores], refs[cores]
+    _, plane = plane_place(group)
+    core = lax.axis_index("head")
+    fill_planes(plane, weight_ref, pieces, offsets)
+    for step, out_ref in enumerate(outs):
+        rows = out_ref.shape[0]
+        out_ref[...] = weight_ref[pl.ds(pl.multiple_of((core ^ step) * rows, rows), rows), :]
+
+
 def gate_kernel(heads, state, c_ref, y_ref, step_ref, carry_ref, keep_ref, silu_ref, *refs):
     earlier, gated_ref = refs[:-1], refs[-1]
     total, width = y_ref.shape
@@ -574,24 +550,19 @@
 
     offsets = (0, 1, 2, 3, 3) if planes == 4 else tuple(range(planes))
     half_count = frame_count // 2
-    down, across_tiles, depth_tiles = rows // 16, channels // LANES, depth // LANES
-    tiles = down * (across_tiles + 1) + depth_tiles + 1
-    fold = max(1, min(depth // (2 * width), down))
-    inner_shape = (half_count + rows // fold, max(depth, fold * 2 * width))
+    down, depth_tiles = rows // 16, depth // LANES
     payloads = call(
         functools.partial(first_kernel, group, planes),
         (
-            shape((rows // fold, fold * 2 * width), BF16),
-            *(shape(inner_shape, BF16) for _ in range(1, group)),
-            *(shape((-(-tiles // 8) * 16, depth), BF16) for _ in range(planes)),
+            *(shape((rows, 3 * width), BF16) for _ in range(group)),
+            *(shape((-(-(down + depth_tiles + 1) // 8) * 16, depth), BF16) for _ in range(planes)),
         ),
-        [log_decay, bc_weight, out_weight.T, frames, x_weight, z_weight],
+        [log_decay, bc_weight, frames, x_weight, z_weight, out_weight.T],
         [
             pltpu.VMEM((rows, LANES), BF16),
-            pltpu.VMEM((rows, channels), BF16),
             pltpu.VMEM((2, EDGE, depth), BF16),
             pltpu.VMEM(log_decay.shape, F32),
-            pltpu.SemaphoreType.DMA((4 + group * (2 * fold + 1),)),
+            pltpu.SemaphoreType.DMA((4 + 3 * group,)),
         ],
         smem=0,
         anywhere=6,
@@ -599,11 +570,12 @@
     )
     inner, outer = payloads[:group], payloads[group:]
     parts = [inner[0]] + [in_plane(inner[step], step) for step in range(1, group)]
-    pieces = along_planes(outer)
-    xz_stack = call(
+    pieces = [outer[0]] + [between_planes(outer[step], step) for step in range(1, planes)]
+    xz_stack, out_stack = call(
         functools.partial(stack_kernel, group),
-        shape((group * rows, 2 * width), BF16),
+        (shape((group * rows, 2 * width), BF16), shape((group * rows, width), BF16)),
         parts,
+        flops=STACK_HINT,
         smem=0,
     )
     xz_pieces = along_planes([xz_stack] * planes)
@@ -615,29 +587,25 @@
         smem=0,
     )
     decay_blocks = jnp.pad(log_decay.reshape(group, heads, frame_count), ((0, 0), (0, 8 - heads), (0, 0)))
-    tiles = planes * down * (width // LANES + 1) + depth_tiles + 1 + frame_count // SPAN * 2
+    tiles = planes * down + depth_tiles + 1 + frame_count // SPAN * 2
     inward = call(
-        functools.partial(inward_kernel, group, planes, rows, channels),
-        tuple(shape((-(-tiles // 8) * 16, depth), BF16) for _ in range(group)),
-        [decay_blocks, *pieces],
-        [pltpu.VMEM(pieces[0].shape, BF16)],
+        functools.partial(inward_kernel, group, rows),
+        tuple(shape((half_count + -(-tiles // 8) * 16, depth), BF16) for _ in range(group)),
+        [decay_blocks, frames, *pieces],
         flops=INWARD_HINT,
         smem=0,
     )
     inward = [inward[0]] + [in_plane(inward[step], step) for step in range(1, group)]
-    share = depth // cores
-    swap, bc_mine, halo, decay, *out_parts = call(
+    swap, bc_mine, halo, decay = call(
         functools.partial(swap_kernel, group, rows),
         (
             shape(((group - 1) * half_count + LANES, depth), BF16),
             shape((depth, LANES), BF16),
             shape((2 * EDGE, depth), BF16),
             shape((count * 8 + 8, SPAN), F32),
-            shape((share, width), BF16),
-            shape(((cores - 1) * share, width), BF16),
         ),
-        [*inward, *parts[1:]],
-        [pltpu.VMEM((depth, width), BF16), pltpu.VMEM((count, 8, SPAN), F32)],
+        inward,
+        [pltpu.VMEM((count, 8, SPAN), F32)],
         smem=0,
     )
     swap = across(swap, 1)
@@ -655,7 +623,7 @@
             shape((-(-count // 8) * 8, width), F32),
             shape((state + EDGE, width), BF16),
         ),
-        [record_lengths, decay, x_columns, bc_mine, frames, swap, halo, *parts[1:]],
+        [record_lengths, decay, x_columns, bc_mine, frames, swap, halo, *inward[1:]],
         [pltpu.VMEM((depth, 2 * state), BF16), pltpu.VMEM((total, width), F32)],
         flops=2 * total * depth * (width + 2 * state),
     )
@@ -674,6 +642,8 @@
         flops=2 * total * depth * width,
         smem=0,
     )
+    out_stack, summaries, y, silu = lax.optimization_barrier((out_stack, summaries, y, silu))
+    out_pieces = [out_stack] + [between_planes(out_stack, step) for step in range(1, planes)]
     gated = call(
         functools.partial(gate_kernel, heads, state),
         shape((all_rows, width), BF16),
@@ -704,13 +674,18 @@
 
     far_act = conv(far, gated)
     far_swapped = [across(far_act, step) for step in range(1, cores)]
-    own_out, other_out = out_parts
-    other_out, gated = lax.optimization_barrier((other_out, gated))
-    out_parts = [own_out]
-    for step in range(1, cores):
-        out_parts.append(across(other_out[(step - 1) * share : step * share], step))
     gated, far_act = lax.optimization_barrier((gated, far_act))
     near_act = conv(near, gated)
+    near_act, out_pieces = lax.optimization_barrier((near_act, out_pieces))
+    share = depth // cores
+    out_parts = call(
+        functools.partial(share_kernel, cores, tuple(range(planes)), group),
+        tuple(shape((share, width), BF16) for _ in range(cores)),
+        out_pieces,
+        [pltpu.VMEM((depth, width), BF16)],
+        smem=0,
+    )
+    out_parts = [out_parts[0]] + [across(out_parts[step], step) for step in range(1, cores)]
     near_act, far_swapped, out_parts = lax.optimization_barrier((near_act, far_swapped, out_parts))
     (far_out,) = out(far, far_act, far_swapped)
     near_act, far_out = lax.optimization_barrier((near_act, far_out))

time: 88.9 us -> 85.7 us (0.964)
  waiting for transfers between devices: 35.8 us -> 30.7 us
  starting transfers between devices: 32.2 us -> 34 us
    ppermute x4 -> x8, starting transfers between devices: 6.56 us -> 13.4 us  [between_planes(): lax.ppermute(array, 'tm', [(i, i ^ step * group) for i in range(times)])]
    ppermute x2 -> x1, waiting for transfers between devices: 5.57 us -> 0.01 us  [along_planes(): third = lax.ppermute(again, 'tm', pairs([(1, 0), (2, 3)]))]
    ppermute x4 -> x8, waiting for transfers between devices: 13.7 us -> 9.57 us  [between_planes(): lax.ppermute(array, 'tm', [(i, i ^ step * group) for i in range(times)])]
    ppermute x4, waiting for transfers between devices: 0.01 us -> 3.88 us  [across(): return lax.ppermute(array, 'head', [(i, i ^ step) for i in range(cores)])]
    ppermute x3, starting transfers between devices: 9.25 us -> 6.15 us  [later(): lax.ppermute(array, 'tm', [(i, i + step * group) for i in range(times - s...]
    ppermute x2 -> x1, starting transfers between devices: 2.56 us -> 1.28 us  [along_planes(): third = lax.ppermute(again, 'tm', pairs([(1, 0), (2, 3)]))]
    pallas_call x13 -> x14, Pallas kernels: 17.6 us -> 17.7 us  [call(): pl.pallas_call(kernel, out_shape=out_shape, in_specs=in_specs, out_specs=...]
  transfers between devices with their start and end apart: 24 -> 26, of which waited for: 9 -> 12; matrix products, arithmetic and copies ran while one was open for 1% -> 1% of each run, Pallas kernels for 12% -> 15%
where the time goes in v11:
time: 85.7 us; the launch traced here: 85.3 us
  starting transfers between devices  34 us (40%)
  waiting for transfers between devices  30.7 us (36%)
  Pallas kernels  17.7 us (21%)
  local copies, waits for them, and re-layouts  1.85 us (2%)
    pallas_call x14, Pallas kernels, call(): pl.pallas_call(kernel, out_shape=out_shape, in_specs=in_specs, out_specs=...  17.7 us
    ppermute x9, waiting for transfers between devices, in_plane(): return lax.ppermute(array, 'tm', [(i, i ^ step) for i in range(times)])  17.2 us
    ppermute x8, starting transfers between devices, between_planes(): lax.ppermute(array, 'tm', [(i, i ^ step * group) for i in range(times)])  13.4 us
    ppermute x9, starting transfers between devices, in_plane(): return lax.ppermute(array, 'tm', [(i, i ^ step) for i in range(times)])  11.6 us
    ppermute x8, waiting for transfers between devices, between_planes(): lax.ppermute(array, 'tm', [(i, i ^ step * group) for i in range(times)])  9.57 us
    ppermute x3, starting transfers between devices, later(): lax.ppermute(array, 'tm', [(i, i + step * group) for i in range(times - s...  6.15 us
    ppermute x4, waiting for transfers between devices, across(): return lax.ppermute(array, 'head', [(i, i ^ step) for i in range(cores)])  3.88 us
  transfers between devices with their start and end apart: 26, of which 12 were waited for; matrix products, arithmetic and copies ran while one was open for 1% of the time, Pallas kernels for 15%

profile of v11, /device:TPU:0, one launch (start us, length us, event | category | flops | bytes accessed | tf_op | source)
XLA Modules:
  0.0 85.3 jit_solution(5890402146050901759)
XLA Ops:
  0.0 2.0 %shard_map.91 = (bf16[64,768]{1,0:T(8,128)(2,1)}, bf16[64,768]{1,0:T(8,128)(2,1)}, bf16[64,768]{1,0:T(8,128)(2,1)}, bf16[64,768]{1,0:T(8,128)(2,1)}, bf16[32,102...) custom-call(f32[16,256]{1,0:T(8,128)} %log_decay_ref.1, ...), custom_call_target="tpu_custom_call" | custom-call | bytes 1622016 | tf_op jit(solution)/shard_map/pallas_call | solution.py:33
  2.0 3.0 %collective-permute-start.6 = (bf16[64,768]{1,0:T(8,128)(2,1)}, bf16[64,768]{1,0:T(8,128)(2,1)S(1)}, u32[]{:S(2)}, u32[]{:S(2)}) collective-permute-start(bf16[64,768]{1,0:T(8,128)(2,1)} %get-tuple-element.72), channel_id=1, source_target_pairs={{0,2},{2,0},{4,6},{6,4},{8,10},{10,8},{12,14},{14,12},{16,18},{18,... | collective-permute-start | bytes 294920 | tf_op jit(solution)/shard_map/ppermute | solution.py:522
  5.0 1.5 %collective-permute-start.7 = (bf16[64,768]{1,0:T(8,128)(2,1)}, bf16[64,768]{1,0:T(8,128)(2,1)S(1)}, u32[]{:S(2)}, u32[]{:S(2)}) collective-permute-start(bf16[64,768]{1,0:T(8,128)(2,1)} %get-tuple-element.73), channel_id=1, source_target_pairs={{0,4},{2,6},{4,0},{6,2},{8,12},{10,14},{12,8},{14,10},{16,20},{18,... | collective-permute-start | bytes 294920 | tf_op jit(solution)/shard_map/ppermute | solution.py:522
  6.5 2.0 %collective-permute-start = (bf16[32,1024]{1,0:T(8,128)(2,1)}, bf16[32,1024]{1,0:T(8,128)(2,1)S(1)}, u32[]{:S(2)}, u32[]{:S(2)}) collective-permute-start(bf16[32,1024]{1,0:T(8,128)(2,1)} %get-tuple-element.63), channel_id=1, source_target_pairs={{0,8},{2,10},{4,12},{6,14},{8,0},{10,2},{12,4},{14,6},{16,24},{18,... | collective-permute-start | bytes 196616 | tf_op jit(solution)/shard_map/ppermute | solution.py:531
  8.5 2.6 %collective-permute-start.1 = (bf16[32,1024]{1,0:T(8,128)(2,1)}, bf16[32,1024]{1,0:T(8,128)(2,1)S(1)}, u32[]{:S(2)}, u32[]{:S(2)}) collective-permute-start(bf16[32,1024]{1,0:T(8,128)(2,1)} %get-tuple-element.64), channel_id=1, source_target_pairs={{0,16},{2,18},{4,20},{6,22},{8,24},{10,26},{12,28},{14,30},{16,0},... | collective-permute-start | bytes 196616 | tf_op jit(solution)/shard_map/ppermute | solution.py:531
  11.1 0.7 reshape.3
  12.0 0.2 collective-permute-done.8.refs_3_
  12.2 0.9 %copy-done.4 = bf16[64,768]{1,0:T(8,128)(2,1)S(1)} copy-done((bf16[64,768]{1,0:T(8,128)(2,1)S(1)}, bf16[64,768]{1,0:T(8,128)(2,1)}, u32[]{:S(2)}) %copy-start.4) | copy-done | bytes 98328
  13.2 1.6 %collective-permute-start.10 = (bf16[256,512]{1,0:T(8,128)(2,1)S(1)}, bf16[256,512]{1,0:T(8,128)(2,1)S(1)}, u32[]{:S(2)}, u32[]{:S(2)}) collective-permute-start(bf16[256,512]{1,0:T(8,128)(2,1)S(1)} %get-tuple-element.78.refs_0_), channel_id=1, source_target_pairs={{0,8},{2,10},{4,12},{6,14},{8,0},{10,2},{12,4},{14,6},{16,24},{18,... | collective-permute-start | bytes 786440 | tf_op jit(solution)/shard_map/ppermute | solution.py:531
  14.8 2.6 %collective-permute-start.9 = (bf16[256,512]{1,0:T(8,128)(2,1)S(1)}, bf16[256,512]{1,0:T(8,128)(2,1)S(1)}, u32[]{:S(2)}, u32[]{:S(2)}) collective-permute-start(bf16[256,512]{1,0:T(8,128)(2,1)S(1)} %get-tuple-element.78.refs_0_), channel_id=1, source_target_pairs={{0,16},{2,18},{4,20},{6,22},{8,24},{10,26},{12,28},{14,30},{16,0},... | collective-permute-start | bytes 786440 | tf_op jit(solution)/shard_map/ppermute | solution.py:531
  17.4 1.6 %collective-permute-done.2.refs_3_ = bf16[32,1024]{1,0:T(8,128)(2,1)S(1)} collective-permute-done((bf16[32,1024]{1,0:T(8,128)(2,1)}, bf16[32,1024]{1,0:T(8,128)(2,1)S(1)}, u32[]{:S(2)}, u32[]{:S(2)}) %collective-permute-start.2) | collective-permute-done | bytes 65568 | tf_op jit(solution)/shard_map/ppermute | solution.py:531
  19.0 0.2 shard_map.92
  19.2 1.6 %collective-permute-start.3 = (bf16[192,1024]{1,0:T(8,128)(2,1)S(1)}, bf16[192,1024]{1,0:T(8,128)(2,1)S(1)}, u32[]{:S(2)}, u32[]{:S(2)}) collective-permute-start(bf16[192,1024]{1,0:T(8,128)(2,1)S(1)} %get-tuple-element.67), channel_id=1, source_target_pairs={{0,2},{2,0},{4,6},{6,4},{8,10},{10,8},{12,14},{14,12},{16,18},{18,... | collective-permute-start | bytes 1179656 | tf_op jit(solution)/shard_map/ppermute | solution.py:522
  20.8 1.5 %collective-permute-start.4 = (bf16[192,1024]{1,0:T(8,128)(2,1)S(1)}, bf16[192,1024]{1,0:T(8,128)(2,1)S(1)}, u32[]{:S(2)}, u32[]{:S(2)}) collective-permute-start(bf16[192,1024]{1,0:T(8,128)(2,1)S(1)} %get-tuple-element.68), channel_id=1, source_target_pairs={{0,4},{2,6},{4,0},{6,2},{8,12},{10,14},{12,8},{14,10},{16,20},{18,... | collective-permute-start | bytes 1179656 | tf_op jit(solution)/shard_map/ppermute | solution.py:522
  22.3 0.5 collective-permute-start.5
  22.7 4.0 %collective-permute-done.10.refs_1_ = bf16[256,512]{1,0:T(8,128)(2,1)S(1)} collective-permute-done((bf16[256,512]{1,0:T(8,128)(2,1)S(1)}, bf16[256,512]{1,0:T(8,128)(2,1)S(1)}, u32[]{:S(2)}, u32[]{:S(2)}) %collective-permute-start.10) | collective-permute-done | bytes 262176 | tf_op jit(solution)/shard_map/ppermute | solution.py:531
  26.8 1.7 %collective-permute-done.9.refs_2_ = bf16[256,512]{1,0:T(8,128)(2,1)S(1)} collective-permute-done((bf16[256,512]{1,0:T(8,128)(2,1)S(1)}, bf16[256,512]{1,0:T(8,128)(2,1)S(1)}, u32[]{:S(2)}, u32[]{:S(2)}) %collective-permute-start.9) | collective-permute-done | bytes 262176 | tf_op jit(solution)/shard_map/ppermute | solution.py:531
  28.5 1.3 %collective-permute-start.11 = (bf16[256,512]{1,0:T(8,128)(2,1)S(1)}, bf16[256,512]{1,0:T(8,128)(2,1)S(1)}, u32[]{:S(2)}, u32[]{:S(2)}) collective-permute-start(bf16[256,512]{1,0:T(8,128)(2,1)S(1)} %collective-permute-done.9.refs_2_), channel_id=1, source_target_pairs={{8,0},{10,2},{12,4},{14,6},{16,24},{18,26},{20,28},{22,30},{9,1},{... | collective-permute-start | bytes 786440 | tf_op jit(solution)/shard_map/ppermute | solution.py:547
  29.8 0.7 collective-permute-start.12
  30.5 0.7 collective-permute-done.3.refs_1_.refs_0_
  31.1 5.4 %collective-permute-done.4.refs_2_.refs_1_ = bf16[192,1024]{1,0:T(8,128)(2,1)S(1)} collective-permute-done((bf16[192,1024]{1,0:T(8,128)(2,1)S(1)}, bf16[192,1024]{1,0:T(8,128)(2,1)S(1)}, u32[]{:S(2)}, u32[]{:S(2)}) %collective-permute-start.4) | collective-permute-done | bytes 393248 | tf_op jit(solution)/shard_map/ppermute | solution.py:522
  36.6 0.5 shard_map.93
  37.3 2.5 %collective-permute-done.13.swap_ref = bf16[512,1024]{1,0:T(8,128)(2,1)S(1)} collective-permute-done((bf16[512,1024]{1,0:T(8,128)(2,1)S(1)}, bf16[512,1024]{1,0:T(8,128)(2,1)S(1)}, u32[]{:S(2)}, u32[]{:S(2)}) %collective-permute-start.13) | collective-permute-done | bytes 1048608 | tf_op jit(solution)/shard_map/ppermute | solution.py:528
  39.8 2.8 %shard_map.96 = (bf16[1152,1024]{1,0:T(8,128)(2,1)S(1)}, bf16[1152,256]{1,0:T(8,128)(2,1)S(1)}, bf16[1152,128]{1,0:T(8,128)(2,1)S(1)}, bf16[1152,128]{1,0:T(8,12...) custom-call(s32[8]{0:T(128)S(1)} %copy-done.3, ...), custom_call_target="tpu_custom_call" | custom-call | flops 1073741824 | bytes 8421408 | tf_op jit(solution)/shard_map/pallas_call | solution.py:33
  42.6 2.4 %collective-permute-start.16 = (bf16[144,256]{1,0:T(8,128)(2,1)S(1)}, bf16[144,256]{1,0:T(8,128)(2,1)S(1)}, u32[]{:S(2)}, u32[]{:S(2)}) collective-permute-start(bf16[144,256]{1,0:T(8,128)(2,1)S(1)} %get-tuple-element.85), channel_id=1, source_target_pairs={{0,24},{2,26},{4,28},{6,30},{1,25},{3,27},{5,29},{7,31}} | collective-permute-start | bytes 221192 | tf_op jit(solution)/shard_map/ppermute | solution.py:525
  45.0 1.8 %collective-permute-start.15 = (bf16[144,256]{1,0:T(8,128)(2,1)S(1)}, bf16[144,256]{1,0:T(8,128)(2,1)S(1)}, u32[]{:S(2)}, u32[]{:S(2)}) collective-permute-start(bf16[144,256]{1,0:T(8,128)(2,1)S(1)} %get-tuple-element.85), channel_id=1, source_target_pairs={{0,16},{2,18},{4,20},{6,22},{8,24},{10,26},{12,28},{14,30},{1,17},... | collective-permute-start | bytes 221192 | tf_op jit(solution)/shard_map/ppermute | solution.py:525
  46.8 1.9 %collective-permute-start.14 = (bf16[144,256]{1,0:T(8,128)(2,1)S(1)}, bf16[144,256]{1,0:T(8,128)(2,1)S(1)}, u32[]{:S(2)}, u32[]{:S(2)}) collective-permute-start(bf16[144,256]{1,0:T(8,128)(2,1)S(1)} %get-tuple-element.85), channel_id=1, source_target_pairs={{0,8},{2,10},{4,12},{6,14},{8,16},{10,18},{12,20},{14,22},{16,24},... | collective-permute-start | bytes 221192 | tf_op jit(solution)/shard_map/ppermute | solution.py:525
  48.8 1.9 %shard_map.97 = (f32[1152,256]{1,0:T(8,128)S(1)}, f32[1152,256]{1,0:T(8,128)S(1)}) custom-call(bf16[1152,256]{1,0:T(8,128)(2,1)S(1)} %get-tuple-element.86.x_ref, bf16[1152,128]{1,0:T(8,128)(2,1)S(1)} %get-tuple-element.87.b_ref, bf16[1152,128]{1,0:T(8,128)(2,1)S(1)} %get-tuple-element.83.c_ref, f32[216,128]{1,0:T(8,128)S(1)} %get-tuple-element.88.rows_ref), custom_call_target="tpu_custom_call" | custom-call | flops 134217728 | bytes 3649536 | tf_op jit(solution)/shard_map/pallas_call | solution.py:33
  50.7 0.9 %shard_map.98.silu_ref = f32[1152,256]{1,0:T(8,128)S(1)} custom-call(f32[1,1024]{1,0:T(1,128)S(1)} %bitcast.2, bf16[1152,1024]{1,0:T(8,128)(2,1)S(1)} %get-tuple-element.90.frames_ref, bf16[1024,256]{1,0:T(8,128)(2,1)S(1)} %get-tuple-element.91.weight_ref), custom_call_target="tpu_custom_call" | custom-call | flops 536870912 | bytes 4067328 | tf_op jit(solution)/shard_map/pallas_call | solution.py:33
  51.6 2.7 %collective-permute-start.19 = (bf16[256,256]{1,0:T(8,128)(2,1)S(1)}, bf16[256,256]{1,0:T(8,128)(2,1)S(1)}, u32[]{:S(2)}, u32[]{:S(2)}) collective-permute-start(bf16[256,256]{1,0:T(8,128)(2,1)S(1)} %get-tuple-element.103.refs_0_), channel_id=1, source_target_pairs={{0,24},{2,26},{4,28},{6,30},{8,16},{10,18},{12,20},{14,22},{16,8},... | collective-permute-start | bytes 393224 | tf_op jit(solution)/shard_map/ppermute | solution.py:531
  54.3 0.6 collective-permute-start.18
  54.9 1.1 %collective-permute-start.17 = (bf16[256,256]{1,0:T(8,128)(2,1)S(1)}, bf16[256,256]{1,0:T(8,128)(2,1)S(1)}, u32[]{:S(2)}, u32[]{:S(2)}) collective-permute-start(bf16[256,256]{1,0:T(8,128)(2,1)S(1)} %get-tuple-element.103.refs_0_), channel_id=1, source_target_pairs={{0,8},{2,10},{4,12},{6,14},{8,0},{10,2},{12,4},{14,6},{16,24},{18,... | collective-permute-start | bytes 393224 | tf_op jit(solution)/shard_map/ppermute | solution.py:531
  56.1 0.7 shard_map.99.gated_ref
  56.8 0.2 copy-done.1
  57.0 2.3 %shard_map.100.refs_0_ = bf16[256,256]{1,0:T(8,128)(2,1)S(1)} custom-call(s32[8]{0:T(128)S(1)} %copy-done.3, f32[31,1024]{1,0:T(8,128)S(1)} %copy-done.1, bf16[1152,256]{1,0:T(8,128)(2,1)S(1)} %shard_map.99.gated_ref), custom_call_target="tpu_custom_call" | custom-call | flops 4063232 | bytes 847904 | tf_op jit(solution)/shard_map/pallas_call | solution.py:33
  59.2 5.5 %shard_map.101.refs_0_ = bf16[768,256]{1,0:T(8,128)(2,1)S(1)} custom-call(s32[8]{0:T(128)S(1)} %copy-done.3, f32[31,1024]{1,0:T(8,128)S(1)} %copy-done.1, bf16[1152,256]{1,0:T(8,128)(2,1)S(1)} %shard_map.99.gated_ref), custom_call_target="tpu_custom_call" | custom-call | flops 12189696 | bytes 1110048 | tf_op jit(solution)/shard_map/pallas_call | solution.py:33
  64.7 2.2 %collective-permute-done.18.refs_2_ = bf16[256,256]{1,0:T(8,128)(2,1)S(1)} collective-permute-done((bf16[256,256]{1,0:T(8,128)(2,1)S(1)}, bf16[256,256]{1,0:T(8,128)(2,1)S(1)}, u32[]{:S(2)}, u32[]{:S(2)}) %collective-permute-start.18) | collective-permute-done | bytes 131104 | tf_op jit(solution)/shard_map/ppermute | solution.py:531
  67.1 0.5 collective-permute-start.20
  67.5 1.2 %collective-permute-done.20.refs_1_ = bf16[256,256]{1,0:T(8,128)(2,1)S(1)} collective-permute-done((bf16[256,256]{1,0:T(8,128)(2,1)S(1)}, bf16[256,256]{1,0:T(8,128)(2,1)S(1)}, u32[]{:S(2)}, u32[]{:S(2)}) %collective-permute-start.20) | collective-permute-done | bytes 131104 | tf_op jit(solution)/shard_map/ppermute | solution.py:528
  68.8 0.3 shard_map.103
  69.1 0.2 collective-permute-start.22
  69.3 1.5 %collective-permute-start.23 = (bf16[256,512]{1,0:T(8,128)(2,1)S(1)}, bf16[256,512]{1,0:T(8,128)(2,1)S(1)}, u32[]{:S(2)}, u32[]{:S(2)}) collective-permute-start(bf16[256,512]{1,0:T(8,128)(2,1)S(1)} %shard_map.103), channel_id=1, source_target_pairs={{0,6},{2,4},{4,2},{6,0},{8,14},{10,12},{12,10},{14,8},{16,22},{18,... | collective-permute-start | bytes 786440 | tf_op jit(solution)/shard_map/ppermute | solution.py:522
  70.9 0.6 shard_map.104
  71.5 1.4 %collective-permute-start.24 = (bf16[256,512]{1,0:T(8,128)(2,1)S(1)}, bf16[256,512]{1,0:T(8,128)(2,1)S(1)}, u32[]{:S(2)}, u32[]{:S(2)}) collective-permute-start(bf16[256,512]{1,0:T(8,128)(2,1)S(1)} %get-tuple-element.117), channel_id=1, source_target_pairs={{0,2},{2,0},{4,6},{6,4},{8,10},{10,8},{12,14},{14,12},{16,18},{18,... | collective-permute-start | bytes 786440 | tf_op jit(solution)/shard_map/ppermute | solution.py:522
  72.9 0.6 collective-permute-start.25
  73.6 5.8 %collective-permute-done.23 = bf16[256,512]{1,0:T(8,128)(2,1)S(1)} collective-permute-done((bf16[256,512]{1,0:T(8,128)(2,1)S(1)}, bf16[256,512]{1,0:T(8,128)(2,1)S(1)}, u32[]{:S(2)}, u32[]{:S(2)}) %collective-permute-start.23) | collective-permute-done | bytes 262176 | tf_op jit(solution)/shard_map/ppermute | solution.py:522
  79.4 5.1 %collective-permute-done.24 = bf16[256,512]{1,0:T(8,128)(2,1)S(1)} collective-permute-done((bf16[256,512]{1,0:T(8,128)(2,1)S(1)}, bf16[256,512]{1,0:T(8,128)(2,1)S(1)}, u32[]{:S(2)}, u32[]{:S(2)}) %collective-permute-start.24) | collective-permute-done | bytes 262176 | tf_op jit(solution)/shard_map/ppermute | solution.py:522
  84.5 0.8 add_convert_fusion
  (33 shorter events, 0.7 us)
Async XLA Ops:
  2.0 9.9 %collective-permute-start.6 = (bf16[64,768]{1,0:T(8,128)(2,1)}, bf16[64,768]{1,0:T(8,128)(2,1)S(1)}, u32[]{:S(2)}, u32[]{:S(2)}) collective-permute-start(bf16[64,768]{1,0:T(8,128)(2,1)} %get-tuple-element.72), channel_id=1, source_target_pairs={{0,2},{2,0},{4,6},{6,4},{8,10},{10,8},{12,14},{14,12},{16,18},{18,... | collective-permute-start | bytes 294920 | tf_op jit(solution)/shard_map/ppermute | solution.py:522
  5.0 7.0 %collective-permute-start.7 = (bf16[64,768]{1,0:T(8,128)(2,1)}, bf16[64,768]{1,0:T(8,128)(2,1)S(1)}, u32[]{:S(2)}, u32[]{:S(2)}) collective-permute-start(bf16[64,768]{1,0:T(8,128)(2,1)} %get-tuple-element.73), channel_id=1, source_target_pairs={{0,4},{2,6},{4,0},{6,2},{8,12},{10,14},{12,8},{14,10},{16,20},{18,... | collective-permute-start | bytes 294920 | tf_op jit(solution)/shard_map/ppermute | solution.py:522
  6.5 5.7 %collective-permute-start.8 = (bf16[64,768]{1,0:T(8,128)(2,1)}, bf16[64,768]{1,0:T(8,128)(2,1)S(1)}, u32[]{:S(2)}, u32[]{:S(2)}) collective-permute-start(bf16[64,768]{1,0:T(8,128)(2,1)} %get-tuple-element.74), channel_id=1, source_target_pairs={{0,6},{2,4},{4,2},{6,0},{8,14},{10,12},{12,10},{14,8},{16,22},{18,... | collective-permute-start | bytes 294920 | tf_op jit(solution)/shard_map/ppermute | solution.py:522
  6.5 10.9 %collective-permute-start = (bf16[32,1024]{1,0:T(8,128)(2,1)}, bf16[32,1024]{1,0:T(8,128)(2,1)S(1)}, u32[]{:S(2)}, u32[]{:S(2)}) collective-permute-start(bf16[32,1024]{1,0:T(8,128)(2,1)} %get-tuple-element.63), channel_id=1, source_target_pairs={{0,8},{2,10},{4,12},{6,14},{8,0},{10,2},{12,4},{14,6},{16,24},{18,... | collective-permute-start | bytes 196616 | tf_op jit(solution)/shard_map/ppermute | solution.py:531
  8.5 8.8 %collective-permute-start.1 = (bf16[32,1024]{1,0:T(8,128)(2,1)}, bf16[32,1024]{1,0:T(8,128)(2,1)S(1)}, u32[]{:S(2)}, u32[]{:S(2)}) collective-permute-start(bf16[32,1024]{1,0:T(8,128)(2,1)} %get-tuple-element.64), channel_id=1, source_target_pairs={{0,16},{2,18},{4,20},{6,22},{8,24},{10,26},{12,28},{14,30},{16,0},... | collective-permute-start | bytes 196616 | tf_op jit(solution)/shard_map/ppermute | solution.py:531
  11.9 7.2 %collective-permute-start.2 = (bf16[32,1024]{1,0:T(8,128)(2,1)}, bf16[32,1024]{1,0:T(8,128)(2,1)S(1)}, u32[]{:S(2)}, u32[]{:S(2)}) collective-permute-start(bf16[32,1024]{1,0:T(8,128)(2,1)} %get-tuple-element.65), channel_id=1, source_target_pairs={{0,24},{2,26},{4,28},{6,30},{8,16},{10,18},{12,20},{14,22},{16,8},... | collective-permute-start | bytes 196616 | tf_op jit(solution)/shard_map/ppermute | solution.py:531
  12.2 0.9 %copy-start.4 = (bf16[64,768]{1,0:T(8,128)(2,1)S(1)}, bf16[64,768]{1,0:T(8,128)(2,1)}, u32[]{:S(2)}) copy-start(bf16[64,768]{1,0:T(8,128)(2,1)} %get-tuple-element.71.refs_0_) | copy-start | bytes 294916
  13.1 5.9 %copy-start = (bf16[256,1024]{1,0:T(8,128)(2,1)S(1)}, bf16[256,1024]{1,0:T(8,128)(2,1)}, u32[]{:S(2)}) copy-start(bf16[256,1024]{1,0:T(8,128)(2,1)} %own_ref.1) | copy-start | bytes 1572868
  13.1 5.9 %copy-start.5 = (bf16[32,1024]{1,0:T(8,128)(2,1)S(1)}, bf16[32,1024]{1,0:T(8,128)(2,1)}, u32[]{:S(2)}) copy-start(bf16[32,1024]{1,0:T(8,128)(2,1)} %get-tuple-element.62.refs_0_) | copy-start | bytes 196612
  13.2 13.6 %collective-permute-start.10 = (bf16[256,512]{1,0:T(8,128)(2,1)S(1)}, bf16[256,512]{1,0:T(8,128)(2,1)S(1)}, u32[]{:S(2)}, u32[]{:S(2)}) collective-permute-start(bf16[256,512]{1,0:T(8,128)(2,1)S(1)} %get-tuple-element.78.refs_0_), channel_id=1, source_target_pairs={{0,8},{2,10},{4,12},{6,14},{8,0},{10,2},{12,4},{14,6},{16,24},{18,... | collective-permute-start | bytes 786440 | tf_op jit(solution)/shard_map/ppermute | solution.py:531
  14.8 13.7 %collective-permute-start.9 = (bf16[256,512]{1,0:T(8,128)(2,1)S(1)}, bf16[256,512]{1,0:T(8,128)(2,1)S(1)}, u32[]{:S(2)}, u32[]{:S(2)}) collective-permute-start(bf16[256,512]{1,0:T(8,128)(2,1)S(1)} %get-tuple-element.78.refs_0_), channel_id=1, source_target_pairs={{0,16},{2,18},{4,20},{6,22},{8,24},{10,26},{12,28},{14,30},{16,0},... | collective-permute-start | bytes 786440 | tf_op jit(solution)/shard_map/ppermute | solution.py:531
  19.2 12.0 %collective-permute-start.3 = (bf16[192,1024]{1,0:T(8,128)(2,1)S(1)}, bf16[192,1024]{1,0:T(8,128)(2,1)S(1)}, u32[]{:S(2)}, u32[]{:S(2)}) collective-permute-start(bf16[192,1024]{1,0:T(8,128)(2,1)S(1)} %get-tuple-element.67), channel_id=1, source_target_pairs={{0,2},{2,0},{4,6},{6,4},{8,10},{10,8},{12,14},{14,12},{16,18},{18,... | collective-permute-start | bytes 1179656 | tf_op jit(solution)/shard_map/ppermute | solution.py:522
  20.8 15.8 %collective-permute-start.4 = (bf16[192,1024]{1,0:T(8,128)(2,1)S(1)}, bf16[192,1024]{1,0:T(8,128)(2,1)S(1)}, u32[]{:S(2)}, u32[]{:S(2)}) collective-permute-start(bf16[192,1024]{1,0:T(8,128)(2,1)S(1)} %get-tuple-element.68), channel_id=1, source_target_pairs={{0,4},{2,6},{4,0},{6,2},{8,12},{10,14},{12,8},{14,10},{16,20},{18,... | collective-permute-start | bytes 1179656 | tf_op jit(solution)/shard_map/ppermute | solution.py:522
  22.3 14.3 %collective-permute-start.5 = (bf16[192,1024]{1,0:T(8,128)(2,1)S(1)}, bf16[192,1024]{1,0:T(8,128)(2,1)S(1)}, u32[]{:S(2)}, u32[]{:S(2)}) collective-permute-start(bf16[192,1024]{1,0:T(8,128)(2,1)S(1)} %get-tuple-element.69), channel_id=1, source_target_pairs={{0,6},{2,4},{4,2},{6,0},{8,14},{10,12},{12,10},{14,8},{16,22},{18,... | collective-permute-start | bytes 1179656 | tf_op jit(solution)/shard_map/ppermute | solution.py:522
  28.5 8.6 %collective-permute-start.11 = (bf16[256,512]{1,0:T(8,128)(2,1)S(1)}, bf16[256,512]{1,0:T(8,128)(2,1)S(1)}, u32[]{:S(2)}, u32[]{:S(2)}) collective-permute-start(bf16[256,512]{1,0:T(8,128)(2,1)S(1)} %collective-permute-done.9.refs_2_), channel_id=1, source_target_pairs={{8,0},{10,2},{12,4},{14,6},{16,24},{18,26},{20,28},{22,30},{9,1},{... | collective-permute-start | bytes 786440 | tf_op jit(solution)/shard_map/ppermute | solution.py:547
  29.8 7.4 %collective-permute-start.12 = (bf16[256,512]{1,0:T(8,128)(2,1)S(1)}, bf16[256,512]{1,0:T(8,128)(2,1)S(1)}, u32[]{:S(2)}, u32[]{:S(2)}) collective-permute-start(bf16[256,512]{1,0:T(8,128)(2,1)S(1)} %get-tuple-element.78.refs_0_), channel_id=1, source_target_pairs={{8,16},{10,18},{12,20},{14,22},{16,8},{18,10},{20,12},{22,14},{9,1... | collective-permute-start | bytes 786440 | tf_op jit(solution)/shard_map/ppermute | solution.py:548
  37.1 2.7 %copy-start.3 = (s32[8]{0:T(128)S(1)}, s32[8]{0:T(128)}, u32[]{:S(2)}) copy-start(s32[8]{0:T(128)} %len_ref.5) | copy-start | bytes 100
  37.1 2.7 %collective-permute-start.13 = (bf16[512,1024]{1,0:T(8,128)(2,1)S(1)}, bf16[512,1024]{1,0:T(8,128)(2,1)S(1)}, u32[]{:S(2)}, u32[]{:S(2)}) collective-permute-start(bf16[512,1024]{1,0:T(8,128)(2,1)S(1)} %get-tuple-element.81), channel_id=1, source_target_pairs={{0,1},{1,0},{2,3},{3,2},{4,5},{5,4},{6,7},{7,6},{8,9},{9,8},{10,11... | collective-permute-start | bytes 3145736 | tf_op jit(solution)/shard_map/ppermute | solution.py:528
  42.6 8.1 %copy-start.2 = (f32[1024]{0:T(1024)S(1)}, f32[1024]{0:T(1024)}, u32[]{:S(2)}) copy-start(f32[1024]{0:T(1024)} %param.14) | copy-start | bytes 12292
  42.6 9.0 %collective-permute-start.16 = (bf16[144,256]{1,0:T(8,128)(2,1)S(1)}, bf16[144,256]{1,0:T(8,128)(2,1)S(1)}, u32[]{:S(2)}, u32[]{:S(2)}) collective-permute-start(bf16[144,256]{1,0:T(8,128)(2,1)S(1)} %get-tuple-element.85), channel_id=1, source_target_pairs={{0,24},{2,26},{4,28},{6,30},{1,25},{3,27},{5,29},{7,31}} | collective-permute-start | bytes 221192 | tf_op jit(solution)/shard_map/ppermute | solution.py:525
  45.0 6.6 %collective-permute-start.15 = (bf16[144,256]{1,0:T(8,128)(2,1)S(1)}, bf16[144,256]{1,0:T(8,128)(2,1)S(1)}, u32[]{:S(2)}, u32[]{:S(2)}) collective-permute-start(bf16[144,256]{1,0:T(8,128)(2,1)S(1)} %get-tuple-element.85), channel_id=1, source_target_pairs={{0,16},{2,18},{4,20},{6,22},{8,24},{10,26},{12,28},{14,30},{1,17},... | collective-permute-start | bytes 221192 | tf_op jit(solution)/shard_map/ppermute | solution.py:525
  46.8 4.8 %collective-permute-start.14 = (bf16[144,256]{1,0:T(8,128)(2,1)S(1)}, bf16[144,256]{1,0:T(8,128)(2,1)S(1)}, u32[]{:S(2)}, u32[]{:S(2)}) collective-permute-start(bf16[144,256]{1,0:T(8,128)(2,1)S(1)} %get-tuple-element.85), channel_id=1, source_target_pairs={{0,8},{2,10},{4,12},{6,14},{8,16},{10,18},{12,20},{14,22},{16,24},... | collective-permute-start | bytes 221192 | tf_op jit(solution)/shard_map/ppermute | solution.py:525
  51.6 13.1 %collective-permute-start.19 = (bf16[256,256]{1,0:T(8,128)(2,1)S(1)}, bf16[256,256]{1,0:T(8,128)(2,1)S(1)}, u32[]{:S(2)}, u32[]{:S(2)}) collective-permute-start(bf16[256,256]{1,0:T(8,128)(2,1)S(1)} %get-tuple-element.103.refs_0_), channel_id=1, source_target_pairs={{0,24},{2,26},{4,28},{6,30},{8,16},{10,18},{12,20},{14,22},{16,8},... | collective-permute-start | bytes 393224 | tf_op jit(solution)/shard_map/ppermute | solution.py:531
  54.3 12.5 %collective-permute-start.18 = (bf16[256,256]{1,0:T(8,128)(2,1)S(1)}, bf16[256,256]{1,0:T(8,128)(2,1)S(1)}, u32[]{:S(2)}, u32[]{:S(2)}) collective-permute-start(bf16[256,256]{1,0:T(8,128)(2,1)S(1)} %get-tuple-element.103.refs_0_), channel_id=1, source_target_pairs={{0,16},{2,18},{4,20},{6,22},{8,24},{10,26},{12,28},{14,30},{16,0},... | collective-permute-start | bytes 393224 | tf_op jit(solution)/shard_map/ppermute | solution.py:531
  54.9 11.9 %collective-permute-start.17 = (bf16[256,256]{1,0:T(8,128)(2,1)S(1)}, bf16[256,256]{1,0:T(8,128)(2,1)S(1)}, u32[]{:S(2)}, u32[]{:S(2)}) collective-permute-start(bf16[256,256]{1,0:T(8,128)(2,1)S(1)} %get-tuple-element.103.refs_0_), channel_id=1, source_target_pairs={{0,8},{2,10},{4,12},{6,14},{8,0},{10,2},{12,4},{14,6},{16,24},{18,... | collective-permute-start | bytes 393224 | tf_op jit(solution)/shard_map/ppermute | solution.py:531
  56.1 0.9 %copy-start.1 = (f32[31,1024]{1,0:T(8,128)S(1)}, f32[31,1024]{1,0:T(8,128)}, u32[]{:S(2)}) copy-start(f32[31,1024]{1,0:T(8,128)} %taps_ref.3) | copy-start | bytes 380932
  67.0 1.8 %collective-permute-start.21 = (bf16[512,256]{1,0:T(8,128)(2,1)S(1)}, bf16[512,256]{1,0:T(8,128)(2,1)S(1)}, u32[]{:S(2)}, u32[]{:S(2)}) collective-permute-start(bf16[512,256]{1,0:T(8,128)(2,1)S(1)} %get-tuple-element.108), channel_id=1, source_target_pairs={{0,1},{1,0},{2,3},{3,2},{4,5},{5,4},{6,7},{7,6},{8,9},{9,8},{10,11... | collective-permute-start | bytes 786440 | tf_op jit(solution)/shard_map/ppermute | solution.py:528
  67.1 1.7 %collective-permute-start.20 = (bf16[256,256]{1,0:T(8,128)(2,1)S(1)}, bf16[256,256]{1,0:T(8,128)(2,1)S(1)}, u32[]{:S(2)}, u32[]{:S(2)}) collective-permute-start(bf16[256,256]{1,0:T(8,128)(2,1)S(1)} %shard_map.100.refs_0_), channel_id=1, source_target_pairs={{0,1},{1,0},{2,3},{3,2},{4,5},{5,4},{6,7},{7,6},{8,9},{9,8},{10,11... | collective-permute-start | bytes 393224 | tf_op jit(solution)/shard_map/ppermute | solution.py:528
  69.1 1.8 %collective-permute-start.22 = (bf16[768,256]{1,0:T(8,128)(2,1)S(1)}, bf16[768,256]{1,0:T(8,128)(2,1)S(1)}, u32[]{:S(2)}, u32[]{:S(2)}) collective-permute-start(bf16[768,256]{1,0:T(8,128)(2,1)S(1)} %shard_map.101.refs_0_), channel_id=1, source_target_pairs={{0,1},{1,0},{2,3},{3,2},{4,5},{5,4},{6,7},{7,6},{8,9},{9,8},{10,11... | collective-permute-start | bytes 1179656 | tf_op jit(solution)/shard_map/ppermute | solution.py:528
  69.3 10.1 %collective-permute-start.23 = (bf16[256,512]{1,0:T(8,128)(2,1)S(1)}, bf16[256,512]{1,0:T(8,128)(2,1)S(1)}, u32[]{:S(2)}, u32[]{:S(2)}) collective-permute-start(bf16[256,512]{1,0:T(8,128)(2,1)S(1)} %shard_map.103), channel_id=1, source_target_pairs={{0,6},{2,4},{4,2},{6,0},{8,14},{10,12},{12,10},{14,8},{16,22},{18,... | collective-permute-start | bytes 786440 | tf_op jit(solution)/shard_map/ppermute | solution.py:522
  71.5 13.0 %collective-permute-start.24 = (bf16[256,512]{1,0:T(8,128)(2,1)S(1)}, bf16[256,512]{1,0:T(8,128)(2,1)S(1)}, u32[]{:S(2)}, u32[]{:S(2)}) collective-permute-start(bf16[256,512]{1,0:T(8,128)(2,1)S(1)} %get-tuple-element.117), channel_id=1, source_target_pairs={{0,2},{2,0},{4,6},{6,4},{8,10},{10,8},{12,14},{14,12},{16,18},{18,... | collective-permute-start | bytes 786440 | tf_op jit(solution)/shard_map/ppermute | solution.py:522
  72.9 11.5 %collective-permute-start.25 = (bf16[256,512]{1,0:T(8,128)(2,1)S(1)}, bf16[256,512]{1,0:T(8,128)(2,1)S(1)}, u32[]{:S(2)}, u32[]{:S(2)}) collective-permute-start(bf16[256,512]{1,0:T(8,128)(2,1)S(1)} %get-tuple-element.118), channel_id=1, source_target_pairs={{0,4},{2,6},{4,0},{6,2},{8,12},{10,14},{12,8},{14,10},{16,20},{18,... | collective-permute-start | bytes 786440 | tf_op jit(solution)/shard_map/ppermute | solution.py:522

commit v12 on v11

--- a/solution.py
+++ b/solution.py
@@ -24,12 +24,14 @@
     return lax.dot_general(a, b, (dims, ((), ())), precision=precision, preferred_element_type=F32)
 
 
-def call(kernel, out_shape, operands, scratch=(), flops=0, smem=1, anywhere=0, vmem=VMEM_BYTES):
+def call(kernel, out_shape, operands, scratch=(), flops=0, smem=1, anywhere=0, vmem=VMEM_BYTES, hidden=False):
     in_specs = [pl.BlockSpec(memory_space=pltpu.SMEM)] * smem
     in_specs += [pl.BlockSpec(memory_space=pltpu.VMEM)] * (len(operands) - smem - anywhere)
     in_specs += [pl.BlockSpec(memory_space=pl.ANY)] * anywhere
     moved = sum(a.size * a.dtype.itemsize for a in operands)
     moved += sum(a.size * a.dtype.itemsize for a in jax.tree.leaves(out_shape))
+    if hidden:
+        flops = moved = 0
     return pl.pallas_call(
         kernel,
         out_shape=out_shape,
@@ -625,8 +627,10 @@
         ),
         [record_lengths, decay, x_columns, bc_mine, frames, swap, halo, *inward[1:]],
         [pltpu.VMEM((depth, 2 * state), BF16), pltpu.VMEM((total, width), F32)],
-        flops=2 * total * depth * (width + 2 * state),
-    )
+        hidden=True,
+    )
+    early = between_planes(out_stack, 2) if planes > 2 else None
+    x_rows, early = lax.optimization_barrier((x_rows, early))
     summaries = [later(summary, step) for step in range(1, planes)]
     y, carry = call(
         functools.partial(inner_kernel, group, heads),
@@ -643,7 +647,9 @@
         smem=0,
     )
     out_stack, summaries, y, silu = lax.optimization_barrier((out_stack, summaries, y, silu))
-    out_pieces = [out_stack] + [between_planes(out_stack, step) for step in range(1, planes)]
+    out_pieces = [out_stack]
+    for step in range(1, planes):
+        out_pieces.append(early if step == 2 else between_planes(out_stack, step))
     gated = call(
         functools.partial(gate_kernel, heads, state),
         shape((all_rows, width), BF16),
@@ -674,9 +680,7 @@
 
     far_act = conv(far, gated)
     far_swapped = [across(far_act, step) for step in range(1, cores)]
-    gated, far_act = lax.optimization_barrier((gated, far_act))
-    near_act = conv(near, gated)
-    near_act, out_pieces = lax.optimization_barrier((near_act, out_pieces))
+    far_act, out_pieces = lax.optimization_barrier((far_act, out_pieces))
     share = depth // cores
     out_parts = call(
         functools.partial(share_kernel, cores, tuple(range(planes)), group),
@@ -686,10 +690,11 @@
         smem=0,
     )
     out_parts = [out_parts[0]] + [across(out_parts[step], step) for step in range(1, cores)]
-    near_act, far_swapped, out_parts = lax.optimization_barrier((near_act, far_swapped, out_parts))
     (far_out,) = out(far, far_act, far_swapped)
+    gated, far_out = lax.optimization_barrier((gated, far_out))
+    far_out = in_plane(far_out, far[0])
+    near_act = conv(near, gated)
     near_act, far_out = lax.optimization_barrier((near_act, far_out))
-    far_out = in_plane(far_out, far[0])
     near_swapped = [across(near_act, step) for step in range(1, cores)]
     near_outs = out(near, near_act, near_swapped)
     mixed = near_outs[-1] + far_out.astype(F32)

time: 85.7 us -> 90.9 us (1.061)
  starting transfers between devices: 34 us -> 45.9 us
  waiting for transfers between devices: 30.7 us -> 24.5 us
    ppermute x9, waiting for transfers between devices: 17.2 us -> 9.76 us  [in_plane(): return lax.ppermute(array, 'tm', [(i, i ^ step) for i in range(times)])]
    ppermute x3, starting transfers between devices: 6.15 us -> 11.9 us  [later(): lax.ppermute(array, 'tm', [(i, i + step * group) for i in range(times - s...]
    ppermute x8, starting transfers between devices: 13.4 us -> 17.9 us  [between_planes(): lax.ppermute(array, 'tm', [(i, i ^ step * group) for i in range(times)])]
    ppermute x9, starting transfers between devices: 11.6 us -> 13.5 us  [in_plane(): return lax.ppermute(array, 'tm', [(i, i ^ step) for i in range(times)])]
  transfers between devices with their start and end apart: 26 -> 26, of which waited for: 12 -> 13; matrix products, arithmetic and copies ran while one was open for 1% -> 1% of each run, Pallas kernels for 15% -> 16%
where the time goes in v12:
time: 90.9 us; the launch traced here: 90.5 us
  starting transfers between devices  45.9 us (50%)
  waiting for transfers between devices  24.5 us (27%)
  Pallas kernels  17 us (19%)
  local copies, waits for them, and re-layouts  1.85 us (2%)
    ppermute x8, starting transfers between devices, between_planes(): lax.ppermute(array, 'tm', [(i, i ^ step * group) for i in range(times)])  17.9 us
    pallas_call x14, Pallas kernels, call(): pl.pallas_call(kernel, out_shape=out_shape, in_specs=in_specs, out_specs=...  17 us
    ppermute x9, starting transfers between devices, in_plane(): return lax.ppermute(array, 'tm', [(i, i ^ step) for i in range(times)])  13.5 us
    ppermute x3, starting transfers between devices, later(): lax.ppermute(array, 'tm', [(i, i + step * group) for i in range(times - s...  11.9 us
    ppermute x9, waiting for transfers between devices, in_plane(): return lax.ppermute(array, 'tm', [(i, i ^ step) for i in range(times)])  9.76 us
    ppermute x8, waiting for transfers between devices, between_planes(): lax.ppermute(array, 'tm', [(i, i ^ step * group) for i in range(times)])  9.29 us
    ppermute x4, waiting for transfers between devices, across(): return lax.ppermute(array, 'head', [(i, i ^ step) for i in range(cores)])  4.7 us
  transfers between devices with their start and end apart: 26, of which 13 were waited for; matrix products, arithmetic and copies ran while one was open for 1% of the time, Pallas kernels for 16%

profile of v12, /device:TPU:0, one launch (start us, length us, event | category | flops | bytes accessed | tf_op | source)
XLA Modules:
  0.0 90.5 jit_solution(15597405314367049260)
XLA Ops:
  0.0 2.0 %shard_map.91 = (bf16[64,768]{1,0:T(8,128)(2,1)}, bf16[64,768]{1,0:T(8,128)(2,1)}, bf16[64,768]{1,0:T(8,128)(2,1)}, bf16[64,768]{1,0:T(8,128)(2,1)}, bf16[32,102...) custom-call(f32[16,256]{1,0:T(8,128)} %log_decay_ref.1, ...), custom_call_target="tpu_custom_call" | custom-call | bytes 1622016 | tf_op jit(solution)/shard_map/pallas_call | solution.py:35
  2.0 3.0 %collective-permute-start.6 = (bf16[64,768]{1,0:T(8,128)(2,1)}, bf16[64,768]{1,0:T(8,128)(2,1)S(1)}, u32[]{:S(2)}, u32[]{:S(2)}) collective-permute-start(bf16[64,768]{1,0:T(8,128)(2,1)} %get-tuple-element.70), channel_id=1, source_target_pairs={{0,2},{2,0},{4,6},{6,4},{8,10},{10,8},{12,14},{14,12},{16,18},{18,... | collective-permute-start | bytes 294920 | tf_op jit(solution)/shard_map/ppermute | solution.py:524
  5.0 1.5 %collective-permute-start.7 = (bf16[64,768]{1,0:T(8,128)(2,1)}, bf16[64,768]{1,0:T(8,128)(2,1)S(1)}, u32[]{:S(2)}, u32[]{:S(2)}) collective-permute-start(bf16[64,768]{1,0:T(8,128)(2,1)} %get-tuple-element.71), channel_id=1, source_target_pairs={{0,4},{2,6},{4,0},{6,2},{8,12},{10,14},{12,8},{14,10},{16,20},{18,... | collective-permute-start | bytes 294920 | tf_op jit(solution)/shard_map/ppermute | solution.py:524
  6.5 2.0 %collective-permute-start = (bf16[32,1024]{1,0:T(8,128)(2,1)}, bf16[32,1024]{1,0:T(8,128)(2,1)S(1)}, u32[]{:S(2)}, u32[]{:S(2)}) collective-permute-start(bf16[32,1024]{1,0:T(8,128)(2,1)} %get-tuple-element.61), channel_id=1, source_target_pairs={{0,8},{2,10},{4,12},{6,14},{8,0},{10,2},{12,4},{14,6},{16,24},{18,... | collective-permute-start | bytes 196616 | tf_op jit(solution)/shard_map/ppermute | solution.py:533
  8.5 2.6 %collective-permute-start.1 = (bf16[32,1024]{1,0:T(8,128)(2,1)}, bf16[32,1024]{1,0:T(8,128)(2,1)S(1)}, u32[]{:S(2)}, u32[]{:S(2)}) collective-permute-start(bf16[32,1024]{1,0:T(8,128)(2,1)} %get-tuple-element.62), channel_id=1, source_target_pairs={{0,16},{2,18},{4,20},{6,22},{8,24},{10,26},{12,28},{14,30},{16,0},... | collective-permute-start | bytes 196616 | tf_op jit(solution)/shard_map/ppermute | solution.py:533
  11.1 0.7 reshape.3
  12.0 0.2 collective-permute-done.8.refs_3_
  12.2 0.9 copy-done.4
  13.2 2.7 %collective-permute-start.9 = (bf16[256,512]{1,0:T(8,128)(2,1)S(1)}, bf16[256,512]{1,0:T(8,128)(2,1)S(1)}, u32[]{:S(2)}, u32[]{:S(2)}) collective-permute-start(bf16[256,512]{1,0:T(8,128)(2,1)S(1)} %get-tuple-element.76.refs_0_), channel_id=1, source_target_pairs={{0,16},{2,18},{4,20},{6,22},{8,24},{10,26},{12,28},{14,30},{16,0},... | collective-permute-start | bytes 786440 | tf_op jit(solution)/shard_map/ppermute | solution.py:533
  15.8 1.6 %collective-permute-start.10 = (bf16[256,512]{1,0:T(8,128)(2,1)S(1)}, bf16[256,512]{1,0:T(8,128)(2,1)S(1)}, u32[]{:S(2)}, u32[]{:S(2)}) collective-permute-start(bf16[256,512]{1,0:T(8,128)(2,1)S(1)} %get-tuple-element.76.refs_0_), channel_id=1, source_target_pairs={{0,8},{2,10},{4,12},{6,14},{8,0},{10,2},{12,4},{14,6},{16,24},{18,... | collective-permute-start | bytes 786440 | tf_op jit(solution)/shard_map/ppermute | solution.py:533
  17.4 2.7 %collective-permute-done.1.refs_2_ = bf16[32,1024]{1,0:T(8,128)(2,1)S(1)} collective-permute-done((bf16[32,1024]{1,0:T(8,128)(2,1)}, bf16[32,1024]{1,0:T(8,128)(2,1)S(1)}, u32[]{:S(2)}, u32[]{:S(2)}) %collective-permute-start.1) | collective-permute-done | bytes 65568 | tf_op jit(solution)/shard_map/ppermute | solution.py:533
  20.1 0.2 shard_map.92
  20.2 1.6 %collective-permute-start.3 = (bf16[192,1024]{1,0:T(8,128)(2,1)S(1)}, bf16[192,1024]{1,0:T(8,128)(2,1)S(1)}, u32[]{:S(2)}, u32[]{:S(2)}) collective-permute-start(bf16[192,1024]{1,0:T(8,128)(2,1)S(1)} %get-tuple-element.65), channel_id=1, source_target_pairs={{0,2},{2,0},{4,6},{6,4},{8,10},{10,8},{12,14},{14,12},{16,18},{18,... | collective-permute-start | bytes 1179656 | tf_op jit(solution)/shard_map/ppermute | solution.py:524
  21.8 1.5 %collective-permute-start.4 = (bf16[192,1024]{1,0:T(8,128)(2,1)S(1)}, bf16[192,1024]{1,0:T(8,128)(2,1)S(1)}, u32[]{:S(2)}, u32[]{:S(2)}) collective-permute-start(bf16[192,1024]{1,0:T(8,128)(2,1)S(1)} %get-tuple-element.66), channel_id=1, source_target_pairs={{0,4},{2,6},{4,0},{6,2},{8,12},{10,14},{12,8},{14,10},{16,20},{18,... | collective-permute-start | bytes 1179656 | tf_op jit(solution)/shard_map/ppermute | solution.py:524
  23.3 0.5 collective-permute-start.5
  23.8 4.7 %collective-permute-done.9.refs_2_ = bf16[256,512]{1,0:T(8,128)(2,1)S(1)} collective-permute-done((bf16[256,512]{1,0:T(8,128)(2,1)S(1)}, bf16[256,512]{1,0:T(8,128)(2,1)S(1)}, u32[]{:S(2)}, u32[]{:S(2)}) %collective-permute-start.9) | collective-permute-done | bytes 262176 | tf_op jit(solution)/shard_map/ppermute | solution.py:533
  28.5 1.3 %collective-permute-start.11 = (bf16[256,512]{1,0:T(8,128)(2,1)S(1)}, bf16[256,512]{1,0:T(8,128)(2,1)S(1)}, u32[]{:S(2)}, u32[]{:S(2)}) collective-permute-start(bf16[256,512]{1,0:T(8,128)(2,1)S(1)} %collective-permute-done.9.refs_2_), channel_id=1, source_target_pairs={{8,0},{10,2},{12,4},{14,6},{16,24},{18,26},{20,28},{22,30},{9,1},{... | collective-permute-start | bytes 786440 | tf_op jit(solution)/shard_map/ppermute | solution.py:549
  29.8 0.7 collective-permute-start.12
  30.5 0.6 collective-permute-done.3.refs_1_.refs_0_
  31.1 4.8 %collective-permute-start.17 = (bf16[256,256]{1,0:T(8,128)(2,1)S(1)}, bf16[256,256]{1,0:T(8,128)(2,1)S(1)}, u32[]{:S(2)}, u32[]{:S(2)}) collective-permute-start(bf16[256,256]{1,0:T(8,128)(2,1)S(1)} %get-tuple-element.102.refs_0_), channel_id=1, source_target_pairs={{0,16},{2,18},{4,20},{6,22},{8,24},{10,26},{12,28},{14,30},{16,0},... | collective-permute-start | bytes 393224 | tf_op jit(solution)/shard_map/ppermute | solution.py:533
  35.9 0.6 collective-permute-done.4.refs_2_.refs_1_
  36.5 0.5 shard_map.93
  37.1 0.8 collective-permute-done.11.refs_3_
  38.0 1.8 %collective-permute-done.13.swap_ref = bf16[512,1024]{1,0:T(8,128)(2,1)S(1)} collective-permute-done((bf16[512,1024]{1,0:T(8,128)(2,1)S(1)}, bf16[512,1024]{1,0:T(8,128)(2,1)S(1)}, u32[]{:S(2)}, u32[]{:S(2)}) %collective-permute-start.13) | collective-permute-done | bytes 1048608 | tf_op jit(solution)/shard_map/ppermute | solution.py:530
  39.7 2.8 %shard_map.96 = (bf16[1152,1024]{1,0:T(8,128)(2,1)S(1)}, bf16[1152,256]{1,0:T(8,128)(2,1)S(1)}, bf16[1152,128]{1,0:T(8,128)(2,1)S(1)}, bf16[1152,128]{1,0:T(8,12...) custom-call(s32[8]{0:T(128)S(1)} %copy-done.2, ...), custom_call_target="tpu_custom_call" | custom-call | tf_op jit(solution)/shard_map/pallas_call | solution.py:35
  42.5 8.1 %collective-permute-start.14 = (bf16[144,256]{1,0:T(8,128)(2,1)S(1)}, bf16[144,256]{1,0:T(8,128)(2,1)S(1)}, u32[]{:S(2)}, u32[]{:S(2)}) collective-permute-start(bf16[144,256]{1,0:T(8,128)(2,1)S(1)} %get-tuple-element.83), channel_id=1, source_target_pairs={{0,8},{2,10},{4,12},{6,14},{8,16},{10,18},{12,20},{14,22},{16,24},... | collective-permute-start | bytes 221192 | tf_op jit(solution)/shard_map/ppermute | solution.py:527
  50.6 2.5 %collective-permute-start.15 = (bf16[144,256]{1,0:T(8,128)(2,1)S(1)}, bf16[144,256]{1,0:T(8,128)(2,1)S(1)}, u32[]{:S(2)}, u32[]{:S(2)}) collective-permute-start(bf16[144,256]{1,0:T(8,128)(2,1)S(1)} %get-tuple-element.83), channel_id=1, source_target_pairs={{0,16},{2,18},{4,20},{6,22},{8,24},{10,26},{12,28},{14,30},{1,17},... | collective-permute-start | bytes 221192 | tf_op jit(solution)/shard_map/ppermute | solution.py:527
  53.1 1.3 %collective-permute-start.16 = (bf16[144,256]{1,0:T(8,128)(2,1)S(1)}, bf16[144,256]{1,0:T(8,128)(2,1)S(1)}, u32[]{:S(2)}, u32[]{:S(2)}) collective-permute-start(bf16[144,256]{1,0:T(8,128)(2,1)S(1)} %get-tuple-element.83), channel_id=1, source_target_pairs={{0,24},{2,26},{4,28},{6,30},{1,25},{3,27},{5,29},{7,31}} | collective-permute-start | bytes 221192 | tf_op jit(solution)/shard_map/ppermute | solution.py:527
  54.4 1.9 %shard_map.97 = (f32[1152,256]{1,0:T(8,128)S(1)}, f32[1152,256]{1,0:T(8,128)S(1)}) custom-call(bf16[1152,256]{1,0:T(8,128)(2,1)S(1)} %get-tuple-element.85.x_ref, bf16[1152,128]{1,0:T(8,128)(2,1)S(1)} %get-tuple-element.86.b_ref, bf16[1152,128]{1,0:T(8,128)(2,1)S(1)} %get-tuple-element.81.c_ref, f32[216,128]{1,0:T(8,128)S(1)} %get-tuple-element.87.rows_ref), custom_call_target="tpu_custom_call" | custom-call | flops 134217728 | bytes 3649536 | tf_op jit(solution)/shard_map/pallas_call | solution.py:35
  56.4 0.8 shard_map.98.silu_ref
  57.3 4.1 %collective-permute-start.19 = (bf16[256,256]{1,0:T(8,128)(2,1)S(1)}, bf16[256,256]{1,0:T(8,128)(2,1)S(1)}, u32[]{:S(2)}, u32[]{:S(2)}) collective-permute-start(bf16[256,256]{1,0:T(8,128)(2,1)S(1)} %get-tuple-element.102.refs_0_), channel_id=1, source_target_pairs={{0,24},{2,26},{4,28},{6,30},{8,16},{10,18},{12,20},{14,22},{16,8},... | collective-permute-start | bytes 393224 | tf_op jit(solution)/shard_map/ppermute | solution.py:533
  61.5 0.7 shard_map.99.gated_ref
  62.2 0.2 copy-done.1
  62.4 1.6 %shard_map.100.refs_0_ = bf16[256,256]{1,0:T(8,128)(2,1)S(1)} custom-call(s32[8]{0:T(128)S(1)} %copy-done.2, f32[31,1024]{1,0:T(8,128)S(1)} %copy-done.1, bf16[1152,256]{1,0:T(8,128)(2,1)S(1)} %shard_map.99.gated_ref), custom_call_target="tpu_custom_call" | custom-call | flops 4063232 | bytes 847904 | tf_op jit(solution)/shard_map/pallas_call | solution.py:35
  64.0 1.9 %collective-permute-done.19.refs_3_ = bf16[256,256]{1,0:T(8,128)(2,1)S(1)} collective-permute-done((bf16[256,256]{1,0:T(8,128)(2,1)S(1)}, bf16[256,256]{1,0:T(8,128)(2,1)S(1)}, u32[]{:S(2)}, u32[]{:S(2)}) %collective-permute-start.19) | collective-permute-done | bytes 131104 | tf_op jit(solution)/shard_map/ppermute | solution.py:533
  66.1 0.5 collective-permute-start.20
  66.6 1.2 %collective-permute-done.20.refs_1_ = bf16[256,256]{1,0:T(8,128)(2,1)S(1)} collective-permute-done((bf16[256,256]{1,0:T(8,128)(2,1)S(1)}, bf16[256,256]{1,0:T(8,128)(2,1)S(1)}, u32[]{:S(2)}, u32[]{:S(2)}) %collective-permute-start.20) | collective-permute-done | bytes 131104 | tf_op jit(solution)/shard_map/ppermute | solution.py:530
  67.8 0.3 shard_map.102
  68.1 2.4 %collective-permute-start.22 = (bf16[256,512]{1,0:T(8,128)(2,1)S(1)}, bf16[256,512]{1,0:T(8,128)(2,1)S(1)}, u32[]{:S(2)}, u32[]{:S(2)}) collective-permute-start(bf16[256,512]{1,0:T(8,128)(2,1)S(1)} %shard_map.102), channel_id=1, source_target_pairs={{0,6},{2,4},{4,2},{6,0},{8,14},{10,12},{12,10},{14,8},{16,22},{18,... | collective-permute-start | bytes 786440 | tf_op jit(solution)/shard_map/ppermute | solution.py:524
  70.6 5.5 %shard_map.103.refs_0_ = bf16[768,256]{1,0:T(8,128)(2,1)S(1)} custom-call(s32[8]{0:T(128)S(1)} %copy-done.2, f32[31,1024]{1,0:T(8,128)S(1)} %copy-done.1, bf16[1152,256]{1,0:T(8,128)(2,1)S(1)} %shard_map.99.gated_ref), custom_call_target="tpu_custom_call" | custom-call | flops 12189696 | bytes 1110048 | tf_op jit(solution)/shard_map/pallas_call | solution.py:35
  76.0 1.4 %collective-permute-done.22 = bf16[256,512]{1,0:T(8,128)(2,1)S(1)} collective-permute-done((bf16[256,512]{1,0:T(8,128)(2,1)S(1)}, bf16[256,512]{1,0:T(8,128)(2,1)S(1)}, u32[]{:S(2)}, u32[]{:S(2)}) %collective-permute-start.22) | collective-permute-done | bytes 262176 | tf_op jit(solution)/shard_map/ppermute | solution.py:524
  77.4 1.7 %collective-permute-done.23.refs_1_ = bf16[768,256]{1,0:T(8,128)(2,1)S(1)} collective-permute-done((bf16[768,256]{1,0:T(8,128)(2,1)S(1)}, bf16[768,256]{1,0:T(8,128)(2,1)S(1)}, u32[]{:S(2)}, u32[]{:S(2)}) %collective-permute-start.23) | collective-permute-done | bytes 393248 | tf_op jit(solution)/shard_map/ppermute | solution.py:530
  79.2 0.6 shard_map.104
  79.8 1.8 %collective-permute-start.24 = (bf16[256,512]{1,0:T(8,128)(2,1)S(1)}, bf16[256,512]{1,0:T(8,128)(2,1)S(1)}, u32[]{:S(2)}, u32[]{:S(2)}) collective-permute-start(bf16[256,512]{1,0:T(8,128)(2,1)S(1)} %get-tuple-element.113), channel_id=1, source_target_pairs={{0,2},{2,0},{4,6},{6,4},{8,10},{10,8},{12,14},{14,12},{16,18},{18,... | collective-permute-start | bytes 786440 | tf_op jit(solution)/shard_map/ppermute | solution.py:524
  81.6 1.2 %collective-permute-start.25 = (bf16[256,512]{1,0:T(8,128)(2,1)S(1)}, bf16[256,512]{1,0:T(8,128)(2,1)S(1)}, u32[]{:S(2)}, u32[]{:S(2)}) collective-permute-start(bf16[256,512]{1,0:T(8,128)(2,1)S(1)} %get-tuple-element.114), channel_id=1, source_target_pairs={{0,4},{2,6},{4,0},{6,2},{8,12},{10,14},{12,8},{14,10},{16,20},{18,... | collective-permute-start | bytes 786440 | tf_op jit(solution)/shard_map/ppermute | solution.py:524
  82.8 5.4 %collective-permute-done.24 = bf16[256,512]{1,0:T(8,128)(2,1)S(1)} collective-permute-done((bf16[256,512]{1,0:T(8,128)(2,1)S(1)}, bf16[256,512]{1,0:T(8,128)(2,1)S(1)}, u32[]{:S(2)}, u32[]{:S(2)}) %collective-permute-start.24) | collective-permute-done | bytes 262176 | tf_op jit(solution)/shard_map/ppermute | solution.py:524
  88.2 1.5 %collective-permute-done.25 = bf16[256,512]{1,0:T(8,128)(2,1)S(1)} collective-permute-done((bf16[256,512]{1,0:T(8,128)(2,1)S(1)}, bf16[256,512]{1,0:T(8,128)(2,1)S(1)}, u32[]{:S(2)}, u32[]{:S(2)}) %collective-permute-start.25) | collective-permute-done | bytes 262176 | tf_op jit(solution)/shard_map/ppermute | solution.py:524
  89.6 0.8 add_convert_fusion
  (33 shorter events, 0.6 us)
Async XLA Ops:
  2.0 9.9 %collective-permute-start.6 = (bf16[64,768]{1,0:T(8,128)(2,1)}, bf16[64,768]{1,0:T(8,128)(2,1)S(1)}, u32[]{:S(2)}, u32[]{:S(2)}) collective-permute-start(bf16[64,768]{1,0:T(8,128)(2,1)} %get-tuple-element.70), channel_id=1, source_target_pairs={{0,2},{2,0},{4,6},{6,4},{8,10},{10,8},{12,14},{14,12},{16,18},{18,... | collective-permute-start | bytes 294920 | tf_op jit(solution)/shard_map/ppermute | solution.py:524
  5.0 7.0 %collective-permute-start.7 = (bf16[64,768]{1,0:T(8,128)(2,1)}, bf16[64,768]{1,0:T(8,128)(2,1)S(1)}, u32[]{:S(2)}, u32[]{:S(2)}) collective-permute-start(bf16[64,768]{1,0:T(8,128)(2,1)} %get-tuple-element.71), channel_id=1, source_target_pairs={{0,4},{2,6},{4,0},{6,2},{8,12},{10,14},{12,8},{14,10},{16,20},{18,... | collective-permute-start | bytes 294920 | tf_op jit(solution)/shard_map/ppermute | solution.py:524
  6.5 5.7 %collective-permute-start.8 = (bf16[64,768]{1,0:T(8,128)(2,1)}, bf16[64,768]{1,0:T(8,128)(2,1)S(1)}, u32[]{:S(2)}, u32[]{:S(2)}) collective-permute-start(bf16[64,768]{1,0:T(8,128)(2,1)} %get-tuple-element.72), channel_id=1, source_target_pairs={{0,6},{2,4},{4,2},{6,0},{8,14},{10,12},{12,10},{14,8},{16,22},{18,... | collective-permute-start | bytes 294920 | tf_op jit(solution)/shard_map/ppermute | solution.py:524
  6.5 10.9 %collective-permute-start = (bf16[32,1024]{1,0:T(8,128)(2,1)}, bf16[32,1024]{1,0:T(8,128)(2,1)S(1)}, u32[]{:S(2)}, u32[]{:S(2)}) collective-permute-start(bf16[32,1024]{1,0:T(8,128)(2,1)} %get-tuple-element.61), channel_id=1, source_target_pairs={{0,8},{2,10},{4,12},{6,14},{8,0},{10,2},{12,4},{14,6},{16,24},{18,... | collective-permute-start | bytes 196616 | tf_op jit(solution)/shard_map/ppermute | solution.py:533
  8.5 11.5 %collective-permute-start.1 = (bf16[32,1024]{1,0:T(8,128)(2,1)}, bf16[32,1024]{1,0:T(8,128)(2,1)S(1)}, u32[]{:S(2)}, u32[]{:S(2)}) collective-permute-start(bf16[32,1024]{1,0:T(8,128)(2,1)} %get-tuple-element.62), channel_id=1, source_target_pairs={{0,16},{2,18},{4,20},{6,22},{8,24},{10,26},{12,28},{14,30},{16,0},... | collective-permute-start | bytes 196616 | tf_op jit(solution)/shard_map/ppermute | solution.py:533
  11.9 8.2 %collective-permute-start.2 = (bf16[32,1024]{1,0:T(8,128)(2,1)}, bf16[32,1024]{1,0:T(8,128)(2,1)S(1)}, u32[]{:S(2)}, u32[]{:S(2)}) collective-permute-start(bf16[32,1024]{1,0:T(8,128)(2,1)} %get-tuple-element.63), channel_id=1, source_target_pairs={{0,24},{2,26},{4,28},{6,30},{8,16},{10,18},{12,20},{14,22},{16,8},... | collective-permute-start | bytes 196616 | tf_op jit(solution)/shard_map/ppermute | solution.py:533
  12.2 0.9 copy-start.4
  13.1 7.0 %copy-start = (bf16[256,1024]{1,0:T(8,128)(2,1)S(1)}, bf16[256,1024]{1,0:T(8,128)(2,1)}, u32[]{:S(2)}) copy-start(bf16[256,1024]{1,0:T(8,128)(2,1)} %own_ref.1) | copy-start | bytes 1572868
  13.1 7.0 %copy-start.5 = (bf16[32,1024]{1,0:T(8,128)(2,1)S(1)}, bf16[32,1024]{1,0:T(8,128)(2,1)}, u32[]{:S(2)}) copy-start(bf16[32,1024]{1,0:T(8,128)(2,1)} %get-tuple-element.60.refs_0_) | copy-start | bytes 196612
  13.2 15.4 %collective-permute-start.9 = (bf16[256,512]{1,0:T(8,128)(2,1)S(1)}, bf16[256,512]{1,0:T(8,128)(2,1)S(1)}, u32[]{:S(2)}, u32[]{:S(2)}) collective-permute-start(bf16[256,512]{1,0:T(8,128)(2,1)S(1)} %get-tuple-element.76.refs_0_), channel_id=1, source_target_pairs={{0,16},{2,18},{4,20},{6,22},{8,24},{10,26},{12,28},{14,30},{16,0},... | collective-permute-start | bytes 786440 | tf_op jit(solution)/shard_map/ppermute | solution.py:533
  15.8 12.7 %collective-permute-start.10 = (bf16[256,512]{1,0:T(8,128)(2,1)S(1)}, bf16[256,512]{1,0:T(8,128)(2,1)S(1)}, u32[]{:S(2)}, u32[]{:S(2)}) collective-permute-start(bf16[256,512]{1,0:T(8,128)(2,1)S(1)} %get-tuple-element.76.refs_0_), channel_id=1, source_target_pairs={{0,8},{2,10},{4,12},{6,14},{8,0},{10,2},{12,4},{14,6},{16,24},{18,... | collective-permute-start | bytes 786440 | tf_op jit(solution)/shard_map/ppermute | solution.py:533
  20.2 10.9 %collective-permute-start.3 = (bf16[192,1024]{1,0:T(8,128)(2,1)S(1)}, bf16[192,1024]{1,0:T(8,128)(2,1)S(1)}, u32[]{:S(2)}, u32[]{:S(2)}) collective-permute-start(bf16[192,1024]{1,0:T(8,128)(2,1)S(1)} %get-tuple-element.65), channel_id=1, source_target_pairs={{0,2},{2,0},{4,6},{6,4},{8,10},{10,8},{12,14},{14,12},{16,18},{18,... | collective-permute-start | bytes 1179656 | tf_op jit(solution)/shard_map/ppermute | solution.py:524
  21.8 14.7 %collective-permute-start.4 = (bf16[192,1024]{1,0:T(8,128)(2,1)S(1)}, bf16[192,1024]{1,0:T(8,128)(2,1)S(1)}, u32[]{:S(2)}, u32[]{:S(2)}) collective-permute-start(bf16[192,1024]{1,0:T(8,128)(2,1)S(1)} %get-tuple-element.66), channel_id=1, source_target_pairs={{0,4},{2,6},{4,0},{6,2},{8,12},{10,14},{12,8},{14,10},{16,20},{18,... | collective-permute-start | bytes 1179656 | tf_op jit(solution)/shard_map/ppermute | solution.py:524
  23.3 13.2 %collective-permute-start.5 = (bf16[192,1024]{1,0:T(8,128)(2,1)S(1)}, bf16[192,1024]{1,0:T(8,128)(2,1)S(1)}, u32[]{:S(2)}, u32[]{:S(2)}) collective-permute-start(bf16[192,1024]{1,0:T(8,128)(2,1)S(1)} %get-tuple-element.67), channel_id=1, source_target_pairs={{0,6},{2,4},{4,2},{6,0},{8,14},{10,12},{12,10},{14,8},{16,22},{18,... | collective-permute-start | bytes 1179656 | tf_op jit(solution)/shard_map/ppermute | solution.py:524
  28.5 9.4 %collective-permute-start.11 = (bf16[256,512]{1,0:T(8,128)(2,1)S(1)}, bf16[256,512]{1,0:T(8,128)(2,1)S(1)}, u32[]{:S(2)}, u32[]{:S(2)}) collective-permute-start(bf16[256,512]{1,0:T(8,128)(2,1)S(1)} %collective-permute-done.9.refs_2_), channel_id=1, source_target_pairs={{8,0},{10,2},{12,4},{14,6},{16,24},{18,26},{20,28},{22,30},{9,1},{... | collective-permute-start | bytes 786440 | tf_op jit(solution)/shard_map/ppermute | solution.py:549
  29.8 8.1 %collective-permute-start.12 = (bf16[256,512]{1,0:T(8,128)(2,1)S(1)}, bf16[256,512]{1,0:T(8,128)(2,1)S(1)}, u32[]{:S(2)}, u32[]{:S(2)}) collective-permute-start(bf16[256,512]{1,0:T(8,128)(2,1)S(1)} %get-tuple-element.76.refs_0_), channel_id=1, source_target_pairs={{8,16},{10,18},{12,20},{14,22},{16,8},{18,10},{20,12},{22,14},{9,1... | collective-permute-start | bytes 786440 | tf_op jit(solution)/shard_map/ppermute | solution.py:550
  31.1 23.3 %collective-permute-start.17 = (bf16[256,256]{1,0:T(8,128)(2,1)S(1)}, bf16[256,256]{1,0:T(8,128)(2,1)S(1)}, u32[]{:S(2)}, u32[]{:S(2)}) collective-permute-start(bf16[256,256]{1,0:T(8,128)(2,1)S(1)} %get-tuple-element.102.refs_0_), channel_id=1, source_target_pairs={{0,16},{2,18},{4,20},{6,22},{8,24},{10,26},{12,28},{14,30},{16,0},... | collective-permute-start | bytes 393224 | tf_op jit(solution)/shard_map/ppermute | solution.py:533
  37.0 2.7 %copy-start.2 = (s32[8]{0:T(128)S(1)}, s32[8]{0:T(128)}, u32[]{:S(2)}) copy-start(s32[8]{0:T(128)} %len_ref.5) | copy-start | bytes 100
  37.0 2.7 %collective-permute-start.13 = (bf16[512,1024]{1,0:T(8,128)(2,1)S(1)}, bf16[512,1024]{1,0:T(8,128)(2,1)S(1)}, u32[]{:S(2)}, u32[]{:S(2)}) collective-permute-start(bf16[512,1024]{1,0:T(8,128)(2,1)S(1)} %get-tuple-element.79), channel_id=1, source_target_pairs={{0,1},{1,0},{2,3},{3,2},{4,5},{5,4},{6,7},{7,6},{8,9},{9,8},{10,11... | collective-permute-start | bytes 3145736 | tf_op jit(solution)/shard_map/ppermute | solution.py:530
  42.5 13.8 %copy-start.3 = (f32[1024]{0:T(1024)S(1)}, f32[1024]{0:T(1024)}, u32[]{:S(2)}) copy-start(f32[1024]{0:T(1024)} %param.14) | copy-start | bytes 12292
  42.5 14.7 %collective-permute-start.14 = (bf16[144,256]{1,0:T(8,128)(2,1)S(1)}, bf16[144,256]{1,0:T(8,128)(2,1)S(1)}, u32[]{:S(2)}, u32[]{:S(2)}) collective-permute-start(bf16[144,256]{1,0:T(8,128)(2,1)S(1)} %get-tuple-element.83), channel_id=1, source_target_pairs={{0,8},{2,10},{4,12},{6,14},{8,16},{10,18},{12,20},{14,22},{16,24},... | collective-permute-start | bytes 221192 | tf_op jit(solution)/shard_map/ppermute | solution.py:527
  50.6 6.6 %collective-permute-start.15 = (bf16[144,256]{1,0:T(8,128)(2,1)S(1)}, bf16[144,256]{1,0:T(8,128)(2,1)S(1)}, u32[]{:S(2)}, u32[]{:S(2)}) collective-permute-start(bf16[144,256]{1,0:T(8,128)(2,1)S(1)} %get-tuple-element.83), channel_id=1, source_target_pairs={{0,16},{2,18},{4,20},{6,22},{8,24},{10,26},{12,28},{14,30},{1,17},... | collective-permute-start | bytes 221192 | tf_op jit(solution)/shard_map/ppermute | solution.py:527
  53.1 4.1 %collective-permute-start.16 = (bf16[144,256]{1,0:T(8,128)(2,1)S(1)}, bf16[144,256]{1,0:T(8,128)(2,1)S(1)}, u32[]{:S(2)}, u32[]{:S(2)}) collective-permute-start(bf16[144,256]{1,0:T(8,128)(2,1)S(1)} %get-tuple-element.83), channel_id=1, source_target_pairs={{0,24},{2,26},{4,28},{6,30},{1,25},{3,27},{5,29},{7,31}} | collective-permute-start | bytes 221192 | tf_op jit(solution)/shard_map/ppermute | solution.py:527
  57.2 6.8 %collective-permute-start.18 = (bf16[256,256]{1,0:T(8,128)(2,1)S(1)}, bf16[256,256]{1,0:T(8,128)(2,1)S(1)}, u32[]{:S(2)}, u32[]{:S(2)}) collective-permute-start(bf16[256,256]{1,0:T(8,128)(2,1)S(1)} %get-tuple-element.102.refs_0_), channel_id=1, source_target_pairs={{0,8},{2,10},{4,12},{6,14},{8,0},{10,2},{12,4},{14,6},{16,24},{18,... | collective-permute-start | bytes 393224 | tf_op jit(solution)/shard_map/ppermute | solution.py:533
  57.3 8.6 %collective-permute-start.19 = (bf16[256,256]{1,0:T(8,128)(2,1)S(1)}, bf16[256,256]{1,0:T(8,128)(2,1)S(1)}, u32[]{:S(2)}, u32[]{:S(2)}) collective-permute-start(bf16[256,256]{1,0:T(8,128)(2,1)S(1)} %get-tuple-element.102.refs_0_), channel_id=1, source_target_pairs={{0,24},{2,26},{4,28},{6,30},{8,16},{10,18},{12,20},{14,22},{16,8},... | collective-permute-start | bytes 393224 | tf_op jit(solution)/shard_map/ppermute | solution.py:533
  61.5 0.9 copy-start.1
  66.0 1.8 %collective-permute-start.21 = (bf16[512,256]{1,0:T(8,128)(2,1)S(1)}, bf16[512,256]{1,0:T(8,128)(2,1)S(1)}, u32[]{:S(2)}, u32[]{:S(2)}) collective-permute-start(bf16[512,256]{1,0:T(8,128)(2,1)S(1)} %get-tuple-element.107), channel_id=1, source_target_pairs={{0,1},{1,0},{2,3},{3,2},{4,5},{5,4},{6,7},{7,6},{8,9},{9,8},{10,11... | collective-permute-start | bytes 786440 | tf_op jit(solution)/shard_map/ppermute | solution.py:530
  66.1 1.7 %collective-permute-start.20 = (bf16[256,256]{1,0:T(8,128)(2,1)S(1)}, bf16[256,256]{1,0:T(8,128)(2,1)S(1)}, u32[]{:S(2)}, u32[]{:S(2)}) collective-permute-start(bf16[256,256]{1,0:T(8,128)(2,1)S(1)} %shard_map.100.refs_0_), channel_id=1, source_target_pairs={{0,1},{1,0},{2,3},{3,2},{4,5},{5,4},{6,7},{7,6},{8,9},{9,8},{10,11... | collective-permute-start | bytes 393224 | tf_op jit(solution)/shard_map/ppermute | solution.py:530
  68.1 9.3 %collective-permute-start.22 = (bf16[256,512]{1,0:T(8,128)(2,1)S(1)}, bf16[256,512]{1,0:T(8,128)(2,1)S(1)}, u32[]{:S(2)}, u32[]{:S(2)}) collective-permute-start(bf16[256,512]{1,0:T(8,128)(2,1)S(1)} %shard_map.102), channel_id=1, source_target_pairs={{0,6},{2,4},{4,2},{6,0},{8,14},{10,12},{12,10},{14,8},{16,22},{18,... | collective-permute-start | bytes 786440 | tf_op jit(solution)/shard_map/ppermute | solution.py:524
  77.4 1.7 %collective-permute-start.23 = (bf16[768,256]{1,0:T(8,128)(2,1)S(1)}, bf16[768,256]{1,0:T(8,128)(2,1)S(1)}, u32[]{:S(2)}, u32[]{:S(2)}) collective-permute-start(bf16[768,256]{1,0:T(8,128)(2,1)S(1)} %shard_map.103.refs_0_), channel_id=1, source_target_pairs={{0,1},{1,0},{2,3},{3,2},{4,5},{5,4},{6,7},{7,6},{8,9},{9,8},{10,11... | collective-permute-start | bytes 1179656 | tf_op jit(solution)/shard_map/ppermute | solution.py:530
  79.8 8.4 %collective-permute-start.24 = (bf16[256,512]{1,0:T(8,128)(2,1)S(1)}, bf16[256,512]{1,0:T(8,128)(2,1)S(1)}, u32[]{:S(2)}, u32[]{:S(2)}) collective-permute-start(bf16[256,512]{1,0:T(8,128)(2,1)S(1)} %get-tuple-element.113), channel_id=1, source_target_pairs={{0,2},{2,0},{4,6},{6,4},{8,10},{10,8},{12,14},{14,12},{16,18},{18,... | collective-permute-start | bytes 786440 | tf_op jit(solution)/shard_map/ppermute | solution.py:524
  81.6 8.1 %collective-permute-start.25 = (bf16[256,512]{1,0:T(8,128)(2,1)S(1)}, bf16[256,512]{1,0:T(8,128)(2,1)S(1)}, u32[]{:S(2)}, u32[]{:S(2)}) collective-permute-start(bf16[256,512]{1,0:T(8,128)(2,1)S(1)} %get-tuple-element.114), channel_id=1, source_target_pairs={{0,4},{2,6},{4,0},{6,2},{8,12},{10,14},{12,8},{14,10},{16,20},{18,... | collective-permute-start | bytes 786440 | tf_op jit(solution)/shard_map/ppermute | solution.py:524

commit v13 on v11

--- a/solution.py
+++ b/solution.py
@@ -24,12 +24,14 @@
     return lax.dot_general(a, b, (dims, ((), ())), precision=precision, preferred_element_type=F32)
 
 
-def call(kernel, out_shape, operands, scratch=(), flops=0, smem=1, anywhere=0, vmem=VMEM_BYTES):
+def call(kernel, out_shape, operands, scratch=(), flops=0, smem=1, anywhere=0, vmem=VMEM_BYTES, hidden=False):
     in_specs = [pl.BlockSpec(memory_space=pltpu.SMEM)] * smem
     in_specs += [pl.BlockSpec(memory_space=pltpu.VMEM)] * (len(operands) - smem - anywhere)
     in_specs += [pl.BlockSpec(memory_space=pl.ANY)] * anywhere
     moved = sum(a.size * a.dtype.itemsize for a in operands)
     moved += sum(a.size * a.dtype.itemsize for a in jax.tree.leaves(out_shape))
+    if hidden:
+        flops = moved = 0
     return pl.pallas_call(
         kernel,
         out_shape=out_shape,
@@ -579,6 +581,8 @@
         smem=0,
     )
     xz_pieces = along_planes([xz_stack] * planes)
+    xz_pieces, out_stack = lax.optimization_barrier((xz_pieces, out_stack))
+    out_pieces = [out_stack] + [between_planes(out_stack, step) for step in range(1, planes)]
     x_columns, z_columns = call(
         functools.partial(assemble_kernel, group, offsets),
         (shape((depth, width), BF16), shape((depth, width), BF16)),
@@ -625,9 +629,10 @@
         ),
         [record_lengths, decay, x_columns, bc_mine, frames, swap, halo, *inward[1:]],
         [pltpu.VMEM((depth, 2 * state), BF16), pltpu.VMEM((total, width), F32)],
-        flops=2 * total * depth * (width + 2 * state),
+        hidden=True,
     )
     summaries = [later(summary, step) for step in range(1, planes)]
+    x_rows, out_pieces = lax.optimization_barrier((x_rows, out_pieces))
     y, carry = call(
         functools.partial(inner_kernel, group, heads),
         (shape((all_rows, width), F32), shape((all_rows, width), F32)),
@@ -642,8 +647,6 @@
         flops=2 * total * depth * width,
         smem=0,
     )
-    out_stack, summaries, y, silu = lax.optimization_barrier((out_stack, summaries, y, silu))
-    out_pieces = [out_stack] + [between_planes(out_stack, step) for step in range(1, planes)]
     gated = call(
         functools.partial(gate_kernel, heads, state),
         shape((all_rows, width), BF16),
@@ -672,11 +675,6 @@
             smem=0,
         )
 
-    far_act = conv(far, gated)
-    far_swapped = [across(far_act, step) for step in range(1, cores)]
-    gated, far_act = lax.optimization_barrier((gated, far_act))
-    near_act = conv(near, gated)
-    near_act, out_pieces = lax.optimization_barrier((near_act, out_pieces))
     share = depth // cores
     out_parts = call(
         functools.partial(share_kernel, cores, tuple(range(planes)), group),
@@ -685,7 +683,12 @@
         [pltpu.VMEM((depth, width), BF16)],
         smem=0,
     )
+    out_parts, gated = lax.optimization_barrier((out_parts, gated))
     out_parts = [out_parts[0]] + [across(out_parts[step], step) for step in range(1, cores)]
+    far_act = conv(far, gated)
+    far_swapped = [across(far_act, step) for step in range(1, cores)]
+    gated, far_act = lax.optimization_barrier((gated, far_act))
+    near_act = conv(near, gated)
     near_act, far_swapped, out_parts = lax.optimization_barrier((near_act, far_swapped, out_parts))
     (far_out,) = out(far, far_act, far_swapped)
     near_act, far_out = lax.optimization_barrier((near_act, far_out))

time: 85.7 us -> 83.2 us (0.971)
  waiting for transfers between devices: 30.7 us -> 24.7 us
  starting transfers between devices: 34 us -> 37.9 us
    ppermute x4, waiting for transfers between devices: 3.88 us -> 0.01 us  [across(): return lax.ppermute(array, 'head', [(i, i ^ step) for i in range(cores)])]
    ppermute x8, waiting for transfers between devices: 9.57 us -> 7.41 us  [between_planes(): lax.ppermute(array, 'tm', [(i, i ^ step * group) for i in range(times)])]
    ppermute x8, starting transfers between devices: 13.4 us -> 15 us  [between_planes(): lax.ppermute(array, 'tm', [(i, i ^ step * group) for i in range(times)])]
    ppermute x3, starting transfers between devices: 6.15 us -> 7.73 us  [later(): lax.ppermute(array, 'tm', [(i, i + step * group) for i in range(times - s...]
  transfers between devices with their start and end apart: 26 -> 26, of which waited for: 12 -> 9; matrix products, arithmetic and copies ran while one was open for 1% -> 1% of each run, Pallas kernels for 15% -> 17%
where the time goes in v13:
time: 83.2 us; the launch traced here: 82.3 us
  starting transfers between devices  37.9 us (46%)
  waiting for transfers between devices  24.7 us (30%)
  Pallas kernels  16.9 us (20%)
  local copies, waits for them, and re-layouts  1.76 us (2%)
  other arithmetic  0.84 us (1%)
    pallas_call x14, Pallas kernels, call(): pl.pallas_call(kernel, out_shape=out_shape, in_specs=in_specs, out_specs=...  16.9 us
    ppermute x9, waiting for transfers between devices, in_plane(): return lax.ppermute(array, 'tm', [(i, i ^ step) for i in range(times)])  16.5 us
    ppermute x8, starting transfers between devices, between_planes(): lax.ppermute(array, 'tm', [(i, i ^ step * group) for i in range(times)])  15 us
    ppermute x9, starting transfers between devices, in_plane(): return lax.ppermute(array, 'tm', [(i, i ^ step) for i in range(times)])  12.4 us
    ppermute x3, starting transfers between devices, later(): lax.ppermute(array, 'tm', [(i, i + step * group) for i in range(times - s...  7.73 us
    ppermute x8, waiting for transfers between devices, between_planes(): lax.ppermute(array, 'tm', [(i, i ^ step * group) for i in range(times)])  7.41 us
  transfers between devices with their start and end apart: 26, of which 9 were waited for; matrix products, arithmetic and copies ran while one was open for 1% of the time, Pallas kernels for 17%

profile of v13, /device:TPU:0, one launch (start us, length us, event | category | flops | bytes accessed | tf_op | source)
XLA Modules:
  0.0 82.3 jit_solution(14908409195877510400)
XLA Ops:
  0.0 2.0 %shard_map.91 = (bf16[64,768]{1,0:T(8,128)(2,1)}, bf16[64,768]{1,0:T(8,128)(2,1)}, bf16[64,768]{1,0:T(8,128)(2,1)}, bf16[64,768]{1,0:T(8,128)(2,1)}, bf16[32,102...) custom-call(f32[16,256]{1,0:T(8,128)} %log_decay_ref.1, ...), custom_call_target="tpu_custom_call" | custom-call | bytes 1622016 | tf_op jit(solution)/shard_map/pallas_call | solution.py:35
  2.0 3.0 %collective-permute-start.6 = (bf16[64,768]{1,0:T(8,128)(2,1)}, bf16[64,768]{1,0:T(8,128)(2,1)S(1)}, u32[]{:S(2)}, u32[]{:S(2)}) collective-permute-start(bf16[64,768]{1,0:T(8,128)(2,1)} %get-tuple-element.75), channel_id=1, source_target_pairs={{0,2},{2,0},{4,6},{6,4},{8,10},{10,8},{12,14},{14,12},{16,18},{18,... | collective-permute-start | bytes 294920 | tf_op jit(solution)/shard_map/ppermute | solution.py:524
  5.0 1.5 %collective-permute-start.7 = (bf16[64,768]{1,0:T(8,128)(2,1)}, bf16[64,768]{1,0:T(8,128)(2,1)S(1)}, u32[]{:S(2)}, u32[]{:S(2)}) collective-permute-start(bf16[64,768]{1,0:T(8,128)(2,1)} %get-tuple-element.76), channel_id=1, source_target_pairs={{0,4},{2,6},{4,0},{6,2},{8,12},{10,14},{12,8},{14,10},{16,20},{18,... | collective-permute-start | bytes 294920 | tf_op jit(solution)/shard_map/ppermute | solution.py:524
  6.5 2.0 %collective-permute-start = (bf16[32,1024]{1,0:T(8,128)(2,1)}, bf16[32,1024]{1,0:T(8,128)(2,1)S(1)}, u32[]{:S(2)}, u32[]{:S(2)}) collective-permute-start(bf16[32,1024]{1,0:T(8,128)(2,1)} %get-tuple-element.66), channel_id=1, source_target_pairs={{0,8},{2,10},{4,12},{6,14},{8,0},{10,2},{12,4},{14,6},{16,24},{18,... | collective-permute-start | bytes 196616 | tf_op jit(solution)/shard_map/ppermute | solution.py:533
  8.5 2.6 %collective-permute-start.1 = (bf16[32,1024]{1,0:T(8,128)(2,1)}, bf16[32,1024]{1,0:T(8,128)(2,1)S(1)}, u32[]{:S(2)}, u32[]{:S(2)}) collective-permute-start(bf16[32,1024]{1,0:T(8,128)(2,1)} %get-tuple-element.67), channel_id=1, source_target_pairs={{0,16},{2,18},{4,20},{6,22},{8,24},{10,26},{12,28},{14,30},{16,0},... | collective-permute-start | bytes 196616 | tf_op jit(solution)/shard_map/ppermute | solution.py:533
  11.1 0.7 reshape.3
  12.0 0.2 collective-permute-done.8.refs_3_
  12.2 0.9 %copy-done.4 = bf16[64,768]{1,0:T(8,128)(2,1)S(1)} copy-done((bf16[64,768]{1,0:T(8,128)(2,1)S(1)}, bf16[64,768]{1,0:T(8,128)(2,1)}, u32[]{:S(2)}) %copy-start.4) | copy-done | bytes 98328
  13.2 2.7 %collective-permute-start.9 = (bf16[256,512]{1,0:T(8,128)(2,1)S(1)}, bf16[256,512]{1,0:T(8,128)(2,1)S(1)}, u32[]{:S(2)}, u32[]{:S(2)}) collective-permute-start(bf16[256,512]{1,0:T(8,128)(2,1)S(1)} %get-tuple-element.83.refs_0_), channel_id=1, source_target_pairs={{0,16},{2,18},{4,20},{6,22},{8,24},{10,26},{12,28},{14,30},{16,0},... | collective-permute-start | bytes 786440 | tf_op jit(solution)/shard_map/ppermute | solution.py:533
  15.8 1.6 %collective-permute-start.10 = (bf16[256,512]{1,0:T(8,128)(2,1)S(1)}, bf16[256,512]{1,0:T(8,128)(2,1)S(1)}, u32[]{:S(2)}, u32[]{:S(2)}) collective-permute-start(bf16[256,512]{1,0:T(8,128)(2,1)S(1)} %get-tuple-element.83.refs_0_), channel_id=1, source_target_pairs={{0,8},{2,10},{4,12},{6,14},{8,0},{10,2},{12,4},{14,6},{16,24},{18,... | collective-permute-start | bytes 786440 | tf_op jit(solution)/shard_map/ppermute | solution.py:533
  17.4 2.7 %collective-permute-done.1.refs_2_ = bf16[32,1024]{1,0:T(8,128)(2,1)S(1)} collective-permute-done((bf16[32,1024]{1,0:T(8,128)(2,1)}, bf16[32,1024]{1,0:T(8,128)(2,1)S(1)}, u32[]{:S(2)}, u32[]{:S(2)}) %collective-permute-start.1) | collective-permute-done | bytes 65568 | tf_op jit(solution)/shard_map/ppermute | solution.py:533
  20.1 0.2 shard_map.92
  20.2 1.6 %collective-permute-start.3 = (bf16[192,1024]{1,0:T(8,128)(2,1)S(1)}, bf16[192,1024]{1,0:T(8,128)(2,1)S(1)}, u32[]{:S(2)}, u32[]{:S(2)}) collective-permute-start(bf16[192,1024]{1,0:T(8,128)(2,1)S(1)} %get-tuple-element.70), channel_id=1, source_target_pairs={{0,2},{2,0},{4,6},{6,4},{8,10},{10,8},{12,14},{14,12},{16,18},{18,... | collective-permute-start | bytes 1179656 | tf_op jit(solution)/shard_map/ppermute | solution.py:524
  21.8 1.5 %collective-permute-start.4 = (bf16[192,1024]{1,0:T(8,128)(2,1)S(1)}, bf16[192,1024]{1,0:T(8,128)(2,1)S(1)}, u32[]{:S(2)}, u32[]{:S(2)}) collective-permute-start(bf16[192,1024]{1,0:T(8,128)(2,1)S(1)} %get-tuple-element.71), channel_id=1, source_target_pairs={{0,4},{2,6},{4,0},{6,2},{8,12},{10,14},{12,8},{14,10},{16,20},{18,... | collective-permute-start | bytes 1179656 | tf_op jit(solution)/shard_map/ppermute | solution.py:524
  23.3 0.5 collective-permute-start.5
  23.8 4.7 %collective-permute-done.9.refs_2_ = bf16[256,512]{1,0:T(8,128)(2,1)S(1)} collective-permute-done((bf16[256,512]{1,0:T(8,128)(2,1)S(1)}, bf16[256,512]{1,0:T(8,128)(2,1)S(1)}, u32[]{:S(2)}, u32[]{:S(2)}) %collective-permute-start.9) | collective-permute-done | bytes 262176 | tf_op jit(solution)/shard_map/ppermute | solution.py:533
  28.5 1.3 %collective-permute-start.11 = (bf16[256,512]{1,0:T(8,128)(2,1)S(1)}, bf16[256,512]{1,0:T(8,128)(2,1)S(1)}, u32[]{:S(2)}, u32[]{:S(2)}) collective-permute-start(bf16[256,512]{1,0:T(8,128)(2,1)S(1)} %collective-permute-done.9.refs_2_), channel_id=1, source_target_pairs={{8,0},{10,2},{12,4},{14,6},{16,24},{18,26},{20,28},{22,30},{9,1},{... | collective-permute-start | bytes 786440 | tf_op jit(solution)/shard_map/ppermute | solution.py:549
  29.8 0.7 collective-permute-start.12
  30.5 0.6 collective-permute-done.3.refs_1_.refs_0_
  31.1 5.4 %collective-permute-done.4.refs_2_.refs_1_ = bf16[192,1024]{1,0:T(8,128)(2,1)S(1)} collective-permute-done((bf16[192,1024]{1,0:T(8,128)(2,1)S(1)}, bf16[192,1024]{1,0:T(8,128)(2,1)S(1)}, u32[]{:S(2)}, u32[]{:S(2)}) %collective-permute-start.4) | collective-permute-done | bytes 393248 | tf_op jit(solution)/shard_map/ppermute | solution.py:524
  36.5 0.5 shard_map.93
  37.1 0.8 collective-permute-done.11.refs_3_
  37.9 3.7 %collective-permute-start.14 = (bf16[256,256]{1,0:T(8,128)(2,1)S(1)}, bf16[256,256]{1,0:T(8,128)(2,1)S(1)}, u32[]{:S(2)}, u32[]{:S(2)}) collective-permute-start(bf16[256,256]{1,0:T(8,128)(2,1)S(1)} %get-tuple-element.94.refs_0_), channel_id=1, source_target_pairs={{0,8},{2,10},{4,12},{6,14},{8,0},{10,2},{12,4},{14,6},{16,24},{18,... | collective-permute-start | bytes 393224 | tf_op jit(solution)/shard_map/ppermute | solution.py:533
  41.6 0.6 collective-permute-start.15
  42.2 1.8 %collective-permute-start.16 = (bf16[256,256]{1,0:T(8,128)(2,1)S(1)}, bf16[256,256]{1,0:T(8,128)(2,1)S(1)}, u32[]{:S(2)}, u32[]{:S(2)}) collective-permute-start(bf16[256,256]{1,0:T(8,128)(2,1)S(1)} %get-tuple-element.94.refs_0_), channel_id=1, source_target_pairs={{0,24},{2,26},{4,28},{6,30},{8,16},{10,18},{12,20},{14,22},{16,8},... | collective-permute-start | bytes 393224 | tf_op jit(solution)/shard_map/ppermute | solution.py:533
  43.9 0.1 shard_map.95
  44.0 2.8 %shard_map.96 = (bf16[1152,1024]{1,0:T(8,128)(2,1)S(1)}, bf16[1152,256]{1,0:T(8,128)(2,1)S(1)}, bf16[1152,128]{1,0:T(8,128)(2,1)S(1)}, bf16[1152,128]{1,0:T(8,12...) custom-call(s32[8]{0:T(128)S(1)} %copy-done.2, ...), custom_call_target="tpu_custom_call" | custom-call | tf_op jit(solution)/shard_map/pallas_call | solution.py:35
  46.9 3.0 %collective-permute-start.17 = (bf16[144,256]{1,0:T(8,128)(2,1)S(1)}, bf16[144,256]{1,0:T(8,128)(2,1)S(1)}, u32[]{:S(2)}, u32[]{:S(2)}) collective-permute-start(bf16[144,256]{1,0:T(8,128)(2,1)S(1)} %get-tuple-element.110), channel_id=1, source_target_pairs={{0,8},{2,10},{4,12},{6,14},{8,16},{10,18},{12,20},{14,22},{16,24},... | collective-permute-start | bytes 221192 | tf_op jit(solution)/shard_map/ppermute | solution.py:527
  49.9 3.4 %collective-permute-start.18 = (bf16[144,256]{1,0:T(8,128)(2,1)S(1)}, bf16[144,256]{1,0:T(8,128)(2,1)S(1)}, u32[]{:S(2)}, u32[]{:S(2)}) collective-permute-start(bf16[144,256]{1,0:T(8,128)(2,1)S(1)} %get-tuple-element.110), channel_id=1, source_target_pairs={{0,16},{2,18},{4,20},{6,22},{8,24},{10,26},{12,28},{14,30},{1,17},... | collective-permute-start | bytes 221192 | tf_op jit(solution)/shard_map/ppermute | solution.py:527
  53.3 1.3 %collective-permute-start.19 = (bf16[144,256]{1,0:T(8,128)(2,1)S(1)}, bf16[144,256]{1,0:T(8,128)(2,1)S(1)}, u32[]{:S(2)}, u32[]{:S(2)}) collective-permute-start(bf16[144,256]{1,0:T(8,128)(2,1)S(1)} %get-tuple-element.110), channel_id=1, source_target_pairs={{0,24},{2,26},{4,28},{6,30},{1,25},{3,27},{5,29},{7,31}} | collective-permute-start | bytes 221192 | tf_op jit(solution)/shard_map/ppermute | solution.py:527
  54.6 0.1 shard_map.97
  54.7 1.9 %shard_map.98 = (f32[1152,256]{1,0:T(8,128)S(1)}, f32[1152,256]{1,0:T(8,128)S(1)}) custom-call(bf16[1152,256]{1,0:T(8,128)(2,1)S(1)} %get-tuple-element.101.x_ref, bf16[1152,128]{1,0:T(8,128)(2,1)S(1)} %get-tuple-element.102.b_ref, bf16[1152,128]{1,0:T(8,128)(2,1)S(1)} %get-tuple-element.100.c_ref, f32[216,128]{1,0:T(8,128)S(1)} %get-tuple-element.103.rows_ref), custom_call_target="tpu_custom_call" | custom-call | flops 134217728 | bytes 3649536 | tf_op jit(solution)/shard_map/pallas_call | solution.py:35
  56.6 0.8 %shard_map.99.silu_ref = f32[1152,256]{1,0:T(8,128)S(1)} custom-call(f32[1,1024]{1,0:T(1,128)S(1)} %bitcast.2, bf16[1152,1024]{1,0:T(8,128)(2,1)S(1)} %get-tuple-element.108.frames_ref, bf16[1024,256]{1,0:T(8,128)(2,1)S(1)} %get-tuple-element.109.weight_ref), custom_call_target="tpu_custom_call" | custom-call | flops 536870912 | bytes 4067328 | tf_op jit(solution)/shard_map/pallas_call | solution.py:35
  57.5 0.7 shard_map.100.gated_ref
  58.3 0.1 copy-done.1
  58.4 2.1 %shard_map.101.refs_0_ = bf16[256,256]{1,0:T(8,128)(2,1)S(1)} custom-call(s32[8]{0:T(128)S(1)} %copy-done.2, f32[31,1024]{1,0:T(8,128)S(1)} %copy-done.1, bf16[1152,256]{1,0:T(8,128)(2,1)S(1)} %shard_map.100.gated_ref), custom_call_target="tpu_custom_call" | custom-call | flops 4063232 | bytes 847904 | tf_op jit(solution)/shard_map/pallas_call | solution.py:35
  60.5 0.5 collective-permute-start.20
  60.9 4.9 %shard_map.102.refs_0_ = bf16[768,256]{1,0:T(8,128)(2,1)S(1)} custom-call(s32[8]{0:T(128)S(1)} %copy-done.2, f32[31,1024]{1,0:T(8,128)S(1)} %copy-done.1, bf16[1152,256]{1,0:T(8,128)(2,1)S(1)} %shard_map.100.gated_ref), custom_call_target="tpu_custom_call" | custom-call | flops 12189696 | bytes 1110048 | tf_op jit(solution)/shard_map/pallas_call | solution.py:35
  65.8 0.3 shard_map.103
  66.2 0.2 collective-permute-start.22
  66.4 2.1 %collective-permute-start.23 = (bf16[256,512]{1,0:T(8,128)(2,1)S(1)}, bf16[256,512]{1,0:T(8,128)(2,1)S(1)}, u32[]{:S(2)}, u32[]{:S(2)}) collective-permute-start(bf16[256,512]{1,0:T(8,128)(2,1)S(1)} %shard_map.103), channel_id=1, source_target_pairs={{0,6},{2,4},{4,2},{6,0},{8,14},{10,12},{12,10},{14,8},{16,22},{18,... | collective-permute-start | bytes 786440 | tf_op jit(solution)/shard_map/ppermute | solution.py:524
  68.5 0.6 shard_map.104
  69.1 1.6 %collective-permute-start.24 = (bf16[256,512]{1,0:T(8,128)(2,1)S(1)}, bf16[256,512]{1,0:T(8,128)(2,1)S(1)}, u32[]{:S(2)}, u32[]{:S(2)}) collective-permute-start(bf16[256,512]{1,0:T(8,128)(2,1)S(1)} %get-tuple-element.123), channel_id=1, source_target_pairs={{0,2},{2,0},{4,6},{6,4},{8,10},{10,8},{12,14},{14,12},{16,18},{18,... | collective-permute-start | bytes 786440 | tf_op jit(solution)/shard_map/ppermute | solution.py:524
  70.7 0.6 collective-permute-start.25
  71.3 5.2 %collective-permute-done.23 = bf16[256,512]{1,0:T(8,128)(2,1)S(1)} collective-permute-done((bf16[256,512]{1,0:T(8,128)(2,1)S(1)}, bf16[256,512]{1,0:T(8,128)(2,1)S(1)}, u32[]{:S(2)}, u32[]{:S(2)}) %collective-permute-start.23) | collective-permute-done | bytes 262176 | tf_op jit(solution)/shard_map/ppermute | solution.py:524
  76.5 4.8 %collective-permute-done.24 = bf16[256,512]{1,0:T(8,128)(2,1)S(1)} collective-permute-done((bf16[256,512]{1,0:T(8,128)(2,1)S(1)}, bf16[256,512]{1,0:T(8,128)(2,1)S(1)}, u32[]{:S(2)}, u32[]{:S(2)}) %collective-permute-start.24) | collective-permute-done | bytes 262176 | tf_op jit(solution)/shard_map/ppermute | solution.py:524
  81.2 0.3 collective-permute-done.25
  81.5 0.8 %add_convert_fusion = bf16[256,512]{1,0:T(8,128)(2,1)} fusion(bf16[256,512]{1,0:T(8,128)(2,1)S(1)} %collective-permute-done.25, bf16[256,512]{1,0:T(8,128)(2,1)S(1)} %collective-permute-done.24, f32[256,512]{1,0:T(8,128)S(1)} %get-tuple-element.121, bf16[256,512]{1,0:T(8,128)(2,1)S(1)} %collective-permute-done.23), kind=kLoop, calls=%fused_computation | loop fusion | flops 917504 | bytes 1572864 | tf_op jit(solution)/shard_map/convert_element_type | solution.py:701
  (33 shorter events, 0.3 us)
Async XLA Ops:
  2.0 9.9 %collective-permute-start.6 = (bf16[64,768]{1,0:T(8,128)(2,1)}, bf16[64,768]{1,0:T(8,128)(2,1)S(1)}, u32[]{:S(2)}, u32[]{:S(2)}) collective-permute-start(bf16[64,768]{1,0:T(8,128)(2,1)} %get-tuple-element.75), channel_id=1, source_target_pairs={{0,2},{2,0},{4,6},{6,4},{8,10},{10,8},{12,14},{14,12},{16,18},{18,... | collective-permute-start | bytes 294920 | tf_op jit(solution)/shard_map/ppermute | solution.py:524
  5.0 7.0 %collective-permute-start.7 = (bf16[64,768]{1,0:T(8,128)(2,1)}, bf16[64,768]{1,0:T(8,128)(2,1)S(1)}, u32[]{:S(2)}, u32[]{:S(2)}) collective-permute-start(bf16[64,768]{1,0:T(8,128)(2,1)} %get-tuple-element.76), channel_id=1, source_target_pairs={{0,4},{2,6},{4,0},{6,2},{8,12},{10,14},{12,8},{14,10},{16,20},{18,... | collective-permute-start | bytes 294920 | tf_op jit(solution)/shard_map/ppermute | solution.py:524
  6.5 5.7 %collective-permute-start.8 = (bf16[64,768]{1,0:T(8,128)(2,1)}, bf16[64,768]{1,0:T(8,128)(2,1)S(1)}, u32[]{:S(2)}, u32[]{:S(2)}) collective-permute-start(bf16[64,768]{1,0:T(8,128)(2,1)} %get-tuple-element.77), channel_id=1, source_target_pairs={{0,6},{2,4},{4,2},{6,0},{8,14},{10,12},{12,10},{14,8},{16,22},{18,... | collective-permute-start | bytes 294920 | tf_op jit(solution)/shard_map/ppermute | solution.py:524
  6.5 10.9 %collective-permute-start = (bf16[32,1024]{1,0:T(8,128)(2,1)}, bf16[32,1024]{1,0:T(8,128)(2,1)S(1)}, u32[]{:S(2)}, u32[]{:S(2)}) collective-permute-start(bf16[32,1024]{1,0:T(8,128)(2,1)} %get-tuple-element.66), channel_id=1, source_target_pairs={{0,8},{2,10},{4,12},{6,14},{8,0},{10,2},{12,4},{14,6},{16,24},{18,... | collective-permute-start | bytes 196616 | tf_op jit(solution)/shard_map/ppermute | solution.py:533
  8.5 11.5 %collective-permute-start.1 = (bf16[32,1024]{1,0:T(8,128)(2,1)}, bf16[32,1024]{1,0:T(8,128)(2,1)S(1)}, u32[]{:S(2)}, u32[]{:S(2)}) collective-permute-start(bf16[32,1024]{1,0:T(8,128)(2,1)} %get-tuple-element.67), channel_id=1, source_target_pairs={{0,16},{2,18},{4,20},{6,22},{8,24},{10,26},{12,28},{14,30},{16,0},... | collective-permute-start | bytes 196616 | tf_op jit(solution)/shard_map/ppermute | solution.py:533
  11.9 8.2 %collective-permute-start.2 = (bf16[32,1024]{1,0:T(8,128)(2,1)}, bf16[32,1024]{1,0:T(8,128)(2,1)S(1)}, u32[]{:S(2)}, u32[]{:S(2)}) collective-permute-start(bf16[32,1024]{1,0:T(8,128)(2,1)} %get-tuple-element.68), channel_id=1, source_target_pairs={{0,24},{2,26},{4,28},{6,30},{8,16},{10,18},{12,20},{14,22},{16,8},... | collective-permute-start | bytes 196616 | tf_op jit(solution)/shard_map/ppermute | solution.py:533
  12.2 0.9 %copy-start.4 = (bf16[64,768]{1,0:T(8,128)(2,1)S(1)}, bf16[64,768]{1,0:T(8,128)(2,1)}, u32[]{:S(2)}) copy-start(bf16[64,768]{1,0:T(8,128)(2,1)} %get-tuple-element.74.refs_0_) | copy-start | bytes 294916
  13.1 7.0 %copy-start = (bf16[256,1024]{1,0:T(8,128)(2,1)S(1)}, bf16[256,1024]{1,0:T(8,128)(2,1)}, u32[]{:S(2)}) copy-start(bf16[256,1024]{1,0:T(8,128)(2,1)} %own_ref.1) | copy-start | bytes 1572868
  13.1 7.0 %copy-start.5 = (bf16[32,1024]{1,0:T(8,128)(2,1)S(1)}, bf16[32,1024]{1,0:T(8,128)(2,1)}, u32[]{:S(2)}) copy-start(bf16[32,1024]{1,0:T(8,128)(2,1)} %get-tuple-element.65.refs_0_) | copy-start | bytes 196612
  13.2 15.4 %collective-permute-start.9 = (bf16[256,512]{1,0:T(8,128)(2,1)S(1)}, bf16[256,512]{1,0:T(8,128)(2,1)S(1)}, u32[]{:S(2)}, u32[]{:S(2)}) collective-permute-start(bf16[256,512]{1,0:T(8,128)(2,1)S(1)} %get-tuple-element.83.refs_0_), channel_id=1, source_target_pairs={{0,16},{2,18},{4,20},{6,22},{8,24},{10,26},{12,28},{14,30},{16,0},... | collective-permute-start | bytes 786440 | tf_op jit(solution)/shard_map/ppermute | solution.py:533
  15.8 12.7 %collective-permute-start.10 = (bf16[256,512]{1,0:T(8,128)(2,1)S(1)}, bf16[256,512]{1,0:T(8,128)(2,1)S(1)}, u32[]{:S(2)}, u32[]{:S(2)}) collective-permute-start(bf16[256,512]{1,0:T(8,128)(2,1)S(1)} %get-tuple-element.83.refs_0_), channel_id=1, source_target_pairs={{0,8},{2,10},{4,12},{6,14},{8,0},{10,2},{12,4},{14,6},{16,24},{18,... | collective-permute-start | bytes 786440 | tf_op jit(solution)/shard_map/ppermute | solution.py:533
  20.2 10.9 %collective-permute-start.3 = (bf16[192,1024]{1,0:T(8,128)(2,1)S(1)}, bf16[192,1024]{1,0:T(8,128)(2,1)S(1)}, u32[]{:S(2)}, u32[]{:S(2)}) collective-permute-start(bf16[192,1024]{1,0:T(8,128)(2,1)S(1)} %get-tuple-element.70), channel_id=1, source_target_pairs={{0,2},{2,0},{4,6},{6,4},{8,10},{10,8},{12,14},{14,12},{16,18},{18,... | collective-permute-start | bytes 1179656 | tf_op jit(solution)/shard_map/ppermute | solution.py:524
  21.8 14.7 %collective-permute-start.4 = (bf16[192,1024]{1,0:T(8,128)(2,1)S(1)}, bf16[192,1024]{1,0:T(8,128)(2,1)S(1)}, u32[]{:S(2)}, u32[]{:S(2)}) collective-permute-start(bf16[192,1024]{1,0:T(8,128)(2,1)S(1)} %get-tuple-element.71), channel_id=1, source_target_pairs={{0,4},{2,6},{4,0},{6,2},{8,12},{10,14},{12,8},{14,10},{16,20},{18,... | collective-permute-start | bytes 1179656 | tf_op jit(solution)/shard_map/ppermute | solution.py:524
  23.3 13.2 %collective-permute-start.5 = (bf16[192,1024]{1,0:T(8,128)(2,1)S(1)}, bf16[192,1024]{1,0:T(8,128)(2,1)S(1)}, u32[]{:S(2)}, u32[]{:S(2)}) collective-permute-start(bf16[192,1024]{1,0:T(8,128)(2,1)S(1)} %get-tuple-element.72), channel_id=1, source_target_pairs={{0,6},{2,4},{4,2},{6,0},{8,14},{10,12},{12,10},{14,8},{16,22},{18,... | collective-permute-start | bytes 1179656 | tf_op jit(solution)/shard_map/ppermute | solution.py:524
  28.5 9.4 %collective-permute-start.11 = (bf16[256,512]{1,0:T(8,128)(2,1)S(1)}, bf16[256,512]{1,0:T(8,128)(2,1)S(1)}, u32[]{:S(2)}, u32[]{:S(2)}) collective-permute-start(bf16[256,512]{1,0:T(8,128)(2,1)S(1)} %collective-permute-done.9.refs_2_), channel_id=1, source_target_pairs={{8,0},{10,2},{12,4},{14,6},{16,24},{18,26},{20,28},{22,30},{9,1},{... | collective-permute-start | bytes 786440 | tf_op jit(solution)/shard_map/ppermute | solution.py:549
  29.8 8.1 %collective-permute-start.12 = (bf16[256,512]{1,0:T(8,128)(2,1)S(1)}, bf16[256,512]{1,0:T(8,128)(2,1)S(1)}, u32[]{:S(2)}, u32[]{:S(2)}) collective-permute-start(bf16[256,512]{1,0:T(8,128)(2,1)S(1)} %get-tuple-element.83.refs_0_), channel_id=1, source_target_pairs={{8,16},{10,18},{12,20},{14,22},{16,8},{18,10},{20,12},{22,14},{9,1... | collective-permute-start | bytes 786440 | tf_op jit(solution)/shard_map/ppermute | solution.py:550
  37.0 7.0 %collective-permute-start.13 = (bf16[512,1024]{1,0:T(8,128)(2,1)S(1)}, bf16[512,1024]{1,0:T(8,128)(2,1)S(1)}, u32[]{:S(2)}, u32[]{:S(2)}) collective-permute-start(bf16[512,1024]{1,0:T(8,128)(2,1)S(1)} %get-tuple-element.90), channel_id=1, source_target_pairs={{0,1},{1,0},{2,3},{3,2},{4,5},{5,4},{6,7},{7,6},{8,9},{9,8},{10,11... | collective-permute-start | bytes 3145736 | tf_op jit(solution)/shard_map/ppermute | solution.py:530
  37.9 6.2 %copy-start.2 = (s32[8]{0:T(128)S(1)}, s32[8]{0:T(128)}, u32[]{:S(2)}) copy-start(s32[8]{0:T(128)} %len_ref.5) | copy-start | bytes 100
  37.9 15.4 %collective-permute-start.14 = (bf16[256,256]{1,0:T(8,128)(2,1)S(1)}, bf16[256,256]{1,0:T(8,128)(2,1)S(1)}, u32[]{:S(2)}, u32[]{:S(2)}) collective-permute-start(bf16[256,256]{1,0:T(8,128)(2,1)S(1)} %get-tuple-element.94.refs_0_), channel_id=1, source_target_pairs={{0,8},{2,10},{4,12},{6,14},{8,0},{10,2},{12,4},{14,6},{16,24},{18,... | collective-permute-start | bytes 393224 | tf_op jit(solution)/shard_map/ppermute | solution.py:533
  41.6 13.1 %collective-permute-start.15 = (bf16[256,256]{1,0:T(8,128)(2,1)S(1)}, bf16[256,256]{1,0:T(8,128)(2,1)S(1)}, u32[]{:S(2)}, u32[]{:S(2)}) collective-permute-start(bf16[256,256]{1,0:T(8,128)(2,1)S(1)} %get-tuple-element.94.refs_0_), channel_id=1, source_target_pairs={{0,16},{2,18},{4,20},{6,22},{8,24},{10,26},{12,28},{14,30},{16,0},... | collective-permute-start | bytes 393224 | tf_op jit(solution)/shard_map/ppermute | solution.py:533
  42.2 12.5 %collective-permute-start.16 = (bf16[256,256]{1,0:T(8,128)(2,1)S(1)}, bf16[256,256]{1,0:T(8,128)(2,1)S(1)}, u32[]{:S(2)}, u32[]{:S(2)}) collective-permute-start(bf16[256,256]{1,0:T(8,128)(2,1)S(1)} %get-tuple-element.94.refs_0_), channel_id=1, source_target_pairs={{0,24},{2,26},{4,28},{6,30},{8,16},{10,18},{12,20},{14,22},{16,8},... | collective-permute-start | bytes 393224 | tf_op jit(solution)/shard_map/ppermute | solution.py:533
  46.8 9.8 %copy-start.3 = (f32[1024]{0:T(1024)S(1)}, f32[1024]{0:T(1024)}, u32[]{:S(2)}) copy-start(f32[1024]{0:T(1024)} %param.14) | copy-start | bytes 12292
  46.9 10.6 %collective-permute-start.17 = (bf16[144,256]{1,0:T(8,128)(2,1)S(1)}, bf16[144,256]{1,0:T(8,128)(2,1)S(1)}, u32[]{:S(2)}, u32[]{:S(2)}) collective-permute-start(bf16[144,256]{1,0:T(8,128)(2,1)S(1)} %get-tuple-element.110), channel_id=1, source_target_pairs={{0,8},{2,10},{4,12},{6,14},{8,16},{10,18},{12,20},{14,22},{16,24},... | collective-permute-start | bytes 221192 | tf_op jit(solution)/shard_map/ppermute | solution.py:527
  49.9 7.6 %collective-permute-start.18 = (bf16[144,256]{1,0:T(8,128)(2,1)S(1)}, bf16[144,256]{1,0:T(8,128)(2,1)S(1)}, u32[]{:S(2)}, u32[]{:S(2)}) collective-permute-start(bf16[144,256]{1,0:T(8,128)(2,1)S(1)} %get-tuple-element.110), channel_id=1, source_target_pairs={{0,16},{2,18},{4,20},{6,22},{8,24},{10,26},{12,28},{14,30},{1,17},... | collective-permute-start | bytes 221192 | tf_op jit(solution)/shard_map/ppermute | solution.py:527
  53.3 4.2 %collective-permute-start.19 = (bf16[144,256]{1,0:T(8,128)(2,1)S(1)}, bf16[144,256]{1,0:T(8,128)(2,1)S(1)}, u32[]{:S(2)}, u32[]{:S(2)}) collective-permute-start(bf16[144,256]{1,0:T(8,128)(2,1)S(1)} %get-tuple-element.110), channel_id=1, source_target_pairs={{0,24},{2,26},{4,28},{6,30},{1,25},{3,27},{5,29},{7,31}} | collective-permute-start | bytes 221192 | tf_op jit(solution)/shard_map/ppermute | solution.py:527
  57.5 0.9 %copy-start.1 = (f32[31,1024]{1,0:T(8,128)S(1)}, f32[31,1024]{1,0:T(8,128)}, u32[]{:S(2)}) copy-start(f32[31,1024]{1,0:T(8,128)} %taps_ref.3) | copy-start | bytes 380932
  58.2 7.6 %collective-permute-start.21 = (bf16[512,256]{1,0:T(8,128)(2,1)S(1)}, bf16[512,256]{1,0:T(8,128)(2,1)S(1)}, u32[]{:S(2)}, u32[]{:S(2)}) collective-permute-start(bf16[512,256]{1,0:T(8,128)(2,1)S(1)} %get-tuple-element.114), channel_id=1, source_target_pairs={{0,1},{1,0},{2,3},{3,2},{4,5},{5,4},{6,7},{7,6},{8,9},{9,8},{10,11... | collective-permute-start | bytes 786440 | tf_op jit(solution)/shard_map/ppermute | solution.py:530
  60.5 5.3 %collective-permute-start.20 = (bf16[256,256]{1,0:T(8,128)(2,1)S(1)}, bf16[256,256]{1,0:T(8,128)(2,1)S(1)}, u32[]{:S(2)}, u32[]{:S(2)}) collective-permute-start(bf16[256,256]{1,0:T(8,128)(2,1)S(1)} %shard_map.101.refs_0_), channel_id=1, source_target_pairs={{0,1},{1,0},{2,3},{3,2},{4,5},{5,4},{6,7},{7,6},{8,9},{9,8},{10,11... | collective-permute-start | bytes 393224 | tf_op jit(solution)/shard_map/ppermute | solution.py:530
  66.2 2.3 %collective-permute-start.22 = (bf16[768,256]{1,0:T(8,128)(2,1)S(1)}, bf16[768,256]{1,0:T(8,128)(2,1)S(1)}, u32[]{:S(2)}, u32[]{:S(2)}) collective-permute-start(bf16[768,256]{1,0:T(8,128)(2,1)S(1)} %shard_map.102.refs_0_), channel_id=1, source_target_pairs={{0,1},{1,0},{2,3},{3,2},{4,5},{5,4},{6,7},{7,6},{8,9},{9,8},{10,11... | collective-permute-start | bytes 1179656 | tf_op jit(solution)/shard_map/ppermute | solution.py:530
  66.4 10.1 %collective-permute-start.23 = (bf16[256,512]{1,0:T(8,128)(2,1)S(1)}, bf16[256,512]{1,0:T(8,128)(2,1)S(1)}, u32[]{:S(2)}, u32[]{:S(2)}) collective-permute-start(bf16[256,512]{1,0:T(8,128)(2,1)S(1)} %shard_map.103), channel_id=1, source_target_pairs={{0,6},{2,4},{4,2},{6,0},{8,14},{10,12},{12,10},{14,8},{16,22},{18,... | collective-permute-start | bytes 786440 | tf_op jit(solution)/shard_map/ppermute | solution.py:524
  69.1 12.1 %collective-permute-start.24 = (bf16[256,512]{1,0:T(8,128)(2,1)S(1)}, bf16[256,512]{1,0:T(8,128)(2,1)S(1)}, u32[]{:S(2)}, u32[]{:S(2)}) collective-permute-start(bf16[256,512]{1,0:T(8,128)(2,1)S(1)} %get-tuple-element.123), channel_id=1, source_target_pairs={{0,2},{2,0},{4,6},{6,4},{8,10},{10,8},{12,14},{14,12},{16,18},{18,... | collective-permute-start | bytes 786440 | tf_op jit(solution)/shard_map/ppermute | solution.py:524
  70.7 10.7 %collective-permute-start.25 = (bf16[256,512]{1,0:T(8,128)(2,1)S(1)}, bf16[256,512]{1,0:T(8,128)(2,1)S(1)}, u32[]{:S(2)}, u32[]{:S(2)}) collective-permute-start(bf16[256,512]{1,0:T(8,128)(2,1)S(1)} %get-tuple-element.124), channel_id=1, source_target_pairs={{0,4},{2,6},{4,0},{6,2},{8,12},{10,14},{12,8},{14,10},{16,20},{18,... | collective-permute-start | bytes 786440 | tf_op jit(solution)/shard_map/ppermute | solution.py:524

commit v14 on v13

--- a/solution.py
+++ b/solution.py
@@ -655,7 +655,6 @@
         smem=0,
     )
     ends = pltpu.SMEM((record_lengths.shape[0] + 1,), jnp.int32)
-    far, near = (group - 1,), (*range(1, group - 1), 0)
 
     def conv(steps, gated):
         return call(
@@ -685,19 +684,27 @@
     )
     out_parts, gated = lax.optimization_barrier((out_parts, gated))
     out_parts = [out_parts[0]] + [across(out_parts[step], step) for step in range(1, cores)]
-    far_act = conv(far, gated)
-    far_swapped = [across(far_act, step) for step in range(1, cores)]
-    gated, far_act = lax.optimization_barrier((gated, far_act))
-    near_act = conv(near, gated)
-    near_act, far_swapped, out_parts = lax.optimization_barrier((near_act, far_swapped, out_parts))
-    (far_out,) = out(far, far_act, far_swapped)
-    near_act, far_out = lax.optimization_barrier((near_act, far_out))
-    far_out = in_plane(far_out, far[0])
-    near_swapped = [across(near_act, step) for step in range(1, cores)]
-    near_outs = out(near, near_act, near_swapped)
-    mixed = near_outs[-1] + far_out.astype(F32)
-    for step, partial in zip(near[:-1], near_outs[:-1]):
-        mixed = mixed + in_plane(partial, step).astype(F32)
+    stages = [(step,) for step in range(group - 1, 1, -2)] + [(1,)] if group > 2 else [(1,)]
+    stages.append((*(step for step in range(2, group) if (step,) not in stages), 0))
+    act, products = None, []
+    for number, steps in enumerate(stages):
+        gated, act = lax.optimization_barrier((gated, act))
+        act = conv(steps, gated)
+        if number:
+            act, swapped = lax.optimization_barrier((act, swapped))
+            done = out(stages[number - 1], last_act, swapped)
+            act, done = lax.optimization_barrier((act, done))
+            received = [in_plane(part, step) for part, step in zip(done, stages[number - 1])]
+            products += received
+            if number == len(stages) - 1:
+                act, products[0] = lax.optimization_barrier((act, products[0]))
+        swapped = [across(act, step) for step in range(1, cores)]
+        last_act = act
+    done = out(stages[-1], last_act, swapped)
+    products += [in_plane(part, step) for part, step in zip(done[:-1], stages[-1])]
+    mixed = done[-1]
+    for product in products:
+        mixed = mixed + product.astype(F32)
     return mixed.astype(BF16)
 
 

time: 83.2 us -> 84.6 us (1.017)
  waiting for transfers between devices: 24.7 us -> 25.8 us
  Pallas kernels: 16.9 us -> 17.8 us
    ppermute x9, waiting for transfers between devices: 16.5 us -> 17.6 us  [in_plane(): return lax.ppermute(array, 'tm', [(i, i ^ step) for i in range(times)])]
    pallas_call x14 -> x16, Pallas kernels: 16.9 us -> 17.8 us  [call(): pl.pallas_call(kernel, out_shape=out_shape, in_specs=in_specs, out_specs=...]
  transfers between devices with their start and end apart: 26 -> 27, of which waited for: 9 -> 9; matrix products, arithmetic and copies ran while one was open for 1% -> 1% of each run, Pallas kernels for 17% -> 18%
where the time goes in v14:
time: 84.6 us; the launch traced here: 84.4 us
  starting transfers between devices  37.8 us (45%)
  waiting for transfers between devices  25.8 us (30%)
  Pallas kernels  17.8 us (21%)
  local copies, waits for them, and re-layouts  1.78 us (2%)
    pallas_call x16, Pallas kernels, call(): pl.pallas_call(kernel, out_shape=out_shape, in_specs=in_specs, out_specs=...  17.8 us
    ppermute x9, waiting for transfers between devices, in_plane(): return lax.ppermute(array, 'tm', [(i, i ^ step) for i in range(times)])  17.6 us
    ppermute x8, starting transfers between devices, between_planes(): lax.ppermute(array, 'tm', [(i, i ^ step * group) for i in range(times)])  15 us
    ppermute x9, starting transfers between devices, in_plane(): return lax.ppermute(array, 'tm', [(i, i ^ step) for i in range(times)])  12.6 us
    ppermute x3, starting transfers between devices, later(): lax.ppermute(array, 'tm', [(i, i + step * group) for i in range(times - s...  7.73 us
    ppermute x8, waiting for transfers between devices, between_planes(): lax.ppermute(array, 'tm', [(i, i ^ step * group) for i in range(times)])  7.41 us
  transfers between devices with their start and end apart: 27, of which 9 were waited for; matrix products, arithmetic and copies ran while one was open for 1% of the time, Pallas kernels for 18%

profile of v14, /device:TPU:0, one launch (start us, length us, event | category | flops | bytes accessed | tf_op | source)
XLA Modules:
  0.0 84.4 jit_solution(10472878497480463801)
XLA Ops:
  0.0 2.0 %shard_map.91 = (bf16[64,768]{1,0:T(8,128)(2,1)}, bf16[64,768]{1,0:T(8,128)(2,1)}, bf16[64,768]{1,0:T(8,128)(2,1)}, bf16[64,768]{1,0:T(8,128)(2,1)}, bf16[32,102...) custom-call(f32[16,256]{1,0:T(8,128)} %log_decay_ref.1, ...), custom_call_target="tpu_custom_call" | custom-call | bytes 1622016 | tf_op jit(solution)/shard_map/pallas_call | solution.py:35
  2.0 3.0 %collective-permute-start.6 = (bf16[64,768]{1,0:T(8,128)(2,1)}, bf16[64,768]{1,0:T(8,128)(2,1)S(1)}, u32[]{:S(2)}, u32[]{:S(2)}) collective-permute-start(bf16[64,768]{1,0:T(8,128)(2,1)} %get-tuple-element.78), channel_id=1, source_target_pairs={{0,2},{2,0},{4,6},{6,4},{8,10},{10,8},{12,14},{14,12},{16,18},{18,... | collective-permute-start | bytes 294920 | tf_op jit(solution)/shard_map/ppermute | solution.py:524
  5.0 1.5 %collective-permute-start.7 = (bf16[64,768]{1,0:T(8,128)(2,1)}, bf16[64,768]{1,0:T(8,128)(2,1)S(1)}, u32[]{:S(2)}, u32[]{:S(2)}) collective-permute-start(bf16[64,768]{1,0:T(8,128)(2,1)} %get-tuple-element.79), channel_id=1, source_target_pairs={{0,4},{2,6},{4,0},{6,2},{8,12},{10,14},{12,8},{14,10},{16,20},{18,... | collective-permute-start | bytes 294920 | tf_op jit(solution)/shard_map/ppermute | solution.py:524
  6.5 2.0 %collective-permute-start = (bf16[32,1024]{1,0:T(8,128)(2,1)}, bf16[32,1024]{1,0:T(8,128)(2,1)S(1)}, u32[]{:S(2)}, u32[]{:S(2)}) collective-permute-start(bf16[32,1024]{1,0:T(8,128)(2,1)} %get-tuple-element.69), channel_id=1, source_target_pairs={{0,8},{2,10},{4,12},{6,14},{8,0},{10,2},{12,4},{14,6},{16,24},{18,... | collective-permute-start | bytes 196616 | tf_op jit(solution)/shard_map/ppermute | solution.py:533
  8.5 2.6 %collective-permute-start.1 = (bf16[32,1024]{1,0:T(8,128)(2,1)}, bf16[32,1024]{1,0:T(8,128)(2,1)S(1)}, u32[]{:S(2)}, u32[]{:S(2)}) collective-permute-start(bf16[32,1024]{1,0:T(8,128)(2,1)} %get-tuple-element.70), channel_id=1, source_target_pairs={{0,16},{2,18},{4,20},{6,22},{8,24},{10,26},{12,28},{14,30},{16,0},... | collective-permute-start | bytes 196616 | tf_op jit(solution)/shard_map/ppermute | solution.py:533
  11.1 0.7 reshape.3
  12.0 0.2 collective-permute-done.8.refs_3_
  12.2 0.9 %copy-done.4 = bf16[64,768]{1,0:T(8,128)(2,1)S(1)} copy-done((bf16[64,768]{1,0:T(8,128)(2,1)S(1)}, bf16[64,768]{1,0:T(8,128)(2,1)}, u32[]{:S(2)}) %copy-start.4) | copy-done | bytes 98328
  13.2 2.7 %collective-permute-start.9 = (bf16[256,512]{1,0:T(8,128)(2,1)S(1)}, bf16[256,512]{1,0:T(8,128)(2,1)S(1)}, u32[]{:S(2)}, u32[]{:S(2)}) collective-permute-start(bf16[256,512]{1,0:T(8,128)(2,1)S(1)} %get-tuple-element.86.refs_0_), channel_id=1, source_target_pairs={{0,16},{2,18},{4,20},{6,22},{8,24},{10,26},{12,28},{14,30},{16,0},... | collective-permute-start | bytes 786440 | tf_op jit(solution)/shard_map/ppermute | solution.py:533
  15.8 1.6 %collective-permute-start.10 = (bf16[256,512]{1,0:T(8,128)(2,1)S(1)}, bf16[256,512]{1,0:T(8,128)(2,1)S(1)}, u32[]{:S(2)}, u32[]{:S(2)}) collective-permute-start(bf16[256,512]{1,0:T(8,128)(2,1)S(1)} %get-tuple-element.86.refs_0_), channel_id=1, source_target_pairs={{0,8},{2,10},{4,12},{6,14},{8,0},{10,2},{12,4},{14,6},{16,24},{18,... | collective-permute-start | bytes 786440 | tf_op jit(solution)/shard_map/ppermute | solution.py:533
  17.4 2.7 %collective-permute-done.1.refs_2_ = bf16[32,1024]{1,0:T(8,128)(2,1)S(1)} collective-permute-done((bf16[32,1024]{1,0:T(8,128)(2,1)}, bf16[32,1024]{1,0:T(8,128)(2,1)S(1)}, u32[]{:S(2)}, u32[]{:S(2)}) %collective-permute-start.1) | collective-permute-done | bytes 65568 | tf_op jit(solution)/shard_map/ppermute | solution.py:533
  20.1 0.2 shard_map.92
  20.2 1.6 %collective-permute-start.3 = (bf16[192,1024]{1,0:T(8,128)(2,1)S(1)}, bf16[192,1024]{1,0:T(8,128)(2,1)S(1)}, u32[]{:S(2)}, u32[]{:S(2)}) collective-permute-start(bf16[192,1024]{1,0:T(8,128)(2,1)S(1)} %get-tuple-element.73), channel_id=1, source_target_pairs={{0,2},{2,0},{4,6},{6,4},{8,10},{10,8},{12,14},{14,12},{16,18},{18,... | collective-permute-start | bytes 1179656 | tf_op jit(solution)/shard_map/ppermute | solution.py:524
  21.8 1.5 %collective-permute-start.4 = (bf16[192,1024]{1,0:T(8,128)(2,1)S(1)}, bf16[192,1024]{1,0:T(8,128)(2,1)S(1)}, u32[]{:S(2)}, u32[]{:S(2)}) collective-permute-start(bf16[192,1024]{1,0:T(8,128)(2,1)S(1)} %get-tuple-element.74), channel_id=1, source_target_pairs={{0,4},{2,6},{4,0},{6,2},{8,12},{10,14},{12,8},{14,10},{16,20},{18,... | collective-permute-start | bytes 1179656 | tf_op jit(solution)/shard_map/ppermute | solution.py:524
  23.3 0.5 collective-permute-start.5
  23.8 4.7 %collective-permute-done.9.refs_2_ = bf16[256,512]{1,0:T(8,128)(2,1)S(1)} collective-permute-done((bf16[256,512]{1,0:T(8,128)(2,1)S(1)}, bf16[256,512]{1,0:T(8,128)(2,1)S(1)}, u32[]{:S(2)}, u32[]{:S(2)}) %collective-permute-start.9) | collective-permute-done | bytes 262176 | tf_op jit(solution)/shard_map/ppermute | solution.py:533
  28.5 1.3 %collective-permute-start.11 = (bf16[256,512]{1,0:T(8,128)(2,1)S(1)}, bf16[256,512]{1,0:T(8,128)(2,1)S(1)}, u32[]{:S(2)}, u32[]{:S(2)}) collective-permute-start(bf16[256,512]{1,0:T(8,128)(2,1)S(1)} %collective-permute-done.9.refs_2_), channel_id=1, source_target_pairs={{8,0},{10,2},{12,4},{14,6},{16,24},{18,26},{20,28},{22,30},{9,1},{... | collective-permute-start | bytes 786440 | tf_op jit(solution)/shard_map/ppermute | solution.py:549
  29.8 0.7 collective-permute-start.12
  30.5 0.6 collective-permute-done.3.refs_1_.refs_0_
  31.1 5.4 %collective-permute-done.4.refs_2_.refs_1_ = bf16[192,1024]{1,0:T(8,128)(2,1)S(1)} collective-permute-done((bf16[192,1024]{1,0:T(8,128)(2,1)S(1)}, bf16[192,1024]{1,0:T(8,128)(2,1)S(1)}, u32[]{:S(2)}, u32[]{:S(2)}) %collective-permute-start.4) | collective-permute-done | bytes 393248 | tf_op jit(solution)/shard_map/ppermute | solution.py:524
  36.5 0.5 shard_map.93
  37.1 0.8 collective-permute-done.11.refs_3_
  37.9 3.7 %collective-permute-start.14 = (bf16[256,256]{1,0:T(8,128)(2,1)S(1)}, bf16[256,256]{1,0:T(8,128)(2,1)S(1)}, u32[]{:S(2)}, u32[]{:S(2)}) collective-permute-start(bf16[256,256]{1,0:T(8,128)(2,1)S(1)} %get-tuple-element.97.refs_0_), channel_id=1, source_target_pairs={{0,8},{2,10},{4,12},{6,14},{8,0},{10,2},{12,4},{14,6},{16,24},{18,... | collective-permute-start | bytes 393224 | tf_op jit(solution)/shard_map/ppermute | solution.py:533
  41.6 0.6 collective-permute-start.15
  42.2 1.8 %collective-permute-start.16 = (bf16[256,256]{1,0:T(8,128)(2,1)S(1)}, bf16[256,256]{1,0:T(8,128)(2,1)S(1)}, u32[]{:S(2)}, u32[]{:S(2)}) collective-permute-start(bf16[256,256]{1,0:T(8,128)(2,1)S(1)} %get-tuple-element.97.refs_0_), channel_id=1, source_target_pairs={{0,24},{2,26},{4,28},{6,30},{8,16},{10,18},{12,20},{14,22},{16,8},... | collective-permute-start | bytes 393224 | tf_op jit(solution)/shard_map/ppermute | solution.py:533
  43.9 0.1 shard_map.95
  44.0 2.8 %shard_map.96 = (bf16[1152,1024]{1,0:T(8,128)(2,1)S(1)}, bf16[1152,256]{1,0:T(8,128)(2,1)S(1)}, bf16[1152,128]{1,0:T(8,128)(2,1)S(1)}, bf16[1152,128]{1,0:T(8,12...) custom-call(s32[8]{0:T(128)S(1)} %copy-done.2, ...), custom_call_target="tpu_custom_call" | custom-call | tf_op jit(solution)/shard_map/pallas_call | solution.py:35
  46.8 3.0 %collective-permute-start.17 = (bf16[144,256]{1,0:T(8,128)(2,1)S(1)}, bf16[144,256]{1,0:T(8,128)(2,1)S(1)}, u32[]{:S(2)}, u32[]{:S(2)}) collective-permute-start(bf16[144,256]{1,0:T(8,128)(2,1)S(1)} %get-tuple-element.113), channel_id=1, source_target_pairs={{0,8},{2,10},{4,12},{6,14},{8,16},{10,18},{12,20},{14,22},{16,24},... | collective-permute-start | bytes 221192 | tf_op jit(solution)/shard_map/ppermute | solution.py:527
  49.9 3.4 %collective-permute-start.18 = (bf16[144,256]{1,0:T(8,128)(2,1)S(1)}, bf16[144,256]{1,0:T(8,128)(2,1)S(1)}, u32[]{:S(2)}, u32[]{:S(2)}) collective-permute-start(bf16[144,256]{1,0:T(8,128)(2,1)S(1)} %get-tuple-element.113), channel_id=1, source_target_pairs={{0,16},{2,18},{4,20},{6,22},{8,24},{10,26},{12,28},{14,30},{1,17},... | collective-permute-start | bytes 221192 | tf_op jit(solution)/shard_map/ppermute | solution.py:527
  53.3 1.3 %collective-permute-start.19 = (bf16[144,256]{1,0:T(8,128)(2,1)S(1)}, bf16[144,256]{1,0:T(8,128)(2,1)S(1)}, u32[]{:S(2)}, u32[]{:S(2)}) collective-permute-start(bf16[144,256]{1,0:T(8,128)(2,1)S(1)} %get-tuple-element.113), channel_id=1, source_target_pairs={{0,24},{2,26},{4,28},{6,30},{1,25},{3,27},{5,29},{7,31}} | collective-permute-start | bytes 221192 | tf_op jit(solution)/shard_map/ppermute | solution.py:527
  54.7 1.9 %shard_map.98 = (f32[1152,256]{1,0:T(8,128)S(1)}, f32[1152,256]{1,0:T(8,128)S(1)}) custom-call(bf16[1152,256]{1,0:T(8,128)(2,1)S(1)} %get-tuple-element.104.x_ref, bf16[1152,128]{1,0:T(8,128)(2,1)S(1)} %get-tuple-element.105.b_ref, bf16[1152,128]{1,0:T(8,128)(2,1)S(1)} %get-tuple-element.103.c_ref, f32[216,128]{1,0:T(8,128)S(1)} %get-tuple-element.106.rows_ref), custom_call_target="tpu_custom_call" | custom-call | flops 134217728 | bytes 3649536 | tf_op jit(solution)/shard_map/pallas_call | solution.py:35
  56.6 0.8 shard_map.99.silu_ref
  57.5 0.7 shard_map.100.gated_ref
  58.3 0.1 copy-done.1
  58.4 2.1 %shard_map.101.refs_0_ = bf16[256,256]{1,0:T(8,128)(2,1)S(1)} custom-call(s32[8]{0:T(128)S(1)} %copy-done.2, f32[31,1024]{1,0:T(8,128)S(1)} %copy-done.1, bf16[1152,256]{1,0:T(8,128)(2,1)S(1)} %shard_map.100.gated_ref), custom_call_target="tpu_custom_call" | custom-call | flops 4063232 | bytes 847904 | tf_op jit(solution)/shard_map/pallas_call | solution.py:35
  60.5 0.4 collective-permute-start.20
  60.9 2.3 %shard_map.102.refs_0_ = bf16[256,256]{1,0:T(8,128)(2,1)S(1)} custom-call(s32[8]{0:T(128)S(1)} %copy-done.2, f32[31,1024]{1,0:T(8,128)S(1)} %copy-done.1, bf16[1152,256]{1,0:T(8,128)(2,1)S(1)} %shard_map.100.gated_ref), custom_call_target="tpu_custom_call" | custom-call | flops 4063232 | bytes 847904 | tf_op jit(solution)/shard_map/pallas_call | solution.py:35
  63.2 0.3 shard_map.103
  63.5 1.8 %collective-permute-start.23 = (bf16[256,512]{1,0:T(8,128)(2,1)S(1)}, bf16[256,512]{1,0:T(8,128)(2,1)S(1)}, u32[]{:S(2)}, u32[]{:S(2)}) collective-permute-start(bf16[256,512]{1,0:T(8,128)(2,1)S(1)} %shard_map.103), channel_id=1, source_target_pairs={{0,6},{2,4},{4,2},{6,0},{8,14},{10,12},{12,10},{14,8},{16,22},{18,... | collective-permute-start | bytes 786440 | tf_op jit(solution)/shard_map/ppermute | solution.py:524
  65.3 3.4 %shard_map.104.refs_0_ = bf16[512,256]{1,0:T(8,128)(2,1)S(1)} custom-call(s32[8]{0:T(128)S(1)} %copy-done.2, f32[31,1024]{1,0:T(8,128)S(1)} %copy-done.1, bf16[1152,256]{1,0:T(8,128)(2,1)S(1)} %shard_map.100.gated_ref), custom_call_target="tpu_custom_call" | custom-call | flops 8126464 | bytes 978976 | tf_op jit(solution)/shard_map/pallas_call | solution.py:35
  68.7 0.3 shard_map.105
  69.0 3.8 %collective-permute-done.23 = bf16[256,512]{1,0:T(8,128)(2,1)S(1)} collective-permute-done((bf16[256,512]{1,0:T(8,128)(2,1)S(1)}, bf16[256,512]{1,0:T(8,128)(2,1)S(1)}, u32[]{:S(2)}, u32[]{:S(2)}) %collective-permute-start.23) | collective-permute-done | bytes 262176 | tf_op jit(solution)/shard_map/ppermute | solution.py:524
  72.9 1.7 %collective-permute-start.25 = (bf16[256,512]{1,0:T(8,128)(2,1)S(1)}, bf16[256,512]{1,0:T(8,128)(2,1)S(1)}, u32[]{:S(2)}, u32[]{:S(2)}) collective-permute-start(bf16[256,512]{1,0:T(8,128)(2,1)S(1)} %shard_map.105), channel_id=1, source_target_pairs={{0,2},{2,0},{4,6},{6,4},{8,10},{10,8},{12,14},{14,12},{16,18},{18,... | collective-permute-start | bytes 786440 | tf_op jit(solution)/shard_map/ppermute | solution.py:524
  74.5 0.5 shard_map.106
  75.0 1.1 %collective-permute-start.26 = (bf16[256,512]{1,0:T(8,128)(2,1)S(1)}, bf16[256,512]{1,0:T(8,128)(2,1)S(1)}, u32[]{:S(2)}, u32[]{:S(2)}) collective-permute-start(bf16[256,512]{1,0:T(8,128)(2,1)S(1)} %get-tuple-element.130), channel_id=1, source_target_pairs={{0,4},{2,6},{4,0},{6,2},{8,12},{10,14},{12,8},{14,10},{16,20},{18,... | collective-permute-start | bytes 786440 | tf_op jit(solution)/shard_map/ppermute | solution.py:524
  76.1 5.5 %collective-permute-done.25 = bf16[256,512]{1,0:T(8,128)(2,1)S(1)} collective-permute-done((bf16[256,512]{1,0:T(8,128)(2,1)S(1)}, bf16[256,512]{1,0:T(8,128)(2,1)S(1)}, u32[]{:S(2)}, u32[]{:S(2)}) %collective-permute-start.25) | collective-permute-done | bytes 262176 | tf_op jit(solution)/shard_map/ppermute | solution.py:524
  81.6 1.9 %collective-permute-done.26 = bf16[256,512]{1,0:T(8,128)(2,1)S(1)} collective-permute-done((bf16[256,512]{1,0:T(8,128)(2,1)S(1)}, bf16[256,512]{1,0:T(8,128)(2,1)S(1)}, u32[]{:S(2)}, u32[]{:S(2)}) %collective-permute-start.26) | collective-permute-done | bytes 262176 | tf_op jit(solution)/shard_map/ppermute | solution.py:524
  83.5 0.8 add_convert_fusion
  (37 shorter events, 0.4 us)
Async XLA Ops:
  2.0 9.9 %collective-permute-start.6 = (bf16[64,768]{1,0:T(8,128)(2,1)}, bf16[64,768]{1,0:T(8,128)(2,1)S(1)}, u32[]{:S(2)}, u32[]{:S(2)}) collective-permute-start(bf16[64,768]{1,0:T(8,128)(2,1)} %get-tuple-element.78), channel_id=1, source_target_pairs={{0,2},{2,0},{4,6},{6,4},{8,10},{10,8},{12,14},{14,12},{16,18},{18,... | collective-permute-start | bytes 294920 | tf_op jit(solution)/shard_map/ppermute | solution.py:524
  5.0 7.0 %collective-permute-start.7 = (bf16[64,768]{1,0:T(8,128)(2,1)}, bf16[64,768]{1,0:T(8,128)(2,1)S(1)}, u32[]{:S(2)}, u32[]{:S(2)}) collective-permute-start(bf16[64,768]{1,0:T(8,128)(2,1)} %get-tuple-element.79), channel_id=1, source_target_pairs={{0,4},{2,6},{4,0},{6,2},{8,12},{10,14},{12,8},{14,10},{16,20},{18,... | collective-permute-start | bytes 294920 | tf_op jit(solution)/shard_map/ppermute | solution.py:524
  6.5 5.7 %collective-permute-start.8 = (bf16[64,768]{1,0:T(8,128)(2,1)}, bf16[64,768]{1,0:T(8,128)(2,1)S(1)}, u32[]{:S(2)}, u32[]{:S(2)}) collective-permute-start(bf16[64,768]{1,0:T(8,128)(2,1)} %get-tuple-element.80), channel_id=1, source_target_pairs={{0,6},{2,4},{4,2},{6,0},{8,14},{10,12},{12,10},{14,8},{16,22},{18,... | collective-permute-start | bytes 294920 | tf_op jit(solution)/shard_map/ppermute | solution.py:524
  6.5 10.9 %collective-permute-start = (bf16[32,1024]{1,0:T(8,128)(2,1)}, bf16[32,1024]{1,0:T(8,128)(2,1)S(1)}, u32[]{:S(2)}, u32[]{:S(2)}) collective-permute-start(bf16[32,1024]{1,0:T(8,128)(2,1)} %get-tuple-element.69), channel_id=1, source_target_pairs={{0,8},{2,10},{4,12},{6,14},{8,0},{10,2},{12,4},{14,6},{16,24},{18,... | collective-permute-start | bytes 196616 | tf_op jit(solution)/shard_map/ppermute | solution.py:533
  8.5 11.5 %collective-permute-start.1 = (bf16[32,1024]{1,0:T(8,128)(2,1)}, bf16[32,1024]{1,0:T(8,128)(2,1)S(1)}, u32[]{:S(2)}, u32[]{:S(2)}) collective-permute-start(bf16[32,1024]{1,0:T(8,128)(2,1)} %get-tuple-element.70), channel_id=1, source_target_pairs={{0,16},{2,18},{4,20},{6,22},{8,24},{10,26},{12,28},{14,30},{16,0},... | collective-permute-start | bytes 196616 | tf_op jit(solution)/shard_map/ppermute | solution.py:533
  11.9 8.2 %collective-permute-start.2 = (bf16[32,1024]{1,0:T(8,128)(2,1)}, bf16[32,1024]{1,0:T(8,128)(2,1)S(1)}, u32[]{:S(2)}, u32[]{:S(2)}) collective-permute-start(bf16[32,1024]{1,0:T(8,128)(2,1)} %get-tuple-element.71), channel_id=1, source_target_pairs={{0,24},{2,26},{4,28},{6,30},{8,16},{10,18},{12,20},{14,22},{16,8},... | collective-permute-start | bytes 196616 | tf_op jit(solution)/shard_map/ppermute | solution.py:533
  12.2 0.9 %copy-start.4 = (bf16[64,768]{1,0:T(8,128)(2,1)S(1)}, bf16[64,768]{1,0:T(8,128)(2,1)}, u32[]{:S(2)}) copy-start(bf16[64,768]{1,0:T(8,128)(2,1)} %get-tuple-element.77.refs_0_) | copy-start | bytes 294916
  13.1 7.0 %copy-start = (bf16[256,1024]{1,0:T(8,128)(2,1)S(1)}, bf16[256,1024]{1,0:T(8,128)(2,1)}, u32[]{:S(2)}) copy-start(bf16[256,1024]{1,0:T(8,128)(2,1)} %own_ref.1) | copy-start | bytes 1572868
  13.1 7.0 %copy-start.5 = (bf16[32,1024]{1,0:T(8,128)(2,1)S(1)}, bf16[32,1024]{1,0:T(8,128)(2,1)}, u32[]{:S(2)}) copy-start(bf16[32,1024]{1,0:T(8,128)(2,1)} %get-tuple-element.68.refs_0_) | copy-start | bytes 196612
  13.2 15.4 %collective-permute-start.9 = (bf16[256,512]{1,0:T(8,128)(2,1)S(1)}, bf16[256,512]{1,0:T(8,128)(2,1)S(1)}, u32[]{:S(2)}, u32[]{:S(2)}) collective-permute-start(bf16[256,512]{1,0:T(8,128)(2,1)S(1)} %get-tuple-element.86.refs_0_), channel_id=1, source_target_pairs={{0,16},{2,18},{4,20},{6,22},{8,24},{10,26},{12,28},{14,30},{16,0},... | collective-permute-start | bytes 786440 | tf_op jit(solution)/shard_map/ppermute | solution.py:533
  15.8 12.7 %collective-permute-start.10 = (bf16[256,512]{1,0:T(8,128)(2,1)S(1)}, bf16[256,512]{1,0:T(8,128)(2,1)S(1)}, u32[]{:S(2)}, u32[]{:S(2)}) collective-permute-start(bf16[256,512]{1,0:T(8,128)(2,1)S(1)} %get-tuple-element.86.refs_0_), channel_id=1, source_target_pairs={{0,8},{2,10},{4,12},{6,14},{8,0},{10,2},{12,4},{14,6},{16,24},{18,... | collective-permute-start | bytes 786440 | tf_op jit(solution)/shard_map/ppermute | solution.py:533
  20.2 10.9 %collective-permute-start.3 = (bf16[192,1024]{1,0:T(8,128)(2,1)S(1)}, bf16[192,1024]{1,0:T(8,128)(2,1)S(1)}, u32[]{:S(2)}, u32[]{:S(2)}) collective-permute-start(bf16[192,1024]{1,0:T(8,128)(2,1)S(1)} %get-tuple-element.73), channel_id=1, source_target_pairs={{0,2},{2,0},{4,6},{6,4},{8,10},{10,8},{12,14},{14,12},{16,18},{18,... | collective-permute-start | bytes 1179656 | tf_op jit(solution)/shard_map/ppermute | solution.py:524
  21.8 14.7 %collective-permute-start.4 = (bf16[192,1024]{1,0:T(8,128)(2,1)S(1)}, bf16[192,1024]{1,0:T(8,128)(2,1)S(1)}, u32[]{:S(2)}, u32[]{:S(2)}) collective-permute-start(bf16[192,1024]{1,0:T(8,128)(2,1)S(1)} %get-tuple-element.74), channel_id=1, source_target_pairs={{0,4},{2,6},{4,0},{6,2},{8,12},{10,14},{12,8},{14,10},{16,20},{18,... | collective-permute-start | bytes 1179656 | tf_op jit(solution)/shard_map/ppermute | solution.py:524
  23.3 13.2 %collective-permute-start.5 = (bf16[192,1024]{1,0:T(8,128)(2,1)S(1)}, bf16[192,1024]{1,0:T(8,128)(2,1)S(1)}, u32[]{:S(2)}, u32[]{:S(2)}) collective-permute-start(bf16[192,1024]{1,0:T(8,128)(2,1)S(1)} %get-tuple-element.75), channel_id=1, source_target_pairs={{0,6},{2,4},{4,2},{6,0},{8,14},{10,12},{12,10},{14,8},{16,22},{18,... | collective-permute-start | bytes 1179656 | tf_op jit(solution)/shard_map/ppermute | solution.py:524
  28.5 9.4 %collective-permute-start.11 = (bf16[256,512]{1,0:T(8,128)(2,1)S(1)}, bf16[256,512]{1,0:T(8,128)(2,1)S(1)}, u32[]{:S(2)}, u32[]{:S(2)}) collective-permute-start(bf16[256,512]{1,0:T(8,128)(2,1)S(1)} %collective-permute-done.9.refs_2_), channel_id=1, source_target_pairs={{8,0},{10,2},{12,4},{14,6},{16,24},{18,26},{20,28},{22,30},{9,1},{... | collective-permute-start | bytes 786440 | tf_op jit(solution)/shard_map/ppermute | solution.py:549
  29.8 8.1 %collective-permute-start.12 = (bf16[256,512]{1,0:T(8,128)(2,1)S(1)}, bf16[256,512]{1,0:T(8,128)(2,1)S(1)}, u32[]{:S(2)}, u32[]{:S(2)}) collective-permute-start(bf16[256,512]{1,0:T(8,128)(2,1)S(1)} %get-tuple-element.86.refs_0_), channel_id=1, source_target_pairs={{8,16},{10,18},{12,20},{14,22},{16,8},{18,10},{20,12},{22,14},{9,1... | collective-permute-start | bytes 786440 | tf_op jit(solution)/shard_map/ppermute | solution.py:550
  37.0 7.0 %collective-permute-start.13 = (bf16[512,1024]{1,0:T(8,128)(2,1)S(1)}, bf16[512,1024]{1,0:T(8,128)(2,1)S(1)}, u32[]{:S(2)}, u32[]{:S(2)}) collective-permute-start(bf16[512,1024]{1,0:T(8,128)(2,1)S(1)} %get-tuple-element.93), channel_id=1, source_target_pairs={{0,1},{1,0},{2,3},{3,2},{4,5},{5,4},{6,7},{7,6},{8,9},{9,8},{10,11... | collective-permute-start | bytes 3145736 | tf_op jit(solution)/shard_map/ppermute | solution.py:530
  37.9 6.2 %copy-start.2 = (s32[8]{0:T(128)S(1)}, s32[8]{0:T(128)}, u32[]{:S(2)}) copy-start(s32[8]{0:T(128)} %len_ref.7) | copy-start | bytes 100
  37.9 15.4 %collective-permute-start.14 = (bf16[256,256]{1,0:T(8,128)(2,1)S(1)}, bf16[256,256]{1,0:T(8,128)(2,1)S(1)}, u32[]{:S(2)}, u32[]{:S(2)}) collective-permute-start(bf16[256,256]{1,0:T(8,128)(2,1)S(1)} %get-tuple-element.97.refs_0_), channel_id=1, source_target_pairs={{0,8},{2,10},{4,12},{6,14},{8,0},{10,2},{12,4},{14,6},{16,24},{18,... | collective-permute-start | bytes 393224 | tf_op jit(solution)/shard_map/ppermute | solution.py:533
  41.6 13.1 %collective-permute-start.15 = (bf16[256,256]{1,0:T(8,128)(2,1)S(1)}, bf16[256,256]{1,0:T(8,128)(2,1)S(1)}, u32[]{:S(2)}, u32[]{:S(2)}) collective-permute-start(bf16[256,256]{1,0:T(8,128)(2,1)S(1)} %get-tuple-element.97.refs_0_), channel_id=1, source_target_pairs={{0,16},{2,18},{4,20},{6,22},{8,24},{10,26},{12,28},{14,30},{16,0},... | collective-permute-start | bytes 393224 | tf_op jit(solution)/shard_map/ppermute | solution.py:533
  42.2 12.5 %collective-permute-start.16 = (bf16[256,256]{1,0:T(8,128)(2,1)S(1)}, bf16[256,256]{1,0:T(8,128)(2,1)S(1)}, u32[]{:S(2)}, u32[]{:S(2)}) collective-permute-start(bf16[256,256]{1,0:T(8,128)(2,1)S(1)} %get-tuple-element.97.refs_0_), channel_id=1, source_target_pairs={{0,24},{2,26},{4,28},{6,30},{8,16},{10,18},{12,20},{14,22},{16,8},... | collective-permute-start | bytes 393224 | tf_op jit(solution)/shard_map/ppermute | solution.py:533
  46.8 9.8 %copy-start.3 = (f32[1024]{0:T(1024)S(1)}, f32[1024]{0:T(1024)}, u32[]{:S(2)}) copy-start(f32[1024]{0:T(1024)} %param.14) | copy-start | bytes 12292
  46.8 10.6 %collective-permute-start.17 = (bf16[144,256]{1,0:T(8,128)(2,1)S(1)}, bf16[144,256]{1,0:T(8,128)(2,1)S(1)}, u32[]{:S(2)}, u32[]{:S(2)}) collective-permute-start(bf16[144,256]{1,0:T(8,128)(2,1)S(1)} %get-tuple-element.113), channel_id=1, source_target_pairs={{0,8},{2,10},{4,12},{6,14},{8,16},{10,18},{12,20},{14,22},{16,24},... | collective-permute-start | bytes 221192 | tf_op jit(solution)/shard_map/ppermute | solution.py:527
  49.9 7.6 %collective-permute-start.18 = (bf16[144,256]{1,0:T(8,128)(2,1)S(1)}, bf16[144,256]{1,0:T(8,128)(2,1)S(1)}, u32[]{:S(2)}, u32[]{:S(2)}) collective-permute-start(bf16[144,256]{1,0:T(8,128)(2,1)S(1)} %get-tuple-element.113), channel_id=1, source_target_pairs={{0,16},{2,18},{4,20},{6,22},{8,24},{10,26},{12,28},{14,30},{1,17},... | collective-permute-start | bytes 221192 | tf_op jit(solution)/shard_map/ppermute | solution.py:527
  53.3 4.2 %collective-permute-start.19 = (bf16[144,256]{1,0:T(8,128)(2,1)S(1)}, bf16[144,256]{1,0:T(8,128)(2,1)S(1)}, u32[]{:S(2)}, u32[]{:S(2)}) collective-permute-start(bf16[144,256]{1,0:T(8,128)(2,1)S(1)} %get-tuple-element.113), channel_id=1, source_target_pairs={{0,24},{2,26},{4,28},{6,30},{1,25},{3,27},{5,29},{7,31}} | collective-permute-start | bytes 221192 | tf_op jit(solution)/shard_map/ppermute | solution.py:527
  57.5 0.9 %copy-start.1 = (f32[31,1024]{1,0:T(8,128)S(1)}, f32[31,1024]{1,0:T(8,128)}, u32[]{:S(2)}) copy-start(f32[31,1024]{1,0:T(8,128)} %taps_ref.5) | copy-start | bytes 380932
  58.2 5.0 %collective-permute-start.21 = (bf16[512,256]{1,0:T(8,128)(2,1)S(1)}, bf16[512,256]{1,0:T(8,128)(2,1)S(1)}, u32[]{:S(2)}, u32[]{:S(2)}) collective-permute-start(bf16[512,256]{1,0:T(8,128)(2,1)S(1)} %get-tuple-element.119), channel_id=1, source_target_pairs={{0,1},{1,0},{2,3},{3,2},{4,5},{5,4},{6,7},{7,6},{8,9},{9,8},{10,11... | collective-permute-start | bytes 786440 | tf_op jit(solution)/shard_map/ppermute | solution.py:530
  60.5 2.7 %collective-permute-start.20 = (bf16[256,256]{1,0:T(8,128)(2,1)S(1)}, bf16[256,256]{1,0:T(8,128)(2,1)S(1)}, u32[]{:S(2)}, u32[]{:S(2)}) collective-permute-start(bf16[256,256]{1,0:T(8,128)(2,1)S(1)} %shard_map.101.refs_0_), channel_id=1, source_target_pairs={{0,1},{1,0},{2,3},{3,2},{4,5},{5,4},{6,7},{7,6},{8,9},{9,8},{10,11... | collective-permute-start | bytes 393224 | tf_op jit(solution)/shard_map/ppermute | solution.py:530
  63.5 9.3 %collective-permute-start.23 = (bf16[256,512]{1,0:T(8,128)(2,1)S(1)}, bf16[256,512]{1,0:T(8,128)(2,1)S(1)}, u32[]{:S(2)}, u32[]{:S(2)}) collective-permute-start(bf16[256,512]{1,0:T(8,128)(2,1)S(1)} %shard_map.103), channel_id=1, source_target_pairs={{0,6},{2,4},{4,2},{6,0},{8,14},{10,12},{12,10},{14,8},{16,22},{18,... | collective-permute-start | bytes 786440 | tf_op jit(solution)/shard_map/ppermute | solution.py:524
  65.3 3.4 %collective-permute-start.22 = (bf16[256,256]{1,0:T(8,128)(2,1)S(1)}, bf16[256,256]{1,0:T(8,128)(2,1)S(1)}, u32[]{:S(2)}, u32[]{:S(2)}) collective-permute-start(bf16[256,256]{1,0:T(8,128)(2,1)S(1)} %shard_map.102.refs_0_), channel_id=1, source_target_pairs={{0,1},{1,0},{2,3},{3,2},{4,5},{5,4},{6,7},{7,6},{8,9},{9,8},{10,11... | collective-permute-start | bytes 393224 | tf_op jit(solution)/shard_map/ppermute | solution.py:530
  72.9 1.7 %collective-permute-start.24 = (bf16[512,256]{1,0:T(8,128)(2,1)S(1)}, bf16[512,256]{1,0:T(8,128)(2,1)S(1)}, u32[]{:S(2)}, u32[]{:S(2)}) collective-permute-start(bf16[512,256]{1,0:T(8,128)(2,1)S(1)} %shard_map.104.refs_0_), channel_id=1, source_target_pairs={{0,1},{1,0},{2,3},{3,2},{4,5},{5,4},{6,7},{7,6},{8,9},{9,8},{10,11... | collective-permute-start | bytes 786440 | tf_op jit(solution)/shard_map/ppermute | solution.py:530
  72.9 8.7 %collective-permute-start.25 = (bf16[256,512]{1,0:T(8,128)(2,1)S(1)}, bf16[256,512]{1,0:T(8,128)(2,1)S(1)}, u32[]{:S(2)}, u32[]{:S(2)}) collective-permute-start(bf16[256,512]{1,0:T(8,128)(2,1)S(1)} %shard_map.105), channel_id=1, source_target_pairs={{0,2},{2,0},{4,6},{6,4},{8,10},{10,8},{12,14},{14,12},{16,18},{18,... | collective-permute-start | bytes 786440 | tf_op jit(solution)/shard_map/ppermute | solution.py:524
  75.0 8.5 %collective-permute-start.26 = (bf16[256,512]{1,0:T(8,128)(2,1)S(1)}, bf16[256,512]{1,0:T(8,128)(2,1)S(1)}, u32[]{:S(2)}, u32[]{:S(2)}) collective-permute-start(bf16[256,512]{1,0:T(8,128)(2,1)S(1)} %get-tuple-element.130), channel_id=1, source_target_pairs={{0,4},{2,6},{4,0},{6,2},{8,12},{10,14},{12,8},{14,10},{16,20},{18,... | collective-permute-start | bytes 786440 | tf_op jit(solution)/shard_map/ppermute | solution.py:524

commit v15 on v13

--- a/solution.py
+++ b/solution.py
@@ -582,7 +582,7 @@
     )
     xz_pieces = along_planes([xz_stack] * planes)
     xz_pieces, out_stack = lax.optimization_barrier((xz_pieces, out_stack))
-    out_pieces = [out_stack] + [between_planes(out_stack, step) for step in range(1, planes)]
+    out_pieces = [out_stack] + [between_planes(out_stack, step) for step in range(1, min(3, planes))]
     x_columns, z_columns = call(
         functools.partial(assemble_kernel, group, offsets),
         (shape((depth, width), BF16), shape((depth, width), BF16)),
@@ -647,6 +647,8 @@
         flops=2 * total * depth * width,
         smem=0,
     )
+    out_pieces, summaries, y, silu = lax.optimization_barrier((out_pieces, summaries, y, silu))
+    out_pieces += [between_planes(out_pieces[0], step) for step in range(3, planes)]
     gated = call(
         functools.partial(gate_kernel, heads, state),
         shape((all_rows, width), BF16),
@@ -675,6 +677,11 @@
             smem=0,
         )
 
+    far_act = conv(far, gated)
+    far_swapped = [across(far_act, step) for step in range(1, cores)]
+    gated, far_act = lax.optimization_barrier((gated, far_act))
+    near_act = conv(near, gated)
+    near_act, far_swapped, out_pieces = lax.optimization_barrier((near_act, far_swapped, out_pieces))
     share = depth // cores
     out_parts = call(
         functools.partial(share_kernel, cores, tuple(range(planes)), group),
@@ -683,13 +690,8 @@
         [pltpu.VMEM((depth, width), BF16)],
         smem=0,
     )
-    out_parts, gated = lax.optimization_barrier((out_parts, gated))
     out_parts = [out_parts[0]] + [across(out_parts[step], step) for step in range(1, cores)]
-    far_act = conv(far, gated)
-    far_swapped = [across(far_act, step) for step in range(1, cores)]
-    gated, far_act = lax.optimization_barrier((gated, far_act))
-    near_act = conv(near, gated)
-    near_act, far_swapped, out_parts = lax.optimization_barrier((near_act, far_swapped, out_parts))
+    near_act, out_parts = lax.optimization_barrier((near_act, out_parts))
     (far_out,) = out(far, far_act, far_swapped)
     near_act, far_out = lax.optimization_barrier((near_act, far_out))
     far_out = in_plane(far_out, far[0])

time: 83.2 us -> 85.4 us (1.026)
  starting transfers between devices: 37.9 us -> 39.4 us
  waiting for transfers between devices: 24.7 us -> 25.9 us
    ppermute x8, starting transfers between devices: 15 us -> 16.8 us  [between_planes(): lax.ppermute(array, 'tm', [(i, i ^ step * group) for i in range(times)])]
    ppermute x4, waiting for transfers between devices: 0.01 us -> 1.38 us  [across(): return lax.ppermute(array, 'head', [(i, i ^ step) for i in range(cores)])]
  transfers between devices with their start and end apart: 26 -> 26, of which waited for: 9 -> 10; matrix products, arithmetic and copies ran while one was open for 1% -> 1% of each run, Pallas kernels for 17% -> 14%
where the time goes in v15:
time: 85.4 us; the launch traced here: 85.1 us
  starting transfers between devices  39.4 us (46%)
  waiting for transfers between devices  25.9 us (30%)
  Pallas kernels  16.9 us (20%)
  local copies, waits for them, and re-layouts  1.84 us (2%)
    pallas_call x14, Pallas kernels, call(): pl.pallas_call(kernel, out_shape=out_shape, in_specs=in_specs, out_specs=...  16.9 us
    ppermute x8, starting transfers between devices, between_planes(): lax.ppermute(array, 'tm', [(i, i ^ step * group) for i in range(times)])  16.8 us
    ppermute x9, waiting for transfers between devices, in_plane(): return lax.ppermute(array, 'tm', [(i, i ^ step) for i in range(times)])  16.3 us
    ppermute x9, starting transfers between devices, in_plane(): return lax.ppermute(array, 'tm', [(i, i ^ step) for i in range(times)])  12.6 us
    ppermute x3, starting transfers between devices, later(): lax.ppermute(array, 'tm', [(i, i + step * group) for i in range(times - s...  7.44 us
    ppermute x8, waiting for transfers between devices, between_planes(): lax.ppermute(array, 'tm', [(i, i ^ step * group) for i in range(times)])  7.41 us
  transfers between devices with their start and end apart: 26, of which 10 were waited for; matrix products, arithmetic and copies ran while one was open for 1% of the time, Pallas kernels for 14%

profile of v15, /device:TPU:0, one launch (start us, length us, event | category | flops | bytes accessed | tf_op | source)
XLA Modules:
  0.0 85.1 jit_solution(7453056086471481633)
XLA Ops:
  0.0 2.0 %shard_map.91 = (bf16[64,768]{1,0:T(8,128)(2,1)}, bf16[64,768]{1,0:T(8,128)(2,1)}, bf16[64,768]{1,0:T(8,128)(2,1)}, bf16[64,768]{1,0:T(8,128)(2,1)}, bf16[32,102...) custom-call(f32[16,256]{1,0:T(8,128)} %log_decay_ref.1, ...), custom_call_target="tpu_custom_call" | custom-call | bytes 1622016 | tf_op jit(solution)/shard_map/pallas_call | solution.py:35
  2.0 3.0 %collective-permute-start.6 = (bf16[64,768]{1,0:T(8,128)(2,1)}, bf16[64,768]{1,0:T(8,128)(2,1)S(1)}, u32[]{:S(2)}, u32[]{:S(2)}) collective-permute-start(bf16[64,768]{1,0:T(8,128)(2,1)} %get-tuple-element.84), channel_id=1, source_target_pairs={{0,2},{2,0},{4,6},{6,4},{8,10},{10,8},{12,14},{14,12},{16,18},{18,... | collective-permute-start | bytes 294920 | tf_op jit(solution)/shard_map/ppermute | solution.py:524
  5.0 1.5 %collective-permute-start.7 = (bf16[64,768]{1,0:T(8,128)(2,1)}, bf16[64,768]{1,0:T(8,128)(2,1)S(1)}, u32[]{:S(2)}, u32[]{:S(2)}) collective-permute-start(bf16[64,768]{1,0:T(8,128)(2,1)} %get-tuple-element.85), channel_id=1, source_target_pairs={{0,4},{2,6},{4,0},{6,2},{8,12},{10,14},{12,8},{14,10},{16,20},{18,... | collective-permute-start | bytes 294920 | tf_op jit(solution)/shard_map/ppermute | solution.py:524
  6.5 2.0 %collective-permute-start = (bf16[32,1024]{1,0:T(8,128)(2,1)}, bf16[32,1024]{1,0:T(8,128)(2,1)S(1)}, u32[]{:S(2)}, u32[]{:S(2)}) collective-permute-start(bf16[32,1024]{1,0:T(8,128)(2,1)} %get-tuple-element.75), channel_id=1, source_target_pairs={{0,8},{2,10},{4,12},{6,14},{8,0},{10,2},{12,4},{14,6},{16,24},{18,... | collective-permute-start | bytes 196616 | tf_op jit(solution)/shard_map/ppermute | solution.py:533
  8.5 2.6 %collective-permute-start.1 = (bf16[32,1024]{1,0:T(8,128)(2,1)}, bf16[32,1024]{1,0:T(8,128)(2,1)S(1)}, u32[]{:S(2)}, u32[]{:S(2)}) collective-permute-start(bf16[32,1024]{1,0:T(8,128)(2,1)} %get-tuple-element.76), channel_id=1, source_target_pairs={{0,16},{2,18},{4,20},{6,22},{8,24},{10,26},{12,28},{14,30},{16,0},... | collective-permute-start | bytes 196616 | tf_op jit(solution)/shard_map/ppermute | solution.py:533
  11.1 0.7 reshape.3
  12.0 0.2 collective-permute-done.8.refs_3_
  12.2 0.9 %copy-done.4 = bf16[64,768]{1,0:T(8,128)(2,1)S(1)} copy-done((bf16[64,768]{1,0:T(8,128)(2,1)S(1)}, bf16[64,768]{1,0:T(8,128)(2,1)}, u32[]{:S(2)}) %copy-start.4) | copy-done | bytes 98328
  13.2 2.7 %collective-permute-start.9 = (bf16[256,512]{1,0:T(8,128)(2,1)S(1)}, bf16[256,512]{1,0:T(8,128)(2,1)S(1)}, u32[]{:S(2)}, u32[]{:S(2)}) collective-permute-start(bf16[256,512]{1,0:T(8,128)(2,1)S(1)} %get-tuple-element.92.refs_0_), channel_id=1, source_target_pairs={{0,16},{2,18},{4,20},{6,22},{8,24},{10,26},{12,28},{14,30},{16,0},... | collective-permute-start | bytes 786440 | tf_op jit(solution)/shard_map/ppermute | solution.py:533
  15.8 1.6 %collective-permute-start.10 = (bf16[256,512]{1,0:T(8,128)(2,1)S(1)}, bf16[256,512]{1,0:T(8,128)(2,1)S(1)}, u32[]{:S(2)}, u32[]{:S(2)}) collective-permute-start(bf16[256,512]{1,0:T(8,128)(2,1)S(1)} %get-tuple-element.92.refs_0_), channel_id=1, source_target_pairs={{0,8},{2,10},{4,12},{6,14},{8,0},{10,2},{12,4},{14,6},{16,24},{18,... | collective-permute-start | bytes 786440 | tf_op jit(solution)/shard_map/ppermute | solution.py:533
  17.4 2.7 %collective-permute-done.1.refs_2_ = bf16[32,1024]{1,0:T(8,128)(2,1)S(1)} collective-permute-done((bf16[32,1024]{1,0:T(8,128)(2,1)}, bf16[32,1024]{1,0:T(8,128)(2,1)S(1)}, u32[]{:S(2)}, u32[]{:S(2)}) %collective-permute-start.1) | collective-permute-done | bytes 65568 | tf_op jit(solution)/shard_map/ppermute | solution.py:533
  20.1 0.2 shard_map.92
  20.2 1.6 %collective-permute-start.3 = (bf16[192,1024]{1,0:T(8,128)(2,1)S(1)}, bf16[192,1024]{1,0:T(8,128)(2,1)S(1)}, u32[]{:S(2)}, u32[]{:S(2)}) collective-permute-start(bf16[192,1024]{1,0:T(8,128)(2,1)S(1)} %get-tuple-element.79), channel_id=1, source_target_pairs={{0,2},{2,0},{4,6},{6,4},{8,10},{10,8},{12,14},{14,12},{16,18},{18,... | collective-permute-start | bytes 1179656 | tf_op jit(solution)/shard_map/ppermute | solution.py:524
  21.8 1.5 %collective-permute-start.4 = (bf16[192,1024]{1,0:T(8,128)(2,1)S(1)}, bf16[192,1024]{1,0:T(8,128)(2,1)S(1)}, u32[]{:S(2)}, u32[]{:S(2)}) collective-permute-start(bf16[192,1024]{1,0:T(8,128)(2,1)S(1)} %get-tuple-element.80), channel_id=1, source_target_pairs={{0,4},{2,6},{4,0},{6,2},{8,12},{10,14},{12,8},{14,10},{16,20},{18,... | collective-permute-start | bytes 1179656 | tf_op jit(solution)/shard_map/ppermute | solution.py:524
  23.3 0.5 collective-permute-start.5
  23.8 4.7 %collective-permute-done.9.refs_2_ = bf16[256,512]{1,0:T(8,128)(2,1)S(1)} collective-permute-done((bf16[256,512]{1,0:T(8,128)(2,1)S(1)}, bf16[256,512]{1,0:T(8,128)(2,1)S(1)}, u32[]{:S(2)}, u32[]{:S(2)}) %collective-permute-start.9) | collective-permute-done | bytes 262176 | tf_op jit(solution)/shard_map/ppermute | solution.py:533
  28.5 1.3 %collective-permute-start.11 = (bf16[256,512]{1,0:T(8,128)(2,1)S(1)}, bf16[256,512]{1,0:T(8,128)(2,1)S(1)}, u32[]{:S(2)}, u32[]{:S(2)}) collective-permute-start(bf16[256,512]{1,0:T(8,128)(2,1)S(1)} %collective-permute-done.9.refs_2_), channel_id=1, source_target_pairs={{8,0},{10,2},{12,4},{14,6},{16,24},{18,26},{20,28},{22,30},{9,1},{... | collective-permute-start | bytes 786440 | tf_op jit(solution)/shard_map/ppermute | solution.py:549
  29.8 0.7 collective-permute-start.12
  30.5 0.6 collective-permute-done.3.refs_1_.refs_0_
  31.1 5.4 %collective-permute-done.4.refs_2_.refs_1_ = bf16[192,1024]{1,0:T(8,128)(2,1)S(1)} collective-permute-done((bf16[192,1024]{1,0:T(8,128)(2,1)S(1)}, bf16[192,1024]{1,0:T(8,128)(2,1)S(1)}, u32[]{:S(2)}, u32[]{:S(2)}) %collective-permute-start.4) | collective-permute-done | bytes 393248 | tf_op jit(solution)/shard_map/ppermute | solution.py:524
  36.5 0.5 shard_map.93
  37.1 0.8 collective-permute-done.11.refs_3_
  37.9 3.7 %collective-permute-start.14 = (bf16[256,256]{1,0:T(8,128)(2,1)S(1)}, bf16[256,256]{1,0:T(8,128)(2,1)S(1)}, u32[]{:S(2)}, u32[]{:S(2)}) collective-permute-start(bf16[256,256]{1,0:T(8,128)(2,1)S(1)} %get-tuple-element.127.refs_0_), channel_id=1, source_target_pairs={{0,8},{2,10},{4,12},{6,14},{8,0},{10,2},{12,4},{14,6},{16,24},{18,... | collective-permute-start | bytes 393224 | tf_op jit(solution)/shard_map/ppermute | solution.py:533
  41.6 0.6 collective-permute-start.15
  42.2 0.1 shard_map.95
  42.3 2.8 %shard_map.96 = (bf16[1152,1024]{1,0:T(8,128)(2,1)S(1)}, bf16[1152,256]{1,0:T(8,128)(2,1)S(1)}, bf16[1152,128]{1,0:T(8,128)(2,1)S(1)}, bf16[1152,128]{1,0:T(8,12...) custom-call(s32[8]{0:T(128)S(1)} %copy-done.2, ...), custom_call_target="tpu_custom_call" | custom-call | tf_op jit(solution)/shard_map/pallas_call | solution.py:35
  45.1 3.9 %collective-permute-start.16 = (bf16[144,256]{1,0:T(8,128)(2,1)S(1)}, bf16[144,256]{1,0:T(8,128)(2,1)S(1)}, u32[]{:S(2)}, u32[]{:S(2)}) collective-permute-start(bf16[144,256]{1,0:T(8,128)(2,1)S(1)} %get-tuple-element.107), channel_id=1, source_target_pairs={{0,8},{2,10},{4,12},{6,14},{8,16},{10,18},{12,20},{14,22},{16,24},... | collective-permute-start | bytes 221192 | tf_op jit(solution)/shard_map/ppermute | solution.py:527
  49.0 2.2 %collective-permute-start.17 = (bf16[144,256]{1,0:T(8,128)(2,1)S(1)}, bf16[144,256]{1,0:T(8,128)(2,1)S(1)}, u32[]{:S(2)}, u32[]{:S(2)}) collective-permute-start(bf16[144,256]{1,0:T(8,128)(2,1)S(1)} %get-tuple-element.107), channel_id=1, source_target_pairs={{0,16},{2,18},{4,20},{6,22},{8,24},{10,26},{12,28},{14,30},{1,17},... | collective-permute-start | bytes 221192 | tf_op jit(solution)/shard_map/ppermute | solution.py:527
  51.3 1.3 %collective-permute-start.18 = (bf16[144,256]{1,0:T(8,128)(2,1)S(1)}, bf16[144,256]{1,0:T(8,128)(2,1)S(1)}, u32[]{:S(2)}, u32[]{:S(2)}) collective-permute-start(bf16[144,256]{1,0:T(8,128)(2,1)S(1)} %get-tuple-element.107), channel_id=1, source_target_pairs={{0,24},{2,26},{4,28},{6,30},{1,25},{3,27},{5,29},{7,31}} | collective-permute-start | bytes 221192 | tf_op jit(solution)/shard_map/ppermute | solution.py:527
  52.6 1.9 %shard_map.97 = (f32[1152,256]{1,0:T(8,128)S(1)}, f32[1152,256]{1,0:T(8,128)S(1)}) custom-call(bf16[1152,256]{1,0:T(8,128)(2,1)S(1)} %get-tuple-element.108.x_ref, bf16[1152,128]{1,0:T(8,128)(2,1)S(1)} %get-tuple-element.109.b_ref, bf16[1152,128]{1,0:T(8,128)(2,1)S(1)} %get-tuple-element.101.c_ref, f32[216,128]{1,0:T(8,128)S(1)} %get-tuple-element.110.rows_ref), custom_call_target="tpu_custom_call" | custom-call | flops 134217728 | bytes 3649536 | tf_op jit(solution)/shard_map/pallas_call | solution.py:35
  54.5 0.8 shard_map.98.silu_ref
  55.4 0.7 shard_map.99.gated_ref
  56.1 0.2 copy-done.1
  56.3 1.6 %shard_map.100.refs_0_ = bf16[256,256]{1,0:T(8,128)(2,1)S(1)} custom-call(s32[8]{0:T(128)S(1)} %copy-done.2, f32[31,1024]{1,0:T(8,128)S(1)} %copy-done.1, bf16[1152,256]{1,0:T(8,128)(2,1)S(1)} %shard_map.99.gated_ref), custom_call_target="tpu_custom_call" | custom-call | flops 4063232 | bytes 847904 | tf_op jit(solution)/shard_map/pallas_call | solution.py:35
  58.0 3.6 %collective-permute-start.20 = (bf16[256,256]{1,0:T(8,128)(2,1)S(1)}, bf16[256,256]{1,0:T(8,128)(2,1)S(1)}, u32[]{:S(2)}, u32[]{:S(2)}) collective-permute-start(bf16[256,256]{1,0:T(8,128)(2,1)S(1)} %get-tuple-element.127.refs_0_), channel_id=1, source_target_pairs={{0,24},{2,26},{4,28},{6,30},{8,16},{10,18},{12,20},{14,22},{16,8},... | collective-permute-start | bytes 393224 | tf_op jit(solution)/shard_map/ppermute | solution.py:533
  61.6 5.3 %shard_map.101.refs_0_ = bf16[768,256]{1,0:T(8,128)(2,1)S(1)} custom-call(s32[8]{0:T(128)S(1)} %copy-done.2, f32[31,1024]{1,0:T(8,128)S(1)} %copy-done.1, bf16[1152,256]{1,0:T(8,128)(2,1)S(1)} %shard_map.99.gated_ref), custom_call_target="tpu_custom_call" | custom-call | flops 12189696 | bytes 1110048 | tf_op jit(solution)/shard_map/pallas_call | solution.py:35
  67.0 0.2 collective-permute-start.21
  67.2 1.4 %collective-permute-done.21.refs_3_ = bf16[512,256]{1,0:T(8,128)(2,1)S(1)} collective-permute-done((bf16[512,256]{1,0:T(8,128)(2,1)S(1)}, bf16[512,256]{1,0:T(8,128)(2,1)S(1)}, u32[]{:S(2)}, u32[]{:S(2)}) %collective-permute-start.21) | collective-permute-done | bytes 262176 | tf_op jit(solution)/shard_map/ppermute | solution.py:530
  68.6 0.3 shard_map.103
  68.9 0.2 collective-permute-start.22
  69.2 2.3 %collective-permute-start.23 = (bf16[256,512]{1,0:T(8,128)(2,1)S(1)}, bf16[256,512]{1,0:T(8,128)(2,1)S(1)}, u32[]{:S(2)}, u32[]{:S(2)}) collective-permute-start(bf16[256,512]{1,0:T(8,128)(2,1)S(1)} %shard_map.103), channel_id=1, source_target_pairs={{0,6},{2,4},{4,2},{6,0},{8,14},{10,12},{12,10},{14,8},{16,22},{18,... | collective-permute-start | bytes 786440 | tf_op jit(solution)/shard_map/ppermute | solution.py:524
  71.4 0.6 shard_map.104
  72.0 1.1 %collective-permute-start.24 = (bf16[256,512]{1,0:T(8,128)(2,1)S(1)}, bf16[256,512]{1,0:T(8,128)(2,1)S(1)}, u32[]{:S(2)}, u32[]{:S(2)}) collective-permute-start(bf16[256,512]{1,0:T(8,128)(2,1)S(1)} %get-tuple-element.141), channel_id=1, source_target_pairs={{0,2},{2,0},{4,6},{6,4},{8,10},{10,8},{12,14},{14,12},{16,18},{18,... | collective-permute-start | bytes 786440 | tf_op jit(solution)/shard_map/ppermute | solution.py:524
  73.2 1.1 %collective-permute-start.25 = (bf16[256,512]{1,0:T(8,128)(2,1)S(1)}, bf16[256,512]{1,0:T(8,128)(2,1)S(1)}, u32[]{:S(2)}, u32[]{:S(2)}) collective-permute-start(bf16[256,512]{1,0:T(8,128)(2,1)S(1)} %get-tuple-element.142), channel_id=1, source_target_pairs={{0,4},{2,6},{4,0},{6,2},{8,12},{10,14},{12,8},{14,10},{16,20},{18,... | collective-permute-start | bytes 786440 | tf_op jit(solution)/shard_map/ppermute | solution.py:524
  74.2 5.0 %collective-permute-done.23 = bf16[256,512]{1,0:T(8,128)(2,1)S(1)} collective-permute-done((bf16[256,512]{1,0:T(8,128)(2,1)S(1)}, bf16[256,512]{1,0:T(8,128)(2,1)S(1)}, u32[]{:S(2)}, u32[]{:S(2)}) %collective-permute-start.23) | collective-permute-done | bytes 262176 | tf_op jit(solution)/shard_map/ppermute | solution.py:524
  79.2 4.9 %collective-permute-done.24 = bf16[256,512]{1,0:T(8,128)(2,1)S(1)} collective-permute-done((bf16[256,512]{1,0:T(8,128)(2,1)S(1)}, bf16[256,512]{1,0:T(8,128)(2,1)S(1)}, u32[]{:S(2)}, u32[]{:S(2)}) %collective-permute-start.24) | collective-permute-done | bytes 262176 | tf_op jit(solution)/shard_map/ppermute | solution.py:524
  84.1 0.1 collective-permute-done.25
  84.2 0.8 add_convert_fusion
  (33 shorter events, 0.4 us)
Async XLA Ops:
  2.0 9.9 %collective-permute-start.6 = (bf16[64,768]{1,0:T(8,128)(2,1)}, bf16[64,768]{1,0:T(8,128)(2,1)S(1)}, u32[]{:S(2)}, u32[]{:S(2)}) collective-permute-start(bf16[64,768]{1,0:T(8,128)(2,1)} %get-tuple-element.84), channel_id=1, source_target_pairs={{0,2},{2,0},{4,6},{6,4},{8,10},{10,8},{12,14},{14,12},{16,18},{18,... | collective-permute-start | bytes 294920 | tf_op jit(solution)/shard_map/ppermute | solution.py:524
  5.0 7.0 %collective-permute-start.7 = (bf16[64,768]{1,0:T(8,128)(2,1)}, bf16[64,768]{1,0:T(8,128)(2,1)S(1)}, u32[]{:S(2)}, u32[]{:S(2)}) collective-permute-start(bf16[64,768]{1,0:T(8,128)(2,1)} %get-tuple-element.85), channel_id=1, source_target_pairs={{0,4},{2,6},{4,0},{6,2},{8,12},{10,14},{12,8},{14,10},{16,20},{18,... | collective-permute-start | bytes 294920 | tf_op jit(solution)/shard_map/ppermute | solution.py:524
  6.5 5.7 %collective-permute-start.8 = (bf16[64,768]{1,0:T(8,128)(2,1)}, bf16[64,768]{1,0:T(8,128)(2,1)S(1)}, u32[]{:S(2)}, u32[]{:S(2)}) collective-permute-start(bf16[64,768]{1,0:T(8,128)(2,1)} %get-tuple-element.86), channel_id=1, source_target_pairs={{0,6},{2,4},{4,2},{6,0},{8,14},{10,12},{12,10},{14,8},{16,22},{18,... | collective-permute-start | bytes 294920 | tf_op jit(solution)/shard_map/ppermute | solution.py:524
  6.5 10.9 %collective-permute-start = (bf16[32,1024]{1,0:T(8,128)(2,1)}, bf16[32,1024]{1,0:T(8,128)(2,1)S(1)}, u32[]{:S(2)}, u32[]{:S(2)}) collective-permute-start(bf16[32,1024]{1,0:T(8,128)(2,1)} %get-tuple-element.75), channel_id=1, source_target_pairs={{0,8},{2,10},{4,12},{6,14},{8,0},{10,2},{12,4},{14,6},{16,24},{18,... | collective-permute-start | bytes 196616 | tf_op jit(solution)/shard_map/ppermute | solution.py:533
  8.5 11.5 %collective-permute-start.1 = (bf16[32,1024]{1,0:T(8,128)(2,1)}, bf16[32,1024]{1,0:T(8,128)(2,1)S(1)}, u32[]{:S(2)}, u32[]{:S(2)}) collective-permute-start(bf16[32,1024]{1,0:T(8,128)(2,1)} %get-tuple-element.76), channel_id=1, source_target_pairs={{0,16},{2,18},{4,20},{6,22},{8,24},{10,26},{12,28},{14,30},{16,0},... | collective-permute-start | bytes 196616 | tf_op jit(solution)/shard_map/ppermute | solution.py:533
  11.9 8.2 %collective-permute-start.2 = (bf16[32,1024]{1,0:T(8,128)(2,1)}, bf16[32,1024]{1,0:T(8,128)(2,1)S(1)}, u32[]{:S(2)}, u32[]{:S(2)}) collective-permute-start(bf16[32,1024]{1,0:T(8,128)(2,1)} %get-tuple-element.77), channel_id=1, source_target_pairs={{0,24},{2,26},{4,28},{6,30},{8,16},{10,18},{12,20},{14,22},{16,8},... | collective-permute-start | bytes 196616 | tf_op jit(solution)/shard_map/ppermute | solution.py:533
  12.2 0.9 %copy-start.4 = (bf16[64,768]{1,0:T(8,128)(2,1)S(1)}, bf16[64,768]{1,0:T(8,128)(2,1)}, u32[]{:S(2)}) copy-start(bf16[64,768]{1,0:T(8,128)(2,1)} %get-tuple-element.83.refs_0_) | copy-start | bytes 294916
  13.1 7.0 %copy-start = (bf16[256,1024]{1,0:T(8,128)(2,1)S(1)}, bf16[256,1024]{1,0:T(8,128)(2,1)}, u32[]{:S(2)}) copy-start(bf16[256,1024]{1,0:T(8,128)(2,1)} %own_ref.1) | copy-start | bytes 1572868
  13.1 7.0 %copy-start.5 = (bf16[32,1024]{1,0:T(8,128)(2,1)S(1)}, bf16[32,1024]{1,0:T(8,128)(2,1)}, u32[]{:S(2)}) copy-start(bf16[32,1024]{1,0:T(8,128)(2,1)} %get-tuple-element.74.refs_0_) | copy-start | bytes 196612
  13.2 15.4 %collective-permute-start.9 = (bf16[256,512]{1,0:T(8,128)(2,1)S(1)}, bf16[256,512]{1,0:T(8,128)(2,1)S(1)}, u32[]{:S(2)}, u32[]{:S(2)}) collective-permute-start(bf16[256,512]{1,0:T(8,128)(2,1)S(1)} %get-tuple-element.92.refs_0_), channel_id=1, source_target_pairs={{0,16},{2,18},{4,20},{6,22},{8,24},{10,26},{12,28},{14,30},{16,0},... | collective-permute-start | bytes 786440 | tf_op jit(solution)/shard_map/ppermute | solution.py:533
  15.8 12.7 %collective-permute-start.10 = (bf16[256,512]{1,0:T(8,128)(2,1)S(1)}, bf16[256,512]{1,0:T(8,128)(2,1)S(1)}, u32[]{:S(2)}, u32[]{:S(2)}) collective-permute-start(bf16[256,512]{1,0:T(8,128)(2,1)S(1)} %get-tuple-element.92.refs_0_), channel_id=1, source_target_pairs={{0,8},{2,10},{4,12},{6,14},{8,0},{10,2},{12,4},{14,6},{16,24},{18,... | collective-permute-start | bytes 786440 | tf_op jit(solution)/shard_map/ppermute | solution.py:533
  20.2 10.9 %collective-permute-start.3 = (bf16[192,1024]{1,0:T(8,128)(2,1)S(1)}, bf16[192,1024]{1,0:T(8,128)(2,1)S(1)}, u32[]{:S(2)}, u32[]{:S(2)}) collective-permute-start(bf16[192,1024]{1,0:T(8,128)(2,1)S(1)} %get-tuple-element.79), channel_id=1, source_target_pairs={{0,2},{2,0},{4,6},{6,4},{8,10},{10,8},{12,14},{14,12},{16,18},{18,... | collective-permute-start | bytes 1179656 | tf_op jit(solution)/shard_map/ppermute | solution.py:524
  21.8 14.7 %collective-permute-start.4 = (bf16[192,1024]{1,0:T(8,128)(2,1)S(1)}, bf16[192,1024]{1,0:T(8,128)(2,1)S(1)}, u32[]{:S(2)}, u32[]{:S(2)}) collective-permute-start(bf16[192,1024]{1,0:T(8,128)(2,1)S(1)} %get-tuple-element.80), channel_id=1, source_target_pairs={{0,4},{2,6},{4,0},{6,2},{8,12},{10,14},{12,8},{14,10},{16,20},{18,... | collective-permute-start | bytes 1179656 | tf_op jit(solution)/shard_map/ppermute | solution.py:524
  23.3 13.2 %collective-permute-start.5 = (bf16[192,1024]{1,0:T(8,128)(2,1)S(1)}, bf16[192,1024]{1,0:T(8,128)(2,1)S(1)}, u32[]{:S(2)}, u32[]{:S(2)}) collective-permute-start(bf16[192,1024]{1,0:T(8,128)(2,1)S(1)} %get-tuple-element.81), channel_id=1, source_target_pairs={{0,6},{2,4},{4,2},{6,0},{8,14},{10,12},{12,10},{14,8},{16,22},{18,... | collective-permute-start | bytes 1179656 | tf_op jit(solution)/shard_map/ppermute | solution.py:524
  28.5 9.4 %collective-permute-start.11 = (bf16[256,512]{1,0:T(8,128)(2,1)S(1)}, bf16[256,512]{1,0:T(8,128)(2,1)S(1)}, u32[]{:S(2)}, u32[]{:S(2)}) collective-permute-start(bf16[256,512]{1,0:T(8,128)(2,1)S(1)} %collective-permute-done.9.refs_2_), channel_id=1, source_target_pairs={{8,0},{10,2},{12,4},{14,6},{16,24},{18,26},{20,28},{22,30},{9,1},{... | collective-permute-start | bytes 786440 | tf_op jit(solution)/shard_map/ppermute | solution.py:549
  29.8 8.1 %collective-permute-start.12 = (bf16[256,512]{1,0:T(8,128)(2,1)S(1)}, bf16[256,512]{1,0:T(8,128)(2,1)S(1)}, u32[]{:S(2)}, u32[]{:S(2)}) collective-permute-start(bf16[256,512]{1,0:T(8,128)(2,1)S(1)} %get-tuple-element.92.refs_0_), channel_id=1, source_target_pairs={{8,16},{10,18},{12,20},{14,22},{16,8},{18,10},{20,12},{22,14},{9,1... | collective-permute-start | bytes 786440 | tf_op jit(solution)/shard_map/ppermute | solution.py:550
  37.0 5.3 %collective-permute-start.13 = (bf16[512,1024]{1,0:T(8,128)(2,1)S(1)}, bf16[512,1024]{1,0:T(8,128)(2,1)S(1)}, u32[]{:S(2)}, u32[]{:S(2)}) collective-permute-start(bf16[512,1024]{1,0:T(8,128)(2,1)S(1)} %get-tuple-element.99), channel_id=1, source_target_pairs={{0,1},{1,0},{2,3},{3,2},{4,5},{5,4},{6,7},{7,6},{8,9},{9,8},{10,11... | collective-permute-start | bytes 3145736 | tf_op jit(solution)/shard_map/ppermute | solution.py:530
  37.9 4.4 %copy-start.2 = (s32[8]{0:T(128)S(1)}, s32[8]{0:T(128)}, u32[]{:S(2)}) copy-start(s32[8]{0:T(128)} %len_ref.5) | copy-start | bytes 100
  37.9 14.7 %collective-permute-start.14 = (bf16[256,256]{1,0:T(8,128)(2,1)S(1)}, bf16[256,256]{1,0:T(8,128)(2,1)S(1)}, u32[]{:S(2)}, u32[]{:S(2)}) collective-permute-start(bf16[256,256]{1,0:T(8,128)(2,1)S(1)} %get-tuple-element.127.refs_0_), channel_id=1, source_target_pairs={{0,8},{2,10},{4,12},{6,14},{8,0},{10,2},{12,4},{14,6},{16,24},{18,... | collective-permute-start | bytes 393224 | tf_op jit(solution)/shard_map/ppermute | solution.py:533
  41.6 11.0 %collective-permute-start.15 = (bf16[256,256]{1,0:T(8,128)(2,1)S(1)}, bf16[256,256]{1,0:T(8,128)(2,1)S(1)}, u32[]{:S(2)}, u32[]{:S(2)}) collective-permute-start(bf16[256,256]{1,0:T(8,128)(2,1)S(1)} %get-tuple-element.127.refs_0_), channel_id=1, source_target_pairs={{0,16},{2,18},{4,20},{6,22},{8,24},{10,26},{12,28},{14,30},{16,0},... | collective-permute-start | bytes 393224 | tf_op jit(solution)/shard_map/ppermute | solution.py:533
  45.1 9.4 %copy-start.3 = (f32[1024]{0:T(1024)S(1)}, f32[1024]{0:T(1024)}, u32[]{:S(2)}) copy-start(f32[1024]{0:T(1024)} %param.14) | copy-start | bytes 12292
  45.1 10.2 %collective-permute-start.16 = (bf16[144,256]{1,0:T(8,128)(2,1)S(1)}, bf16[144,256]{1,0:T(8,128)(2,1)S(1)}, u32[]{:S(2)}, u32[]{:S(2)}) collective-permute-start(bf16[144,256]{1,0:T(8,128)(2,1)S(1)} %get-tuple-element.107), channel_id=1, source_target_pairs={{0,8},{2,10},{4,12},{6,14},{8,16},{10,18},{12,20},{14,22},{16,24},... | collective-permute-start | bytes 221192 | tf_op jit(solution)/shard_map/ppermute | solution.py:527
  49.0 6.3 %collective-permute-start.17 = (bf16[144,256]{1,0:T(8,128)(2,1)S(1)}, bf16[144,256]{1,0:T(8,128)(2,1)S(1)}, u32[]{:S(2)}, u32[]{:S(2)}) collective-permute-start(bf16[144,256]{1,0:T(8,128)(2,1)S(1)} %get-tuple-element.107), channel_id=1, source_target_pairs={{0,16},{2,18},{4,20},{6,22},{8,24},{10,26},{12,28},{14,30},{1,17},... | collective-permute-start | bytes 221192 | tf_op jit(solution)/shard_map/ppermute | solution.py:527
  51.3 4.1 %collective-permute-start.18 = (bf16[144,256]{1,0:T(8,128)(2,1)S(1)}, bf16[144,256]{1,0:T(8,128)(2,1)S(1)}, u32[]{:S(2)}, u32[]{:S(2)}) collective-permute-start(bf16[144,256]{1,0:T(8,128)(2,1)S(1)} %get-tuple-element.107), channel_id=1, source_target_pairs={{0,24},{2,26},{4,28},{6,30},{1,25},{3,27},{5,29},{7,31}} | collective-permute-start | bytes 221192 | tf_op jit(solution)/shard_map/ppermute | solution.py:527
  55.4 0.9 %copy-start.1 = (f32[31,1024]{1,0:T(8,128)S(1)}, f32[31,1024]{1,0:T(8,128)}, u32[]{:S(2)}) copy-start(f32[31,1024]{1,0:T(8,128)} %taps_ref.3) | copy-start | bytes 380932
  57.9 8.9 %collective-permute-start.19 = (bf16[256,256]{1,0:T(8,128)(2,1)S(1)}, bf16[256,256]{1,0:T(8,128)(2,1)S(1)}, u32[]{:S(2)}, u32[]{:S(2)}) collective-permute-start(bf16[256,256]{1,0:T(8,128)(2,1)S(1)} %shard_map.100.refs_0_), channel_id=1, source_target_pairs={{0,1},{1,0},{2,3},{3,2},{4,5},{5,4},{6,7},{7,6},{8,9},{9,8},{10,11... | collective-permute-start | bytes 393224 | tf_op jit(solution)/shard_map/ppermute | solution.py:530
  58.0 8.9 %collective-permute-start.20 = (bf16[256,256]{1,0:T(8,128)(2,1)S(1)}, bf16[256,256]{1,0:T(8,128)(2,1)S(1)}, u32[]{:S(2)}, u32[]{:S(2)}) collective-permute-start(bf16[256,256]{1,0:T(8,128)(2,1)S(1)} %get-tuple-element.127.refs_0_), channel_id=1, source_target_pairs={{0,24},{2,26},{4,28},{6,30},{8,16},{10,18},{12,20},{14,22},{16,8},... | collective-permute-start | bytes 393224 | tf_op jit(solution)/shard_map/ppermute | solution.py:533
  67.0 1.6 %collective-permute-start.21 = (bf16[512,256]{1,0:T(8,128)(2,1)S(1)}, bf16[512,256]{1,0:T(8,128)(2,1)S(1)}, u32[]{:S(2)}, u32[]{:S(2)}) collective-permute-start(bf16[512,256]{1,0:T(8,128)(2,1)S(1)} %get-tuple-element.132), channel_id=1, source_target_pairs={{0,1},{1,0},{2,3},{3,2},{4,5},{5,4},{6,7},{7,6},{8,9},{9,8},{10,11... | collective-permute-start | bytes 786440 | tf_op jit(solution)/shard_map/ppermute | solution.py:530
  68.9 2.5 %collective-permute-start.22 = (bf16[768,256]{1,0:T(8,128)(2,1)S(1)}, bf16[768,256]{1,0:T(8,128)(2,1)S(1)}, u32[]{:S(2)}, u32[]{:S(2)}) collective-permute-start(bf16[768,256]{1,0:T(8,128)(2,1)S(1)} %shard_map.101.refs_0_), channel_id=1, source_target_pairs={{0,1},{1,0},{2,3},{3,2},{4,5},{5,4},{6,7},{7,6},{8,9},{9,8},{10,11... | collective-permute-start | bytes 1179656 | tf_op jit(solution)/shard_map/ppermute | solution.py:530
  69.2 10.1 %collective-permute-start.23 = (bf16[256,512]{1,0:T(8,128)(2,1)S(1)}, bf16[256,512]{1,0:T(8,128)(2,1)S(1)}, u32[]{:S(2)}, u32[]{:S(2)}) collective-permute-start(bf16[256,512]{1,0:T(8,128)(2,1)S(1)} %shard_map.103), channel_id=1, source_target_pairs={{0,6},{2,4},{4,2},{6,0},{8,14},{10,12},{12,10},{14,8},{16,22},{18,... | collective-permute-start | bytes 786440 | tf_op jit(solution)/shard_map/ppermute | solution.py:524
  72.0 12.1 %collective-permute-start.24 = (bf16[256,512]{1,0:T(8,128)(2,1)S(1)}, bf16[256,512]{1,0:T(8,128)(2,1)S(1)}, u32[]{:S(2)}, u32[]{:S(2)}) collective-permute-start(bf16[256,512]{1,0:T(8,128)(2,1)S(1)} %get-tuple-element.141), channel_id=1, source_target_pairs={{0,2},{2,0},{4,6},{6,4},{8,10},{10,8},{12,14},{14,12},{16,18},{18,... | collective-permute-start | bytes 786440 | tf_op jit(solution)/shard_map/ppermute | solution.py:524
  73.2 11.1 %collective-permute-start.25 = (bf16[256,512]{1,0:T(8,128)(2,1)S(1)}, bf16[256,512]{1,0:T(8,128)(2,1)S(1)}, u32[]{:S(2)}, u32[]{:S(2)}) collective-permute-start(bf16[256,512]{1,0:T(8,128)(2,1)S(1)} %get-tuple-element.142), channel_id=1, source_target_pairs={{0,4},{2,6},{4,0},{6,2},{8,12},{10,14},{12,8},{14,10},{16,20},{18,... | collective-permute-start | bytes 786440 | tf_op jit(solution)/shard_map/ppermute | solution.py:524

commit v16 on v13

--- a/solution.py
+++ b/solution.py
@@ -483,8 +483,8 @@
         lax.fori_loop(0, frames // CONV_ROWS, one_block, 0)
 
 
-def out_kernel(cores, *refs):
-    acts, weights, outs = refs[:cores], refs[cores : 2 * cores], refs[2 * cores :]
+def out_kernel(cores, count, *refs):
+    acts, weights, sent, outs = refs[:cores], refs[cores : 2 * cores], refs[2 * cores : -count], refs[-count:]
     frames = outs[0].shape[0]
     for number, out_ref in enumerate(outs):
         rows = slice(number * frames, (number + 1) * frames)
@@ -492,6 +492,8 @@
         for act, weight in zip(acts, weights):
             product = dot(act[rows, :], weight[...], ((1,), (1,)))
             total = product if total is None else total + product
+        for part in sent:
+            total = total + part[...].astype(F32)
         out_ref[...] = total.astype(out_ref.dtype)
 
 
@@ -655,7 +657,7 @@
         smem=0,
     )
     ends = pltpu.SMEM((record_lengths.shape[0] + 1,), jnp.int32)
-    far, near = (group - 1,), (*range(1, group - 1), 0)
+    far, near = (group - 1,), tuple(range(1, group - 1))
 
     def conv(steps, gated):
         return call(
@@ -666,11 +668,11 @@
             flops=2 * len(steps) * frame_count * width * conv_weight.shape[0],
         )
 
-    def out(steps, act, swapped):
+    def out(steps, act, swapped, sent=()):
         return call(
-            functools.partial(out_kernel, cores),
-            tuple(shape((frame_count, share), BF16 if step else F32) for step in steps),
-            [act, *swapped, *out_parts],
+            functools.partial(out_kernel, cores, len(steps)),
+            tuple(shape((frame_count, share), BF16) for _ in steps),
+            [act, *swapped, *out_parts, *sent],
             flops=2 * len(steps) * frame_count * width * cores * share,
             smem=0,
         )
@@ -688,17 +690,22 @@
     far_act = conv(far, gated)
     far_swapped = [across(far_act, step) for step in range(1, cores)]
     gated, far_act = lax.optimization_barrier((gated, far_act))
-    near_act = conv(near, gated)
-    near_act, far_swapped, out_parts = lax.optimization_barrier((near_act, far_swapped, out_parts))
+    if near:
+        near_act = conv(near, gated)
+        near_act, far_swapped, out_parts = lax.optimization_barrier((near_act, far_swapped, out_parts))
     (far_out,) = out(far, far_act, far_swapped)
-    near_act, far_out = lax.optimization_barrier((near_act, far_out))
-    far_out = in_plane(far_out, far[0])
-    near_swapped = [across(near_act, step) for step in range(1, cores)]
-    near_outs = out(near, near_act, near_swapped)
-    mixed = near_outs[-1] + far_out.astype(F32)
-    for step, partial in zip(near[:-1], near_outs[:-1]):
-        mixed = mixed + in_plane(partial, step).astype(F32)
-    return mixed.astype(BF16)
+    if near:
+        near_act, far_out = lax.optimization_barrier((near_act, far_out))
+    sent = [in_plane(far_out, far[0])]
+    if near:
+        near_swapped = [across(near_act, step) for step in range(1, cores)]
+        near_outs = out(near, near_act, near_swapped)
+        gated, near_outs = lax.optimization_barrier((gated, near_outs))
+        sent += [in_plane(part, step) for part, step in zip(near_outs, near)]
+    own_act = conv((0,), gated)
+    own_swapped = [across(own_act, step) for step in range(1, cores)]
+    (mixed,) = out((0,), own_act, own_swapped, sent)
+    return mixed
 
 
 def solution(mesh):

time: 83.2 us -> 81.9 us (0.984)
  waiting for transfers between devices: 24.7 us -> 22.6 us
  Pallas kernels: 16.9 us -> 18.1 us
  other arithmetic: 0.84 us -> 0 us
    ppermute x9, waiting for transfers between devices: 16.5 us -> 14.4 us  [in_plane(): return lax.ppermute(array, 'tm', [(i, i ^ step) for i in range(times)])]
    pallas_call x14 -> x16, Pallas kernels: 16.9 us -> 18.1 us  [call(): pl.pallas_call(kernel, out_shape=out_shape, in_specs=in_specs, out_specs=...]
    convert_element_type x1 -> x0, other arithmetic: 0.84 us -> none  [local(): return mixed.astype(BF16)]
  transfers between devices with their start and end apart: 26 -> 27, of which waited for: 9 -> 8; matrix products, arithmetic and copies ran while one was open for 1% -> 1% of each run, Pallas kernels for 17% -> 17%
where the time goes in v16:
time: 81.9 us; the launch traced here: 80.9 us
  starting transfers between devices  38.1 us (47%)
  waiting for transfers between devices  22.6 us (28%)
  Pallas kernels  18.1 us (22%)
  local copies, waits for them, and re-layouts  1.78 us (2%)
    pallas_call x16, Pallas kernels, call(): pl.pallas_call(kernel, out_shape=out_shape, in_specs=in_specs, out_specs=...  18.1 us
    ppermute x8, starting transfers between devices, between_planes(): lax.ppermute(array, 'tm', [(i, i ^ step * group) for i in range(times)])  15 us
    ppermute x9, waiting for transfers between devices, in_plane(): return lax.ppermute(array, 'tm', [(i, i ^ step) for i in range(times)])  14.4 us
    ppermute x9, starting transfers between devices, in_plane(): return lax.ppermute(array, 'tm', [(i, i ^ step) for i in range(times)])  12.6 us
    ppermute x3, starting transfers between devices, later(): lax.ppermute(array, 'tm', [(i, i + step * group) for i in range(times - s...  7.73 us
    ppermute x8, waiting for transfers between devices, between_planes(): lax.ppermute(array, 'tm', [(i, i ^ step * group) for i in range(times)])  7.41 us
  transfers between devices with their start and end apart: 27, of which 8 were waited for; matrix products, arithmetic and copies ran while one was open for 1% of the time, Pallas kernels for 17%

profile of v16, /device:TPU:0, one launch (start us, length us, event | category | flops | bytes accessed | tf_op | source)
XLA Modules:
  0.0 80.9 jit_solution(11996802130997864253)
XLA Ops:
  0.0 2.0 %shard_map.91 = (bf16[64,768]{1,0:T(8,128)(2,1)}, bf16[64,768]{1,0:T(8,128)(2,1)}, bf16[64,768]{1,0:T(8,128)(2,1)}, bf16[64,768]{1,0:T(8,128)(2,1)}, bf16[32,102...) custom-call(f32[16,256]{1,0:T(8,128)} %log_decay_ref.1, ...), custom_call_target="tpu_custom_call" | custom-call | bytes 1622016 | tf_op jit(solution)/shard_map/pallas_call | solution.py:35
  2.0 3.0 %collective-permute-start.6 = (bf16[64,768]{1,0:T(8,128)(2,1)}, bf16[64,768]{1,0:T(8,128)(2,1)S(1)}, u32[]{:S(2)}, u32[]{:S(2)}) collective-permute-start(bf16[64,768]{1,0:T(8,128)(2,1)} %get-tuple-element.77), channel_id=1, source_target_pairs={{0,2},{2,0},{4,6},{6,4},{8,10},{10,8},{12,14},{14,12},{16,18},{18,... | collective-permute-start | bytes 294920 | tf_op jit(solution)/shard_map/ppermute | solution.py:526
  5.0 1.5 %collective-permute-start.7 = (bf16[64,768]{1,0:T(8,128)(2,1)}, bf16[64,768]{1,0:T(8,128)(2,1)S(1)}, u32[]{:S(2)}, u32[]{:S(2)}) collective-permute-start(bf16[64,768]{1,0:T(8,128)(2,1)} %get-tuple-element.78), channel_id=1, source_target_pairs={{0,4},{2,6},{4,0},{6,2},{8,12},{10,14},{12,8},{14,10},{16,20},{18,... | collective-permute-start | bytes 294920 | tf_op jit(solution)/shard_map/ppermute | solution.py:526
  6.5 2.0 %collective-permute-start = (bf16[32,1024]{1,0:T(8,128)(2,1)}, bf16[32,1024]{1,0:T(8,128)(2,1)S(1)}, u32[]{:S(2)}, u32[]{:S(2)}) collective-permute-start(bf16[32,1024]{1,0:T(8,128)(2,1)} %get-tuple-element.68), channel_id=1, source_target_pairs={{0,8},{2,10},{4,12},{6,14},{8,0},{10,2},{12,4},{14,6},{16,24},{18,... | collective-permute-start | bytes 196616 | tf_op jit(solution)/shard_map/ppermute | solution.py:535
  8.5 2.6 %collective-permute-start.1 = (bf16[32,1024]{1,0:T(8,128)(2,1)}, bf16[32,1024]{1,0:T(8,128)(2,1)S(1)}, u32[]{:S(2)}, u32[]{:S(2)}) collective-permute-start(bf16[32,1024]{1,0:T(8,128)(2,1)} %get-tuple-element.69), channel_id=1, source_target_pairs={{0,16},{2,18},{4,20},{6,22},{8,24},{10,26},{12,28},{14,30},{16,0},... | collective-permute-start | bytes 196616 | tf_op jit(solution)/shard_map/ppermute | solution.py:535
  11.1 0.7 reshape.3
  12.0 0.2 collective-permute-done.8.refs_3_
  12.2 0.9 %copy-done.4 = bf16[64,768]{1,0:T(8,128)(2,1)S(1)} copy-done((bf16[64,768]{1,0:T(8,128)(2,1)S(1)}, bf16[64,768]{1,0:T(8,128)(2,1)}, u32[]{:S(2)}) %copy-start.4) | copy-done | bytes 98328
  13.2 2.7 %collective-permute-start.9 = (bf16[256,512]{1,0:T(8,128)(2,1)S(1)}, bf16[256,512]{1,0:T(8,128)(2,1)S(1)}, u32[]{:S(2)}, u32[]{:S(2)}) collective-permute-start(bf16[256,512]{1,0:T(8,128)(2,1)S(1)} %get-tuple-element.85.refs_0_), channel_id=1, source_target_pairs={{0,16},{2,18},{4,20},{6,22},{8,24},{10,26},{12,28},{14,30},{16,0},... | collective-permute-start | bytes 786440 | tf_op jit(solution)/shard_map/ppermute | solution.py:535
  15.8 1.6 %collective-permute-start.10 = (bf16[256,512]{1,0:T(8,128)(2,1)S(1)}, bf16[256,512]{1,0:T(8,128)(2,1)S(1)}, u32[]{:S(2)}, u32[]{:S(2)}) collective-permute-start(bf16[256,512]{1,0:T(8,128)(2,1)S(1)} %get-tuple-element.85.refs_0_), channel_id=1, source_target_pairs={{0,8},{2,10},{4,12},{6,14},{8,0},{10,2},{12,4},{14,6},{16,24},{18,... | collective-permute-start | bytes 786440 | tf_op jit(solution)/shard_map/ppermute | solution.py:535
  17.4 2.7 %collective-permute-done.1.refs_2_ = bf16[32,1024]{1,0:T(8,128)(2,1)S(1)} collective-permute-done((bf16[32,1024]{1,0:T(8,128)(2,1)}, bf16[32,1024]{1,0:T(8,128)(2,1)S(1)}, u32[]{:S(2)}, u32[]{:S(2)}) %collective-permute-start.1) | collective-permute-done | bytes 65568 | tf_op jit(solution)/shard_map/ppermute | solution.py:535
  20.1 0.2 shard_map.92
  20.2 1.6 %collective-permute-start.3 = (bf16[192,1024]{1,0:T(8,128)(2,1)S(1)}, bf16[192,1024]{1,0:T(8,128)(2,1)S(1)}, u32[]{:S(2)}, u32[]{:S(2)}) collective-permute-start(bf16[192,1024]{1,0:T(8,128)(2,1)S(1)} %get-tuple-element.72), channel_id=1, source_target_pairs={{0,2},{2,0},{4,6},{6,4},{8,10},{10,8},{12,14},{14,12},{16,18},{18,... | collective-permute-start | bytes 1179656 | tf_op jit(solution)/shard_map/ppermute | solution.py:526
  21.8 1.5 %collective-permute-start.4 = (bf16[192,1024]{1,0:T(8,128)(2,1)S(1)}, bf16[192,1024]{1,0:T(8,128)(2,1)S(1)}, u32[]{:S(2)}, u32[]{:S(2)}) collective-permute-start(bf16[192,1024]{1,0:T(8,128)(2,1)S(1)} %get-tuple-element.73), channel_id=1, source_target_pairs={{0,4},{2,6},{4,0},{6,2},{8,12},{10,14},{12,8},{14,10},{16,20},{18,... | collective-permute-start | bytes 1179656 | tf_op jit(solution)/shard_map/ppermute | solution.py:526
  23.3 0.5 collective-permute-start.5
  23.8 4.7 %collective-permute-done.9.refs_2_ = bf16[256,512]{1,0:T(8,128)(2,1)S(1)} collective-permute-done((bf16[256,512]{1,0:T(8,128)(2,1)S(1)}, bf16[256,512]{1,0:T(8,128)(2,1)S(1)}, u32[]{:S(2)}, u32[]{:S(2)}) %collective-permute-start.9) | collective-permute-done | bytes 262176 | tf_op jit(solution)/shard_map/ppermute | solution.py:535
  28.5 1.3 %collective-permute-start.11 = (bf16[256,512]{1,0:T(8,128)(2,1)S(1)}, bf16[256,512]{1,0:T(8,128)(2,1)S(1)}, u32[]{:S(2)}, u32[]{:S(2)}) collective-permute-start(bf16[256,512]{1,0:T(8,128)(2,1)S(1)} %collective-permute-done.9.refs_2_), channel_id=1, source_target_pairs={{8,0},{10,2},{12,4},{14,6},{16,24},{18,26},{20,28},{22,30},{9,1},{... | collective-permute-start | bytes 786440 | tf_op jit(solution)/shard_map/ppermute | solution.py:551
  29.8 0.7 collective-permute-start.12
  30.5 0.6 collective-permute-done.3.refs_1_.refs_0_
  31.1 5.4 %collective-permute-done.4.refs_2_.refs_1_ = bf16[192,1024]{1,0:T(8,128)(2,1)S(1)} collective-permute-done((bf16[192,1024]{1,0:T(8,128)(2,1)S(1)}, bf16[192,1024]{1,0:T(8,128)(2,1)S(1)}, u32[]{:S(2)}, u32[]{:S(2)}) %collective-permute-start.4) | collective-permute-done | bytes 393248 | tf_op jit(solution)/shard_map/ppermute | solution.py:526
  36.5 0.5 shard_map.93
  37.1 0.8 collective-permute-done.11.refs_3_
  37.9 3.7 %collective-permute-start.14 = (bf16[256,256]{1,0:T(8,128)(2,1)S(1)}, bf16[256,256]{1,0:T(8,128)(2,1)S(1)}, u32[]{:S(2)}, u32[]{:S(2)}) collective-permute-start(bf16[256,256]{1,0:T(8,128)(2,1)S(1)} %get-tuple-element.96.refs_0_), channel_id=1, source_target_pairs={{0,8},{2,10},{4,12},{6,14},{8,0},{10,2},{12,4},{14,6},{16,24},{18,... | collective-permute-start | bytes 393224 | tf_op jit(solution)/shard_map/ppermute | solution.py:535
  41.6 0.6 collective-permute-start.15
  42.2 1.8 %collective-permute-start.16 = (bf16[256,256]{1,0:T(8,128)(2,1)S(1)}, bf16[256,256]{1,0:T(8,128)(2,1)S(1)}, u32[]{:S(2)}, u32[]{:S(2)}) collective-permute-start(bf16[256,256]{1,0:T(8,128)(2,1)S(1)} %get-tuple-element.96.refs_0_), channel_id=1, source_target_pairs={{0,24},{2,26},{4,28},{6,30},{8,16},{10,18},{12,20},{14,22},{16,8},... | collective-permute-start | bytes 393224 | tf_op jit(solution)/shard_map/ppermute | solution.py:535
  43.9 0.1 shard_map.95
  44.0 2.8 %shard_map.96 = (bf16[1152,1024]{1,0:T(8,128)(2,1)S(1)}, bf16[1152,256]{1,0:T(8,128)(2,1)S(1)}, bf16[1152,128]{1,0:T(8,128)(2,1)S(1)}, bf16[1152,128]{1,0:T(8,12...) custom-call(s32[8]{0:T(128)S(1)} %copy-done.2, ...), custom_call_target="tpu_custom_call" | custom-call | tf_op jit(solution)/shard_map/pallas_call | solution.py:35
  46.8 3.0 %collective-permute-start.17 = (bf16[144,256]{1,0:T(8,128)(2,1)S(1)}, bf16[144,256]{1,0:T(8,128)(2,1)S(1)}, u32[]{:S(2)}, u32[]{:S(2)}) collective-permute-start(bf16[144,256]{1,0:T(8,128)(2,1)S(1)} %get-tuple-element.112), channel_id=1, source_target_pairs={{0,8},{2,10},{4,12},{6,14},{8,16},{10,18},{12,20},{14,22},{16,24},... | collective-permute-start | bytes 221192 | tf_op jit(solution)/shard_map/ppermute | solution.py:529
  49.9 3.4 %collective-permute-start.18 = (bf16[144,256]{1,0:T(8,128)(2,1)S(1)}, bf16[144,256]{1,0:T(8,128)(2,1)S(1)}, u32[]{:S(2)}, u32[]{:S(2)}) collective-permute-start(bf16[144,256]{1,0:T(8,128)(2,1)S(1)} %get-tuple-element.112), channel_id=1, source_target_pairs={{0,16},{2,18},{4,20},{6,22},{8,24},{10,26},{12,28},{14,30},{1,17},... | collective-permute-start | bytes 221192 | tf_op jit(solution)/shard_map/ppermute | solution.py:529
  53.3 1.3 %collective-permute-start.19 = (bf16[144,256]{1,0:T(8,128)(2,1)S(1)}, bf16[144,256]{1,0:T(8,128)(2,1)S(1)}, u32[]{:S(2)}, u32[]{:S(2)}) collective-permute-start(bf16[144,256]{1,0:T(8,128)(2,1)S(1)} %get-tuple-element.112), channel_id=1, source_target_pairs={{0,24},{2,26},{4,28},{6,30},{1,25},{3,27},{5,29},{7,31}} | collective-permute-start | bytes 221192 | tf_op jit(solution)/shard_map/ppermute | solution.py:529
  54.6 0.1 shard_map.97
  54.7 1.9 %shard_map.98 = (f32[1152,256]{1,0:T(8,128)S(1)}, f32[1152,256]{1,0:T(8,128)S(1)}) custom-call(bf16[1152,256]{1,0:T(8,128)(2,1)S(1)} %get-tuple-element.103.x_ref, bf16[1152,128]{1,0:T(8,128)(2,1)S(1)} %get-tuple-element.104.b_ref, bf16[1152,128]{1,0:T(8,128)(2,1)S(1)} %get-tuple-element.102.c_ref, f32[216,128]{1,0:T(8,128)S(1)} %get-tuple-element.105.rows_ref), custom_call_target="tpu_custom_call" | custom-call | flops 134217728 | bytes 3649536 | tf_op jit(solution)/shard_map/pallas_call | solution.py:35
  56.6 0.8 %shard_map.99.silu_ref = f32[1152,256]{1,0:T(8,128)S(1)} custom-call(f32[1,1024]{1,0:T(1,128)S(1)} %bitcast.2, bf16[1152,1024]{1,0:T(8,128)(2,1)S(1)} %get-tuple-element.110.frames_ref, bf16[1024,256]{1,0:T(8,128)(2,1)S(1)} %get-tuple-element.111.weight_ref), custom_call_target="tpu_custom_call" | custom-call | flops 536870912 | bytes 4067328 | tf_op jit(solution)/shard_map/pallas_call | solution.py:35
  57.5 0.7 shard_map.100.gated_ref
  58.3 0.1 copy-done.1
  58.4 1.9 %shard_map.101.refs_0_ = bf16[256,256]{1,0:T(8,128)(2,1)S(1)} custom-call(s32[8]{0:T(128)S(1)} %copy-done.2, f32[31,1024]{1,0:T(8,128)S(1)} %copy-done.1, bf16[1152,256]{1,0:T(8,128)(2,1)S(1)} %shard_map.100.gated_ref), custom_call_target="tpu_custom_call" | custom-call | flops 4063232 | bytes 847904 | tf_op jit(solution)/shard_map/pallas_call | solution.py:35
  60.3 0.4 collective-permute-start.20
  60.7 3.1 %shard_map.102.refs_0_ = bf16[512,256]{1,0:T(8,128)(2,1)S(1)} custom-call(s32[8]{0:T(128)S(1)} %copy-done.2, f32[31,1024]{1,0:T(8,128)S(1)} %copy-done.1, bf16[1152,256]{1,0:T(8,128)(2,1)S(1)} %shard_map.100.gated_ref), custom_call_target="tpu_custom_call" | custom-call | flops 8126464 | bytes 978976 | tf_op jit(solution)/shard_map/pallas_call | solution.py:35
  63.9 0.3 shard_map.103
  64.2 0.2 collective-permute-start.22
  64.4 2.5 %collective-permute-start.24 = (bf16[256,512]{1,0:T(8,128)(2,1)S(1)}, bf16[256,512]{1,0:T(8,128)(2,1)S(1)}, u32[]{:S(2)}, u32[]{:S(2)}) collective-permute-start(bf16[256,512]{1,0:T(8,128)(2,1)S(1)} %shard_map.103), channel_id=1, source_target_pairs={{0,6},{2,4},{4,2},{6,0},{8,14},{10,12},{12,10},{14,8},{16,22},{18,... | collective-permute-start | bytes 786440 | tf_op jit(solution)/shard_map/ppermute | solution.py:526
  67.0 0.5 shard_map.104
  67.4 1.2 %collective-permute-start.25 = (bf16[256,512]{1,0:T(8,128)(2,1)S(1)}, bf16[256,512]{1,0:T(8,128)(2,1)S(1)}, u32[]{:S(2)}, u32[]{:S(2)}) collective-permute-start(bf16[256,512]{1,0:T(8,128)(2,1)S(1)} %get-tuple-element.127), channel_id=1, source_target_pairs={{0,2},{2,0},{4,6},{6,4},{8,10},{10,8},{12,14},{14,12},{16,18},{18,... | collective-permute-start | bytes 786440 | tf_op jit(solution)/shard_map/ppermute | solution.py:526
  68.6 0.8 collective-permute-start.26
  69.4 2.3 %shard_map.105.refs_0_ = bf16[256,256]{1,0:T(8,128)(2,1)S(1)} custom-call(s32[8]{0:T(128)S(1)} %copy-done.2, f32[31,1024]{1,0:T(8,128)S(1)} %copy-done.1, bf16[1152,256]{1,0:T(8,128)(2,1)S(1)} %shard_map.100.gated_ref), custom_call_target="tpu_custom_call" | custom-call | flops 4063232 | bytes 847904 | tf_op jit(solution)/shard_map/pallas_call | solution.py:35
  71.8 2.7 %collective-permute-done.24.refs_4_ = bf16[256,512]{1,0:T(8,128)(2,1)S(1)} collective-permute-done((bf16[256,512]{1,0:T(8,128)(2,1)S(1)}, bf16[256,512]{1,0:T(8,128)(2,1)S(1)}, u32[]{:S(2)}, u32[]{:S(2)}) %collective-permute-start.24) | collective-permute-done | bytes 262176 | tf_op jit(solution)/shard_map/ppermute | solution.py:526
  74.5 5.4 %collective-permute-done.25.refs_5_ = bf16[256,512]{1,0:T(8,128)(2,1)S(1)} collective-permute-done((bf16[256,512]{1,0:T(8,128)(2,1)S(1)}, bf16[256,512]{1,0:T(8,128)(2,1)S(1)}, u32[]{:S(2)}, u32[]{:S(2)}) %collective-permute-start.25) | collective-permute-done | bytes 262176 | tf_op jit(solution)/shard_map/ppermute | solution.py:526
  79.9 1.1 %shard_map.106 = bf16[256,512]{1,0:T(8,128)(2,1)} custom-call(bf16[256,256]{1,0:T(8,128)(2,1)S(1)} %shard_map.105.refs_0_, bf16[256,256]{1,0:T(8,128)(2,1)S(1)} %collective-permute-done.23.refs_1_, bf16[512,256]{1,0:T(8,128)(2,1)S(1)} %get-tuple-element.120.refs_2_, bf16[512,256]{1,0:T(8,128)(2,1)S(1)} %collective-permute-done.21.refs_3_, ...), custom_call_target="tpu_custom_call" | custom-call | flops 134217728 | bytes 1835008 | tf_op jit(solution)/shard_map/pallas_call | solution.py:35
  (36 shorter events, 0.4 us)
Async XLA Ops:
  2.0 9.9 %collective-permute-start.6 = (bf16[64,768]{1,0:T(8,128)(2,1)}, bf16[64,768]{1,0:T(8,128)(2,1)S(1)}, u32[]{:S(2)}, u32[]{:S(2)}) collective-permute-start(bf16[64,768]{1,0:T(8,128)(2,1)} %get-tuple-element.77), channel_id=1, source_target_pairs={{0,2},{2,0},{4,6},{6,4},{8,10},{10,8},{12,14},{14,12},{16,18},{18,... | collective-permute-start | bytes 294920 | tf_op jit(solution)/shard_map/ppermute | solution.py:526
  5.0 7.0 %collective-permute-start.7 = (bf16[64,768]{1,0:T(8,128)(2,1)}, bf16[64,768]{1,0:T(8,128)(2,1)S(1)}, u32[]{:S(2)}, u32[]{:S(2)}) collective-permute-start(bf16[64,768]{1,0:T(8,128)(2,1)} %get-tuple-element.78), channel_id=1, source_target_pairs={{0,4},{2,6},{4,0},{6,2},{8,12},{10,14},{12,8},{14,10},{16,20},{18,... | collective-permute-start | bytes 294920 | tf_op jit(solution)/shard_map/ppermute | solution.py:526
  6.5 5.7 %collective-permute-start.8 = (bf16[64,768]{1,0:T(8,128)(2,1)}, bf16[64,768]{1,0:T(8,128)(2,1)S(1)}, u32[]{:S(2)}, u32[]{:S(2)}) collective-permute-start(bf16[64,768]{1,0:T(8,128)(2,1)} %get-tuple-element.79), channel_id=1, source_target_pairs={{0,6},{2,4},{4,2},{6,0},{8,14},{10,12},{12,10},{14,8},{16,22},{18,... | collective-permute-start | bytes 294920 | tf_op jit(solution)/shard_map/ppermute | solution.py:526
  6.5 10.9 %collective-permute-start = (bf16[32,1024]{1,0:T(8,128)(2,1)}, bf16[32,1024]{1,0:T(8,128)(2,1)S(1)}, u32[]{:S(2)}, u32[]{:S(2)}) collective-permute-start(bf16[32,1024]{1,0:T(8,128)(2,1)} %get-tuple-element.68), channel_id=1, source_target_pairs={{0,8},{2,10},{4,12},{6,14},{8,0},{10,2},{12,4},{14,6},{16,24},{18,... | collective-permute-start | bytes 196616 | tf_op jit(solution)/shard_map/ppermute | solution.py:535
  8.5 11.5 %collective-permute-start.1 = (bf16[32,1024]{1,0:T(8,128)(2,1)}, bf16[32,1024]{1,0:T(8,128)(2,1)S(1)}, u32[]{:S(2)}, u32[]{:S(2)}) collective-permute-start(bf16[32,1024]{1,0:T(8,128)(2,1)} %get-tuple-element.69), channel_id=1, source_target_pairs={{0,16},{2,18},{4,20},{6,22},{8,24},{10,26},{12,28},{14,30},{16,0},... | collective-permute-start | bytes 196616 | tf_op jit(solution)/shard_map/ppermute | solution.py:535
  11.9 8.2 %collective-permute-start.2 = (bf16[32,1024]{1,0:T(8,128)(2,1)}, bf16[32,1024]{1,0:T(8,128)(2,1)S(1)}, u32[]{:S(2)}, u32[]{:S(2)}) collective-permute-start(bf16[32,1024]{1,0:T(8,128)(2,1)} %get-tuple-element.70), channel_id=1, source_target_pairs={{0,24},{2,26},{4,28},{6,30},{8,16},{10,18},{12,20},{14,22},{16,8},... | collective-permute-start | bytes 196616 | tf_op jit(solution)/shard_map/ppermute | solution.py:535
  12.2 0.9 %copy-start.4 = (bf16[64,768]{1,0:T(8,128)(2,1)S(1)}, bf16[64,768]{1,0:T(8,128)(2,1)}, u32[]{:S(2)}) copy-start(bf16[64,768]{1,0:T(8,128)(2,1)} %get-tuple-element.76.refs_0_) | copy-start | bytes 294916
  13.1 7.0 %copy-start = (bf16[256,1024]{1,0:T(8,128)(2,1)S(1)}, bf16[256,1024]{1,0:T(8,128)(2,1)}, u32[]{:S(2)}) copy-start(bf16[256,1024]{1,0:T(8,128)(2,1)} %own_ref.1) | copy-start | bytes 1572868
  13.1 7.0 %copy-start.5 = (bf16[32,1024]{1,0:T(8,128)(2,1)S(1)}, bf16[32,1024]{1,0:T(8,128)(2,1)}, u32[]{:S(2)}) copy-start(bf16[32,1024]{1,0:T(8,128)(2,1)} %get-tuple-element.67.refs_0_) | copy-start | bytes 196612
  13.2 15.4 %collective-permute-start.9 = (bf16[256,512]{1,0:T(8,128)(2,1)S(1)}, bf16[256,512]{1,0:T(8,128)(2,1)S(1)}, u32[]{:S(2)}, u32[]{:S(2)}) collective-permute-start(bf16[256,512]{1,0:T(8,128)(2,1)S(1)} %get-tuple-element.85.refs_0_), channel_id=1, source_target_pairs={{0,16},{2,18},{4,20},{6,22},{8,24},{10,26},{12,28},{14,30},{16,0},... | collective-permute-start | bytes 786440 | tf_op jit(solution)/shard_map/ppermute | solution.py:535
  15.8 12.7 %collective-permute-start.10 = (bf16[256,512]{1,0:T(8,128)(2,1)S(1)}, bf16[256,512]{1,0:T(8,128)(2,1)S(1)}, u32[]{:S(2)}, u32[]{:S(2)}) collective-permute-start(bf16[256,512]{1,0:T(8,128)(2,1)S(1)} %get-tuple-element.85.refs_0_), channel_id=1, source_target_pairs={{0,8},{2,10},{4,12},{6,14},{8,0},{10,2},{12,4},{14,6},{16,24},{18,... | collective-permute-start | bytes 786440 | tf_op jit(solution)/shard_map/ppermute | solution.py:535
  20.2 10.9 %collective-permute-start.3 = (bf16[192,1024]{1,0:T(8,128)(2,1)S(1)}, bf16[192,1024]{1,0:T(8,128)(2,1)S(1)}, u32[]{:S(2)}, u32[]{:S(2)}) collective-permute-start(bf16[192,1024]{1,0:T(8,128)(2,1)S(1)} %get-tuple-element.72), channel_id=1, source_target_pairs={{0,2},{2,0},{4,6},{6,4},{8,10},{10,8},{12,14},{14,12},{16,18},{18,... | collective-permute-start | bytes 1179656 | tf_op jit(solution)/shard_map/ppermute | solution.py:526
  21.8 14.7 %collective-permute-start.4 = (bf16[192,1024]{1,0:T(8,128)(2,1)S(1)}, bf16[192,1024]{1,0:T(8,128)(2,1)S(1)}, u32[]{:S(2)}, u32[]{:S(2)}) collective-permute-start(bf16[192,1024]{1,0:T(8,128)(2,1)S(1)} %get-tuple-element.73), channel_id=1, source_target_pairs={{0,4},{2,6},{4,0},{6,2},{8,12},{10,14},{12,8},{14,10},{16,20},{18,... | collective-permute-start | bytes 1179656 | tf_op jit(solution)/shard_map/ppermute | solution.py:526
  23.3 13.2 %collective-permute-start.5 = (bf16[192,1024]{1,0:T(8,128)(2,1)S(1)}, bf16[192,1024]{1,0:T(8,128)(2,1)S(1)}, u32[]{:S(2)}, u32[]{:S(2)}) collective-permute-start(bf16[192,1024]{1,0:T(8,128)(2,1)S(1)} %get-tuple-element.74), channel_id=1, source_target_pairs={{0,6},{2,4},{4,2},{6,0},{8,14},{10,12},{12,10},{14,8},{16,22},{18,... | collective-permute-start | bytes 1179656 | tf_op jit(solution)/shard_map/ppermute | solution.py:526
  28.5 9.4 %collective-permute-start.11 = (bf16[256,512]{1,0:T(8,128)(2,1)S(1)}, bf16[256,512]{1,0:T(8,128)(2,1)S(1)}, u32[]{:S(2)}, u32[]{:S(2)}) collective-permute-start(bf16[256,512]{1,0:T(8,128)(2,1)S(1)} %collective-permute-done.9.refs_2_), channel_id=1, source_target_pairs={{8,0},{10,2},{12,4},{14,6},{16,24},{18,26},{20,28},{22,30},{9,1},{... | collective-permute-start | bytes 786440 | tf_op jit(solution)/shard_map/ppermute | solution.py:551
  29.8 8.1 %collective-permute-start.12 = (bf16[256,512]{1,0:T(8,128)(2,1)S(1)}, bf16[256,512]{1,0:T(8,128)(2,1)S(1)}, u32[]{:S(2)}, u32[]{:S(2)}) collective-permute-start(bf16[256,512]{1,0:T(8,128)(2,1)S(1)} %get-tuple-element.85.refs_0_), channel_id=1, source_target_pairs={{8,16},{10,18},{12,20},{14,22},{16,8},{18,10},{20,12},{22,14},{9,1... | collective-permute-start | bytes 786440 | tf_op jit(solution)/shard_map/ppermute | solution.py:552
  37.0 7.0 %collective-permute-start.13 = (bf16[512,1024]{1,0:T(8,128)(2,1)S(1)}, bf16[512,1024]{1,0:T(8,128)(2,1)S(1)}, u32[]{:S(2)}, u32[]{:S(2)}) collective-permute-start(bf16[512,1024]{1,0:T(8,128)(2,1)S(1)} %get-tuple-element.92), channel_id=1, source_target_pairs={{0,1},{1,0},{2,3},{3,2},{4,5},{5,4},{6,7},{7,6},{8,9},{9,8},{10,11... | collective-permute-start | bytes 3145736 | tf_op jit(solution)/shard_map/ppermute | solution.py:532
  37.9 6.2 %copy-start.2 = (s32[8]{0:T(128)S(1)}, s32[8]{0:T(128)}, u32[]{:S(2)}) copy-start(s32[8]{0:T(128)} %len_ref.7) | copy-start | bytes 100
  37.9 15.4 %collective-permute-start.14 = (bf16[256,256]{1,0:T(8,128)(2,1)S(1)}, bf16[256,256]{1,0:T(8,128)(2,1)S(1)}, u32[]{:S(2)}, u32[]{:S(2)}) collective-permute-start(bf16[256,256]{1,0:T(8,128)(2,1)S(1)} %get-tuple-element.96.refs_0_), channel_id=1, source_target_pairs={{0,8},{2,10},{4,12},{6,14},{8,0},{10,2},{12,4},{14,6},{16,24},{18,... | collective-permute-start | bytes 393224 | tf_op jit(solution)/shard_map/ppermute | solution.py:535
  41.6 13.1 %collective-permute-start.15 = (bf16[256,256]{1,0:T(8,128)(2,1)S(1)}, bf16[256,256]{1,0:T(8,128)(2,1)S(1)}, u32[]{:S(2)}, u32[]{:S(2)}) collective-permute-start(bf16[256,256]{1,0:T(8,128)(2,1)S(1)} %get-tuple-element.96.refs_0_), channel_id=1, source_target_pairs={{0,16},{2,18},{4,20},{6,22},{8,24},{10,26},{12,28},{14,30},{16,0},... | collective-permute-start | bytes 393224 | tf_op jit(solution)/shard_map/ppermute | solution.py:535
  42.2 12.5 %collective-permute-start.16 = (bf16[256,256]{1,0:T(8,128)(2,1)S(1)}, bf16[256,256]{1,0:T(8,128)(2,1)S(1)}, u32[]{:S(2)}, u32[]{:S(2)}) collective-permute-start(bf16[256,256]{1,0:T(8,128)(2,1)S(1)} %get-tuple-element.96.refs_0_), channel_id=1, source_target_pairs={{0,24},{2,26},{4,28},{6,30},{8,16},{10,18},{12,20},{14,22},{16,8},... | collective-permute-start | bytes 393224 | tf_op jit(solution)/shard_map/ppermute | solution.py:535
  46.8 9.8 %copy-start.3 = (f32[1024]{0:T(1024)S(1)}, f32[1024]{0:T(1024)}, u32[]{:S(2)}) copy-start(f32[1024]{0:T(1024)} %param.14) | copy-start | bytes 12292
  46.8 10.6 %collective-permute-start.17 = (bf16[144,256]{1,0:T(8,128)(2,1)S(1)}, bf16[144,256]{1,0:T(8,128)(2,1)S(1)}, u32[]{:S(2)}, u32[]{:S(2)}) collective-permute-start(bf16[144,256]{1,0:T(8,128)(2,1)S(1)} %get-tuple-element.112), channel_id=1, source_target_pairs={{0,8},{2,10},{4,12},{6,14},{8,16},{10,18},{12,20},{14,22},{16,24},... | collective-permute-start | bytes 221192 | tf_op jit(solution)/shard_map/ppermute | solution.py:529
  49.9 7.6 %collective-permute-start.18 = (bf16[144,256]{1,0:T(8,128)(2,1)S(1)}, bf16[144,256]{1,0:T(8,128)(2,1)S(1)}, u32[]{:S(2)}, u32[]{:S(2)}) collective-permute-start(bf16[144,256]{1,0:T(8,128)(2,1)S(1)} %get-tuple-element.112), channel_id=1, source_target_pairs={{0,16},{2,18},{4,20},{6,22},{8,24},{10,26},{12,28},{14,30},{1,17},... | collective-permute-start | bytes 221192 | tf_op jit(solution)/shard_map/ppermute | solution.py:529
  53.3 4.2 %collective-permute-start.19 = (bf16[144,256]{1,0:T(8,128)(2,1)S(1)}, bf16[144,256]{1,0:T(8,128)(2,1)S(1)}, u32[]{:S(2)}, u32[]{:S(2)}) collective-permute-start(bf16[144,256]{1,0:T(8,128)(2,1)S(1)} %get-tuple-element.112), channel_id=1, source_target_pairs={{0,24},{2,26},{4,28},{6,30},{1,25},{3,27},{5,29},{7,31}} | collective-permute-start | bytes 221192 | tf_op jit(solution)/shard_map/ppermute | solution.py:529
  57.5 0.9 %copy-start.1 = (f32[31,1024]{1,0:T(8,128)S(1)}, f32[31,1024]{1,0:T(8,128)}, u32[]{:S(2)}) copy-start(f32[31,1024]{1,0:T(8,128)} %taps_ref.5) | copy-start | bytes 380932
  58.2 5.7 %collective-permute-start.21 = (bf16[512,256]{1,0:T(8,128)(2,1)S(1)}, bf16[512,256]{1,0:T(8,128)(2,1)S(1)}, u32[]{:S(2)}, u32[]{:S(2)}) collective-permute-start(bf16[512,256]{1,0:T(8,128)(2,1)S(1)} %get-tuple-element.116), channel_id=1, source_target_pairs={{0,1},{1,0},{2,3},{3,2},{4,5},{5,4},{6,7},{7,6},{8,9},{9,8},{10,11... | collective-permute-start | bytes 786440 | tf_op jit(solution)/shard_map/ppermute | solution.py:532
  60.3 3.6 %collective-permute-start.20 = (bf16[256,256]{1,0:T(8,128)(2,1)S(1)}, bf16[256,256]{1,0:T(8,128)(2,1)S(1)}, u32[]{:S(2)}, u32[]{:S(2)}) collective-permute-start(bf16[256,256]{1,0:T(8,128)(2,1)S(1)} %shard_map.101.refs_0_), channel_id=1, source_target_pairs={{0,1},{1,0},{2,3},{3,2},{4,5},{5,4},{6,7},{7,6},{8,9},{9,8},{10,11... | collective-permute-start | bytes 393224 | tf_op jit(solution)/shard_map/ppermute | solution.py:532
  64.2 2.7 %collective-permute-start.22 = (bf16[512,256]{1,0:T(8,128)(2,1)S(1)}, bf16[512,256]{1,0:T(8,128)(2,1)S(1)}, u32[]{:S(2)}, u32[]{:S(2)}) collective-permute-start(bf16[512,256]{1,0:T(8,128)(2,1)S(1)} %shard_map.102.refs_0_), channel_id=1, source_target_pairs={{0,1},{1,0},{2,3},{3,2},{4,5},{5,4},{6,7},{7,6},{8,9},{9,8},{10,11... | collective-permute-start | bytes 786440 | tf_op jit(solution)/shard_map/ppermute | solution.py:532
  64.4 10.1 %collective-permute-start.24 = (bf16[256,512]{1,0:T(8,128)(2,1)S(1)}, bf16[256,512]{1,0:T(8,128)(2,1)S(1)}, u32[]{:S(2)}, u32[]{:S(2)}) collective-permute-start(bf16[256,512]{1,0:T(8,128)(2,1)S(1)} %shard_map.103), channel_id=1, source_target_pairs={{0,6},{2,4},{4,2},{6,0},{8,14},{10,12},{12,10},{14,8},{16,22},{18,... | collective-permute-start | bytes 786440 | tf_op jit(solution)/shard_map/ppermute | solution.py:526
  67.4 12.4 %collective-permute-start.25 = (bf16[256,512]{1,0:T(8,128)(2,1)S(1)}, bf16[256,512]{1,0:T(8,128)(2,1)S(1)}, u32[]{:S(2)}, u32[]{:S(2)}) collective-permute-start(bf16[256,512]{1,0:T(8,128)(2,1)S(1)} %get-tuple-element.127), channel_id=1, source_target_pairs={{0,2},{2,0},{4,6},{6,4},{8,10},{10,8},{12,14},{14,12},{16,18},{18,... | collective-permute-start | bytes 786440 | tf_op jit(solution)/shard_map/ppermute | solution.py:526
  68.6 11.2 %collective-permute-start.26 = (bf16[256,512]{1,0:T(8,128)(2,1)S(1)}, bf16[256,512]{1,0:T(8,128)(2,1)S(1)}, u32[]{:S(2)}, u32[]{:S(2)}) collective-permute-start(bf16[256,512]{1,0:T(8,128)(2,1)S(1)} %get-tuple-element.128), channel_id=1, source_target_pairs={{0,4},{2,6},{4,0},{6,2},{8,12},{10,14},{12,8},{14,10},{16,20},{18,... | collective-permute-start | bytes 786440 | tf_op jit(solution)/shard_map/ppermute | solution.py:526
  71.7 2.8 %collective-permute-start.23 = (bf16[256,256]{1,0:T(8,128)(2,1)S(1)}, bf16[256,256]{1,0:T(8,128)(2,1)S(1)}, u32[]{:S(2)}, u32[]{:S(2)}) collective-permute-start(bf16[256,256]{1,0:T(8,128)(2,1)S(1)} %shard_map.105.refs_0_), channel_id=1, source_target_pairs={{0,1},{1,0},{2,3},{3,2},{4,5},{5,4},{6,7},{7,6},{8,9},{9,8},{10,11... | collective-permute-start | bytes 393224 | tf_op jit(solution)/shard_map/ppermute | solution.py:532

commit v17 on v16

--- a/solution.py
+++ b/solution.py
@@ -582,6 +582,7 @@
         flops=STACK_HINT,
         smem=0,
     )
+    xz_stack, pieces = lax.optimization_barrier((xz_stack, pieces))
     xz_pieces = along_planes([xz_stack] * planes)
     xz_pieces, out_stack = lax.optimization_barrier((xz_pieces, out_stack))
     out_pieces = [out_stack] + [between_planes(out_stack, step) for step in range(1, planes)]

time: 81.9 us -> 82.6 us (level)
  waiting for transfers between devices: 22.6 us -> 28.2 us
  starting transfers between devices: 38.1 us -> 33.4 us
    ppermute x8, waiting for transfers between devices: 7.41 us -> 12.2 us  [between_planes(): lax.ppermute(array, 'tm', [(i, i ^ step * group) for i in range(times)])]
    ppermute x8, starting transfers between devices: 15 us -> 11.7 us  [between_planes(): lax.ppermute(array, 'tm', [(i, i ^ step * group) for i in range(times)])]
    ppermute x9, starting transfers between devices: 12.6 us -> 11.7 us  [in_plane(): return lax.ppermute(array, 'tm', [(i, i ^ step) for i in range(times)])]
  transfers between devices with their start and end apart: 27 -> 27, of which waited for: 8 -> 10; matrix products, arithmetic and copies ran while one was open for 1% -> 1% of each run, Pallas kernels for 17% -> 18%
where the time goes in v17:
time: 82.6 us; the launch traced here: 82.4 us
  starting transfers between devices  33.4 us (40%)
  waiting for transfers between devices  28.2 us (34%)
  Pallas kernels  18.7 us (23%)
  local copies, waits for them, and re-layouts  1.78 us (2%)
    pallas_call x16, Pallas kernels, call(): pl.pallas_call(kernel, out_shape=out_shape, in_specs=in_specs, out_specs=...  18.7 us
    ppermute x9, waiting for transfers between devices, in_plane(): return lax.ppermute(array, 'tm', [(i, i ^ step) for i in range(times)])  14.7 us
    ppermute x8, waiting for transfers between devices, between_planes(): lax.ppermute(array, 'tm', [(i, i ^ step * group) for i in range(times)])  12.2 us
    ppermute x9, starting transfers between devices, in_plane(): return lax.ppermute(array, 'tm', [(i, i ^ step) for i in range(times)])  11.7 us
    ppermute x8, starting transfers between devices, between_planes(): lax.ppermute(array, 'tm', [(i, i ^ step * group) for i in range(times)])  11.7 us
    ppermute x3, starting transfers between devices, later(): lax.ppermute(array, 'tm', [(i, i + step * group) for i in range(times - s...  7.14 us
  transfers between devices with their start and end apart: 27, of which 10 were waited for; matrix products, arithmetic and copies ran while one was open for 1% of the time, Pallas kernels for 18%

profile of v17, /device:TPU:0, one launch (start us, length us, event | category | flops | bytes accessed | tf_op | source)
XLA Modules:
  0.0 82.4 jit_solution(15628180305652390771)
XLA Ops:
  0.0 2.0 %shard_map.91 = (bf16[64,768]{1,0:T(8,128)(2,1)}, bf16[64,768]{1,0:T(8,128)(2,1)}, bf16[64,768]{1,0:T(8,128)(2,1)}, bf16[64,768]{1,0:T(8,128)(2,1)}, bf16[32,102...) custom-call(f32[16,256]{1,0:T(8,128)} %log_decay_ref.1, ...), custom_call_target="tpu_custom_call" | custom-call | bytes 1622016 | tf_op jit(solution)/shard_map/pallas_call | solution.py:35
  2.0 3.0 %collective-permute-start = (bf16[64,768]{1,0:T(8,128)(2,1)}, bf16[64,768]{1,0:T(8,128)(2,1)S(1)}, u32[]{:S(2)}, u32[]{:S(2)}) collective-permute-start(bf16[64,768]{1,0:T(8,128)(2,1)} %get-tuple-element.73), channel_id=1, source_target_pairs={{0,2},{2,0},{4,6},{6,4},{8,10},{10,8},{12,14},{14,12},{16,18},{18,... | collective-permute-start | bytes 294920 | tf_op jit(solution)/shard_map/ppermute | solution.py:526
  5.0 1.5 %collective-permute-start.1 = (bf16[64,768]{1,0:T(8,128)(2,1)}, bf16[64,768]{1,0:T(8,128)(2,1)S(1)}, u32[]{:S(2)}, u32[]{:S(2)}) collective-permute-start(bf16[64,768]{1,0:T(8,128)(2,1)} %get-tuple-element.74), channel_id=1, source_target_pairs={{0,4},{2,6},{4,0},{6,2},{8,12},{10,14},{12,8},{14,10},{16,20},{18,... | collective-permute-start | bytes 294920 | tf_op jit(solution)/shard_map/ppermute | solution.py:526
  6.5 2.0 %collective-permute-start.3 = (bf16[32,1024]{1,0:T(8,128)(2,1)}, bf16[32,1024]{1,0:T(8,128)(2,1)S(1)}, u32[]{:S(2)}, u32[]{:S(2)}) collective-permute-start(bf16[32,1024]{1,0:T(8,128)(2,1)} %get-tuple-element.78), channel_id=1, source_target_pairs={{0,8},{2,10},{4,12},{6,14},{8,0},{10,2},{12,4},{14,6},{16,24},{18,... | collective-permute-start | bytes 196616 | tf_op jit(solution)/shard_map/ppermute | solution.py:535
  8.5 2.6 %collective-permute-start.4 = (bf16[32,1024]{1,0:T(8,128)(2,1)}, bf16[32,1024]{1,0:T(8,128)(2,1)S(1)}, u32[]{:S(2)}, u32[]{:S(2)}) collective-permute-start(bf16[32,1024]{1,0:T(8,128)(2,1)} %get-tuple-element.79), channel_id=1, source_target_pairs={{0,16},{2,18},{4,20},{6,22},{8,24},{10,26},{12,28},{14,30},{16,0},... | collective-permute-start | bytes 196616 | tf_op jit(solution)/shard_map/ppermute | solution.py:535
  11.1 0.7 reshape.3
  12.0 0.2 collective-permute-done.2.refs_3_
  12.2 0.9 %copy-done.4 = bf16[64,768]{1,0:T(8,128)(2,1)S(1)} copy-done((bf16[64,768]{1,0:T(8,128)(2,1)S(1)}, bf16[64,768]{1,0:T(8,128)(2,1)}, u32[]{:S(2)}) %copy-start.4) | copy-done | bytes 98328
  13.2 2.7 %collective-permute-done.4.refs_2_ = bf16[32,1024]{1,0:T(8,128)(2,1)S(1)} collective-permute-done((bf16[32,1024]{1,0:T(8,128)(2,1)}, bf16[32,1024]{1,0:T(8,128)(2,1)S(1)}, u32[]{:S(2)}, u32[]{:S(2)}) %collective-permute-start.4) | collective-permute-done | bytes 65568 | tf_op jit(solution)/shard_map/ppermute | solution.py:535
  15.9 2.3 %collective-permute-done.5.refs_3_ = bf16[32,1024]{1,0:T(8,128)(2,1)S(1)} collective-permute-done((bf16[32,1024]{1,0:T(8,128)(2,1)}, bf16[32,1024]{1,0:T(8,128)(2,1)S(1)}, u32[]{:S(2)}, u32[]{:S(2)}) %collective-permute-start.5) | collective-permute-done | bytes 65568 | tf_op jit(solution)/shard_map/ppermute | solution.py:535
  18.2 0.2 collective-permute-start.9
  18.4 0.8 collective-permute-start.10
  19.2 0.2 shard_map.93
  19.4 2.0 %collective-permute-start.6 = (bf16[192,1024]{1,0:T(8,128)(2,1)S(1)}, bf16[192,1024]{1,0:T(8,128)(2,1)S(1)}, u32[]{:S(2)}, u32[]{:S(2)}) collective-permute-start(bf16[192,1024]{1,0:T(8,128)(2,1)S(1)} %get-tuple-element.86), channel_id=1, source_target_pairs={{0,2},{2,0},{4,6},{6,4},{8,10},{10,8},{12,14},{14,12},{16,18},{18,... | collective-permute-start | bytes 1179656 | tf_op jit(solution)/shard_map/ppermute | solution.py:526
  21.3 1.5 %collective-permute-start.7 = (bf16[192,1024]{1,0:T(8,128)(2,1)S(1)}, bf16[192,1024]{1,0:T(8,128)(2,1)S(1)}, u32[]{:S(2)}, u32[]{:S(2)}) collective-permute-start(bf16[192,1024]{1,0:T(8,128)(2,1)S(1)} %get-tuple-element.87), channel_id=1, source_target_pairs={{0,4},{2,6},{4,0},{6,2},{8,12},{10,14},{12,8},{14,10},{16,20},{18,... | collective-permute-start | bytes 1179656 | tf_op jit(solution)/shard_map/ppermute | solution.py:526
  22.9 6.8 %collective-permute-done.9.refs_2_ = bf16[256,512]{1,0:T(8,128)(2,1)S(1)} collective-permute-done((bf16[256,512]{1,0:T(8,128)(2,1)S(1)}, bf16[256,512]{1,0:T(8,128)(2,1)S(1)}, u32[]{:S(2)}, u32[]{:S(2)}) %collective-permute-start.9) | collective-permute-done | bytes 262176 | tf_op jit(solution)/shard_map/ppermute | solution.py:535
  29.7 0.3 collective-permute-done.10.refs_1_
  30.0 1.3 %collective-permute-start.11 = (bf16[256,512]{1,0:T(8,128)(2,1)S(1)}, bf16[256,512]{1,0:T(8,128)(2,1)S(1)}, u32[]{:S(2)}, u32[]{:S(2)}) collective-permute-start(bf16[256,512]{1,0:T(8,128)(2,1)S(1)} %collective-permute-done.9.refs_2_), channel_id=1, source_target_pairs={{8,0},{10,2},{12,4},{14,6},{16,24},{18,26},{20,28},{22,30},{9,1},{... | collective-permute-start | bytes 786440 | tf_op jit(solution)/shard_map/ppermute | solution.py:551
  31.3 0.7 collective-permute-start.12
  32.0 5.2 %collective-permute-done.7.refs_2_.refs_1_ = bf16[192,1024]{1,0:T(8,128)(2,1)S(1)} collective-permute-done((bf16[192,1024]{1,0:T(8,128)(2,1)S(1)}, bf16[192,1024]{1,0:T(8,128)(2,1)S(1)}, u32[]{:S(2)}, u32[]{:S(2)}) %collective-permute-start.7) | collective-permute-done | bytes 393248 | tf_op jit(solution)/shard_map/ppermute | solution.py:526
  37.2 0.5 shard_map.94
  37.8 1.3 %collective-permute-done.11.refs_3_ = bf16[256,512]{1,0:T(8,128)(2,1)S(1)} collective-permute-done((bf16[256,512]{1,0:T(8,128)(2,1)S(1)}, bf16[256,512]{1,0:T(8,128)(2,1)S(1)}, u32[]{:S(2)}, u32[]{:S(2)}) %collective-permute-start.11) | collective-permute-done | bytes 262176 | tf_op jit(solution)/shard_map/ppermute | solution.py:551
  39.0 3.7 %collective-permute-start.14 = (bf16[256,256]{1,0:T(8,128)(2,1)S(1)}, bf16[256,256]{1,0:T(8,128)(2,1)S(1)}, u32[]{:S(2)}, u32[]{:S(2)}) collective-permute-start(bf16[256,256]{1,0:T(8,128)(2,1)S(1)} %get-tuple-element.106.refs_0_), channel_id=1, source_target_pairs={{0,8},{2,10},{4,12},{6,14},{8,0},{10,2},{12,4},{14,6},{16,24},{18,... | collective-permute-start | bytes 393224 | tf_op jit(solution)/shard_map/ppermute | solution.py:535
  42.7 2.4 %collective-permute-start.16 = (bf16[256,256]{1,0:T(8,128)(2,1)S(1)}, bf16[256,256]{1,0:T(8,128)(2,1)S(1)}, u32[]{:S(2)}, u32[]{:S(2)}) collective-permute-start(bf16[256,256]{1,0:T(8,128)(2,1)S(1)} %get-tuple-element.106.refs_0_), channel_id=1, source_target_pairs={{0,24},{2,26},{4,28},{6,30},{8,16},{10,18},{12,20},{14,22},{16,8},... | collective-permute-start | bytes 393224 | tf_op jit(solution)/shard_map/ppermute | solution.py:535
  45.1 0.1 shard_map.95
  45.2 2.8 %shard_map.96 = (bf16[1152,1024]{1,0:T(8,128)(2,1)S(1)}, bf16[1152,256]{1,0:T(8,128)(2,1)S(1)}, bf16[1152,128]{1,0:T(8,128)(2,1)S(1)}, bf16[1152,128]{1,0:T(8,12...) custom-call(s32[8]{0:T(128)S(1)} %copy-done.2, ...), custom_call_target="tpu_custom_call" | custom-call | tf_op jit(solution)/shard_map/pallas_call | solution.py:35
  48.0 3.0 %collective-permute-start.17 = (bf16[144,256]{1,0:T(8,128)(2,1)S(1)}, bf16[144,256]{1,0:T(8,128)(2,1)S(1)}, u32[]{:S(2)}, u32[]{:S(2)}) collective-permute-start(bf16[144,256]{1,0:T(8,128)(2,1)S(1)} %get-tuple-element.122), channel_id=1, source_target_pairs={{0,8},{2,10},{4,12},{6,14},{8,16},{10,18},{12,20},{14,22},{16,24},... | collective-permute-start | bytes 221192 | tf_op jit(solution)/shard_map/ppermute | solution.py:529
  51.0 2.8 %collective-permute-start.18 = (bf16[144,256]{1,0:T(8,128)(2,1)S(1)}, bf16[144,256]{1,0:T(8,128)(2,1)S(1)}, u32[]{:S(2)}, u32[]{:S(2)}) collective-permute-start(bf16[144,256]{1,0:T(8,128)(2,1)S(1)} %get-tuple-element.122), channel_id=1, source_target_pairs={{0,16},{2,18},{4,20},{6,22},{8,24},{10,26},{12,28},{14,30},{1,17},... | collective-permute-start | bytes 221192 | tf_op jit(solution)/shard_map/ppermute | solution.py:529
  53.9 1.3 %collective-permute-start.19 = (bf16[144,256]{1,0:T(8,128)(2,1)S(1)}, bf16[144,256]{1,0:T(8,128)(2,1)S(1)}, u32[]{:S(2)}, u32[]{:S(2)}) collective-permute-start(bf16[144,256]{1,0:T(8,128)(2,1)S(1)} %get-tuple-element.122), channel_id=1, source_target_pairs={{0,24},{2,26},{4,28},{6,30},{1,25},{3,27},{5,29},{7,31}} | collective-permute-start | bytes 221192 | tf_op jit(solution)/shard_map/ppermute | solution.py:529
  55.2 0.1 shard_map.97
  55.3 1.9 %shard_map.98 = (f32[1152,256]{1,0:T(8,128)S(1)}, f32[1152,256]{1,0:T(8,128)S(1)}) custom-call(bf16[1152,256]{1,0:T(8,128)(2,1)S(1)} %get-tuple-element.113.x_ref, bf16[1152,128]{1,0:T(8,128)(2,1)S(1)} %get-tuple-element.114.b_ref, bf16[1152,128]{1,0:T(8,128)(2,1)S(1)} %get-tuple-element.112.c_ref, f32[216,128]{1,0:T(8,128)S(1)} %get-tuple-element.115.rows_ref), custom_call_target="tpu_custom_call" | custom-call | flops 134217728 | bytes 3649536 | tf_op jit(solution)/shard_map/pallas_call | solution.py:35
  57.2 0.8 %shard_map.99.silu_ref = f32[1152,256]{1,0:T(8,128)S(1)} custom-call(f32[1,1024]{1,0:T(1,128)S(1)} %bitcast.2, bf16[1152,1024]{1,0:T(8,128)(2,1)S(1)} %get-tuple-element.120.frames_ref, bf16[1024,256]{1,0:T(8,128)(2,1)S(1)} %get-tuple-element.121.weight_ref), custom_call_target="tpu_custom_call" | custom-call | flops 536870912 | bytes 4067328 | tf_op jit(solution)/shard_map/pallas_call | solution.py:35
  58.1 0.7 shard_map.100.gated_ref
  58.8 0.1 copy-done.1
  59.0 2.5 %shard_map.101.refs_0_ = bf16[256,256]{1,0:T(8,128)(2,1)S(1)} custom-call(s32[8]{0:T(128)S(1)} %copy-done.2, f32[31,1024]{1,0:T(8,128)S(1)} %copy-done.1, bf16[1152,256]{1,0:T(8,128)(2,1)S(1)} %shard_map.100.gated_ref), custom_call_target="tpu_custom_call" | custom-call | flops 4063232 | bytes 847904 | tf_op jit(solution)/shard_map/pallas_call | solution.py:35
  61.4 0.4 collective-permute-start.20
  61.9 3.8 %shard_map.102.refs_0_ = bf16[512,256]{1,0:T(8,128)(2,1)S(1)} custom-call(s32[8]{0:T(128)S(1)} %copy-done.2, f32[31,1024]{1,0:T(8,128)S(1)} %copy-done.1, bf16[1152,256]{1,0:T(8,128)(2,1)S(1)} %shard_map.100.gated_ref), custom_call_target="tpu_custom_call" | custom-call | flops 8126464 | bytes 978976 | tf_op jit(solution)/shard_map/pallas_call | solution.py:35
  65.7 0.3 shard_map.103
  66.0 0.2 collective-permute-start.22
  66.2 1.6 %collective-permute-start.24 = (bf16[256,512]{1,0:T(8,128)(2,1)S(1)}, bf16[256,512]{1,0:T(8,128)(2,1)S(1)}, u32[]{:S(2)}, u32[]{:S(2)}) collective-permute-start(bf16[256,512]{1,0:T(8,128)(2,1)S(1)} %shard_map.103), channel_id=1, source_target_pairs={{0,6},{2,4},{4,2},{6,0},{8,14},{10,12},{12,10},{14,8},{16,22},{18,... | collective-permute-start | bytes 786440 | tf_op jit(solution)/shard_map/ppermute | solution.py:526
  67.9 0.5 shard_map.104
  68.3 1.0 %collective-permute-start.25 = (bf16[256,512]{1,0:T(8,128)(2,1)S(1)}, bf16[256,512]{1,0:T(8,128)(2,1)S(1)}, u32[]{:S(2)}, u32[]{:S(2)}) collective-permute-start(bf16[256,512]{1,0:T(8,128)(2,1)S(1)} %get-tuple-element.137), channel_id=1, source_target_pairs={{0,2},{2,0},{4,6},{6,4},{8,10},{10,8},{12,14},{14,12},{16,18},{18,... | collective-permute-start | bytes 786440 | tf_op jit(solution)/shard_map/ppermute | solution.py:526
  69.3 1.0 %collective-permute-start.26 = (bf16[256,512]{1,0:T(8,128)(2,1)S(1)}, bf16[256,512]{1,0:T(8,128)(2,1)S(1)}, u32[]{:S(2)}, u32[]{:S(2)}) collective-permute-start(bf16[256,512]{1,0:T(8,128)(2,1)S(1)} %get-tuple-element.138), channel_id=1, source_target_pairs={{0,4},{2,6},{4,0},{6,2},{8,12},{10,14},{12,8},{14,10},{16,20},{18,... | collective-permute-start | bytes 786440 | tf_op jit(solution)/shard_map/ppermute | solution.py:526
  70.3 1.6 %shard_map.105.refs_0_ = bf16[256,256]{1,0:T(8,128)(2,1)S(1)} custom-call(s32[8]{0:T(128)S(1)} %copy-done.2, f32[31,1024]{1,0:T(8,128)S(1)} %copy-done.1, bf16[1152,256]{1,0:T(8,128)(2,1)S(1)} %shard_map.100.gated_ref), custom_call_target="tpu_custom_call" | custom-call | flops 4063232 | bytes 847904 | tf_op jit(solution)/shard_map/pallas_call | solution.py:35
  72.1 4.2 %collective-permute-done.24.refs_4_ = bf16[256,512]{1,0:T(8,128)(2,1)S(1)} collective-permute-done((bf16[256,512]{1,0:T(8,128)(2,1)S(1)}, bf16[256,512]{1,0:T(8,128)(2,1)S(1)}, u32[]{:S(2)}, u32[]{:S(2)}) %collective-permute-start.24) | collective-permute-done | bytes 262176 | tf_op jit(solution)/shard_map/ppermute | solution.py:526
  76.3 4.7 %collective-permute-done.25.refs_5_ = bf16[256,512]{1,0:T(8,128)(2,1)S(1)} collective-permute-done((bf16[256,512]{1,0:T(8,128)(2,1)S(1)}, bf16[256,512]{1,0:T(8,128)(2,1)S(1)}, u32[]{:S(2)}, u32[]{:S(2)}) %collective-permute-start.25) | collective-permute-done | bytes 262176 | tf_op jit(solution)/shard_map/ppermute | solution.py:526
  81.0 0.3 collective-permute-done.26.refs_6_
  81.3 1.1 %shard_map.106 = bf16[256,512]{1,0:T(8,128)(2,1)} custom-call(bf16[256,256]{1,0:T(8,128)(2,1)S(1)} %shard_map.105.refs_0_, bf16[256,256]{1,0:T(8,128)(2,1)S(1)} %collective-permute-done.23.refs_1_, bf16[512,256]{1,0:T(8,128)(2,1)S(1)} %get-tuple-element.130.refs_2_, bf16[512,256]{1,0:T(8,128)(2,1)S(1)} %collective-permute-done.21.refs_3_, ...), custom_call_target="tpu_custom_call" | custom-call | flops 134217728 | bytes 1835008 | tf_op jit(solution)/shard_map/pallas_call | solution.py:35
  (36 shorter events, 0.5 us)
Async XLA Ops:
  2.0 9.9 %collective-permute-start = (bf16[64,768]{1,0:T(8,128)(2,1)}, bf16[64,768]{1,0:T(8,128)(2,1)S(1)}, u32[]{:S(2)}, u32[]{:S(2)}) collective-permute-start(bf16[64,768]{1,0:T(8,128)(2,1)} %get-tuple-element.73), channel_id=1, source_target_pairs={{0,2},{2,0},{4,6},{6,4},{8,10},{10,8},{12,14},{14,12},{16,18},{18,... | collective-permute-start | bytes 294920 | tf_op jit(solution)/shard_map/ppermute | solution.py:526
  5.0 7.0 %collective-permute-start.1 = (bf16[64,768]{1,0:T(8,128)(2,1)}, bf16[64,768]{1,0:T(8,128)(2,1)S(1)}, u32[]{:S(2)}, u32[]{:S(2)}) collective-permute-start(bf16[64,768]{1,0:T(8,128)(2,1)} %get-tuple-element.74), channel_id=1, source_target_pairs={{0,4},{2,6},{4,0},{6,2},{8,12},{10,14},{12,8},{14,10},{16,20},{18,... | collective-permute-start | bytes 294920 | tf_op jit(solution)/shard_map/ppermute | solution.py:526
  6.5 5.7 %collective-permute-start.2 = (bf16[64,768]{1,0:T(8,128)(2,1)}, bf16[64,768]{1,0:T(8,128)(2,1)S(1)}, u32[]{:S(2)}, u32[]{:S(2)}) collective-permute-start(bf16[64,768]{1,0:T(8,128)(2,1)} %get-tuple-element.75), channel_id=1, source_target_pairs={{0,6},{2,4},{4,2},{6,0},{8,14},{10,12},{12,10},{14,8},{16,22},{18,... | collective-permute-start | bytes 294920 | tf_op jit(solution)/shard_map/ppermute | solution.py:526
  6.5 6.6 %collective-permute-start.3 = (bf16[32,1024]{1,0:T(8,128)(2,1)}, bf16[32,1024]{1,0:T(8,128)(2,1)S(1)}, u32[]{:S(2)}, u32[]{:S(2)}) collective-permute-start(bf16[32,1024]{1,0:T(8,128)(2,1)} %get-tuple-element.78), channel_id=1, source_target_pairs={{0,8},{2,10},{4,12},{6,14},{8,0},{10,2},{12,4},{14,6},{16,24},{18,... | collective-permute-start | bytes 196616 | tf_op jit(solution)/shard_map/ppermute | solution.py:535
  8.5 7.3 %collective-permute-start.4 = (bf16[32,1024]{1,0:T(8,128)(2,1)}, bf16[32,1024]{1,0:T(8,128)(2,1)S(1)}, u32[]{:S(2)}, u32[]{:S(2)}) collective-permute-start(bf16[32,1024]{1,0:T(8,128)(2,1)} %get-tuple-element.79), channel_id=1, source_target_pairs={{0,16},{2,18},{4,20},{6,22},{8,24},{10,26},{12,28},{14,30},{16,0},... | collective-permute-start | bytes 196616 | tf_op jit(solution)/shard_map/ppermute | solution.py:535
  11.9 6.3 %collective-permute-start.5 = (bf16[32,1024]{1,0:T(8,128)(2,1)}, bf16[32,1024]{1,0:T(8,128)(2,1)S(1)}, u32[]{:S(2)}, u32[]{:S(2)}) collective-permute-start(bf16[32,1024]{1,0:T(8,128)(2,1)} %get-tuple-element.80), channel_id=1, source_target_pairs={{0,24},{2,26},{4,28},{6,30},{8,16},{10,18},{12,20},{14,22},{16,8},... | collective-permute-start | bytes 196616 | tf_op jit(solution)/shard_map/ppermute | solution.py:535
  12.2 0.9 %copy-start.4 = (bf16[64,768]{1,0:T(8,128)(2,1)S(1)}, bf16[64,768]{1,0:T(8,128)(2,1)}, u32[]{:S(2)}) copy-start(bf16[64,768]{1,0:T(8,128)(2,1)} %get-tuple-element.72.refs_0_) | copy-start | bytes 294916
  13.1 6.1 %copy-start = (bf16[256,1024]{1,0:T(8,128)(2,1)S(1)}, bf16[256,1024]{1,0:T(8,128)(2,1)}, u32[]{:S(2)}) copy-start(bf16[256,1024]{1,0:T(8,128)(2,1)} %own_ref.1) | copy-start | bytes 1572868
  13.1 6.1 %copy-start.5 = (bf16[32,1024]{1,0:T(8,128)(2,1)S(1)}, bf16[32,1024]{1,0:T(8,128)(2,1)}, u32[]{:S(2)}) copy-start(bf16[32,1024]{1,0:T(8,128)(2,1)} %get-tuple-element.81.refs_0_) | copy-start | bytes 196612
  18.2 11.5 %collective-permute-start.9 = (bf16[256,512]{1,0:T(8,128)(2,1)S(1)}, bf16[256,512]{1,0:T(8,128)(2,1)S(1)}, u32[]{:S(2)}, u32[]{:S(2)}) collective-permute-start(bf16[256,512]{1,0:T(8,128)(2,1)S(1)} %get-tuple-element.95.refs_0_), channel_id=1, source_target_pairs={{0,16},{2,18},{4,20},{6,22},{8,24},{10,26},{12,28},{14,30},{16,0},... | collective-permute-start | bytes 786440 | tf_op jit(solution)/shard_map/ppermute | solution.py:535
  18.4 11.6 %collective-permute-start.10 = (bf16[256,512]{1,0:T(8,128)(2,1)S(1)}, bf16[256,512]{1,0:T(8,128)(2,1)S(1)}, u32[]{:S(2)}, u32[]{:S(2)}) collective-permute-start(bf16[256,512]{1,0:T(8,128)(2,1)S(1)} %get-tuple-element.95.refs_0_), channel_id=1, source_target_pairs={{0,8},{2,10},{4,12},{6,14},{8,0},{10,2},{12,4},{14,6},{16,24},{18,... | collective-permute-start | bytes 786440 | tf_op jit(solution)/shard_map/ppermute | solution.py:535
  19.4 12.6 %collective-permute-start.6 = (bf16[192,1024]{1,0:T(8,128)(2,1)S(1)}, bf16[192,1024]{1,0:T(8,128)(2,1)S(1)}, u32[]{:S(2)}, u32[]{:S(2)}) collective-permute-start(bf16[192,1024]{1,0:T(8,128)(2,1)S(1)} %get-tuple-element.86), channel_id=1, source_target_pairs={{0,2},{2,0},{4,6},{6,4},{8,10},{10,8},{12,14},{14,12},{16,18},{18,... | collective-permute-start | bytes 1179656 | tf_op jit(solution)/shard_map/ppermute | solution.py:526
  21.3 15.9 %collective-permute-start.7 = (bf16[192,1024]{1,0:T(8,128)(2,1)S(1)}, bf16[192,1024]{1,0:T(8,128)(2,1)S(1)}, u32[]{:S(2)}, u32[]{:S(2)}) collective-permute-start(bf16[192,1024]{1,0:T(8,128)(2,1)S(1)} %get-tuple-element.87), channel_id=1, source_target_pairs={{0,4},{2,6},{4,0},{6,2},{8,12},{10,14},{12,8},{14,10},{16,20},{18,... | collective-permute-start | bytes 1179656 | tf_op jit(solution)/shard_map/ppermute | solution.py:526
  22.8 14.4 %collective-permute-start.8 = (bf16[192,1024]{1,0:T(8,128)(2,1)S(1)}, bf16[192,1024]{1,0:T(8,128)(2,1)S(1)}, u32[]{:S(2)}, u32[]{:S(2)}) collective-permute-start(bf16[192,1024]{1,0:T(8,128)(2,1)S(1)} %get-tuple-element.88), channel_id=1, source_target_pairs={{0,6},{2,4},{4,2},{6,0},{8,14},{10,12},{12,10},{14,8},{16,22},{18,... | collective-permute-start | bytes 1179656 | tf_op jit(solution)/shard_map/ppermute | solution.py:526
  30.0 9.0 %collective-permute-start.11 = (bf16[256,512]{1,0:T(8,128)(2,1)S(1)}, bf16[256,512]{1,0:T(8,128)(2,1)S(1)}, u32[]{:S(2)}, u32[]{:S(2)}) collective-permute-start(bf16[256,512]{1,0:T(8,128)(2,1)S(1)} %collective-permute-done.9.refs_2_), channel_id=1, source_target_pairs={{8,0},{10,2},{12,4},{14,6},{16,24},{18,26},{20,28},{22,30},{9,1},{... | collective-permute-start | bytes 786440 | tf_op jit(solution)/shard_map/ppermute | solution.py:551
  31.3 7.7 %collective-permute-start.12 = (bf16[256,512]{1,0:T(8,128)(2,1)S(1)}, bf16[256,512]{1,0:T(8,128)(2,1)S(1)}, u32[]{:S(2)}, u32[]{:S(2)}) collective-permute-start(bf16[256,512]{1,0:T(8,128)(2,1)S(1)} %get-tuple-element.95.refs_0_), channel_id=1, source_target_pairs={{8,16},{10,18},{12,20},{14,22},{16,8},{18,10},{20,12},{22,14},{9,1... | collective-permute-start | bytes 786440 | tf_op jit(solution)/shard_map/ppermute | solution.py:552
  37.7 7.5 %collective-permute-start.13 = (bf16[512,1024]{1,0:T(8,128)(2,1)S(1)}, bf16[512,1024]{1,0:T(8,128)(2,1)S(1)}, u32[]{:S(2)}, u32[]{:S(2)}) collective-permute-start(bf16[512,1024]{1,0:T(8,128)(2,1)S(1)} %get-tuple-element.102), channel_id=1, source_target_pairs={{0,1},{1,0},{2,3},{3,2},{4,5},{5,4},{6,7},{7,6},{8,9},{9,8},{10,11... | collective-permute-start | bytes 3145736 | tf_op jit(solution)/shard_map/ppermute | solution.py:532
  39.0 6.2 %copy-start.2 = (s32[8]{0:T(128)S(1)}, s32[8]{0:T(128)}, u32[]{:S(2)}) copy-start(s32[8]{0:T(128)} %len_ref.7) | copy-start | bytes 100
  39.0 14.8 %collective-permute-start.14 = (bf16[256,256]{1,0:T(8,128)(2,1)S(1)}, bf16[256,256]{1,0:T(8,128)(2,1)S(1)}, u32[]{:S(2)}, u32[]{:S(2)}) collective-permute-start(bf16[256,256]{1,0:T(8,128)(2,1)S(1)} %get-tuple-element.106.refs_0_), channel_id=1, source_target_pairs={{0,8},{2,10},{4,12},{6,14},{8,0},{10,2},{12,4},{14,6},{16,24},{18,... | collective-permute-start | bytes 393224 | tf_op jit(solution)/shard_map/ppermute | solution.py:535
  42.7 12.5 %collective-permute-start.15 = (bf16[256,256]{1,0:T(8,128)(2,1)S(1)}, bf16[256,256]{1,0:T(8,128)(2,1)S(1)}, u32[]{:S(2)}, u32[]{:S(2)}) collective-permute-start(bf16[256,256]{1,0:T(8,128)(2,1)S(1)} %get-tuple-element.106.refs_0_), channel_id=1, source_target_pairs={{0,16},{2,18},{4,20},{6,22},{8,24},{10,26},{12,28},{14,30},{16,0},... | collective-permute-start | bytes 393224 | tf_op jit(solution)/shard_map/ppermute | solution.py:535
  42.7 12.5 %collective-permute-start.16 = (bf16[256,256]{1,0:T(8,128)(2,1)S(1)}, bf16[256,256]{1,0:T(8,128)(2,1)S(1)}, u32[]{:S(2)}, u32[]{:S(2)}) collective-permute-start(bf16[256,256]{1,0:T(8,128)(2,1)S(1)} %get-tuple-element.106.refs_0_), channel_id=1, source_target_pairs={{0,24},{2,26},{4,28},{6,30},{8,16},{10,18},{12,20},{14,22},{16,8},... | collective-permute-start | bytes 393224 | tf_op jit(solution)/shard_map/ppermute | solution.py:535
  48.0 9.2 %copy-start.3 = (f32[1024]{0:T(1024)S(1)}, f32[1024]{0:T(1024)}, u32[]{:S(2)}) copy-start(f32[1024]{0:T(1024)} %param.14) | copy-start | bytes 12292
  48.0 10.0 %collective-permute-start.17 = (bf16[144,256]{1,0:T(8,128)(2,1)S(1)}, bf16[144,256]{1,0:T(8,128)(2,1)S(1)}, u32[]{:S(2)}, u32[]{:S(2)}) collective-permute-start(bf16[144,256]{1,0:T(8,128)(2,1)S(1)} %get-tuple-element.122), channel_id=1, source_target_pairs={{0,8},{2,10},{4,12},{6,14},{8,16},{10,18},{12,20},{14,22},{16,24},... | collective-permute-start | bytes 221192 | tf_op jit(solution)/shard_map/ppermute | solution.py:529
  51.0 7.0 %collective-permute-start.18 = (bf16[144,256]{1,0:T(8,128)(2,1)S(1)}, bf16[144,256]{1,0:T(8,128)(2,1)S(1)}, u32[]{:S(2)}, u32[]{:S(2)}) collective-permute-start(bf16[144,256]{1,0:T(8,128)(2,1)S(1)} %get-tuple-element.122), channel_id=1, source_target_pairs={{0,16},{2,18},{4,20},{6,22},{8,24},{10,26},{12,28},{14,30},{1,17},... | collective-permute-start | bytes 221192 | tf_op jit(solution)/shard_map/ppermute | solution.py:529
  53.9 4.2 %collective-permute-start.19 = (bf16[144,256]{1,0:T(8,128)(2,1)S(1)}, bf16[144,256]{1,0:T(8,128)(2,1)S(1)}, u32[]{:S(2)}, u32[]{:S(2)}) collective-permute-start(bf16[144,256]{1,0:T(8,128)(2,1)S(1)} %get-tuple-element.122), channel_id=1, source_target_pairs={{0,24},{2,26},{4,28},{6,30},{1,25},{3,27},{5,29},{7,31}} | collective-permute-start | bytes 221192 | tf_op jit(solution)/shard_map/ppermute | solution.py:529
  58.1 0.9 %copy-start.1 = (f32[31,1024]{1,0:T(8,128)S(1)}, f32[31,1024]{1,0:T(8,128)}, u32[]{:S(2)}) copy-start(f32[31,1024]{1,0:T(8,128)} %taps_ref.5) | copy-start | bytes 380932
  58.8 6.9 %collective-permute-start.21 = (bf16[512,256]{1,0:T(8,128)(2,1)S(1)}, bf16[512,256]{1,0:T(8,128)(2,1)S(1)}, u32[]{:S(2)}, u32[]{:S(2)}) collective-permute-start(bf16[512,256]{1,0:T(8,128)(2,1)S(1)} %get-tuple-element.126), channel_id=1, source_target_pairs={{0,1},{1,0},{2,3},{3,2},{4,5},{5,4},{6,7},{7,6},{8,9},{9,8},{10,11... | collective-permute-start | bytes 786440 | tf_op jit(solution)/shard_map/ppermute | solution.py:532
  61.4 4.2 %collective-permute-start.20 = (bf16[256,256]{1,0:T(8,128)(2,1)S(1)}, bf16[256,256]{1,0:T(8,128)(2,1)S(1)}, u32[]{:S(2)}, u32[]{:S(2)}) collective-permute-start(bf16[256,256]{1,0:T(8,128)(2,1)S(1)} %shard_map.101.refs_0_), channel_id=1, source_target_pairs={{0,1},{1,0},{2,3},{3,2},{4,5},{5,4},{6,7},{7,6},{8,9},{9,8},{10,11... | collective-permute-start | bytes 393224 | tf_op jit(solution)/shard_map/ppermute | solution.py:532
  66.0 1.9 %collective-permute-start.22 = (bf16[512,256]{1,0:T(8,128)(2,1)S(1)}, bf16[512,256]{1,0:T(8,128)(2,1)S(1)}, u32[]{:S(2)}, u32[]{:S(2)}) collective-permute-start(bf16[512,256]{1,0:T(8,128)(2,1)S(1)} %shard_map.102.refs_0_), channel_id=1, source_target_pairs={{0,1},{1,0},{2,3},{3,2},{4,5},{5,4},{6,7},{7,6},{8,9},{9,8},{10,11... | collective-permute-start | bytes 786440 | tf_op jit(solution)/shard_map/ppermute | solution.py:532
  66.2 10.1 %collective-permute-start.24 = (bf16[256,512]{1,0:T(8,128)(2,1)S(1)}, bf16[256,512]{1,0:T(8,128)(2,1)S(1)}, u32[]{:S(2)}, u32[]{:S(2)}) collective-permute-start(bf16[256,512]{1,0:T(8,128)(2,1)S(1)} %shard_map.103), channel_id=1, source_target_pairs={{0,6},{2,4},{4,2},{6,0},{8,14},{10,12},{12,10},{14,8},{16,22},{18,... | collective-permute-start | bytes 786440 | tf_op jit(solution)/shard_map/ppermute | solution.py:526
  68.3 12.7 %collective-permute-start.25 = (bf16[256,512]{1,0:T(8,128)(2,1)S(1)}, bf16[256,512]{1,0:T(8,128)(2,1)S(1)}, u32[]{:S(2)}, u32[]{:S(2)}) collective-permute-start(bf16[256,512]{1,0:T(8,128)(2,1)S(1)} %get-tuple-element.137), channel_id=1, source_target_pairs={{0,2},{2,0},{4,6},{6,4},{8,10},{10,8},{12,14},{14,12},{16,18},{18,... | collective-permute-start | bytes 786440 | tf_op jit(solution)/shard_map/ppermute | solution.py:526
  69.3 12.0 %collective-permute-start.26 = (bf16[256,512]{1,0:T(8,128)(2,1)S(1)}, bf16[256,512]{1,0:T(8,128)(2,1)S(1)}, u32[]{:S(2)}, u32[]{:S(2)}) collective-permute-start(bf16[256,512]{1,0:T(8,128)(2,1)S(1)} %get-tuple-element.138), channel_id=1, source_target_pairs={{0,4},{2,6},{4,0},{6,2},{8,12},{10,14},{12,8},{14,10},{16,20},{18,... | collective-permute-start | bytes 786440 | tf_op jit(solution)/shard_map/ppermute | solution.py:526
  72.0 4.3 %collective-permute-start.23 = (bf16[256,256]{1,0:T(8,128)(2,1)S(1)}, bf16[256,256]{1,0:T(8,128)(2,1)S(1)}, u32[]{:S(2)}, u32[]{:S(2)}) collective-permute-start(bf16[256,256]{1,0:T(8,128)(2,1)S(1)} %shard_map.105.refs_0_), channel_id=1, source_target_pairs={{0,1},{1,0},{2,3},{3,2},{4,5},{5,4},{6,7},{7,6},{8,9},{9,8},{10,11... | collective-permute-start | bytes 393224 | tf_op jit(solution)/shard_map/ppermute | solution.py:532

commit v18 on v16

--- a/solution.py
+++ b/solution.py
@@ -419,7 +419,7 @@
             entry = keep_ref[block : block + 1, :] * entry + step_ref[block * state : (block + 1) * state, :]
 
 
-def conv_kernel(group, steps, len_ref, taps_ref, gated_ref, act_ref, ext_ref, ends_ref):
+def conv_kernel(group, steps, len_ref, taps_ref, gated_ref, act_ref, ext_ref, spread_ref, ends_ref):
     place, plane = plane_place(group)
     rows_all, width = gated_ref.shape
     total = rows_all - SPAN
@@ -431,6 +431,9 @@
     reach = CONV_ROWS + 2 * EDGE
     first_tap = EDGE - half
     pitch = frames + 2 * EDGE
+    ours = taps_ref[:, pl.ds(pl.multiple_of(place * width, LANES), width)]
+    for tap in range(taps):
+        spread_ref[tap * 8 : (tap + 1) * 8, :] = jnp.broadcast_to(ours[tap : tap + 1, :], (8, width))
     ends_ref[0] = 0
     for record in range(records):
         ends_ref[record + 1] = ends_ref[record] + len_ref[record]
@@ -457,22 +460,21 @@
             near = lax.broadcasted_iota(jnp.int32, (reach, LANES), 0) + (at - EDGE)
             for tile in range(width // LANES):
                 lanes = slice(tile * LANES, (tile + 1) * LANES)
-                weights = taps_ref[:, pl.ds(pl.multiple_of(place * width + tile * LANES, LANES), LANES)]
-
                 def one_record(record, done):
                     inside = (near >= ends_ref[record]) & (near < ends_ref[record + 1])
-                    g = jnp.where(inside, ext_ref[pl.ds(source, reach), lanes], 0.0)
+                    g = jnp.where(inside, ext_ref[pl.ds(source, reach), lanes], 0.0).reshape(reach // 8, 8, LANES)
                     out = None
                     for phase in range(8):
                         part = None
                         for offset in range(phase, reach - CONV_ROWS, 8):
                             tap = offset - first_tap
                             if 0 <= tap < taps:
-                                aligned = offset - phase
-                                term = weights[tap : tap + 1, :] * g[aligned : aligned + CONV_ROWS + 8, :]
+                                first = (offset - phase) // 8
+                                weight = spread_ref[tap * 8 : (tap + 1) * 8, lanes]
+                                term = weight[None] * g[first : first + CONV_ROWS // 8 + 1]
                                 part = term if part is None else part + term
                         if part is not None:
-                            moved = part[phase : phase + CONV_ROWS, :]
+                            moved = part.reshape(CONV_ROWS + 8, LANES)[phase : phase + CONV_ROWS, :]
                             out = moved if out is None else out + moved
                     return jnp.where(inside[EDGE : EDGE + CONV_ROWS], out, done)
 
@@ -483,8 +485,15 @@
         lax.fori_loop(0, frames // CONV_ROWS, one_block, 0)
 
 
-def out_kernel(cores, count, *refs):
-    acts, weights, sent, outs = refs[:cores], refs[cores : 2 * cores], refs[2 * cores : -count], refs[-count:]
+def sum_kernel(own_ref, *refs):
+    total = own_ref[...]
+    for part in refs[:-1]:
+        total = total + part[...].astype(F32)
+    refs[-1][...] = total.astype(refs[-1].dtype)
+
+
+def out_kernel(cores, *refs):
+    acts, weights, outs = refs[:cores], refs[cores : 2 * cores], refs[2 * cores :]
     frames = outs[0].shape[0]
     for number, out_ref in enumerate(outs):
         rows = slice(number * frames, (number + 1) * frames)
@@ -492,8 +501,6 @@
         for act, weight in zip(acts, weights):
             product = dot(act[rows, :], weight[...], ((1,), (1,)))
             total = product if total is None else total + product
-        for part in sent:
-            total = total + part[...].astype(F32)
         out_ref[...] = total.astype(out_ref.dtype)
 
 
@@ -664,15 +671,19 @@
             functools.partial(conv_kernel, group, steps),
             shape((len(steps) * frame_count, width), BF16),
             [record_lengths, conv_weight, gated],
-            [pltpu.VMEM((len(steps) * (frame_count + 2 * EDGE), width), F32), ends],
+            [
+                pltpu.VMEM((len(steps) * (frame_count + 2 * EDGE), width), F32),
+                pltpu.VMEM((conv_weight.shape[0] * 8, width), F32),
+                ends,
+            ],
             flops=2 * len(steps) * frame_count * width * conv_weight.shape[0],
         )
 
-    def out(steps, act, swapped, sent=()):
+    def out(steps, act, swapped):
         return call(
-            functools.partial(out_kernel, cores, len(steps)),
-            tuple(shape((frame_count, share), BF16) for _ in steps),
-            [act, *swapped, *out_parts, *sent],
+            functools.partial(out_kernel, cores),
+            tuple(shape((frame_count, share), BF16 if step else F32) for step in steps),
+            [act, *swapped, *out_parts],
             flops=2 * len(steps) * frame_count * width * cores * share,
             smem=0,
         )
@@ -704,8 +715,8 @@
         sent += [in_plane(part, step) for part, step in zip(near_outs, near)]
     own_act = conv((0,), gated)
     own_swapped = [across(own_act, step) for step in range(1, cores)]
-    (mixed,) = out((0,), own_act, own_swapped, sent)
-    return mixed
+    (own_out,) = out((0,), own_act, own_swapped)
+    return call(sum_kernel, shape((frame_count, share), BF16), [own_out, *sent], smem=0)
 
 
 def solution(mesh):

time: 81.9 us -> 81.9 us (level)
    ppermute x5, waiting for transfers between devices: 0.01 us -> 1.35 us  [across(): return lax.ppermute(array, 'head', [(i, i ^ step) for i in range(cores)])]
    ppermute x9, waiting for transfers between devices: 14.4 us -> 13.2 us  [in_plane(): return lax.ppermute(array, 'tm', [(i, i ^ step) for i in range(times)])]
    pallas_call x16 -> x17, Pallas kernels: 18.1 us -> 18.7 us  [call(): pl.pallas_call(kernel, out_shape=out_shape, in_specs=in_specs, out_specs=...]
  transfers between devices with their start and end apart: 27 -> 27, of which waited for: 8 -> 10; matrix products, arithmetic and copies ran while one was open for 1% -> 1% of each run, Pallas kernels for 17% -> 18%
where the time goes in v18:
time: 81.9 us; the launch traced here: 81 us
  starting transfers between devices  37.5 us (46%)
  waiting for transfers between devices  22.8 us (28%)
  Pallas kernels  18.7 us (23%)
  local copies, waits for them, and re-layouts  1.78 us (2%)
    pallas_call x17, Pallas kernels, call(): pl.pallas_call(kernel, out_shape=out_shape, in_specs=in_specs, out_specs=...  18.7 us
    ppermute x8, starting transfers between devices, between_planes(): lax.ppermute(array, 'tm', [(i, i ^ step * group) for i in range(times)])  15 us
    ppermute x9, waiting for transfers between devices, in_plane(): return lax.ppermute(array, 'tm', [(i, i ^ step) for i in range(times)])  13.2 us
    ppermute x9, starting transfers between devices, in_plane(): return lax.ppermute(array, 'tm', [(i, i ^ step) for i in range(times)])  12 us
    ppermute x3, starting transfers between devices, later(): lax.ppermute(array, 'tm', [(i, i + step * group) for i in range(times - s...  7.74 us
    ppermute x8, waiting for transfers between devices, between_planes(): lax.ppermute(array, 'tm', [(i, i ^ step * group) for i in range(times)])  7.41 us
  transfers between devices with their start and end apart: 27, of which 10 were waited for; matrix products, arithmetic and copies ran while one was open for 1% of the time, Pallas kernels for 18%

profile of v18, /device:TPU:0, one launch (start us, length us, event | category | flops | bytes accessed | tf_op | source)
XLA Modules:
  0.0 81.0 jit_solution(3666423008952061139)
XLA Ops:
  0.0 2.0 %shard_map.91 = (bf16[64,768]{1,0:T(8,128)(2,1)}, bf16[64,768]{1,0:T(8,128)(2,1)}, bf16[64,768]{1,0:T(8,128)(2,1)}, bf16[64,768]{1,0:T(8,128)(2,1)}, bf16[32,102...) custom-call(f32[16,256]{1,0:T(8,128)} %log_decay_ref.1, ...), custom_call_target="tpu_custom_call" | custom-call | bytes 1622016 | tf_op jit(solution)/shard_map/pallas_call | solution.py:35
  2.0 3.0 %collective-permute-start.6 = (bf16[64,768]{1,0:T(8,128)(2,1)}, bf16[64,768]{1,0:T(8,128)(2,1)S(1)}, u32[]{:S(2)}, u32[]{:S(2)}) collective-permute-start(bf16[64,768]{1,0:T(8,128)(2,1)} %get-tuple-element.77), channel_id=1, source_target_pairs={{0,2},{2,0},{4,6},{6,4},{8,10},{10,8},{12,14},{14,12},{16,18},{18,... | collective-permute-start | bytes 294920 | tf_op jit(solution)/shard_map/ppermute | solution.py:533
  5.0 1.5 %collective-permute-start.7 = (bf16[64,768]{1,0:T(8,128)(2,1)}, bf16[64,768]{1,0:T(8,128)(2,1)S(1)}, u32[]{:S(2)}, u32[]{:S(2)}) collective-permute-start(bf16[64,768]{1,0:T(8,128)(2,1)} %get-tuple-element.78), channel_id=1, source_target_pairs={{0,4},{2,6},{4,0},{6,2},{8,12},{10,14},{12,8},{14,10},{16,20},{18,... | collective-permute-start | bytes 294920 | tf_op jit(solution)/shard_map/ppermute | solution.py:533
  6.5 2.0 %collective-permute-start = (bf16[32,1024]{1,0:T(8,128)(2,1)}, bf16[32,1024]{1,0:T(8,128)(2,1)S(1)}, u32[]{:S(2)}, u32[]{:S(2)}) collective-permute-start(bf16[32,1024]{1,0:T(8,128)(2,1)} %get-tuple-element.68), channel_id=1, source_target_pairs={{0,8},{2,10},{4,12},{6,14},{8,0},{10,2},{12,4},{14,6},{16,24},{18,... | collective-permute-start | bytes 196616 | tf_op jit(solution)/shard_map/ppermute | solution.py:542
  8.5 2.6 %collective-permute-start.1 = (bf16[32,1024]{1,0:T(8,128)(2,1)}, bf16[32,1024]{1,0:T(8,128)(2,1)S(1)}, u32[]{:S(2)}, u32[]{:S(2)}) collective-permute-start(bf16[32,1024]{1,0:T(8,128)(2,1)} %get-tuple-element.69), channel_id=1, source_target_pairs={{0,16},{2,18},{4,20},{6,22},{8,24},{10,26},{12,28},{14,30},{16,0},... | collective-permute-start | bytes 196616 | tf_op jit(solution)/shard_map/ppermute | solution.py:542
  11.1 0.7 reshape.3
  12.0 0.2 collective-permute-done.8.refs_3_
  12.2 0.9 %copy-done.4 = bf16[64,768]{1,0:T(8,128)(2,1)S(1)} copy-done((bf16[64,768]{1,0:T(8,128)(2,1)S(1)}, bf16[64,768]{1,0:T(8,128)(2,1)}, u32[]{:S(2)}) %copy-start.4) | copy-done | bytes 98328
  13.2 2.7 %collective-permute-start.9 = (bf16[256,512]{1,0:T(8,128)(2,1)S(1)}, bf16[256,512]{1,0:T(8,128)(2,1)S(1)}, u32[]{:S(2)}, u32[]{:S(2)}) collective-permute-start(bf16[256,512]{1,0:T(8,128)(2,1)S(1)} %get-tuple-element.85.refs_0_), channel_id=1, source_target_pairs={{0,16},{2,18},{4,20},{6,22},{8,24},{10,26},{12,28},{14,30},{16,0},... | collective-permute-start | bytes 786440 | tf_op jit(solution)/shard_map/ppermute | solution.py:542
  15.8 1.6 %collective-permute-start.10 = (bf16[256,512]{1,0:T(8,128)(2,1)S(1)}, bf16[256,512]{1,0:T(8,128)(2,1)S(1)}, u32[]{:S(2)}, u32[]{:S(2)}) collective-permute-start(bf16[256,512]{1,0:T(8,128)(2,1)S(1)} %get-tuple-element.85.refs_0_), channel_id=1, source_target_pairs={{0,8},{2,10},{4,12},{6,14},{8,0},{10,2},{12,4},{14,6},{16,24},{18,... | collective-permute-start | bytes 786440 | tf_op jit(solution)/shard_map/ppermute | solution.py:542
  17.4 2.7 %collective-permute-done.1.refs_2_ = bf16[32,1024]{1,0:T(8,128)(2,1)S(1)} collective-permute-done((bf16[32,1024]{1,0:T(8,128)(2,1)}, bf16[32,1024]{1,0:T(8,128)(2,1)S(1)}, u32[]{:S(2)}, u32[]{:S(2)}) %collective-permute-start.1) | collective-permute-done | bytes 65568 | tf_op jit(solution)/shard_map/ppermute | solution.py:542
  20.1 0.2 shard_map.92
  20.2 1.6 %collective-permute-start.3 = (bf16[192,1024]{1,0:T(8,128)(2,1)S(1)}, bf16[192,1024]{1,0:T(8,128)(2,1)S(1)}, u32[]{:S(2)}, u32[]{:S(2)}) collective-permute-start(bf16[192,1024]{1,0:T(8,128)(2,1)S(1)} %get-tuple-element.72), channel_id=1, source_target_pairs={{0,2},{2,0},{4,6},{6,4},{8,10},{10,8},{12,14},{14,12},{16,18},{18,... | collective-permute-start | bytes 1179656 | tf_op jit(solution)/shard_map/ppermute | solution.py:533
  21.8 1.5 %collective-permute-start.4 = (bf16[192,1024]{1,0:T(8,128)(2,1)S(1)}, bf16[192,1024]{1,0:T(8,128)(2,1)S(1)}, u32[]{:S(2)}, u32[]{:S(2)}) collective-permute-start(bf16[192,1024]{1,0:T(8,128)(2,1)S(1)} %get-tuple-element.73), channel_id=1, source_target_pairs={{0,4},{2,6},{4,0},{6,2},{8,12},{10,14},{12,8},{14,10},{16,20},{18,... | collective-permute-start | bytes 1179656 | tf_op jit(solution)/shard_map/ppermute | solution.py:533
  23.3 0.5 collective-permute-start.5
  23.8 4.7 %collective-permute-done.9.refs_2_ = bf16[256,512]{1,0:T(8,128)(2,1)S(1)} collective-permute-done((bf16[256,512]{1,0:T(8,128)(2,1)S(1)}, bf16[256,512]{1,0:T(8,128)(2,1)S(1)}, u32[]{:S(2)}, u32[]{:S(2)}) %collective-permute-start.9) | collective-permute-done | bytes 262176 | tf_op jit(solution)/shard_map/ppermute | solution.py:542
  28.5 1.3 %collective-permute-start.11 = (bf16[256,512]{1,0:T(8,128)(2,1)S(1)}, bf16[256,512]{1,0:T(8,128)(2,1)S(1)}, u32[]{:S(2)}, u32[]{:S(2)}) collective-permute-start(bf16[256,512]{1,0:T(8,128)(2,1)S(1)} %collective-permute-done.9.refs_2_), channel_id=1, source_target_pairs={{8,0},{10,2},{12,4},{14,6},{16,24},{18,26},{20,28},{22,30},{9,1},{... | collective-permute-start | bytes 786440 | tf_op jit(solution)/shard_map/ppermute | solution.py:558
  29.8 0.7 collective-permute-start.12
  30.5 0.6 collective-permute-done.3.refs_1_.refs_0_
  31.1 5.4 %collective-permute-done.4.refs_2_.refs_1_ = bf16[192,1024]{1,0:T(8,128)(2,1)S(1)} collective-permute-done((bf16[192,1024]{1,0:T(8,128)(2,1)S(1)}, bf16[192,1024]{1,0:T(8,128)(2,1)S(1)}, u32[]{:S(2)}, u32[]{:S(2)}) %collective-permute-start.4) | collective-permute-done | bytes 393248 | tf_op jit(solution)/shard_map/ppermute | solution.py:533
  36.5 0.5 shard_map.93
  37.1 0.8 collective-permute-done.11.refs_3_
  37.9 3.7 %collective-permute-start.14 = (bf16[256,256]{1,0:T(8,128)(2,1)S(1)}, bf16[256,256]{1,0:T(8,128)(2,1)S(1)}, u32[]{:S(2)}, u32[]{:S(2)}) collective-permute-start(bf16[256,256]{1,0:T(8,128)(2,1)S(1)} %get-tuple-element.96.refs_0_), channel_id=1, source_target_pairs={{0,8},{2,10},{4,12},{6,14},{8,0},{10,2},{12,4},{14,6},{16,24},{18,... | collective-permute-start | bytes 393224 | tf_op jit(solution)/shard_map/ppermute | solution.py:542
  41.6 0.6 collective-permute-start.15
  42.2 1.8 %collective-permute-start.16 = (bf16[256,256]{1,0:T(8,128)(2,1)S(1)}, bf16[256,256]{1,0:T(8,128)(2,1)S(1)}, u32[]{:S(2)}, u32[]{:S(2)}) collective-permute-start(bf16[256,256]{1,0:T(8,128)(2,1)S(1)} %get-tuple-element.96.refs_0_), channel_id=1, source_target_pairs={{0,24},{2,26},{4,28},{6,30},{8,16},{10,18},{12,20},{14,22},{16,8},... | collective-permute-start | bytes 393224 | tf_op jit(solution)/shard_map/ppermute | solution.py:542
  44.0 2.8 %shard_map.96 = (bf16[1152,1024]{1,0:T(8,128)(2,1)S(1)}, bf16[1152,256]{1,0:T(8,128)(2,1)S(1)}, bf16[1152,128]{1,0:T(8,128)(2,1)S(1)}, bf16[1152,128]{1,0:T(8,12...) custom-call(s32[8]{0:T(128)S(1)} %copy-done.2, ...), custom_call_target="tpu_custom_call" | custom-call | tf_op jit(solution)/shard_map/pallas_call | solution.py:35
  46.8 3.0 %collective-permute-start.17 = (bf16[144,256]{1,0:T(8,128)(2,1)S(1)}, bf16[144,256]{1,0:T(8,128)(2,1)S(1)}, u32[]{:S(2)}, u32[]{:S(2)}) collective-permute-start(bf16[144,256]{1,0:T(8,128)(2,1)S(1)} %get-tuple-element.112), channel_id=1, source_target_pairs={{0,8},{2,10},{4,12},{6,14},{8,16},{10,18},{12,20},{14,22},{16,24},... | collective-permute-start | bytes 221192 | tf_op jit(solution)/shard_map/ppermute | solution.py:536
  49.9 3.4 %collective-permute-start.18 = (bf16[144,256]{1,0:T(8,128)(2,1)S(1)}, bf16[144,256]{1,0:T(8,128)(2,1)S(1)}, u32[]{:S(2)}, u32[]{:S(2)}) collective-permute-start(bf16[144,256]{1,0:T(8,128)(2,1)S(1)} %get-tuple-element.112), channel_id=1, source_target_pairs={{0,16},{2,18},{4,20},{6,22},{8,24},{10,26},{12,28},{14,30},{1,17},... | collective-permute-start | bytes 221192 | tf_op jit(solution)/shard_map/ppermute | solution.py:536
  53.3 1.3 %collective-permute-start.19 = (bf16[144,256]{1,0:T(8,128)(2,1)S(1)}, bf16[144,256]{1,0:T(8,128)(2,1)S(1)}, u32[]{:S(2)}, u32[]{:S(2)}) collective-permute-start(bf16[144,256]{1,0:T(8,128)(2,1)S(1)} %get-tuple-element.112), channel_id=1, source_target_pairs={{0,24},{2,26},{4,28},{6,30},{1,25},{3,27},{5,29},{7,31}} | collective-permute-start | bytes 221192 | tf_op jit(solution)/shard_map/ppermute | solution.py:536
  54.7 1.9 %shard_map.98 = (f32[1152,256]{1,0:T(8,128)S(1)}, f32[1152,256]{1,0:T(8,128)S(1)}) custom-call(bf16[1152,256]{1,0:T(8,128)(2,1)S(1)} %get-tuple-element.103.x_ref, bf16[1152,128]{1,0:T(8,128)(2,1)S(1)} %get-tuple-element.104.b_ref, bf16[1152,128]{1,0:T(8,128)(2,1)S(1)} %get-tuple-element.102.c_ref, f32[216,128]{1,0:T(8,128)S(1)} %get-tuple-element.105.rows_ref), custom_call_target="tpu_custom_call" | custom-call | flops 134217728 | bytes 3649536 | tf_op jit(solution)/shard_map/pallas_call | solution.py:35
  56.6 0.8 %shard_map.99.silu_ref = f32[1152,256]{1,0:T(8,128)S(1)} custom-call(f32[1,1024]{1,0:T(1,128)S(1)} %bitcast.2, bf16[1152,1024]{1,0:T(8,128)(2,1)S(1)} %get-tuple-element.110.frames_ref, bf16[1024,256]{1,0:T(8,128)(2,1)S(1)} %get-tuple-element.111.weight_ref), custom_call_target="tpu_custom_call" | custom-call | flops 536870912 | bytes 4067328 | tf_op jit(solution)/shard_map/pallas_call | solution.py:35
  57.5 0.7 shard_map.100.gated_ref
  58.4 2.2 %shard_map.101.refs_0_ = bf16[256,256]{1,0:T(8,128)(2,1)S(1)} custom-call(s32[8]{0:T(128)S(1)} %copy-done.2, f32[31,1024]{1,0:T(8,128)S(1)} %copy-done.1, bf16[1152,256]{1,0:T(8,128)(2,1)S(1)} %shard_map.100.gated_ref), custom_call_target="tpu_custom_call" | custom-call | flops 4063232 | bytes 847904 | tf_op jit(solution)/shard_map/pallas_call | solution.py:35
  60.6 0.4 collective-permute-start.20
  61.1 3.5 %shard_map.102.refs_0_ = bf16[512,256]{1,0:T(8,128)(2,1)S(1)} custom-call(s32[8]{0:T(128)S(1)} %copy-done.2, f32[31,1024]{1,0:T(8,128)S(1)} %copy-done.1, bf16[1152,256]{1,0:T(8,128)(2,1)S(1)} %shard_map.100.gated_ref), custom_call_target="tpu_custom_call" | custom-call | flops 8126464 | bytes 978976 | tf_op jit(solution)/shard_map/pallas_call | solution.py:35
  64.6 0.3 shard_map.103
  64.9 0.2 collective-permute-start.22
  65.1 1.9 %collective-permute-start.24 = (bf16[256,512]{1,0:T(8,128)(2,1)S(1)}, bf16[256,512]{1,0:T(8,128)(2,1)S(1)}, u32[]{:S(2)}, u32[]{:S(2)}) collective-permute-start(bf16[256,512]{1,0:T(8,128)(2,1)S(1)} %shard_map.103), channel_id=1, source_target_pairs={{0,6},{2,4},{4,2},{6,0},{8,14},{10,12},{12,10},{14,8},{16,22},{18,... | collective-permute-start | bytes 786440 | tf_op jit(solution)/shard_map/ppermute | solution.py:533
  67.0 0.5 shard_map.104
  67.5 1.8 %collective-permute-start.25 = (bf16[256,512]{1,0:T(8,128)(2,1)S(1)}, bf16[256,512]{1,0:T(8,128)(2,1)S(1)}, u32[]{:S(2)}, u32[]{:S(2)}) collective-permute-start(bf16[256,512]{1,0:T(8,128)(2,1)S(1)} %get-tuple-element.127), channel_id=1, source_target_pairs={{0,2},{2,0},{4,6},{6,4},{8,10},{10,8},{12,14},{14,12},{16,18},{18,... | collective-permute-start | bytes 786440 | tf_op jit(solution)/shard_map/ppermute | solution.py:533
  69.4 0.2 collective-permute-start.26
  69.5 2.0 %shard_map.105.refs_0_ = bf16[256,256]{1,0:T(8,128)(2,1)S(1)} custom-call(s32[8]{0:T(128)S(1)} %copy-done.2, f32[31,1024]{1,0:T(8,128)S(1)} %copy-done.1, bf16[1152,256]{1,0:T(8,128)(2,1)S(1)} %shard_map.100.gated_ref), custom_call_target="tpu_custom_call" | custom-call | flops 4063232 | bytes 847904 | tf_op jit(solution)/shard_map/pallas_call | solution.py:35
  71.6 1.3 %collective-permute-done.23.refs_1_ = bf16[256,256]{1,0:T(8,128)(2,1)S(1)} collective-permute-done((bf16[256,256]{1,0:T(8,128)(2,1)S(1)}, bf16[256,256]{1,0:T(8,128)(2,1)S(1)}, u32[]{:S(2)}, u32[]{:S(2)}) %collective-permute-start.23) | collective-permute-done | bytes 131104 | tf_op jit(solution)/shard_map/ppermute | solution.py:539
  73.0 0.3 shard_map.106.own_ref
  73.3 1.9 %collective-permute-done.24.refs_0_ = bf16[256,512]{1,0:T(8,128)(2,1)S(1)} collective-permute-done((bf16[256,512]{1,0:T(8,128)(2,1)S(1)}, bf16[256,512]{1,0:T(8,128)(2,1)S(1)}, u32[]{:S(2)}, u32[]{:S(2)}) %collective-permute-start.24) | collective-permute-done | bytes 262176 | tf_op jit(solution)/shard_map/ppermute | solution.py:533
  75.2 4.7 %collective-permute-done.25.refs_1_ = bf16[256,512]{1,0:T(8,128)(2,1)S(1)} collective-permute-done((bf16[256,512]{1,0:T(8,128)(2,1)S(1)}, bf16[256,512]{1,0:T(8,128)(2,1)S(1)}, u32[]{:S(2)}, u32[]{:S(2)}) %collective-permute-start.25) | collective-permute-done | bytes 262176 | tf_op jit(solution)/shard_map/ppermute | solution.py:533
  79.9 0.3 collective-permute-done.26.refs_2_
  80.2 0.8 %shard_map.107 = bf16[256,512]{1,0:T(8,128)(2,1)} custom-call(f32[256,512]{1,0:T(8,128)S(1)} %shard_map.106.own_ref, bf16[256,512]{1,0:T(8,128)(2,1)S(1)} %collective-permute-done.24.refs_0_, bf16[256,512]{1,0:T(8,128)(2,1)S(1)} %collective-permute-done.25.refs_1_, bf16[256,512]{1,0:T(8,128)(2,1)S(1)} %collective-permute-done.26.refs_2_), custom_call_target="tpu_custom_call" | custom-call | bytes 1572864 | tf_op jit(solution)/shard_map/pallas_call | solution.py:35
  (37 shorter events, 0.7 us)
Async XLA Ops:
  2.0 9.9 %collective-permute-start.6 = (bf16[64,768]{1,0:T(8,128)(2,1)}, bf16[64,768]{1,0:T(8,128)(2,1)S(1)}, u32[]{:S(2)}, u32[]{:S(2)}) collective-permute-start(bf16[64,768]{1,0:T(8,128)(2,1)} %get-tuple-element.77), channel_id=1, source_target_pairs={{0,2},{2,0},{4,6},{6,4},{8,10},{10,8},{12,14},{14,12},{16,18},{18,... | collective-permute-start | bytes 294920 | tf_op jit(solution)/shard_map/ppermute | solution.py:533
  5.0 7.0 %collective-permute-start.7 = (bf16[64,768]{1,0:T(8,128)(2,1)}, bf16[64,768]{1,0:T(8,128)(2,1)S(1)}, u32[]{:S(2)}, u32[]{:S(2)}) collective-permute-start(bf16[64,768]{1,0:T(8,128)(2,1)} %get-tuple-element.78), channel_id=1, source_target_pairs={{0,4},{2,6},{4,0},{6,2},{8,12},{10,14},{12,8},{14,10},{16,20},{18,... | collective-permute-start | bytes 294920 | tf_op jit(solution)/shard_map/ppermute | solution.py:533
  6.5 5.7 %collective-permute-start.8 = (bf16[64,768]{1,0:T(8,128)(2,1)}, bf16[64,768]{1,0:T(8,128)(2,1)S(1)}, u32[]{:S(2)}, u32[]{:S(2)}) collective-permute-start(bf16[64,768]{1,0:T(8,128)(2,1)} %get-tuple-element.79), channel_id=1, source_target_pairs={{0,6},{2,4},{4,2},{6,0},{8,14},{10,12},{12,10},{14,8},{16,22},{18,... | collective-permute-start | bytes 294920 | tf_op jit(solution)/shard_map/ppermute | solution.py:533
  6.5 10.9 %collective-permute-start = (bf16[32,1024]{1,0:T(8,128)(2,1)}, bf16[32,1024]{1,0:T(8,128)(2,1)S(1)}, u32[]{:S(2)}, u32[]{:S(2)}) collective-permute-start(bf16[32,1024]{1,0:T(8,128)(2,1)} %get-tuple-element.68), channel_id=1, source_target_pairs={{0,8},{2,10},{4,12},{6,14},{8,0},{10,2},{12,4},{14,6},{16,24},{18,... | collective-permute-start | bytes 196616 | tf_op jit(solution)/shard_map/ppermute | solution.py:542
  8.5 11.5 %collective-permute-start.1 = (bf16[32,1024]{1,0:T(8,128)(2,1)}, bf16[32,1024]{1,0:T(8,128)(2,1)S(1)}, u32[]{:S(2)}, u32[]{:S(2)}) collective-permute-start(bf16[32,1024]{1,0:T(8,128)(2,1)} %get-tuple-element.69), channel_id=1, source_target_pairs={{0,16},{2,18},{4,20},{6,22},{8,24},{10,26},{12,28},{14,30},{16,0},... | collective-permute-start | bytes 196616 | tf_op jit(solution)/shard_map/ppermute | solution.py:542
  11.9 8.2 %collective-permute-start.2 = (bf16[32,1024]{1,0:T(8,128)(2,1)}, bf16[32,1024]{1,0:T(8,128)(2,1)S(1)}, u32[]{:S(2)}, u32[]{:S(2)}) collective-permute-start(bf16[32,1024]{1,0:T(8,128)(2,1)} %get-tuple-element.70), channel_id=1, source_target_pairs={{0,24},{2,26},{4,28},{6,30},{8,16},{10,18},{12,20},{14,22},{16,8},... | collective-permute-start | bytes 196616 | tf_op jit(solution)/shard_map/ppermute | solution.py:542
  12.2 0.9 %copy-start.4 = (bf16[64,768]{1,0:T(8,128)(2,1)S(1)}, bf16[64,768]{1,0:T(8,128)(2,1)}, u32[]{:S(2)}) copy-start(bf16[64,768]{1,0:T(8,128)(2,1)} %get-tuple-element.76.refs_0_) | copy-start | bytes 294916
  13.1 7.0 %copy-start = (bf16[256,1024]{1,0:T(8,128)(2,1)S(1)}, bf16[256,1024]{1,0:T(8,128)(2,1)}, u32[]{:S(2)}) copy-start(bf16[256,1024]{1,0:T(8,128)(2,1)} %own_ref.1) | copy-start | bytes 1572868
  13.1 7.0 %copy-start.5 = (bf16[32,1024]{1,0:T(8,128)(2,1)S(1)}, bf16[32,1024]{1,0:T(8,128)(2,1)}, u32[]{:S(2)}) copy-start(bf16[32,1024]{1,0:T(8,128)(2,1)} %get-tuple-element.67.refs_0_) | copy-start | bytes 196612
  13.2 15.4 %collective-permute-start.9 = (bf16[256,512]{1,0:T(8,128)(2,1)S(1)}, bf16[256,512]{1,0:T(8,128)(2,1)S(1)}, u32[]{:S(2)}, u32[]{:S(2)}) collective-permute-start(bf16[256,512]{1,0:T(8,128)(2,1)S(1)} %get-tuple-element.85.refs_0_), channel_id=1, source_target_pairs={{0,16},{2,18},{4,20},{6,22},{8,24},{10,26},{12,28},{14,30},{16,0},... | collective-permute-start | bytes 786440 | tf_op jit(solution)/shard_map/ppermute | solution.py:542
  15.8 12.7 %collective-permute-start.10 = (bf16[256,512]{1,0:T(8,128)(2,1)S(1)}, bf16[256,512]{1,0:T(8,128)(2,1)S(1)}, u32[]{:S(2)}, u32[]{:S(2)}) collective-permute-start(bf16[256,512]{1,0:T(8,128)(2,1)S(1)} %get-tuple-element.85.refs_0_), channel_id=1, source_target_pairs={{0,8},{2,10},{4,12},{6,14},{8,0},{10,2},{12,4},{14,6},{16,24},{18,... | collective-permute-start | bytes 786440 | tf_op jit(solution)/shard_map/ppermute | solution.py:542
  20.2 10.9 %collective-permute-start.3 = (bf16[192,1024]{1,0:T(8,128)(2,1)S(1)}, bf16[192,1024]{1,0:T(8,128)(2,1)S(1)}, u32[]{:S(2)}, u32[]{:S(2)}) collective-permute-start(bf16[192,1024]{1,0:T(8,128)(2,1)S(1)} %get-tuple-element.72), channel_id=1, source_target_pairs={{0,2},{2,0},{4,6},{6,4},{8,10},{10,8},{12,14},{14,12},{16,18},{18,... | collective-permute-start | bytes 1179656 | tf_op jit(solution)/shard_map/ppermute | solution.py:533
  21.8 14.7 %collective-permute-start.4 = (bf16[192,1024]{1,0:T(8,128)(2,1)S(1)}, bf16[192,1024]{1,0:T(8,128)(2,1)S(1)}, u32[]{:S(2)}, u32[]{:S(2)}) collective-permute-start(bf16[192,1024]{1,0:T(8,128)(2,1)S(1)} %get-tuple-element.73), channel_id=1, source_target_pairs={{0,4},{2,6},{4,0},{6,2},{8,12},{10,14},{12,8},{14,10},{16,20},{18,... | collective-permute-start | bytes 1179656 | tf_op jit(solution)/shard_map/ppermute | solution.py:533
  23.3 13.2 %collective-permute-start.5 = (bf16[192,1024]{1,0:T(8,128)(2,1)S(1)}, bf16[192,1024]{1,0:T(8,128)(2,1)S(1)}, u32[]{:S(2)}, u32[]{:S(2)}) collective-permute-start(bf16[192,1024]{1,0:T(8,128)(2,1)S(1)} %get-tuple-element.74), channel_id=1, source_target_pairs={{0,6},{2,4},{4,2},{6,0},{8,14},{10,12},{12,10},{14,8},{16,22},{18,... | collective-permute-start | bytes 1179656 | tf_op jit(solution)/shard_map/ppermute | solution.py:533
  28.5 9.4 %collective-permute-start.11 = (bf16[256,512]{1,0:T(8,128)(2,1)S(1)}, bf16[256,512]{1,0:T(8,128)(2,1)S(1)}, u32[]{:S(2)}, u32[]{:S(2)}) collective-permute-start(bf16[256,512]{1,0:T(8,128)(2,1)S(1)} %collective-permute-done.9.refs_2_), channel_id=1, source_target_pairs={{8,0},{10,2},{12,4},{14,6},{16,24},{18,26},{20,28},{22,30},{9,1},{... | collective-permute-start | bytes 786440 | tf_op jit(solution)/shard_map/ppermute | solution.py:558
  29.8 8.1 %collective-permute-start.12 = (bf16[256,512]{1,0:T(8,128)(2,1)S(1)}, bf16[256,512]{1,0:T(8,128)(2,1)S(1)}, u32[]{:S(2)}, u32[]{:S(2)}) collective-permute-start(bf16[256,512]{1,0:T(8,128)(2,1)S(1)} %get-tuple-element.85.refs_0_), channel_id=1, source_target_pairs={{8,16},{10,18},{12,20},{14,22},{16,8},{18,10},{20,12},{22,14},{9,1... | collective-permute-start | bytes 786440 | tf_op jit(solution)/shard_map/ppermute | solution.py:559
  37.0 7.0 %collective-permute-start.13 = (bf16[512,1024]{1,0:T(8,128)(2,1)S(1)}, bf16[512,1024]{1,0:T(8,128)(2,1)S(1)}, u32[]{:S(2)}, u32[]{:S(2)}) collective-permute-start(bf16[512,1024]{1,0:T(8,128)(2,1)S(1)} %get-tuple-element.92), channel_id=1, source_target_pairs={{0,1},{1,0},{2,3},{3,2},{4,5},{5,4},{6,7},{7,6},{8,9},{9,8},{10,11... | collective-permute-start | bytes 3145736 | tf_op jit(solution)/shard_map/ppermute | solution.py:539
  37.9 6.1 %copy-start.2 = (s32[8]{0:T(128)S(1)}, s32[8]{0:T(128)}, u32[]{:S(2)}) copy-start(s32[8]{0:T(128)} %len_ref.7) | copy-start | bytes 100
  37.9 15.4 %collective-permute-start.14 = (bf16[256,256]{1,0:T(8,128)(2,1)S(1)}, bf16[256,256]{1,0:T(8,128)(2,1)S(1)}, u32[]{:S(2)}, u32[]{:S(2)}) collective-permute-start(bf16[256,256]{1,0:T(8,128)(2,1)S(1)} %get-tuple-element.96.refs_0_), channel_id=1, source_target_pairs={{0,8},{2,10},{4,12},{6,14},{8,0},{10,2},{12,4},{14,6},{16,24},{18,... | collective-permute-start | bytes 393224 | tf_op jit(solution)/shard_map/ppermute | solution.py:542
  41.6 13.0 %collective-permute-start.15 = (bf16[256,256]{1,0:T(8,128)(2,1)S(1)}, bf16[256,256]{1,0:T(8,128)(2,1)S(1)}, u32[]{:S(2)}, u32[]{:S(2)}) collective-permute-start(bf16[256,256]{1,0:T(8,128)(2,1)S(1)} %get-tuple-element.96.refs_0_), channel_id=1, source_target_pairs={{0,16},{2,18},{4,20},{6,22},{8,24},{10,26},{12,28},{14,30},{16,0},... | collective-permute-start | bytes 393224 | tf_op jit(solution)/shard_map/ppermute | solution.py:542
  42.2 12.5 %collective-permute-start.16 = (bf16[256,256]{1,0:T(8,128)(2,1)S(1)}, bf16[256,256]{1,0:T(8,128)(2,1)S(1)}, u32[]{:S(2)}, u32[]{:S(2)}) collective-permute-start(bf16[256,256]{1,0:T(8,128)(2,1)S(1)} %get-tuple-element.96.refs_0_), channel_id=1, source_target_pairs={{0,24},{2,26},{4,28},{6,30},{8,16},{10,18},{12,20},{14,22},{16,8},... | collective-permute-start | bytes 393224 | tf_op jit(solution)/shard_map/ppermute | solution.py:542
  46.8 9.8 %copy-start.3 = (f32[1024]{0:T(1024)S(1)}, f32[1024]{0:T(1024)}, u32[]{:S(2)}) copy-start(f32[1024]{0:T(1024)} %param.14) | copy-start | bytes 12292
  46.8 10.6 %collective-permute-start.17 = (bf16[144,256]{1,0:T(8,128)(2,1)S(1)}, bf16[144,256]{1,0:T(8,128)(2,1)S(1)}, u32[]{:S(2)}, u32[]{:S(2)}) collective-permute-start(bf16[144,256]{1,0:T(8,128)(2,1)S(1)} %get-tuple-element.112), channel_id=1, source_target_pairs={{0,8},{2,10},{4,12},{6,14},{8,16},{10,18},{12,20},{14,22},{16,24},... | collective-permute-start | bytes 221192 | tf_op jit(solution)/shard_map/ppermute | solution.py:536
  49.9 7.6 %collective-permute-start.18 = (bf16[144,256]{1,0:T(8,128)(2,1)S(1)}, bf16[144,256]{1,0:T(8,128)(2,1)S(1)}, u32[]{:S(2)}, u32[]{:S(2)}) collective-permute-start(bf16[144,256]{1,0:T(8,128)(2,1)S(1)} %get-tuple-element.112), channel_id=1, source_target_pairs={{0,16},{2,18},{4,20},{6,22},{8,24},{10,26},{12,28},{14,30},{1,17},... | collective-permute-start | bytes 221192 | tf_op jit(solution)/shard_map/ppermute | solution.py:536
  53.3 4.2 %collective-permute-start.19 = (bf16[144,256]{1,0:T(8,128)(2,1)S(1)}, bf16[144,256]{1,0:T(8,128)(2,1)S(1)}, u32[]{:S(2)}, u32[]{:S(2)}) collective-permute-start(bf16[144,256]{1,0:T(8,128)(2,1)S(1)} %get-tuple-element.112), channel_id=1, source_target_pairs={{0,24},{2,26},{4,28},{6,30},{1,25},{3,27},{5,29},{7,31}} | collective-permute-start | bytes 221192 | tf_op jit(solution)/shard_map/ppermute | solution.py:536
  57.5 0.9 %copy-start.1 = (f32[31,1024]{1,0:T(8,128)S(1)}, f32[31,1024]{1,0:T(8,128)}, u32[]{:S(2)}) copy-start(f32[31,1024]{1,0:T(8,128)} %taps_ref.5) | copy-start | bytes 380932
  58.2 6.4 %collective-permute-start.21 = (bf16[512,256]{1,0:T(8,128)(2,1)S(1)}, bf16[512,256]{1,0:T(8,128)(2,1)S(1)}, u32[]{:S(2)}, u32[]{:S(2)}) collective-permute-start(bf16[512,256]{1,0:T(8,128)(2,1)S(1)} %get-tuple-element.116), channel_id=1, source_target_pairs={{0,1},{1,0},{2,3},{3,2},{4,5},{5,4},{6,7},{7,6},{8,9},{9,8},{10,11... | collective-permute-start | bytes 786440 | tf_op jit(solution)/shard_map/ppermute | solution.py:539
  60.6 3.9 %collective-permute-start.20 = (bf16[256,256]{1,0:T(8,128)(2,1)S(1)}, bf16[256,256]{1,0:T(8,128)(2,1)S(1)}, u32[]{:S(2)}, u32[]{:S(2)}) collective-permute-start(bf16[256,256]{1,0:T(8,128)(2,1)S(1)} %shard_map.101.refs_0_), channel_id=1, source_target_pairs={{0,1},{1,0},{2,3},{3,2},{4,5},{5,4},{6,7},{7,6},{8,9},{9,8},{10,11... | collective-permute-start | bytes 393224 | tf_op jit(solution)/shard_map/ppermute | solution.py:539
  64.9 2.1 %collective-permute-start.22 = (bf16[512,256]{1,0:T(8,128)(2,1)S(1)}, bf16[512,256]{1,0:T(8,128)(2,1)S(1)}, u32[]{:S(2)}, u32[]{:S(2)}) collective-permute-start(bf16[512,256]{1,0:T(8,128)(2,1)S(1)} %shard_map.102.refs_0_), channel_id=1, source_target_pairs={{0,1},{1,0},{2,3},{3,2},{4,5},{5,4},{6,7},{7,6},{8,9},{9,8},{10,11... | collective-permute-start | bytes 786440 | tf_op jit(solution)/shard_map/ppermute | solution.py:539
  65.1 10.1 %collective-permute-start.24 = (bf16[256,512]{1,0:T(8,128)(2,1)S(1)}, bf16[256,512]{1,0:T(8,128)(2,1)S(1)}, u32[]{:S(2)}, u32[]{:S(2)}) collective-permute-start(bf16[256,512]{1,0:T(8,128)(2,1)S(1)} %shard_map.103), channel_id=1, source_target_pairs={{0,6},{2,4},{4,2},{6,0},{8,14},{10,12},{12,10},{14,8},{16,22},{18,... | collective-permute-start | bytes 786440 | tf_op jit(solution)/shard_map/ppermute | solution.py:533
  67.5 12.4 %collective-permute-start.25 = (bf16[256,512]{1,0:T(8,128)(2,1)S(1)}, bf16[256,512]{1,0:T(8,128)(2,1)S(1)}, u32[]{:S(2)}, u32[]{:S(2)}) collective-permute-start(bf16[256,512]{1,0:T(8,128)(2,1)S(1)} %get-tuple-element.127), channel_id=1, source_target_pairs={{0,2},{2,0},{4,6},{6,4},{8,10},{10,8},{12,14},{14,12},{16,18},{18,... | collective-permute-start | bytes 786440 | tf_op jit(solution)/shard_map/ppermute | solution.py:533
  69.4 10.9 %collective-permute-start.26 = (bf16[256,512]{1,0:T(8,128)(2,1)S(1)}, bf16[256,512]{1,0:T(8,128)(2,1)S(1)}, u32[]{:S(2)}, u32[]{:S(2)}) collective-permute-start(bf16[256,512]{1,0:T(8,128)(2,1)S(1)} %get-tuple-element.128), channel_id=1, source_target_pairs={{0,4},{2,6},{4,0},{6,2},{8,12},{10,14},{12,8},{14,10},{16,20},{18,... | collective-permute-start | bytes 786440 | tf_op jit(solution)/shard_map/ppermute | solution.py:533
  71.6 1.4 %collective-permute-start.23 = (bf16[256,256]{1,0:T(8,128)(2,1)S(1)}, bf16[256,256]{1,0:T(8,128)(2,1)S(1)}, u32[]{:S(2)}, u32[]{:S(2)}) collective-permute-start(bf16[256,256]{1,0:T(8,128)(2,1)S(1)} %shard_map.105.refs_0_), channel_id=1, source_target_pairs={{0,1},{1,0},{2,3},{3,2},{4,5},{5,4},{6,7},{7,6},{8,9},{9,8},{10,11... | collective-permute-start | bytes 393224 | tf_op jit(solution)/shard_map/ppermute | solution.py:539

commit v19 on v18

--- a/solution.py
+++ b/solution.py
@@ -10,7 +10,7 @@
 SPAN = 128
 LANES = 128
 EDGE = 16
-CONV_ROWS = 64
+CONV_ROWS = 128
 BF16 = jnp.bfloat16
 F32 = jnp.float32
 STACK_HINT = 40_000_000_000

time: 81.9 us -> 81.8 us (level)
  starting transfers between devices: 37.5 us -> 39.2 us
  waiting for transfers between devices: 22.8 us -> 21.3 us
    ppermute x9, starting transfers between devices: 12 us -> 13.7 us  [in_plane(): return lax.ppermute(array, 'tm', [(i, i ^ step) for i in range(times)])]
    ppermute x9, waiting for transfers between devices: 13.2 us -> 11.7 us  [in_plane(): return lax.ppermute(array, 'tm', [(i, i ^ step) for i in range(times)])]
  transfers between devices with their start and end apart: 27 -> 27, of which waited for: 10 -> 8; matrix products, arithmetic and copies ran while one was open for 1% -> 1% of each run, Pallas kernels for 18% -> 18%
where the time goes in v19:
time: 81.8 us; the launch traced here: 81.4 us
  starting transfers between devices  39.2 us (48%)
  waiting for transfers between devices  21.3 us (26%)
  Pallas kernels  18.8 us (23%)
  local copies, waits for them, and re-layouts  1.78 us (2%)
    pallas_call x17, Pallas kernels, call(): pl.pallas_call(kernel, out_shape=out_shape, in_specs=in_specs, out_specs=...  18.8 us
    ppermute x8, starting transfers between devices, between_planes(): lax.ppermute(array, 'tm', [(i, i ^ step * group) for i in range(times)])  15 us
    ppermute x9, starting transfers between devices, in_plane(): return lax.ppermute(array, 'tm', [(i, i ^ step) for i in range(times)])  13.7 us
    ppermute x9, waiting for transfers between devices, in_plane(): return lax.ppermute(array, 'tm', [(i, i ^ step) for i in range(times)])  11.7 us
    ppermute x3, starting transfers between devices, later(): lax.ppermute(array, 'tm', [(i, i + step * group) for i in range(times - s...  7.74 us
    ppermute x8, waiting for transfers between devices, between_planes(): lax.ppermute(array, 'tm', [(i, i ^ step * group) for i in range(times)])  7.41 us
  transfers between devices with their start and end apart: 27, of which 8 were waited for; matrix products, arithmetic and copies ran while one was open for 1% of the time, Pallas kernels for 18%

profile of v19, /device:TPU:0, one launch (start us, length us, event | category | flops | bytes accessed | tf_op | source)
XLA Modules:
  0.0 81.4 jit_solution(10668383530662498616)
XLA Ops:
  0.0 2.0 %shard_map.91 = (bf16[64,768]{1,0:T(8,128)(2,1)}, bf16[64,768]{1,0:T(8,128)(2,1)}, bf16[64,768]{1,0:T(8,128)(2,1)}, bf16[64,768]{1,0:T(8,128)(2,1)}, bf16[32,102...) custom-call(f32[16,256]{1,0:T(8,128)} %log_decay_ref.1, ...), custom_call_target="tpu_custom_call" | custom-call | bytes 1622016 | tf_op jit(solution)/shard_map/pallas_call | solution.py:35
  2.0 3.0 %collective-permute-start.6 = (bf16[64,768]{1,0:T(8,128)(2,1)}, bf16[64,768]{1,0:T(8,128)(2,1)S(1)}, u32[]{:S(2)}, u32[]{:S(2)}) collective-permute-start(bf16[64,768]{1,0:T(8,128)(2,1)} %get-tuple-element.77), channel_id=1, source_target_pairs={{0,2},{2,0},{4,6},{6,4},{8,10},{10,8},{12,14},{14,12},{16,18},{18,... | collective-permute-start | bytes 294920 | tf_op jit(solution)/shard_map/ppermute | solution.py:533
  5.0 1.5 %collective-permute-start.7 = (bf16[64,768]{1,0:T(8,128)(2,1)}, bf16[64,768]{1,0:T(8,128)(2,1)S(1)}, u32[]{:S(2)}, u32[]{:S(2)}) collective-permute-start(bf16[64,768]{1,0:T(8,128)(2,1)} %get-tuple-element.78), channel_id=1, source_target_pairs={{0,4},{2,6},{4,0},{6,2},{8,12},{10,14},{12,8},{14,10},{16,20},{18,... | collective-permute-start | bytes 294920 | tf_op jit(solution)/shard_map/ppermute | solution.py:533
  6.5 2.0 %collective-permute-start = (bf16[32,1024]{1,0:T(8,128)(2,1)}, bf16[32,1024]{1,0:T(8,128)(2,1)S(1)}, u32[]{:S(2)}, u32[]{:S(2)}) collective-permute-start(bf16[32,1024]{1,0:T(8,128)(2,1)} %get-tuple-element.68), channel_id=1, source_target_pairs={{0,8},{2,10},{4,12},{6,14},{8,0},{10,2},{12,4},{14,6},{16,24},{18,... | collective-permute-start | bytes 196616 | tf_op jit(solution)/shard_map/ppermute | solution.py:542
  8.5 2.6 %collective-permute-start.1 = (bf16[32,1024]{1,0:T(8,128)(2,1)}, bf16[32,1024]{1,0:T(8,128)(2,1)S(1)}, u32[]{:S(2)}, u32[]{:S(2)}) collective-permute-start(bf16[32,1024]{1,0:T(8,128)(2,1)} %get-tuple-element.69), channel_id=1, source_target_pairs={{0,16},{2,18},{4,20},{6,22},{8,24},{10,26},{12,28},{14,30},{16,0},... | collective-permute-start | bytes 196616 | tf_op jit(solution)/shard_map/ppermute | solution.py:542
  11.1 0.7 reshape.3
  12.0 0.2 collective-permute-done.8.refs_3_
  12.2 0.9 %copy-done.4 = bf16[64,768]{1,0:T(8,128)(2,1)S(1)} copy-done((bf16[64,768]{1,0:T(8,128)(2,1)S(1)}, bf16[64,768]{1,0:T(8,128)(2,1)}, u32[]{:S(2)}) %copy-start.4) | copy-done | bytes 98328
  13.2 2.7 %collective-permute-start.9 = (bf16[256,512]{1,0:T(8,128)(2,1)S(1)}, bf16[256,512]{1,0:T(8,128)(2,1)S(1)}, u32[]{:S(2)}, u32[]{:S(2)}) collective-permute-start(bf16[256,512]{1,0:T(8,128)(2,1)S(1)} %get-tuple-element.85.refs_0_), channel_id=1, source_target_pairs={{0,16},{2,18},{4,20},{6,22},{8,24},{10,26},{12,28},{14,30},{16,0},... | collective-permute-start | bytes 786440 | tf_op jit(solution)/shard_map/ppermute | solution.py:542
  15.8 1.6 %collective-permute-start.10 = (bf16[256,512]{1,0:T(8,128)(2,1)S(1)}, bf16[256,512]{1,0:T(8,128)(2,1)S(1)}, u32[]{:S(2)}, u32[]{:S(2)}) collective-permute-start(bf16[256,512]{1,0:T(8,128)(2,1)S(1)} %get-tuple-element.85.refs_0_), channel_id=1, source_target_pairs={{0,8},{2,10},{4,12},{6,14},{8,0},{10,2},{12,4},{14,6},{16,24},{18,... | collective-permute-start | bytes 786440 | tf_op jit(solution)/shard_map/ppermute | solution.py:542
  17.4 2.7 %collective-permute-done.1.refs_2_ = bf16[32,1024]{1,0:T(8,128)(2,1)S(1)} collective-permute-done((bf16[32,1024]{1,0:T(8,128)(2,1)}, bf16[32,1024]{1,0:T(8,128)(2,1)S(1)}, u32[]{:S(2)}, u32[]{:S(2)}) %collective-permute-start.1) | collective-permute-done | bytes 65568 | tf_op jit(solution)/shard_map/ppermute | solution.py:542
  20.1 0.2 shard_map.92
  20.2 1.6 %collective-permute-start.3 = (bf16[192,1024]{1,0:T(8,128)(2,1)S(1)}, bf16[192,1024]{1,0:T(8,128)(2,1)S(1)}, u32[]{:S(2)}, u32[]{:S(2)}) collective-permute-start(bf16[192,1024]{1,0:T(8,128)(2,1)S(1)} %get-tuple-element.72), channel_id=1, source_target_pairs={{0,2},{2,0},{4,6},{6,4},{8,10},{10,8},{12,14},{14,12},{16,18},{18,... | collective-permute-start | bytes 1179656 | tf_op jit(solution)/shard_map/ppermute | solution.py:533
  21.8 1.5 %collective-permute-start.4 = (bf16[192,1024]{1,0:T(8,128)(2,1)S(1)}, bf16[192,1024]{1,0:T(8,128)(2,1)S(1)}, u32[]{:S(2)}, u32[]{:S(2)}) collective-permute-start(bf16[192,1024]{1,0:T(8,128)(2,1)S(1)} %get-tuple-element.73), channel_id=1, source_target_pairs={{0,4},{2,6},{4,0},{6,2},{8,12},{10,14},{12,8},{14,10},{16,20},{18,... | collective-permute-start | bytes 1179656 | tf_op jit(solution)/shard_map/ppermute | solution.py:533
  23.3 0.5 collective-permute-start.5
  23.8 4.7 %collective-permute-done.9.refs_2_ = bf16[256,512]{1,0:T(8,128)(2,1)S(1)} collective-permute-done((bf16[256,512]{1,0:T(8,128)(2,1)S(1)}, bf16[256,512]{1,0:T(8,128)(2,1)S(1)}, u32[]{:S(2)}, u32[]{:S(2)}) %collective-permute-start.9) | collective-permute-done | bytes 262176 | tf_op jit(solution)/shard_map/ppermute | solution.py:542
  28.5 1.3 %collective-permute-start.11 = (bf16[256,512]{1,0:T(8,128)(2,1)S(1)}, bf16[256,512]{1,0:T(8,128)(2,1)S(1)}, u32[]{:S(2)}, u32[]{:S(2)}) collective-permute-start(bf16[256,512]{1,0:T(8,128)(2,1)S(1)} %collective-permute-done.9.refs_2_), channel_id=1, source_target_pairs={{8,0},{10,2},{12,4},{14,6},{16,24},{18,26},{20,28},{22,30},{9,1},{... | collective-permute-start | bytes 786440 | tf_op jit(solution)/shard_map/ppermute | solution.py:558
  29.8 0.7 collective-permute-start.12
  30.5 0.6 collective-permute-done.3.refs_1_.refs_0_
  31.1 5.4 %collective-permute-done.4.refs_2_.refs_1_ = bf16[192,1024]{1,0:T(8,128)(2,1)S(1)} collective-permute-done((bf16[192,1024]{1,0:T(8,128)(2,1)S(1)}, bf16[192,1024]{1,0:T(8,128)(2,1)S(1)}, u32[]{:S(2)}, u32[]{:S(2)}) %collective-permute-start.4) | collective-permute-done | bytes 393248 | tf_op jit(solution)/shard_map/ppermute | solution.py:533
  36.5 0.5 shard_map.93
  37.1 0.8 collective-permute-done.11.refs_3_
  37.9 3.7 %collective-permute-start.14 = (bf16[256,256]{1,0:T(8,128)(2,1)S(1)}, bf16[256,256]{1,0:T(8,128)(2,1)S(1)}, u32[]{:S(2)}, u32[]{:S(2)}) collective-permute-start(bf16[256,256]{1,0:T(8,128)(2,1)S(1)} %get-tuple-element.96.refs_0_), channel_id=1, source_target_pairs={{0,8},{2,10},{4,12},{6,14},{8,0},{10,2},{12,4},{14,6},{16,24},{18,... | collective-permute-start | bytes 393224 | tf_op jit(solution)/shard_map/ppermute | solution.py:542
  41.6 0.6 collective-permute-start.15
  42.2 1.8 %collective-permute-start.16 = (bf16[256,256]{1,0:T(8,128)(2,1)S(1)}, bf16[256,256]{1,0:T(8,128)(2,1)S(1)}, u32[]{:S(2)}, u32[]{:S(2)}) collective-permute-start(bf16[256,256]{1,0:T(8,128)(2,1)S(1)} %get-tuple-element.96.refs_0_), channel_id=1, source_target_pairs={{0,24},{2,26},{4,28},{6,30},{8,16},{10,18},{12,20},{14,22},{16,8},... | collective-permute-start | bytes 393224 | tf_op jit(solution)/shard_map/ppermute | solution.py:542
  43.9 0.1 shard_map.95
  44.0 2.8 %shard_map.96 = (bf16[1152,1024]{1,0:T(8,128)(2,1)S(1)}, bf16[1152,256]{1,0:T(8,128)(2,1)S(1)}, bf16[1152,128]{1,0:T(8,128)(2,1)S(1)}, bf16[1152,128]{1,0:T(8,12...) custom-call(s32[8]{0:T(128)S(1)} %copy-done.2, ...), custom_call_target="tpu_custom_call" | custom-call | tf_op jit(solution)/shard_map/pallas_call | solution.py:35
  46.8 3.0 %collective-permute-start.17 = (bf16[144,256]{1,0:T(8,128)(2,1)S(1)}, bf16[144,256]{1,0:T(8,128)(2,1)S(1)}, u32[]{:S(2)}, u32[]{:S(2)}) collective-permute-start(bf16[144,256]{1,0:T(8,128)(2,1)S(1)} %get-tuple-element.112), channel_id=1, source_target_pairs={{0,8},{2,10},{4,12},{6,14},{8,16},{10,18},{12,20},{14,22},{16,24},... | collective-permute-start | bytes 221192 | tf_op jit(solution)/shard_map/ppermute | solution.py:536
  49.9 3.4 %collective-permute-start.18 = (bf16[144,256]{1,0:T(8,128)(2,1)S(1)}, bf16[144,256]{1,0:T(8,128)(2,1)S(1)}, u32[]{:S(2)}, u32[]{:S(2)}) collective-permute-start(bf16[144,256]{1,0:T(8,128)(2,1)S(1)} %get-tuple-element.112), channel_id=1, source_target_pairs={{0,16},{2,18},{4,20},{6,22},{8,24},{10,26},{12,28},{14,30},{1,17},... | collective-permute-start | bytes 221192 | tf_op jit(solution)/shard_map/ppermute | solution.py:536
  53.3 1.3 %collective-permute-start.19 = (bf16[144,256]{1,0:T(8,128)(2,1)S(1)}, bf16[144,256]{1,0:T(8,128)(2,1)S(1)}, u32[]{:S(2)}, u32[]{:S(2)}) collective-permute-start(bf16[144,256]{1,0:T(8,128)(2,1)S(1)} %get-tuple-element.112), channel_id=1, source_target_pairs={{0,24},{2,26},{4,28},{6,30},{1,25},{3,27},{5,29},{7,31}} | collective-permute-start | bytes 221192 | tf_op jit(solution)/shard_map/ppermute | solution.py:536
  54.7 1.9 %shard_map.98 = (f32[1152,256]{1,0:T(8,128)S(1)}, f32[1152,256]{1,0:T(8,128)S(1)}) custom-call(bf16[1152,256]{1,0:T(8,128)(2,1)S(1)} %get-tuple-element.103.x_ref, bf16[1152,128]{1,0:T(8,128)(2,1)S(1)} %get-tuple-element.104.b_ref, bf16[1152,128]{1,0:T(8,128)(2,1)S(1)} %get-tuple-element.102.c_ref, f32[216,128]{1,0:T(8,128)S(1)} %get-tuple-element.105.rows_ref), custom_call_target="tpu_custom_call" | custom-call | flops 134217728 | bytes 3649536 | tf_op jit(solution)/shard_map/pallas_call | solution.py:35
  56.6 0.8 %shard_map.99.silu_ref = f32[1152,256]{1,0:T(8,128)S(1)} custom-call(f32[1,1024]{1,0:T(1,128)S(1)} %bitcast.2, bf16[1152,1024]{1,0:T(8,128)(2,1)S(1)} %get-tuple-element.110.frames_ref, bf16[1024,256]{1,0:T(8,128)(2,1)S(1)} %get-tuple-element.111.weight_ref), custom_call_target="tpu_custom_call" | custom-call | flops 536870912 | bytes 4067328 | tf_op jit(solution)/shard_map/pallas_call | solution.py:35
  57.5 0.7 shard_map.100.gated_ref
  58.3 0.1 copy-done.1
  58.4 1.5 %shard_map.101.refs_0_ = bf16[256,256]{1,0:T(8,128)(2,1)S(1)} custom-call(s32[8]{0:T(128)S(1)} %copy-done.2, f32[31,1024]{1,0:T(8,128)S(1)} %copy-done.1, bf16[1152,256]{1,0:T(8,128)(2,1)S(1)} %shard_map.100.gated_ref), custom_call_target="tpu_custom_call" | custom-call | flops 4063232 | bytes 847904 | tf_op jit(solution)/shard_map/pallas_call | solution.py:35
  59.9 0.4 collective-permute-start.20
  60.4 3.3 %shard_map.102.refs_0_ = bf16[512,256]{1,0:T(8,128)(2,1)S(1)} custom-call(s32[8]{0:T(128)S(1)} %copy-done.2, f32[31,1024]{1,0:T(8,128)S(1)} %copy-done.1, bf16[1152,256]{1,0:T(8,128)(2,1)S(1)} %shard_map.100.gated_ref), custom_call_target="tpu_custom_call" | custom-call | flops 8126464 | bytes 978976 | tf_op jit(solution)/shard_map/pallas_call | solution.py:35
  63.7 0.3 shard_map.103
  64.0 0.2 collective-permute-start.22
  64.2 3.6 %collective-permute-start.24 = (bf16[256,512]{1,0:T(8,128)(2,1)S(1)}, bf16[256,512]{1,0:T(8,128)(2,1)S(1)}, u32[]{:S(2)}, u32[]{:S(2)}) collective-permute-start(bf16[256,512]{1,0:T(8,128)(2,1)S(1)} %shard_map.103), channel_id=1, source_target_pairs={{0,6},{2,4},{4,2},{6,0},{8,14},{10,12},{12,10},{14,8},{16,22},{18,... | collective-permute-start | bytes 786440 | tf_op jit(solution)/shard_map/ppermute | solution.py:533
  67.9 0.5 shard_map.104
  68.3 0.7 collective-permute-start.25
  69.0 1.3 %collective-permute-start.26 = (bf16[256,512]{1,0:T(8,128)(2,1)S(1)}, bf16[256,512]{1,0:T(8,128)(2,1)S(1)}, u32[]{:S(2)}, u32[]{:S(2)}) collective-permute-start(bf16[256,512]{1,0:T(8,128)(2,1)S(1)} %get-tuple-element.128), channel_id=1, source_target_pairs={{0,4},{2,6},{4,0},{6,2},{8,12},{10,14},{12,8},{14,10},{16,20},{18,... | collective-permute-start | bytes 786440 | tf_op jit(solution)/shard_map/ppermute | solution.py:533
  70.3 3.1 %shard_map.105.refs_0_ = bf16[256,256]{1,0:T(8,128)(2,1)S(1)} custom-call(s32[8]{0:T(128)S(1)} %copy-done.2, f32[31,1024]{1,0:T(8,128)S(1)} %copy-done.1, bf16[1152,256]{1,0:T(8,128)(2,1)S(1)} %shard_map.100.gated_ref), custom_call_target="tpu_custom_call" | custom-call | flops 4063232 | bytes 847904 | tf_op jit(solution)/shard_map/pallas_call | solution.py:35
  73.5 1.3 %collective-permute-done.23.refs_1_ = bf16[256,256]{1,0:T(8,128)(2,1)S(1)} collective-permute-done((bf16[256,256]{1,0:T(8,128)(2,1)S(1)}, bf16[256,256]{1,0:T(8,128)(2,1)S(1)}, u32[]{:S(2)}, u32[]{:S(2)}) %collective-permute-start.23) | collective-permute-done | bytes 131104 | tf_op jit(solution)/shard_map/ppermute | solution.py:539
  74.8 0.3 shard_map.106.own_ref
  75.2 5.4 %collective-permute-done.25.refs_1_ = bf16[256,512]{1,0:T(8,128)(2,1)S(1)} collective-permute-done((bf16[256,512]{1,0:T(8,128)(2,1)S(1)}, bf16[256,512]{1,0:T(8,128)(2,1)S(1)}, u32[]{:S(2)}, u32[]{:S(2)}) %collective-permute-start.25) | collective-permute-done | bytes 262176 | tf_op jit(solution)/shard_map/ppermute | solution.py:533
  80.6 0.8 %shard_map.107 = bf16[256,512]{1,0:T(8,128)(2,1)} custom-call(f32[256,512]{1,0:T(8,128)S(1)} %shard_map.106.own_ref, bf16[256,512]{1,0:T(8,128)(2,1)S(1)} %collective-permute-done.24.refs_0_, bf16[256,512]{1,0:T(8,128)(2,1)S(1)} %collective-permute-done.25.refs_1_, bf16[256,512]{1,0:T(8,128)(2,1)S(1)} %collective-permute-done.26.refs_2_), custom_call_target="tpu_custom_call" | custom-call | bytes 1572864 | tf_op jit(solution)/shard_map/pallas_call | solution.py:35
  (37 shorter events, 0.5 us)
Async XLA Ops:
  2.0 9.9 %collective-permute-start.6 = (bf16[64,768]{1,0:T(8,128)(2,1)}, bf16[64,768]{1,0:T(8,128)(2,1)S(1)}, u32[]{:S(2)}, u32[]{:S(2)}) collective-permute-start(bf16[64,768]{1,0:T(8,128)(2,1)} %get-tuple-element.77), channel_id=1, source_target_pairs={{0,2},{2,0},{4,6},{6,4},{8,10},{10,8},{12,14},{14,12},{16,18},{18,... | collective-permute-start | bytes 294920 | tf_op jit(solution)/shard_map/ppermute | solution.py:533
  5.0 7.0 %collective-permute-start.7 = (bf16[64,768]{1,0:T(8,128)(2,1)}, bf16[64,768]{1,0:T(8,128)(2,1)S(1)}, u32[]{:S(2)}, u32[]{:S(2)}) collective-permute-start(bf16[64,768]{1,0:T(8,128)(2,1)} %get-tuple-element.78), channel_id=1, source_target_pairs={{0,4},{2,6},{4,0},{6,2},{8,12},{10,14},{12,8},{14,10},{16,20},{18,... | collective-permute-start | bytes 294920 | tf_op jit(solution)/shard_map/ppermute | solution.py:533
  6.5 5.7 %collective-permute-start.8 = (bf16[64,768]{1,0:T(8,128)(2,1)}, bf16[64,768]{1,0:T(8,128)(2,1)S(1)}, u32[]{:S(2)}, u32[]{:S(2)}) collective-permute-start(bf16[64,768]{1,0:T(8,128)(2,1)} %get-tuple-element.79), channel_id=1, source_target_pairs={{0,6},{2,4},{4,2},{6,0},{8,14},{10,12},{12,10},{14,8},{16,22},{18,... | collective-permute-start | bytes 294920 | tf_op jit(solution)/shard_map/ppermute | solution.py:533
  6.5 10.9 %collective-permute-start = (bf16[32,1024]{1,0:T(8,128)(2,1)}, bf16[32,1024]{1,0:T(8,128)(2,1)S(1)}, u32[]{:S(2)}, u32[]{:S(2)}) collective-permute-start(bf16[32,1024]{1,0:T(8,128)(2,1)} %get-tuple-element.68), channel_id=1, source_target_pairs={{0,8},{2,10},{4,12},{6,14},{8,0},{10,2},{12,4},{14,6},{16,24},{18,... | collective-permute-start | bytes 196616 | tf_op jit(solution)/shard_map/ppermute | solution.py:542
  8.5 11.5 %collective-permute-start.1 = (bf16[32,1024]{1,0:T(8,128)(2,1)}, bf16[32,1024]{1,0:T(8,128)(2,1)S(1)}, u32[]{:S(2)}, u32[]{:S(2)}) collective-permute-start(bf16[32,1024]{1,0:T(8,128)(2,1)} %get-tuple-element.69), channel_id=1, source_target_pairs={{0,16},{2,18},{4,20},{6,22},{8,24},{10,26},{12,28},{14,30},{16,0},... | collective-permute-start | bytes 196616 | tf_op jit(solution)/shard_map/ppermute | solution.py:542
  11.9 8.2 %collective-permute-start.2 = (bf16[32,1024]{1,0:T(8,128)(2,1)}, bf16[32,1024]{1,0:T(8,128)(2,1)S(1)}, u32[]{:S(2)}, u32[]{:S(2)}) collective-permute-start(bf16[32,1024]{1,0:T(8,128)(2,1)} %get-tuple-element.70), channel_id=1, source_target_pairs={{0,24},{2,26},{4,28},{6,30},{8,16},{10,18},{12,20},{14,22},{16,8},... | collective-permute-start | bytes 196616 | tf_op jit(solution)/shard_map/ppermute | solution.py:542
  12.2 0.9 %copy-start.4 = (bf16[64,768]{1,0:T(8,128)(2,1)S(1)}, bf16[64,768]{1,0:T(8,128)(2,1)}, u32[]{:S(2)}) copy-start(bf16[64,768]{1,0:T(8,128)(2,1)} %get-tuple-element.76.refs_0_) | copy-start | bytes 294916
  13.1 7.0 %copy-start = (bf16[256,1024]{1,0:T(8,128)(2,1)S(1)}, bf16[256,1024]{1,0:T(8,128)(2,1)}, u32[]{:S(2)}) copy-start(bf16[256,1024]{1,0:T(8,128)(2,1)} %own_ref.1) | copy-start | bytes 1572868
  13.1 7.0 %copy-start.5 = (bf16[32,1024]{1,0:T(8,128)(2,1)S(1)}, bf16[32,1024]{1,0:T(8,128)(2,1)}, u32[]{:S(2)}) copy-start(bf16[32,1024]{1,0:T(8,128)(2,1)} %get-tuple-element.67.refs_0_) | copy-start | bytes 196612
  13.2 15.4 %collective-permute-start.9 = (bf16[256,512]{1,0:T(8,128)(2,1)S(1)}, bf16[256,512]{1,0:T(8,128)(2,1)S(1)}, u32[]{:S(2)}, u32[]{:S(2)}) collective-permute-start(bf16[256,512]{1,0:T(8,128)(2,1)S(1)} %get-tuple-element.85.refs_0_), channel_id=1, source_target_pairs={{0,16},{2,18},{4,20},{6,22},{8,24},{10,26},{12,28},{14,30},{16,0},... | collective-permute-start | bytes 786440 | tf_op jit(solution)/shard_map/ppermute | solution.py:542
  15.8 12.7 %collective-permute-start.10 = (bf16[256,512]{1,0:T(8,128)(2,1)S(1)}, bf16[256,512]{1,0:T(8,128)(2,1)S(1)}, u32[]{:S(2)}, u32[]{:S(2)}) collective-permute-start(bf16[256,512]{1,0:T(8,128)(2,1)S(1)} %get-tuple-element.85.refs_0_), channel_id=1, source_target_pairs={{0,8},{2,10},{4,12},{6,14},{8,0},{10,2},{12,4},{14,6},{16,24},{18,... | collective-permute-start | bytes 786440 | tf_op jit(solution)/shard_map/ppermute | solution.py:542
  20.2 10.9 %collective-permute-start.3 = (bf16[192,1024]{1,0:T(8,128)(2,1)S(1)}, bf16[192,1024]{1,0:T(8,128)(2,1)S(1)}, u32[]{:S(2)}, u32[]{:S(2)}) collective-permute-start(bf16[192,1024]{1,0:T(8,128)(2,1)S(1)} %get-tuple-element.72), channel_id=1, source_target_pairs={{0,2},{2,0},{4,6},{6,4},{8,10},{10,8},{12,14},{14,12},{16,18},{18,... | collective-permute-start | bytes 1179656 | tf_op jit(solution)/shard_map/ppermute | solution.py:533
  21.8 14.7 %collective-permute-start.4 = (bf16[192,1024]{1,0:T(8,128)(2,1)S(1)}, bf16[192,1024]{1,0:T(8,128)(2,1)S(1)}, u32[]{:S(2)}, u32[]{:S(2)}) collective-permute-start(bf16[192,1024]{1,0:T(8,128)(2,1)S(1)} %get-tuple-element.73), channel_id=1, source_target_pairs={{0,4},{2,6},{4,0},{6,2},{8,12},{10,14},{12,8},{14,10},{16,20},{18,... | collective-permute-start | bytes 1179656 | tf_op jit(solution)/shard_map/ppermute | solution.py:533
  23.3 13.2 %collective-permute-start.5 = (bf16[192,1024]{1,0:T(8,128)(2,1)S(1)}, bf16[192,1024]{1,0:T(8,128)(2,1)S(1)}, u32[]{:S(2)}, u32[]{:S(2)}) collective-permute-start(bf16[192,1024]{1,0:T(8,128)(2,1)S(1)} %get-tuple-element.74), channel_id=1, source_target_pairs={{0,6},{2,4},{4,2},{6,0},{8,14},{10,12},{12,10},{14,8},{16,22},{18,... | collective-permute-start | bytes 1179656 | tf_op jit(solution)/shard_map/ppermute | solution.py:533
  28.5 9.4 %collective-permute-start.11 = (bf16[256,512]{1,0:T(8,128)(2,1)S(1)}, bf16[256,512]{1,0:T(8,128)(2,1)S(1)}, u32[]{:S(2)}, u32[]{:S(2)}) collective-permute-start(bf16[256,512]{1,0:T(8,128)(2,1)S(1)} %collective-permute-done.9.refs_2_), channel_id=1, source_target_pairs={{8,0},{10,2},{12,4},{14,6},{16,24},{18,26},{20,28},{22,30},{9,1},{... | collective-permute-start | bytes 786440 | tf_op jit(solution)/shard_map/ppermute | solution.py:558
  29.8 8.1 %collective-permute-start.12 = (bf16[256,512]{1,0:T(8,128)(2,1)S(1)}, bf16[256,512]{1,0:T(8,128)(2,1)S(1)}, u32[]{:S(2)}, u32[]{:S(2)}) collective-permute-start(bf16[256,512]{1,0:T(8,128)(2,1)S(1)} %get-tuple-element.85.refs_0_), channel_id=1, source_target_pairs={{8,16},{10,18},{12,20},{14,22},{16,8},{18,10},{20,12},{22,14},{9,1... | collective-permute-start | bytes 786440 | tf_op jit(solution)/shard_map/ppermute | solution.py:559
  37.0 7.0 %collective-permute-start.13 = (bf16[512,1024]{1,0:T(8,128)(2,1)S(1)}, bf16[512,1024]{1,0:T(8,128)(2,1)S(1)}, u32[]{:S(2)}, u32[]{:S(2)}) collective-permute-start(bf16[512,1024]{1,0:T(8,128)(2,1)S(1)} %get-tuple-element.92), channel_id=1, source_target_pairs={{0,1},{1,0},{2,3},{3,2},{4,5},{5,4},{6,7},{7,6},{8,9},{9,8},{10,11... | collective-permute-start | bytes 3145736 | tf_op jit(solution)/shard_map/ppermute | solution.py:539
  37.9 6.1 %copy-start.2 = (s32[8]{0:T(128)S(1)}, s32[8]{0:T(128)}, u32[]{:S(2)}) copy-start(s32[8]{0:T(128)} %len_ref.7) | copy-start | bytes 100
  37.9 15.4 %collective-permute-start.14 = (bf16[256,256]{1,0:T(8,128)(2,1)S(1)}, bf16[256,256]{1,0:T(8,128)(2,1)S(1)}, u32[]{:S(2)}, u32[]{:S(2)}) collective-permute-start(bf16[256,256]{1,0:T(8,128)(2,1)S(1)} %get-tuple-element.96.refs_0_), channel_id=1, source_target_pairs={{0,8},{2,10},{4,12},{6,14},{8,0},{10,2},{12,4},{14,6},{16,24},{18,... | collective-permute-start | bytes 393224 | tf_op jit(solution)/shard_map/ppermute | solution.py:542
  41.6 13.0 %collective-permute-start.15 = (bf16[256,256]{1,0:T(8,128)(2,1)S(1)}, bf16[256,256]{1,0:T(8,128)(2,1)S(1)}, u32[]{:S(2)}, u32[]{:S(2)}) collective-permute-start(bf16[256,256]{1,0:T(8,128)(2,1)S(1)} %get-tuple-element.96.refs_0_), channel_id=1, source_target_pairs={{0,16},{2,18},{4,20},{6,22},{8,24},{10,26},{12,28},{14,30},{16,0},... | collective-permute-start | bytes 393224 | tf_op jit(solution)/shard_map/ppermute | solution.py:542
  42.2 12.5 %collective-permute-start.16 = (bf16[256,256]{1,0:T(8,128)(2,1)S(1)}, bf16[256,256]{1,0:T(8,128)(2,1)S(1)}, u32[]{:S(2)}, u32[]{:S(2)}) collective-permute-start(bf16[256,256]{1,0:T(8,128)(2,1)S(1)} %get-tuple-element.96.refs_0_), channel_id=1, source_target_pairs={{0,24},{2,26},{4,28},{6,30},{8,16},{10,18},{12,20},{14,22},{16,8},... | collective-permute-start | bytes 393224 | tf_op jit(solution)/shard_map/ppermute | solution.py:542
  46.8 9.8 %copy-start.3 = (f32[1024]{0:T(1024)S(1)}, f32[1024]{0:T(1024)}, u32[]{:S(2)}) copy-start(f32[1024]{0:T(1024)} %param.14) | copy-start | bytes 12292
  46.8 10.6 %collective-permute-start.17 = (bf16[144,256]{1,0:T(8,128)(2,1)S(1)}, bf16[144,256]{1,0:T(8,128)(2,1)S(1)}, u32[]{:S(2)}, u32[]{:S(2)}) collective-permute-start(bf16[144,256]{1,0:T(8,128)(2,1)S(1)} %get-tuple-element.112), channel_id=1, source_target_pairs={{0,8},{2,10},{4,12},{6,14},{8,16},{10,18},{12,20},{14,22},{16,24},... | collective-permute-start | bytes 221192 | tf_op jit(solution)/shard_map/ppermute | solution.py:536
  49.9 7.6 %collective-permute-start.18 = (bf16[144,256]{1,0:T(8,128)(2,1)S(1)}, bf16[144,256]{1,0:T(8,128)(2,1)S(1)}, u32[]{:S(2)}, u32[]{:S(2)}) collective-permute-start(bf16[144,256]{1,0:T(8,128)(2,1)S(1)} %get-tuple-element.112), channel_id=1, source_target_pairs={{0,16},{2,18},{4,20},{6,22},{8,24},{10,26},{12,28},{14,30},{1,17},... | collective-permute-start | bytes 221192 | tf_op jit(solution)/shard_map/ppermute | solution.py:536
  53.3 4.2 %collective-permute-start.19 = (bf16[144,256]{1,0:T(8,128)(2,1)S(1)}, bf16[144,256]{1,0:T(8,128)(2,1)S(1)}, u32[]{:S(2)}, u32[]{:S(2)}) collective-permute-start(bf16[144,256]{1,0:T(8,128)(2,1)S(1)} %get-tuple-element.112), channel_id=1, source_target_pairs={{0,24},{2,26},{4,28},{6,30},{1,25},{3,27},{5,29},{7,31}} | collective-permute-start | bytes 221192 | tf_op jit(solution)/shard_map/ppermute | solution.py:536
  57.5 0.9 %copy-start.1 = (f32[31,1024]{1,0:T(8,128)S(1)}, f32[31,1024]{1,0:T(8,128)}, u32[]{:S(2)}) copy-start(f32[31,1024]{1,0:T(8,128)} %taps_ref.5) | copy-start | bytes 380932
  58.2 5.5 %collective-permute-start.21 = (bf16[512,256]{1,0:T(8,128)(2,1)S(1)}, bf16[512,256]{1,0:T(8,128)(2,1)S(1)}, u32[]{:S(2)}, u32[]{:S(2)}) collective-permute-start(bf16[512,256]{1,0:T(8,128)(2,1)S(1)} %get-tuple-element.116), channel_id=1, source_target_pairs={{0,1},{1,0},{2,3},{3,2},{4,5},{5,4},{6,7},{7,6},{8,9},{9,8},{10,11... | collective-permute-start | bytes 786440 | tf_op jit(solution)/shard_map/ppermute | solution.py:539
  59.9 3.7 %collective-permute-start.20 = (bf16[256,256]{1,0:T(8,128)(2,1)S(1)}, bf16[256,256]{1,0:T(8,128)(2,1)S(1)}, u32[]{:S(2)}, u32[]{:S(2)}) collective-permute-start(bf16[256,256]{1,0:T(8,128)(2,1)S(1)} %shard_map.101.refs_0_), channel_id=1, source_target_pairs={{0,1},{1,0},{2,3},{3,2},{4,5},{5,4},{6,7},{7,6},{8,9},{9,8},{10,11... | collective-permute-start | bytes 393224 | tf_op jit(solution)/shard_map/ppermute | solution.py:539
  64.0 3.9 %collective-permute-start.22 = (bf16[512,256]{1,0:T(8,128)(2,1)S(1)}, bf16[512,256]{1,0:T(8,128)(2,1)S(1)}, u32[]{:S(2)}, u32[]{:S(2)}) collective-permute-start(bf16[512,256]{1,0:T(8,128)(2,1)S(1)} %shard_map.102.refs_0_), channel_id=1, source_target_pairs={{0,1},{1,0},{2,3},{3,2},{4,5},{5,4},{6,7},{7,6},{8,9},{9,8},{10,11... | collective-permute-start | bytes 786440 | tf_op jit(solution)/shard_map/ppermute | solution.py:539
  64.2 11.0 %collective-permute-start.24 = (bf16[256,512]{1,0:T(8,128)(2,1)S(1)}, bf16[256,512]{1,0:T(8,128)(2,1)S(1)}, u32[]{:S(2)}, u32[]{:S(2)}) collective-permute-start(bf16[256,512]{1,0:T(8,128)(2,1)S(1)} %shard_map.103), channel_id=1, source_target_pairs={{0,6},{2,4},{4,2},{6,0},{8,14},{10,12},{12,10},{14,8},{16,22},{18,... | collective-permute-start | bytes 786440 | tf_op jit(solution)/shard_map/ppermute | solution.py:533
  68.3 12.2 %collective-permute-start.25 = (bf16[256,512]{1,0:T(8,128)(2,1)S(1)}, bf16[256,512]{1,0:T(8,128)(2,1)S(1)}, u32[]{:S(2)}, u32[]{:S(2)}) collective-permute-start(bf16[256,512]{1,0:T(8,128)(2,1)S(1)} %get-tuple-element.127), channel_id=1, source_target_pairs={{0,2},{2,0},{4,6},{6,4},{8,10},{10,8},{12,14},{14,12},{16,18},{18,... | collective-permute-start | bytes 786440 | tf_op jit(solution)/shard_map/ppermute | solution.py:533
  69.0 11.6 %collective-permute-start.26 = (bf16[256,512]{1,0:T(8,128)(2,1)S(1)}, bf16[256,512]{1,0:T(8,128)(2,1)S(1)}, u32[]{:S(2)}, u32[]{:S(2)}) collective-permute-start(bf16[256,512]{1,0:T(8,128)(2,1)S(1)} %get-tuple-element.128), channel_id=1, source_target_pairs={{0,4},{2,6},{4,0},{6,2},{8,12},{10,14},{12,8},{14,10},{16,20},{18,... | collective-permute-start | bytes 786440 | tf_op jit(solution)/shard_map/ppermute | solution.py:533
  73.4 1.4 %collective-permute-start.23 = (bf16[256,256]{1,0:T(8,128)(2,1)S(1)}, bf16[256,256]{1,0:T(8,128)(2,1)S(1)}, u32[]{:S(2)}, u32[]{:S(2)}) collective-permute-start(bf16[256,256]{1,0:T(8,128)(2,1)S(1)} %shard_map.105.refs_0_), channel_id=1, source_target_pairs={{0,1},{1,0},{2,3},{3,2},{4,5},{5,4},{6,7},{7,6},{8,9},{9,8},{10,11... | collective-permute-start | bytes 393224 | tf_op jit(solution)/shard_map/ppermute | solution.py:539

commit v20 on v18

--- a/solution.py
+++ b/solution.py
@@ -589,6 +589,7 @@
         flops=STACK_HINT,
         smem=0,
     )
+    xz_stack, pieces = lax.optimization_barrier((xz_stack, pieces))
     xz_pieces = along_planes([xz_stack] * planes)
     xz_pieces, out_stack = lax.optimization_barrier((xz_pieces, out_stack))
     out_pieces = [out_stack] + [between_planes(out_stack, step) for step in range(1, planes)]

time: 81.9 us -> 81.6 us (level)
  waiting for transfers between devices: 22.8 us -> 27 us
  starting transfers between devices: 37.5 us -> 34.2 us
    ppermute x8, waiting for transfers between devices: 7.41 us -> 12.2 us  [between_planes(): lax.ppermute(array, 'tm', [(i, i ^ step * group) for i in range(times)])]
    ppermute x8, starting transfers between devices: 15 us -> 11.7 us  [between_planes(): lax.ppermute(array, 'tm', [(i, i ^ step * group) for i in range(times)])]
    ppermute x9, waiting for transfers between devices: 13.2 us -> 12.2 us  [in_plane(): return lax.ppermute(array, 'tm', [(i, i ^ step) for i in range(times)])]
  transfers between devices with their start and end apart: 27 -> 27, of which waited for: 10 -> 11; matrix products, arithmetic and copies ran while one was open for 1% -> 1% of each run, Pallas kernels for 18% -> 18%
where the time goes in v20:
time: 81.6 us; the launch traced here: 81.4 us
  starting transfers between devices  34.2 us (42%)
  waiting for transfers between devices  27 us (33%)
  Pallas kernels  18.1 us (22%)
  local copies, waits for them, and re-layouts  1.78 us (2%)
    pallas_call x17, Pallas kernels, call(): pl.pallas_call(kernel, out_shape=out_shape, in_specs=in_specs, out_specs=...  18.1 us
    ppermute x9, starting transfers between devices, in_plane(): return lax.ppermute(array, 'tm', [(i, i ^ step) for i in range(times)])  12.6 us
    ppermute x9, waiting for transfers between devices, in_plane(): return lax.ppermute(array, 'tm', [(i, i ^ step) for i in range(times)])  12.2 us
    ppermute x8, waiting for transfers between devices, between_planes(): lax.ppermute(array, 'tm', [(i, i ^ step * group) for i in range(times)])  12.2 us
    ppermute x8, starting transfers between devices, between_planes(): lax.ppermute(array, 'tm', [(i, i ^ step * group) for i in range(times)])  11.7 us
    ppermute x3, starting transfers between devices, later(): lax.ppermute(array, 'tm', [(i, i + step * group) for i in range(times - s...  7.14 us
  transfers between devices with their start and end apart: 27, of which 11 were waited for; matrix products, arithmetic and copies ran while one was open for 1% of the time, Pallas kernels for 18%

profile of v20, /device:TPU:0, one launch (start us, length us, event | category | flops | bytes accessed | tf_op | source)
XLA Modules:
  0.0 81.4 jit_solution(3756633161504841532)
XLA Ops:
  0.0 2.0 %shard_map.91 = (bf16[64,768]{1,0:T(8,128)(2,1)}, bf16[64,768]{1,0:T(8,128)(2,1)}, bf16[64,768]{1,0:T(8,128)(2,1)}, bf16[64,768]{1,0:T(8,128)(2,1)}, bf16[32,102...) custom-call(f32[16,256]{1,0:T(8,128)} %log_decay_ref.1, ...), custom_call_target="tpu_custom_call" | custom-call | bytes 1622016 | tf_op jit(solution)/shard_map/pallas_call | solution.py:35
  2.0 3.0 %collective-permute-start = (bf16[64,768]{1,0:T(8,128)(2,1)}, bf16[64,768]{1,0:T(8,128)(2,1)S(1)}, u32[]{:S(2)}, u32[]{:S(2)}) collective-permute-start(bf16[64,768]{1,0:T(8,128)(2,1)} %get-tuple-element.73), channel_id=1, source_target_pairs={{0,2},{2,0},{4,6},{6,4},{8,10},{10,8},{12,14},{14,12},{16,18},{18,... | collective-permute-start | bytes 294920 | tf_op jit(solution)/shard_map/ppermute | solution.py:533
  5.0 1.5 %collective-permute-start.1 = (bf16[64,768]{1,0:T(8,128)(2,1)}, bf16[64,768]{1,0:T(8,128)(2,1)S(1)}, u32[]{:S(2)}, u32[]{:S(2)}) collective-permute-start(bf16[64,768]{1,0:T(8,128)(2,1)} %get-tuple-element.74), channel_id=1, source_target_pairs={{0,4},{2,6},{4,0},{6,2},{8,12},{10,14},{12,8},{14,10},{16,20},{18,... | collective-permute-start | bytes 294920 | tf_op jit(solution)/shard_map/ppermute | solution.py:533
  6.5 2.0 %collective-permute-start.3 = (bf16[32,1024]{1,0:T(8,128)(2,1)}, bf16[32,1024]{1,0:T(8,128)(2,1)S(1)}, u32[]{:S(2)}, u32[]{:S(2)}) collective-permute-start(bf16[32,1024]{1,0:T(8,128)(2,1)} %get-tuple-element.78), channel_id=1, source_target_pairs={{0,8},{2,10},{4,12},{6,14},{8,0},{10,2},{12,4},{14,6},{16,24},{18,... | collective-permute-start | bytes 196616 | tf_op jit(solution)/shard_map/ppermute | solution.py:542
  8.5 2.6 %collective-permute-start.4 = (bf16[32,1024]{1,0:T(8,128)(2,1)}, bf16[32,1024]{1,0:T(8,128)(2,1)S(1)}, u32[]{:S(2)}, u32[]{:S(2)}) collective-permute-start(bf16[32,1024]{1,0:T(8,128)(2,1)} %get-tuple-element.79), channel_id=1, source_target_pairs={{0,16},{2,18},{4,20},{6,22},{8,24},{10,26},{12,28},{14,30},{16,0},... | collective-permute-start | bytes 196616 | tf_op jit(solution)/shard_map/ppermute | solution.py:542
  11.1 0.7 reshape.3
  12.0 0.2 collective-permute-done.2.refs_3_
  12.2 0.9 %copy-done.4 = bf16[64,768]{1,0:T(8,128)(2,1)S(1)} copy-done((bf16[64,768]{1,0:T(8,128)(2,1)S(1)}, bf16[64,768]{1,0:T(8,128)(2,1)}, u32[]{:S(2)}) %copy-start.4) | copy-done | bytes 98328
  13.2 2.7 %collective-permute-done.4.refs_2_ = bf16[32,1024]{1,0:T(8,128)(2,1)S(1)} collective-permute-done((bf16[32,1024]{1,0:T(8,128)(2,1)}, bf16[32,1024]{1,0:T(8,128)(2,1)S(1)}, u32[]{:S(2)}, u32[]{:S(2)}) %collective-permute-start.4) | collective-permute-done | bytes 65568 | tf_op jit(solution)/shard_map/ppermute | solution.py:542
  15.9 2.3 %collective-permute-done.5.refs_3_ = bf16[32,1024]{1,0:T(8,128)(2,1)S(1)} collective-permute-done((bf16[32,1024]{1,0:T(8,128)(2,1)}, bf16[32,1024]{1,0:T(8,128)(2,1)S(1)}, u32[]{:S(2)}, u32[]{:S(2)}) %collective-permute-start.5) | collective-permute-done | bytes 65568 | tf_op jit(solution)/shard_map/ppermute | solution.py:542
  18.2 0.2 collective-permute-start.9
  18.4 0.8 collective-permute-start.10
  19.2 0.2 shard_map.93
  19.4 2.0 %collective-permute-start.6 = (bf16[192,1024]{1,0:T(8,128)(2,1)S(1)}, bf16[192,1024]{1,0:T(8,128)(2,1)S(1)}, u32[]{:S(2)}, u32[]{:S(2)}) collective-permute-start(bf16[192,1024]{1,0:T(8,128)(2,1)S(1)} %get-tuple-element.86), channel_id=1, source_target_pairs={{0,2},{2,0},{4,6},{6,4},{8,10},{10,8},{12,14},{14,12},{16,18},{18,... | collective-permute-start | bytes 1179656 | tf_op jit(solution)/shard_map/ppermute | solution.py:533
  21.3 1.5 %collective-permute-start.7 = (bf16[192,1024]{1,0:T(8,128)(2,1)S(1)}, bf16[192,1024]{1,0:T(8,128)(2,1)S(1)}, u32[]{:S(2)}, u32[]{:S(2)}) collective-permute-start(bf16[192,1024]{1,0:T(8,128)(2,1)S(1)} %get-tuple-element.87), channel_id=1, source_target_pairs={{0,4},{2,6},{4,0},{6,2},{8,12},{10,14},{12,8},{14,10},{16,20},{18,... | collective-permute-start | bytes 1179656 | tf_op jit(solution)/shard_map/ppermute | solution.py:533
  22.9 6.8 %collective-permute-done.9.refs_2_ = bf16[256,512]{1,0:T(8,128)(2,1)S(1)} collective-permute-done((bf16[256,512]{1,0:T(8,128)(2,1)S(1)}, bf16[256,512]{1,0:T(8,128)(2,1)S(1)}, u32[]{:S(2)}, u32[]{:S(2)}) %collective-permute-start.9) | collective-permute-done | bytes 262176 | tf_op jit(solution)/shard_map/ppermute | solution.py:542
  29.7 0.3 collective-permute-done.10.refs_1_
  30.0 1.3 %collective-permute-start.11 = (bf16[256,512]{1,0:T(8,128)(2,1)S(1)}, bf16[256,512]{1,0:T(8,128)(2,1)S(1)}, u32[]{:S(2)}, u32[]{:S(2)}) collective-permute-start(bf16[256,512]{1,0:T(8,128)(2,1)S(1)} %collective-permute-done.9.refs_2_), channel_id=1, source_target_pairs={{8,0},{10,2},{12,4},{14,6},{16,24},{18,26},{20,28},{22,30},{9,1},{... | collective-permute-start | bytes 786440 | tf_op jit(solution)/shard_map/ppermute | solution.py:558
  31.3 0.7 collective-permute-start.12
  32.0 5.2 %collective-permute-done.7.refs_2_.refs_1_ = bf16[192,1024]{1,0:T(8,128)(2,1)S(1)} collective-permute-done((bf16[192,1024]{1,0:T(8,128)(2,1)S(1)}, bf16[192,1024]{1,0:T(8,128)(2,1)S(1)}, u32[]{:S(2)}, u32[]{:S(2)}) %collective-permute-start.7) | collective-permute-done | bytes 393248 | tf_op jit(solution)/shard_map/ppermute | solution.py:533
  37.2 0.5 shard_map.94
  37.8 1.3 %collective-permute-done.11.refs_3_ = bf16[256,512]{1,0:T(8,128)(2,1)S(1)} collective-permute-done((bf16[256,512]{1,0:T(8,128)(2,1)S(1)}, bf16[256,512]{1,0:T(8,128)(2,1)S(1)}, u32[]{:S(2)}, u32[]{:S(2)}) %collective-permute-start.11) | collective-permute-done | bytes 262176 | tf_op jit(solution)/shard_map/ppermute | solution.py:558
  39.0 3.7 %collective-permute-start.14 = (bf16[256,256]{1,0:T(8,128)(2,1)S(1)}, bf16[256,256]{1,0:T(8,128)(2,1)S(1)}, u32[]{:S(2)}, u32[]{:S(2)}) collective-permute-start(bf16[256,256]{1,0:T(8,128)(2,1)S(1)} %get-tuple-element.106.refs_0_), channel_id=1, source_target_pairs={{0,8},{2,10},{4,12},{6,14},{8,0},{10,2},{12,4},{14,6},{16,24},{18,... | collective-permute-start | bytes 393224 | tf_op jit(solution)/shard_map/ppermute | solution.py:542
  42.7 2.4 %collective-permute-start.16 = (bf16[256,256]{1,0:T(8,128)(2,1)S(1)}, bf16[256,256]{1,0:T(8,128)(2,1)S(1)}, u32[]{:S(2)}, u32[]{:S(2)}) collective-permute-start(bf16[256,256]{1,0:T(8,128)(2,1)S(1)} %get-tuple-element.106.refs_0_), channel_id=1, source_target_pairs={{0,24},{2,26},{4,28},{6,30},{8,16},{10,18},{12,20},{14,22},{16,8},... | collective-permute-start | bytes 393224 | tf_op jit(solution)/shard_map/ppermute | solution.py:542
  45.1 0.1 shard_map.95
  45.2 2.8 %shard_map.96 = (bf16[1152,1024]{1,0:T(8,128)(2,1)S(1)}, bf16[1152,256]{1,0:T(8,128)(2,1)S(1)}, bf16[1152,128]{1,0:T(8,128)(2,1)S(1)}, bf16[1152,128]{1,0:T(8,12...) custom-call(s32[8]{0:T(128)S(1)} %copy-done.2, ...), custom_call_target="tpu_custom_call" | custom-call | tf_op jit(solution)/shard_map/pallas_call | solution.py:35
  48.0 3.0 %collective-permute-start.17 = (bf16[144,256]{1,0:T(8,128)(2,1)S(1)}, bf16[144,256]{1,0:T(8,128)(2,1)S(1)}, u32[]{:S(2)}, u32[]{:S(2)}) collective-permute-start(bf16[144,256]{1,0:T(8,128)(2,1)S(1)} %get-tuple-element.122), channel_id=1, source_target_pairs={{0,8},{2,10},{4,12},{6,14},{8,16},{10,18},{12,20},{14,22},{16,24},... | collective-permute-start | bytes 221192 | tf_op jit(solution)/shard_map/ppermute | solution.py:536
  51.0 2.8 %collective-permute-start.18 = (bf16[144,256]{1,0:T(8,128)(2,1)S(1)}, bf16[144,256]{1,0:T(8,128)(2,1)S(1)}, u32[]{:S(2)}, u32[]{:S(2)}) collective-permute-start(bf16[144,256]{1,0:T(8,128)(2,1)S(1)} %get-tuple-element.122), channel_id=1, source_target_pairs={{0,16},{2,18},{4,20},{6,22},{8,24},{10,26},{12,28},{14,30},{1,17},... | collective-permute-start | bytes 221192 | tf_op jit(solution)/shard_map/ppermute | solution.py:536
  53.9 1.3 %collective-permute-start.19 = (bf16[144,256]{1,0:T(8,128)(2,1)S(1)}, bf16[144,256]{1,0:T(8,128)(2,1)S(1)}, u32[]{:S(2)}, u32[]{:S(2)}) collective-permute-start(bf16[144,256]{1,0:T(8,128)(2,1)S(1)} %get-tuple-element.122), channel_id=1, source_target_pairs={{0,24},{2,26},{4,28},{6,30},{1,25},{3,27},{5,29},{7,31}} | collective-permute-start | bytes 221192 | tf_op jit(solution)/shard_map/ppermute | solution.py:536
  55.3 1.9 %shard_map.98 = (f32[1152,256]{1,0:T(8,128)S(1)}, f32[1152,256]{1,0:T(8,128)S(1)}) custom-call(bf16[1152,256]{1,0:T(8,128)(2,1)S(1)} %get-tuple-element.113.x_ref, bf16[1152,128]{1,0:T(8,128)(2,1)S(1)} %get-tuple-element.114.b_ref, bf16[1152,128]{1,0:T(8,128)(2,1)S(1)} %get-tuple-element.112.c_ref, f32[216,128]{1,0:T(8,128)S(1)} %get-tuple-element.115.rows_ref), custom_call_target="tpu_custom_call" | custom-call | flops 134217728 | bytes 3649536 | tf_op jit(solution)/shard_map/pallas_call | solution.py:35
  57.2 0.8 %shard_map.99.silu_ref = f32[1152,256]{1,0:T(8,128)S(1)} custom-call(f32[1,1024]{1,0:T(1,128)S(1)} %bitcast.2, bf16[1152,1024]{1,0:T(8,128)(2,1)S(1)} %get-tuple-element.120.frames_ref, bf16[1024,256]{1,0:T(8,128)(2,1)S(1)} %get-tuple-element.121.weight_ref), custom_call_target="tpu_custom_call" | custom-call | flops 536870912 | bytes 4067328 | tf_op jit(solution)/shard_map/pallas_call | solution.py:35
  58.1 0.7 shard_map.100.gated_ref
  58.8 0.1 copy-done.1
  59.0 1.6 %shard_map.101.refs_0_ = bf16[256,256]{1,0:T(8,128)(2,1)S(1)} custom-call(s32[8]{0:T(128)S(1)} %copy-done.2, f32[31,1024]{1,0:T(8,128)S(1)} %copy-done.1, bf16[1152,256]{1,0:T(8,128)(2,1)S(1)} %shard_map.100.gated_ref), custom_call_target="tpu_custom_call" | custom-call | flops 4063232 | bytes 847904 | tf_op jit(solution)/shard_map/pallas_call | solution.py:35
  60.6 0.4 collective-permute-start.20
  61.0 3.9 %shard_map.102.refs_0_ = bf16[512,256]{1,0:T(8,128)(2,1)S(1)} custom-call(s32[8]{0:T(128)S(1)} %copy-done.2, f32[31,1024]{1,0:T(8,128)S(1)} %copy-done.1, bf16[1152,256]{1,0:T(8,128)(2,1)S(1)} %shard_map.100.gated_ref), custom_call_target="tpu_custom_call" | custom-call | flops 8126464 | bytes 978976 | tf_op jit(solution)/shard_map/pallas_call | solution.py:35
  64.9 0.3 shard_map.103
  65.3 0.2 collective-permute-start.22
  65.5 2.5 %collective-permute-start.24 = (bf16[256,512]{1,0:T(8,128)(2,1)S(1)}, bf16[256,512]{1,0:T(8,128)(2,1)S(1)}, u32[]{:S(2)}, u32[]{:S(2)}) collective-permute-start(bf16[256,512]{1,0:T(8,128)(2,1)S(1)} %shard_map.103), channel_id=1, source_target_pairs={{0,6},{2,4},{4,2},{6,0},{8,14},{10,12},{12,10},{14,8},{16,22},{18,... | collective-permute-start | bytes 786440 | tf_op jit(solution)/shard_map/ppermute | solution.py:533
  68.0 0.5 shard_map.104
  68.5 1.9 %collective-permute-start.26 = (bf16[256,512]{1,0:T(8,128)(2,1)S(1)}, bf16[256,512]{1,0:T(8,128)(2,1)S(1)}, u32[]{:S(2)}, u32[]{:S(2)}) collective-permute-start(bf16[256,512]{1,0:T(8,128)(2,1)S(1)} %get-tuple-element.138), channel_id=1, source_target_pairs={{0,4},{2,6},{4,0},{6,2},{8,12},{10,14},{12,8},{14,10},{16,20},{18,... | collective-permute-start | bytes 786440 | tf_op jit(solution)/shard_map/ppermute | solution.py:533
  70.4 1.6 %shard_map.105.refs_0_ = bf16[256,256]{1,0:T(8,128)(2,1)S(1)} custom-call(s32[8]{0:T(128)S(1)} %copy-done.2, f32[31,1024]{1,0:T(8,128)S(1)} %copy-done.1, bf16[1152,256]{1,0:T(8,128)(2,1)S(1)} %shard_map.100.gated_ref), custom_call_target="tpu_custom_call" | custom-call | flops 4063232 | bytes 847904 | tf_op jit(solution)/shard_map/pallas_call | solution.py:35
  72.2 1.3 %collective-permute-done.23.refs_1_ = bf16[256,256]{1,0:T(8,128)(2,1)S(1)} collective-permute-done((bf16[256,256]{1,0:T(8,128)(2,1)S(1)}, bf16[256,256]{1,0:T(8,128)(2,1)S(1)}, u32[]{:S(2)}, u32[]{:S(2)}) %collective-permute-start.23) | collective-permute-done | bytes 131104 | tf_op jit(solution)/shard_map/ppermute | solution.py:539
  73.5 0.3 shard_map.106.own_ref
  73.8 1.7 %collective-permute-done.24.refs_0_ = bf16[256,512]{1,0:T(8,128)(2,1)S(1)} collective-permute-done((bf16[256,512]{1,0:T(8,128)(2,1)S(1)}, bf16[256,512]{1,0:T(8,128)(2,1)S(1)}, u32[]{:S(2)}, u32[]{:S(2)}) %collective-permute-start.24) | collective-permute-done | bytes 262176 | tf_op jit(solution)/shard_map/ppermute | solution.py:533
  75.6 4.5 %collective-permute-done.25.refs_1_ = bf16[256,512]{1,0:T(8,128)(2,1)S(1)} collective-permute-done((bf16[256,512]{1,0:T(8,128)(2,1)S(1)}, bf16[256,512]{1,0:T(8,128)(2,1)S(1)}, u32[]{:S(2)}, u32[]{:S(2)}) %collective-permute-start.25) | collective-permute-done | bytes 262176 | tf_op jit(solution)/shard_map/ppermute | solution.py:533
  80.1 0.5 collective-permute-done.26.refs_2_
  80.6 0.8 %shard_map.107 = bf16[256,512]{1,0:T(8,128)(2,1)} custom-call(f32[256,512]{1,0:T(8,128)S(1)} %shard_map.106.own_ref, bf16[256,512]{1,0:T(8,128)(2,1)S(1)} %collective-permute-done.24.refs_0_, bf16[256,512]{1,0:T(8,128)(2,1)S(1)} %collective-permute-done.25.refs_1_, bf16[256,512]{1,0:T(8,128)(2,1)S(1)} %collective-permute-done.26.refs_2_), custom_call_target="tpu_custom_call" | custom-call | bytes 1572864 | tf_op jit(solution)/shard_map/pallas_call | solution.py:35
  (37 shorter events, 0.6 us)
Async XLA Ops:
  2.0 9.9 %collective-permute-start = (bf16[64,768]{1,0:T(8,128)(2,1)}, bf16[64,768]{1,0:T(8,128)(2,1)S(1)}, u32[]{:S(2)}, u32[]{:S(2)}) collective-permute-start(bf16[64,768]{1,0:T(8,128)(2,1)} %get-tuple-element.73), channel_id=1, source_target_pairs={{0,2},{2,0},{4,6},{6,4},{8,10},{10,8},{12,14},{14,12},{16,18},{18,... | collective-permute-start | bytes 294920 | tf_op jit(solution)/shard_map/ppermute | solution.py:533
  5.0 7.0 %collective-permute-start.1 = (bf16[64,768]{1,0:T(8,128)(2,1)}, bf16[64,768]{1,0:T(8,128)(2,1)S(1)}, u32[]{:S(2)}, u32[]{:S(2)}) collective-permute-start(bf16[64,768]{1,0:T(8,128)(2,1)} %get-tuple-element.74), channel_id=1, source_target_pairs={{0,4},{2,6},{4,0},{6,2},{8,12},{10,14},{12,8},{14,10},{16,20},{18,... | collective-permute-start | bytes 294920 | tf_op jit(solution)/shard_map/ppermute | solution.py:533
  6.5 5.7 %collective-permute-start.2 = (bf16[64,768]{1,0:T(8,128)(2,1)}, bf16[64,768]{1,0:T(8,128)(2,1)S(1)}, u32[]{:S(2)}, u32[]{:S(2)}) collective-permute-start(bf16[64,768]{1,0:T(8,128)(2,1)} %get-tuple-element.75), channel_id=1, source_target_pairs={{0,6},{2,4},{4,2},{6,0},{8,14},{10,12},{12,10},{14,8},{16,22},{18,... | collective-permute-start | bytes 294920 | tf_op jit(solution)/shard_map/ppermute | solution.py:533
  6.5 6.6 %collective-permute-start.3 = (bf16[32,1024]{1,0:T(8,128)(2,1)}, bf16[32,1024]{1,0:T(8,128)(2,1)S(1)}, u32[]{:S(2)}, u32[]{:S(2)}) collective-permute-start(bf16[32,1024]{1,0:T(8,128)(2,1)} %get-tuple-element.78), channel_id=1, source_target_pairs={{0,8},{2,10},{4,12},{6,14},{8,0},{10,2},{12,4},{14,6},{16,24},{18,... | collective-permute-start | bytes 196616 | tf_op jit(solution)/shard_map/ppermute | solution.py:542
  8.5 7.3 %collective-permute-start.4 = (bf16[32,1024]{1,0:T(8,128)(2,1)}, bf16[32,1024]{1,0:T(8,128)(2,1)S(1)}, u32[]{:S(2)}, u32[]{:S(2)}) collective-permute-start(bf16[32,1024]{1,0:T(8,128)(2,1)} %get-tuple-element.79), channel_id=1, source_target_pairs={{0,16},{2,18},{4,20},{6,22},{8,24},{10,26},{12,28},{14,30},{16,0},... | collective-permute-start | bytes 196616 | tf_op jit(solution)/shard_map/ppermute | solution.py:542
  11.9 6.3 %collective-permute-start.5 = (bf16[32,1024]{1,0:T(8,128)(2,1)}, bf16[32,1024]{1,0:T(8,128)(2,1)S(1)}, u32[]{:S(2)}, u32[]{:S(2)}) collective-permute-start(bf16[32,1024]{1,0:T(8,128)(2,1)} %get-tuple-element.80), channel_id=1, source_target_pairs={{0,24},{2,26},{4,28},{6,30},{8,16},{10,18},{12,20},{14,22},{16,8},... | collective-permute-start | bytes 196616 | tf_op jit(solution)/shard_map/ppermute | solution.py:542
  12.2 0.9 %copy-start.4 = (bf16[64,768]{1,0:T(8,128)(2,1)S(1)}, bf16[64,768]{1,0:T(8,128)(2,1)}, u32[]{:S(2)}) copy-start(bf16[64,768]{1,0:T(8,128)(2,1)} %get-tuple-element.72.refs_0_) | copy-start | bytes 294916
  13.1 6.1 %copy-start = (bf16[256,1024]{1,0:T(8,128)(2,1)S(1)}, bf16[256,1024]{1,0:T(8,128)(2,1)}, u32[]{:S(2)}) copy-start(bf16[256,1024]{1,0:T(8,128)(2,1)} %own_ref.1) | copy-start | bytes 1572868
  13.1 6.1 %copy-start.5 = (bf16[32,1024]{1,0:T(8,128)(2,1)S(1)}, bf16[32,1024]{1,0:T(8,128)(2,1)}, u32[]{:S(2)}) copy-start(bf16[32,1024]{1,0:T(8,128)(2,1)} %get-tuple-element.81.refs_0_) | copy-start | bytes 196612
  18.2 11.5 %collective-permute-start.9 = (bf16[256,512]{1,0:T(8,128)(2,1)S(1)}, bf16[256,512]{1,0:T(8,128)(2,1)S(1)}, u32[]{:S(2)}, u32[]{:S(2)}) collective-permute-start(bf16[256,512]{1,0:T(8,128)(2,1)S(1)} %get-tuple-element.95.refs_0_), channel_id=1, source_target_pairs={{0,16},{2,18},{4,20},{6,22},{8,24},{10,26},{12,28},{14,30},{16,0},... | collective-permute-start | bytes 786440 | tf_op jit(solution)/shard_map/ppermute | solution.py:542
  18.4 11.6 %collective-permute-start.10 = (bf16[256,512]{1,0:T(8,128)(2,1)S(1)}, bf16[256,512]{1,0:T(8,128)(2,1)S(1)}, u32[]{:S(2)}, u32[]{:S(2)}) collective-permute-start(bf16[256,512]{1,0:T(8,128)(2,1)S(1)} %get-tuple-element.95.refs_0_), channel_id=1, source_target_pairs={{0,8},{2,10},{4,12},{6,14},{8,0},{10,2},{12,4},{14,6},{16,24},{18,... | collective-permute-start | bytes 786440 | tf_op jit(solution)/shard_map/ppermute | solution.py:542
  19.4 12.6 %collective-permute-start.6 = (bf16[192,1024]{1,0:T(8,128)(2,1)S(1)}, bf16[192,1024]{1,0:T(8,128)(2,1)S(1)}, u32[]{:S(2)}, u32[]{:S(2)}) collective-permute-start(bf16[192,1024]{1,0:T(8,128)(2,1)S(1)} %get-tuple-element.86), channel_id=1, source_target_pairs={{0,2},{2,0},{4,6},{6,4},{8,10},{10,8},{12,14},{14,12},{16,18},{18,... | collective-permute-start | bytes 1179656 | tf_op jit(solution)/shard_map/ppermute | solution.py:533
  21.3 15.9 %collective-permute-start.7 = (bf16[192,1024]{1,0:T(8,128)(2,1)S(1)}, bf16[192,1024]{1,0:T(8,128)(2,1)S(1)}, u32[]{:S(2)}, u32[]{:S(2)}) collective-permute-start(bf16[192,1024]{1,0:T(8,128)(2,1)S(1)} %get-tuple-element.87), channel_id=1, source_target_pairs={{0,4},{2,6},{4,0},{6,2},{8,12},{10,14},{12,8},{14,10},{16,20},{18,... | collective-permute-start | bytes 1179656 | tf_op jit(solution)/shard_map/ppermute | solution.py:533
  22.8 14.4 %collective-permute-start.8 = (bf16[192,1024]{1,0:T(8,128)(2,1)S(1)}, bf16[192,1024]{1,0:T(8,128)(2,1)S(1)}, u32[]{:S(2)}, u32[]{:S(2)}) collective-permute-start(bf16[192,1024]{1,0:T(8,128)(2,1)S(1)} %get-tuple-element.88), channel_id=1, source_target_pairs={{0,6},{2,4},{4,2},{6,0},{8,14},{10,12},{12,10},{14,8},{16,22},{18,... | collective-permute-start | bytes 1179656 | tf_op jit(solution)/shard_map/ppermute | solution.py:533
  30.0 9.0 %collective-permute-start.11 = (bf16[256,512]{1,0:T(8,128)(2,1)S(1)}, bf16[256,512]{1,0:T(8,128)(2,1)S(1)}, u32[]{:S(2)}, u32[]{:S(2)}) collective-permute-start(bf16[256,512]{1,0:T(8,128)(2,1)S(1)} %collective-permute-done.9.refs_2_), channel_id=1, source_target_pairs={{8,0},{10,2},{12,4},{14,6},{16,24},{18,26},{20,28},{22,30},{9,1},{... | collective-permute-start | bytes 786440 | tf_op jit(solution)/shard_map/ppermute | solution.py:558
  31.3 7.7 %collective-permute-start.12 = (bf16[256,512]{1,0:T(8,128)(2,1)S(1)}, bf16[256,512]{1,0:T(8,128)(2,1)S(1)}, u32[]{:S(2)}, u32[]{:S(2)}) collective-permute-start(bf16[256,512]{1,0:T(8,128)(2,1)S(1)} %get-tuple-element.95.refs_0_), channel_id=1, source_target_pairs={{8,16},{10,18},{12,20},{14,22},{16,8},{18,10},{20,12},{22,14},{9,1... | collective-permute-start | bytes 786440 | tf_op jit(solution)/shard_map/ppermute | solution.py:559
  37.7 7.5 %collective-permute-start.13 = (bf16[512,1024]{1,0:T(8,128)(2,1)S(1)}, bf16[512,1024]{1,0:T(8,128)(2,1)S(1)}, u32[]{:S(2)}, u32[]{:S(2)}) collective-permute-start(bf16[512,1024]{1,0:T(8,128)(2,1)S(1)} %get-tuple-element.102), channel_id=1, source_target_pairs={{0,1},{1,0},{2,3},{3,2},{4,5},{5,4},{6,7},{7,6},{8,9},{9,8},{10,11... | collective-permute-start | bytes 3145736 | tf_op jit(solution)/shard_map/ppermute | solution.py:539
  39.0 6.1 %copy-start.2 = (s32[8]{0:T(128)S(1)}, s32[8]{0:T(128)}, u32[]{:S(2)}) copy-start(s32[8]{0:T(128)} %len_ref.7) | copy-start | bytes 100
  39.0 14.8 %collective-permute-start.14 = (bf16[256,256]{1,0:T(8,128)(2,1)S(1)}, bf16[256,256]{1,0:T(8,128)(2,1)S(1)}, u32[]{:S(2)}, u32[]{:S(2)}) collective-permute-start(bf16[256,256]{1,0:T(8,128)(2,1)S(1)} %get-tuple-element.106.refs_0_), channel_id=1, source_target_pairs={{0,8},{2,10},{4,12},{6,14},{8,0},{10,2},{12,4},{14,6},{16,24},{18,... | collective-permute-start | bytes 393224 | tf_op jit(solution)/shard_map/ppermute | solution.py:542
  42.7 12.5 %collective-permute-start.15 = (bf16[256,256]{1,0:T(8,128)(2,1)S(1)}, bf16[256,256]{1,0:T(8,128)(2,1)S(1)}, u32[]{:S(2)}, u32[]{:S(2)}) collective-permute-start(bf16[256,256]{1,0:T(8,128)(2,1)S(1)} %get-tuple-element.106.refs_0_), channel_id=1, source_target_pairs={{0,16},{2,18},{4,20},{6,22},{8,24},{10,26},{12,28},{14,30},{16,0},... | collective-permute-start | bytes 393224 | tf_op jit(solution)/shard_map/ppermute | solution.py:542
  42.7 12.5 %collective-permute-start.16 = (bf16[256,256]{1,0:T(8,128)(2,1)S(1)}, bf16[256,256]{1,0:T(8,128)(2,1)S(1)}, u32[]{:S(2)}, u32[]{:S(2)}) collective-permute-start(bf16[256,256]{1,0:T(8,128)(2,1)S(1)} %get-tuple-element.106.refs_0_), channel_id=1, source_target_pairs={{0,24},{2,26},{4,28},{6,30},{8,16},{10,18},{12,20},{14,22},{16,8},... | collective-permute-start | bytes 393224 | tf_op jit(solution)/shard_map/ppermute | solution.py:542
  48.0 9.2 %copy-start.3 = (f32[1024]{0:T(1024)S(1)}, f32[1024]{0:T(1024)}, u32[]{:S(2)}) copy-start(f32[1024]{0:T(1024)} %param.14) | copy-start | bytes 12292
  48.0 10.0 %collective-permute-start.17 = (bf16[144,256]{1,0:T(8,128)(2,1)S(1)}, bf16[144,256]{1,0:T(8,128)(2,1)S(1)}, u32[]{:S(2)}, u32[]{:S(2)}) collective-permute-start(bf16[144,256]{1,0:T(8,128)(2,1)S(1)} %get-tuple-element.122), channel_id=1, source_target_pairs={{0,8},{2,10},{4,12},{6,14},{8,16},{10,18},{12,20},{14,22},{16,24},... | collective-permute-start | bytes 221192 | tf_op jit(solution)/shard_map/ppermute | solution.py:536
  51.0 7.0 %collective-permute-start.18 = (bf16[144,256]{1,0:T(8,128)(2,1)S(1)}, bf16[144,256]{1,0:T(8,128)(2,1)S(1)}, u32[]{:S(2)}, u32[]{:S(2)}) collective-permute-start(bf16[144,256]{1,0:T(8,128)(2,1)S(1)} %get-tuple-element.122), channel_id=1, source_target_pairs={{0,16},{2,18},{4,20},{6,22},{8,24},{10,26},{12,28},{14,30},{1,17},... | collective-permute-start | bytes 221192 | tf_op jit(solution)/shard_map/ppermute | solution.py:536
  53.9 4.2 %collective-permute-start.19 = (bf16[144,256]{1,0:T(8,128)(2,1)S(1)}, bf16[144,256]{1,0:T(8,128)(2,1)S(1)}, u32[]{:S(2)}, u32[]{:S(2)}) collective-permute-start(bf16[144,256]{1,0:T(8,128)(2,1)S(1)} %get-tuple-element.122), channel_id=1, source_target_pairs={{0,24},{2,26},{4,28},{6,30},{1,25},{3,27},{5,29},{7,31}} | collective-permute-start | bytes 221192 | tf_op jit(solution)/shard_map/ppermute | solution.py:536
  58.1 0.9 %copy-start.1 = (f32[31,1024]{1,0:T(8,128)S(1)}, f32[31,1024]{1,0:T(8,128)}, u32[]{:S(2)}) copy-start(f32[31,1024]{1,0:T(8,128)} %taps_ref.5) | copy-start | bytes 380932
  58.8 6.2 %collective-permute-start.21 = (bf16[512,256]{1,0:T(8,128)(2,1)S(1)}, bf16[512,256]{1,0:T(8,128)(2,1)S(1)}, u32[]{:S(2)}, u32[]{:S(2)}) collective-permute-start(bf16[512,256]{1,0:T(8,128)(2,1)S(1)} %get-tuple-element.126), channel_id=1, source_target_pairs={{0,1},{1,0},{2,3},{3,2},{4,5},{5,4},{6,7},{7,6},{8,9},{9,8},{10,11... | collective-permute-start | bytes 786440 | tf_op jit(solution)/shard_map/ppermute | solution.py:539
  60.6 4.3 %collective-permute-start.20 = (bf16[256,256]{1,0:T(8,128)(2,1)S(1)}, bf16[256,256]{1,0:T(8,128)(2,1)S(1)}, u32[]{:S(2)}, u32[]{:S(2)}) collective-permute-start(bf16[256,256]{1,0:T(8,128)(2,1)S(1)} %shard_map.101.refs_0_), channel_id=1, source_target_pairs={{0,1},{1,0},{2,3},{3,2},{4,5},{5,4},{6,7},{7,6},{8,9},{9,8},{10,11... | collective-permute-start | bytes 393224 | tf_op jit(solution)/shard_map/ppermute | solution.py:539
  65.3 2.7 %collective-permute-start.22 = (bf16[512,256]{1,0:T(8,128)(2,1)S(1)}, bf16[512,256]{1,0:T(8,128)(2,1)S(1)}, u32[]{:S(2)}, u32[]{:S(2)}) collective-permute-start(bf16[512,256]{1,0:T(8,128)(2,1)S(1)} %shard_map.102.refs_0_), channel_id=1, source_target_pairs={{0,1},{1,0},{2,3},{3,2},{4,5},{5,4},{6,7},{7,6},{8,9},{9,8},{10,11... | collective-permute-start | bytes 786440 | tf_op jit(solution)/shard_map/ppermute | solution.py:539
  65.5 10.1 %collective-permute-start.24 = (bf16[256,512]{1,0:T(8,128)(2,1)S(1)}, bf16[256,512]{1,0:T(8,128)(2,1)S(1)}, u32[]{:S(2)}, u32[]{:S(2)}) collective-permute-start(bf16[256,512]{1,0:T(8,128)(2,1)S(1)} %shard_map.103), channel_id=1, source_target_pairs={{0,6},{2,4},{4,2},{6,0},{8,14},{10,12},{12,10},{14,8},{16,22},{18,... | collective-permute-start | bytes 786440 | tf_op jit(solution)/shard_map/ppermute | solution.py:533
  68.4 11.7 %collective-permute-start.25 = (bf16[256,512]{1,0:T(8,128)(2,1)S(1)}, bf16[256,512]{1,0:T(8,128)(2,1)S(1)}, u32[]{:S(2)}, u32[]{:S(2)}) collective-permute-start(bf16[256,512]{1,0:T(8,128)(2,1)S(1)} %get-tuple-element.137), channel_id=1, source_target_pairs={{0,2},{2,0},{4,6},{6,4},{8,10},{10,8},{12,14},{14,12},{16,18},{18,... | collective-permute-start | bytes 786440 | tf_op jit(solution)/shard_map/ppermute | solution.py:533
  68.5 12.1 %collective-permute-start.26 = (bf16[256,512]{1,0:T(8,128)(2,1)S(1)}, bf16[256,512]{1,0:T(8,128)(2,1)S(1)}, u32[]{:S(2)}, u32[]{:S(2)}) collective-permute-start(bf16[256,512]{1,0:T(8,128)(2,1)S(1)} %get-tuple-element.138), channel_id=1, source_target_pairs={{0,4},{2,6},{4,0},{6,2},{8,12},{10,14},{12,8},{14,10},{16,20},{18,... | collective-permute-start | bytes 786440 | tf_op jit(solution)/shard_map/ppermute | solution.py:533
  72.1 1.4 %collective-permute-start.23 = (bf16[256,256]{1,0:T(8,128)(2,1)S(1)}, bf16[256,256]{1,0:T(8,128)(2,1)S(1)}, u32[]{:S(2)}, u32[]{:S(2)}) collective-permute-start(bf16[256,256]{1,0:T(8,128)(2,1)S(1)} %shard_map.105.refs_0_), channel_id=1, source_target_pairs={{0,1},{1,0},{2,3},{3,2},{4,5},{5,4},{6,7},{7,6},{8,9},{9,8},{10,11... | collective-permute-start | bytes 393224 | tf_op jit(solution)/shard_map/ppermute | solution.py:539
